TPU v7x, 128 devices: a whole 4x4x4 slice. The times are simulated.
128 devices in a mesh: roll: 8 (over y, core), frame: 16 (over z, x).
Axes of the slice: x: 4, y: 4, z: 4, core: 2. Of those that a mesh axis runs over, the one named last changes fastest.
Arguments:
- patch_activation_tensor: bfloat16 [8, 16, 576, 2048], P('roll', 'frame'), may hold values from -900 to 900
- conditioning_affine: float32 [8, 16, 2, 2048], P('roll', 'frame'), may hold values from -3 to 3
- entry_projection_matrix: bfloat16 [2048, 3072], replicated, may hold values from -0.125 to 0.125
- exit_projection_matrix: bfloat16 [1024, 2048], replicated, may hold values from -0.1875 to 0.1875
- softmax_sharpness: float32 [2, 4], replicated, may hold values from 15 to 45
- cached_past_pairs: bfloat16 [64, 576, 2, 512], P('roll', 'frame'), may hold values from -6 to 6
- recalled_picture_holder: int32 [8, 16, 6, 1], P('roll', 'frame'), may hold values from 0 to 7; in each aligned block of 6 rows (0 to 5, 6 to 11, ..., all dimensions but the last counted through in order) at most 2 rows name the same one
- recalled_picture_position: int32 [8, 16, 6], P('roll', 'frame'), may hold values from 0 to 7
- lookback_lengths: int32 [8], P('roll'), may hold values from 2 to 16, as said below
Outputs:
- attended: bfloat16 [8, 16, 576, 2048], P('roll', 'frame')
Inputs may be any that keep to these rules, and one draw needn't show every extreme that they name: `recalled_picture_holder`: among the 6 retrievals of one frame no owner appears more than 2 times, and some frames name one owner exactly 2 times. `lookback_lengths`: some rollout has context 16 and some has 2.
All inputs are finite; a program needn't handle non-finite values.
Results may differ from a plain program's by a relative error of at most 0.011.
Values may be sent and summed in bfloat16 or wider, within the bound.
No kernel may reach another device: no remote copies, remote signals or barrier semaphores. Data moves between devices by JAX's collectives and lax.ppermute only.
A program may use at most 192 MiB of HBM per device.

v0:
```python
import jax
import jax.numpy as jnp
from jax import lax
from jax.sharding import PartitionSpec as P

D = 2048
PLANAR_GROUPS = 4
ATTN_CHANNELS = 128
TOPM = 6
CAP = 2


EPSILON = 1e-06


def normed(values):
    return values * lax.rsqrt(jnp.mean(values * values, axis=-1, keepdims=True) + EPSILON)


def entries_multiplied(values, factor):
    return (normed(values.astype(jnp.float32)) * (factor[:, None] / ATTN_CHANNELS)).astype(
        jnp.bfloat16
    )


def unit_rows(values):
    return normed(values.astype(jnp.float32)).astype(jnp.bfloat16)


def rank_within(owner_lists):
    same_owner = owner_lists[:, :, None] == owner_lists[:, None, :]
    earlier = (
        jnp.arange(TOPM, dtype=jnp.int32)[:, None] < jnp.arange(TOPM, dtype=jnp.int32)[None, :]
    )
    return jnp.sum(same_owner & earlier[None], axis=1)


def on_device(
    patch_activation_tensor,
    conditioning_affine,
    entry_projection_matrix,
    exit_projection_matrix,
    softmax_sharpness,
    cached_past_pairs,
    recalled_picture_holder,
    recalled_picture_position,
    lookback_lengths,
):
    roll_count = lax.axis_size("roll")
    frame_count = lax.axis_size("frame")
    my_roll = lax.axis_index("roll")
    patches = patch_activation_tensor.shape[2]
    piece_rows = cached_past_pairs.shape[1]
    head_width = PLANAR_GROUPS * ATTN_CHANNELS
    activation = patch_activation_tensor[0, 0].astype(jnp.float32)
    hidden = (
        normed(activation) * (1.0 + conditioning_affine[0, 0, 0]) + conditioning_affine[0, 0, 1]
    ).astype(jnp.bfloat16)
    owners = recalled_picture_holder.reshape(1, TOPM)
    slots = recalled_picture_position.reshape(1, TOPM)
    all_owner, all_slot = (
        lax.all_gather(owners, ("roll", "frame"), axis=0, tiled=True),
        lax.all_gather(slots, ("roll", "frame"), axis=0, tiled=True),
    )
    all_rank = rank_within(all_owner)
    wanted = all_owner == my_roll
    picked = []
    for slot_rank in range(CAP):
        match = wanted & (all_rank == slot_rank)
        picked.append(jnp.sum(jnp.where(match, all_slot, 0), axis=1))
    send_slot = jnp.stack(picked, axis=1)
    outgoing = cached_past_pairs[send_slot]
    incoming = lax.all_to_all(outgoing, ("roll", "frame"), split_axis=0, concat_axis=0, tiled=True)
    incoming = incoming.reshape(roll_count, frame_count, CAP, piece_rows, 2, head_width)
    my_rank = rank_within(owners)[0]
    fetched = incoming[owners[0], :, my_rank]
    memory_key = unit_rows(
        fetched[:, :, :, 0, :].reshape(TOPM * patches, PLANAR_GROUPS, ATTN_CHANNELS)
    )
    memory_value = fetched[:, :, :, 1, :].reshape(TOPM * patches, PLANAR_GROUPS, ATTN_CHANNELS)
    length = lookback_lengths[0]
    moved = lax.all_to_all(hidden[None], "frame", split_axis=1, concat_axis=0, tiled=True)
    total_frames = moved.shape[0]
    chronal_mapped_result = jnp.dot(
        moved.reshape(-1, D),
        entry_projection_matrix[:, 3 * head_width :],
        preferred_element_type=jnp.float32,
    ).astype(jnp.bfloat16)
    chronal_mapped_result = chronal_mapped_result.reshape(
        total_frames, moved.shape[1], 3, PLANAR_GROUPS, ATTN_CHANNELS
    )
    chronal_probe_vector = entries_multiplied(chronal_mapped_result[:, :, 0], softmax_sharpness[1])
    time_key = unit_rows(chronal_mapped_result[:, :, 1])
    key_rows = time_key
    value_rows = chronal_mapped_result[:, :, 2]
    total_frames = chronal_probe_vector.shape[0]
    attend_scores = jnp.einsum(
        "tphd,sphd->phts", chronal_probe_vector, key_rows, preferred_element_type=jnp.float32
    )
    target = jnp.arange(total_frames, dtype=jnp.int32)[:, None]
    source = jnp.arange(total_frames, dtype=jnp.int32)[None, :]
    window_mask = (source <= target) & (source > target - length)
    attend_weights = jnp.where(window_mask, jnp.exp(attend_scores), 0.0)
    attend_shares = (attend_weights / jnp.sum(attend_weights, axis=-1, keepdims=True)).astype(
        jnp.bfloat16
    )
    result = jnp.einsum(
        "phts,sphd->tphd", attend_shares, value_rows, preferred_element_type=jnp.float32
    )
    time_out = lax.all_to_all(
        result.astype(jnp.bfloat16), "frame", split_axis=0, concat_axis=1, tiled=True
    )
    planar_mapped_result = jnp.dot(
        hidden, entry_projection_matrix[:, : 3 * head_width], preferred_element_type=jnp.float32
    ).astype(jnp.bfloat16)
    planar_mapped_result = planar_mapped_result.reshape(patches, 3, PLANAR_GROUPS, ATTN_CHANNELS)
    planar_probe_vector = entries_multiplied(planar_mapped_result[:, 0], softmax_sharpness[0])
    space_key = unit_rows(planar_mapped_result[:, 1])
    key_rows = jnp.concatenate([space_key, memory_key], axis=0)
    value_rows = jnp.concatenate([planar_mapped_result[:, 2], memory_value], axis=0)
    head_results = []
    for head_index in range(PLANAR_GROUPS):
        scores = jnp.einsum(
            "qd,kd->qk",
            planar_probe_vector[:, head_index],
            key_rows[:, head_index],
            preferred_element_type=jnp.float32,
        )
        weights = jnp.exp(scores)
        shares = (weights / jnp.sum(weights, axis=-1, keepdims=True)).astype(jnp.bfloat16)
        head_results.append(
            jnp.dot(shares, value_rows[:, head_index], preferred_element_type=jnp.float32).astype(
                jnp.bfloat16
            )
        )
    space_out = jnp.stack(head_results, axis=1).reshape(patches, head_width)
    combined = jnp.concatenate([space_out, time_out.reshape(patches, head_width)], axis=1)
    attended = jnp.dot(combined, exit_projection_matrix, preferred_element_type=jnp.float32).astype(
        jnp.bfloat16
    )
    return attended.reshape(1, 1, patches, D)


def solution(mesh):
    return jax.shard_map(
        on_device,
        mesh=mesh,
        in_specs=(
            P("roll", "frame", None, None),
            P("roll", "frame", None, None),
            P(),
            P(),
            P(),
            P("roll", "frame", None, None),
            P("roll", "frame", None, None),
            P("roll", "frame", None),
            P("roll"),
        ),
        out_specs=P("roll", "frame", None, None),
        check_vma=False,
    )
```

profile of v0, /device:TPU:106, one launch (start us, length us, event | category | flops | bytes accessed | tf_op | source)
XLA Modules:
  0.0 700.7 jit_solution(7554210358124980148)
XLA Ops:
  0.0 0.9 slice_add_fusion
  0.9 2.2 fusion.6
  3.2 0.8 fusion.13
  4.0 5.8 copy.269
  9.7 0.5 broadcast.318
  10.2 14.6 %reduce.1 = bf16[576,2048]{1,0:T(8,128)(2,1)S(1)} reduce(bf16[576,1,2048]{2,1,0:T(2,128)(2,1)} %bitcast.186, bf16[]{:T(256)} %broadcast.318), dimensions={1}, to_apply=%bitcast.183.reduce_sub_computation | reduce | bytes 4718594
  24.8 3.9 reshape.479
  28.7 7.1 %all-to-all-start.1 = ((bf16[16,2,36864]{2,1,0:T(2,128)(2,1)}), bf16[16,2,36864]{2,1,0:T(2,128)(2,1)S(1)}, u32[]{:S(2)}, u32[]{:S(2)}) async-start(bf16[16,2,36864]{2,1,0:T(2,128)(2,1)} %reshape.479), calls=%async_computation.1 | async-start | bytes 4718592 | tf_op jit(solution)/shard_map/all_to_all | solution.py:82
  35.8 65.3 %all-gather = s32[128,1,6,1]{2,3,1,0:T(1,128)S(1)} all-gather(s32[1,1,6,1]{2,3,1,0:T(1,128)S(1)} %copy-done.19), channel_id=2, replica_groups=mesh['roll'=8,'frame'=16] {'roll','frame'}, dimensions={0}, use_global_device_ids=true | all-gather | bytes 3096 | tf_op jit(solution)/shard_map/all_gather | solution.py:62
  101.1 0.1 copy.163
  101.2 44.6 %all-gather.1 = s32[128,1,6]{2,1,0:T(1,128)S(1)} all-gather(s32[1,1,6]{2,1,0:T(1,128)S(1)} %copy-done.18), channel_id=3, replica_groups=mesh['roll'=8,'frame'=16] {'roll','frame'}, dimensions={0}, use_global_device_ids=true | all-gather | bytes 3096 | tf_op jit(solution)/shard_map/all_gather | solution.py:63
  145.8 0.1 copy.164
  146.6 0.0 copy-done.17
  146.6 0.5 multiply_bitcast_fusion.1
  147.1 0.0 all-to-all-done.1
  147.1 7.0 reshape.480
  154.1 9.5 %fusion.21 = bf16[576,1536]{1,0:T(8,128)(2,1)} fusion(bf16[2048,3072]{1,0:T(8,128)(2,1)} %param.11, bf16[1,576,2048]{2,0,1:T(2,128)(2,1)} %bitcast.187), kind=kOutput, calls=%fused_computation.40 | convolution fusion | flops 3624763392 | bytes 12779520 | tf_op jit(solution)/shard_map/dot_general | solution.py:84
  163.6 3.2 reshape.452
  166.8 0.6 fusion.100
  167.4 0.8 fusion.44
  168.3 0.8 fusion.37
  169.1 0.5 fusion.38
  169.6 1.0 copy.179
  170.6 6.3 all-to-all-start.2
  177.0 0.1 convert_reduce_fusion
  177.1 0.1 copy.165
  177.2 0.1 reshape.464
  177.4 41.3 %gather_fusion = bf16[256,36,2,512]{3,2,1,0:T(2,128)(2,1)} fusion(bf16[8,36,2,512]{3,2,1,0:T(2,128)(2,1)S(1)} %copy-done, s32[1024]{0:T(1024)S(1)} %pad_clamp_fusion), kind=kCustom, calls=%fused_computation | custom fusion | bytes 37749760 | tf_op jit(solution)/shard_map/gather | solution.py:72
  218.6 0.0 all-to-all-done.2
  218.7 12.7 %all-to-all-start = ((bf16[128,2,36,2,512]{4,3,2,1,0:T(2,128)(2,1)}), bf16[128,2,36,2,512]{4,3,2,1,0:T(2,128)(2,1)}, u32[]{:S(2)}, u32[]{:S(2)}) async-start(bf16[128,2,36,2,512]{4,3,2,1,0:T(2,128)(2,1)} %bitcast.185), calls=%async_computation | async-start | bytes 37748736 | tf_op jit(solution)/shard_map/all_to_all | solution.py:73
  231.4 7.9 %fusion.18 = bf16[576,1536]{1,0:T(8,128)(2,1)} fusion(bf16[2048,3072]{1,0:T(8,128)(2,1)} %param.11, bf16[1,1,576,2048]{3,2,1,0:T(8,128)(2,1)S(1)} %copy-done.6, f32[2048]{0:T(1024)S(1)} %bitcast.194, f32[2048]{0:T(1024)S(1)} %bitcast.192, f32[576]{0:T(1024)S(1)} %copy-done.15), kind=kOutput, calls=%fused_computation.39 | convolution fusion | flops 3630661632 | bytes 10438912 | tf_op jit(solution)/shard_map/dot_general | solution.py:113
  239.3 3.2 reshape.446
  242.5 0.1 fusion.90
  242.6 1.2 slice_bitcast_fusion
  243.9 0.4 fusion.39
  244.3 0.7 fusion.42
  245.1 1.2 fusion.41
  246.3 0.8 fusion.43
  247.1 0.9 copy.268
  248.0 269.2 %all-to-all-done = bf16[128,2,36,2,512]{4,3,2,1,0:T(2,128)(2,1)} async-done(((bf16[128,2,36,2,512]{4,3,2,1,0:T(2,128)(2,1)}), bf16[128,2,36,2,512]{4,3,2,1,0:T(2,128)(2,1)}, u32[]{:S(2)}, u32[]{:S(2)}) %all-to-all-start) | async-done | bytes 18874400 | tf_op jit(solution)/shard_map/all_to_all | solution.py:73
  517.2 35.5 %copy.167 = bf16[8,16,2,36,2,512]{5,1,4,3,2,0:T(8,128)(2,1)} copy(bf16[8,16,2,36,2,512]{5,4,3,2,1,0:T(2,128)(2,1)} %bitcast.14) | data formatting | bytes 37748736 | tf_op jit(solution)/shard_map/reshape | solution.py:74
  552.6 11.0 %gather_fusion.1 = bf16[6,16,36,2,512]{4,1,3,2,0:T(8,128)(2,1)} fusion(bf16[8,16,2,36,2,512]{5,1,4,3,2,0:T(8,128)(2,1)} %copy.167, s32[6]{0:T(128)S(1)} %fusion.96), kind=kCustom, calls=%fused_computation.1 | custom fusion | bytes 14155824 | tf_op jit(solution)/shard_map/gather | solution.py:76
  563.7 6.3 fusion.99
  570.0 7.1 %copy.168 = f32[6,16,36,1,512]{4,2,1,0,3:T(8,128)} copy(f32[6,16,36,1,512]{4,1,3,2,0:T(8,128)S(1)} %get-tuple-element.8) | data formatting | bytes 14155776 | tf_op jit(solution)/shard_map/convert_element_type | solution.py:27
  577.1 9.5 %reshape.458 = f32[3456,4,128]{2,1,0:T(4,128)} reshape(f32[6,16,36,1,512]{4,2,1,0,3:T(8,128)} %copy.168) | data formatting | bytes 14155776 | tf_op jit(solution)/shard_map/convert_element_type | solution.py:27
  586.7 7.6 %multiply_reduce_fusion = f32[3456,4]{1,0:T(8,128)S(1)} fusion(f32[3456,4,128]{2,1,0:T(4,128)} %reshape.458), kind=kLoop, calls=%fused_computation.11 | loop fusion | flops 3525120 | bytes 7133184 | tf_op jit(solution)/shard_map/reduce_sum | solution.py:17
  594.3 0.2 add_rsqrt_fusion
  594.5 5.1 multiply_convert_fusion
  599.6 4.0 copy.172
  603.7 7.4 %reshape_squeeze.4 = bf16[3456,4,128]{2,1,0:T(4,128)(2,1)} reshape(bf16[6,16,36,1,512]{4,2,1,0,3:T(8,128)(2,1)} %copy.172) | data formatting | bytes 7077888 | tf_op jit(solution)/shard_map/reshape;squeeze | solution.py:80
  611.0 22.1 %fusion.35 = (bf16[4032,1,128]{2,1,0:T(2,128)(2,1)S(1)}, bf16[4032,1,128]{2,1,0:T(2,128)(2,1)S(1)}, bf16[4032,1,128]{2,1,0:T(2,128)(2,1)}, bf16[4032,1,128]{2,1,0:T(2,128)(2,1)S(1)}) fusion(bf16[3456,4,128]{2,1,0:T(4,128)(2,1)} %multiply_convert_fusion, bf16[576,4,128]{2,1,0:T(4,128)(2,1)S(1)} %fusion.43), kind=kLoop, calls=%fused_computation.58 | loop fusion | flops 8257536 | bytes 8257536 | tf_op jit(solution)/shard_map/concatenate | solution.py:119
  633.2 1.5 exponential_reduce_fusion.3
  634.7 1.5 exponential_reduce_fusion.2
  636.2 1.5 exponential_reduce_fusion.1
  637.7 3.2 exponential_reduce_fusion
  641.0 45.2 %fusion.32 = (bf16[4032,1,128]{2,1,0:T(2,128)(2,1)}, bf16[4032,1,128]{2,1,0:T(2,128)(2,1)}, bf16[4032,1,128]{2,1,0:T(2,128)(2,1)}, bf16[4032,1,128]{2,1,0:T(2,128)(2,1)}) fusion(bf16[3456,4,128]{2,1,0:T(4,128)(2,1)S(1)} %copy-done.3, bf16[576,4,128]{2,1,0:T(4,128)(2,1)S(1)} %copy-done.8), kind=kLoop, calls=%fused_computation.55 | loop fusion | flops 8257536 | bytes 8257536 | tf_op jit(solution)/shard_map/concatenate | solution.py:120
  686.1 3.1 fusion.56
  689.2 3.2 fusion.57
  692.5 1.5 fusion.58
  693.9 0.1 copy-done.9
  694.0 1.5 fusion.59
  695.5 0.1 copy_bitcast_fusion.1
  695.6 0.8 copy-done.21
  696.4 3.9 fusion.24
  (53 shorter events, 0.3 us)
Async XLA Ops:
  0.0 177.3 %copy-start = (bf16[8,36,2,512]{3,2,1,0:T(2,128)(2,1)S(1)}, bf16[8,36,2,512]{3,2,1,0:T(2,128)(2,1)}, u32[]{:S(2)}) copy-start(bf16[8,36,2,512]{3,2,1,0:T(2,128)(2,1)} %param.14) | copy-start | bytes 1769476
  0.0 3.2 copy-start.5
  0.9 3.0 copy-start.12
  3.2 0.8 copy-start.14
  28.7 7.1 %copy-start.19 = (s32[1,1,6,1]{2,3,1,0:T(1,128)S(1)}, s32[1,1,6,1]{2,3,1,0:T(1,128)}, u32[]{:S(2)}) copy-start(s32[1,1,6,1]{2,3,1,0:T(1,128)} %param.15) | copy-start | bytes 76
  28.7 72.5 %copy-start.18 = (s32[1,1,6]{2,1,0:T(1,128)S(1)}, s32[1,1,6]{2,1,0:T(1,128)}, u32[]{:S(2)}) copy-start(s32[1,1,6]{2,1,0:T(1,128)} %param.16) | copy-start | bytes 76
  28.7 117.8 %copy-start.17 = (f32[2,4]{1,0:T(2,128)S(1)}, f32[2,4]{1,0:T(2,128)}, u32[]{:S(2)}) copy-start(f32[2,4]{1,0:T(2,128)} %param.13) | copy-start | bytes 100
  28.7 118.4 %all-to-all-start.1 = ((bf16[16,2,36864]{2,1,0:T(2,128)(2,1)}), bf16[16,2,36864]{2,1,0:T(2,128)(2,1)S(1)}, u32[]{:S(2)}, u32[]{:S(2)}) async-start(bf16[16,2,36864]{2,1,0:T(2,128)(2,1)} %reshape.479), calls=%async_computation.1 | async-start | bytes 4718592 | tf_op jit(solution)/shard_map/all_to_all | solution.py:82
  170.6 48.0 %all-to-all-start.2 = ((bf16[16,36,4,128]{3,2,1,0:T(4,128)(2,1)}), bf16[16,36,4,128]{3,2,1,0:T(4,128)(2,1)S(1)}, u32[]{:S(2)}, u32[]{:S(2)}) async-start(bf16[16,36,4,128]{3,2,1,0:T(4,128)(2,1)} %copy.179), calls=%async_computation.2 | async-start | bytes 1179648 | tf_op jit(solution)/shard_map/all_to_all | solution.py:110
  218.6 12.7 %copy-start.6 = (bf16[1,1,576,2048]{3,2,1,0:T(8,128)(2,1)S(1)}, bf16[1,1,576,2048]{3,2,1,0:T(8,128)(2,1)}, u32[]{:S(2)}) copy-start(bf16[1,1,576,2048]{3,2,1,0:T(8,128)(2,1)} %param.9) | copy-start | bytes 7077892
  218.6 12.7 %copy-start.13 = (f32[1,1,1,2048]{3,2,1,0:T(1,128)S(1)}, f32[1,1,1,2048]{3,2,1,0:T(1,128)}, u32[]{:S(2)}) copy-start(f32[1,1,1,2048]{3,2,1,0:T(1,128)} %copy-done.12) | copy-start | bytes 24580
  218.6 12.7 %copy-start.15 = (f32[576]{0:T(1024)S(1)}, f32[576]{0:T(1024)}, u32[]{:S(2)}) copy-start(f32[576]{0:T(1024)} %copy-done.14) | copy-start | bytes 6916
  218.7 298.5 %all-to-all-start = ((bf16[128,2,36,2,512]{4,3,2,1,0:T(2,128)(2,1)}), bf16[128,2,36,2,512]{4,3,2,1,0:T(2,128)(2,1)}, u32[]{:S(2)}, u32[]{:S(2)}) async-start(bf16[128,2,36,2,512]{4,3,2,1,0:T(2,128)(2,1)} %bitcast.185), calls=%async_computation | async-start | bytes 37748736 | tf_op jit(solution)/shard_map/all_to_all | solution.py:73
  239.3 3.2 copy-start.20
  242.5 2.6 copy-start.16
  586.7 7.8 %copy-start.2 = (f32[3456,4,128]{2,1,0:T(4,128)S(1)}, f32[3456,4,128]{2,1,0:T(4,128)}, u32[]{:S(2)}) copy-start(f32[3456,4,128]{2,1,0:T(4,128)} %reshape.458) | copy-start | bytes 21233668
  594.5 5.1 copy-start.4
  611.0 22.1 %copy-start.7 = (bf16[576,4,128]{2,0,1:T(8,128)(2,1)S(1)}, bf16[576,4,128]{2,0,1:T(8,128)(2,1)}, u32[]{:S(2)}) copy-start(bf16[576,4,128]{2,0,1:T(8,128)(2,1)} %fusion.41) | copy-start | bytes 1769476
  637.7 3.2 copy-start.3
  637.7 3.2 copy-start.8
  689.2 3.2 copy-start.10
  692.4 1.6 copy-start.9
  694.0 1.6 copy-start.11
  694.0 2.4 copy-start.21
  696.4 3.9 copy-start.1
where the time goes:
time: 708 us; the launch traced here: 701 us
  waiting for transfers between devices  269 us (38%)
  local copies, waits for them, and re-layouts  144 us (20%)
  other arithmetic  110 us (16%)
  blocking collectives  110 us (16%)
  matrix products  39.6 us (6%)
  starting transfers between devices  26.1 us (4%)
    all_to_all x1, waiting for transfers between devices, on_device(): lax.all_to_all(outgoing, ('roll', 'frame'), split_axis=0, concat_axis=0,...  269 us
    all_gather x1, blocking collectives, on_device(): lax.all_gather(owners, ('roll', 'frame'), axis=0, tiled=True)  65.3 us
    concatenate x1, other arithmetic, on_device(): jnp.concatenate([planar_mapped_result[:, 2], memory_value], axis=0)  45.2 us
    all_gather x1, blocking collectives, on_device(): lax.all_gather(slots, ('roll', 'frame'), axis=0, tiled=True)  44.6 us
    gather x1, local copies, waits for them, and re-layouts, on_device(): outgoing = cached_past_pairs[send_slot]  41.3 us
    reshape x1, local copies, waits for them, and re-layouts, on_device(): incoming.reshape(roll_count, frame_count, CAP, piece_rows, 2, head_width)  35.5 us
    concatenate x1, other arithmetic, on_device(): key_rows = jnp.concatenate([space_key, memory_key], axis=0)  22.1 us
    convert_element_type x2, local copies, waits for them, and re-layouts, unit_rows(): return normed(values.astype(jnp.float32)).astype(jnp.bfloat16)  16.7 us
  transfers between devices with their start and end apart: 3, of which 1 were waited for; matrix products, arithmetic and copies ran while one was open for 8% of the time, Pallas kernels for 0%

commit v1 on v0

v1 whole, which is shorter than its diff:
```python
import functools

import jax
import jax.numpy as jnp
from jax import lax
from jax.experimental import pallas as pl
from jax.experimental.pallas import tpu as pltpu
from jax.sharding import Mesh
from jax.sharding import PartitionSpec as P

G = 4
C = 128
HW = G * C
TOPM = 6
EPSILON = 1e-06
BF = jnp.bfloat16
F32 = jnp.float32
PAD = 16
VMEM_LIMIT = 50 * 1024 * 1024


def params(**more):
    return pltpu.CompilerParams(vmem_limit_bytes=VMEM_LIMIT, **more)


def inverse_rms(values):
    return lax.rsqrt(jnp.mean(values * values, axis=-1, keepdims=True) + EPSILON)


def dot(a, b):
    return jnp.dot(a, b, preferred_element_type=F32)


def dot_t(a, b):
    return lax.dot_general(a, b, (((1,), (1,)), ((), ())), preferred_element_type=F32)


def split_store_kernel(rows_ref, out_ref):
    for h in range(G):
        key = rows_ref[:, h * C : (h + 1) * C].astype(F32)
        out_ref[h, :, :C] = (key * inverse_rms(key)).astype(BF)
        out_ref[h, :, C:] = rows_ref[:, HW + h * C : HW + (h + 1) * C]


def split_store(rows):
    n = rows.shape[0]
    return pl.pallas_call(
        split_store_kernel,
        out_shape=jax.ShapeDtypeStruct((G, n, 2 * C), BF),
        compiler_params=params(),
        name="split_store",
        cost_estimate=pl.CostEstimate(
            flops=8 * n * HW, bytes_accessed=8 * n * HW, transcendentals=n * G
        ),
    )(rows)


def join_pieces_kernel(piece, in_ref, out_ref, wide_ref, joined_ref):
    pieces = in_ref.shape[0]
    wide_ref[...] = in_ref[...].astype(F32)
    for m in range(out_ref.shape[0]):
        for i in range(pieces):
            joined_ref[m, i * piece : (i + 1) * piece, :] = wide_ref[
                i, m * piece : (m + 1) * piece, :
            ]
    out_ref[...] = joined_ref[...].astype(BF)


def join_pieces(parts, frames):
    pieces, rows, width = parts.shape
    piece = rows // frames
    return pl.pallas_call(
        functools.partial(join_pieces_kernel, piece),
        out_shape=jax.ShapeDtypeStruct((frames, pieces * piece, width), BF),
        scratch_shapes=[
            pltpu.VMEM((pieces, rows, width), F32),
            pltpu.VMEM((frames, pieces * piece, width), F32),
        ],
        compiler_params=params(),
        name="join_pieces",
        cost_estimate=pl.CostEstimate(
            flops=0, bytes_accessed=4 * pieces * rows * width, transcendentals=0
        ),
    )(parts)


def modulate_kernel(act_ref, affine_ref, weight_ref, factor_ref, tail_ref, hidden_ref, query_ref):
    step = pl.program_id(0)
    rows = act_ref.shape[0]
    patches = query_ref.shape[1] - PAD
    act = act_ref[...].astype(F32)
    hidden = act * inverse_rms(act) * (1.0 + affine_ref[0:1, :]) + affine_ref[1:2, :]
    hidden = hidden.astype(BF)
    hidden_ref[...] = hidden
    mapped = dot(hidden, weight_ref[...]).astype(BF).astype(F32)
    for h in range(G):
        one = mapped[:, h * C : (h + 1) * C]
        query_ref[h, pl.ds(pl.multiple_of(step * rows, 16), rows), :] = (
            one * inverse_rms(one) * factor_ref[0, h]
        ).astype(BF)

    @pl.when(step == 0)
    def _():
        for h in range(G):
            query_ref[h, patches:, :] = tail_ref[...]


def modulate(act, affine, weight, factor, tail):
    patches, depth = act.shape
    steps = 2
    rows = patches // steps
    return pl.pallas_call(
        modulate_kernel,
        grid=(steps,),
        in_specs=[
            pl.BlockSpec((rows, depth), lambda i: (i, 0)),
            pl.BlockSpec((2, depth), lambda i: (0, 0)),
            pl.BlockSpec((depth, HW), lambda i: (0, 0)),
            pl.BlockSpec(memory_space=pltpu.SMEM),
            pl.BlockSpec((PAD, C), lambda i: (0, 0)),
        ],
        out_specs=[
            pl.BlockSpec((rows, depth), lambda i: (i, 0)),
            pl.BlockSpec((G, patches + PAD, C), lambda i: (0, 0, 0)),
        ],
        out_shape=[
            jax.ShapeDtypeStruct((patches, depth), BF),
            jax.ShapeDtypeStruct((G, patches + PAD, C), BF),
        ],
        compiler_params=params(),
        name="modulate",
        cost_estimate=pl.CostEstimate(
            flops=2 * patches * depth * HW,
            bytes_accessed=4 * patches * depth + 2 * depth * HW + 2 * patches * HW,
            transcendentals=patches,
        ),
    )(act, affine, weight, factor, tail)


def temporal_entry_kernel(quarters, hidden_ref, weight_ref, factor_ref, out_ref):
    part = pl.program_id(0)
    rows = hidden_ref.shape[0] // quarters
    mapped = dot(hidden_ref[...], weight_ref[...]).astype(BF).astype(F32)
    for h in range(G):
        one = mapped[:, h * C : (h + 1) * C]
        scale = jnp.where(part < 2, inverse_rms(one), 1.0)
        factor = jnp.where(part == 0, factor_ref[1, h], 1.0)
        done = (one * scale * factor).astype(BF)
        for z in range(quarters):
            out_ref[z, h, 0] = done[z * rows : (z + 1) * rows, :]


def temporal_entry(hidden, weight, factor, quarters):
    patches, depth = hidden.shape
    rows = patches // quarters
    return pl.pallas_call(
        functools.partial(temporal_entry_kernel, quarters),
        grid=(3,),
        in_specs=[
            pl.BlockSpec((patches, depth), lambda i: (0, 0)),
            pl.BlockSpec((depth, HW), lambda i: (0, 3 + i)),
            pl.BlockSpec(memory_space=pltpu.SMEM),
        ],
        out_specs=pl.BlockSpec((quarters, G, 1, rows, C), lambda i: (0, 0, i, 0, 0)),
        out_shape=jax.ShapeDtypeStruct((quarters, G, 3, rows, C), BF),
        compiler_params=params(),
        name="temporal_entry",
        cost_estimate=pl.CostEstimate(
            flops=6 * patches * depth * HW,
            bytes_accessed=2 * patches * depth + 6 * depth * HW + 6 * patches * HW,
            transcendentals=patches,
        ),
    )(hidden, weight, factor)


def temporal_attend_kernel(length_ref, in_ref, out_ref):
    frames, _, rows, _ = in_ref.shape
    group = 16
    size = frames * group
    length = length_ref[0]
    row = lax.broadcasted_iota(jnp.int32, (size, size), 0)
    column = lax.broadcasted_iota(jnp.int32, (size, size), 1)
    target, source = row // group, column // group
    keep = (row % group == column % group) & (source <= target) & (source > target - length)
    for g in range(rows // group):
        at = slice(g * group, (g + 1) * group)
        query = in_ref[:, 0, at, :].reshape(size, C)
        key = in_ref[:, 1, at, :].reshape(size, C)
        value = in_ref[:, 2, at, :].reshape(size, C)
        weights = jnp.where(keep, jnp.exp(dot_t(query, key)), 0.0)
        shares = weights / jnp.sum(weights, axis=-1, keepdims=True)
        result = dot(shares.astype(BF), value).astype(BF)
        out_ref[:, at, :] = result.reshape(frames, group, C)


def temporal_attend(length, parts):
    frames, _, rows, _ = parts.shape
    return pl.pallas_call(
        temporal_attend_kernel,
        in_specs=[
            pl.BlockSpec(memory_space=pltpu.SMEM),
            pl.BlockSpec(memory_space=pltpu.VMEM),
        ],
        out_shape=jax.ShapeDtypeStruct((frames, rows, C), BF),
        compiler_params=params(),
        name="temporal_attend",
        cost_estimate=pl.CostEstimate(
            flops=4 * frames * rows * 256 * C,
            bytes_accessed=8 * frames * rows * C,
            transcendentals=frames * rows * 256,
        ),
    )(length, parts)


def own_attend_kernel(hidden_ref, key_weight_ref, value_weight_ref, query_ref, out_ref):
    heads = query_ref.shape[0]
    patches = hidden_ref.shape[0]
    hidden = hidden_ref[...]
    keys = dot(hidden, key_weight_ref[...]).astype(BF).astype(F32)
    values = dot(hidden, value_weight_ref[...]).astype(BF)
    ones = jnp.ones((patches, C), BF)
    for h in range(heads):
        key = keys[:, h * C : (h + 1) * C]
        key = (key * inverse_rms(key)).astype(BF)
        both = jnp.concatenate([values[:, h * C : (h + 1) * C], ones], axis=1)
        weights = jnp.exp(dot_t(query_ref[h, :patches, :], key)).astype(BF)
        out_ref[h] = dot(weights, both)


def own_attend(hidden, weight, query):
    patches, depth = hidden.shape
    heads = 2
    wide = heads * C
    per = HW // wide
    return pl.pallas_call(
        own_attend_kernel,
        grid=(G // heads,),
        in_specs=[
            pl.BlockSpec((patches, depth), lambda i: (0, 0)),
            pl.BlockSpec((depth, wide), lambda i: (0, per + i)),
            pl.BlockSpec((depth, wide), lambda i: (0, 2 * per + i)),
            pl.BlockSpec((heads, patches + PAD, C), lambda i: (i, 0, 0)),
        ],
        out_specs=pl.BlockSpec((heads, patches, 2 * C), lambda i: (i, 0, 0)),
        out_shape=jax.ShapeDtypeStruct((G, patches, 2 * C), F32),
        compiler_params=params(),
        name="own_attend",
        cost_estimate=pl.CostEstimate(
            flops=4 * patches * depth * HW + 6 * patches * patches * HW,
            bytes_accessed=2 * patches * depth + 4 * depth * HW + 10 * patches * HW,
            transcendentals=G * patches * patches,
        ),
    )(hidden, weight, weight, query)


def memory_attend_kernel(index_ref, query_ref, *refs):
    stores, out_ref = refs[:TOPM], refs[TOPM]
    patches = query_ref.shape[1] - PAD
    keys = jnp.concatenate([ref[0, :, :C] for ref in stores], axis=0)
    values = jnp.concatenate([ref[0, :, C:] for ref in stores], axis=0)
    both = jnp.concatenate([values, jnp.ones(values.shape, BF)], axis=1)
    row = lax.broadcasted_iota(jnp.int32, (C, C), 0)
    column = lax.broadcasted_iota(jnp.int32, (C, C), 1)
    rows = []
    start = 0
    while start < patches:
        size = min(C, patches - start)
        weights = jnp.exp(dot_t(query_ref[0, start : start + size, :], keys)).astype(BF)
        result = dot(weights, both)
        out_ref[0, start : start + size, :] = result[:, :C].astype(BF)
        diagonal = jnp.where(row[:size] == column[:size], result[:, C:], 0.0)
        rows.append(jnp.sum(diagonal, axis=0, keepdims=True))
        start += size
    rows.append(jnp.zeros((8 - len(rows), C), F32))
    total = jnp.concatenate(rows, axis=0)
    high = total.astype(BF).astype(F32)
    out_ref[0, patches:, :] = jnp.concatenate([high, total - high], axis=0).astype(BF)


def memory_attend(index, query, store):
    frames, rows, _ = query.shape
    patches = rows - PAD
    quarter = store.shape[1]

    def place(j):
        return lambda i, index_ref: (index_ref[i, j], 0, 0)

    return pl.pallas_call(
        memory_attend_kernel,
        grid_spec=pltpu.PrefetchScalarGridSpec(
            num_scalar_prefetch=1,
            grid=(frames,),
            in_specs=[pl.BlockSpec((1, rows, C), lambda i, index_ref: (i, 0, 0))]
            + [pl.BlockSpec((1, quarter, 2 * C), place(j)) for j in range(TOPM)],
            out_specs=pl.BlockSpec((1, rows, C), lambda i, index_ref: (i, 0, 0)),
        ),
        out_shape=jax.ShapeDtypeStruct(query.shape, BF),
        compiler_params=params(),
        name="memory_attend",
        cost_estimate=pl.CostEstimate(
            flops=8 * frames * patches * TOPM * quarter * C,
            bytes_accessed=4 * query.size + 4 * frames * TOPM * quarter * C,
            transcendentals=frames * patches * TOPM * quarter,
        ),
    )(index, query, *([store] * TOPM))


def add_partials_kernel(*refs):
    ins, out_ref = refs[:-1], refs[-1]
    patches = out_ref.shape[1] - PAD
    total = ins[0][0, :patches, :].astype(F32)
    tail = ins[0][0, patches:, :].astype(F32)
    for ref in ins[1:]:
        total += ref[0, :patches, :].astype(F32)
        tail += ref[0, patches:, :].astype(F32)
    out_ref[0, :patches, :] = total.astype(BF)
    denominator = tail[:8] + tail[8:]
    high = denominator.astype(BF).astype(F32)
    out_ref[0, patches:, :] = jnp.concatenate([high, denominator - high], axis=0).astype(BF)


def add_partials(parts):
    frames, rows, _ = parts[0].shape
    spec = pl.BlockSpec((1, rows, C), lambda i: (i, 0, 0))
    return pl.pallas_call(
        add_partials_kernel,
        grid=(frames,),
        in_specs=[spec] * len(parts),
        out_specs=spec,
        out_shape=jax.ShapeDtypeStruct(parts[0].shape, BF),
        compiler_params=params(),
        name="add_partials",
        cost_estimate=pl.CostEstimate(
            flops=4 * parts[0].size, bytes_accessed=10 * parts[0].size, transcendentals=0
        ),
    )(*parts)


def leave_kernel(own_ref, memory_ref, time_ref, weight_ref, out_ref, combined_ref):
    patches = own_ref.shape[1]
    quarters = time_ref.shape[0] // G
    rows = time_ref.shape[1]

    @pl.when(pl.program_id(0) == 0)
    def _():
        row = lax.broadcasted_iota(jnp.int32, (C, C), 0)
        column = lax.broadcasted_iota(jnp.int32, (C, C), 1)
        for h in range(G):
            tail = memory_ref[h, patches:, :].astype(F32)
            denominators = tail[:8] + tail[8:]
            for j in range(-(-patches // C)):
                start = j * C
                size = min(C, patches - start)
                at = slice(start, start + size)
                line = jnp.broadcast_to(denominators[j : j + 1, :], (size, C))
                memory_sum = jnp.sum(
                    jnp.where(row[:size] == column[:size], line, 0.0), axis=1, keepdims=True
                )
                top = own_ref[h, at, :C] + memory_ref[h, at, :].astype(F32)
                combined_ref[at, h * C : (h + 1) * C] = (
                    top / (own_ref[h, at, C:] + memory_sum)
                ).astype(BF)
            for z in range(quarters):
                combined_ref[z * rows : (z + 1) * rows, HW + h * C : HW + (h + 1) * C] = time_ref[
                    z * G + h
                ]

    out_ref[...] = dot(combined_ref[...], weight_ref[...]).astype(BF)


def leave(own, memory, time, weight):
    patches = own.shape[1]
    depth, width = weight.shape
    step = 512
    return pl.pallas_call(
        leave_kernel,
        grid=(width // step,),
        in_specs=[
            pl.BlockSpec(own.shape, lambda i: (0, 0, 0)),
            pl.BlockSpec(memory.shape, lambda i: (0, 0, 0)),
            pl.BlockSpec(time.shape, lambda i: (0, 0, 0)),
            pl.BlockSpec((depth, step), lambda i: (0, i)),
        ],
        out_specs=pl.BlockSpec((patches, step), lambda i: (0, i)),
        out_shape=jax.ShapeDtypeStruct((patches, width), BF),
        scratch_shapes=[pltpu.VMEM((patches, depth), BF)],
        compiler_params=params(),
        name="leave",
        cost_estimate=pl.CostEstimate(
            flops=2 * patches * depth * width,
            bytes_accessed=2 * depth * width + 2 * patches * width + 6 * patches * depth,
            transcendentals=0,
        ),
    )(own, memory, time, weight)


def on_device(
    patch_activation_tensor,
    conditioning_affine,
    entry_projection_matrix,
    exit_projection_matrix,
    softmax_sharpness,
    cached_past_pairs,
    recalled_picture_holder,
    recalled_picture_position,
    lookback_lengths,
):
    rings = lax.axis_size("z")
    patches, depth = patch_activation_tensor.shape[2:]
    held, piece = cached_past_pairs.shape[:2]

    with jax.named_scope("store"):
        store = split_store(cached_past_pairs.reshape(held * piece, 2 * HW))
        store = lax.all_to_all(store, "x", split_axis=0, concat_axis=0, tiled=True)
        store = join_pieces(store, held)
        store = lax.all_gather(store, ("y", "c"), axis=0, tiled=True)

    with jax.named_scope("queries"):
        factor = softmax_sharpness / C
        index = recalled_picture_holder.reshape(TOPM) * held + recalled_picture_position.reshape(
            TOPM
        )
        tail = jnp.zeros((PAD, C), BF).at[0, :TOPM].set(index.astype(BF))
        hidden, query = modulate(
            patch_activation_tensor.reshape(patches, depth),
            conditioning_affine.reshape(2, depth),
            entry_projection_matrix,
            factor,
            tail,
        )
        group = lax.all_to_all(query, "x", split_axis=0, concat_axis=0, tiled=True)
        groups = [group]
        for step in range(1, rings):
            groups.append(
                lax.ppermute(group, "z", [(s, (s + step) % rings) for s in range(rings)])
            )

    with jax.named_scope("temporal"):
        parts = temporal_entry(hidden, entry_projection_matrix, factor, rings)
        parts = parts.reshape((rings * G,) + parts.shape[2:])
        parts = lax.all_to_all(parts, ("z", "x"), split_axis=0, concat_axis=0, tiled=True)

    with jax.named_scope("own"):
        own = own_attend(hidden, entry_projection_matrix, query)

    with jax.named_scope("temporal"):
        time = temporal_attend(lookback_lengths, parts)
        time = lax.all_to_all(time, ("z", "x"), split_axis=0, concat_axis=0, tiled=True)

    with jax.named_scope("memory"):
        partials = []
        for step, group in enumerate(groups):
            chosen = group[:, patches, :TOPM].astype(jnp.int32)
            partial = memory_attend(chosen, group, store)
            if step:
                partial = lax.ppermute(
                    partial, "z", [(s, (s - step) % rings) for s in range(rings)]
                )
            partials.append(partial)
        memory = add_partials(partials)
        memory = lax.all_to_all(memory, "x", split_axis=0, concat_axis=0, tiled=True)

    with jax.named_scope("exit"):
        attended = leave(own, memory, time, exit_projection_matrix)
    return attended.reshape(1, 1, patches, depth)


def solution(mesh):
    apart = Mesh(mesh.devices.reshape(4, 2, 4, 4), ("y", "c", "z", "x"))
    roll, frame = ("y", "c"), ("z", "x")
    return jax.shard_map(
        on_device,
        mesh=apart,
        in_specs=(
            P(roll, frame, None, None),
            P(roll, frame, None, None),
            P(),
            P(),
            P(),
            P(roll, frame, None, None),
            P(roll, frame, None, None),
            P(roll, frame, None),
            P(roll),
        ),
        out_specs=P(roll, frame, None, None),
        check_vma=False,
    )
```

time: 708 us -> 164 us (0.23)
  the two profiles are of different devices: /device:TPU:106 before, /device:TPU:0 now
where the time goes in v1:
time: 164 us; the launch traced here: 163 us
  Pallas kernels  59.2 us (36%)
  waiting for transfers between devices  33.9 us (21%)
  blocking collectives  25.9 us (16%)
  starting transfers between devices  24.7 us (15%)
  between operations  14.2 us (9%)
  local copies, waits for them, and re-layouts  5.35 us (3%)
    ppermute x3, waiting for transfers between devices, on_device(): lax.ppermute(group, 'z', [(s, (s + step) % rings) for s in range(rings)])  29.2 us
    pallas_call x4, Pallas kernels, memory_attend(): pl.pallas_call(memory_attend_kernel, grid_spec=pltpu.PrefetchScalarGridSp...  25.9 us
    all_to_all x1, blocking collectives, on_device(): store = lax.all_to_all(store, 'x', split_axis=0, concat_axis=0, tiled=True)  14.4 us
    all_to_all x1, blocking collectives, on_device(): group = lax.all_to_all(query, 'x', split_axis=0, concat_axis=0, tiled=True)  11.5 us
    pallas_call x1, Pallas kernels, temporal_entry(): pl.pallas_call(functools.partial(temporal_entry_kernel, quarters), grid=(...  8.42 us
    pallas_call x1, Pallas kernels, own_attend(): pl.pallas_call(own_attend_kernel, grid=(G // heads,), in_specs=[pl.BlockS...  7.12 us
    ppermute x3, starting transfers between devices, on_device(): lax.ppermute(group, 'z', [(s, (s + step) % rings) for s in range(rings)])  6.96 us
    pallas_call x1, Pallas kernels, leave(): pl.pallas_call(leave_kernel, grid=(width // step,), in_specs=[pl.BlockSpe...  6.42 us
  transfers between devices with their start and end apart: 10, of which 4 were waited for; matrix products, arithmetic and copies ran while one was open for 0% of the time, Pallas kernels for 32%

profile of v1, /device:TPU:0, one launch (start us, length us, event | category | flops | bytes accessed | tf_op | source)
XLA Modules:
  0.0 163.3 jit_solution(1525505285500824411)
XLA Ops:
  6.5 0.0 all-gather.2.cloned.1.call-start
  6.5 1.1 copy.10
  7.7 0.0 copy-start.9
  7.7 0.0 copy-start.10
  7.7 0.0 copy-start.8
  7.7 0.0 copy-start.7
  7.7 0.3 split_store.1
  8.0 14.4 %all_to_all.25.in_ref = bf16[4,288,256]{2,1,0:T(8,128)(2,1)S(1)} all-to-all(bf16[4,288,256]{2,1,0:T(8,128)(2,1)S(1)} %split_store.1), channel_id=1, replica_groups=mesh['y'=4,'c'=2,'z'=4,'x'=4] {'x'}, dimensions={0} | all-to-all | bytes 1179648 | tf_op jit(solution)/shard_map/store/all_to_all | solution.py:414
  22.4 1.0 join_pieces.1
  23.4 0.0 all-gather.2.cloned.1.call-update
  23.4 0.0 copy-done.9
  23.4 0.0 copy-done.10
  23.4 0.0 copy-done.8
  23.5 0.0 copy-done.7
  23.5 4.5 %modulate.1 = (bf16[576,2048]{1,0:T(8,128)(2,1)S(1)}, bf16[4,592,128]{2,1,0:T(8,128)(2,1)S(1)}) custom-call(bf16[576,2048]{1,0:T(8,128)(2,1)} %bitcast.23, f32[2,2048]{1,0:T(2,128)S(1)} %bitcast.18, bf16[2048,3072]{1,0:T(8,128)(2,1)} %weight_ref.4, f32[2,4]{1,0:T(2,128)S(1)} %broadcast_multiply_fusion.factor_ref, bf16[16,128]{1,0:T(8,128)(2,1)S(1)} %scatter.4.tail_ref), custom_call_target="tpu_custom_call" | custom-call | flops 1207959552 | bytes 7405568 | tf_op jit(solution)/shard_map/queries/modulate/pallas_call | solution.py:112
  27.9 0.0 copy-start
  28.0 1.4 copy-done
  29.4 0.0 copy-start.1
  29.4 11.5 %all_to_all.26.query_ref = bf16[4,592,128]{2,1,0:T(8,128)(2,1)S(1)} all-to-all(bf16[4,592,128]{2,1,0:T(8,128)(2,1)S(1)} %get-tuple-element.20.query_ref), channel_id=1, replica_groups=mesh['y'=4,'c'=2,'z'=4,'x'=4] {'x'}, dimensions={0} | all-to-all | bytes 1212416 | tf_op jit(solution)/shard_map/queries/all_to_all | solution.py:431
  40.9 3.9 %collective-permute-start.2 = (bf16[4,592,128]{2,1,0:T(8,128)(2,1)S(1)}, bf16[4,592,128]{2,1,0:T(8,128)(2,1)S(1)}, u32[]{:S(2)}, u32[]{:S(2)}) collective-permute-start(bf16[4,592,128]{2,1,0:T(8,128)(2,1)S(1)} %all_to_all.26.query_ref), channel_id=1, source_target_pairs={{0,8},{4,12},{8,0},{12,4},{1,9},{5,13},{9,1},{13,5},{2,10},{6,14},... | collective-permute-start | bytes 1818632 | tf_op jit(solution)/shard_map/queries/ppermute | solution.py:435
  44.8 8.4 %temporal_entry.1 = bf16[4,4,3,144,128]{4,3,2,1,0:T(8,128)(2,1)} custom-call(bf16[576,2048]{1,0:T(8,128)(2,1)} %copy-done, bf16[2048,3072]{1,0:T(8,128)(2,1)} %weight_ref.4, f32[2,4]{1,0:T(2,128)S(1)} %broadcast_multiply_fusion.factor_ref), custom_call_target="tpu_custom_call" | custom-call | flops 3623878656 | bytes 10420224 | tf_op jit(solution)/shard_map/temporal/temporal_entry/pallas_call | solution.py:156
  53.2 0.0 copy-done.1
  53.2 3.7 %all-to-all-start.3 = ((bf16[16,3,144,128]{3,2,1,0:T(8,128)(2,1)}), bf16[16,3,144,128]{3,2,1,0:T(8,128)(2,1)S(1)}, u32[]{:S(2)}, u32[]{:S(2)}) async-start(bf16[16,3,144,128]{3,2,1,0:T(8,128)(2,1)} %bitcast.8), calls=%async_computation.3 | async-start | bytes 3538944 | tf_op jit(solution)/shard_map/temporal/all_to_all | solution.py:441
  56.9 3.1 %collective-permute-start.4 = (bf16[4,592,128]{2,1,0:T(8,128)(2,1)S(1)}, bf16[4,592,128]{2,1,0:T(8,128)(2,1)S(1)}, u32[]{:S(2)}, u32[]{:S(2)}) collective-permute-start(bf16[4,592,128]{2,1,0:T(8,128)(2,1)S(1)} %all_to_all.26.query_ref), channel_id=1, source_target_pairs={{0,12},{4,0},{8,4},{12,8},{1,13},{5,1},{9,5},{13,9},{2,14},{6,2},{... | collective-permute-start | bytes 1818632 | tf_op jit(solution)/shard_map/queries/ppermute | solution.py:435
  60.0 0.0 collective-permute-start
  60.0 0.0 collective-permute-done.2.query_ref
  60.0 28.8 %collective-permute-done.4.query_ref = bf16[4,592,128]{2,1,0:T(8,128)(2,1)S(1)} collective-permute-done((bf16[4,592,128]{2,1,0:T(8,128)(2,1)S(1)}, bf16[4,592,128]{2,1,0:T(8,128)(2,1)S(1)}, u32[]{:S(2)}, u32[]{:S(2)}) %collective-permute-start.4) | collective-permute-done | bytes 606240 | tf_op jit(solution)/shard_map/queries/ppermute | solution.py:435
  88.8 0.0 copy-start.5
  88.8 0.9 copy-done.5
  89.7 0.4 collective-permute-done.query_ref
  90.1 0.0 copy-start.3
  90.1 0.8 copy-done.3
  90.9 0.0 all-gather.2.cloned.1.call-done.refs_0_.refs_1_.refs_2_.refs_3_.refs_4_.refs_5_
  90.9 0.0 copy-start.6
  90.9 6.6 %memory_attend.6 = bf16[4,592,128]{2,1,0:T(8,128)(2,1)} custom-call(s32[4,6]{1,0:T(4,128)S(1)} %bitcast.21, bf16[4,592,128]{2,1,0:T(8,128)(2,1)S(1)} %collective-permute-done.2.query_ref, bf16[64,144,256]{2,1,0:T(8,128)(2,1)} %all-gather.2.cloned.1.call-done.refs_0_.refs_1_.refs_2_.refs_3_.refs_4_.refs_5_, ...), custom_call_target="tpu_custom_call" | custom-call | flops 2038431744 | bytes 2981888 | tf_op jit(solution)/shard_map/memory/memory_attend/pallas_call | solution.py:288
  97.6 2.1 %collective-permute-start.3 = (bf16[4,592,128]{2,1,0:T(8,128)(2,1)}, bf16[4,592,128]{2,1,0:T(8,128)(2,1)}, u32[]{:S(2)}, u32[]{:S(2)}) collective-permute-start(bf16[4,592,128]{2,1,0:T(8,128)(2,1)} %memory_attend.6), channel_id=1, source_target_pairs={{0,8},{4,12},{8,0},{12,4},{1,9},{5,13},{9,1},{13,5},{2,10},{6,14},... | collective-permute-start | bytes 1818632 | tf_op jit(solution)/shard_map/memory/ppermute | solution.py:456
  99.7 0.0 copy-done.6
  99.7 0.0 copy-start.4
  99.7 6.6 %memory_attend.7 = bf16[4,592,128]{2,1,0:T(8,128)(2,1)} custom-call(s32[4,6]{1,0:T(4,128)S(1)} %bitcast.20, bf16[4,592,128]{2,1,0:T(8,128)(2,1)S(1)} %copy-done.6, bf16[64,144,256]{2,1,0:T(8,128)(2,1)} %all-gather.2.cloned.1.call-done.refs_0_.refs_1_.refs_2_.refs_3_.refs_4_.refs_5_, ...), custom_call_target="tpu_custom_call" | custom-call | flops 2038431744 | bytes 2981888 | tf_op jit(solution)/shard_map/memory/memory_attend/pallas_call | solution.py:288
  106.3 0.9 collective-permute-start.5
  107.2 0.0 copy-done.4
  107.2 6.6 %memory_attend.5 = bf16[4,592,128]{2,1,0:T(8,128)(2,1)} custom-call(s32[4,6]{1,0:T(4,128)S(1)} %bitcast.19, bf16[4,592,128]{2,1,0:T(8,128)(2,1)S(1)} %copy-done.4, bf16[64,144,256]{2,1,0:T(8,128)(2,1)} %all-gather.2.cloned.1.call-done.refs_0_.refs_1_.refs_2_.refs_3_.refs_4_.refs_5_, ...), custom_call_target="tpu_custom_call" | custom-call | flops 2038431744 | bytes 2981888 | tf_op jit(solution)/shard_map/memory/memory_attend/pallas_call | solution.py:288
  113.9 2.3 %collective-permute-start.1 = (bf16[4,592,128]{2,1,0:T(8,128)(2,1)}, bf16[4,592,128]{2,1,0:T(8,128)(2,1)}, u32[]{:S(2)}, u32[]{:S(2)}) collective-permute-start(bf16[4,592,128]{2,1,0:T(8,128)(2,1)} %memory_attend.5), channel_id=1, source_target_pairs={{0,12},{4,0},{8,4},{12,8},{1,13},{5,1},{9,5},{13,9},{2,14},{6,2},{... | collective-permute-start | bytes 1818632 | tf_op jit(solution)/shard_map/memory/ppermute | solution.py:456
  116.9 0.0 all-to-all-done.3.in_ref
  116.9 2.0 %temporal_attend.1 = bf16[16,144,128]{2,1,0:T(8,128)(2,1)} custom-call(s32[1]{0:T(128)S(6)} %copy.11.length_ref, bf16[16,3,144,128]{3,2,1,0:T(8,128)(2,1)S(1)} %all-to-all-done.3.in_ref), custom_call_target="tpu_custom_call" | custom-call | flops 301989888 | bytes 2359296 | tf_op jit(solution)/shard_map/temporal/temporal_attend/pallas_call | solution.py:198
  118.9 4.4 %all-to-all-start.4 = ((bf16[16,144,128]{2,1,0:T(8,128)(2,1)}), bf16[16,144,128]{2,1,0:T(8,128)(2,1)S(1)}, u32[]{:S(2)}, u32[]{:S(2)}) async-start(bf16[16,144,128]{2,1,0:T(8,128)(2,1)} %temporal_attend.1), calls=%async_computation.4 | async-start | bytes 1179648 | tf_op jit(solution)/shard_map/temporal/all_to_all | solution.py:448
  123.3 6.0 %memory_attend.4.refs_0_ = bf16[4,592,128]{2,1,0:T(8,128)(2,1)S(1)} custom-call(s32[4,6]{1,0:T(4,128)S(1)} %bitcast.22, bf16[4,592,128]{2,1,0:T(8,128)(2,1)S(1)} %all_to_all.26.query_ref, bf16[64,144,256]{2,1,0:T(8,128)(2,1)} %all-gather.2.cloned.1.call-done.refs_0_.refs_1_.refs_2_.refs_3_.refs_4_.refs_5_, ...), custom_call_target="tpu_custom_call" | custom-call | flops 2038431744 | bytes 2981888 | tf_op jit(solution)/shard_map/memory/memory_attend/pallas_call | solution.py:288
  129.3 0.0 collective-permute-done.3.refs_2_
  129.3 0.0 collective-permute-done.5.refs_3_
  129.3 4.3 %collective-permute-done.1.refs_1_ = bf16[4,592,128]{2,1,0:T(8,128)(2,1)} collective-permute-done((bf16[4,592,128]{2,1,0:T(8,128)(2,1)}, bf16[4,592,128]{2,1,0:T(8,128)(2,1)}, u32[]{:S(2)}, u32[]{:S(2)}) %collective-permute-start.1) | collective-permute-done | bytes 606240 | tf_op jit(solution)/shard_map/memory/ppermute | solution.py:456
  133.6 3.6 %add_partials.1 = bf16[4,592,128]{2,1,0:T(8,128)(2,1)} custom-call(bf16[4,592,128]{2,1,0:T(8,128)(2,1)S(1)} %memory_attend.4.refs_0_, bf16[4,592,128]{2,1,0:T(8,128)(2,1)} %collective-permute-done.1.refs_1_, bf16[4,592,128]{2,1,0:T(8,128)(2,1)} %collective-permute-done.3.refs_2_, bf16[4,592,128]{2,1,0:T(8,128)(2,1)} %collective-permute-done.5.refs_3_), custom_call_target="tpu_custom_call" | custom-call | flops 1212416 | bytes 3031040 | tf_op jit(solution)/shard_map/memory/add_partials/pallas_call | solution.py:325
  137.2 0.0 all-to-all-done.4.time_ref
  137.2 4.3 %all-to-all-start.2 = ((bf16[4,592,128]{2,1,0:T(8,128)(2,1)}), bf16[4,592,128]{2,1,0:T(8,128)(2,1)S(1)}, u32[]{:S(2)}, u32[]{:S(2)}) async-start(bf16[4,592,128]{2,1,0:T(8,128)(2,1)} %add_partials.1), calls=%async_computation.2 | async-start | bytes 1212416 | tf_op jit(solution)/shard_map/memory/all_to_all | solution.py:461
  141.5 0.0 copy-start.2
  141.5 1.1 copy-done.2
  142.6 7.1 %own_attend.1.own_ref = f32[4,576,256]{2,1,0:T(8,128)S(1)} custom-call(bf16[576,2048]{1,0:T(8,128)(2,1)} %copy-done, bf16[2048,3072]{1,0:T(8,128)(2,1)} %weight_ref.4, bf16[2048,3072]{1,0:T(8,128)(2,1)} %weight_ref.4, bf16[4,592,128]{2,1,0:T(8,128)(2,1)S(1)} %copy-done.2), custom_call_target="tpu_custom_call" | custom-call | flops 3435134976 | bytes 9502720 | tf_op jit(solution)/shard_map/own/own_attend/pallas_call | solution.py:235
  149.7 0.3 all-to-all-done.2.memory_ref
  150.0 6.4 %leave.1 = bf16[576,2048]{1,0:T(8,128)(2,1)} custom-call(f32[4,576,256]{2,1,0:T(8,128)S(1)} %own_attend.1.own_ref, bf16[4,592,128]{2,1,0:T(8,128)(2,1)S(1)} %all-to-all-done.2.memory_ref, bf16[16,144,128]{2,1,0:T(8,128)(2,1)S(1)} %all-to-all-done.4.time_ref, bf16[1024,2048]{1,0:T(8,128)(2,1)} %weight_ref.5), custom_call_target="tpu_custom_call" | custom-call | flops 2415919104 | bytes 10092544 | tf_op jit(solution)/shard_map/exit/leave/pallas_call | solution.py:375
  (7 shorter events, 0.0 us)
Async XLA Ops:
  6.5 84.4 %all-gather.2.cloned.1.call-start = ((), (), s32[]{:S(2)}) async-start(), calls=%async_computation.5 | async-start | bytes 5308416 | tf_op jit(solution)/shard_map/store/all_gather | solution.py:416
  7.7 15.7 %copy-start.9 = (s32[1,1,6]{2,1,0:T(1,128)S(1)}, s32[1,1,6]{2,1,0:T(1,128)}, u32[]{:S(2)}) copy-start(s32[1,1,6]{2,1,0:T(1,128)} %param.18) | copy-start | bytes 76
  7.7 15.7 %copy-start.10 = (s32[1,1,6,1]{2,3,1,0:T(1,128)S(1)}, s32[1,1,6,1]{2,3,1,0:T(1,128)}, u32[]{:S(2)}) copy-start(s32[1,1,6,1]{2,3,1,0:T(1,128)} %param.17) | copy-start | bytes 76
  7.7 15.7 %copy-start.8 = (f32[2,4]{1,0:T(2,128)S(1)}, f32[2,4]{1,0:T(2,128)}, u32[]{:S(2)}) copy-start(f32[2,4]{1,0:T(2,128)} %param.15) | copy-start | bytes 100
  7.7 15.7 %copy-start.7 = (f32[1,1,2,2048]{3,2,1,0:T(2,128)S(1)}, f32[1,1,2,2048]{3,2,1,0:T(2,128)}, u32[]{:S(2)}) copy-start(f32[1,1,2,2048]{3,2,1,0:T(2,128)} %param.12) | copy-start | bytes 49156
  27.9 1.4 copy-start
  29.4 23.8 %copy-start.1 = (bf16[4,592,128]{2,1,0:T(8,128)(2,1)}, bf16[4,592,128]{2,1,0:T(8,128)(2,1)S(1)}, u32[]{:S(2)}) copy-start(bf16[4,592,128]{2,1,0:T(8,128)(2,1)S(1)} %get-tuple-element.20.query_ref) | copy-start | bytes 1818628
  40.9 19.1 %collective-permute-start.2 = (bf16[4,592,128]{2,1,0:T(8,128)(2,1)S(1)}, bf16[4,592,128]{2,1,0:T(8,128)(2,1)S(1)}, u32[]{:S(2)}, u32[]{:S(2)}) collective-permute-start(bf16[4,592,128]{2,1,0:T(8,128)(2,1)S(1)} %all_to_all.26.query_ref), channel_id=1, source_target_pairs={{0,8},{4,12},{8,0},{12,4},{1,9},{5,13},{9,1},{13,5},{2,10},{6,14},... | collective-permute-start | bytes 1818632 | tf_op jit(solution)/shard_map/queries/ppermute | solution.py:435
  53.2 63.7 %all-to-all-start.3 = ((bf16[16,3,144,128]{3,2,1,0:T(8,128)(2,1)}), bf16[16,3,144,128]{3,2,1,0:T(8,128)(2,1)S(1)}, u32[]{:S(2)}, u32[]{:S(2)}) async-start(bf16[16,3,144,128]{3,2,1,0:T(8,128)(2,1)} %bitcast.8), calls=%async_computation.3 | async-start | bytes 3538944 | tf_op jit(solution)/shard_map/temporal/all_to_all | solution.py:441
  56.9 31.9 %collective-permute-start.4 = (bf16[4,592,128]{2,1,0:T(8,128)(2,1)S(1)}, bf16[4,592,128]{2,1,0:T(8,128)(2,1)S(1)}, u32[]{:S(2)}, u32[]{:S(2)}) collective-permute-start(bf16[4,592,128]{2,1,0:T(8,128)(2,1)S(1)} %all_to_all.26.query_ref), channel_id=1, source_target_pairs={{0,12},{4,0},{8,4},{12,8},{1,13},{5,1},{9,5},{13,9},{2,14},{6,2},{... | collective-permute-start | bytes 1818632 | tf_op jit(solution)/shard_map/queries/ppermute | solution.py:435
  60.0 30.1 %collective-permute-start = (bf16[4,592,128]{2,1,0:T(8,128)(2,1)S(1)}, bf16[4,592,128]{2,1,0:T(8,128)(2,1)S(1)}, u32[]{:S(2)}, u32[]{:S(2)}) collective-permute-start(bf16[4,592,128]{2,1,0:T(8,128)(2,1)S(1)} %all_to_all.26.query_ref), channel_id=1, source_target_pairs={{0,4},{4,8},{8,12},{12,0},{1,5},{5,9},{9,13},{13,1},{2,6},{6,10},{... | collective-permute-start | bytes 1818632 | tf_op jit(solution)/shard_map/queries/ppermute | solution.py:435
  88.8 0.9 copy-start.5
  90.1 0.8 copy-start.3
  90.9 8.8 %copy-start.6 = (bf16[4,592,128]{2,1,0:T(8,128)(2,1)S(1)}, bf16[4,592,128]{2,1,0:T(8,128)(2,1)}, u32[]{:S(2)}) copy-start(bf16[4,592,128]{2,1,0:T(8,128)(2,1)} %copy-done.5) | copy-start | bytes 1818628
  97.6 31.7 %collective-permute-start.3 = (bf16[4,592,128]{2,1,0:T(8,128)(2,1)}, bf16[4,592,128]{2,1,0:T(8,128)(2,1)}, u32[]{:S(2)}, u32[]{:S(2)}) collective-permute-start(bf16[4,592,128]{2,1,0:T(8,128)(2,1)} %memory_attend.6), channel_id=1, source_target_pairs={{0,8},{4,12},{8,0},{12,4},{1,9},{5,13},{9,1},{13,5},{2,10},{6,14},... | collective-permute-start | bytes 1818632 | tf_op jit(solution)/shard_map/memory/ppermute | solution.py:456
  99.7 7.5 %copy-start.4 = (bf16[4,592,128]{2,1,0:T(8,128)(2,1)S(1)}, bf16[4,592,128]{2,1,0:T(8,128)(2,1)}, u32[]{:S(2)}) copy-start(bf16[4,592,128]{2,1,0:T(8,128)(2,1)} %copy-done.3) | copy-start | bytes 1818628
  106.3 23.0 %collective-permute-start.5 = (bf16[4,592,128]{2,1,0:T(8,128)(2,1)}, bf16[4,592,128]{2,1,0:T(8,128)(2,1)}, u32[]{:S(2)}, u32[]{:S(2)}) collective-permute-start(bf16[4,592,128]{2,1,0:T(8,128)(2,1)} %memory_attend.7), channel_id=1, source_target_pairs={{0,4},{4,8},{8,12},{12,0},{1,5},{5,9},{9,13},{13,1},{2,6},{6,10},{... | collective-permute-start | bytes 1818632 | tf_op jit(solution)/shard_map/memory/ppermute | solution.py:456
  113.9 19.7 %collective-permute-start.1 = (bf16[4,592,128]{2,1,0:T(8,128)(2,1)}, bf16[4,592,128]{2,1,0:T(8,128)(2,1)}, u32[]{:S(2)}, u32[]{:S(2)}) collective-permute-start(bf16[4,592,128]{2,1,0:T(8,128)(2,1)} %memory_attend.5), channel_id=1, source_target_pairs={{0,12},{4,0},{8,4},{12,8},{1,13},{5,1},{9,5},{13,9},{2,14},{6,2},{... | collective-permute-start | bytes 1818632 | tf_op jit(solution)/shard_map/memory/ppermute | solution.py:456
  118.9 18.3 %all-to-all-start.4 = ((bf16[16,144,128]{2,1,0:T(8,128)(2,1)}), bf16[16,144,128]{2,1,0:T(8,128)(2,1)S(1)}, u32[]{:S(2)}, u32[]{:S(2)}) async-start(bf16[16,144,128]{2,1,0:T(8,128)(2,1)} %temporal_attend.1), calls=%async_computation.4 | async-start | bytes 1179648 | tf_op jit(solution)/shard_map/temporal/all_to_all | solution.py:448
  137.2 12.8 %all-to-all-start.2 = ((bf16[4,592,128]{2,1,0:T(8,128)(2,1)}), bf16[4,592,128]{2,1,0:T(8,128)(2,1)S(1)}, u32[]{:S(2)}, u32[]{:S(2)}) async-start(bf16[4,592,128]{2,1,0:T(8,128)(2,1)} %add_partials.1), calls=%async_computation.2 | async-start | bytes 1212416 | tf_op jit(solution)/shard_map/memory/all_to_all | solution.py:461
  141.5 1.1 copy-start.2
Sparse Core Ops, SparseCore 0:
  23.5 34.8 all-gather.1

commit v2 on v1

v2 whole, which is shorter than its diff:
```python
import functools

import jax
import jax.numpy as jnp
from jax import lax
from jax.experimental import pallas as pl
from jax.experimental.pallas import tpu as pltpu
from jax.sharding import Mesh
from jax.sharding import PartitionSpec as P

G = 4
C = 128
HW = G * C
TOPM = 6
EPSILON = 1e-06
BF = jnp.bfloat16
F32 = jnp.float32
PAD = 16
VMEM_LIMIT = 28 * 1024 * 1024
ANY = pl.BlockSpec(memory_space=pl.ANY)
WHOLE = pl.BlockSpec(memory_space=pltpu.VMEM)
SCALARS = pl.BlockSpec(memory_space=pltpu.SMEM)


def params(**more):
    return pltpu.CompilerParams(vmem_limit_bytes=VMEM_LIMIT, **more)


def cost(flops, bytes_accessed):
    return pl.CostEstimate(
        flops=flops // 16, bytes_accessed=bytes_accessed // 16, transcendentals=0
    )


def inverse_rms(values):
    return lax.rsqrt(jnp.mean(values * values, axis=-1, keepdims=True) + EPSILON)


def dot(a, b):
    return jnp.dot(a, b, preferred_element_type=F32)


def dot_t(a, b):
    return lax.dot_general(a, b, (((1,), (1,)), ((), ())), preferred_element_type=F32)


def split_store_kernel(rows_ref, out_ref):
    for h in range(G):
        key = rows_ref[:, h * C : (h + 1) * C].astype(F32)
        out_ref[h, :, :C] = (key * inverse_rms(key)).astype(BF)
        out_ref[h, :, C:] = rows_ref[:, HW + h * C : HW + (h + 1) * C]


def split_store(rows):
    n = rows.shape[0]
    return pl.pallas_call(
        split_store_kernel,
        out_shape=jax.ShapeDtypeStruct((G, n, 2 * C), BF),
        compiler_params=params(),
        name="split_store",
        cost_estimate=cost(8 * n * HW, 8 * n * HW),
    )(rows)


def join_pieces_kernel(piece, in_ref, _, out_ref, wide_ref, joined_ref):
    pieces = in_ref.shape[0]
    wide_ref[...] = in_ref[...].astype(F32)
    for m in range(out_ref.shape[0]):
        for i in range(pieces):
            joined_ref[m, i * piece : (i + 1) * piece, :] = wide_ref[
                i, m * piece : (m + 1) * piece, :
            ]
    out_ref[...] = joined_ref[...].astype(BF)


def join_pieces(parts, frames, after):
    pieces, rows, width = parts.shape
    piece = rows // frames
    return pl.pallas_call(
        functools.partial(join_pieces_kernel, piece),
        in_specs=[WHOLE, ANY],
        out_shape=jax.ShapeDtypeStruct((frames, pieces * piece, width), BF),
        scratch_shapes=[
            pltpu.VMEM((pieces, rows, width), F32),
            pltpu.VMEM((frames, pieces * piece, width), F32),
        ],
        compiler_params=params(),
        name="join_pieces",
        cost_estimate=cost(parts.size, 4 * parts.size),
    )(parts, after)


def modulate_kernel(
    act_ref, affine_ref, weight_ref, factor_ref, tail_ref, _, hidden_ref, query_ref
):
    step = pl.program_id(0)
    rows = act_ref.shape[0]
    patches = query_ref.shape[1] - PAD
    act = act_ref[...].astype(F32)
    hidden = act * inverse_rms(act) * (1.0 + affine_ref[0:1, :]) + affine_ref[1:2, :]
    hidden = hidden.astype(BF)
    hidden_ref[...] = hidden
    mapped = dot(hidden, weight_ref[...]).astype(BF).astype(F32)
    for h in range(G):
        one = mapped[:, h * C : (h + 1) * C]
        query_ref[h, pl.ds(pl.multiple_of(step * rows, 16), rows), :] = (
            one * inverse_rms(one) * factor_ref[0, h]
        ).astype(BF)

    @pl.when(step == 0)
    def _():
        for h in range(G):
            query_ref[h, patches:, :] = tail_ref[...]


def modulate(act, affine, weight, factor, tail, after):
    patches, depth = act.shape
    steps = 2
    rows = patches // steps
    return pl.pallas_call(
        modulate_kernel,
        grid=(steps,),
        in_specs=[
            pl.BlockSpec((rows, depth), lambda i: (i, 0)),
            pl.BlockSpec((2, depth), lambda i: (0, 0)),
            pl.BlockSpec((depth, HW), lambda i: (0, 0)),
            SCALARS,
            pl.BlockSpec((PAD, C), lambda i: (0, 0)),
            ANY,
        ],
        out_specs=[
            pl.BlockSpec((rows, depth), lambda i: (i, 0)),
            pl.BlockSpec((G, patches + PAD, C), lambda i: (0, 0, 0)),
        ],
        out_shape=[
            jax.ShapeDtypeStruct((patches, depth), BF),
            jax.ShapeDtypeStruct((G, patches + PAD, C), BF),
        ],
        compiler_params=params(),
        name="modulate",
        cost_estimate=cost(
            2 * patches * depth * HW, 4 * patches * depth + 2 * depth * HW + 2 * patches * HW
        ),
    )(act, affine, weight, factor, tail, after)


def temporal_entry_kernel(quarters, hidden_ref, weight_ref, factor_ref, _, out_ref):
    part = pl.program_id(0)
    rows = hidden_ref.shape[0] // quarters
    mapped = dot(hidden_ref[...], weight_ref[...]).astype(BF).astype(F32)
    for h in range(G):
        one = mapped[:, h * C : (h + 1) * C]
        scale = jnp.where(part < 2, inverse_rms(one), 1.0)
        factor = jnp.where(part == 0, factor_ref[1, h], 1.0)
        done = (one * scale * factor).astype(BF)
        for z in range(quarters):
            out_ref[z, h, 0] = done[z * rows : (z + 1) * rows, :]


def temporal_entry(hidden, weight, factor, quarters, after):
    patches, depth = hidden.shape
    rows = patches // quarters
    return pl.pallas_call(
        functools.partial(temporal_entry_kernel, quarters),
        grid=(3,),
        in_specs=[
            pl.BlockSpec((patches, depth), lambda i: (0, 0)),
            pl.BlockSpec((depth, HW), lambda i: (0, 3 + i)),
            SCALARS,
            ANY,
        ],
        out_specs=pl.BlockSpec((quarters, G, 1, rows, C), lambda i: (0, 0, i, 0, 0)),
        out_shape=jax.ShapeDtypeStruct((quarters, G, 3, rows, C), BF),
        compiler_params=params(),
        name="temporal_entry",
        cost_estimate=cost(
            6 * patches * depth * HW, 2 * patches * depth + 6 * depth * HW + 6 * patches * HW
        ),
    )(hidden, weight, factor, after)


def temporal_attend_kernel(length_ref, in_ref, _, out_ref):
    frames, _, rows, _ = in_ref.shape
    group = 16
    size = frames * group
    length = length_ref[0]
    row = lax.broadcasted_iota(jnp.int32, (size, size), 0)
    column = lax.broadcasted_iota(jnp.int32, (size, size), 1)
    target, source = row // group, column // group
    keep = (row % group == column % group) & (source <= target) & (source > target - length)
    for g in range(rows // group):
        at = slice(g * group, (g + 1) * group)
        query = in_ref[:, 0, at, :].reshape(size, C)
        key = in_ref[:, 1, at, :].reshape(size, C)
        value = in_ref[:, 2, at, :].reshape(size, C)
        weights = jnp.where(keep, jnp.exp(dot_t(query, key)), 0.0)
        shares = weights / jnp.sum(weights, axis=-1, keepdims=True)
        result = dot(shares.astype(BF), value).astype(BF)
        out_ref[:, at, :] = result.reshape(frames, group, C)


def temporal_attend(length, parts, after):
    frames, _, rows, _ = parts.shape
    return pl.pallas_call(
        temporal_attend_kernel,
        in_specs=[SCALARS, WHOLE, ANY],
        out_shape=jax.ShapeDtypeStruct((frames, rows, C), BF),
        compiler_params=params(),
        name="temporal_attend",
        cost_estimate=cost(4 * frames * rows * 256 * C, 8 * frames * rows * C),
    )(length, parts, after)


def own_attend_kernel(hidden_ref, key_weight_ref, value_weight_ref, query_ref, out_ref):
    heads = query_ref.shape[0]
    patches = hidden_ref.shape[0]
    hidden = hidden_ref[...]
    keys = dot(hidden, key_weight_ref[...]).astype(BF).astype(F32)
    values = dot(hidden, value_weight_ref[...]).astype(BF)
    ones = jnp.ones((patches, C), BF)
    for h in range(heads):
        key = keys[:, h * C : (h + 1) * C]
        key = (key * inverse_rms(key)).astype(BF)
        both = jnp.concatenate([values[:, h * C : (h + 1) * C], ones], axis=1)
        weights = jnp.exp(dot_t(query_ref[h, :patches, :], key)).astype(BF)
        out_ref[h] = dot(weights, both)


def own_attend(hidden, weight, query):
    patches, depth = hidden.shape
    heads = 2
    wide = heads * C
    per = HW // wide
    return pl.pallas_call(
        own_attend_kernel,
        grid=(G // heads,),
        in_specs=[
            pl.BlockSpec((patches, depth), lambda i: (0, 0)),
            pl.BlockSpec((depth, wide), lambda i: (0, per + i)),
            pl.BlockSpec((depth, wide), lambda i: (0, 2 * per + i)),
            pl.BlockSpec((heads, patches + PAD, C), lambda i: (i, 0, 0)),
        ],
        out_specs=pl.BlockSpec((heads, patches, 2 * C), lambda i: (i, 0, 0)),
        out_shape=jax.ShapeDtypeStruct((G, patches, 2 * C), F32),
        compiler_params=params(),
        name="own_attend",
        cost_estimate=cost(
            4 * patches * depth * HW + 6 * patches * patches * HW,
            2 * patches * depth + 4 * depth * HW + 10 * patches * HW,
        ),
    )(hidden, weight, weight, query)


LINE = 96


def halves(denominators):
    high = denominators.astype(BF).astype(F32)
    return jnp.concatenate([high, denominators - high], axis=0).astype(BF)


def memory_attend_kernel(carried, index_ref, query_ref, *refs):
    stores, out_ref = refs[:TOPM], refs[-1]
    patches = query_ref.shape[1] - PAD
    chunk = 3 * LINE
    keys = jnp.concatenate([ref[0, :, :C] for ref in stores], axis=0)
    values = jnp.concatenate([ref[0, :, C:] for ref in stores], axis=0)
    both = jnp.concatenate([values, jnp.ones(values.shape, BF)], axis=1)
    row = lax.broadcasted_iota(jnp.int32, (LINE, C), 0)
    column = lax.broadcasted_iota(jnp.int32, (LINE, C), 1)
    carry = None
    if carried is not None:
        first, count = carried
        step = pl.program_id(0)
        here = jnp.logical_and(step >= first, step < first + count).astype(F32)
        carry_ref = refs[TOPM]
        carry = here * carry_ref[0].astype(F32)
    lines = []
    for start in range(0, patches, chunk):
        at = slice(start, start + chunk)
        weights = jnp.exp(dot_t(query_ref[0, at, :], keys)).astype(BF)
        result = dot(weights, both)
        top = result[:, :C]
        if carry is not None:
            top = top + carry[at]
        out_ref[0, at, :] = top.astype(BF)
        for j in range(0, chunk, LINE):
            diagonal = jnp.where(row == column, result[j : j + LINE, C:], 0.0)
            lines.append(jnp.sum(diagonal, axis=0, keepdims=True))
    lines.append(jnp.zeros((8 - len(lines), C), F32))
    total = jnp.concatenate(lines, axis=0)
    if carry is not None:
        total = total + carry[patches : patches + 8] + carry[patches + 8 :]
    out_ref[0, patches:, :] = halves(total)


def memory_attend(index, query, store, after, carry=None, first=0):
    frames, rows, _ = query.shape
    patches = rows - PAD
    quarter = store.shape[1]
    block = pl.BlockSpec((1, rows, C), lambda i, index_ref: (i, 0, 0))
    carried, extra, extra_specs = None, [], []
    if carry is not None:
        count = carry.shape[0]
        carried, extra = (first, count), [carry]
        extra_specs = [
            pl.BlockSpec(
                (1, rows, C),
                lambda i, index_ref: (jnp.clip(i - first, 0, count - 1), 0, 0),
            )
        ]

    def place(j):
        return lambda i, index_ref: (index_ref[i, j], 0, 0)

    return pl.pallas_call(
        functools.partial(memory_attend_kernel, carried),
        grid_spec=pltpu.PrefetchScalarGridSpec(
            num_scalar_prefetch=1,
            grid=(frames,),
            in_specs=[block]
            + [pl.BlockSpec((1, quarter, 2 * C), place(j)) for j in range(TOPM)]
            + extra_specs
            + [ANY],
            out_specs=block,
        ),
        out_shape=jax.ShapeDtypeStruct(query.shape, BF),
        compiler_params=params(),
        name="memory_attend",
        cost_estimate=cost(
            8 * frames * patches * TOPM * quarter * C,
            4 * query.size + 4 * frames * TOPM * quarter * C,
        ),
    )(index, query, *([store] * TOPM), *extra, after)


def add_partials_kernel(*refs):
    ins, out_ref = refs[:-1], refs[-1]
    patches = out_ref.shape[1] - PAD
    total = ins[0][:, :patches, :].astype(F32)
    tail = ins[0][:, patches:, :].astype(F32)
    for ref in ins[1:]:
        total += ref[:, :patches, :].astype(F32)
        tail += ref[:, patches:, :].astype(F32)
    out_ref[:, :patches, :] = total.astype(BF)
    for i in range(out_ref.shape[0]):
        out_ref[i, patches:, :] = halves(tail[i, :8] + tail[i, 8:])


def add_partials(parts):
    return pl.pallas_call(
        add_partials_kernel,
        out_shape=jax.ShapeDtypeStruct(parts[0].shape, BF),
        compiler_params=params(),
        name="add_partials",
        cost_estimate=cost(4 * parts[0].size, 8 * parts[0].size),
    )(*parts)


def leave_kernel(own_ref, memory_ref, time_ref, weight_ref, out_ref, combined_ref):
    patches = own_ref.shape[1]
    quarters = time_ref.shape[0] // G
    rows = time_ref.shape[1]

    @pl.when(pl.program_id(0) == 0)
    def _():
        row = lax.broadcasted_iota(jnp.int32, (LINE, C), 0)
        column = lax.broadcasted_iota(jnp.int32, (LINE, C), 1)
        for h in range(G):
            tail = memory_ref[h, patches:, :].astype(F32)
            denominators = tail[:8] + tail[8:]
            for j in range(patches // LINE):
                at = slice(j * LINE, (j + 1) * LINE)
                line = jnp.broadcast_to(denominators[j : j + 1, :], (LINE, C))
                memory_sum = jnp.sum(
                    jnp.where(row == column, line, 0.0), axis=1, keepdims=True
                )
                top = own_ref[h, at, :C] + memory_ref[h, at, :].astype(F32)
                combined_ref[at, h * C : (h + 1) * C] = (
                    top / (own_ref[h, at, C:] + memory_sum)
                ).astype(BF)
            for z in range(quarters):
                combined_ref[z * rows : (z + 1) * rows, HW + h * C : HW + (h + 1) * C] = time_ref[
                    z * G + h
                ]

    out_ref[...] = dot(combined_ref[...], weight_ref[...]).astype(BF)


def leave(own, memory, time, weight):
    patches = own.shape[1]
    depth, width = weight.shape
    step = 512
    return pl.pallas_call(
        leave_kernel,
        grid=(width // step,),
        in_specs=[
            pl.BlockSpec(own.shape, lambda i: (0, 0, 0)),
            pl.BlockSpec(memory.shape, lambda i: (0, 0, 0)),
            pl.BlockSpec(time.shape, lambda i: (0, 0, 0)),
            pl.BlockSpec((depth, step), lambda i: (0, i)),
        ],
        out_specs=pl.BlockSpec((patches, step), lambda i: (0, i)),
        out_shape=jax.ShapeDtypeStruct((patches, width), BF),
        scratch_shapes=[pltpu.VMEM((patches, depth), BF)],
        compiler_params=params(),
        name="leave",
        cost_estimate=cost(
            2 * patches * depth * width,
            2 * depth * width + 2 * patches * width + 6 * patches * depth,
        ),
    )(own, memory, time, weight)


def on_device(
    patch_activation_tensor,
    conditioning_affine,
    entry_projection_matrix,
    exit_projection_matrix,
    softmax_sharpness,
    cached_past_pairs,
    recalled_picture_holder,
    recalled_picture_position,
    lookback_lengths,
):
    rings = lax.axis_size("z")
    patches, depth = patch_activation_tensor.shape[2:]
    held, piece = cached_past_pairs.shape[:2]
    up = [(s, (s + 1) % rings) for s in range(rings)]
    down = [(s, (s - 1) % rings) for s in range(rings)]

    def swap(blocks, axes):
        return lax.all_to_all(blocks, axes, split_axis=0, concat_axis=0, tiled=True)

    def attend(group, store, after, **more):
        chosen = group[:, patches, :TOPM].astype(jnp.int32)
        return memory_attend(chosen, group, store, after, **more)

    with jax.named_scope("store"):
        split = split_store(cached_past_pairs.reshape(held * piece, 2 * HW))
        pieces = swap(split, "x")

    with jax.named_scope("queries"):
        factor = softmax_sharpness / C
        index = recalled_picture_holder.reshape(TOPM) * held + recalled_picture_position.reshape(
            TOPM
        )
        tail = jnp.zeros((PAD, C), BF).at[0, :TOPM].set(index.astype(BF))
        hidden, query = modulate(
            patch_activation_tensor.reshape(patches, depth),
            conditioning_affine.reshape(2, depth),
            entry_projection_matrix,
            factor,
            tail,
            after=split,
        )
        here = swap(query, "x")

    with jax.named_scope("own"):
        own = own_attend(hidden, entry_projection_matrix, query)

    with jax.named_scope("store"):
        joined = join_pieces(pieces, held, after=own)
        store = lax.all_gather(joined, ("y", "c"), axis=0, tiled=True)

    with jax.named_scope("queries"):
        below = lax.ppermute(here, "z", up)
        above = lax.ppermute(here, "z", down)
        half = here.shape[0] // 2
        far_first = lax.ppermute(below[:half], "z", up)
        far_last = lax.ppermute(above[half:], "z", down)

    with jax.named_scope("temporal"):
        parts = temporal_entry(hidden, entry_projection_matrix, factor, rings, after=joined)
        sent = swap(parts.reshape((rings * G,) + parts.shape[2:]), ("z", "x"))

    with jax.named_scope("memory"):
        sum_first = attend(far_first, store, parts)
        sum_last = attend(far_last, store, sum_first)
        carry_first = lax.ppermute(sum_first, "z", down)
        carry_last = lax.ppermute(sum_last, "z", up)
        sum_below = attend(below, store, sum_last, carry=carry_first, first=0)
        from_above = lax.ppermute(sum_below, "z", down)
        sum_above = attend(above, store, sum_below, carry=carry_last, first=half)
        from_below = lax.ppermute(sum_above, "z", up)

    with jax.named_scope("temporal"):
        timed = temporal_attend(lookback_lengths, sent, after=sum_above)
        time = swap(timed, ("z", "x"))

    with jax.named_scope("memory"):
        sum_here = attend(here, store, timed)
        memory = swap(add_partials([sum_here, from_above, from_below]), "x")

    with jax.named_scope("exit"):
        attended = leave(own, memory, time, exit_projection_matrix)
    return attended.reshape(1, 1, patches, depth)


def solution(mesh):
    apart = Mesh(mesh.devices.reshape(4, 2, 4, 4), ("y", "c", "z", "x"))
    roll, frame = ("y", "c"), ("z", "x")
    return jax.shard_map(
        on_device,
        mesh=apart,
        in_specs=(
            P(roll, frame, None, None),
            P(roll, frame, None, None),
            P(),
            P(),
            P(),
            P(roll, frame, None, None),
            P(roll, frame, None, None),
            P(roll, frame, None),
            P(roll),
        ),
        out_specs=P(roll, frame, None, None),
        check_vma=False,
    )
```

time: 164 us -> 172 us (1.049)
  local copies, waits for them, and re-layouts: 5.35 us -> 30 us
  Pallas kernels: 59.2 us -> 45 us
  waiting for transfers between devices: 33.9 us -> 26.7 us
  starting transfers between devices: 24.7 us -> 26.8 us
    unnamed x23 -> x39, local copies, waits for them, and re-layouts: 5.34 us -> 28 us
    pallas_call x7 -> x8, Pallas kernels: 32.5 us -> 24.7 us  [the longest x5 18.7 us: memory_attend(): pl.pallas_call(functools.partial(memory_attend_kernel, carried), grid_spe...]
    ppermute x6 -> x8, waiting for transfers between devices: 33.5 us -> 26 us  [the longest x1 21.5 us: on_device(): far_first = lax.ppermute(below[:half], 'z', up)]
    pallas_call x1, Pallas kernels: 8.42 us -> 5.9 us  [temporal_entry(): pl.pallas_call(functools.partial(temporal_entry_kernel, quarters), grid=(...]
    slice x0 -> x2, local copies, waits for them, and re-layouts: none -> 1.97 us  [the longest x1 0.99 us: on_device(): far_first = lax.ppermute(below[:half], 'z', up)]
    pallas_call x1, Pallas kernels: 7.12 us -> 5.31 us  [own_attend(): pl.pallas_call(own_attend_kernel, grid=(G // heads,), in_specs=[pl.BlockS...]
    ppermute x6 -> x8, starting transfers between devices: 12.3 us -> 12.8 us  [the longest x1 2.12 us: on_device(): above = lax.ppermute(here, 'z', down)]
  transfers between devices with their start and end apart: 10 -> 12, of which waited for: 4 -> 5; matrix products, arithmetic and copies ran while one was open for 0% -> 2% of each run, Pallas kernels for 32% -> 22%
where the time goes in v2:
time: 172 us; the launch traced here: 171 us
  Pallas kernels  45 us (26%)
  local copies, waits for them, and re-layouts  30 us (17%)
  starting transfers between devices  26.8 us (16%)
  waiting for transfers between devices  26.7 us (16%)
  blocking collectives  26.5 us (15%)
  between operations  14.3 us (8%)
    unnamed x39, local copies, waits for them, and re-layouts  28 us
    all_to_all x2, blocking collectives, swap(): return lax.all_to_all(blocks, axes, split_axis=0, concat_axis=0, tiled=True)  26.5 us
    ppermute x1, waiting for transfers between devices, on_device(): far_first = lax.ppermute(below[:half], 'z', up)  21.5 us
    pallas_call x5, Pallas kernels, memory_attend(): pl.pallas_call(functools.partial(memory_attend_kernel, carried), grid_spe...  18.7 us
    all_to_all x3, starting transfers between devices, swap(): return lax.all_to_all(blocks, axes, split_axis=0, concat_axis=0, tiled=True)  14 us
    pallas_call x1, Pallas kernels, temporal_entry(): pl.pallas_call(functools.partial(temporal_entry_kernel, quarters), grid=(...  5.9 us
    pallas_call x1, Pallas kernels, own_attend(): pl.pallas_call(own_attend_kernel, grid=(G // heads,), in_specs=[pl.BlockS...  5.31 us
    pallas_call x1, Pallas kernels, leave(): pl.pallas_call(leave_kernel, grid=(width // step,), in_specs=[pl.BlockSpe...  4.8 us
  transfers between devices with their start and end apart: 12, of which 5 were waited for; matrix products, arithmetic and copies ran while one was open for 2% of the time, Pallas kernels for 22%

profile of v2, /device:TPU:0, one launch (start us, length us, event | category | flops | bytes accessed | tf_op | source)
XLA Modules:
  0.0 170.7 jit_solution(6763594088543290020)
XLA Ops:
  6.5 1.2 copy.10
  7.7 1.1 split_store.1._
  8.8 4.4 %all-to-all-start.1 = ((bf16[4,288,256]{2,1,0:T(8,128)(2,1)}), bf16[4,288,256]{2,1,0:T(8,128)(2,1)S(1)}, u32[]{:S(2)}, u32[]{:S(2)}) async-start(bf16[4,288,256]{2,1,0:T(8,128)(2,1)} %split_store.1._), calls=%async_computation.1 | async-start | bytes 1179648 | tf_op jit(solution)/shard_map/store/all_to_all | solution.py:433
  13.2 0.0 copy-done.18
  13.2 0.0 copy-done.16
  13.3 0.0 copy-start.3
  13.3 4.6 %copy-done.3 = bf16[2048,3072]{1,0:T(8,128)(2,1)S(1)} copy-done((bf16[2048,3072]{1,0:T(8,128)(2,1)S(1)}, bf16[2048,3072]{1,0:T(8,128)(2,1)}, u32[]{:S(2)}) %copy-start.3) | copy-done | bytes 12582936
  17.9 1.7 copy-done.12
  19.5 3.2 %modulate.1 = (bf16[576,2048]{1,0:T(8,128)(2,1)S(1)}, bf16[4,592,128]{2,1,0:T(8,128)(2,1)S(1)}) custom-call(bf16[576,2048]{1,0:T(8,128)(2,1)S(1)} %bitcast.20, f32[2,2048]{1,0:T(2,128)S(1)} %bitcast.21, bf16[2048,3072]{1,0:T(8,128)(2,1)S(1)} %copy-done.3, f32[2,4]{1,0:T(2,128)S(1)} %broadcast_multiply_fusion.factor_ref, ...), custom_call_target="tpu_custom_call" | custom-call | flops 75497472 | bytes 462848 | tf_op jit(solution)/shard_map/queries/modulate/pallas_call | solution.py:120
  22.7 1.4 copy-done.4
  24.1 5.3 %own_attend.1._.own_ref = f32[4,576,256]{2,1,0:T(8,128)S(1)} custom-call(bf16[576,2048]{1,0:T(8,128)(2,1)S(1)} %get-tuple-element.19.hidden_ref, bf16[2048,3072]{1,0:T(8,128)(2,1)S(1)} %copy-done.4, bf16[2048,3072]{1,0:T(8,128)(2,1)S(1)} %copy-done.4, bf16[4,592,128]{2,1,0:T(8,128)(2,1)S(1)} %get-tuple-element.20.query_ref), custom_call_target="tpu_custom_call" | custom-call | flops 214695936 | bytes 593920 | tf_op jit(solution)/shard_map/own/own_attend/pallas_call | solution.py:234
  29.4 0.0 copy-start.8
  29.4 1.4 copy-done.8
  30.8 0.8 copy-done.11
  31.7 0.0 all-to-all-done.1.in_ref
  31.7 1.0 join_pieces.1._
  32.7 0.0 all-gather.2.cloned.1.call-update
  32.7 14.6 %all_to_all.25.query_ref = bf16[4,592,128]{2,1,0:T(8,128)(2,1)S(1)} all-to-all(bf16[4,592,128]{2,1,0:T(8,128)(2,1)} %copy-done.11), channel_id=1, replica_groups=mesh['y'=4,'c'=2,'z'=4,'x'=4] {'x'}, dimensions={0} | all-to-all | bytes 1212416 | tf_op jit(solution)/shard_map/queries/all_to_all | solution.py:433
  47.3 1.9 %collective-permute-start.2 = (bf16[4,592,128]{2,1,0:T(8,128)(2,1)S(1)}, bf16[4,592,128]{2,1,0:T(8,128)(2,1)}, u32[]{:S(2)}, u32[]{:S(2)}) collective-permute-start(bf16[4,592,128]{2,1,0:T(8,128)(2,1)S(1)} %all_to_all.25.query_ref), channel_id=1, source_target_pairs={{0,4},{4,8},{8,12},{12,0},{1,5},{5,9},{9,13},{13,1},{2,6},{6,10},{... | collective-permute-start | bytes 1818632 | tf_op jit(solution)/shard_map/queries/ppermute | solution.py:467
  49.2 2.1 %collective-permute-start = (bf16[4,592,128]{2,1,0:T(8,128)(2,1)S(1)}, bf16[4,592,128]{2,1,0:T(8,128)(2,1)}, u32[]{:S(2)}, u32[]{:S(2)}) collective-permute-start(bf16[4,592,128]{2,1,0:T(8,128)(2,1)S(1)} %all_to_all.25.query_ref), channel_id=1, source_target_pairs={{0,12},{4,0},{8,4},{12,8},{1,13},{5,1},{9,5},{13,9},{2,14},{6,2},{... | collective-permute-start | bytes 1818632 | tf_op jit(solution)/shard_map/queries/ppermute | solution.py:468
  51.4 4.8 %copy-done.5 = bf16[2048,3072]{1,0:T(8,128)(2,1)S(1)} copy-done((bf16[2048,3072]{1,0:T(8,128)(2,1)S(1)}, bf16[2048,3072]{1,0:T(8,128)(2,1)}, u32[]{:S(2)}) %copy-start.5) | copy-done | bytes 12582936
  56.2 1.8 %copy-done.9 = bf16[576,2048]{1,0:T(8,128)(2,1)S(1)} copy-done((bf16[576,2048]{1,0:T(8,128)(2,1)S(1)}, bf16[576,2048]{1,0:T(8,128)(2,1)}, u32[]{:S(2)}) %copy-start.9) | copy-done | bytes 2359320
  58.0 5.9 %temporal_entry.1.refs_6_ = bf16[4,4,3,144,128]{4,3,2,1,0:T(8,128)(2,1)S(1)} custom-call(bf16[576,2048]{1,0:T(8,128)(2,1)S(1)} %copy-done.9, bf16[2048,3072]{1,0:T(8,128)(2,1)S(1)} %copy-done.5, f32[2,4]{1,0:T(2,128)S(1)} %broadcast_multiply_fusion.factor_ref, bf16[8,144,256]{2,1,0:T(8,128)(2,1)} %join_pieces.1._), custom_call_target="tpu_custom_call" | custom-call | flops 226492416 | bytes 651264 | tf_op jit(solution)/shard_map/temporal/temporal_entry/pallas_call | solution.py:163
  63.9 0.0 copy-start.6
  63.9 1.2 copy-done.6
  65.1 4.4 %all-to-all-start.2 = ((bf16[16,3,144,128]{3,2,1,0:T(8,128)(2,1)}), bf16[16,3,144,128]{3,2,1,0:T(8,128)(2,1)}, u32[]{:S(2)}, u32[]{:S(2)}) async-start(bf16[16,3,144,128]{3,2,1,0:T(8,128)(2,1)} %bitcast.18), calls=%async_computation.2 | async-start | bytes 3538944 | tf_op jit(solution)/shard_map/temporal/all_to_all | solution.py:433
  69.5 0.0 collective-permute-done.2.query_ref
  69.5 1.0 slice.48
  70.5 1.8 %collective-permute-start.3 = (bf16[2,592,128]{2,1,0:T(8,128)(2,1)S(1)}, bf16[2,592,128]{2,1,0:T(8,128)(2,1)S(1)}, u32[]{:S(2)}, u32[]{:S(2)}) collective-permute-start(bf16[2,592,128]{2,1,0:T(8,128)(2,1)S(1)} %slice.48), channel_id=1, source_target_pairs={{0,4},{4,8},{8,12},{12,0},{1,5},{5,9},{9,13},{13,1},{2,6},{6,10},{... | collective-permute-start | bytes 909320 | tf_op jit(solution)/shard_map/queries/ppermute | solution.py:470
  72.3 0.0 collective-permute-done.query_ref
  72.3 1.0 slice.46
  73.3 1.5 collective-permute-start.1
  74.9 21.5 %collective-permute-done.3.query_ref = bf16[2,592,128]{2,1,0:T(8,128)(2,1)S(1)} collective-permute-done((bf16[2,592,128]{2,1,0:T(8,128)(2,1)S(1)}, bf16[2,592,128]{2,1,0:T(8,128)(2,1)S(1)}, u32[]{:S(2)}, u32[]{:S(2)}) %collective-permute-start.3) | collective-permute-done | bytes 303136 | tf_op jit(solution)/shard_map/queries/ppermute | solution.py:470
  96.3 0.0 collective-permute-done.1.query_ref
  96.4 0.0 copy-start.13
  96.4 0.7 copy-done.13
  97.1 2.3 %copy-done = bf16[64,144,256]{2,1,0:T(8,128)(2,1)S(1)} copy-done((bf16[64,144,256]{2,1,0:T(8,128)(2,1)S(1)}, bf16[64,144,256]{2,1,0:T(8,128)(2,1)}, u32[]{:S(2)}) %copy-start) | copy-done | bytes 4718616
  99.4 1.5 copy-done.7
  100.9 2.1 %memory_attend.5.refs_6_ = bf16[2,592,128]{2,1,0:T(8,128)(2,1)S(1)} custom-call(s32[2,6]{1,0:T(2,128)S(1)} %bitcast.26, bf16[2,592,128]{2,1,0:T(8,128)(2,1)S(1)} %collective-permute-done.3.query_ref, bf16[64,144,256]{2,1,0:T(8,128)(2,1)S(1)} %copy-done, bf16[64,144,256]{2,1,0:T(8,128)(2,1)S(1)} %copy-done, bf16[64,144,256]{2,1,0:T(8,128)(2,1)S(1)} %copy-done, ...), custom_call_target="tpu_custom_call" | custom-call | flops 63700992 | bytes 93184 | tf_op jit(solution)/shard_map/memory/memory_attend/pallas_call | solution.py:316
  103.0 1.2 collective-permute-start.5
  104.2 0.0 copy-done.1
  104.2 2.1 %memory_attend.6.refs_7_ = bf16[2,592,128]{2,1,0:T(8,128)(2,1)S(1)} custom-call(s32[2,6]{1,0:T(2,128)S(1)} %bitcast.25, bf16[2,592,128]{2,1,0:T(8,128)(2,1)S(1)} %copy-done.14, bf16[64,144,256]{2,1,0:T(8,128)(2,1)S(1)} %copy-done.1, bf16[64,144,256]{2,1,0:T(8,128)(2,1)S(1)} %copy-done.1, bf16[64,144,256]{2,1,0:T(8,128)(2,1)S(1)} %copy-done.1, ...), custom_call_target="tpu_custom_call" | custom-call | flops 63700992 | bytes 93184 | tf_op jit(solution)/shard_map/memory/memory_attend/pallas_call | solution.py:316
  106.3 1.0 collective-permute-start.4
  107.3 0.7 slice_convert_fusion
  108.0 0.7 slice_convert_fusion.1
  108.7 2.0 %collective-permute-done.5.refs_6_ = bf16[2,592,128]{2,1,0:T(8,128)(2,1)S(1)} collective-permute-done((bf16[2,592,128]{2,1,0:T(8,128)(2,1)S(1)}, bf16[2,592,128]{2,1,0:T(8,128)(2,1)S(1)}, u32[]{:S(2)}, u32[]{:S(2)}) %collective-permute-start.5) | collective-permute-done | bytes 303136 | tf_op jit(solution)/shard_map/memory/ppermute | solution.py:480
  110.7 5.4 %memory_attend.7.refs_7_ = bf16[4,592,128]{2,1,0:T(8,128)(2,1)} custom-call(s32[4,6]{1,0:T(4,128)S(1)} %bitcast.23, bf16[4,592,128]{2,1,0:T(8,128)(2,1)} %collective-permute-done.2.query_ref, bf16[64,144,256]{2,1,0:T(8,128)(2,1)S(1)} %copy-done.1, bf16[64,144,256]{2,1,0:T(8,128)(2,1)S(1)} %copy-done.1, bf16[64,144,256]{2,1,0:T(8,128)(2,1)S(1)} %copy-done.1, ...), custom_call_target="tpu_custom_call" | custom-call | flops 127401984 | bytes 186368 | tf_op jit(solution)/shard_map/memory/memory_attend/pallas_call | solution.py:316
  116.1 0.0 collective-permute-done.4.refs_6_
  116.1 5.4 %memory_attend.8._ = bf16[4,592,128]{2,1,0:T(8,128)(2,1)} custom-call(s32[4,6]{1,0:T(4,128)S(1)} %bitcast.22, bf16[4,592,128]{2,1,0:T(8,128)(2,1)} %collective-permute-done.query_ref, bf16[64,144,256]{2,1,0:T(8,128)(2,1)S(1)} %copy-done.1, bf16[64,144,256]{2,1,0:T(8,128)(2,1)S(1)} %copy-done.1, bf16[64,144,256]{2,1,0:T(8,128)(2,1)S(1)} %copy-done.1, ...), custom_call_target="tpu_custom_call" | custom-call | flops 127401984 | bytes 186368 | tf_op jit(solution)/shard_map/memory/memory_attend/pallas_call | solution.py:316
  121.6 1.4 collective-permute-start.7
  123.0 1.8 %collective-permute-start.6 = (bf16[4,592,128]{2,1,0:T(8,128)(2,1)}, bf16[4,592,128]{2,1,0:T(8,128)(2,1)}, u32[]{:S(2)}, u32[]{:S(2)}) collective-permute-start(bf16[4,592,128]{2,1,0:T(8,128)(2,1)} %memory_attend.7.refs_7_), channel_id=1, source_target_pairs={{0,12},{4,0},{8,4},{12,8},{1,13},{5,1},{9,5},{13,9},{2,14},{6,2},{... | collective-permute-start | bytes 1818632 | tf_op jit(solution)/shard_map/memory/ppermute | solution.py:483
  125.5 0.0 all-to-all-done.2.in_ref
  125.5 3.5 %temporal_attend.1.refs_6_ = bf16[16,144,128]{2,1,0:T(8,128)(2,1)} custom-call(s32[1]{0:T(128)S(6)} %copy.11.length_ref, bf16[16,3,144,128]{3,2,1,0:T(8,128)(2,1)} %all-to-all-done.2.in_ref, bf16[4,592,128]{2,1,0:T(8,128)(2,1)} %memory_attend.8._), custom_call_target="tpu_custom_call" | custom-call | flops 18874368 | bytes 147456 | tf_op jit(solution)/shard_map/temporal/temporal_attend/pallas_call | solution.py:204
  129.0 5.2 %all-to-all-start.4 = ((bf16[16,144,128]{2,1,0:T(8,128)(2,1)}), bf16[16,144,128]{2,1,0:T(8,128)(2,1)S(1)}, u32[]{:S(2)}, u32[]{:S(2)}) async-start(bf16[16,144,128]{2,1,0:T(8,128)(2,1)} %temporal_attend.1.refs_6_), calls=%async_computation.4 | async-start | bytes 1179648 | tf_op jit(solution)/shard_map/temporal/all_to_all | solution.py:433
  134.2 0.0 copy-start.2
  134.2 2.3 %copy-done.2 = bf16[64,144,256]{2,1,0:T(8,128)(2,1)S(1)} copy-done((bf16[64,144,256]{2,1,0:T(8,128)(2,1)S(1)}, bf16[64,144,256]{2,1,0:T(8,128)(2,1)}, u32[]{:S(2)}) %copy-start.2) | copy-done | bytes 4718616
  136.6 3.6 %memory_attend.9.refs_0_ = bf16[4,592,128]{2,1,0:T(8,128)(2,1)S(1)} custom-call(s32[4,6]{1,0:T(4,128)S(1)} %bitcast.24, bf16[4,592,128]{2,1,0:T(8,128)(2,1)S(1)} %all_to_all.25.query_ref, bf16[64,144,256]{2,1,0:T(8,128)(2,1)S(1)} %copy-done.2, bf16[64,144,256]{2,1,0:T(8,128)(2,1)S(1)} %copy-done.2, bf16[64,144,256]{2,1,0:T(8,128)(2,1)S(1)} %copy-done.2, ...), custom_call_target="tpu_custom_call" | custom-call | flops 127401984 | bytes 186368 | tf_op jit(solution)/shard_map/memory/memory_attend/pallas_call | solution.py:316
  140.2 0.1 collective-permute-done.7.refs_2_
  140.3 2.5 %collective-permute-done.6.refs_1_ = bf16[4,592,128]{2,1,0:T(8,128)(2,1)} collective-permute-done((bf16[4,592,128]{2,1,0:T(8,128)(2,1)}, bf16[4,592,128]{2,1,0:T(8,128)(2,1)}, u32[]{:S(2)}, u32[]{:S(2)}) %collective-permute-start.6) | collective-permute-done | bytes 606240 | tf_op jit(solution)/shard_map/memory/ppermute | solution.py:483
  142.8 1.5 add_partials.1
  144.3 0.7 all-to-all-done.4.time_ref
  145.0 11.9 %all_to_all.26.memory_ref = bf16[4,592,128]{2,1,0:T(8,128)(2,1)S(1)} all-to-all(bf16[4,592,128]{2,1,0:T(8,128)(2,1)S(1)} %add_partials.1), channel_id=1, replica_groups=mesh['y'=4,'c'=2,'z'=4,'x'=4] {'x'}, dimensions={0} | all-to-all | bytes 1212416 | tf_op jit(solution)/shard_map/memory/all_to_all | solution.py:433
  156.9 2.2 %copy-done.10 = bf16[1024,2048]{1,0:T(8,128)(2,1)S(1)} copy-done((bf16[1024,2048]{1,0:T(8,128)(2,1)S(1)}, bf16[1024,2048]{1,0:T(8,128)(2,1)}, u32[]{:S(2)}) %copy-start.10) | copy-done | bytes 4194328
  159.1 4.8 %leave.1 = bf16[576,2048]{1,0:T(8,128)(2,1)} custom-call(f32[4,576,256]{2,1,0:T(8,128)S(1)} %own_attend.1._.own_ref, bf16[4,592,128]{2,1,0:T(8,128)(2,1)S(1)} %all_to_all.26.memory_ref, bf16[16,144,128]{2,1,0:T(8,128)(2,1)S(1)} %all-to-all-done.4.time_ref, bf16[1024,2048]{1,0:T(8,128)(2,1)S(1)} %copy-done.10), custom_call_target="tpu_custom_call" | custom-call | flops 150994944 | bytes 630784 | tf_op jit(solution)/shard_map/exit/leave/pallas_call | solution.py:394
  (25 shorter events, 0.1 us)
Async XLA Ops:
  6.5 6.7 %copy-start.18 = (s32[1,1,6,1]{2,3,1,0:T(1,128)S(1)}, s32[1,1,6,1]{2,3,1,0:T(1,128)}, u32[]{:S(2)}) copy-start(s32[1,1,6,1]{2,3,1,0:T(1,128)} %param.17) | copy-start | bytes 76
  6.5 6.7 %copy-start.17 = (s32[1,1,6]{2,1,0:T(1,128)S(1)}, s32[1,1,6]{2,1,0:T(1,128)}, u32[]{:S(2)}) copy-start(s32[1,1,6]{2,1,0:T(1,128)} %param.18) | copy-start | bytes 76
  6.5 6.7 %copy-start.16 = (f32[2,4]{1,0:T(2,128)S(1)}, f32[2,4]{1,0:T(2,128)}, u32[]{:S(2)}) copy-start(f32[2,4]{1,0:T(2,128)} %param.15) | copy-start | bytes 100
  6.5 6.7 %copy-start.15 = (f32[1,1,2,2048]{3,2,1,0:T(2,128)S(1)}, f32[1,1,2,2048]{3,2,1,0:T(2,128)}, u32[]{:S(2)}) copy-start(f32[1,1,2,2048]{3,2,1,0:T(2,128)} %param.12) | copy-start | bytes 49156
  8.8 22.8 %all-to-all-start.1 = ((bf16[4,288,256]{2,1,0:T(8,128)(2,1)}), bf16[4,288,256]{2,1,0:T(8,128)(2,1)S(1)}, u32[]{:S(2)}, u32[]{:S(2)}) async-start(bf16[4,288,256]{2,1,0:T(8,128)(2,1)} %split_store.1._), calls=%async_computation.1 | async-start | bytes 1179648 | tf_op jit(solution)/shard_map/store/all_to_all | solution.py:433
  13.2 83.9 %all-gather.2.cloned.1.call-start = ((), (), s32[]{:S(2)}) async-start(), calls=%async_computation.5 | async-start | bytes 5308416 | tf_op jit(solution)/shard_map/store/all_gather | solution.py:464
  13.3 4.6 %copy-start.3 = (bf16[2048,3072]{1,0:T(8,128)(2,1)S(1)}, bf16[2048,3072]{1,0:T(8,128)(2,1)}, u32[]{:S(2)}) copy-start(bf16[2048,3072]{1,0:T(8,128)(2,1)} %weight_ref.4) | copy-start | bytes 37748740
  17.9 1.7 copy-start.12
  19.5 4.6 %copy-start.4 = (bf16[2048,3072]{1,0:T(8,128)(2,1)S(1)}, bf16[2048,3072]{1,0:T(8,128)(2,1)}, u32[]{:S(2)}) copy-start(bf16[2048,3072]{1,0:T(8,128)(2,1)} %weight_ref.4) | copy-start | bytes 37748740
  29.4 1.4 copy-start.8
  30.8 0.8 copy-start.11
  47.3 22.2 %collective-permute-start.2 = (bf16[4,592,128]{2,1,0:T(8,128)(2,1)S(1)}, bf16[4,592,128]{2,1,0:T(8,128)(2,1)}, u32[]{:S(2)}, u32[]{:S(2)}) collective-permute-start(bf16[4,592,128]{2,1,0:T(8,128)(2,1)S(1)} %all_to_all.25.query_ref), channel_id=1, source_target_pairs={{0,4},{4,8},{8,12},{12,0},{1,5},{5,9},{9,13},{13,1},{2,6},{6,10},{... | collective-permute-start | bytes 1818632 | tf_op jit(solution)/shard_map/queries/ppermute | solution.py:467
  49.2 23.1 %collective-permute-start = (bf16[4,592,128]{2,1,0:T(8,128)(2,1)S(1)}, bf16[4,592,128]{2,1,0:T(8,128)(2,1)}, u32[]{:S(2)}, u32[]{:S(2)}) collective-permute-start(bf16[4,592,128]{2,1,0:T(8,128)(2,1)S(1)} %all_to_all.25.query_ref), channel_id=1, source_target_pairs={{0,12},{4,0},{8,4},{12,8},{1,13},{5,1},{9,5},{13,9},{2,14},{6,2},{... | collective-permute-start | bytes 1818632 | tf_op jit(solution)/shard_map/queries/ppermute | solution.py:468
  51.4 4.8 %copy-start.5 = (bf16[2048,3072]{1,0:T(8,128)(2,1)S(1)}, bf16[2048,3072]{1,0:T(8,128)(2,1)}, u32[]{:S(2)}) copy-start(bf16[2048,3072]{1,0:T(8,128)(2,1)} %weight_ref.4) | copy-start | bytes 37748740
  56.2 1.8 %copy-start.9 = (bf16[576,2048]{1,0:T(8,128)(2,1)S(1)}, bf16[576,2048]{1,0:T(8,128)(2,1)}, u32[]{:S(2)}) copy-start(bf16[576,2048]{1,0:T(8,128)(2,1)} %copy-done.8) | copy-start | bytes 7077892
  63.9 1.2 copy-start.6
  65.1 60.4 %all-to-all-start.2 = ((bf16[16,3,144,128]{3,2,1,0:T(8,128)(2,1)}), bf16[16,3,144,128]{3,2,1,0:T(8,128)(2,1)}, u32[]{:S(2)}, u32[]{:S(2)}) async-start(bf16[16,3,144,128]{3,2,1,0:T(8,128)(2,1)} %bitcast.18), calls=%async_computation.2 | async-start | bytes 3538944 | tf_op jit(solution)/shard_map/temporal/all_to_all | solution.py:433
  70.5 25.8 %collective-permute-start.3 = (bf16[2,592,128]{2,1,0:T(8,128)(2,1)S(1)}, bf16[2,592,128]{2,1,0:T(8,128)(2,1)S(1)}, u32[]{:S(2)}, u32[]{:S(2)}) collective-permute-start(bf16[2,592,128]{2,1,0:T(8,128)(2,1)S(1)} %slice.48), channel_id=1, source_target_pairs={{0,4},{4,8},{8,12},{12,0},{1,5},{5,9},{9,13},{13,1},{2,6},{6,10},{... | collective-permute-start | bytes 909320 | tf_op jit(solution)/shard_map/queries/ppermute | solution.py:470
  73.3 23.0 %collective-permute-start.1 = (bf16[2,592,128]{2,1,0:T(8,128)(2,1)S(1)}, bf16[2,592,128]{2,1,0:T(8,128)(2,1)S(1)}, u32[]{:S(2)}, u32[]{:S(2)}) collective-permute-start(bf16[2,592,128]{2,1,0:T(8,128)(2,1)S(1)} %slice.46), channel_id=1, source_target_pairs={{0,12},{4,0},{8,4},{12,8},{1,13},{5,1},{9,5},{13,9},{2,14},{6,2},{... | collective-permute-start | bytes 909320 | tf_op jit(solution)/shard_map/queries/ppermute | solution.py:471
  96.4 0.7 copy-start.13
  97.1 2.3 %copy-start = (bf16[64,144,256]{2,1,0:T(8,128)(2,1)S(1)}, bf16[64,144,256]{2,1,0:T(8,128)(2,1)}, u32[]{:S(2)}) copy-start(bf16[64,144,256]{2,1,0:T(8,128)(2,1)} %all-gather.2.cloned.1.call-done.refs_0_.refs_1_.refs_2_.refs_3_.refs_4_.refs_5_) | copy-start | bytes 14155780
  99.4 1.5 copy-start.7
  100.9 3.3 %copy-start.1 = (bf16[64,144,256]{2,1,0:T(8,128)(2,1)S(1)}, bf16[64,144,256]{2,1,0:T(8,128)(2,1)}, u32[]{:S(2)}) copy-start(bf16[64,144,256]{2,1,0:T(8,128)(2,1)} %all-gather.2.cloned.1.call-done.refs_0_.refs_1_.refs_2_.refs_3_.refs_4_.refs_5_) | copy-start | bytes 14155780
  100.9 3.3 %copy-start.14 = (bf16[2,592,128]{2,1,0:T(8,128)(2,1)S(1)}, bf16[2,592,128]{2,1,0:T(8,128)(2,1)}, u32[]{:S(2)}) copy-start(bf16[2,592,128]{2,1,0:T(8,128)(2,1)} %copy-done.13) | copy-start | bytes 909316
  103.0 7.7 %collective-permute-start.5 = (bf16[2,592,128]{2,1,0:T(8,128)(2,1)S(1)}, bf16[2,592,128]{2,1,0:T(8,128)(2,1)S(1)}, u32[]{:S(2)}, u32[]{:S(2)}) collective-permute-start(bf16[2,592,128]{2,1,0:T(8,128)(2,1)S(1)} %memory_attend.5.refs_6_), channel_id=1, source_target_pairs={{0,12},{4,0},{8,4},{12,8},{1,13},{5,1},{9,5},{13,9},{2,14},{6,2},{... | collective-permute-start | bytes 909320 | tf_op jit(solution)/shard_map/memory/ppermute | solution.py:480
  106.3 9.8 %collective-permute-start.4 = (bf16[2,592,128]{2,1,0:T(8,128)(2,1)S(1)}, bf16[2,592,128]{2,1,0:T(8,128)(2,1)S(1)}, u32[]{:S(2)}, u32[]{:S(2)}) collective-permute-start(bf16[2,592,128]{2,1,0:T(8,128)(2,1)S(1)} %memory_attend.6.refs_7_), channel_id=1, source_target_pairs={{0,4},{4,8},{8,12},{12,0},{1,5},{5,9},{9,13},{13,1},{2,6},{6,10},{... | collective-permute-start | bytes 909320 | tf_op jit(solution)/shard_map/memory/ppermute | solution.py:481
  121.6 18.7 %collective-permute-start.7 = (bf16[4,592,128]{2,1,0:T(8,128)(2,1)}, bf16[4,592,128]{2,1,0:T(8,128)(2,1)}, u32[]{:S(2)}, u32[]{:S(2)}) collective-permute-start(bf16[4,592,128]{2,1,0:T(8,128)(2,1)} %memory_attend.8._), channel_id=1, source_target_pairs={{0,4},{4,8},{8,12},{12,0},{1,5},{5,9},{9,13},{13,1},{2,6},{6,10},{... | collective-permute-start | bytes 1818632 | tf_op jit(solution)/shard_map/memory/ppermute | solution.py:485
  123.0 19.8 %collective-permute-start.6 = (bf16[4,592,128]{2,1,0:T(8,128)(2,1)}, bf16[4,592,128]{2,1,0:T(8,128)(2,1)}, u32[]{:S(2)}, u32[]{:S(2)}) collective-permute-start(bf16[4,592,128]{2,1,0:T(8,128)(2,1)} %memory_attend.7.refs_7_), channel_id=1, source_target_pairs={{0,12},{4,0},{8,4},{12,8},{1,13},{5,1},{9,5},{13,9},{2,14},{6,2},{... | collective-permute-start | bytes 1818632 | tf_op jit(solution)/shard_map/memory/ppermute | solution.py:483
  129.0 16.0 %all-to-all-start.4 = ((bf16[16,144,128]{2,1,0:T(8,128)(2,1)}), bf16[16,144,128]{2,1,0:T(8,128)(2,1)S(1)}, u32[]{:S(2)}, u32[]{:S(2)}) async-start(bf16[16,144,128]{2,1,0:T(8,128)(2,1)} %temporal_attend.1.refs_6_), calls=%async_computation.4 | async-start | bytes 1179648 | tf_op jit(solution)/shard_map/temporal/all_to_all | solution.py:433
  134.2 2.3 %copy-start.2 = (bf16[64,144,256]{2,1,0:T(8,128)(2,1)S(1)}, bf16[64,144,256]{2,1,0:T(8,128)(2,1)}, u32[]{:S(2)}) copy-start(bf16[64,144,256]{2,1,0:T(8,128)(2,1)} %all-gather.2.cloned.1.call-done.refs_0_.refs_1_.refs_2_.refs_3_.refs_4_.refs_5_) | copy-start | bytes 14155780
  156.9 2.2 %copy-start.10 = (bf16[1024,2048]{1,0:T(8,128)(2,1)S(1)}, bf16[1024,2048]{1,0:T(8,128)(2,1)}, u32[]{:S(2)}) copy-start(bf16[1024,2048]{1,0:T(8,128)(2,1)} %weight_ref.5) | copy-start | bytes 12582916
Sparse Core Ops, SparseCore 0:
  32.8 37.1 all-gather.1

commit v3 on v2

v3 whole, which is shorter than its diff:
```python
import functools

import jax
import jax.numpy as jnp
from jax import lax
from jax.experimental import pallas as pl
from jax.experimental.pallas import tpu as pltpu
from jax.sharding import Mesh
from jax.sharding import PartitionSpec as P

G = 4
C = 128
HW = G * C
TOPM = 6
EPSILON = 1e-06
BF = jnp.bfloat16
F32 = jnp.float32
PAD = 16
VMEM_LIMIT = 28 * 1024 * 1024
ANY = pl.BlockSpec(memory_space=pl.ANY)
HBM = pl.BlockSpec(memory_space=pltpu.HBM)
WHOLE = pl.BlockSpec(memory_space=pltpu.VMEM)
SCALARS = pl.BlockSpec(memory_space=pltpu.SMEM)


def params(**more):
    return pltpu.CompilerParams(vmem_limit_bytes=VMEM_LIMIT, **more)


def cost(flops, bytes_accessed):
    return pl.CostEstimate(
        flops=flops // 16, bytes_accessed=bytes_accessed // 16, transcendentals=0
    )


def in_hbm(array):
    return pltpu.with_memory_space_constraint(array, pltpu.HBM)


def inverse_rms(values):
    return lax.rsqrt(jnp.mean(values * values, axis=-1, keepdims=True) + EPSILON)


def dot(a, b):
    return jnp.dot(a, b, preferred_element_type=F32)


def dot_t(a, b):
    return lax.dot_general(a, b, (((1,), (1,)), ((), ())), preferred_element_type=F32)


def split_store_kernel(rows_ref, out_ref):
    for h in range(G):
        key = rows_ref[:, h * C : (h + 1) * C].astype(F32)
        out_ref[h, :, :C] = (key * inverse_rms(key)).astype(BF)
        out_ref[h, :, C:] = rows_ref[:, HW + h * C : HW + (h + 1) * C]


def split_store(rows):
    n = rows.shape[0]
    return pl.pallas_call(
        split_store_kernel,
        out_shape=jax.ShapeDtypeStruct((G, n, 2 * C), BF),
        compiler_params=params(),
        name="split_store",
        cost_estimate=cost(8 * n * HW, 8 * n * HW),
    )(rows)


def join_pieces_kernel(piece, in_ref, _, out_ref, wide_ref, joined_ref):
    pieces = in_ref.shape[0]
    wide_ref[...] = in_ref[...].astype(F32)
    for m in range(out_ref.shape[0]):
        for i in range(pieces):
            joined_ref[m, i * piece : (i + 1) * piece, :] = wide_ref[
                i, m * piece : (m + 1) * piece, :
            ]
    out_ref[...] = joined_ref[...].astype(BF)


def join_pieces(parts, frames, after):
    pieces, rows, width = parts.shape
    piece = rows // frames
    return pl.pallas_call(
        functools.partial(join_pieces_kernel, piece),
        in_specs=[WHOLE, ANY],
        out_shape=jax.ShapeDtypeStruct((frames, pieces * piece, width), BF),
        scratch_shapes=[
            pltpu.VMEM((pieces, rows, width), F32),
            pltpu.VMEM((frames, pieces * piece, width), F32),
        ],
        compiler_params=params(),
        name="join_pieces",
        cost_estimate=cost(parts.size, 4 * parts.size),
    )(parts, after)


def modulate_kernel(
    act_hbm, affine_ref, weight_hbm, factor_ref, tail_ref, _, hidden_ref, query_ref,
    act_ref, weight_ref, act_sem, weight_sem,
):
    steps, rows, _ = act_ref.shape
    patches = query_ref.shape[1] - PAD
    loads = [
        pltpu.make_async_copy(act_hbm.at[pl.ds(i * rows, rows), :], act_ref.at[i], act_sem.at[i])
        for i in range(steps)
    ]
    weight_load = pltpu.make_async_copy(weight_hbm.at[:, pl.ds(0, HW)], weight_ref, weight_sem)
    loads[0].start()
    weight_load.start()
    for load in loads[1:]:
        load.start()
    for h in range(G):
        query_ref[h, patches:, :] = tail_ref[...]
    for i in range(steps):
        at = slice(i * rows, (i + 1) * rows)
        loads[i].wait()
        act = act_ref[i].astype(F32)
        hidden = act * inverse_rms(act) * (1.0 + affine_ref[0:1, :]) + affine_ref[1:2, :]
        hidden = hidden.astype(BF)
        hidden_ref[at, :] = hidden
        if i == 0:
            weight_load.wait()
        mapped = dot(hidden, weight_ref[...]).astype(BF).astype(F32)
        for h in range(G):
            one = mapped[:, h * C : (h + 1) * C]
            query_ref[h, at, :] = (one * inverse_rms(one) * factor_ref[0, h]).astype(BF)


def modulate(act, affine, weight, factor, tail, after):
    patches, depth = act.shape
    steps = 2
    rows = patches // steps
    return pl.pallas_call(
        modulate_kernel,
        in_specs=[HBM, WHOLE, HBM, SCALARS, WHOLE, ANY],
        out_specs=[WHOLE, WHOLE],
        out_shape=[
            jax.ShapeDtypeStruct((patches, depth), BF),
            jax.ShapeDtypeStruct((G, patches + PAD, C), BF),
        ],
        scratch_shapes=[
            pltpu.VMEM((steps, rows, depth), BF),
            pltpu.VMEM((depth, HW), BF),
            pltpu.SemaphoreType.DMA((steps,)),
            pltpu.SemaphoreType.DMA,
        ],
        compiler_params=params(),
        name="modulate",
        cost_estimate=cost(
            2 * patches * depth * HW, 4 * patches * depth + 2 * depth * HW + 2 * patches * HW
        ),
    )(in_hbm(act), affine, in_hbm(weight), factor, tail, after)


def temporal_entry_kernel(
    quarters, hidden_ref, weight_hbm, factor_ref, _, out_ref, weight_ref, sem
):
    rows = hidden_ref.shape[0] // quarters
    loads = [
        pltpu.make_async_copy(
            weight_hbm.at[:, pl.ds((3 + part) * HW, HW)], weight_ref.at[part], sem.at[part]
        )
        for part in range(3)
    ]
    for load in loads:
        load.start()
    for part in range(3):
        loads[part].wait()
        mapped = dot(hidden_ref[...], weight_ref[part]).astype(BF)
        for h in range(G):
            done = mapped[:, h * C : (h + 1) * C]
            if part < 2:
                one = done.astype(F32)
                one = one * inverse_rms(one)
                if part == 0:
                    one = one * factor_ref[1, h]
                done = one.astype(BF)
            for z in range(quarters):
                out_ref[z, h, part] = done[z * rows : (z + 1) * rows, :]


def temporal_entry(hidden, weight, factor, quarters, after):
    patches, depth = hidden.shape
    rows = patches // quarters
    return pl.pallas_call(
        functools.partial(temporal_entry_kernel, quarters),
        in_specs=[WHOLE, HBM, SCALARS, ANY],
        out_specs=WHOLE,
        out_shape=jax.ShapeDtypeStruct((quarters, G, 3, rows, C), BF),
        scratch_shapes=[pltpu.VMEM((3, depth, HW), BF), pltpu.SemaphoreType.DMA((3,))],
        compiler_params=params(),
        name="temporal_entry",
        cost_estimate=cost(
            6 * patches * depth * HW, 2 * patches * depth + 6 * depth * HW + 6 * patches * HW
        ),
    )(hidden, in_hbm(weight), factor, after)


def temporal_attend_kernel(length_ref, in_ref, _, out_ref):
    frames, _, rows, _ = in_ref.shape
    group = 16
    size = frames * group
    length = length_ref[0]
    row = lax.broadcasted_iota(jnp.int32, (size, size), 0)
    column = lax.broadcasted_iota(jnp.int32, (size, size), 1)
    target, source = row // group, column // group
    keep = (row % group == column % group) & (source <= target) & (source > target - length)
    for g in range(rows // group):
        at = slice(g * group, (g + 1) * group)
        query = in_ref[:, 0, at, :].reshape(size, C)
        key = in_ref[:, 1, at, :].reshape(size, C)
        value = in_ref[:, 2, at, :].reshape(size, C)
        weights = jnp.where(keep, jnp.exp(dot_t(query, key)), 0.0)
        shares = weights / jnp.sum(weights, axis=-1, keepdims=True)
        result = dot(shares.astype(BF), value).astype(BF)
        out_ref[:, at, :] = result.reshape(frames, group, C)


def temporal_attend(length, parts, after):
    frames, _, rows, _ = parts.shape
    return pl.pallas_call(
        temporal_attend_kernel,
        in_specs=[SCALARS, WHOLE, ANY],
        out_shape=jax.ShapeDtypeStruct((frames, rows, C), BF),
        compiler_params=params(),
        name="temporal_attend",
        cost_estimate=cost(4 * frames * rows * 256 * C, 8 * frames * rows * C),
    )(length, parts, after)


def own_attend_kernel(hidden_ref, weight_hbm, query_ref, _, out_ref, weight_ref, sem):
    patches = hidden_ref.shape[0]
    loads = [
        pltpu.make_async_copy(
            weight_hbm.at[:, pl.ds((1 + part) * HW, HW)], weight_ref.at[part], sem.at[part]
        )
        for part in range(2)
    ]
    for load in loads:
        load.start()
    loads[0].wait()
    keys = dot(hidden_ref[...], weight_ref[0]).astype(BF)
    loads[1].wait()
    values = dot(hidden_ref[...], weight_ref[1]).astype(BF)
    ones = jnp.ones((patches, C), BF)
    for h in range(G):
        key = keys[:, h * C : (h + 1) * C].astype(F32)
        key = (key * inverse_rms(key)).astype(BF)
        both = jnp.concatenate([values[:, h * C : (h + 1) * C], ones], axis=1)
        weights = jnp.exp(dot_t(query_ref[h, :patches, :], key)).astype(BF)
        out_ref[h] = dot(weights, both)


def own_attend(hidden, weight, query, after):
    patches, depth = hidden.shape
    return pl.pallas_call(
        own_attend_kernel,
        in_specs=[WHOLE, HBM, WHOLE, ANY],
        out_specs=WHOLE,
        out_shape=jax.ShapeDtypeStruct((G, patches, 2 * C), F32),
        scratch_shapes=[pltpu.VMEM((2, depth, HW), BF), pltpu.SemaphoreType.DMA((2,))],
        compiler_params=params(),
        name="own_attend",
        cost_estimate=cost(
            4 * patches * depth * HW + 6 * patches * patches * HW,
            2 * patches * depth + 4 * depth * HW + 10 * patches * HW,
        ),
    )(hidden, in_hbm(weight), query, after)


LINE = 96


def halves(denominators):
    high = denominators.astype(BF).astype(F32)
    return jnp.concatenate([high, denominators - high], axis=0).astype(BF)


def memory_attend_kernel(carried, index_ref, query_ref, store_ref, *refs):
    out_ref = refs[-1]
    frames = query_ref.shape[0]
    patches = query_ref.shape[1] - PAD
    chunk = 3 * LINE
    row = lax.broadcasted_iota(jnp.int32, (LINE, C), 0)
    column = lax.broadcasted_iota(jnp.int32, (LINE, C), 1)
    for i in range(frames):
        blocks = [store_ref[index_ref[i, j]] for j in range(TOPM)]
        keys = jnp.concatenate([block[:, :C] for block in blocks], axis=0)
        values = jnp.concatenate([block[:, C:] for block in blocks], axis=0)
        both = jnp.concatenate([values, jnp.ones(values.shape, BF)], axis=1)
        carry = None
        if carried is not None and carried[0] <= i < carried[1]:
            carry = refs[0].at[i - carried[0]]
        lines = []
        for start in range(0, patches, chunk):
            at = slice(start, start + chunk)
            weights = jnp.exp(dot_t(query_ref[i, at, :], keys)).astype(BF)
            result = dot(weights, both)
            top = result[:, :C]
            if carry is not None:
                top = top + carry[at, :].astype(F32)
            out_ref[i, at, :] = top.astype(BF)
            for j in range(0, chunk, LINE):
                diagonal = jnp.where(row == column, result[j : j + LINE, C:], 0.0)
                lines.append(jnp.sum(diagonal, axis=0, keepdims=True))
        lines.append(jnp.zeros((8 - len(lines), C), F32))
        total = jnp.concatenate(lines, axis=0)
        if carry is not None:
            tail = carry[patches:, :].astype(F32)
            total = total + tail[:8] + tail[8:]
        out_ref[i, patches:, :] = halves(total)


def memory_attend(query, store, after, carry=None, first=0):
    frames, rows, _ = query.shape
    patches = rows - PAD
    quarter = store.shape[1]
    index = query[:, patches, :TOPM].astype(jnp.int32)
    carried, extra = None, []
    if carry is not None:
        carried, extra = (first, first + carry.shape[0]), [carry]
    return pl.pallas_call(
        functools.partial(memory_attend_kernel, carried),
        in_specs=[SCALARS, WHOLE, WHOLE] + [WHOLE] * len(extra) + [ANY],
        out_specs=WHOLE,
        out_shape=jax.ShapeDtypeStruct(query.shape, BF),
        compiler_params=params(),
        name="memory_attend",
        cost_estimate=cost(
            8 * frames * patches * TOPM * quarter * C,
            4 * query.size + 4 * frames * TOPM * quarter * C,
        ),
    )(index, query, store, *extra, after)


def add_partials_kernel(*refs):
    ins, out_ref = refs[:-1], refs[-1]
    patches = out_ref.shape[1] - PAD
    total = ins[0][:, :patches, :].astype(F32)
    tail = ins[0][:, patches:, :].astype(F32)
    for ref in ins[1:]:
        total += ref[:, :patches, :].astype(F32)
        tail += ref[:, patches:, :].astype(F32)
    out_ref[:, :patches, :] = total.astype(BF)
    for i in range(out_ref.shape[0]):
        out_ref[i, patches:, :] = halves(tail[i, :8] + tail[i, 8:])


def add_partials(parts):
    return pl.pallas_call(
        add_partials_kernel,
        out_shape=jax.ShapeDtypeStruct(parts[0].shape, BF),
        compiler_params=params(),
        name="add_partials",
        cost_estimate=cost(4 * parts[0].size, 8 * parts[0].size),
    )(*parts)


def leave_kernel(
    own_ref, memory_ref, time_ref, weight_hbm, out_hbm,
    combined_ref, weight_ref, out_ref, load_sem, store_sem,
):
    patches = own_ref.shape[1]
    quarters = time_ref.shape[0] // G
    rows = time_ref.shape[1]
    steps, _, width = weight_ref.shape
    loads, stores = [], []
    for i in range(steps):
        at = pl.ds(i * width, width)
        loads.append(
            pltpu.make_async_copy(weight_hbm.at[:, at], weight_ref.at[i], load_sem.at[i])
        )
        stores.append(pltpu.make_async_copy(out_ref.at[i], out_hbm.at[:, at], store_sem.at[i]))
    for load in loads:
        load.start()
    row = lax.broadcasted_iota(jnp.int32, (LINE, C), 0)
    column = lax.broadcasted_iota(jnp.int32, (LINE, C), 1)
    for h in range(G):
        tail = memory_ref[h, patches:, :].astype(F32)
        denominators = tail[:8] + tail[8:]
        for j in range(patches // LINE):
            at = slice(j * LINE, (j + 1) * LINE)
            line = jnp.broadcast_to(denominators[j : j + 1, :], (LINE, C))
            memory_sum = jnp.sum(jnp.where(row == column, line, 0.0), axis=1, keepdims=True)
            top = own_ref[h, at, :C] + memory_ref[h, at, :].astype(F32)
            combined_ref[at, h * C : (h + 1) * C] = (
                top / (own_ref[h, at, C:] + memory_sum)
            ).astype(BF)
        for z in range(quarters):
            combined_ref[z * rows : (z + 1) * rows, HW + h * C : HW + (h + 1) * C] = time_ref[
                z * G + h
            ]
    for i in range(steps):
        loads[i].wait()
        out_ref[i] = dot(combined_ref[...], weight_ref[i]).astype(BF)
        stores[i].start()
    for store in stores:
        store.wait()


def leave(own, memory, time, weight):
    patches = own.shape[1]
    depth, width = weight.shape
    steps = 4
    step = width // steps
    return pl.pallas_call(
        leave_kernel,
        in_specs=[WHOLE, WHOLE, WHOLE, HBM],
        out_specs=HBM,
        out_shape=jax.ShapeDtypeStruct((patches, width), BF),
        scratch_shapes=[
            pltpu.VMEM((patches, depth), BF),
            pltpu.VMEM((steps, depth, step), BF),
            pltpu.VMEM((steps, patches, step), BF),
            pltpu.SemaphoreType.DMA((steps,)),
            pltpu.SemaphoreType.DMA((steps,)),
        ],
        compiler_params=params(),
        name="leave",
        cost_estimate=cost(
            2 * patches * depth * width,
            2 * depth * width + 2 * patches * width + 6 * patches * depth,
        ),
    )(own, memory, time, in_hbm(weight))


def on_device(
    patch_activation_tensor,
    conditioning_affine,
    entry_projection_matrix,
    exit_projection_matrix,
    softmax_sharpness,
    cached_past_pairs,
    recalled_picture_holder,
    recalled_picture_position,
    lookback_lengths,
):
    rings = lax.axis_size("z")
    patches, depth = patch_activation_tensor.shape[2:]
    held, piece = cached_past_pairs.shape[:2]
    up = [(s, (s + 1) % rings) for s in range(rings)]
    down = [(s, (s - 1) % rings) for s in range(rings)]

    def swap(blocks, axes):
        return lax.all_to_all(blocks, axes, split_axis=0, concat_axis=0, tiled=True)

    with jax.named_scope("store"):
        split = split_store(cached_past_pairs.reshape(held * piece, 2 * HW))
        pieces = swap(split, "x")

    with jax.named_scope("queries"):
        factor = softmax_sharpness / C
        index = recalled_picture_holder.reshape(TOPM) * held + recalled_picture_position.reshape(
            TOPM
        )
        tail = jnp.zeros((PAD, C), BF).at[0, :TOPM].set(index.astype(BF))
        hidden, query = modulate(
            patch_activation_tensor.reshape(patches, depth),
            conditioning_affine.reshape(2, depth),
            entry_projection_matrix,
            factor,
            tail,
            after=split,
        )
        here = swap(query, "x")

    with jax.named_scope("store"):
        joined = join_pieces(pieces, held, after=hidden)
        store = lax.all_gather(joined, ("y", "c"), axis=0, tiled=True)

    with jax.named_scope("own"):
        own = own_attend(hidden, entry_projection_matrix, query, after=joined)

    with jax.named_scope("queries"):
        half = here.shape[0] // 2
        below = lax.ppermute(here, "z", up)
        above = lax.ppermute(here, "z", down)
        far_first = lax.ppermute(below[:half], "z", up)
        far_last = lax.ppermute(above[half:], "z", down)

    with jax.named_scope("temporal"):
        parts = temporal_entry(hidden, entry_projection_matrix, factor, rings, after=own)
        parts, far_first, far_last = lax.optimization_barrier((parts, far_first, far_last))
        sent = swap(parts.reshape((rings * G,) + parts.shape[2:]), ("z", "x"))

    with jax.named_scope("memory"):
        sum_first = memory_attend(far_first, store, parts)
        carry_first = lax.ppermute(sum_first, "z", down)
        sum_last = memory_attend(far_last, store, sum_first)
        carry_last = lax.ppermute(sum_last, "z", up)
        sum_below = memory_attend(below, store, sum_last, carry=carry_first, first=0)
        from_above = lax.ppermute(sum_below, "z", down)
        sum_above = memory_attend(above, store, sum_below, carry=carry_last, first=half)
        from_below = lax.ppermute(sum_above, "z", up)

    with jax.named_scope("temporal"):
        timed = temporal_attend(lookback_lengths, sent, after=sum_above)
        time = swap(timed, ("z", "x"))

    with jax.named_scope("memory"):
        sum_here = memory_attend(here, store, timed)
        memory = swap(add_partials([sum_here, from_above, from_below]), "x")

    with jax.named_scope("exit"):
        attended = leave(own, memory, time, exit_projection_matrix)
    return attended.reshape(1, 1, patches, depth)


def solution(mesh):
    apart = Mesh(mesh.devices.reshape(4, 2, 4, 4), ("y", "c", "z", "x"))
    roll, frame = ("y", "c"), ("z", "x")
    return jax.shard_map(
        on_device,
        mesh=apart,
        in_specs=(
            P(roll, frame, None, None),
            P(roll, frame, None, None),
            P(),
            P(),
            P(),
            P(roll, frame, None, None),
            P(roll, frame, None, None),
            P(roll, frame, None),
            P(roll),
        ),
        out_specs=P(roll, frame, None, None),
        check_vma=False,
    )
```

time: 172 us -> 163 us (0.948)
  local copies, waits for them, and re-layouts: 30 us -> 14.8 us
  waiting for transfers between devices: 26.7 us -> 32.7 us
    ppermute x1, waiting for transfers between devices: 21.5 us -> 0.01 us  [on_device(): far_first = lax.ppermute(below[:half], 'z', up)]
    unnamed x39 -> x41, local copies, waits for them, and re-layouts: 28 us -> 14.8 us
    ppermute x1, waiting for transfers between devices: 0.01 us -> 11.3 us  [on_device(): below = lax.ppermute(here, 'z', up)]
    ppermute x1, waiting for transfers between devices: 1.98 us -> 12.1 us  [on_device(): carry_first = lax.ppermute(sum_first, 'z', down)]
    all_to_all x3, waiting for transfers between devices: 0.7 us -> 5.51 us  [swap(): return lax.all_to_all(blocks, axes, split_axis=0, concat_axis=0, tiled=True)]
    ppermute x1, starting transfers between devices: 1.18 us -> 3.09 us  [on_device(): carry_first = lax.ppermute(sum_first, 'z', down)]
    ppermute x1, starting transfers between devices: 1.84 us -> 0.08 us  [on_device(): far_first = lax.ppermute(below[:half], 'z', up)]
  transfers between devices with their start and end apart: 12 -> 12, of which waited for: 5 -> 5; matrix products, arithmetic and copies ran while one was open for 2% -> 0% of each run, Pallas kernels for 22% -> 23%
where the time goes in v3:
time: 163 us; the launch traced here: 162 us
  Pallas kernels  45.4 us (28%)
  waiting for transfers between devices  32.7 us (20%)
  starting transfers between devices  28.1 us (17%)
  blocking collectives  26.1 us (16%)
  local copies, waits for them, and re-layouts  14.8 us (9%)
  between operations  14.3 us (9%)
    all_to_all x2, blocking collectives, swap(): return lax.all_to_all(blocks, axes, split_axis=0, concat_axis=0, tiled=True)  26.1 us
    unnamed x41, local copies, waits for them, and re-layouts  14.8 us
    pallas_call x5, Pallas kernels, memory_attend(): pl.pallas_call(functools.partial(memory_attend_kernel, carried), in_specs...  14.6 us
    all_to_all x3, starting transfers between devices, swap(): return lax.all_to_all(blocks, axes, split_axis=0, concat_axis=0, tiled=True)  14.5 us
    ppermute x1, waiting for transfers between devices, on_device(): carry_first = lax.ppermute(sum_first, 'z', down)  12.1 us
    ppermute x1, waiting for transfers between devices, on_device(): below = lax.ppermute(here, 'z', up)  11.3 us
    pallas_call x1, Pallas kernels, temporal_entry(): pl.pallas_call(functools.partial(temporal_entry_kernel, quarters), in_spe...  6.8 us
    pallas_call x1, Pallas kernels, own_attend(): pl.pallas_call(own_attend_kernel, in_specs=[WHOLE, HBM, WHOLE, ANY], out_...  6.68 us
  transfers between devices with their start and end apart: 12, of which 5 were waited for; matrix products, arithmetic and copies ran while one was open for 0% of the time, Pallas kernels for 23%

profile of v3, /device:TPU:0, one launch (start us, length us, event | category | flops | bytes accessed | tf_op | source)
XLA Modules:
  0.0 162.1 jit_solution(16069357700075411135)
XLA Ops:
  6.5 1.2 copy.10
  7.7 1.1 split_store.1._
  8.8 4.4 %all-to-all-start = ((bf16[4,288,256]{2,1,0:T(8,128)(2,1)}), bf16[4,288,256]{2,1,0:T(8,128)(2,1)S(1)}, u32[]{:S(2)}, u32[]{:S(2)}) async-start(bf16[4,288,256]{2,1,0:T(8,128)(2,1)} %split_store.1._), calls=%async_computation | async-start | bytes 1179648 | tf_op jit(solution)/shard_map/store/all_to_all | solution.py:446
  13.2 0.0 all-gather.2.cloned.1.call-start
  13.2 0.0 copy-done.19
  13.2 0.0 copy-done.18
  13.2 0.0 copy-done.17
  13.3 0.0 copy-done.16
  13.3 4.9 %modulate.1 = (bf16[576,2048]{1,0:T(8,128)(2,1)S(1)}, bf16[4,592,128]{2,1,0:T(8,128)(2,1)S(1)}) custom-call(bf16[576,2048]{1,0:T(8,128)(2,1)} %bitcast.26, f32[2,2048]{1,0:T(2,128)S(1)} %bitcast.20, bf16[2048,3072]{1,0:T(8,128)(2,1)} %weight_hbm.6, f32[2,4]{1,0:T(2,128)S(1)} %broadcast_multiply_fusion.factor_ref, bf16[16,128]{1,0:T(8,128)(2,1)S(1)} %scatter.4.tail_ref, ...), custom_call_target="tpu_custom_call" | custom-call | flops 75497472 | bytes 462848 | tf_op jit(solution)/shard_map/queries/modulate/pallas_call | solution.py:134
  18.2 0.0 copy-start.8
  18.2 0.9 copy-done.8
  19.1 4.3 %all-to-all-done.in_ref = bf16[4,288,256]{2,1,0:T(8,128)(2,1)S(1)} async-done(((bf16[4,288,256]{2,1,0:T(8,128)(2,1)}), bf16[4,288,256]{2,1,0:T(8,128)(2,1)S(1)}, u32[]{:S(2)}, u32[]{:S(2)}) %all-to-all-start) | async-done | bytes 589856 | tf_op jit(solution)/shard_map/store/all_to_all | solution.py:446
  23.4 1.1 join_pieces.1._
  24.4 0.0 all-gather.2.cloned.1.call-update
  24.5 12.9 %all_to_all.25.query_ref = bf16[4,592,128]{2,1,0:T(8,128)(2,1)S(1)} all-to-all(bf16[4,592,128]{2,1,0:T(8,128)(2,1)} %copy-done.8), channel_id=1, replica_groups=mesh['y'=4,'c'=2,'z'=4,'x'=4] {'x'}, dimensions={0} | all-to-all | bytes 1212416 | tf_op jit(solution)/shard_map/queries/all_to_all | solution.py:446
  37.4 0.0 copy-done.3
  37.4 1.9 %collective-permute-start = (bf16[4,592,128]{2,1,0:T(8,128)(2,1)S(1)}, bf16[4,592,128]{2,1,0:T(8,128)(2,1)S(1)}, u32[]{:S(2)}, u32[]{:S(2)}) collective-permute-start(bf16[4,592,128]{2,1,0:T(8,128)(2,1)S(1)} %all_to_all.25.query_ref), channel_id=1, source_target_pairs={{0,4},{4,8},{8,12},{12,0},{1,5},{5,9},{9,13},{13,1},{2,6},{6,10},{... | collective-permute-start | bytes 1818632 | tf_op jit(solution)/shard_map/queries/ppermute | solution.py:477
  39.3 2.1 %collective-permute-start.2 = (bf16[4,592,128]{2,1,0:T(8,128)(2,1)S(1)}, bf16[4,592,128]{2,1,0:T(8,128)(2,1)S(1)}, u32[]{:S(2)}, u32[]{:S(2)}) collective-permute-start(bf16[4,592,128]{2,1,0:T(8,128)(2,1)S(1)} %all_to_all.25.query_ref), channel_id=1, source_target_pairs={{0,12},{4,0},{8,4},{12,8},{1,13},{5,1},{9,5},{13,9},{2,14},{6,2},{... | collective-permute-start | bytes 1818632 | tf_op jit(solution)/shard_map/queries/ppermute | solution.py:478
  41.4 11.3 %collective-permute-done.query_ref = bf16[4,592,128]{2,1,0:T(8,128)(2,1)S(1)} collective-permute-done((bf16[4,592,128]{2,1,0:T(8,128)(2,1)S(1)}, bf16[4,592,128]{2,1,0:T(8,128)(2,1)S(1)}, u32[]{:S(2)}, u32[]{:S(2)}) %collective-permute-start) | collective-permute-done | bytes 606240 | tf_op jit(solution)/shard_map/queries/ppermute | solution.py:477
  52.7 0.1 collective-permute-start.1
  52.8 0.0 collective-permute-done.2.query_ref
  52.8 0.0 copy-start.10
  52.8 0.7 copy-done.12
  53.5 0.2 copy-done.10
  53.7 3.1 %collective-permute-start.3 = (bf16[2,592,128]{2,1,0:T(8,128)(2,1)S(1)}, bf16[2,592,128]{2,1,0:T(8,128)(2,1)S(1)}, u32[]{:S(2)}, u32[]{:S(2)}) collective-permute-start(bf16[2,592,128]{2,1,0:T(8,128)(2,1)S(1)} %slice.46), channel_id=1, source_target_pairs={{0,12},{4,0},{8,4},{12,8},{1,13},{5,1},{9,5},{13,9},{2,14},{6,2},{... | collective-permute-start | bytes 909320 | tf_op jit(solution)/shard_map/queries/ppermute | solution.py:480
  56.8 1.7 %copy-done.4 = bf16[576,2048]{1,0:T(8,128)(2,1)S(1)} copy-done((bf16[576,2048]{1,0:T(8,128)(2,1)S(1)}, bf16[576,2048]{1,0:T(8,128)(2,1)}, u32[]{:S(2)}) %copy-start.4) | copy-done | bytes 2359320
  58.6 1.1 copy-done.9
  59.6 6.7 %own_attend.1._.own_ref = f32[4,576,256]{2,1,0:T(8,128)S(1)} custom-call(bf16[576,2048]{1,0:T(8,128)(2,1)S(1)} %copy-done.4, bf16[2048,3072]{1,0:T(8,128)(2,1)} %weight_hbm.6, bf16[4,592,128]{2,1,0:T(8,128)(2,1)S(1)} %copy-done.9, bf16[8,144,256]{2,1,0:T(8,128)(2,1)} %join_pieces.1._), custom_call_target="tpu_custom_call" | custom-call | flops 214695936 | bytes 593920 | tf_op jit(solution)/shard_map/own/own_attend/pallas_call | solution.py:257
  66.3 0.0 copy-done.5
  66.3 6.8 %temporal_entry.1.refs_0_ = bf16[4,4,3,144,128]{4,3,2,1,0:T(8,128)(2,1)S(1)} custom-call(bf16[576,2048]{1,0:T(8,128)(2,1)S(1)} %copy-done.5, bf16[2048,3072]{1,0:T(8,128)(2,1)} %weight_hbm.6, f32[2,4]{1,0:T(2,128)S(1)} %broadcast_multiply_fusion.factor_ref, f32[4,576,256]{2,1,0:T(8,128)S(1)} %own_attend.1._.own_ref), custom_call_target="tpu_custom_call" | custom-call | flops 226492416 | bytes 651264 | tf_op jit(solution)/shard_map/temporal/temporal_entry/pallas_call | solution.py:186
  73.1 0.0 copy-start.6
  73.1 1.2 copy-done.6
  74.3 0.0 collective-permute-done.1.query_ref
  74.4 0.0 collective-permute-done.3.query_ref
  74.4 0.7 copy-done.14
  75.1 4.6 %all-to-all-start.2 = ((bf16[16,3,144,128]{3,2,1,0:T(8,128)(2,1)}), bf16[16,3,144,128]{3,2,1,0:T(8,128)(2,1)}, u32[]{:S(2)}, u32[]{:S(2)}) async-start(bf16[16,3,144,128]{3,2,1,0:T(8,128)(2,1)} %bitcast.18), calls=%async_computation.2 | async-start | bytes 3538944 | tf_op jit(solution)/shard_map/temporal/all_to_all | solution.py:446
  79.7 0.7 slice_convert_fusion.3
  80.4 2.3 %copy-done = bf16[64,144,256]{2,1,0:T(8,128)(2,1)S(1)} copy-done((bf16[64,144,256]{2,1,0:T(8,128)(2,1)S(1)}, bf16[64,144,256]{2,1,0:T(8,128)(2,1)}, u32[]{:S(2)}) %copy-start) | copy-done | bytes 4718616
  82.7 1.5 copy-done.7
  84.2 1.0 copy-done.15
  85.2 1.9 %memory_attend.5.refs_0_ = bf16[2,592,128]{2,1,0:T(8,128)(2,1)S(1)} custom-call(s32[2,6]{1,0:T(2,128)S(1)} %bitcast.25, bf16[2,592,128]{2,1,0:T(8,128)(2,1)S(1)} %copy-done.15, bf16[64,144,256]{2,1,0:T(8,128)(2,1)S(1)} %copy-done, bf16[4,4,3,144,128]{4,3,2,1,0:T(8,128)(2,1)S(1)} %copy-done.7), custom_call_target="tpu_custom_call" | custom-call | flops 63700992 | bytes 93184 | tf_op jit(solution)/shard_map/memory/memory_attend/pallas_call | solution.py:323
  87.1 3.1 %collective-permute-start.5 = (bf16[2,592,128]{2,1,0:T(8,128)(2,1)S(1)}, bf16[2,592,128]{2,1,0:T(8,128)(2,1)S(1)}, u32[]{:S(2)}, u32[]{:S(2)}) collective-permute-start(bf16[2,592,128]{2,1,0:T(8,128)(2,1)S(1)} %memory_attend.5.refs_0_), channel_id=1, source_target_pairs={{0,12},{4,0},{8,4},{12,8},{1,13},{5,1},{9,5},{13,9},{2,14},{6,2},{... | collective-permute-start | bytes 909320 | tf_op jit(solution)/shard_map/memory/ppermute | solution.py:489
  90.1 0.0 copy-done.1
  90.2 1.9 %memory_attend.6.refs_1_ = bf16[2,592,128]{2,1,0:T(8,128)(2,1)S(1)} custom-call(s32[2,6]{1,0:T(2,128)S(1)} %bitcast.24, bf16[2,592,128]{2,1,0:T(8,128)(2,1)S(1)} %collective-permute-done.3.query_ref, bf16[64,144,256]{2,1,0:T(8,128)(2,1)S(1)} %copy-done.1, bf16[2,592,128]{2,1,0:T(8,128)(2,1)S(1)} %memory_attend.5.refs_0_), custom_call_target="tpu_custom_call" | custom-call | flops 63700992 | bytes 93184 | tf_op jit(solution)/shard_map/memory/memory_attend/pallas_call | solution.py:323
  92.0 0.1 collective-permute-start.4
  92.1 0.0 copy-done.13
  92.2 12.1 %collective-permute-done.5.refs_0_ = bf16[2,592,128]{2,1,0:T(8,128)(2,1)S(1)} collective-permute-done((bf16[2,592,128]{2,1,0:T(8,128)(2,1)S(1)}, bf16[2,592,128]{2,1,0:T(8,128)(2,1)S(1)}, u32[]{:S(2)}, u32[]{:S(2)}) %collective-permute-start.5) | collective-permute-done | bytes 303136 | tf_op jit(solution)/shard_map/memory/ppermute | solution.py:489
  104.3 3.9 %memory_attend.7.refs_1_ = bf16[4,592,128]{2,1,0:T(8,128)(2,1)} custom-call(s32[4,6]{1,0:T(4,128)S(1)} %bitcast.22, bf16[4,592,128]{2,1,0:T(8,128)(2,1)S(1)} %copy-done.13, bf16[64,144,256]{2,1,0:T(8,128)(2,1)S(1)} %copy-done.1, bf16[2,592,128]{2,1,0:T(8,128)(2,1)S(1)} %collective-permute-done.5.refs_0_, bf16[2,592,128]{2,1,0:T(8,128)(2,1)S(1)} %memory_attend.6.refs_1_), custom_call_target="tpu_custom_call" | custom-call | flops 127401984 | bytes 186368 | tf_op jit(solution)/shard_map/memory/memory_attend/pallas_call | solution.py:323
  108.2 0.0 collective-permute-done.4.refs_0_
  108.2 4.0 %memory_attend.8._ = bf16[4,592,128]{2,1,0:T(8,128)(2,1)} custom-call(s32[4,6]{1,0:T(4,128)S(1)} %bitcast.21, bf16[4,592,128]{2,1,0:T(8,128)(2,1)S(1)} %copy-done.11, bf16[64,144,256]{2,1,0:T(8,128)(2,1)S(1)} %copy-done.1, bf16[2,592,128]{2,1,0:T(8,128)(2,1)S(1)} %collective-permute-done.4.refs_0_, bf16[4,592,128]{2,1,0:T(8,128)(2,1)} %memory_attend.7.refs_1_), custom_call_target="tpu_custom_call" | custom-call | flops 127401984 | bytes 186368 | tf_op jit(solution)/shard_map/memory/memory_attend/pallas_call | solution.py:323
  112.1 2.1 %collective-permute-start.7 = (bf16[4,592,128]{2,1,0:T(8,128)(2,1)}, bf16[4,592,128]{2,1,0:T(8,128)(2,1)}, u32[]{:S(2)}, u32[]{:S(2)}) collective-permute-start(bf16[4,592,128]{2,1,0:T(8,128)(2,1)} %memory_attend.8._), channel_id=1, source_target_pairs={{0,4},{4,8},{8,12},{12,0},{1,5},{5,9},{9,13},{13,1},{2,6},{6,10},{... | collective-permute-start | bytes 1818632 | tf_op jit(solution)/shard_map/memory/ppermute | solution.py:495
  114.2 1.2 collective-permute-start.6
  116.0 0.0 all-to-all-done.2.in_ref
  116.0 3.5 %temporal_attend.1.refs_0_ = bf16[16,144,128]{2,1,0:T(8,128)(2,1)} custom-call(s32[1]{0:T(128)S(6)} %copy.11.length_ref, bf16[16,3,144,128]{3,2,1,0:T(8,128)(2,1)} %all-to-all-done.2.in_ref, bf16[4,592,128]{2,1,0:T(8,128)(2,1)} %memory_attend.8._), custom_call_target="tpu_custom_call" | custom-call | flops 18874368 | bytes 147456 | tf_op jit(solution)/shard_map/temporal/temporal_attend/pallas_call | solution.py:222
  119.5 5.5 %all-to-all-start.4 = ((bf16[16,144,128]{2,1,0:T(8,128)(2,1)}), bf16[16,144,128]{2,1,0:T(8,128)(2,1)S(1)}, u32[]{:S(2)}, u32[]{:S(2)}) async-start(bf16[16,144,128]{2,1,0:T(8,128)(2,1)} %temporal_attend.1.refs_0_), calls=%async_computation.4 | async-start | bytes 1179648 | tf_op jit(solution)/shard_map/temporal/all_to_all | solution.py:446
  125.0 0.0 copy-start.2
  125.1 2.3 %copy-done.2 = bf16[64,144,256]{2,1,0:T(8,128)(2,1)S(1)} copy-done((bf16[64,144,256]{2,1,0:T(8,128)(2,1)S(1)}, bf16[64,144,256]{2,1,0:T(8,128)(2,1)}, u32[]{:S(2)}) %copy-start.2) | copy-done | bytes 4718616
  127.4 3.0 %memory_attend.9.refs_0_ = bf16[4,592,128]{2,1,0:T(8,128)(2,1)S(1)} custom-call(s32[4,6]{1,0:T(4,128)S(1)} %bitcast.23, bf16[4,592,128]{2,1,0:T(8,128)(2,1)S(1)} %all_to_all.25.query_ref, bf16[64,144,256]{2,1,0:T(8,128)(2,1)S(1)} %copy-done.2, bf16[16,144,128]{2,1,0:T(8,128)(2,1)} %temporal_attend.1.refs_0_), custom_call_target="tpu_custom_call" | custom-call | flops 127401984 | bytes 186368 | tf_op jit(solution)/shard_map/memory/memory_attend/pallas_call | solution.py:323
  130.4 0.0 collective-permute-done.7.refs_2_
  130.4 3.8 %collective-permute-done.6.refs_1_ = bf16[4,592,128]{2,1,0:T(8,128)(2,1)} collective-permute-done((bf16[4,592,128]{2,1,0:T(8,128)(2,1)}, bf16[4,592,128]{2,1,0:T(8,128)(2,1)}, u32[]{:S(2)}, u32[]{:S(2)}) %collective-permute-start.6) | collective-permute-done | bytes 606240 | tf_op jit(solution)/shard_map/memory/ppermute | solution.py:493
  134.2 1.5 add_partials.1
  135.7 1.2 all-to-all-done.4.time_ref
  136.9 13.2 %all_to_all.26.memory_ref = bf16[4,592,128]{2,1,0:T(8,128)(2,1)S(1)} all-to-all(bf16[4,592,128]{2,1,0:T(8,128)(2,1)S(1)} %add_partials.1), channel_id=1, replica_groups=mesh['y'=4,'c'=2,'z'=4,'x'=4] {'x'}, dimensions={0} | all-to-all | bytes 1212416 | tf_op jit(solution)/shard_map/memory/all_to_all | solution.py:446
  150.0 5.2 %leave.1 = bf16[576,2048]{1,0:T(8,128)(2,1)} custom-call(f32[4,576,256]{2,1,0:T(8,128)S(1)} %own_attend.1._.own_ref, bf16[4,592,128]{2,1,0:T(8,128)(2,1)S(1)} %all_to_all.26.memory_ref, bf16[16,144,128]{2,1,0:T(8,128)(2,1)S(1)} %all-to-all-done.4.time_ref, bf16[1024,2048]{1,0:T(8,128)(2,1)} %weight_hbm.7), custom_call_target="tpu_custom_call" | custom-call | flops 150994944 | bytes 630784 | tf_op jit(solution)/shard_map/exit/leave/pallas_call | solution.py:407
  (27 shorter events, 0.1 us)
Async XLA Ops:
  6.5 6.7 %copy-start.19 = (s32[1,1,6,1]{2,3,1,0:T(1,128)S(1)}, s32[1,1,6,1]{2,3,1,0:T(1,128)}, u32[]{:S(2)}) copy-start(s32[1,1,6,1]{2,3,1,0:T(1,128)} %param.17) | copy-start | bytes 76
  6.5 6.7 %copy-start.18 = (s32[1,1,6]{2,1,0:T(1,128)S(1)}, s32[1,1,6]{2,1,0:T(1,128)}, u32[]{:S(2)}) copy-start(s32[1,1,6]{2,1,0:T(1,128)} %param.18) | copy-start | bytes 76
  6.5 6.7 %copy-start.17 = (f32[2,4]{1,0:T(2,128)S(1)}, f32[2,4]{1,0:T(2,128)}, u32[]{:S(2)}) copy-start(f32[2,4]{1,0:T(2,128)} %param.15) | copy-start | bytes 100
  6.5 6.7 %copy-start.16 = (f32[1,1,2,2048]{3,2,1,0:T(2,128)S(1)}, f32[1,1,2,2048]{3,2,1,0:T(2,128)}, u32[]{:S(2)}) copy-start(f32[1,1,2,2048]{3,2,1,0:T(2,128)} %param.12) | copy-start | bytes 49156
  8.8 14.6 %all-to-all-start = ((bf16[4,288,256]{2,1,0:T(8,128)(2,1)}), bf16[4,288,256]{2,1,0:T(8,128)(2,1)S(1)}, u32[]{:S(2)}, u32[]{:S(2)}) async-start(bf16[4,288,256]{2,1,0:T(8,128)(2,1)} %split_store.1._), calls=%async_computation | async-start | bytes 1179648 | tf_op jit(solution)/shard_map/store/all_to_all | solution.py:446
  13.2 67.2 %all-gather.2.cloned.1.call-start = ((), (), s32[]{:S(2)}) async-start(), calls=%async_computation.5 | async-start | bytes 5308416 | tf_op jit(solution)/shard_map/store/all_gather | solution.py:470
  18.2 0.9 copy-start.8
  19.1 18.3 %copy-start.3 = (bf16[576,2048]{1,0:T(8,128)(2,1)}, bf16[576,2048]{1,0:T(8,128)(2,1)S(1)}, u32[]{:S(2)}) copy-start(bf16[576,2048]{1,0:T(8,128)(2,1)S(1)} %get-tuple-element.22._.hidden_ref) | copy-start | bytes 7077892
  37.4 15.3 %collective-permute-start = (bf16[4,592,128]{2,1,0:T(8,128)(2,1)S(1)}, bf16[4,592,128]{2,1,0:T(8,128)(2,1)S(1)}, u32[]{:S(2)}, u32[]{:S(2)}) collective-permute-start(bf16[4,592,128]{2,1,0:T(8,128)(2,1)S(1)} %all_to_all.25.query_ref), channel_id=1, source_target_pairs={{0,4},{4,8},{8,12},{12,0},{1,5},{5,9},{9,13},{13,1},{2,6},{6,10},{... | collective-permute-start | bytes 1818632 | tf_op jit(solution)/shard_map/queries/ppermute | solution.py:477
  39.3 13.5 %collective-permute-start.2 = (bf16[4,592,128]{2,1,0:T(8,128)(2,1)S(1)}, bf16[4,592,128]{2,1,0:T(8,128)(2,1)S(1)}, u32[]{:S(2)}, u32[]{:S(2)}) collective-permute-start(bf16[4,592,128]{2,1,0:T(8,128)(2,1)S(1)} %all_to_all.25.query_ref), channel_id=1, source_target_pairs={{0,12},{4,0},{8,4},{12,8},{1,13},{5,1},{9,5},{13,9},{2,14},{6,2},{... | collective-permute-start | bytes 1818632 | tf_op jit(solution)/shard_map/queries/ppermute | solution.py:478
  52.7 0.8 copy-start.12
  52.7 21.6 %collective-permute-start.1 = (bf16[2,592,128]{2,1,0:T(8,128)(2,1)S(1)}, bf16[2,592,128]{2,1,0:T(8,128)(2,1)S(1)}, u32[]{:S(2)}, u32[]{:S(2)}) collective-permute-start(bf16[2,592,128]{2,1,0:T(8,128)(2,1)S(1)} %slice.45), channel_id=1, source_target_pairs={{0,4},{4,8},{8,12},{12,0},{1,5},{5,9},{9,13},{13,1},{2,6},{6,10},{... | collective-permute-start | bytes 909320 | tf_op jit(solution)/shard_map/queries/ppermute | solution.py:479
  52.8 0.9 copy-start.10
  53.7 20.6 %collective-permute-start.3 = (bf16[2,592,128]{2,1,0:T(8,128)(2,1)S(1)}, bf16[2,592,128]{2,1,0:T(8,128)(2,1)S(1)}, u32[]{:S(2)}, u32[]{:S(2)}) collective-permute-start(bf16[2,592,128]{2,1,0:T(8,128)(2,1)S(1)} %slice.46), channel_id=1, source_target_pairs={{0,12},{4,0},{8,4},{12,8},{1,13},{5,1},{9,5},{13,9},{2,14},{6,2},{... | collective-permute-start | bytes 909320 | tf_op jit(solution)/shard_map/queries/ppermute | solution.py:480
  56.8 1.7 %copy-start.4 = (bf16[576,2048]{1,0:T(8,128)(2,1)S(1)}, bf16[576,2048]{1,0:T(8,128)(2,1)}, u32[]{:S(2)}) copy-start(bf16[576,2048]{1,0:T(8,128)(2,1)} %copy-done.3) | copy-start | bytes 7077892
  58.6 1.1 copy-start.9
  59.6 6.7 %copy-start.5 = (bf16[576,2048]{1,0:T(8,128)(2,1)S(1)}, bf16[576,2048]{1,0:T(8,128)(2,1)}, u32[]{:S(2)}) copy-start(bf16[576,2048]{1,0:T(8,128)(2,1)} %copy-done.3) | copy-start | bytes 7077892
  73.1 1.2 copy-start.6
  74.3 0.7 copy-start.14
  75.1 40.9 %all-to-all-start.2 = ((bf16[16,3,144,128]{3,2,1,0:T(8,128)(2,1)}), bf16[16,3,144,128]{3,2,1,0:T(8,128)(2,1)}, u32[]{:S(2)}, u32[]{:S(2)}) async-start(bf16[16,3,144,128]{3,2,1,0:T(8,128)(2,1)} %bitcast.18), calls=%async_computation.2 | async-start | bytes 3538944 | tf_op jit(solution)/shard_map/temporal/all_to_all | solution.py:446
  80.4 2.3 %copy-start = (bf16[64,144,256]{2,1,0:T(8,128)(2,1)S(1)}, bf16[64,144,256]{2,1,0:T(8,128)(2,1)}, u32[]{:S(2)}) copy-start(bf16[64,144,256]{2,1,0:T(8,128)(2,1)} %all-gather.2.cloned.1.call-done.store_ref) | copy-start | bytes 14155780
  82.7 1.5 copy-start.7
  84.2 1.0 copy-start.15
  85.2 5.0 %copy-start.1 = (bf16[64,144,256]{2,1,0:T(8,128)(2,1)S(1)}, bf16[64,144,256]{2,1,0:T(8,128)(2,1)}, u32[]{:S(2)}) copy-start(bf16[64,144,256]{2,1,0:T(8,128)(2,1)} %all-gather.2.cloned.1.call-done.store_ref) | copy-start | bytes 14155780
  87.1 17.3 %collective-permute-start.5 = (bf16[2,592,128]{2,1,0:T(8,128)(2,1)S(1)}, bf16[2,592,128]{2,1,0:T(8,128)(2,1)S(1)}, u32[]{:S(2)}, u32[]{:S(2)}) collective-permute-start(bf16[2,592,128]{2,1,0:T(8,128)(2,1)S(1)} %memory_attend.5.refs_0_), channel_id=1, source_target_pairs={{0,12},{4,0},{8,4},{12,8},{1,13},{5,1},{9,5},{13,9},{2,14},{6,2},{... | collective-permute-start | bytes 909320 | tf_op jit(solution)/shard_map/memory/ppermute | solution.py:489
  90.1 2.0 %copy-start.13 = (bf16[4,592,128]{2,1,0:T(8,128)(2,1)S(1)}, bf16[4,592,128]{2,1,0:T(8,128)(2,1)}, u32[]{:S(2)}) copy-start(bf16[4,592,128]{2,1,0:T(8,128)(2,1)} %copy-done.12) | copy-start | bytes 1818628
  90.2 2.0 %copy-start.11 = (bf16[4,592,128]{2,1,0:T(8,128)(2,1)S(1)}, bf16[4,592,128]{2,1,0:T(8,128)(2,1)}, u32[]{:S(2)}) copy-start(bf16[4,592,128]{2,1,0:T(8,128)(2,1)} %copy-done.10) | copy-start | bytes 1818628
  92.0 16.1 %collective-permute-start.4 = (bf16[2,592,128]{2,1,0:T(8,128)(2,1)S(1)}, bf16[2,592,128]{2,1,0:T(8,128)(2,1)S(1)}, u32[]{:S(2)}, u32[]{:S(2)}) collective-permute-start(bf16[2,592,128]{2,1,0:T(8,128)(2,1)S(1)} %memory_attend.6.refs_1_), channel_id=1, source_target_pairs={{0,4},{4,8},{8,12},{12,0},{1,5},{5,9},{9,13},{13,1},{2,6},{6,10},{... | collective-permute-start | bytes 909320 | tf_op jit(solution)/shard_map/memory/ppermute | solution.py:491
  112.1 18.3 %collective-permute-start.7 = (bf16[4,592,128]{2,1,0:T(8,128)(2,1)}, bf16[4,592,128]{2,1,0:T(8,128)(2,1)}, u32[]{:S(2)}, u32[]{:S(2)}) collective-permute-start(bf16[4,592,128]{2,1,0:T(8,128)(2,1)} %memory_attend.8._), channel_id=1, source_target_pairs={{0,4},{4,8},{8,12},{12,0},{1,5},{5,9},{9,13},{13,1},{2,6},{6,10},{... | collective-permute-start | bytes 1818632 | tf_op jit(solution)/shard_map/memory/ppermute | solution.py:495
  114.2 20.0 %collective-permute-start.6 = (bf16[4,592,128]{2,1,0:T(8,128)(2,1)}, bf16[4,592,128]{2,1,0:T(8,128)(2,1)}, u32[]{:S(2)}, u32[]{:S(2)}) collective-permute-start(bf16[4,592,128]{2,1,0:T(8,128)(2,1)} %memory_attend.7.refs_1_), channel_id=1, source_target_pairs={{0,12},{4,0},{8,4},{12,8},{1,13},{5,1},{9,5},{13,9},{2,14},{6,2},{... | collective-permute-start | bytes 1818632 | tf_op jit(solution)/shard_map/memory/ppermute | solution.py:493
  119.5 17.4 %all-to-all-start.4 = ((bf16[16,144,128]{2,1,0:T(8,128)(2,1)}), bf16[16,144,128]{2,1,0:T(8,128)(2,1)S(1)}, u32[]{:S(2)}, u32[]{:S(2)}) async-start(bf16[16,144,128]{2,1,0:T(8,128)(2,1)} %temporal_attend.1.refs_0_), calls=%async_computation.4 | async-start | bytes 1179648 | tf_op jit(solution)/shard_map/temporal/all_to_all | solution.py:446
  125.0 2.3 %copy-start.2 = (bf16[64,144,256]{2,1,0:T(8,128)(2,1)S(1)}, bf16[64,144,256]{2,1,0:T(8,128)(2,1)}, u32[]{:S(2)}) copy-start(bf16[64,144,256]{2,1,0:T(8,128)(2,1)} %all-gather.2.cloned.1.call-done.store_ref) | copy-start | bytes 14155780
Sparse Core Ops, SparseCore 0:
  24.6 34.8 all-gather.1

commit v4 on v3

--- a/solution.py
+++ b/solution.py
@@ -312,11 +312,10 @@
         out_ref[i, patches:, :] = halves(total)
 
 
-def memory_attend(query, store, after, carry=None, first=0):
+def memory_attend(index, query, store, after, carry=None, first=0):
     frames, rows, _ = query.shape
     patches = rows - PAD
     quarter = store.shape[1]
-    index = query[:, patches, :TOPM].astype(jnp.int32)
     carried, extra = None, []
     if carry is not None:
         carried, extra = (first, first + carry.shape[0]), [carry]
@@ -439,8 +438,10 @@
     rings = lax.axis_size("z")
     patches, depth = patch_activation_tensor.shape[2:]
     held, piece = cached_past_pairs.shape[:2]
+    rolls_y, cores = lax.axis_size("y"), lax.axis_size("c")
     up = [(s, (s + 1) % rings) for s in range(rings)]
     down = [(s, (s - 1) % rings) for s in range(rings)]
+    other = [(s, cores - 1 - s) for s in range(cores)]
 
     def swap(blocks, axes):
         return lax.all_to_all(blocks, axes, split_axis=0, concat_axis=0, tiled=True)
@@ -467,39 +468,47 @@
 
     with jax.named_scope("store"):
         joined = join_pieces(pieces, held, after=hidden)
-        store = lax.all_gather(joined, ("y", "c"), axis=0, tiled=True)
+        store_above = lax.ppermute(joined, "y", down)
+        store_below = lax.ppermute(joined, "y", up)
+        store_far = lax.ppermute(store_above, "y", down)
+        near = [joined, store_above, store_far, store_below]
+        beside = [lax.ppermute(block, "c", other) for block in near]
+        store = jnp.concatenate(near + beside, axis=0)
 
     with jax.named_scope("own"):
         own = own_attend(hidden, entry_projection_matrix, query, after=joined)
 
     with jax.named_scope("queries"):
-        half = here.shape[0] // 2
+        here, own = lax.optimization_barrier((here, own))
+        above = lax.ppermute(here, "z", down)
         below = lax.ppermute(here, "z", up)
-        above = lax.ppermute(here, "z", down)
-        far_first = lax.ppermute(below[:half], "z", up)
-        far_last = lax.ppermute(above[half:], "z", down)
+        far = lax.ppermute(above, "z", down)
 
     with jax.named_scope("temporal"):
         parts = temporal_entry(hidden, entry_projection_matrix, factor, rings, after=own)
-        parts, far_first, far_last = lax.optimization_barrier((parts, far_first, far_last))
         sent = swap(parts.reshape((rings * G,) + parts.shape[2:]), ("z", "x"))
 
+    def attend(group, after, **more):
+        named = group[:, patches, :TOPM].astype(jnp.int32)
+        y = (named // (cores * held) - lax.axis_index("y")) & (rolls_y - 1)
+        c = (named // held & (cores - 1)) ^ lax.axis_index("c")
+        index = (c * rolls_y + y) * held + (named & (held - 1))
+        return memory_attend(index, group, store, after, **more)
+
     with jax.named_scope("memory"):
-        sum_first = memory_attend(far_first, store, parts)
-        carry_first = lax.ppermute(sum_first, "z", down)
-        sum_last = memory_attend(far_last, store, sum_first)
-        carry_last = lax.ppermute(sum_last, "z", up)
-        sum_below = memory_attend(below, store, sum_last, carry=carry_first, first=0)
+        sum_far = attend(far, parts)
+        carry = lax.ppermute(sum_far, "z", down)
+        sum_above = attend(above, sum_far)
+        from_below = lax.ppermute(sum_above, "z", up)
+        sum_below = attend(below, sum_above, carry=carry)
         from_above = lax.ppermute(sum_below, "z", down)
-        sum_above = memory_attend(above, store, sum_below, carry=carry_last, first=half)
-        from_below = lax.ppermute(sum_above, "z", up)
 
     with jax.named_scope("temporal"):
-        timed = temporal_attend(lookback_lengths, sent, after=sum_above)
+        timed = temporal_attend(lookback_lengths, sent, after=sum_below)
         time = swap(timed, ("z", "x"))
 
     with jax.named_scope("memory"):
-        sum_here = memory_attend(here, store, timed)
+        sum_here = attend(here, timed)
         memory = swap(add_partials([sum_here, from_above, from_below]), "x")
 
     with jax.named_scope("exit"):

time: 163 us -> 163 us (level)
  blocking collectives: 26.1 us -> 12.5 us
  between operations: 14.3 us -> 1.05 us
  local copies, waits for them, and re-layouts: 14.8 us -> 27.3 us
  starting transfers between devices: 28.1 us -> 38.1 us
  waiting for transfers between devices: 32.7 us -> 36.2 us
    ppermute x4 -> x9, waiting for transfers between devices: 12.2 us -> 30.1 us  [the longest x1 21.6 us: on_device(): far = lax.ppermute(above, 'z', down)]
    all_to_all x2 -> x1, blocking collectives: 26.1 us -> 12.5 us  [swap(): return lax.all_to_all(blocks, axes, split_axis=0, concat_axis=0, tiled=True)]
    unnamed x41 -> x36, local copies, waits for them, and re-layouts: 14.8 us -> 26.5 us
    ppermute x1, waiting for transfers between devices: 11.3 us -> 0.01 us  [on_device(): below = lax.ppermute(here, 'z', up)]
    ppermute x4 -> x9, starting transfers between devices: 6.36 us -> 11.6 us  [the longest x1 3.23 us: on_device(): store_far = lax.ppermute(store_above, 'y', down)]
    all_to_all x3 -> x4, starting transfers between devices: 14.5 us -> 18.9 us  [swap(): return lax.all_to_all(blocks, axes, split_axis=0, concat_axis=0, tiled=True)]
    all_to_all x3 -> x4, waiting for transfers between devices: 5.51 us -> 1.81 us  [swap(): return lax.all_to_all(blocks, axes, split_axis=0, concat_axis=0, tiled=True)]
    ppermute x1, starting transfers between devices: 2.12 us -> 4.11 us  [on_device(): above = lax.ppermute(here, 'z', down)]
  transfers between devices with their start and end apart: 12 -> 17, of which waited for: 5 -> 4; matrix products, arithmetic and copies ran while one was open for 0% -> 8% of each run, Pallas kernels for 23% -> 23%
where the time goes in v4:
time: 163 us; the launch traced here: 162 us
  Pallas kernels  44.2 us (27%)
  starting transfers between devices  38.1 us (23%)
  waiting for transfers between devices  36.2 us (22%)
  local copies, waits for them, and re-layouts  27.3 us (17%)
  blocking collectives  12.5 us (8%)
  other arithmetic  2.18 us (1%)
    unnamed x36, local copies, waits for them, and re-layouts  26.5 us
    ppermute x1, waiting for transfers between devices, on_device(): far = lax.ppermute(above, 'z', down)  21.6 us
    all_to_all x4, starting transfers between devices, swap(): return lax.all_to_all(blocks, axes, split_axis=0, concat_axis=0, tiled=True)  18.9 us
    pallas_call x4, Pallas kernels, memory_attend(): pl.pallas_call(functools.partial(memory_attend_kernel, carried), in_specs...  14.4 us
    all_to_all x1, blocking collectives, swap(): return lax.all_to_all(blocks, axes, split_axis=0, concat_axis=0, tiled=True)  12.5 us
    ppermute x1, waiting for transfers between devices, on_device(): carry = lax.ppermute(sum_far, 'z', down)  8.52 us
    pallas_call x1, Pallas kernels, temporal_entry(): pl.pallas_call(functools.partial(temporal_entry_kernel, quarters), in_spe...  6.8 us
    pallas_call x1, Pallas kernels, own_attend(): pl.pallas_call(own_attend_kernel, in_specs=[WHOLE, HBM, WHOLE, ANY], out_...  6.53 us
  transfers between devices with their start and end apart: 17, of which 4 were waited for; matrix products, arithmetic and copies ran while one was open for 8% of the time, Pallas kernels for 23%

profile of v4, /device:TPU:0, one launch (start us, length us, event | category | flops | bytes accessed | tf_op | source)
XLA Modules:
  0.0 161.7 jit_solution(12883044047381222958)
XLA Ops:
  0.0 1.1 copy.10
  1.2 1.1 split_store.1._
  2.3 4.4 %all-to-all-start.1 = ((bf16[4,288,256]{2,1,0:T(8,128)(2,1)}), bf16[4,288,256]{2,1,0:T(8,128)(2,1)S(1)}, u32[]{:S(2)}, u32[]{:S(2)}) async-start(bf16[4,288,256]{2,1,0:T(8,128)(2,1)} %split_store.1._), calls=%async_computation.1 | async-start | bytes 1179648 | tf_op jit(solution)/shard_map/store/all_to_all | solution.py:447
  6.6 0.7 fusion.44
  7.3 0.7 broadcast_multiply_fusion.factor_ref
  8.0 0.5 copy-done.12
  8.6 0.7 copy-done.11
  9.3 4.9 %modulate.1 = (bf16[576,2048]{1,0:T(8,128)(2,1)S(1)}, bf16[4,592,128]{2,1,0:T(8,128)(2,1)S(1)}) custom-call(bf16[576,2048]{1,0:T(8,128)(2,1)} %bitcast.20, f32[2,2048]{1,0:T(2,128)S(1)} %bitcast.19, bf16[2048,3072]{1,0:T(8,128)(2,1)} %weight_hbm.6, f32[2,4]{1,0:T(2,128)S(1)} %broadcast_multiply_fusion.factor_ref, bf16[16,128]{1,0:T(8,128)(2,1)S(1)} %scatter.4.tail_ref, ...), custom_call_target="tpu_custom_call" | custom-call | flops 75497472 | bytes 462848 | tf_op jit(solution)/shard_map/queries/modulate/pallas_call | solution.py:134
  14.2 0.8 copy-done.7
  15.0 1.8 %all-to-all-done.1.in_ref = bf16[4,288,256]{2,1,0:T(8,128)(2,1)S(1)} async-done(((bf16[4,288,256]{2,1,0:T(8,128)(2,1)}), bf16[4,288,256]{2,1,0:T(8,128)(2,1)S(1)}, u32[]{:S(2)}, u32[]{:S(2)}) %all-to-all-start.1) | async-done | bytes 589856 | tf_op jit(solution)/shard_map/store/all_to_all | solution.py:447
  16.8 0.8 copy-done.9
  17.7 3.5 %all-to-all-start = ((bf16[4,592,128]{2,1,0:T(8,128)(2,1)}), bf16[4,592,128]{2,1,0:T(8,128)(2,1)S(1)}, u32[]{:S(2)}, u32[]{:S(2)}) async-start(bf16[4,592,128]{2,1,0:T(8,128)(2,1)} %copy-done.7), calls=%async_computation | async-start | bytes 1212416 | tf_op jit(solution)/shard_map/queries/all_to_all | solution.py:447
  21.2 1.1 copy-done.10
  22.2 0.2 join_pieces.1._
  22.4 3.1 %collective-permute-start = (bf16[8,144,256]{2,1,0:T(8,128)(2,1)S(1)}, bf16[8,144,256]{2,1,0:T(8,128)(2,1)}, u32[]{:S(2)}, u32[]{:S(2)}) collective-permute-start(bf16[8,144,256]{2,1,0:T(8,128)(2,1)S(1)} %join_pieces.1._), channel_id=1, source_target_pairs={{0,96},{32,0},{64,32},{96,64},{1,97},{33,1},{65,33},{97,65},{2,98}... | collective-permute-start | bytes 1769480 | tf_op jit(solution)/shard_map/store/ppermute | solution.py:471
  25.5 1.7 %copy-done.3 = bf16[576,2048]{1,0:T(8,128)(2,1)S(1)} copy-done((bf16[576,2048]{1,0:T(8,128)(2,1)S(1)}, bf16[576,2048]{1,0:T(8,128)(2,1)}, u32[]{:S(2)}) %copy-start.3) | copy-done | bytes 2359320
  27.2 1.1 copy-done.8
  28.3 6.5 %own_attend.1._.own_ref = f32[4,576,256]{2,1,0:T(8,128)S(1)} custom-call(bf16[576,2048]{1,0:T(8,128)(2,1)S(1)} %copy-done.3, bf16[2048,3072]{1,0:T(8,128)(2,1)} %weight_hbm.6, bf16[4,592,128]{2,1,0:T(8,128)(2,1)S(1)} %copy-done.8, bf16[8,144,256]{2,1,0:T(8,128)(2,1)S(1)} %join_pieces.1._), custom_call_target="tpu_custom_call" | custom-call | flops 214695936 | bytes 593920 | tf_op jit(solution)/shard_map/own/own_attend/pallas_call | solution.py:257
  34.8 0.0 all-to-all-done.query_ref
  34.8 4.1 %collective-permute-start.8 = (bf16[4,592,128]{2,1,0:T(8,128)(2,1)S(1)}, bf16[4,592,128]{2,1,0:T(8,128)(2,1)}, u32[]{:S(2)}, u32[]{:S(2)}) collective-permute-start(bf16[4,592,128]{2,1,0:T(8,128)(2,1)S(1)} %all-to-all-done.query_ref), channel_id=1, source_target_pairs={{0,12},{4,0},{8,4},{12,8},{1,13},{5,1},{9,5},{13,9},{2,14},{6,2},{... | collective-permute-start | bytes 1818632 | tf_op jit(solution)/shard_map/queries/ppermute | solution.py:483
  38.9 3.2 %collective-permute-start.1 = (bf16[8,144,256]{2,1,0:T(8,128)(2,1)}, bf16[8,144,256]{2,1,0:T(8,128)(2,1)}, u32[]{:S(2)}, u32[]{:S(2)}) collective-permute-start(bf16[8,144,256]{2,1,0:T(8,128)(2,1)} %collective-permute-done), channel_id=1, source_target_pairs={{0,96},{32,0},{64,32},{96,64},{1,97},{33,1},{65,33},{97,65},{2,98}... | collective-permute-start | bytes 1769480 | tf_op jit(solution)/shard_map/store/ppermute | solution.py:473
  42.1 0.0 collective-permute-start.3
  42.1 0.8 constant_dynamic-update-slice_fusion.7
  43.0 1.7 %copy-done.4 = bf16[576,2048]{1,0:T(8,128)(2,1)S(1)} copy-done((bf16[576,2048]{1,0:T(8,128)(2,1)S(1)}, bf16[576,2048]{1,0:T(8,128)(2,1)}, u32[]{:S(2)}) %copy-start.4) | copy-done | bytes 2359320
  44.7 0.6 copy-done.13
  45.3 6.8 %temporal_entry.1.refs_0_ = bf16[4,4,3,144,128]{4,3,2,1,0:T(8,128)(2,1)S(1)} custom-call(bf16[576,2048]{1,0:T(8,128)(2,1)S(1)} %copy-done.4, bf16[2048,3072]{1,0:T(8,128)(2,1)} %weight_hbm.6, f32[2,4]{1,0:T(2,128)S(1)} %copy-done.13, f32[4,576,256]{2,1,0:T(8,128)S(1)} %own_attend.1._.own_ref), custom_call_target="tpu_custom_call" | custom-call | flops 226492416 | bytes 651264 | tf_op jit(solution)/shard_map/temporal/temporal_entry/pallas_call | solution.py:186
  52.1 0.0 copy-start.5
  52.1 1.2 copy-done.5
  53.3 6.7 %all-to-all-start.2 = ((bf16[16,3,144,128]{3,2,1,0:T(8,128)(2,1)}), bf16[16,3,144,128]{3,2,1,0:T(8,128)(2,1)}, u32[]{:S(2)}, u32[]{:S(2)}) async-start(bf16[16,3,144,128]{3,2,1,0:T(8,128)(2,1)} %bitcast.17), calls=%async_computation.2 | async-start | bytes 3538944 | tf_op jit(solution)/shard_map/temporal/all_to_all | solution.py:447
  60.0 0.0 copy-start.6
  60.0 0.3 collective-permute-start.4
  60.3 2.1 %constant_dynamic-update-slice_fusion.6 = bf16[64,144,256]{2,1,0:T(8,128)(2,1)} fusion(bf16[64,144,256]{2,1,0:T(8,128)(2,1)} %constant_dynamic-update-slice_fusion.7, bf16[8,144,256]{2,1,0:T(8,128)(2,1)} %collective-permute-done), kind=kLoop, calls=%fused_computation.6 | loop fusion | bytes 1179648
  62.4 0.0 collective-permute-done.8.query_ref
  62.4 2.9 %collective-permute-start.9 = (bf16[4,592,128]{2,1,0:T(8,128)(2,1)}, bf16[4,592,128]{2,1,0:T(8,128)(2,1)S(1)}, u32[]{:S(2)}, u32[]{:S(2)}) collective-permute-start(bf16[4,592,128]{2,1,0:T(8,128)(2,1)} %collective-permute-done.8.query_ref), channel_id=1, source_target_pairs={{0,12},{4,0},{8,4},{12,8},{1,13},{5,1},{9,5},{13,9},{2,14},{6,2},{... | collective-permute-start | bytes 1818632 | tf_op jit(solution)/shard_map/queries/ppermute | solution.py:485
  65.3 0.7 slice_convert_fusion
  66.0 0.0 collective-permute-done.2
  66.0 0.0 collective-permute-done.1
  66.0 0.2 collective-permute-start.6
  66.2 1.9 %constant_dynamic-update-slice_fusion.5 = bf16[64,144,256]{2,1,0:T(8,128)(2,1)} fusion(bf16[64,144,256]{2,1,0:T(8,128)(2,1)} %constant_dynamic-update-slice_fusion.6, bf16[8,144,256]{2,1,0:T(8,128)(2,1)} %collective-permute-done.1), kind=kLoop, calls=%fused_computation.5 | loop fusion | bytes 1179648
  68.1 1.9 %constant_dynamic-update-slice_fusion.4 = bf16[64,144,256]{2,1,0:T(8,128)(2,1)} fusion(bf16[64,144,256]{2,1,0:T(8,128)(2,1)} %constant_dynamic-update-slice_fusion.5, bf16[8,144,256]{2,1,0:T(8,128)(2,1)} %collective-permute-done.2), kind=kLoop, calls=%fused_computation.4 | loop fusion | bytes 1179648
  70.1 0.0 collective-permute-done.3
  70.1 0.4 collective-permute-start.5
  70.5 1.9 %constant_dynamic-update-slice_fusion.3 = bf16[64,144,256]{2,1,0:T(8,128)(2,1)} fusion(bf16[64,144,256]{2,1,0:T(8,128)(2,1)} %constant_dynamic-update-slice_fusion.4, bf16[8,144,256]{2,1,0:T(8,128)(2,1)} %collective-permute-done.3), kind=kLoop, calls=%fused_computation.3 | loop fusion | bytes 1179648
  72.4 0.9 constant_dynamic-update-slice_fusion.2
  73.3 21.6 %collective-permute-done.9.query_ref = bf16[4,592,128]{2,1,0:T(8,128)(2,1)S(1)} collective-permute-done((bf16[4,592,128]{2,1,0:T(8,128)(2,1)}, bf16[4,592,128]{2,1,0:T(8,128)(2,1)S(1)}, u32[]{:S(2)}, u32[]{:S(2)}) %collective-permute-start.9) | collective-permute-done | bytes 606240 | tf_op jit(solution)/shard_map/queries/ppermute | solution.py:485
  94.9 0.0 collective-permute-done.5
  94.9 0.9 constant_dynamic-update-slice_fusion.1
  95.8 0.9 constant_dynamic-update-slice_fusion.store_ref
  96.6 2.3 %copy-done = bf16[64,144,256]{2,1,0:T(8,128)(2,1)S(1)} copy-done((bf16[64,144,256]{2,1,0:T(8,128)(2,1)S(1)}, bf16[64,144,256]{2,1,0:T(8,128)(2,1)}, u32[]{:S(2)}) %copy-start) | copy-done | bytes 4718616
  99.0 3.0 %memory_attend.4.refs_0_ = bf16[4,592,128]{2,1,0:T(8,128)(2,1)S(1)} custom-call(s32[4,6]{1,0:T(4,128)S(1)} %fusion.26.index_ref, bf16[4,592,128]{2,1,0:T(8,128)(2,1)S(1)} %collective-permute-done.9.query_ref, bf16[64,144,256]{2,1,0:T(8,128)(2,1)S(1)} %copy-done, bf16[4,4,3,144,128]{4,3,2,1,0:T(8,128)(2,1)S(1)} %copy-done.6), custom_call_target="tpu_custom_call" | custom-call | flops 127401984 | bytes 186368 | tf_op jit(solution)/shard_map/memory/memory_attend/pallas_call | solution.py:322
  102.0 1.5 collective-permute-start.10
  103.6 4.4 %memory_attend.5.refs_1_ = bf16[4,592,128]{2,1,0:T(8,128)(2,1)} custom-call(s32[4,6]{1,0:T(4,128)S(1)} %fusion.36.index_ref, bf16[4,592,128]{2,1,0:T(8,128)(2,1)} %collective-permute-done.8.query_ref, bf16[64,144,256]{2,1,0:T(8,128)(2,1)S(1)} %copy-done, bf16[4,592,128]{2,1,0:T(8,128)(2,1)S(1)} %memory_attend.4.refs_0_), custom_call_target="tpu_custom_call" | custom-call | flops 127401984 | bytes 186368 | tf_op jit(solution)/shard_map/memory/memory_attend/pallas_call | solution.py:322
  108.0 0.5 collective-permute-start.12
  108.6 8.5 %collective-permute-done.10.refs_0_ = bf16[4,592,128]{2,1,0:T(8,128)(2,1)S(1)} collective-permute-done((bf16[4,592,128]{2,1,0:T(8,128)(2,1)S(1)}, bf16[4,592,128]{2,1,0:T(8,128)(2,1)S(1)}, u32[]{:S(2)}, u32[]{:S(2)}) %collective-permute-start.10) | collective-permute-done | bytes 606240 | tf_op jit(solution)/shard_map/memory/ppermute | solution.py:500
  117.1 4.0 %memory_attend.6._ = bf16[4,592,128]{2,1,0:T(8,128)(2,1)} custom-call(s32[4,6]{1,0:T(4,128)S(1)} %fusion.16.index_ref, bf16[4,592,128]{2,1,0:T(8,128)(2,1)S(1)} %collective-permute-done.7.query_ref, bf16[64,144,256]{2,1,0:T(8,128)(2,1)S(1)} %copy-done, bf16[4,592,128]{2,1,0:T(8,128)(2,1)S(1)} %collective-permute-done.10.refs_0_, ...), custom_call_target="tpu_custom_call" | custom-call | flops 127401984 | bytes 186368 | tf_op jit(solution)/shard_map/memory/memory_attend/pallas_call | solution.py:322
  121.0 3.0 %collective-permute-start.11 = (bf16[4,592,128]{2,1,0:T(8,128)(2,1)}, bf16[4,592,128]{2,1,0:T(8,128)(2,1)}, u32[]{:S(2)}, u32[]{:S(2)}) collective-permute-start(bf16[4,592,128]{2,1,0:T(8,128)(2,1)} %memory_attend.6._), channel_id=1, source_target_pairs={{0,12},{4,0},{8,4},{12,8},{1,13},{5,1},{9,5},{13,9},{2,14},{6,2},{... | collective-permute-start | bytes 1818632 | tf_op jit(solution)/shard_map/memory/ppermute | solution.py:504
  124.7 3.5 %temporal_attend.1.refs_0_ = bf16[16,144,128]{2,1,0:T(8,128)(2,1)} custom-call(s32[1]{0:T(128)S(6)} %copy.18.length_ref, bf16[16,3,144,128]{3,2,1,0:T(8,128)(2,1)} %all-to-all-done.2.in_ref, bf16[4,592,128]{2,1,0:T(8,128)(2,1)} %memory_attend.6._), custom_call_target="tpu_custom_call" | custom-call | flops 18874368 | bytes 147456 | tf_op jit(solution)/shard_map/temporal/temporal_attend/pallas_call | solution.py:222
  128.2 4.3 %all-to-all-start.4 = ((bf16[16,144,128]{2,1,0:T(8,128)(2,1)}), bf16[16,144,128]{2,1,0:T(8,128)(2,1)S(1)}, u32[]{:S(2)}, u32[]{:S(2)}) async-start(bf16[16,144,128]{2,1,0:T(8,128)(2,1)} %temporal_attend.1.refs_0_), calls=%async_computation.4 | async-start | bytes 1179648 | tf_op jit(solution)/shard_map/temporal/all_to_all | solution.py:447
  132.6 2.3 %copy-done.1 = bf16[64,144,256]{2,1,0:T(8,128)(2,1)S(1)} copy-done((bf16[64,144,256]{2,1,0:T(8,128)(2,1)S(1)}, bf16[64,144,256]{2,1,0:T(8,128)(2,1)}, u32[]{:S(2)}) %copy-start.1) | copy-done | bytes 4718616
  134.9 3.0 %memory_attend.7.refs_0_ = bf16[4,592,128]{2,1,0:T(8,128)(2,1)S(1)} custom-call(s32[4,6]{1,0:T(4,128)S(1)} %fusion.6.index_ref, bf16[4,592,128]{2,1,0:T(8,128)(2,1)S(1)} %all-to-all-done.query_ref, bf16[64,144,256]{2,1,0:T(8,128)(2,1)S(1)} %copy-done.1, bf16[16,144,128]{2,1,0:T(8,128)(2,1)} %temporal_attend.1.refs_0_), custom_call_target="tpu_custom_call" | custom-call | flops 127401984 | bytes 186368 | tf_op jit(solution)/shard_map/memory/memory_attend/pallas_call | solution.py:322
  138.0 4.3 %collective-permute-done.11.refs_1_ = bf16[4,592,128]{2,1,0:T(8,128)(2,1)} collective-permute-done((bf16[4,592,128]{2,1,0:T(8,128)(2,1)}, bf16[4,592,128]{2,1,0:T(8,128)(2,1)}, u32[]{:S(2)}, u32[]{:S(2)}) %collective-permute-start.11) | collective-permute-done | bytes 606240 | tf_op jit(solution)/shard_map/memory/ppermute | solution.py:504
  142.2 1.5 add_partials.1
  143.7 12.5 %all_to_all.25.memory_ref = bf16[4,592,128]{2,1,0:T(8,128)(2,1)S(1)} all-to-all(bf16[4,592,128]{2,1,0:T(8,128)(2,1)S(1)} %add_partials.1), channel_id=1, replica_groups=mesh['y'=4,'c'=2,'z'=4,'x'=4] {'x'}, dimensions={0} | all-to-all | bytes 1212416 | tf_op jit(solution)/shard_map/memory/all_to_all | solution.py:447
  156.3 5.2 %leave.1 = bf16[576,2048]{1,0:T(8,128)(2,1)} custom-call(f32[4,576,256]{2,1,0:T(8,128)S(1)} %own_attend.1._.own_ref, bf16[4,592,128]{2,1,0:T(8,128)(2,1)S(1)} %all_to_all.25.memory_ref, bf16[16,144,128]{2,1,0:T(8,128)(2,1)S(1)} %all-to-all-done.4.time_ref, bf16[1024,2048]{1,0:T(8,128)(2,1)} %weight_hbm.7), custom_call_target="tpu_custom_call" | custom-call | flops 150994944 | bytes 630784 | tf_op jit(solution)/shard_map/exit/leave/pallas_call | solution.py:406
  (31 shorter events, 0.1 us)
Async XLA Ops:
  2.3 14.6 %all-to-all-start.1 = ((bf16[4,288,256]{2,1,0:T(8,128)(2,1)}), bf16[4,288,256]{2,1,0:T(8,128)(2,1)S(1)}, u32[]{:S(2)}, u32[]{:S(2)}) async-start(bf16[4,288,256]{2,1,0:T(8,128)(2,1)} %split_store.1._), calls=%async_computation.1 | async-start | bytes 1179648 | tf_op jit(solution)/shard_map/store/all_to_all | solution.py:447
  8.0 0.5 copy-start.12
  8.6 0.7 copy-start.11
  14.2 0.8 copy-start.7
  15.0 7.4 %copy-start.2 = (bf16[576,2048]{1,0:T(8,128)(2,1)}, bf16[576,2048]{1,0:T(8,128)(2,1)S(1)}, u32[]{:S(2)}) copy-start(bf16[576,2048]{1,0:T(8,128)(2,1)S(1)} %get-tuple-element.22._.hidden_ref) | copy-start | bytes 7077892
  16.8 0.8 copy-start.9
  17.7 17.1 %all-to-all-start = ((bf16[4,592,128]{2,1,0:T(8,128)(2,1)}), bf16[4,592,128]{2,1,0:T(8,128)(2,1)S(1)}, u32[]{:S(2)}, u32[]{:S(2)}) async-start(bf16[4,592,128]{2,1,0:T(8,128)(2,1)} %copy-done.7), calls=%async_computation | async-start | bytes 1212416 | tf_op jit(solution)/shard_map/queries/all_to_all | solution.py:447
  21.2 1.1 copy-start.10
  22.4 16.5 %collective-permute-start = (bf16[8,144,256]{2,1,0:T(8,128)(2,1)S(1)}, bf16[8,144,256]{2,1,0:T(8,128)(2,1)}, u32[]{:S(2)}, u32[]{:S(2)}) collective-permute-start(bf16[8,144,256]{2,1,0:T(8,128)(2,1)S(1)} %join_pieces.1._), channel_id=1, source_target_pairs={{0,96},{32,0},{64,32},{96,64},{1,97},{33,1},{65,33},{97,65},{2,98}... | collective-permute-start | bytes 1769480 | tf_op jit(solution)/shard_map/store/ppermute | solution.py:471
  25.5 1.7 %copy-start.3 = (bf16[576,2048]{1,0:T(8,128)(2,1)S(1)}, bf16[576,2048]{1,0:T(8,128)(2,1)}, u32[]{:S(2)}) copy-start(bf16[576,2048]{1,0:T(8,128)(2,1)} %copy-done.2) | copy-start | bytes 7077892
  27.2 1.1 copy-start.8
  34.8 27.6 %collective-permute-start.8 = (bf16[4,592,128]{2,1,0:T(8,128)(2,1)S(1)}, bf16[4,592,128]{2,1,0:T(8,128)(2,1)}, u32[]{:S(2)}, u32[]{:S(2)}) collective-permute-start(bf16[4,592,128]{2,1,0:T(8,128)(2,1)S(1)} %all-to-all-done.query_ref), channel_id=1, source_target_pairs={{0,12},{4,0},{8,4},{12,8},{1,13},{5,1},{9,5},{13,9},{2,14},{6,2},{... | collective-permute-start | bytes 1818632 | tf_op jit(solution)/shard_map/queries/ppermute | solution.py:483
  38.9 27.1 %collective-permute-start.2 = (bf16[8,144,256]{2,1,0:T(8,128)(2,1)S(1)}, bf16[8,144,256]{2,1,0:T(8,128)(2,1)}, u32[]{:S(2)}, u32[]{:S(2)}) collective-permute-start(bf16[8,144,256]{2,1,0:T(8,128)(2,1)S(1)} %join_pieces.1._), channel_id=1, source_target_pairs={{0,32},{32,64},{64,96},{96,0},{1,33},{33,65},{65,97},{97,1},{2,34}... | collective-permute-start | bytes 1769480 | tf_op jit(solution)/shard_map/store/ppermute | solution.py:472
  38.9 27.1 %collective-permute-start.1 = (bf16[8,144,256]{2,1,0:T(8,128)(2,1)}, bf16[8,144,256]{2,1,0:T(8,128)(2,1)}, u32[]{:S(2)}, u32[]{:S(2)}) collective-permute-start(bf16[8,144,256]{2,1,0:T(8,128)(2,1)} %collective-permute-done), channel_id=1, source_target_pairs={{0,96},{32,0},{64,32},{96,64},{1,97},{33,1},{65,33},{97,65},{2,98}... | collective-permute-start | bytes 1769480 | tf_op jit(solution)/shard_map/store/ppermute | solution.py:473
  42.1 27.9 %collective-permute-start.3 = (bf16[8,144,256]{2,1,0:T(8,128)(2,1)S(1)}, bf16[8,144,256]{2,1,0:T(8,128)(2,1)}, u32[]{:S(2)}, u32[]{:S(2)}) collective-permute-start(bf16[8,144,256]{2,1,0:T(8,128)(2,1)S(1)} %join_pieces.1._), channel_id=1, source_target_pairs={{0,16},{16,0},{1,17},{17,1},{2,18},{18,2},{3,19},{19,3},{4,20},{20... | collective-permute-start | bytes 1769480 | tf_op jit(solution)/shard_map/store/ppermute | solution.py:475
  43.0 1.7 %copy-start.4 = (bf16[576,2048]{1,0:T(8,128)(2,1)S(1)}, bf16[576,2048]{1,0:T(8,128)(2,1)}, u32[]{:S(2)}) copy-start(bf16[576,2048]{1,0:T(8,128)(2,1)} %copy-done.2) | copy-start | bytes 7077892
  44.7 0.6 copy-start.13
  52.1 1.2 copy-start.5
  53.3 71.4 %all-to-all-start.2 = ((bf16[16,3,144,128]{3,2,1,0:T(8,128)(2,1)}), bf16[16,3,144,128]{3,2,1,0:T(8,128)(2,1)}, u32[]{:S(2)}, u32[]{:S(2)}) async-start(bf16[16,3,144,128]{3,2,1,0:T(8,128)(2,1)} %bitcast.17), calls=%async_computation.2 | async-start | bytes 3538944 | tf_op jit(solution)/shard_map/temporal/all_to_all | solution.py:447
  60.0 36.6 %copy-start.6 = (bf16[4,4,3,144,128]{4,3,2,1,0:T(8,128)(2,1)S(1)}, bf16[4,4,3,144,128]{4,3,2,1,0:T(8,128)(2,1)}, u32[]{:S(2)}) copy-start(bf16[4,4,3,144,128]{4,3,2,1,0:T(8,128)(2,1)} %copy-done.5) | copy-start | bytes 5308420
  60.0 12.4 %collective-permute-start.4 = (bf16[8,144,256]{2,1,0:T(8,128)(2,1)}, bf16[8,144,256]{2,1,0:T(8,128)(2,1)S(1)}, u32[]{:S(2)}, u32[]{:S(2)}) collective-permute-start(bf16[8,144,256]{2,1,0:T(8,128)(2,1)} %collective-permute-done), channel_id=1, source_target_pairs={{0,16},{16,0},{1,17},{17,1},{2,18},{18,2},{3,19},{19,3},{4,20},{20... | collective-permute-start | bytes 1769480 | tf_op jit(solution)/shard_map/store/ppermute | solution.py:475
  62.4 32.4 %collective-permute-start.9 = (bf16[4,592,128]{2,1,0:T(8,128)(2,1)}, bf16[4,592,128]{2,1,0:T(8,128)(2,1)S(1)}, u32[]{:S(2)}, u32[]{:S(2)}) collective-permute-start(bf16[4,592,128]{2,1,0:T(8,128)(2,1)} %collective-permute-done.8.query_ref), channel_id=1, source_target_pairs={{0,12},{4,0},{8,4},{12,8},{1,13},{5,1},{9,5},{13,9},{2,14},{6,2},{... | collective-permute-start | bytes 1818632 | tf_op jit(solution)/shard_map/queries/ppermute | solution.py:485
  66.0 37.6 %collective-permute-start.7 = (bf16[4,592,128]{2,1,0:T(8,128)(2,1)S(1)}, bf16[4,592,128]{2,1,0:T(8,128)(2,1)S(1)}, u32[]{:S(2)}, u32[]{:S(2)}) collective-permute-start(bf16[4,592,128]{2,1,0:T(8,128)(2,1)S(1)} %all-to-all-done.query_ref), channel_id=1, source_target_pairs={{0,4},{4,8},{8,12},{12,0},{1,5},{5,9},{9,13},{13,1},{2,6},{6,10},{... | collective-permute-start | bytes 1818632 | tf_op jit(solution)/shard_map/queries/ppermute | solution.py:484
  66.0 29.7 %collective-permute-start.6 = (bf16[8,144,256]{2,1,0:T(8,128)(2,1)}, bf16[8,144,256]{2,1,0:T(8,128)(2,1)S(1)}, u32[]{:S(2)}, u32[]{:S(2)}) collective-permute-start(bf16[8,144,256]{2,1,0:T(8,128)(2,1)} %collective-permute-done.2), channel_id=1, source_target_pairs={{0,16},{16,0},{1,17},{17,1},{2,18},{18,2},{3,19},{19,3},{4,20},{20... | collective-permute-start | bytes 1769480 | tf_op jit(solution)/shard_map/store/ppermute | solution.py:475
  70.1 24.8 %collective-permute-start.5 = (bf16[8,144,256]{2,1,0:T(8,128)(2,1)}, bf16[8,144,256]{2,1,0:T(8,128)(2,1)S(1)}, u32[]{:S(2)}, u32[]{:S(2)}) collective-permute-start(bf16[8,144,256]{2,1,0:T(8,128)(2,1)} %collective-permute-done.1), channel_id=1, source_target_pairs={{0,16},{16,0},{1,17},{17,1},{2,18},{18,2},{3,19},{19,3},{4,20},{20... | collective-permute-start | bytes 1769480 | tf_op jit(solution)/shard_map/store/ppermute | solution.py:475
  96.6 2.3 %copy-start = (bf16[64,144,256]{2,1,0:T(8,128)(2,1)S(1)}, bf16[64,144,256]{2,1,0:T(8,128)(2,1)}, u32[]{:S(2)}) copy-start(bf16[64,144,256]{2,1,0:T(8,128)(2,1)} %constant_dynamic-update-slice_fusion.store_ref) | copy-start | bytes 14155780
  102.0 15.1 %collective-permute-start.10 = (bf16[4,592,128]{2,1,0:T(8,128)(2,1)S(1)}, bf16[4,592,128]{2,1,0:T(8,128)(2,1)S(1)}, u32[]{:S(2)}, u32[]{:S(2)}) collective-permute-start(bf16[4,592,128]{2,1,0:T(8,128)(2,1)S(1)} %memory_attend.4.refs_0_), channel_id=1, source_target_pairs={{0,12},{4,0},{8,4},{12,8},{1,13},{5,1},{9,5},{13,9},{2,14},{6,2},{... | collective-permute-start | bytes 1818632 | tf_op jit(solution)/shard_map/memory/ppermute | solution.py:500
  108.0 29.9 %collective-permute-start.12 = (bf16[4,592,128]{2,1,0:T(8,128)(2,1)}, bf16[4,592,128]{2,1,0:T(8,128)(2,1)}, u32[]{:S(2)}, u32[]{:S(2)}) collective-permute-start(bf16[4,592,128]{2,1,0:T(8,128)(2,1)} %memory_attend.5.refs_1_), channel_id=1, source_target_pairs={{0,4},{4,8},{8,12},{12,0},{1,5},{5,9},{9,13},{13,1},{2,6},{6,10},{... | collective-permute-start | bytes 1818632 | tf_op jit(solution)/shard_map/memory/ppermute | solution.py:502
  121.0 21.2 %collective-permute-start.11 = (bf16[4,592,128]{2,1,0:T(8,128)(2,1)}, bf16[4,592,128]{2,1,0:T(8,128)(2,1)}, u32[]{:S(2)}, u32[]{:S(2)}) collective-permute-start(bf16[4,592,128]{2,1,0:T(8,128)(2,1)} %memory_attend.6._), channel_id=1, source_target_pairs={{0,12},{4,0},{8,4},{12,8},{1,13},{5,1},{9,5},{13,9},{2,14},{6,2},{... | collective-permute-start | bytes 1818632 | tf_op jit(solution)/shard_map/memory/ppermute | solution.py:504
  128.2 15.5 %all-to-all-start.4 = ((bf16[16,144,128]{2,1,0:T(8,128)(2,1)}), bf16[16,144,128]{2,1,0:T(8,128)(2,1)S(1)}, u32[]{:S(2)}, u32[]{:S(2)}) async-start(bf16[16,144,128]{2,1,0:T(8,128)(2,1)} %temporal_attend.1.refs_0_), calls=%async_computation.4 | async-start | bytes 1179648 | tf_op jit(solution)/shard_map/temporal/all_to_all | solution.py:447
  132.6 2.3 %copy-start.1 = (bf16[64,144,256]{2,1,0:T(8,128)(2,1)S(1)}, bf16[64,144,256]{2,1,0:T(8,128)(2,1)}, u32[]{:S(2)}) copy-start(bf16[64,144,256]{2,1,0:T(8,128)(2,1)} %constant_dynamic-update-slice_fusion.store_ref) | copy-start | bytes 14155780

commit v5 on v4

v5 whole, which is shorter than its diff:
```python
import functools

import jax
import jax.numpy as jnp
from jax import lax
from jax.experimental import pallas as pl
from jax.experimental.pallas import tpu as pltpu
from jax.sharding import Mesh
from jax.sharding import PartitionSpec as P

G = 4
C = 128
HW = G * C
TOPM = 6
EPSILON = 1e-06
BF = jnp.bfloat16
F32 = jnp.float32
PAD = 16
VMEM_LIMIT = 28 * 1024 * 1024
ANY = pl.BlockSpec(memory_space=pl.ANY)
HBM = pl.BlockSpec(memory_space=pltpu.HBM)
WHOLE = pl.BlockSpec(memory_space=pltpu.VMEM)
SCALARS = pl.BlockSpec(memory_space=pltpu.SMEM)


def params(**more):
    return pltpu.CompilerParams(vmem_limit_bytes=VMEM_LIMIT, **more)


def cost(flops, bytes_accessed):
    return pl.CostEstimate(
        flops=flops // 16, bytes_accessed=bytes_accessed // 16, transcendentals=0
    )


def in_hbm(array):
    return pltpu.with_memory_space_constraint(array, pltpu.HBM)


def hbm_out(shape, dtype=BF):
    return pltpu.HBM(shape, dtype)


def inverse_rms(values):
    return lax.rsqrt(jnp.mean(values * values, axis=-1, keepdims=True) + EPSILON)


def dot(a, b):
    return jnp.dot(a, b, preferred_element_type=F32)


def dot_t(a, b):
    return lax.dot_general(a, b, (((1,), (1,)), ((), ())), preferred_element_type=F32)


DMA = pltpu.SemaphoreType.DMA
copy = pltpu.make_async_copy


def split_store_kernel(rows_ref, out_hbm, out_ref, sem):
    sends = []
    for h in range(G):
        key = rows_ref[:, h * C : (h + 1) * C].astype(F32)
        out_ref[h, :, :C] = (key * inverse_rms(key)).astype(BF)
        out_ref[h, :, C:] = rows_ref[:, HW + h * C : HW + (h + 1) * C]
        sends.append(copy(out_ref.at[h], out_hbm.at[h], sem.at[h]))
        sends[-1].start()
    for send in sends:
        send.wait()


def split_store(rows):
    n = rows.shape[0]
    return pl.pallas_call(
        split_store_kernel,
        in_specs=[WHOLE],
        out_specs=HBM,
        out_shape=hbm_out((G, n, 2 * C)),
        scratch_shapes=[pltpu.VMEM((G, n, 2 * C), BF), DMA((G,))],
        compiler_params=params(),
        name="split_store",
        cost_estimate=cost(8 * n * HW, 8 * n * HW),
    )(rows)


def join_pieces_kernel(piece, in_hbm, _, out_hbm, in_ref, wide_ref, joined_ref, out_ref, sem):
    pieces = in_ref.shape[0]
    loads = [copy(in_hbm.at[i], in_ref.at[i], sem.at[i]) for i in range(pieces)]
    for load in loads:
        load.start()
    for i in range(pieces):
        loads[i].wait()
        wide_ref[i] = in_ref[i].astype(F32)
        for m in range(out_ref.shape[0]):
            joined_ref[m, i * piece : (i + 1) * piece, :] = wide_ref[
                i, m * piece : (m + 1) * piece, :
            ]
    out_ref[...] = joined_ref[...].astype(BF)
    send = copy(out_ref, out_hbm, sem.at[0])
    send.start()
    send.wait()


def join_pieces(parts, frames, after):
    pieces, rows, width = parts.shape
    piece = rows // frames
    shape = (frames, pieces * piece, width)
    return pl.pallas_call(
        functools.partial(join_pieces_kernel, piece),
        in_specs=[ANY, ANY],
        out_specs=HBM,
        out_shape=hbm_out(shape),
        scratch_shapes=[
            pltpu.VMEM(parts.shape, BF),
            pltpu.VMEM(parts.shape, F32),
            pltpu.VMEM(shape, F32),
            pltpu.VMEM(shape, BF),
            DMA((pieces,)),
        ],
        compiler_params=params(),
        name="join_pieces",
        cost_estimate=cost(parts.size, 4 * parts.size),
    )(parts, in_hbm(after))


def modulate_kernel(
    act_hbm, affine_ref, weight_hbm, factor_ref, tail_ref, _, hidden_hbm, query_hbm,
    act_ref, weight_ref, hidden_ref, query_ref, load_sem, weight_sem, store_sem, query_sem,
):
    steps, rows, _ = act_ref.shape
    patches = query_ref.shape[1] - PAD
    loads, stores = [], []
    for i in range(steps):
        at = pl.ds(i * rows, rows)
        loads.append(copy(act_hbm.at[at, :], act_ref.at[i], load_sem.at[i]))
        stores.append(copy(hidden_ref.at[i], hidden_hbm.at[at, :], store_sem.at[i]))
    weight_load = copy(weight_hbm.at[:, pl.ds(0, HW)], weight_ref, weight_sem)
    loads[0].start()
    weight_load.start()
    for load in loads[1:]:
        load.start()
    for h in range(G):
        query_ref[h, patches:, :] = tail_ref[...]
    for i in range(steps):
        at = slice(i * rows, (i + 1) * rows)
        loads[i].wait()
        act = act_ref[i].astype(F32)
        hidden = act * inverse_rms(act) * (1.0 + affine_ref[0:1, :]) + affine_ref[1:2, :]
        hidden = hidden.astype(BF)
        hidden_ref[i] = hidden
        stores[i].start()
        if i == 0:
            weight_load.wait()
        mapped = dot(hidden, weight_ref[...]).astype(BF).astype(F32)
        for h in range(G):
            one = mapped[:, h * C : (h + 1) * C]
            query_ref[h, at, :] = (one * inverse_rms(one) * factor_ref[0, h]).astype(BF)
    send = copy(query_ref, query_hbm, query_sem)
    send.start()
    for store in stores:
        store.wait()
    send.wait()


def modulate(act, affine, weight, factor, tail, after):
    patches, depth = act.shape
    steps = 2
    rows = patches // steps
    shape = (G, patches + PAD, C)
    return pl.pallas_call(
        modulate_kernel,
        in_specs=[HBM, WHOLE, HBM, SCALARS, WHOLE, ANY],
        out_specs=[HBM, HBM],
        out_shape=[hbm_out((patches, depth)), hbm_out(shape)],
        scratch_shapes=[
            pltpu.VMEM((steps, rows, depth), BF),
            pltpu.VMEM((depth, HW), BF),
            pltpu.VMEM((steps, rows, depth), BF),
            pltpu.VMEM(shape, BF),
            DMA((steps,)),
            DMA,
            DMA((steps,)),
            DMA,
        ],
        compiler_params=params(),
        name="modulate",
        cost_estimate=cost(
            2 * patches * depth * HW, 4 * patches * depth + 2 * depth * HW + 2 * patches * HW
        ),
    )(in_hbm(act), affine, in_hbm(weight), factor, tail, in_hbm(after))


def temporal_entry_kernel(
    quarters, hidden_hbm, weight_hbm, factor_ref, out_hbm,
    hidden_ref, weight_ref, out_ref, hidden_sem, weight_sem, store_sem,
):
    rows = hidden_ref.shape[0] // quarters
    hidden_load = copy(hidden_hbm, hidden_ref, hidden_sem)
    loads = [
        copy(
            weight_hbm.at[:, pl.ds((3 + part) * HW, HW)], weight_ref.at[part], weight_sem.at[part]
        )
        for part in range(3)
    ]
    loads[0].start()
    hidden_load.start()
    for load in loads[1:]:
        load.start()
    hidden_load.wait()
    stores = []
    for part in range(3):
        loads[part].wait()
        mapped = dot(hidden_ref[...], weight_ref[part]).astype(BF)
        for h in range(G):
            done = mapped[:, h * C : (h + 1) * C]
            if part < 2:
                one = done.astype(F32)
                one = one * inverse_rms(one)
                if part == 0:
                    one = one * factor_ref[1, h]
                done = one.astype(BF)
            for z in range(quarters):
                out_ref[part, z, h] = done[z * rows : (z + 1) * rows, :]
        stores.append(copy(out_ref.at[part], out_hbm.at[:, :, part], store_sem.at[part]))
        stores[-1].start()
    for store in stores:
        store.wait()


def temporal_entry(hidden, weight, factor, quarters):
    patches, depth = hidden.shape
    rows = patches // quarters
    return pl.pallas_call(
        functools.partial(temporal_entry_kernel, quarters),
        in_specs=[HBM, HBM, SCALARS],
        out_specs=HBM,
        out_shape=hbm_out((quarters, G, 3, rows, C)),
        scratch_shapes=[
            pltpu.VMEM((patches, depth), BF),
            pltpu.VMEM((3, depth, HW), BF),
            pltpu.VMEM((3, quarters, G, rows, C), BF),
            DMA,
            DMA((3,)),
            DMA((3,)),
        ],
        compiler_params=params(),
        name="temporal_entry",
        cost_estimate=cost(
            6 * patches * depth * HW, 2 * patches * depth + 6 * depth * HW + 6 * patches * HW
        ),
    )(in_hbm(hidden), in_hbm(weight), factor)


def temporal_attend_kernel(length_ref, in_hbm_ref, _, out_hbm, in_ref, out_ref, sem):
    frames, _, rows, _ = in_ref.shape
    group = 16
    size = frames * group
    load = copy(in_hbm_ref, in_ref, sem)
    load.start()
    length = length_ref[0]
    row = lax.broadcasted_iota(jnp.int32, (size, size), 0)
    column = lax.broadcasted_iota(jnp.int32, (size, size), 1)
    target, source = row // group, column // group
    keep = (row % group == column % group) & (source <= target) & (source > target - length)
    load.wait()
    for g in range(rows // group):
        at = slice(g * group, (g + 1) * group)
        query = in_ref[:, 0, at, :].reshape(size, C)
        key = in_ref[:, 1, at, :].reshape(size, C)
        value = in_ref[:, 2, at, :].reshape(size, C)
        weights = jnp.where(keep, jnp.exp(dot_t(query, key)), 0.0)
        shares = weights / jnp.sum(weights, axis=-1, keepdims=True)
        result = dot(shares.astype(BF), value).astype(BF)
        out_ref[:, at, :] = result.reshape(frames, group, C)
    store = copy(out_ref, out_hbm, sem)
    store.start()
    store.wait()


def temporal_attend(length, parts, after):
    frames, _, rows, _ = parts.shape
    shape = (frames, rows, C)
    return pl.pallas_call(
        temporal_attend_kernel,
        in_specs=[SCALARS, ANY, ANY],
        out_specs=HBM,
        out_shape=hbm_out(shape),
        scratch_shapes=[pltpu.VMEM(parts.shape, BF), pltpu.VMEM(shape, BF), DMA],
        compiler_params=params(),
        name="temporal_attend",
        cost_estimate=cost(4 * frames * rows * 256 * C, 8 * frames * rows * C),
    )(length, parts, in_hbm(after))


LINE = 96
CHUNK = 3 * LINE


def halves(denominators):
    high = denominators.astype(BF).astype(F32)
    return jnp.concatenate([high, denominators - high], axis=0).astype(BF)


def attend_rows(query, keys, both, out_ref):
    patches = out_ref.shape[0] - PAD
    row = lax.broadcasted_iota(jnp.int32, (LINE, C), 0)
    column = lax.broadcasted_iota(jnp.int32, (LINE, C), 1)
    lines = []
    for start in range(0, patches, CHUNK):
        at = slice(start, start + CHUNK)
        weights = jnp.exp(dot_t(query(at), keys)).astype(BF)
        result = dot(weights, both)
        out_ref[at, :] = result[:, :C].astype(BF)
        for j in range(0, CHUNK, LINE):
            diagonal = jnp.where(row == column, result[j : j + LINE, C:], 0.0)
            lines.append(jnp.sum(diagonal, axis=0, keepdims=True))
    lines.append(jnp.zeros((8 - len(lines), C), F32))
    out_ref[patches:, :] = halves(jnp.concatenate(lines, axis=0))


def with_ones(values):
    return jnp.concatenate([values, jnp.ones(values.shape, BF)], axis=1)


def own_attend_kernel(
    hidden_hbm, weight_hbm, query_hbm, _, out_hbm,
    hidden_ref, weight_ref, query_ref, out_ref, hidden_sem, weight_sem, query_sem, store_sem,
):
    hidden_load = copy(hidden_hbm, hidden_ref, hidden_sem)
    query_load = copy(query_hbm, query_ref, query_sem)
    loads = [
        copy(
            weight_hbm.at[:, pl.ds((1 + part) * HW, HW)], weight_ref.at[part], weight_sem.at[part]
        )
        for part in range(2)
    ]
    loads[0].start()
    hidden_load.start()
    loads[1].start()
    query_load.start()
    hidden_load.wait()
    loads[0].wait()
    keys = dot(hidden_ref[...], weight_ref[0]).astype(BF)
    loads[1].wait()
    values = dot(hidden_ref[...], weight_ref[1]).astype(BF)
    query_load.wait()
    stores = []
    for h in range(G):
        key = keys[:, h * C : (h + 1) * C].astype(F32)
        key = (key * inverse_rms(key)).astype(BF)
        both = with_ones(values[:, h * C : (h + 1) * C])
        attend_rows(lambda at, h=h: query_ref[h, at, :], key, both, out_ref.at[h])
        stores.append(copy(out_ref.at[h], out_hbm.at[h], store_sem.at[h]))
        stores[-1].start()
    for store in stores:
        store.wait()


def own_attend(hidden, weight, query, after):
    patches, depth = hidden.shape
    return pl.pallas_call(
        own_attend_kernel,
        in_specs=[HBM, HBM, HBM, ANY],
        out_specs=HBM,
        out_shape=hbm_out(query.shape),
        scratch_shapes=[
            pltpu.VMEM((patches, depth), BF),
            pltpu.VMEM((2, depth, HW), BF),
            pltpu.VMEM(query.shape, BF),
            pltpu.VMEM(query.shape, BF),
            DMA,
            DMA((2,)),
            DMA,
            DMA((G,)),
        ],
        compiler_params=params(),
        name="own_attend",
        cost_estimate=cost(
            4 * patches * depth * HW + 6 * patches * patches * HW,
            2 * patches * depth + 4 * depth * HW + 10 * patches * HW,
        ),
    )(in_hbm(hidden), in_hbm(weight), in_hbm(query), in_hbm(after))


def memory_attend_kernel(count, index_ref, query_hbm, *refs):
    blocks = refs[:count]
    out_hbm, query_ref, store_ref, out_ref, query_sem, block_sem, store_sem = refs[count + 1 :]
    frames = query_ref.shape[0]
    held = blocks[0].shape[0]
    loads = [
        copy(blocks[i], store_ref.at[pl.ds(i * held, held)], block_sem.at[i]) for i in range(count)
    ]
    query_load = copy(query_hbm, query_ref, query_sem)
    for load in loads:
        load.start()
    query_load.start()
    for load in loads:
        load.wait()
    query_load.wait()
    stores = []
    for i in range(frames):
        chosen = [store_ref[index_ref[i, j]] for j in range(TOPM)]
        keys = jnp.concatenate([block[:, :C] for block in chosen], axis=0)
        values = jnp.concatenate([block[:, C:] for block in chosen], axis=0)
        attend_rows(lambda at, i=i: query_ref[i, at, :], keys, with_ones(values), out_ref.at[i])
        stores.append(copy(out_ref.at[i], out_hbm.at[i], store_sem.at[i]))
        stores[-1].start()
    for store in stores:
        store.wait()


def memory_attend(index, query, blocks, after):
    frames, rows, _ = query.shape
    held, quarter, width = blocks[0].shape
    count = len(blocks)
    return pl.pallas_call(
        functools.partial(memory_attend_kernel, count),
        in_specs=[SCALARS, ANY] + [ANY] * count + [ANY],
        out_specs=HBM,
        out_shape=hbm_out(query.shape),
        scratch_shapes=[
            pltpu.VMEM(query.shape, BF),
            pltpu.VMEM((count * held, quarter, width), BF),
            pltpu.VMEM(query.shape, BF),
            DMA,
            DMA((count,)),
            DMA((frames,)),
        ],
        compiler_params=params(),
        name="memory_attend",
        cost_estimate=cost(
            8 * frames * rows * TOPM * quarter * C,
            4 * query.size + 2 * count * held * quarter * width,
        ),
    )(index, query, *blocks, in_hbm(after))


def add_partials_kernel(*refs):
    ins, out_hbm, parts_ref, out_ref, load_sem, store_sem = (
        refs[: len(refs) - 5], *refs[len(refs) - 5 :],
    )
    frames = out_ref.shape[0]
    patches = out_ref.shape[1] - PAD
    loads = [
        [copy(ref.at[i], parts_ref.at[k, i], load_sem.at[k, i]) for k, ref in enumerate(ins)]
        for i in range(frames)
    ]
    for of_frame in loads:
        for load in of_frame:
            load.start()
    stores = []
    for i in range(frames):
        for load in loads[i]:
            load.wait()
        total = parts_ref[0, i].astype(F32)
        for k in range(1, len(ins)):
            total = total + parts_ref[k, i].astype(F32)
        out_ref[i, :patches, :] = total[:patches].astype(BF)
        out_ref[i, patches:, :] = halves(total[patches : patches + 8] + total[patches + 8 :])
        stores.append(copy(out_ref.at[i], out_hbm.at[i], store_sem.at[i]))
        stores[-1].start()
    for store in stores:
        store.wait()


def add_partials(parts):
    shape = parts[0].shape
    frames = shape[0]
    return pl.pallas_call(
        add_partials_kernel,
        in_specs=[ANY] * len(parts),
        out_specs=HBM,
        out_shape=hbm_out(shape),
        scratch_shapes=[
            pltpu.VMEM((len(parts),) + shape, BF),
            pltpu.VMEM(shape, BF),
            DMA((len(parts), frames)),
            DMA((frames,)),
        ],
        compiler_params=params(),
        name="add_partials",
        cost_estimate=cost(4 * parts[0].size, 8 * parts[0].size),
    )(*parts)


def leave_kernel(
    own_hbm, memory_hbm, time_hbm, weight_hbm, out_hbm,
    own_ref, memory_ref, time_ref, combined_ref, weight_ref, out_ref,
    own_sem, memory_sem, time_sem, weight_sem, store_sem,
):
    patches = own_ref.shape[1] - PAD
    quarters = time_ref.shape[0] // G
    rows = time_ref.shape[1]
    steps, _, width = weight_ref.shape
    own_loads = [copy(own_hbm.at[h], own_ref.at[h], own_sem.at[h]) for h in range(G)]
    memory_loads = [copy(memory_hbm.at[h], memory_ref.at[h], memory_sem.at[h]) for h in range(G)]
    time_load = copy(time_hbm, time_ref, time_sem)
    loads, stores = [], []
    for i in range(steps):
        at = pl.ds(i * width, width)
        loads.append(copy(weight_hbm.at[:, at], weight_ref.at[i], weight_sem.at[i]))
        stores.append(copy(out_ref.at[i], out_hbm.at[:, at], store_sem.at[i]))
    for load in own_loads + memory_loads + [time_load] + loads:
        load.start()
    row = lax.broadcasted_iota(jnp.int32, (LINE, C), 0)
    column = lax.broadcasted_iota(jnp.int32, (LINE, C), 1)
    for h in range(G):
        own_loads[h].wait()
        memory_loads[h].wait()
        tail = own_ref[h, patches:, :].astype(F32) + memory_ref[h, patches:, :].astype(F32)
        denominators = tail[:8] + tail[8:]
        for j in range(patches // LINE):
            at = slice(j * LINE, (j + 1) * LINE)
            line = jnp.broadcast_to(denominators[j : j + 1, :], (LINE, C))
            total = jnp.sum(jnp.where(row == column, line, 0.0), axis=1, keepdims=True)
            top = own_ref[h, at, :].astype(F32) + memory_ref[h, at, :].astype(F32)
            combined_ref[at, h * C : (h + 1) * C] = (top / total).astype(BF)
    time_load.wait()
    for h in range(G):
        for z in range(quarters):
            combined_ref[z * rows : (z + 1) * rows, HW + h * C : HW + (h + 1) * C] = time_ref[
                z * G + h
            ]
    for i in range(steps):
        loads[i].wait()
        out_ref[i] = dot(combined_ref[...], weight_ref[i]).astype(BF)
        stores[i].start()
    for store in stores:
        store.wait()


def leave(own, memory, time, weight):
    patches = own.shape[1] - PAD
    depth, width = weight.shape
    steps = 4
    step = width // steps
    return pl.pallas_call(
        leave_kernel,
        in_specs=[HBM, ANY, ANY, HBM],
        out_specs=HBM,
        out_shape=hbm_out((patches, width)),
        scratch_shapes=[
            pltpu.VMEM(own.shape, BF),
            pltpu.VMEM(memory.shape, BF),
            pltpu.VMEM(time.shape, BF),
            pltpu.VMEM((patches, depth), BF),
            pltpu.VMEM((steps, depth, step), BF),
            pltpu.VMEM((steps, patches, step), BF),
            DMA((G,)),
            DMA((G,)),
            DMA,
            DMA((steps,)),
            DMA((steps,)),
        ],
        compiler_params=params(),
        name="leave",
        cost_estimate=cost(
            2 * patches * depth * width,
            2 * depth * width + 2 * patches * width + 6 * patches * depth,
        ),
    )(in_hbm(own), memory, time, in_hbm(weight))


def on_device(
    patch_activation_tensor,
    conditioning_affine,
    entry_projection_matrix,
    exit_projection_matrix,
    softmax_sharpness,
    cached_past_pairs,
    recalled_picture_holder,
    recalled_picture_position,
    lookback_lengths,
):
    rings = lax.axis_size("z")
    patches, depth = patch_activation_tensor.shape[2:]
    held, piece = cached_past_pairs.shape[:2]
    rolls_y, cores = lax.axis_size("y"), lax.axis_size("c")

    def turn(step):
        return [(s, (s + step) % rings) for s in range(rings)]

    other = [(s, cores - 1 - s) for s in range(cores)]

    def swap(blocks, axes):
        return lax.all_to_all(blocks, axes, split_axis=0, concat_axis=0, tiled=True)

    with jax.named_scope("store"):
        split = split_store(cached_past_pairs.reshape(held * piece, 2 * HW))
        pieces = swap(split, "x")

    with jax.named_scope("queries"):
        factor = softmax_sharpness / C
        index = recalled_picture_holder.reshape(TOPM) * held + recalled_picture_position.reshape(
            TOPM
        )
        tail = jnp.zeros((PAD, C), BF).at[0, :TOPM].set(index.astype(BF))
        hidden, query = modulate(
            patch_activation_tensor.reshape(patches, depth),
            conditioning_affine.reshape(2, depth),
            entry_projection_matrix,
            factor,
            tail,
            after=split,
        )
        here = swap(query, "x")

    with jax.named_scope("temporal"):
        parts = temporal_entry(hidden, entry_projection_matrix, factor, rings)

    with jax.named_scope("store"):
        joined = join_pieces(pieces, held, after=parts)
        near = [joined] + [lax.ppermute(joined, "y", turn(-step)) for step in (1, 2, 3)]
        beside = [lax.ppermute(block, "c", other) for block in near]

    with jax.named_scope("queries"):
        here, joined = lax.optimization_barrier((here, joined))
        groups = [here] + [lax.ppermute(here, "z", turn(-step)) for step in (1, 2, 3)]

    with jax.named_scope("temporal"):
        sent = swap(parts.reshape((rings * G,) + parts.shape[2:]), ("z", "x"))

    with jax.named_scope("own"):
        own = own_attend(hidden, entry_projection_matrix, query, after=joined)

    def attend(group, after):
        named = group[:, patches, :TOPM].astype(jnp.int32)
        y = (named // (cores * held) - lax.axis_index("y")) & (rolls_y - 1)
        c = (named // held & (cores - 1)) ^ lax.axis_index("c")
        index = (c * rolls_y + y) * held + (named & (held - 1))
        return memory_attend(index, group, near + beside, after)

    with jax.named_scope("memory"):
        after, sums = own, []
        for step in (2, 1, 3):
            after = attend(groups[step], after)
            sums.append(lax.ppermute(after, "z", turn(step)))
        sum_here = attend(here, after)

    with jax.named_scope("temporal"):
        timed = temporal_attend(lookback_lengths, sent, after=sum_here)
        time = swap(timed, ("z", "x"))

    with jax.named_scope("memory"):
        memory = swap(add_partials([sum_here] + sums), "x")

    with jax.named_scope("exit"):
        attended = leave(own, memory, time, exit_projection_matrix)
    return attended.reshape(1, 1, patches, depth)


def solution(mesh):
    apart = Mesh(mesh.devices.reshape(4, 2, 4, 4), ("y", "c", "z", "x"))
    roll, frame = ("y", "c"), ("z", "x")
    return jax.shard_map(
        on_device,
        mesh=apart,
        in_specs=(
            P(roll, frame, None, None),
            P(roll, frame, None, None),
            P(),
            P(),
            P(),
            P(roll, frame, None, None),
            P(roll, frame, None, None),
            P(roll, frame, None),
            P(roll),
        ),
        out_specs=P(roll, frame, None, None),
        check_vma=False,
    )
```

time: 163 us -> 147 us (0.902)
  local copies, waits for them, and re-layouts: 27.3 us -> 1.23 us
  Pallas kernels: 44.2 us -> 57.9 us
    unnamed x36 -> x15, local copies, waits for them, and re-layouts: 26.5 us -> 1.22 us
    ppermute x9, waiting for transfers between devices: 34.4 us -> 23.3 us  [the longest x3 15.7 us: on_device(): lax.ppermute(here, 'z', turn(-step))]
    pallas_call x10, Pallas kernels: 32.5 us -> 43.1 us  [the longest x4 20.7 us: memory_attend(): pl.pallas_call(functools.partial(memory_attend_kernel, count), in_specs=[...]
    all_to_all x4, waiting for transfers between devices: 1.81 us -> 9.85 us  [swap(): return lax.all_to_all(blocks, axes, split_axis=0, concat_axis=0, tiled=True)]
    pallas_call x1, Pallas kernels: 6.8 us -> 9.06 us  [temporal_entry(): pl.pallas_call(functools.partial(temporal_entry_kernel, quarters), in_spe...]
    ppermute x4, waiting for transfers between devices: 0.01 us -> 1.91 us  [on_device(): beside = [lax.ppermute(block, 'c', other) for block in near]]
  transfers between devices with their start and end apart: 17 -> 17, of which waited for: 4 -> 8; matrix products, arithmetic and copies ran while one was open for 8% -> 1% of each run, Pallas kernels for 23% -> 35%
where the time goes in v5:
time: 147 us
  Pallas kernels  57.9 us (39%)
  starting transfers between devices  38.2 us (26%)
  waiting for transfers between devices  35.1 us (24%)
  blocking collectives  12.4 us (8%)
    pallas_call x4, Pallas kernels, memory_attend(): pl.pallas_call(functools.partial(memory_attend_kernel, count), in_specs=[...  20.7 us
    all_to_all x4, starting transfers between devices, swap(): return lax.all_to_all(blocks, axes, split_axis=0, concat_axis=0, tiled=True)  18.9 us
    ppermute x3, waiting for transfers between devices, on_device(): lax.ppermute(here, 'z', turn(-step))  15.7 us
    all_to_all x1, blocking collectives, swap(): return lax.all_to_all(blocks, axes, split_axis=0, concat_axis=0, tiled=True)  12.4 us
    all_to_all x4, waiting for transfers between devices, swap(): return lax.all_to_all(blocks, axes, split_axis=0, concat_axis=0, tiled=True)  9.85 us
    ppermute x3, starting transfers between devices, on_device(): lax.ppermute(here, 'z', turn(-step))  9.22 us
    pallas_call x1, Pallas kernels, temporal_entry(): pl.pallas_call(functools.partial(temporal_entry_kernel, quarters), in_spe...  9.06 us
    pallas_call x1, Pallas kernels, own_attend(): pl.pallas_call(own_attend_kernel, in_specs=[HBM, HBM, HBM, ANY], out_spec...  8.06 us
  transfers between devices with their start and end apart: 17, of which 8 were waited for; matrix products, arithmetic and copies ran while one was open for 1% of the time, Pallas kernels for 35%

profile of v5, /device:TPU:0, one launch (start us, length us, event | category | flops | bytes accessed | tf_op | source)
XLA Modules:
  0.0 146.6 jit_solution(8413753039921454431)
XLA Ops:
  0.0 0.0 copy-start.6
  0.0 0.0 copy-start.5
  0.0 0.0 copy-start.4
  0.0 0.0 copy-start.3
  0.0 1.2 copy.10
  1.2 1.0 split_store.1._
  2.2 4.4 %all-to-all-start.1 = ((bf16[4,288,256]{2,1,0:T(8,128)(2,1)}), bf16[4,288,256]{2,1,0:T(8,128)(2,1)S(1)}, u32[]{:S(2)}, u32[]{:S(2)}) async-start(bf16[4,288,256]{2,1,0:T(8,128)(2,1)} %split_store.1._), calls=%async_computation.1 | async-start | bytes 1179648 | tf_op jit(solution)/shard_map/store/all_to_all | solution.py:586
  6.6 0.0 copy-done.6
  6.6 0.0 copy-done.5
  6.7 0.0 copy-done.4
  6.7 0.0 copy-done.3
  6.7 5.8 %modulate.1 = (bf16[576,2048]{1,0:T(8,128)(2,1)}, bf16[4,592,128]{2,1,0:T(8,128)(2,1)}) custom-call(bf16[576,2048]{1,0:T(8,128)(2,1)} %bitcast.20, f32[2,2048]{1,0:T(2,128)S(1)} %bitcast.18, bf16[2048,3072]{1,0:T(8,128)(2,1)} %weight_hbm.6, f32[2,4]{1,0:T(2,128)S(1)} %broadcast_multiply_fusion.factor_ref, bf16[16,128]{1,0:T(8,128)(2,1)S(1)} %scatter.4.tail_ref, ...), custom_call_target="tpu_custom_call" | custom-call | flops 75497472 | bytes 462848 | tf_op jit(solution)/shard_map/queries/modulate/pallas_call | solution.py:170
  12.5 4.4 %all-to-all-done.1.in_hbm = bf16[4,288,256]{2,1,0:T(8,128)(2,1)S(1)} async-done(((bf16[4,288,256]{2,1,0:T(8,128)(2,1)}), bf16[4,288,256]{2,1,0:T(8,128)(2,1)S(1)}, u32[]{:S(2)}, u32[]{:S(2)}) %all-to-all-start.1) | async-done | bytes 589856 | tf_op jit(solution)/shard_map/store/all_to_all | solution.py:586
  16.8 3.5 %all-to-all-start = ((bf16[4,592,128]{2,1,0:T(8,128)(2,1)}), bf16[4,592,128]{2,1,0:T(8,128)(2,1)S(1)}, u32[]{:S(2)}, u32[]{:S(2)}) async-start(bf16[4,592,128]{2,1,0:T(8,128)(2,1)} %get-tuple-element.22.query_hbm), calls=%async_computation | async-start | bytes 1212416 | tf_op jit(solution)/shard_map/queries/all_to_all | solution.py:586
  20.3 9.1 %temporal_entry.1._ = bf16[4,4,3,144,128]{4,3,2,1,0:T(8,128)(2,1)} custom-call(bf16[576,2048]{1,0:T(8,128)(2,1)} %get-tuple-element.21.hidden_hbm, bf16[2048,3072]{1,0:T(8,128)(2,1)} %weight_hbm.6, f32[2,4]{1,0:T(2,128)S(1)} %broadcast_multiply_fusion.factor_ref), custom_call_target="tpu_custom_call" | custom-call | flops 226492416 | bytes 651264 | tf_op jit(solution)/shard_map/temporal/temporal_entry/pallas_call | solution.py:233
  29.4 1.8 %join_pieces.1._.refs_0_ = bf16[8,144,256]{2,1,0:T(8,128)(2,1)} custom-call(bf16[4,288,256]{2,1,0:T(8,128)(2,1)S(1)} %all-to-all-done.1.in_hbm, bf16[4,4,3,144,128]{4,3,2,1,0:T(8,128)(2,1)} %temporal_entry.1._), custom_call_target="tpu_custom_call" | custom-call | flops 18432 | bytes 73728 | tf_op jit(solution)/shard_map/store/join_pieces/pallas_call | solution.py:108
  31.1 0.0 copy-start
  31.1 0.0 all-to-all-done.query_hbm
  31.2 4.0 %collective-permute-start.9 = (bf16[4,592,128]{2,1,0:T(8,128)(2,1)S(1)}, bf16[4,592,128]{2,1,0:T(8,128)(2,1)}, u32[]{:S(2)}, u32[]{:S(2)}) collective-permute-start(bf16[4,592,128]{2,1,0:T(8,128)(2,1)S(1)} %all-to-all-done.query_hbm), channel_id=1, source_target_pairs={{0,8},{4,12},{8,0},{12,4},{1,9},{5,13},{9,1},{13,5},{2,10},{6,14},... | collective-permute-start | bytes 1818632 | tf_op jit(solution)/shard_map/queries/ppermute | solution.py:618
  35.1 5.3 %all-to-all-start.3 = ((bf16[16,3,144,128]{3,2,1,0:T(8,128)(2,1)}), bf16[16,3,144,128]{3,2,1,0:T(8,128)(2,1)S(1)}, u32[]{:S(2)}, u32[]{:S(2)}) async-start(bf16[16,3,144,128]{3,2,1,0:T(8,128)(2,1)} %bitcast.19), calls=%async_computation.3 | async-start | bytes 3538944 | tf_op jit(solution)/shard_map/temporal/all_to_all | solution.py:586
  41.1 0.0 copy-done
  41.1 3.1 %collective-permute-start = (bf16[8,144,256]{2,1,0:T(8,128)(2,1)S(1)}, bf16[8,144,256]{2,1,0:T(8,128)(2,1)S(1)}, u32[]{:S(2)}, u32[]{:S(2)}) collective-permute-start(bf16[8,144,256]{2,1,0:T(8,128)(2,1)S(1)} %copy-done), channel_id=1, source_target_pairs={{0,96},{32,0},{64,32},{96,64},{1,97},{33,1},{65,33},{97,65},{2,98}... | collective-permute-start | bytes 1769480 | tf_op jit(solution)/shard_map/store/ppermute | solution.py:613
  44.2 0.6 collective-permute-start.1
  44.8 1.0 collective-permute-start.2
  45.8 3.1 %collective-permute-start.8 = (bf16[4,592,128]{2,1,0:T(8,128)(2,1)S(1)}, bf16[4,592,128]{2,1,0:T(8,128)(2,1)S(1)}, u32[]{:S(2)}, u32[]{:S(2)}) collective-permute-start(bf16[4,592,128]{2,1,0:T(8,128)(2,1)S(1)} %all-to-all-done.query_hbm), channel_id=1, source_target_pairs={{0,12},{4,0},{8,4},{12,8},{1,13},{5,1},{9,5},{13,9},{2,14},{6,2},{... | collective-permute-start | bytes 1818632 | tf_op jit(solution)/shard_map/queries/ppermute | solution.py:618
  48.9 0.0 copy-start.1
  48.9 8.1 %own_attend.1.refs_8_.own_hbm = bf16[4,592,128]{2,1,0:T(8,128)(2,1)} custom-call(bf16[576,2048]{1,0:T(8,128)(2,1)} %get-tuple-element.21.hidden_hbm, bf16[2048,3072]{1,0:T(8,128)(2,1)} %weight_hbm.6, bf16[4,592,128]{2,1,0:T(8,128)(2,1)} %get-tuple-element.22.query_hbm, bf16[8,144,256]{2,1,0:T(8,128)(2,1)} %join_pieces.1._.refs_0_), custom_call_target="tpu_custom_call" | custom-call | flops 214695936 | bytes 593920 | tf_op jit(solution)/shard_map/own/own_attend/pallas_call | solution.py:361
  57.0 6.5 %collective-permute-done.9.query_hbm = bf16[4,592,128]{2,1,0:T(8,128)(2,1)} collective-permute-done((bf16[4,592,128]{2,1,0:T(8,128)(2,1)S(1)}, bf16[4,592,128]{2,1,0:T(8,128)(2,1)}, u32[]{:S(2)}, u32[]{:S(2)}) %collective-permute-start.9) | collective-permute-done | bytes 606240 | tf_op jit(solution)/shard_map/queries/ppermute | solution.py:618
  63.5 2.1 %collective-permute-start.7 = (bf16[4,592,128]{2,1,0:T(8,128)(2,1)S(1)}, bf16[4,592,128]{2,1,0:T(8,128)(2,1)S(1)}, u32[]{:S(2)}, u32[]{:S(2)}) collective-permute-start(bf16[4,592,128]{2,1,0:T(8,128)(2,1)S(1)} %all-to-all-done.query_hbm), channel_id=1, source_target_pairs={{0,4},{4,8},{8,12},{12,0},{1,5},{5,9},{9,13},{13,1},{2,6},{6,10},{... | collective-permute-start | bytes 1818632 | tf_op jit(solution)/shard_map/queries/ppermute | solution.py:618
  65.6 0.7 slice_convert_fusion
  66.4 1.0 collective-permute-done.refs_1_
  67.4 0.0 copy-done.1
  67.4 0.0 collective-permute-start.3
  67.4 0.0 collective-permute-done.1.refs_2_
  67.4 0.5 collective-permute-start.4
  67.9 3.2 %collective-permute-done.2.refs_3_ = bf16[8,144,256]{2,1,0:T(8,128)(2,1)S(1)} collective-permute-done((bf16[8,144,256]{2,1,0:T(8,128)(2,1)S(1)}, bf16[8,144,256]{2,1,0:T(8,128)(2,1)S(1)}, u32[]{:S(2)}, u32[]{:S(2)}) %collective-permute-start.2) | collective-permute-done | bytes 589856 | tf_op jit(solution)/shard_map/store/ppermute | solution.py:613
  71.1 0.0 collective-permute-start.5
  71.1 9.2 %collective-permute-done.8.query_hbm = bf16[4,592,128]{2,1,0:T(8,128)(2,1)S(1)} collective-permute-done((bf16[4,592,128]{2,1,0:T(8,128)(2,1)S(1)}, bf16[4,592,128]{2,1,0:T(8,128)(2,1)S(1)}, u32[]{:S(2)}, u32[]{:S(2)}) %collective-permute-start.8) | collective-permute-done | bytes 606240 | tf_op jit(solution)/shard_map/queries/ppermute | solution.py:618
  80.3 0.0 collective-permute-start.6
  80.4 0.0 collective-permute-done.7.query_hbm
  80.4 0.0 collective-permute-done.3.refs_4_
  80.4 0.0 collective-permute-done.4.refs_5_
  80.4 0.0 collective-permute-done.5.refs_6_
  80.4 1.9 %collective-permute-done.6.refs_7_ = bf16[8,144,256]{2,1,0:T(8,128)(2,1)S(1)} collective-permute-done((bf16[8,144,256]{2,1,0:T(8,128)(2,1)S(1)}, bf16[8,144,256]{2,1,0:T(8,128)(2,1)S(1)}, u32[]{:S(2)}, u32[]{:S(2)}) %collective-permute-start.6) | collective-permute-done | bytes 589856 | tf_op jit(solution)/shard_map/store/ppermute | solution.py:614
  82.3 5.8 %memory_attend.4.refs_8_ = bf16[4,592,128]{2,1,0:T(8,128)(2,1)} custom-call(s32[4,6]{1,0:T(4,128)S(1)} %fusion.36.index_ref, bf16[4,592,128]{2,1,0:T(8,128)(2,1)} %collective-permute-done.9.query_hbm, bf16[8,144,256]{2,1,0:T(8,128)(2,1)S(1)} %copy-done.1, bf16[8,144,256]{2,1,0:T(8,128)(2,1)S(1)} %collective-permute-done.refs_1_, ...), custom_call_target="tpu_custom_call" | custom-call | flops 130940928 | bytes 370688 | tf_op jit(solution)/shard_map/memory/memory_attend/pallas_call | solution.py:416
  88.2 1.2 collective-permute-start.10
  89.4 4.9 %memory_attend.5.refs_8_ = bf16[4,592,128]{2,1,0:T(8,128)(2,1)} custom-call(s32[4,6]{1,0:T(4,128)S(1)} %fusion.26.index_ref, bf16[4,592,128]{2,1,0:T(8,128)(2,1)S(1)} %collective-permute-done.8.query_hbm, bf16[8,144,256]{2,1,0:T(8,128)(2,1)S(1)} %copy-done.1, bf16[8,144,256]{2,1,0:T(8,128)(2,1)S(1)} %collective-permute-done.refs_1_, ...), custom_call_target="tpu_custom_call" | custom-call | flops 130940928 | bytes 370688 | tf_op jit(solution)/shard_map/memory/memory_attend/pallas_call | solution.py:416
  94.4 2.4 %collective-permute-start.11 = (bf16[4,592,128]{2,1,0:T(8,128)(2,1)}, bf16[4,592,128]{2,1,0:T(8,128)(2,1)}, u32[]{:S(2)}, u32[]{:S(2)}) collective-permute-start(bf16[4,592,128]{2,1,0:T(8,128)(2,1)} %memory_attend.5.refs_8_), channel_id=1, source_target_pairs={{0,4},{4,8},{8,12},{12,0},{1,5},{5,9},{9,13},{13,1},{2,6},{6,10},{... | collective-permute-start | bytes 1818632 | tf_op jit(solution)/shard_map/memory/ppermute | solution.py:637
  96.8 5.0 %memory_attend.6.refs_8_ = bf16[4,592,128]{2,1,0:T(8,128)(2,1)} custom-call(s32[4,6]{1,0:T(4,128)S(1)} %fusion.16.index_ref, bf16[4,592,128]{2,1,0:T(8,128)(2,1)S(1)} %collective-permute-done.7.query_hbm, bf16[8,144,256]{2,1,0:T(8,128)(2,1)S(1)} %copy-done.1, bf16[8,144,256]{2,1,0:T(8,128)(2,1)S(1)} %collective-permute-done.refs_1_, ...), custom_call_target="tpu_custom_call" | custom-call | flops 130940928 | bytes 370688 | tf_op jit(solution)/shard_map/memory/memory_attend/pallas_call | solution.py:416
  101.7 1.2 collective-permute-start.12
  102.9 4.9 %memory_attend.7.refs_0_._ = bf16[4,592,128]{2,1,0:T(8,128)(2,1)} custom-call(s32[4,6]{1,0:T(4,128)S(1)} %fusion.6.index_ref, bf16[4,592,128]{2,1,0:T(8,128)(2,1)S(1)} %all-to-all-done.query_hbm, bf16[8,144,256]{2,1,0:T(8,128)(2,1)S(1)} %copy-done.1, bf16[8,144,256]{2,1,0:T(8,128)(2,1)S(1)} %collective-permute-done.refs_1_, ...), custom_call_target="tpu_custom_call" | custom-call | flops 130940928 | bytes 370688 | tf_op jit(solution)/shard_map/memory/memory_attend/pallas_call | solution.py:416
  107.9 0.0 copy-start.2
  107.9 0.0 all-to-all-done.3.in_hbm_ref
  107.9 2.5 %temporal_attend.1 = bf16[16,144,128]{2,1,0:T(8,128)(2,1)} custom-call(s32[1]{0:T(128)S(6)} %copy.11.length_ref, bf16[16,3,144,128]{3,2,1,0:T(8,128)(2,1)S(1)} %all-to-all-done.3.in_hbm_ref, bf16[4,592,128]{2,1,0:T(8,128)(2,1)} %memory_attend.7.refs_0_._), custom_call_target="tpu_custom_call" | custom-call | flops 18874368 | bytes 147456 | tf_op jit(solution)/shard_map/temporal/temporal_attend/pallas_call | solution.py:283
  110.4 5.7 %all-to-all-start.4 = ((bf16[16,144,128]{2,1,0:T(8,128)(2,1)}), bf16[16,144,128]{2,1,0:T(8,128)(2,1)S(1)}, u32[]{:S(2)}, u32[]{:S(2)}) async-start(bf16[16,144,128]{2,1,0:T(8,128)(2,1)} %temporal_attend.1), calls=%async_computation.4 | async-start | bytes 1179648 | tf_op jit(solution)/shard_map/temporal/all_to_all | solution.py:586
  116.1 3.4 %collective-permute-done.12.refs_3_ = bf16[4,592,128]{2,1,0:T(8,128)(2,1)} collective-permute-done((bf16[4,592,128]{2,1,0:T(8,128)(2,1)}, bf16[4,592,128]{2,1,0:T(8,128)(2,1)}, u32[]{:S(2)}, u32[]{:S(2)}) %collective-permute-start.12) | collective-permute-done | bytes 606240 | tf_op jit(solution)/shard_map/memory/ppermute | solution.py:637
  119.5 0.0 collective-permute-done.11.refs_2_
  119.5 0.0 collective-permute-done.10.refs_1_
  119.5 0.0 copy-done.2
  119.5 2.8 %add_partials.1 = bf16[4,592,128]{2,1,0:T(8,128)(2,1)} custom-call(bf16[4,592,128]{2,1,0:T(8,128)(2,1)S(1)} %copy-done.2, bf16[4,592,128]{2,1,0:T(8,128)(2,1)} %collective-permute-done.10.refs_1_, bf16[4,592,128]{2,1,0:T(8,128)(2,1)} %collective-permute-done.11.refs_2_, bf16[4,592,128]{2,1,0:T(8,128)(2,1)} %collective-permute-done.12.refs_3_), custom_call_target="tpu_custom_call" | custom-call | flops 75776 | bytes 151552 | tf_op jit(solution)/shard_map/memory/add_partials/pallas_call | solution.py:469
  122.4 5.5 %all-to-all-done.4.time_hbm = bf16[16,144,128]{2,1,0:T(8,128)(2,1)S(1)} async-done(((bf16[16,144,128]{2,1,0:T(8,128)(2,1)}), bf16[16,144,128]{2,1,0:T(8,128)(2,1)S(1)}, u32[]{:S(2)}, u32[]{:S(2)}) %all-to-all-start.4) | async-done | bytes 589856 | tf_op jit(solution)/shard_map/temporal/all_to_all | solution.py:586
  127.8 12.4 %all_to_all.25.memory_hbm = bf16[4,592,128]{2,1,0:T(8,128)(2,1)S(1)} all-to-all(bf16[4,592,128]{2,1,0:T(8,128)(2,1)} %add_partials.1), channel_id=1, replica_groups=mesh['y'=4,'c'=2,'z'=4,'x'=4] {'x'}, dimensions={0} | all-to-all | bytes 1212416 | tf_op jit(solution)/shard_map/memory/all_to_all | solution.py:586
  140.2 6.2 %leave.1 = bf16[576,2048]{1,0:T(8,128)(2,1)} custom-call(bf16[4,592,128]{2,1,0:T(8,128)(2,1)} %own_attend.1.refs_8_.own_hbm, bf16[4,592,128]{2,1,0:T(8,128)(2,1)S(1)} %all_to_all.25.memory_hbm, bf16[16,144,128]{2,1,0:T(8,128)(2,1)S(1)} %all-to-all-done.4.time_hbm, bf16[1024,2048]{1,0:T(8,128)(2,1)} %weight_hbm.7), custom_call_target="tpu_custom_call" | custom-call | flops 150994944 | bytes 630784 | tf_op jit(solution)/shard_map/exit/leave/pallas_call | solution.py:537
  (10 shorter events, 0.1 us)
Async XLA Ops:
  0.0 6.6 %copy-start.6 = (s32[1,1,6,1]{2,3,1,0:T(1,128)S(1)}, s32[1,1,6,1]{2,3,1,0:T(1,128)}, u32[]{:S(2)}) copy-start(s32[1,1,6,1]{2,3,1,0:T(1,128)} %param.17) | copy-start | bytes 76
  0.0 6.6 %copy-start.5 = (s32[1,1,6]{2,1,0:T(1,128)S(1)}, s32[1,1,6]{2,1,0:T(1,128)}, u32[]{:S(2)}) copy-start(s32[1,1,6]{2,1,0:T(1,128)} %param.18) | copy-start | bytes 76
  0.0 6.6 %copy-start.4 = (f32[2,4]{1,0:T(2,128)S(1)}, f32[2,4]{1,0:T(2,128)}, u32[]{:S(2)}) copy-start(f32[2,4]{1,0:T(2,128)} %param.15) | copy-start | bytes 100
  0.0 6.7 %copy-start.3 = (f32[1,1,2,2048]{3,2,1,0:T(2,128)S(1)}, f32[1,1,2,2048]{3,2,1,0:T(2,128)}, u32[]{:S(2)}) copy-start(f32[1,1,2,2048]{3,2,1,0:T(2,128)} %param.12) | copy-start | bytes 49156
  2.2 14.6 %all-to-all-start.1 = ((bf16[4,288,256]{2,1,0:T(8,128)(2,1)}), bf16[4,288,256]{2,1,0:T(8,128)(2,1)S(1)}, u32[]{:S(2)}, u32[]{:S(2)}) async-start(bf16[4,288,256]{2,1,0:T(8,128)(2,1)} %split_store.1._), calls=%async_computation.1 | async-start | bytes 1179648 | tf_op jit(solution)/shard_map/store/all_to_all | solution.py:586
  16.8 14.3 %all-to-all-start = ((bf16[4,592,128]{2,1,0:T(8,128)(2,1)}), bf16[4,592,128]{2,1,0:T(8,128)(2,1)S(1)}, u32[]{:S(2)}, u32[]{:S(2)}) async-start(bf16[4,592,128]{2,1,0:T(8,128)(2,1)} %get-tuple-element.22.query_hbm), calls=%async_computation | async-start | bytes 1212416 | tf_op jit(solution)/shard_map/queries/all_to_all | solution.py:586
  31.1 10.0 %copy-start = (bf16[8,144,256]{2,1,0:T(8,128)(2,1)S(1)}, bf16[8,144,256]{2,1,0:T(8,128)(2,1)}, u32[]{:S(2)}) copy-start(bf16[8,144,256]{2,1,0:T(8,128)(2,1)} %join_pieces.1._.refs_0_) | copy-start | bytes 1769476
  31.2 32.4 %collective-permute-start.9 = (bf16[4,592,128]{2,1,0:T(8,128)(2,1)S(1)}, bf16[4,592,128]{2,1,0:T(8,128)(2,1)}, u32[]{:S(2)}, u32[]{:S(2)}) collective-permute-start(bf16[4,592,128]{2,1,0:T(8,128)(2,1)S(1)} %all-to-all-done.query_hbm), channel_id=1, source_target_pairs={{0,8},{4,12},{8,0},{12,4},{1,9},{5,13},{9,1},{13,5},{2,10},{6,14},... | collective-permute-start | bytes 1818632 | tf_op jit(solution)/shard_map/queries/ppermute | solution.py:618
  35.1 72.8 %all-to-all-start.3 = ((bf16[16,3,144,128]{3,2,1,0:T(8,128)(2,1)}), bf16[16,3,144,128]{3,2,1,0:T(8,128)(2,1)S(1)}, u32[]{:S(2)}, u32[]{:S(2)}) async-start(bf16[16,3,144,128]{3,2,1,0:T(8,128)(2,1)} %bitcast.19), calls=%async_computation.3 | async-start | bytes 3538944 | tf_op jit(solution)/shard_map/temporal/all_to_all | solution.py:586
  41.1 26.3 %collective-permute-start = (bf16[8,144,256]{2,1,0:T(8,128)(2,1)S(1)}, bf16[8,144,256]{2,1,0:T(8,128)(2,1)S(1)}, u32[]{:S(2)}, u32[]{:S(2)}) collective-permute-start(bf16[8,144,256]{2,1,0:T(8,128)(2,1)S(1)} %copy-done), channel_id=1, source_target_pairs={{0,96},{32,0},{64,32},{96,64},{1,97},{33,1},{65,33},{97,65},{2,98}... | collective-permute-start | bytes 1769480 | tf_op jit(solution)/shard_map/store/ppermute | solution.py:613
  44.2 23.2 %collective-permute-start.1 = (bf16[8,144,256]{2,1,0:T(8,128)(2,1)S(1)}, bf16[8,144,256]{2,1,0:T(8,128)(2,1)S(1)}, u32[]{:S(2)}, u32[]{:S(2)}) collective-permute-start(bf16[8,144,256]{2,1,0:T(8,128)(2,1)S(1)} %copy-done), channel_id=1, source_target_pairs={{0,64},{32,96},{64,0},{96,32},{1,65},{33,97},{65,1},{97,33},{2,66}... | collective-permute-start | bytes 1769480 | tf_op jit(solution)/shard_map/store/ppermute | solution.py:613
  44.8 26.3 %collective-permute-start.2 = (bf16[8,144,256]{2,1,0:T(8,128)(2,1)S(1)}, bf16[8,144,256]{2,1,0:T(8,128)(2,1)S(1)}, u32[]{:S(2)}, u32[]{:S(2)}) collective-permute-start(bf16[8,144,256]{2,1,0:T(8,128)(2,1)S(1)} %copy-done), channel_id=1, source_target_pairs={{0,32},{32,64},{64,96},{96,0},{1,33},{33,65},{65,97},{97,1},{2,34}... | collective-permute-start | bytes 1769480 | tf_op jit(solution)/shard_map/store/ppermute | solution.py:613
  45.8 34.5 %collective-permute-start.8 = (bf16[4,592,128]{2,1,0:T(8,128)(2,1)S(1)}, bf16[4,592,128]{2,1,0:T(8,128)(2,1)S(1)}, u32[]{:S(2)}, u32[]{:S(2)}) collective-permute-start(bf16[4,592,128]{2,1,0:T(8,128)(2,1)S(1)} %all-to-all-done.query_hbm), channel_id=1, source_target_pairs={{0,12},{4,0},{8,4},{12,8},{1,13},{5,1},{9,5},{13,9},{2,14},{6,2},{... | collective-permute-start | bytes 1818632 | tf_op jit(solution)/shard_map/queries/ppermute | solution.py:618
  48.9 18.5 %copy-start.1 = (bf16[8,144,256]{2,1,0:T(8,128)(2,1)S(1)}, bf16[8,144,256]{2,1,0:T(8,128)(2,1)}, u32[]{:S(2)}) copy-start(bf16[8,144,256]{2,1,0:T(8,128)(2,1)} %join_pieces.1._.refs_0_) | copy-start | bytes 1769476
  63.5 16.8 %collective-permute-start.7 = (bf16[4,592,128]{2,1,0:T(8,128)(2,1)S(1)}, bf16[4,592,128]{2,1,0:T(8,128)(2,1)S(1)}, u32[]{:S(2)}, u32[]{:S(2)}) collective-permute-start(bf16[4,592,128]{2,1,0:T(8,128)(2,1)S(1)} %all-to-all-done.query_hbm), channel_id=1, source_target_pairs={{0,4},{4,8},{8,12},{12,0},{1,5},{5,9},{9,13},{13,1},{2,6},{6,10},{... | collective-permute-start | bytes 1818632 | tf_op jit(solution)/shard_map/queries/ppermute | solution.py:618
  67.4 13.0 %collective-permute-start.3 = (bf16[8,144,256]{2,1,0:T(8,128)(2,1)S(1)}, bf16[8,144,256]{2,1,0:T(8,128)(2,1)S(1)}, u32[]{:S(2)}, u32[]{:S(2)}) collective-permute-start(bf16[8,144,256]{2,1,0:T(8,128)(2,1)S(1)} %copy-done.1), channel_id=1, source_target_pairs={{0,16},{16,0},{1,17},{17,1},{2,18},{18,2},{3,19},{19,3},{4,20},{20... | collective-permute-start | bytes 1769480 | tf_op jit(solution)/shard_map/store/ppermute | solution.py:614
  67.4 13.0 %collective-permute-start.4 = (bf16[8,144,256]{2,1,0:T(8,128)(2,1)S(1)}, bf16[8,144,256]{2,1,0:T(8,128)(2,1)S(1)}, u32[]{:S(2)}, u32[]{:S(2)}) collective-permute-start(bf16[8,144,256]{2,1,0:T(8,128)(2,1)S(1)} %collective-permute-done.refs_1_), channel_id=1, source_target_pairs={{0,16},{16,0},{1,17},{17,1},{2,18},{18,2},{3,19},{19,3},{4,20},{20... | collective-permute-start | bytes 1769480 | tf_op jit(solution)/shard_map/store/ppermute | solution.py:614
  71.1 9.3 %collective-permute-start.5 = (bf16[8,144,256]{2,1,0:T(8,128)(2,1)S(1)}, bf16[8,144,256]{2,1,0:T(8,128)(2,1)S(1)}, u32[]{:S(2)}, u32[]{:S(2)}) collective-permute-start(bf16[8,144,256]{2,1,0:T(8,128)(2,1)S(1)} %collective-permute-done.1.refs_2_), channel_id=1, source_target_pairs={{0,16},{16,0},{1,17},{17,1},{2,18},{18,2},{3,19},{19,3},{4,20},{20... | collective-permute-start | bytes 1769480 | tf_op jit(solution)/shard_map/store/ppermute | solution.py:614
  80.3 2.0 %collective-permute-start.6 = (bf16[8,144,256]{2,1,0:T(8,128)(2,1)S(1)}, bf16[8,144,256]{2,1,0:T(8,128)(2,1)S(1)}, u32[]{:S(2)}, u32[]{:S(2)}) collective-permute-start(bf16[8,144,256]{2,1,0:T(8,128)(2,1)S(1)} %collective-permute-done.2.refs_3_), channel_id=1, source_target_pairs={{0,16},{16,0},{1,17},{17,1},{2,18},{18,2},{3,19},{19,3},{4,20},{20... | collective-permute-start | bytes 1769480 | tf_op jit(solution)/shard_map/store/ppermute | solution.py:614
  88.2 31.3 %collective-permute-start.10 = (bf16[4,592,128]{2,1,0:T(8,128)(2,1)}, bf16[4,592,128]{2,1,0:T(8,128)(2,1)}, u32[]{:S(2)}, u32[]{:S(2)}) collective-permute-start(bf16[4,592,128]{2,1,0:T(8,128)(2,1)} %memory_attend.4.refs_8_), channel_id=1, source_target_pairs={{0,8},{4,12},{8,0},{12,4},{1,9},{5,13},{9,1},{13,5},{2,10},{6,14},... | collective-permute-start | bytes 1818632 | tf_op jit(solution)/shard_map/memory/ppermute | solution.py:637
  94.4 25.1 %collective-permute-start.11 = (bf16[4,592,128]{2,1,0:T(8,128)(2,1)}, bf16[4,592,128]{2,1,0:T(8,128)(2,1)}, u32[]{:S(2)}, u32[]{:S(2)}) collective-permute-start(bf16[4,592,128]{2,1,0:T(8,128)(2,1)} %memory_attend.5.refs_8_), channel_id=1, source_target_pairs={{0,4},{4,8},{8,12},{12,0},{1,5},{5,9},{9,13},{13,1},{2,6},{6,10},{... | collective-permute-start | bytes 1818632 | tf_op jit(solution)/shard_map/memory/ppermute | solution.py:637
  101.7 17.8 %collective-permute-start.12 = (bf16[4,592,128]{2,1,0:T(8,128)(2,1)}, bf16[4,592,128]{2,1,0:T(8,128)(2,1)}, u32[]{:S(2)}, u32[]{:S(2)}) collective-permute-start(bf16[4,592,128]{2,1,0:T(8,128)(2,1)} %memory_attend.6.refs_8_), channel_id=1, source_target_pairs={{0,12},{4,0},{8,4},{12,8},{1,13},{5,1},{9,5},{13,9},{2,14},{6,2},{... | collective-permute-start | bytes 1818632 | tf_op jit(solution)/shard_map/memory/ppermute | solution.py:637
  107.9 11.6 %copy-start.2 = (bf16[4,592,128]{2,1,0:T(8,128)(2,1)S(1)}, bf16[4,592,128]{2,1,0:T(8,128)(2,1)}, u32[]{:S(2)}) copy-start(bf16[4,592,128]{2,1,0:T(8,128)(2,1)} %memory_attend.7.refs_0_._) | copy-start | bytes 1818628
  110.4 17.4 %all-to-all-start.4 = ((bf16[16,144,128]{2,1,0:T(8,128)(2,1)}), bf16[16,144,128]{2,1,0:T(8,128)(2,1)S(1)}, u32[]{:S(2)}, u32[]{:S(2)}) async-start(bf16[16,144,128]{2,1,0:T(8,128)(2,1)} %temporal_attend.1), calls=%async_computation.4 | async-start | bytes 1179648 | tf_op jit(solution)/shard_map/temporal/all_to_all | solution.py:586

commit v6 on v5

--- a/solution.py
+++ b/solution.py
@@ -57,41 +57,46 @@
 copy = pltpu.make_async_copy
 
 
-def split_store_kernel(rows_ref, out_hbm, out_ref, sem):
+def split_store_kernel(x_ref, rows_ref, *refs):
+    outs, out_ref, sem = refs[:G], refs[G], refs[G + 1]
     sends = []
-    for h in range(G):
-        key = rows_ref[:, h * C : (h + 1) * C].astype(F32)
-        out_ref[h, :, :C] = (key * inverse_rms(key)).astype(BF)
-        out_ref[h, :, C:] = rows_ref[:, HW + h * C : HW + (h + 1) * C]
-        sends.append(copy(out_ref.at[h], out_hbm.at[h], sem.at[h]))
+    for j in range(G):
+        start = lax.rem(x_ref[0] + j, G) * C
+        key = rows_ref[:, pl.ds(pl.multiple_of(start, C), C)].astype(F32)
+        out_ref[j, :, :C] = (key * inverse_rms(key)).astype(BF)
+        out_ref[j, :, C:] = rows_ref[:, pl.ds(pl.multiple_of(HW + start, C), C)]
+        sends.append(copy(out_ref.at[j], outs[j], sem.at[j]))
         sends[-1].start()
     for send in sends:
         send.wait()
 
 
-def split_store(rows):
+def split_store(x, rows):
     n = rows.shape[0]
     return pl.pallas_call(
         split_store_kernel,
-        in_specs=[WHOLE],
-        out_specs=HBM,
-        out_shape=hbm_out((G, n, 2 * C)),
+        in_specs=[SCALARS, WHOLE],
+        out_specs=[HBM] * G,
+        out_shape=[hbm_out((n, 2 * C))] * G,
         scratch_shapes=[pltpu.VMEM((G, n, 2 * C), BF), DMA((G,))],
         compiler_params=params(),
         name="split_store",
         cost_estimate=cost(8 * n * HW, 8 * n * HW),
-    )(rows)
-
-
-def join_pieces_kernel(piece, in_hbm, _, out_hbm, in_ref, wide_ref, joined_ref, out_ref, sem):
-    pieces = in_ref.shape[0]
-    loads = [copy(in_hbm.at[i], in_ref.at[i], sem.at[i]) for i in range(pieces)]
+    )(x, rows)
+
+
+def join_pieces_kernel(pieces, *refs):
+    ins = refs[:pieces]
+    out_hbm, in_ref, wide_ref, joined_ref, out_ref, sem = refs[pieces + 1 :]
+    frames = out_ref.shape[0]
+    piece = in_ref.shape[1] // frames
+    loads = [copy(ins[i], in_ref.at[i], sem.at[i]) for i in range(pieces)]
     for load in loads:
         load.start()
     for i in range(pieces):
         loads[i].wait()
         wide_ref[i] = in_ref[i].astype(F32)
-        for m in range(out_ref.shape[0]):
+        for m in range(frames):
             joined_ref[m, i * piece : (i + 1) * piece, :] = wide_ref[
                 i, m * piece : (m + 1) * piece, :
             ]
@@ -102,25 +107,25 @@
 
 
 def join_pieces(parts, frames, after):
-    pieces, rows, width = parts.shape
-    piece = rows // frames
-    shape = (frames, pieces * piece, width)
-    return pl.pallas_call(
-        functools.partial(join_pieces_kernel, piece),
-        in_specs=[ANY, ANY],
+    pieces = len(parts)
+    rows, width = parts[0].shape
+    shape = (frames, pieces * rows // frames, width)
+    return pl.pallas_call(
+        functools.partial(join_pieces_kernel, pieces),
+        in_specs=[ANY] * (pieces + 1),
         out_specs=HBM,
         out_shape=hbm_out(shape),
         scratch_shapes=[
-            pltpu.VMEM(parts.shape, BF),
-            pltpu.VMEM(parts.shape, F32),
+            pltpu.VMEM((pieces, rows, width), BF),
+            pltpu.VMEM((pieces, rows, width), F32),
             pltpu.VMEM(shape, F32),
             pltpu.VMEM(shape, BF),
             DMA((pieces,)),
         ],
         compiler_params=params(),
         name="join_pieces",
-        cost_estimate=cost(parts.size, 4 * parts.size),
-    )(parts, in_hbm(after))
+        cost_estimate=cost(pieces * rows * width, 4 * pieces * rows * width),
+    )(*parts, in_hbm(after))
 
 
 def modulate_kernel(
@@ -137,13 +142,13 @@
     weight_load = copy(weight_hbm.at[:, pl.ds(0, HW)], weight_ref, weight_sem)
     loads[0].start()
     weight_load.start()
-    for load in loads[1:]:
-        load.start()
     for h in range(G):
         query_ref[h, patches:, :] = tail_ref[...]
     for i in range(steps):
         at = slice(i * rows, (i + 1) * rows)
         loads[i].wait()
+        if i + 1 < steps:
+            loads[i + 1].start()
         act = act_ref[i].astype(F32)
         hidden = act * inverse_rms(act) * (1.0 + affine_ref[0:1, :]) + affine_ref[1:2, :]
         hidden = hidden.astype(BF)
@@ -191,7 +196,7 @@
 
 
 def temporal_entry_kernel(
-    quarters, hidden_hbm, weight_hbm, factor_ref, out_hbm,
+    quarters, hidden_hbm, weight_hbm, factor_ref, _, out_hbm,
     hidden_ref, weight_ref, out_ref, hidden_sem, weight_sem, store_sem,
 ):
     rows = hidden_ref.shape[0] // quarters
@@ -202,14 +207,14 @@
         )
         for part in range(3)
     ]
+    hidden_load.start()
     loads[0].start()
-    hidden_load.start()
-    for load in loads[1:]:
-        load.start()
     hidden_load.wait()
     stores = []
     for part in range(3):
         loads[part].wait()
+        if part < 2:
+            loads[part + 1].start()
         mapped = dot(hidden_ref[...], weight_ref[part]).astype(BF)
         for h in range(G):
             done = mapped[:, h * C : (h + 1) * C]
@@ -227,12 +232,12 @@
         store.wait()
 
 
-def temporal_entry(hidden, weight, factor, quarters):
+def temporal_entry(hidden, weight, factor, quarters, after):
     patches, depth = hidden.shape
     rows = patches // quarters
     return pl.pallas_call(
         functools.partial(temporal_entry_kernel, quarters),
-        in_specs=[HBM, HBM, SCALARS],
+        in_specs=[HBM, HBM, SCALARS, ANY],
         out_specs=HBM,
         out_shape=hbm_out((quarters, G, 3, rows, C)),
         scratch_shapes=[
@@ -248,7 +253,7 @@
         cost_estimate=cost(
             6 * patches * depth * HW, 2 * patches * depth + 6 * depth * HW + 6 * patches * HW
         ),
-    )(in_hbm(hidden), in_hbm(weight), factor)
+    )(in_hbm(hidden), in_hbm(weight), factor, in_hbm(after))
 
 
 def temporal_attend_kernel(length_ref, in_hbm_ref, _, out_hbm, in_ref, out_ref, sem):
@@ -334,12 +339,12 @@
         )
         for part in range(2)
     ]
+    hidden_load.start()
     loads[0].start()
-    hidden_load.start()
+    hidden_load.wait()
+    loads[0].wait()
     loads[1].start()
     query_load.start()
-    hidden_load.wait()
-    loads[0].wait()
     keys = dot(hidden_ref[...], weight_ref[0]).astype(BF)
     loads[1].wait()
     values = dot(hidden_ref[...], weight_ref[1]).astype(BF)
@@ -382,109 +387,117 @@
     )(in_hbm(hidden), in_hbm(weight), in_hbm(query), in_hbm(after))
 
 
-def memory_attend_kernel(count, index_ref, query_hbm, *refs):
-    blocks = refs[:count]
-    out_hbm, query_ref, store_ref, out_ref, query_sem, block_sem, store_sem = refs[count + 1 :]
-    frames = query_ref.shape[0]
-    held = blocks[0].shape[0]
-    loads = [
-        copy(blocks[i], store_ref.at[pl.ds(i * held, held)], block_sem.at[i]) for i in range(count)
-    ]
-    query_load = copy(query_hbm, query_ref, query_sem)
-    for load in loads:
+def memory_attend_kernel(groups, count, index_ref, *refs):
+    queries, blocks = refs[:groups], refs[groups : groups + count]
+    outs = refs[groups + count + 1 : 2 * groups + count + 1]
+    query_ref, store_ref, out_ref, query_sem, block_sem, store_sem = refs[2 * groups + count + 1 :]
+    frames = queries[0].shape[0]
+    loads, start = [], 0
+    for i, block in enumerate(blocks):
+        held = block.shape[0]
+        loads.append(copy(block, store_ref.at[pl.ds(start, held)], block_sem.at[i]))
+        start += held
+    query_loads = [copy(queries[k], query_ref.at[k], query_sem.at[k]) for k in range(groups)]
+    for load in query_loads[:1] + loads + query_loads[1:]:
         load.start()
-    query_load.start()
     for load in loads:
         load.wait()
-    query_load.wait()
     stores = []
-    for i in range(frames):
-        chosen = [store_ref[index_ref[i, j]] for j in range(TOPM)]
-        keys = jnp.concatenate([block[:, :C] for block in chosen], axis=0)
-        values = jnp.concatenate([block[:, C:] for block in chosen], axis=0)
-        attend_rows(lambda at, i=i: query_ref[i, at, :], keys, with_ones(values), out_ref.at[i])
-        stores.append(copy(out_ref.at[i], out_hbm.at[i], store_sem.at[i]))
-        stores[-1].start()
+    for k in range(groups):
+        query_loads[k].wait()
+        for i in range(frames):
+            chosen = [store_ref[index_ref[k * frames + i, j]] for j in range(TOPM)]
+            keys = jnp.concatenate([block[:, :C] for block in chosen], axis=0)
+            values = jnp.concatenate([block[:, C:] for block in chosen], axis=0)
+            attend_rows(
+                lambda at, k=k, i=i: query_ref[k, i, at, :],
+                keys,
+                with_ones(values),
+                out_ref.at[k, i],
+            )
+            stores.append(copy(out_ref.at[k, i], outs[k].at[i], store_sem.at[k, i]))
+            stores[-1].start()
     for store in stores:
         store.wait()
 
 
-def memory_attend(index, query, blocks, after):
-    frames, rows, _ = query.shape
-    held, quarter, width = blocks[0].shape
-    count = len(blocks)
-    return pl.pallas_call(
-        functools.partial(memory_attend_kernel, count),
-        in_specs=[SCALARS, ANY] + [ANY] * count + [ANY],
-        out_specs=HBM,
-        out_shape=hbm_out(query.shape),
+def memory_attend(index, queries, blocks, after):
+    groups, count = len(queries), len(blocks)
+    frames, rows, _ = queries[0].shape
+    _, quarter, width = blocks[0].shape
+    total = sum(block.shape[0] for block in blocks)
+    shape = (groups, frames, rows, C)
+    return pl.pallas_call(
+        functools.partial(memory_attend_kernel, groups, count),
+        in_specs=[SCALARS] + [ANY] * (groups + count + 1),
+        out_specs=[HBM] * groups,
+        out_shape=[hbm_out(shape[1:])] * groups,
         scratch_shapes=[
-            pltpu.VMEM(query.shape, BF),
-            pltpu.VMEM((count * held, quarter, width), BF),
-            pltpu.VMEM(query.shape, BF),
-            DMA,
+            pltpu.VMEM(shape, BF),
+            pltpu.VMEM((total, quarter, width), BF),
+            pltpu.VMEM(shape, BF),
+            DMA((groups,)),
             DMA((count,)),
-            DMA((frames,)),
+            DMA((groups, frames)),
         ],
         compiler_params=params(),
         name="memory_attend",
         cost_estimate=cost(
-            8 * frames * rows * TOPM * quarter * C,
-            4 * query.size + 2 * count * held * quarter * width,
+            8 * groups * frames * rows * TOPM * quarter * C,
+            4 * groups * frames * rows * C + 2 * total * quarter * width,
         ),
-    )(index, query, *blocks, in_hbm(after))
-
-
-def add_partials_kernel(*refs):
-    ins, out_hbm, parts_ref, out_ref, load_sem, store_sem = (
-        refs[: len(refs) - 5], *refs[len(refs) - 5 :],
-    )
-    frames = out_ref.shape[0]
+    )(index, *queries, *blocks, in_hbm(after))
+
+
+def add_partials_kernel(count, x_ref, *refs):
+    ins, outs = refs[:count], refs[count : count + G]
+    parts_ref, out_ref, load_sem, store_sem = refs[count + G :]
     patches = out_ref.shape[1] - PAD
-    loads = [
-        [copy(ref.at[i], parts_ref.at[k, i], load_sem.at[k, i]) for k, ref in enumerate(ins)]
-        for i in range(frames)
-    ]
+    loads = []
+    for j in range(G):
+        frame = lax.rem(x_ref[0] + j, G)
+        loads.append(
+            [copy(ref.at[frame], parts_ref.at[k, j], load_sem.at[k, j]) for k, ref in enumerate(ins)]
+        )
     for of_frame in loads:
         for load in of_frame:
             load.start()
     stores = []
-    for i in range(frames):
-        for load in loads[i]:
+    for j in range(G):
+        for load in loads[j]:
             load.wait()
-        total = parts_ref[0, i].astype(F32)
-        for k in range(1, len(ins)):
-            total = total + parts_ref[k, i].astype(F32)
-        out_ref[i, :patches, :] = total[:patches].astype(BF)
-        out_ref[i, patches:, :] = halves(total[patches : patches + 8] + total[patches + 8 :])
-        stores.append(copy(out_ref.at[i], out_hbm.at[i], store_sem.at[i]))
+        total = parts_ref[0, j].astype(F32)
+        for k in range(1, count):
+            total = total + parts_ref[k, j].astype(F32)
+        out_ref[j, :patches, :] = total[:patches].astype(BF)
+        out_ref[j, patches:, :] = halves(total[patches : patches + 8] + total[patches + 8 :])
+        stores.append(copy(out_ref.at[j], outs[j], store_sem.at[j]))
         stores[-1].start()
     for store in stores:
         store.wait()
 
 
-def add_partials(parts):
+def add_partials(x, parts):
     shape = parts[0].shape
-    frames = shape[0]
-    return pl.pallas_call(
-        add_partials_kernel,
-        in_specs=[ANY] * len(parts),
-        out_specs=HBM,
-        out_shape=hbm_out(shape),
+    return pl.pallas_call(
+        functools.partial(add_partials_kernel, len(parts)),
+        in_specs=[SCALARS] + [ANY] * len(parts),
+        out_specs=[HBM] * G,
+        out_shape=[hbm_out(shape[1:])] * G,
         scratch_shapes=[
             pltpu.VMEM((len(parts),) + shape, BF),
             pltpu.VMEM(shape, BF),
-            DMA((len(parts), frames)),
-            DMA((frames,)),
+            DMA((len(parts), G)),
+            DMA((G,)),
         ],
         compiler_params=params(),
         name="add_partials",
         cost_estimate=cost(4 * parts[0].size, 8 * parts[0].size),
-    )(*parts)
+    )(x, *parts)
 
 
 def leave_kernel(
-    own_hbm, memory_hbm, time_hbm, weight_hbm, out_hbm,
+    x_ref, own_hbm, memory_0, memory_1, memory_2, memory_3, time_hbm, weight_hbm, out_hbm,
     own_ref, memory_ref, time_ref, combined_ref, weight_ref, out_ref,
     own_sem, memory_sem, time_sem, weight_sem, store_sem,
 ):
@@ -492,8 +505,10 @@
     quarters = time_ref.shape[0] // G
     rows = time_ref.shape[1]
     steps, _, width = weight_ref.shape
-    own_loads = [copy(own_hbm.at[h], own_ref.at[h], own_sem.at[h]) for h in range(G)]
-    memory_loads = [copy(memory_hbm.at[h], memory_ref.at[h], memory_sem.at[h]) for h in range(G)]
+    heads = [lax.rem(x_ref[0] + G - j, G) for j in range(G)]
+    memories = (memory_0, memory_1, memory_2, memory_3)
+    own_loads = [copy(own_hbm.at[heads[j]], own_ref.at[j], own_sem.at[j]) for j in range(G)]
+    memory_loads = [copy(memories[j], memory_ref.at[j], memory_sem.at[j]) for j in range(G)]
     time_load = copy(time_hbm, time_ref, time_sem)
     loads, stores = [], []
     for i in range(steps):
@@ -507,6 +522,7 @@
     for h in range(G):
         own_loads[h].wait()
         memory_loads[h].wait()
+        column_at = pl.ds(pl.multiple_of(heads[h] * C, C), C)
         tail = own_ref[h, patches:, :].astype(F32) + memory_ref[h, patches:, :].astype(F32)
         denominators = tail[:8] + tail[8:]
         for j in range(patches // LINE):
@@ -514,7 +530,7 @@
             line = jnp.broadcast_to(denominators[j : j + 1, :], (LINE, C))
             total = jnp.sum(jnp.where(row == column, line, 0.0), axis=1, keepdims=True)
             top = own_ref[h, at, :].astype(F32) + memory_ref[h, at, :].astype(F32)
-            combined_ref[at, h * C : (h + 1) * C] = (top / total).astype(BF)
+            combined_ref[at, column_at] = (top / total).astype(BF)
     time_load.wait()
     for h in range(G):
         for z in range(quarters):
@@ -529,19 +545,19 @@
         store.wait()
 
 
-def leave(own, memory, time, weight):
+def leave(x, own, memory, time, weight):
     patches = own.shape[1] - PAD
     depth, width = weight.shape
     steps = 4
     step = width // steps
     return pl.pallas_call(
         leave_kernel,
-        in_specs=[HBM, ANY, ANY, HBM],
+        in_specs=[SCALARS, HBM] + [ANY] * (G + 1) + [HBM],
         out_specs=HBM,
         out_shape=hbm_out((patches, width)),
         scratch_shapes=[
             pltpu.VMEM(own.shape, BF),
-            pltpu.VMEM(memory.shape, BF),
+            pltpu.VMEM(own.shape, BF),
             pltpu.VMEM(time.shape, BF),
             pltpu.VMEM((patches, depth), BF),
             pltpu.VMEM((steps, depth, step), BF),
@@ -558,7 +574,7 @@
             2 * patches * depth * width,
             2 * depth * width + 2 * patches * width + 6 * patches * depth,
         ),
-    )(in_hbm(own), memory, time, in_hbm(weight))
+    )(x, in_hbm(own), *memory, time, in_hbm(weight))
 
 
 def on_device(
@@ -576,6 +592,7 @@
     patches, depth = patch_activation_tensor.shape[2:]
     held, piece = cached_past_pairs.shape[:2]
     rolls_y, cores = lax.axis_size("y"), lax.axis_size("c")
+    x = lax.axis_index("x").astype(jnp.int32).reshape(1)
 
     def turn(step):
         return [(s, (s + step) % rings) for s in range(rings)]
@@ -585,9 +602,12 @@
     def swap(blocks, axes):
         return lax.all_to_all(blocks, axes, split_axis=0, concat_axis=0, tiled=True)
 
+    def swap_apart(blocks):
+        return [blocks[0]] + [lax.ppermute(blocks[j], "x", turn(j)) for j in range(1, G)]
+
     with jax.named_scope("store"):
-        split = split_store(cached_past_pairs.reshape(held * piece, 2 * HW))
-        pieces = swap(split, "x")
+        split = split_store(x, cached_past_pairs.reshape(held * piece, 2 * HW))
+        pieces = swap_apart(split)
 
     with jax.named_scope("queries"):
         factor = softmax_sharpness / C
@@ -601,51 +621,60 @@
             entry_projection_matrix,
             factor,
             tail,
-            after=split,
+            after=split[0],
         )
         here = swap(query, "x")
 
-    with jax.named_scope("temporal"):
-        parts = temporal_entry(hidden, entry_projection_matrix, factor, rings)
-
     with jax.named_scope("store"):
-        joined = join_pieces(pieces, held, after=parts)
-        near = [joined] + [lax.ppermute(joined, "y", turn(-step)) for step in (1, 2, 3)]
-        beside = [lax.ppermute(block, "c", other) for block in near]
+        joined = join_pieces(pieces, held, after=hidden)
+        above = lax.ppermute(joined, "y", turn(-1))
+        below = lax.ppermute(joined, "y", turn(1))
 
     with jax.named_scope("queries"):
         here, joined = lax.optimization_barrier((here, joined))
         groups = [here] + [lax.ppermute(here, "z", turn(-step)) for step in (1, 2, 3)]
 
-    with jax.named_scope("temporal"):
-        sent = swap(parts.reshape((rings * G,) + parts.shape[2:]), ("z", "x"))
-
     with jax.named_scope("own"):
         own = own_attend(hidden, entry_projection_matrix, query, after=joined)
 
-    def attend(group, after):
-        named = group[:, patches, :TOPM].astype(jnp.int32)
+    with jax.named_scope("store"):
+        joined, above, below, own = lax.optimization_barrier((joined, above, below, own))
+        far_first = lax.ppermute(above[: held // 2], "y", turn(-1))
+        far_last = lax.ppermute(below[held // 2 :], "y", turn(1))
+
+    with jax.named_scope("temporal"):
+        parts = temporal_entry(hidden, entry_projection_matrix, factor, rings, after=own)
+        sent = swap(parts.reshape((rings * G,) + parts.shape[2:]), ("z", "x"))
+
+    with jax.named_scope("store"):
+        near = [joined, above, far_first, far_last, below]
+        *near, parts = lax.optimization_barrier((*near, parts))
+        blocks = near + [lax.ppermute(block, "c", other) for block in near]
+
+    def attend(queries, after):
+        named = jnp.concatenate([group[:, patches, :TOPM] for group in queries], axis=0)
+        named = named.astype(jnp.int32)
         y = (named // (cores * held) - lax.axis_index("y")) & (rolls_y - 1)
         c = (named // held & (cores - 1)) ^ lax.axis_index("c")
         index = (c * rolls_y + y) * held + (named & (held - 1))
-        return memory_attend(index, group, near + beside, after)
+        return memory_attend(index, queries, blocks, after)
 
     with jax.named_scope("memory"):
-        after, sums = own, []
-        for step in (2, 1, 3):
-            after = attend(groups[step], after)
-            sums.append(lax.ppermute(after, "z", turn(step)))
-        sum_here = attend(here, after)
+        sum_far, sum_above = attend([groups[2], groups[1]], parts)
+        from_far = lax.ppermute(sum_far, "z", turn(2))
+        from_below = lax.ppermute(sum_above, "z", turn(1))
+        sum_below, sum_here = attend([groups[3], here], sum_far)
+        from_above = lax.ppermute(sum_below, "z", turn(3))
 
     with jax.named_scope("temporal"):
-        timed = temporal_attend(lookback_lengths, sent, after=sum_here)
+        timed = temporal_attend(lookback_lengths, sent, after=sum_below)
         time = swap(timed, ("z", "x"))
 
     with jax.named_scope("memory"):
-        memory = swap(add_partials([sum_here] + sums), "x")
+        memory = swap_apart(add_partials(x, [sum_here, from_far, from_below, from_above]))
 
     with jax.named_scope("exit"):
-        attended = leave(own, memory, time, exit_projection_matrix)
+        attended = leave(x, own, memory, time, exit_projection_matrix)
     return attended.reshape(1, 1, patches, depth)
 
 

time: 147 us -> 172 us (1.17)
  waiting for transfers between devices: 35.1 us -> 56.6 us
  Pallas kernels: 57.9 us -> 53.4 us
  local copies, waits for them, and re-layouts: 1.23 us -> 5.67 us
  starting transfers between devices: 38.2 us -> 40.2 us
    ppermute x10 -> x18, waiting for transfers between devices: 9.48 us -> 26.7 us  [the longest x1 12.2 us: on_device(): from_above = lax.ppermute(sum_below, 'z', turn(3))]
    ppermute x3, waiting for transfers between devices: 15.7 us -> 29.9 us  [on_device(): lax.ppermute(here, 'z', turn(-step))]
    ppermute x10 -> x18, starting transfers between devices: 10 us -> 22.2 us  [the longest x6 11.3 us: swap_apart(): lax.ppermute(blocks[j], 'x', turn(j))]
    all_to_all x4 -> x2, waiting for transfers between devices: 9.85 us -> 0.01 us  [swap(): return lax.all_to_all(blocks, axes, split_axis=0, concat_axis=0, tiled=True)]
    all_to_all x4 -> x2, starting transfers between devices: 18.9 us -> 13.2 us  [swap(): return lax.all_to_all(blocks, axes, split_axis=0, concat_axis=0, tiled=True)]
    ppermute x3, starting transfers between devices: 9.22 us -> 4.85 us  [on_device(): lax.ppermute(here, 'z', turn(-step))]
    pallas_call x8 -> x6, Pallas kernels: 32.5 us -> 28.8 us  [the longest x2 17 us: memory_attend(): pl.pallas_call(functools.partial(memory_attend_kernel, groups, count), in...]
    slice x0 -> x6, local copies, waits for them, and re-layouts: none -> 2.84 us  [the longest x4 2.8 us: attend(): group[:, patches, :TOPM]]
  transfers between devices with their start and end apart: 17 -> 23, of which waited for: 8 -> 9; matrix products, arithmetic and copies ran while one was open for 1% -> 3% of each run, Pallas kernels for 35% -> 21%
where the time goes in v6:
time: 172 us; the launch traced here: 171 us
  waiting for transfers between devices  56.6 us (33%)
  Pallas kernels  53.4 us (31%)
  starting transfers between devices  40.2 us (23%)
  blocking collectives  12.6 us (7%)
  local copies, waits for them, and re-layouts  5.67 us (3%)
    ppermute x3, waiting for transfers between devices, on_device(): lax.ppermute(here, 'z', turn(-step))  29.9 us
    pallas_call x2, Pallas kernels, memory_attend(): pl.pallas_call(functools.partial(memory_attend_kernel, groups, count), in...  17 us
    all_to_all x2, starting transfers between devices, swap(): return lax.all_to_all(blocks, axes, split_axis=0, concat_axis=0, tiled=True)  13.2 us
    all_to_all x1, blocking collectives, swap(): return lax.all_to_all(blocks, axes, split_axis=0, concat_axis=0, tiled=True)  12.6 us
    ppermute x1, waiting for transfers between devices, on_device(): from_above = lax.ppermute(sum_below, 'z', turn(3))  12.2 us
    ppermute x6, starting transfers between devices, swap_apart(): lax.ppermute(blocks[j], 'x', turn(j))  11.3 us
    pallas_call x1, Pallas kernels, temporal_entry(): pl.pallas_call(functools.partial(temporal_entry_kernel, quarters), in_spe...  8.58 us
    pallas_call x1, Pallas kernels, own_attend(): pl.pallas_call(own_attend_kernel, in_specs=[HBM, HBM, HBM, ANY], out_spec...  8.06 us
  transfers between devices with their start and end apart: 23, of which 9 were waited for; matrix products, arithmetic and copies ran while one was open for 3% of the time, Pallas kernels for 21%

profile of v6, /device:TPU:0, one launch (start us, length us, event | category | flops | bytes accessed | tf_op | source)
XLA Modules:
  0.0 171.1 jit_solution(18307646172592449081)
XLA Ops:
  0.0 1.1 copy.14
  1.2 1.0 split_store.1
  2.1 1.6 collective-permute-start
  3.8 2.7 %collective-permute-start.1 = (bf16[288,256]{1,0:T(8,128)(2,1)}, bf16[288,256]{1,0:T(8,128)(2,1)S(1)}, u32[]{:S(2)}, u32[]{:S(2)}) collective-permute-start(bf16[288,256]{1,0:T(8,128)(2,1)} %get-tuple-element.46), channel_id=1, source_target_pairs={{0,2},{1,3},{2,0},{3,1},{4,6},{5,7},{6,4},{7,5},{8,10},{9,11},{10,... | collective-permute-start | bytes 442376 | tf_op jit(solution)/shard_map/store/ppermute | solution.py:606
  6.5 1.4 collective-permute-start.2
  8.0 0.7 fusion.34
  8.6 0.7 broadcast_multiply_fusion.factor_ref
  9.3 0.7 copy-done.5
  10.0 5.5 %modulate.1 = (bf16[576,2048]{1,0:T(8,128)(2,1)}, bf16[4,592,128]{2,1,0:T(8,128)(2,1)}) custom-call(bf16[576,2048]{1,0:T(8,128)(2,1)} %bitcast.29, f32[2,2048]{1,0:T(2,128)S(1)} %bitcast.27, bf16[2048,3072]{1,0:T(8,128)(2,1)} %weight_hbm.6, f32[2,4]{1,0:T(2,128)S(1)} %broadcast_multiply_fusion.factor_ref, bf16[16,128]{1,0:T(8,128)(2,1)S(1)} %scatter.4.tail_ref, ...), custom_call_target="tpu_custom_call" | custom-call | flops 75497472 | bytes 462848 | tf_op jit(solution)/shard_map/queries/modulate/pallas_call | solution.py:175
  15.6 0.0 collective-permute-done.refs_1_
  15.6 0.0 collective-permute-done.1.refs_2_
  15.6 0.0 collective-permute-done.2.refs_3_
  15.6 1.8 %join_pieces.1._.refs_2_ = bf16[8,144,256]{2,1,0:T(8,128)(2,1)} custom-call(bf16[288,256]{1,0:T(8,128)(2,1)S(1)} %copy-done.3, bf16[288,256]{1,0:T(8,128)(2,1)S(1)} %collective-permute-done.refs_1_, bf16[288,256]{1,0:T(8,128)(2,1)S(1)} %collective-permute-done.1.refs_2_, bf16[288,256]{1,0:T(8,128)(2,1)S(1)} %collective-permute-done.2.refs_3_, ...), custom_call_target="tpu_custom_call" | custom-call | flops 18432 | bytes 73728 | tf_op jit(solution)/shard_map/store/join_pieces/pallas_call | solution.py:113
  17.4 3.1 %collective-permute-start.3 = (bf16[8,144,256]{2,1,0:T(8,128)(2,1)}, bf16[8,144,256]{2,1,0:T(8,128)(2,1)S(1)}, u32[]{:S(2)}, u32[]{:S(2)}) collective-permute-start(bf16[8,144,256]{2,1,0:T(8,128)(2,1)} %join_pieces.1._.refs_2_), channel_id=1, source_target_pairs={{0,96},{32,0},{64,32},{96,64},{1,97},{33,1},{65,33},{97,65},{2,98}... | collective-permute-start | bytes 1769480 | tf_op jit(solution)/shard_map/store/ppermute | solution.py:630
  20.5 0.0 collective-permute-start.4
  20.5 12.6 %all_to_all.15.refs_1_ = bf16[4,592,128]{2,1,0:T(8,128)(2,1)} all-to-all(bf16[4,592,128]{2,1,0:T(8,128)(2,1)S(1)} %copy-done.6), channel_id=1, replica_groups=mesh['y'=4,'c'=2,'z'=4,'x'=4] {'x'}, dimensions={0} | all-to-all | bytes 1212416 | tf_op jit(solution)/shard_map/queries/all_to_all | solution.py:603
  33.1 8.1 %own_attend.1._.own_hbm = bf16[4,592,128]{2,1,0:T(8,128)(2,1)} custom-call(bf16[576,2048]{1,0:T(8,128)(2,1)} %get-tuple-element.48.refs_4_.hidden_hbm, bf16[2048,3072]{1,0:T(8,128)(2,1)} %weight_hbm.6, bf16[4,592,128]{2,1,0:T(8,128)(2,1)} %get-tuple-element.44.query_hbm, bf16[8,144,256]{2,1,0:T(8,128)(2,1)} %join_pieces.1._.refs_2_), custom_call_target="tpu_custom_call" | custom-call | flops 214695936 | bytes 593920 | tf_op jit(solution)/shard_map/own/own_attend/pallas_call | solution.py:366
  41.2 0.0 collective-permute-done.3.refs_3_
  41.2 0.0 collective-permute-done.4.refs_6_
  41.2 8.6 %temporal_entry.1.refs_12_ = bf16[4,4,3,144,128]{4,3,2,1,0:T(8,128)(2,1)} custom-call(bf16[576,2048]{1,0:T(8,128)(2,1)} %get-tuple-element.48.refs_4_.hidden_hbm, bf16[2048,3072]{1,0:T(8,128)(2,1)} %weight_hbm.6, f32[2,4]{1,0:T(2,128)S(1)} %broadcast_multiply_fusion.factor_ref, bf16[4,592,128]{2,1,0:T(8,128)(2,1)} %own_attend.1._.own_hbm), custom_call_target="tpu_custom_call" | custom-call | flops 226492416 | bytes 651264 | tf_op jit(solution)/shard_map/temporal/temporal_entry/pallas_call | solution.py:238
  49.8 6.2 %all-to-all-start.1 = ((bf16[16,3,144,128]{3,2,1,0:T(8,128)(2,1)}), bf16[16,3,144,128]{3,2,1,0:T(8,128)(2,1)S(1)}, u32[]{:S(2)}, u32[]{:S(2)}) async-start(bf16[16,3,144,128]{3,2,1,0:T(8,128)(2,1)} %bitcast.28), calls=%async_computation.1 | async-start | bytes 3538944 | tf_op jit(solution)/shard_map/temporal/all_to_all | solution.py:603
  56.0 3.1 %collective-permute-start.14 = (bf16[4,592,128]{2,1,0:T(8,128)(2,1)}, bf16[4,592,128]{2,1,0:T(8,128)(2,1)}, u32[]{:S(2)}, u32[]{:S(2)}) collective-permute-start(bf16[4,592,128]{2,1,0:T(8,128)(2,1)} %all_to_all.15.refs_1_), channel_id=1, source_target_pairs={{0,12},{4,0},{8,4},{12,8},{1,13},{5,1},{9,5},{13,9},{2,14},{6,2},{... | collective-permute-start | bytes 1818632 | tf_op jit(solution)/shard_map/queries/ppermute | solution.py:635
  59.1 0.9 collective-permute-start.13
  60.0 0.9 collective-permute-start.5
  60.9 3.0 %collective-permute-start.6 = (bf16[4,144,256]{2,1,0:T(8,128)(2,1)S(1)}, bf16[4,144,256]{2,1,0:T(8,128)(2,1)}, u32[]{:S(2)}, u32[]{:S(2)}) collective-permute-start(bf16[4,144,256]{2,1,0:T(8,128)(2,1)S(1)} %slice.36), channel_id=1, source_target_pairs={{0,96},{32,0},{64,32},{96,64},{1,97},{33,1},{65,33},{97,65},{2,98}... | collective-permute-start | bytes 884744 | tf_op jit(solution)/shard_map/store/ppermute | solution.py:642
  63.9 0.1 collective-permute-start.7
  64.0 4.1 %collective-permute-done.6.refs_4_ = bf16[4,144,256]{2,1,0:T(8,128)(2,1)} collective-permute-done((bf16[4,144,256]{2,1,0:T(8,128)(2,1)S(1)}, bf16[4,144,256]{2,1,0:T(8,128)(2,1)}, u32[]{:S(2)}, u32[]{:S(2)}) %collective-permute-start.6) | collective-permute-done | bytes 294944 | tf_op jit(solution)/shard_map/store/ppermute | solution.py:642
  68.1 3.9 %collective-permute-done.7.refs_5_ = bf16[4,144,256]{2,1,0:T(8,128)(2,1)} collective-permute-done((bf16[4,144,256]{2,1,0:T(8,128)(2,1)S(1)}, bf16[4,144,256]{2,1,0:T(8,128)(2,1)}, u32[]{:S(2)}, u32[]{:S(2)}) %collective-permute-start.7) | collective-permute-done | bytes 294944 | tf_op jit(solution)/shard_map/store/ppermute | solution.py:643
  72.0 0.0 collective-permute-start.12
  72.0 0.5 collective-permute-start.8
  72.5 18.0 %collective-permute-done.14.refs_1_ = bf16[4,592,128]{2,1,0:T(8,128)(2,1)} collective-permute-done((bf16[4,592,128]{2,1,0:T(8,128)(2,1)}, bf16[4,592,128]{2,1,0:T(8,128)(2,1)}, u32[]{:S(2)}, u32[]{:S(2)}) %collective-permute-start.14) | collective-permute-done | bytes 606240 | tf_op jit(solution)/shard_map/queries/ppermute | solution.py:635
  90.6 0.0 collective-permute-start.9
  90.6 1.2 collective-permute-done.13.refs_0_
  91.7 0.0 collective-permute-start.10
  91.7 10.7 %collective-permute-done.5.refs_0_ = bf16[4,592,128]{2,1,0:T(8,128)(2,1)} collective-permute-done((bf16[4,592,128]{2,1,0:T(8,128)(2,1)}, bf16[4,592,128]{2,1,0:T(8,128)(2,1)}, u32[]{:S(2)}, u32[]{:S(2)}) %collective-permute-start.5) | collective-permute-done | bytes 606240 | tf_op jit(solution)/shard_map/queries/ppermute | solution.py:635
  102.4 0.0 collective-permute-start.11
  102.4 0.7 slice.35
  103.1 0.7 slice.42
  103.9 0.7 slice.41
  104.6 0.7 slice.40
  105.3 0.0 collective-permute-done.10.refs_9_
  105.3 0.0 collective-permute-done.11.refs_10_
  105.3 0.0 collective-permute-done.12.refs_11_
  105.4 0.0 collective-permute-done.9.refs_8_
  105.4 8.5 %memory_attend.2 = (bf16[4,592,128]{2,1,0:T(8,128)(2,1)}, bf16[4,592,128]{2,1,0:T(8,128)(2,1)}) custom-call(s32[8,6]{1,0:T(8,128)S(1)} %fusion.24.index_ref, bf16[4,592,128]{2,1,0:T(8,128)(2,1)} %collective-permute-done.13.refs_0_, bf16[4,592,128]{2,1,0:T(8,128)(2,1)} %collective-permute-done.14.refs_1_, bf16[8,144,256]{2,1,0:T(8,128)(2,1)S(1)} %copy-done, ...), custom_call_target="tpu_custom_call" | custom-call | flops 261881856 | bytes 446464 | tf_op jit(solution)/shard_map/memory/memory_attend/pallas_call | solution.py:430
  113.9 0.6 collective-permute-start.15
  114.5 8.5 %memory_attend.3 = (bf16[4,592,128]{2,1,0:T(8,128)(2,1)}, bf16[4,592,128]{2,1,0:T(8,128)(2,1)}) custom-call(s32[8,6]{1,0:T(8,128)S(1)} %fusion.14.index_ref, bf16[4,592,128]{2,1,0:T(8,128)(2,1)} %collective-permute-done.5.refs_0_, bf16[4,592,128]{2,1,0:T(8,128)(2,1)S(1)} %copy-done.1, bf16[8,144,256]{2,1,0:T(8,128)(2,1)S(1)} %copy-done, ...), custom_call_target="tpu_custom_call" | custom-call | flops 261881856 | bytes 446464 | tf_op jit(solution)/shard_map/memory/memory_attend/pallas_call | solution.py:430
  123.0 3.5 %collective-permute-start.17 = (bf16[4,592,128]{2,1,0:T(8,128)(2,1)}, bf16[4,592,128]{2,1,0:T(8,128)(2,1)}, u32[]{:S(2)}, u32[]{:S(2)}) collective-permute-start(bf16[4,592,128]{2,1,0:T(8,128)(2,1)} %get-tuple-element.64._), channel_id=1, source_target_pairs={{0,12},{4,0},{8,4},{12,8},{1,13},{5,1},{9,5},{13,9},{2,14},{6,2},{... | collective-permute-start | bytes 1818632 | tf_op jit(solution)/shard_map/memory/ppermute | solution.py:667
  126.6 0.0 collective-permute-start.16
  127.2 0.0 all-to-all-done.1.in_hbm_ref
  127.2 2.4 %temporal_attend.1 = bf16[16,144,128]{2,1,0:T(8,128)(2,1)} custom-call(s32[1]{0:T(128)S(6)} %copy.23.length_ref, bf16[16,3,144,128]{3,2,1,0:T(8,128)(2,1)S(1)} %all-to-all-done.1.in_hbm_ref, bf16[4,592,128]{2,1,0:T(8,128)(2,1)} %get-tuple-element.64._), custom_call_target="tpu_custom_call" | custom-call | flops 18874368 | bytes 147456 | tf_op jit(solution)/shard_map/temporal/temporal_attend/pallas_call | solution.py:288
  129.7 7.0 %all-to-all-start.2 = ((bf16[16,144,128]{2,1,0:T(8,128)(2,1)}), bf16[16,144,128]{2,1,0:T(8,128)(2,1)S(1)}, u32[]{:S(2)}, u32[]{:S(2)}) async-start(bf16[16,144,128]{2,1,0:T(8,128)(2,1)} %temporal_attend.1), calls=%async_computation.2 | async-start | bytes 1179648 | tf_op jit(solution)/shard_map/temporal/all_to_all | solution.py:603
  136.7 12.2 %collective-permute-done.17.refs_3_ = bf16[4,592,128]{2,1,0:T(8,128)(2,1)} collective-permute-done((bf16[4,592,128]{2,1,0:T(8,128)(2,1)}, bf16[4,592,128]{2,1,0:T(8,128)(2,1)}, u32[]{:S(2)}, u32[]{:S(2)}) %collective-permute-start.17) | collective-permute-done | bytes 606240 | tf_op jit(solution)/shard_map/memory/ppermute | solution.py:667
  148.9 0.8 collective-permute-done.16.refs_2_
  149.7 2.8 %add_partials.1 = (bf16[592,128]{1,0:T(8,128)(2,1)}, bf16[592,128]{1,0:T(8,128)(2,1)}, bf16[592,128]{1,0:T(8,128)(2,1)}, bf16[592,128]{1,0:T(8,128)(2,1)}) custom-call(s32[1]{0:T(128)} %bitcast.x_ref, bf16[4,592,128]{2,1,0:T(8,128)(2,1)S(1)} %copy-done.2, bf16[4,592,128]{2,1,0:T(8,128)(2,1)} %collective-permute-done.15.refs_1_, ...), custom_call_target="tpu_custom_call" | custom-call | flops 75776 | bytes 151552 | tf_op jit(solution)/shard_map/memory/add_partials/pallas_call | solution.py:482
  152.5 1.5 collective-permute-start.18
  154.0 2.7 %collective-permute-start.19 = (bf16[592,128]{1,0:T(8,128)(2,1)}, bf16[592,128]{1,0:T(8,128)(2,1)S(1)}, u32[]{:S(2)}, u32[]{:S(2)}) collective-permute-start(bf16[592,128]{1,0:T(8,128)(2,1)} %get-tuple-element.67), channel_id=1, source_target_pairs={{0,2},{1,3},{2,0},{3,1},{4,6},{5,7},{6,4},{7,5},{8,10},{9,11},{10,... | collective-permute-start | bytes 454664 | tf_op jit(solution)/shard_map/memory/ppermute | solution.py:606
  156.7 1.4 collective-permute-start.20
  158.1 2.2 %collective-permute-done.18.memory_1 = bf16[592,128]{1,0:T(8,128)(2,1)S(1)} collective-permute-done((bf16[592,128]{1,0:T(8,128)(2,1)}, bf16[592,128]{1,0:T(8,128)(2,1)S(1)}, u32[]{:S(2)}, u32[]{:S(2)}) %collective-permute-start.18) | collective-permute-done | bytes 151584 | tf_op jit(solution)/shard_map/memory/ppermute | solution.py:606
  160.3 3.4 %collective-permute-done.19.memory_2 = bf16[592,128]{1,0:T(8,128)(2,1)S(1)} collective-permute-done((bf16[592,128]{1,0:T(8,128)(2,1)}, bf16[592,128]{1,0:T(8,128)(2,1)S(1)}, u32[]{:S(2)}, u32[]{:S(2)}) %collective-permute-start.19) | collective-permute-done | bytes 151584 | tf_op jit(solution)/shard_map/memory/ppermute | solution.py:606
  163.7 0.0 collective-permute-done.20.memory_3
  163.7 0.0 all-to-all-done.2.time_hbm
  163.7 0.9 copy-done.4
  164.7 6.2 %leave.1 = bf16[576,2048]{1,0:T(8,128)(2,1)} custom-call(s32[1]{0:T(128)} %bitcast.x_ref, bf16[4,592,128]{2,1,0:T(8,128)(2,1)} %own_attend.1._.own_hbm, bf16[592,128]{1,0:T(8,128)(2,1)S(1)} %copy-done.4, bf16[592,128]{1,0:T(8,128)(2,1)S(1)} %collective-permute-done.18.memory_1, bf16[592,128]{1,0:T(8,128)(2,1)S(1)} %collective-permute-done.19.memory_2, ...), custom_call_target="tpu_custom_call" | custom-call | flops 150994944 | bytes 630784 | tf_op jit(solution)/shard_map/exit/leave/pallas_call | solution.py:553
  (23 shorter events, 0.1 us)
Async XLA Ops:
  2.1 13.4 %collective-permute-start = (bf16[288,256]{1,0:T(8,128)(2,1)}, bf16[288,256]{1,0:T(8,128)(2,1)S(1)}, u32[]{:S(2)}, u32[]{:S(2)}) collective-permute-start(bf16[288,256]{1,0:T(8,128)(2,1)} %get-tuple-element.45), channel_id=1, source_target_pairs={{0,1},{1,2},{2,3},{3,0},{4,5},{5,6},{6,7},{7,4},{8,9},{9,10},{10,1... | collective-permute-start | bytes 442376 | tf_op jit(solution)/shard_map/store/ppermute | solution.py:606
  3.8 11.8 %collective-permute-start.1 = (bf16[288,256]{1,0:T(8,128)(2,1)}, bf16[288,256]{1,0:T(8,128)(2,1)S(1)}, u32[]{:S(2)}, u32[]{:S(2)}) collective-permute-start(bf16[288,256]{1,0:T(8,128)(2,1)} %get-tuple-element.46), channel_id=1, source_target_pairs={{0,2},{1,3},{2,0},{3,1},{4,6},{5,7},{6,4},{7,5},{8,10},{9,11},{10,... | collective-permute-start | bytes 442376 | tf_op jit(solution)/shard_map/store/ppermute | solution.py:606
  6.5 9.1 %collective-permute-start.2 = (bf16[288,256]{1,0:T(8,128)(2,1)}, bf16[288,256]{1,0:T(8,128)(2,1)S(1)}, u32[]{:S(2)}, u32[]{:S(2)}) collective-permute-start(bf16[288,256]{1,0:T(8,128)(2,1)} %get-tuple-element.47), channel_id=1, source_target_pairs={{0,3},{1,0},{2,1},{3,2},{4,7},{5,4},{6,5},{7,6},{8,11},{9,8},{10,9... | collective-permute-start | bytes 442376 | tf_op jit(solution)/shard_map/store/ppermute | solution.py:606
  9.3 0.7 copy-start.5
  10.0 5.6 %copy-start.3 = (bf16[288,256]{1,0:T(8,128)(2,1)S(1)}, bf16[288,256]{1,0:T(8,128)(2,1)}, u32[]{:S(2)}) copy-start(bf16[288,256]{1,0:T(8,128)(2,1)} %get-tuple-element.43._.refs_0_) | copy-start | bytes 442372
  15.6 4.9 %copy-start.6 = (bf16[4,592,128]{2,1,0:T(8,128)(2,1)S(1)}, bf16[4,592,128]{2,1,0:T(8,128)(2,1)}, u32[]{:S(2)}) copy-start(bf16[4,592,128]{2,1,0:T(8,128)(2,1)} %get-tuple-element.44.query_hbm) | copy-start | bytes 1818628
  17.4 23.8 %collective-permute-start.3 = (bf16[8,144,256]{2,1,0:T(8,128)(2,1)}, bf16[8,144,256]{2,1,0:T(8,128)(2,1)S(1)}, u32[]{:S(2)}, u32[]{:S(2)}) collective-permute-start(bf16[8,144,256]{2,1,0:T(8,128)(2,1)} %join_pieces.1._.refs_2_), channel_id=1, source_target_pairs={{0,96},{32,0},{64,32},{96,64},{1,97},{33,1},{65,33},{97,65},{2,98}... | collective-permute-start | bytes 1769480 | tf_op jit(solution)/shard_map/store/ppermute | solution.py:630
  20.5 20.7 %collective-permute-start.4 = (bf16[8,144,256]{2,1,0:T(8,128)(2,1)}, bf16[8,144,256]{2,1,0:T(8,128)(2,1)S(1)}, u32[]{:S(2)}, u32[]{:S(2)}) collective-permute-start(bf16[8,144,256]{2,1,0:T(8,128)(2,1)} %join_pieces.1._.refs_2_), channel_id=1, source_target_pairs={{0,32},{32,64},{64,96},{96,0},{1,33},{33,65},{65,97},{97,1},{2,34}... | collective-permute-start | bytes 1769480 | tf_op jit(solution)/shard_map/store/ppermute | solution.py:631
  49.8 22.2 %copy-start = (bf16[8,144,256]{2,1,0:T(8,128)(2,1)S(1)}, bf16[8,144,256]{2,1,0:T(8,128)(2,1)}, u32[]{:S(2)}) copy-start(bf16[8,144,256]{2,1,0:T(8,128)(2,1)} %join_pieces.1._.refs_2_) | copy-start | bytes 1769476
  49.8 77.4 %all-to-all-start.1 = ((bf16[16,3,144,128]{3,2,1,0:T(8,128)(2,1)}), bf16[16,3,144,128]{3,2,1,0:T(8,128)(2,1)S(1)}, u32[]{:S(2)}, u32[]{:S(2)}) async-start(bf16[16,3,144,128]{3,2,1,0:T(8,128)(2,1)} %bitcast.28), calls=%async_computation.1 | async-start | bytes 3538944 | tf_op jit(solution)/shard_map/temporal/all_to_all | solution.py:603
  56.0 34.6 %collective-permute-start.14 = (bf16[4,592,128]{2,1,0:T(8,128)(2,1)}, bf16[4,592,128]{2,1,0:T(8,128)(2,1)}, u32[]{:S(2)}, u32[]{:S(2)}) collective-permute-start(bf16[4,592,128]{2,1,0:T(8,128)(2,1)} %all_to_all.15.refs_1_), channel_id=1, source_target_pairs={{0,12},{4,0},{8,4},{12,8},{1,13},{5,1},{9,5},{13,9},{2,14},{6,2},{... | collective-permute-start | bytes 1818632 | tf_op jit(solution)/shard_map/queries/ppermute | solution.py:635
  59.1 32.6 %collective-permute-start.13 = (bf16[4,592,128]{2,1,0:T(8,128)(2,1)}, bf16[4,592,128]{2,1,0:T(8,128)(2,1)}, u32[]{:S(2)}, u32[]{:S(2)}) collective-permute-start(bf16[4,592,128]{2,1,0:T(8,128)(2,1)} %all_to_all.15.refs_1_), channel_id=1, source_target_pairs={{0,8},{4,12},{8,0},{12,4},{1,9},{5,13},{9,1},{13,5},{2,10},{6,14},... | collective-permute-start | bytes 1818632 | tf_op jit(solution)/shard_map/queries/ppermute | solution.py:635
  60.0 42.5 %collective-permute-start.5 = (bf16[4,592,128]{2,1,0:T(8,128)(2,1)}, bf16[4,592,128]{2,1,0:T(8,128)(2,1)}, u32[]{:S(2)}, u32[]{:S(2)}) collective-permute-start(bf16[4,592,128]{2,1,0:T(8,128)(2,1)} %all_to_all.15.refs_1_), channel_id=1, source_target_pairs={{0,4},{4,8},{8,12},{12,0},{1,5},{5,9},{9,13},{13,1},{2,6},{6,10},{... | collective-permute-start | bytes 1818632 | tf_op jit(solution)/shard_map/queries/ppermute | solution.py:635
  60.9 7.3 %collective-permute-start.6 = (bf16[4,144,256]{2,1,0:T(8,128)(2,1)S(1)}, bf16[4,144,256]{2,1,0:T(8,128)(2,1)}, u32[]{:S(2)}, u32[]{:S(2)}) collective-permute-start(bf16[4,144,256]{2,1,0:T(8,128)(2,1)S(1)} %slice.36), channel_id=1, source_target_pairs={{0,96},{32,0},{64,32},{96,64},{1,97},{33,1},{65,33},{97,65},{2,98}... | collective-permute-start | bytes 884744 | tf_op jit(solution)/shard_map/store/ppermute | solution.py:642
  63.9 8.1 %collective-permute-start.7 = (bf16[4,144,256]{2,1,0:T(8,128)(2,1)S(1)}, bf16[4,144,256]{2,1,0:T(8,128)(2,1)}, u32[]{:S(2)}, u32[]{:S(2)}) collective-permute-start(bf16[4,144,256]{2,1,0:T(8,128)(2,1)S(1)} %slice.37), channel_id=1, source_target_pairs={{0,32},{32,64},{64,96},{96,0},{1,33},{33,65},{65,97},{97,1},{2,34}... | collective-permute-start | bytes 884744 | tf_op jit(solution)/shard_map/store/ppermute | solution.py:643
  72.0 33.4 %collective-permute-start.12 = (bf16[8,144,256]{2,1,0:T(8,128)(2,1)S(1)}, bf16[8,144,256]{2,1,0:T(8,128)(2,1)}, u32[]{:S(2)}, u32[]{:S(2)}) collective-permute-start(bf16[8,144,256]{2,1,0:T(8,128)(2,1)S(1)} %collective-permute-done.4.refs_6_), channel_id=1, source_target_pairs={{0,16},{16,0},{1,17},{17,1},{2,18},{18,2},{3,19},{19,3},{4,20},{20... | collective-permute-start | bytes 1769480 | tf_op jit(solution)/shard_map/store/ppermute | solution.py:652
  72.0 33.4 %collective-permute-start.8 = (bf16[8,144,256]{2,1,0:T(8,128)(2,1)S(1)}, bf16[8,144,256]{2,1,0:T(8,128)(2,1)}, u32[]{:S(2)}, u32[]{:S(2)}) collective-permute-start(bf16[8,144,256]{2,1,0:T(8,128)(2,1)S(1)} %copy-done), channel_id=1, source_target_pairs={{0,16},{16,0},{1,17},{17,1},{2,18},{18,2},{3,19},{19,3},{4,20},{20... | collective-permute-start | bytes 1769480 | tf_op jit(solution)/shard_map/store/ppermute | solution.py:652
  90.6 14.8 %collective-permute-start.9 = (bf16[8,144,256]{2,1,0:T(8,128)(2,1)S(1)}, bf16[8,144,256]{2,1,0:T(8,128)(2,1)}, u32[]{:S(2)}, u32[]{:S(2)}) collective-permute-start(bf16[8,144,256]{2,1,0:T(8,128)(2,1)S(1)} %collective-permute-done.3.refs_3_), channel_id=1, source_target_pairs={{0,16},{16,0},{1,17},{17,1},{2,18},{18,2},{3,19},{19,3},{4,20},{20... | collective-permute-start | bytes 1769480 | tf_op jit(solution)/shard_map/store/ppermute | solution.py:652
  91.7 13.6 %collective-permute-start.10 = (bf16[4,144,256]{2,1,0:T(8,128)(2,1)}, bf16[4,144,256]{2,1,0:T(8,128)(2,1)}, u32[]{:S(2)}, u32[]{:S(2)}) collective-permute-start(bf16[4,144,256]{2,1,0:T(8,128)(2,1)} %collective-permute-done.6.refs_4_), channel_id=1, source_target_pairs={{0,16},{16,0},{1,17},{17,1},{2,18},{18,2},{3,19},{19,3},{4,20},{20... | collective-permute-start | bytes 884744 | tf_op jit(solution)/shard_map/store/ppermute | solution.py:652
  102.4 2.9 %collective-permute-start.11 = (bf16[4,144,256]{2,1,0:T(8,128)(2,1)}, bf16[4,144,256]{2,1,0:T(8,128)(2,1)}, u32[]{:S(2)}, u32[]{:S(2)}) collective-permute-start(bf16[4,144,256]{2,1,0:T(8,128)(2,1)} %collective-permute-done.7.refs_5_), channel_id=1, source_target_pairs={{0,16},{16,0},{1,17},{17,1},{2,18},{18,2},{3,19},{19,3},{4,20},{20... | collective-permute-start | bytes 884744 | tf_op jit(solution)/shard_map/store/ppermute | solution.py:652
  105.3 9.2 %copy-start.1 = (bf16[4,592,128]{2,1,0:T(8,128)(2,1)S(1)}, bf16[4,592,128]{2,1,0:T(8,128)(2,1)}, u32[]{:S(2)}) copy-start(bf16[4,592,128]{2,1,0:T(8,128)(2,1)} %all_to_all.15.refs_1_) | copy-start | bytes 1818628
  113.9 35.0 %collective-permute-start.15 = (bf16[4,592,128]{2,1,0:T(8,128)(2,1)}, bf16[4,592,128]{2,1,0:T(8,128)(2,1)}, u32[]{:S(2)}, u32[]{:S(2)}) collective-permute-start(bf16[4,592,128]{2,1,0:T(8,128)(2,1)} %get-tuple-element.61.refs_12_), channel_id=1, source_target_pairs={{0,8},{4,12},{8,0},{12,4},{1,9},{5,13},{9,1},{13,5},{2,10},{6,14},... | collective-permute-start | bytes 1818632 | tf_op jit(solution)/shard_map/memory/ppermute | solution.py:664
  123.0 26.7 %copy-start.2 = (bf16[4,592,128]{2,1,0:T(8,128)(2,1)S(1)}, bf16[4,592,128]{2,1,0:T(8,128)(2,1)}, u32[]{:S(2)}) copy-start(bf16[4,592,128]{2,1,0:T(8,128)(2,1)} %get-tuple-element.62.refs_0_) | copy-start | bytes 1818628
  123.0 25.9 %collective-permute-start.17 = (bf16[4,592,128]{2,1,0:T(8,128)(2,1)}, bf16[4,592,128]{2,1,0:T(8,128)(2,1)}, u32[]{:S(2)}, u32[]{:S(2)}) collective-permute-start(bf16[4,592,128]{2,1,0:T(8,128)(2,1)} %get-tuple-element.64._), channel_id=1, source_target_pairs={{0,12},{4,0},{8,4},{12,8},{1,13},{5,1},{9,5},{13,9},{2,14},{6,2},{... | collective-permute-start | bytes 1818632 | tf_op jit(solution)/shard_map/memory/ppermute | solution.py:667
  126.6 23.1 %collective-permute-start.16 = (bf16[4,592,128]{2,1,0:T(8,128)(2,1)}, bf16[4,592,128]{2,1,0:T(8,128)(2,1)}, u32[]{:S(2)}, u32[]{:S(2)}) collective-permute-start(bf16[4,592,128]{2,1,0:T(8,128)(2,1)} %get-tuple-element.63), channel_id=1, source_target_pairs={{0,4},{4,8},{8,12},{12,0},{1,5},{5,9},{9,13},{13,1},{2,6},{6,10},{... | collective-permute-start | bytes 1818632 | tf_op jit(solution)/shard_map/memory/ppermute | solution.py:665
  129.7 34.1 %all-to-all-start.2 = ((bf16[16,144,128]{2,1,0:T(8,128)(2,1)}), bf16[16,144,128]{2,1,0:T(8,128)(2,1)S(1)}, u32[]{:S(2)}, u32[]{:S(2)}) async-start(bf16[16,144,128]{2,1,0:T(8,128)(2,1)} %temporal_attend.1), calls=%async_computation.2 | async-start | bytes 1179648 | tf_op jit(solution)/shard_map/temporal/all_to_all | solution.py:603
  152.5 7.7 %collective-permute-start.18 = (bf16[592,128]{1,0:T(8,128)(2,1)}, bf16[592,128]{1,0:T(8,128)(2,1)S(1)}, u32[]{:S(2)}, u32[]{:S(2)}) collective-permute-start(bf16[592,128]{1,0:T(8,128)(2,1)} %get-tuple-element.66), channel_id=1, source_target_pairs={{0,1},{1,2},{2,3},{3,0},{4,5},{5,6},{6,7},{7,4},{8,9},{9,10},{10,1... | collective-permute-start | bytes 454664 | tf_op jit(solution)/shard_map/memory/ppermute | solution.py:606
  154.0 9.7 %collective-permute-start.19 = (bf16[592,128]{1,0:T(8,128)(2,1)}, bf16[592,128]{1,0:T(8,128)(2,1)S(1)}, u32[]{:S(2)}, u32[]{:S(2)}) collective-permute-start(bf16[592,128]{1,0:T(8,128)(2,1)} %get-tuple-element.67), channel_id=1, source_target_pairs={{0,2},{1,3},{2,0},{3,1},{4,6},{5,7},{6,4},{7,5},{8,10},{9,11},{10,... | collective-permute-start | bytes 454664 | tf_op jit(solution)/shard_map/memory/ppermute | solution.py:606
  156.7 7.1 %collective-permute-start.20 = (bf16[592,128]{1,0:T(8,128)(2,1)}, bf16[592,128]{1,0:T(8,128)(2,1)S(1)}, u32[]{:S(2)}, u32[]{:S(2)}) collective-permute-start(bf16[592,128]{1,0:T(8,128)(2,1)} %get-tuple-element.68), channel_id=1, source_target_pairs={{0,3},{1,0},{2,1},{3,2},{4,7},{5,4},{6,5},{7,6},{8,11},{9,8},{10,9... | collective-permute-start | bytes 454664 | tf_op jit(solution)/shard_map/memory/ppermute | solution.py:606
  163.7 0.9 copy-start.4

commit v7 on v6

--- a/solution.py
+++ b/solution.py
@@ -129,8 +129,10 @@
 
 
 def modulate_kernel(
-    act_hbm, affine_ref, weight_hbm, factor_ref, tail_ref, _, hidden_hbm, query_hbm,
-    act_ref, weight_ref, hidden_ref, query_ref, load_sem, weight_sem, store_sem, query_sem,
+    held,
+    act_hbm, affine_hbm, weight_hbm, sharpness_ref, owner_ref, slot_ref, _, hidden_hbm, query_hbm,
+    act_ref, affine_ref, weight_ref, hidden_ref, query_ref,
+    load_sem, affine_sem, weight_sem, store_sem, query_sem,
 ):
     steps, rows, _ = act_ref.shape
     patches = query_ref.shape[1] - PAD
@@ -140,10 +142,18 @@
         loads.append(copy(act_hbm.at[at, :], act_ref.at[i], load_sem.at[i]))
         stores.append(copy(hidden_ref.at[i], hidden_hbm.at[at, :], store_sem.at[i]))
     weight_load = copy(weight_hbm.at[:, pl.ds(0, HW)], weight_ref, weight_sem)
+    affine_load = copy(affine_hbm, affine_ref, affine_sem)
+    affine_load.start()
     loads[0].start()
     weight_load.start()
+    row = lax.broadcasted_iota(jnp.int32, (PAD, C), 0)
+    column = lax.broadcasted_iota(jnp.int32, (PAD, C), 1)
+    tail = jnp.zeros((PAD, C), jnp.int32)
+    for j in range(TOPM):
+        tail = jnp.where((row == 0) & (column == j), owner_ref[j] * held + slot_ref[j], tail)
     for h in range(G):
-        query_ref[h, patches:, :] = tail_ref[...]
+        query_ref[h, patches:, :] = tail.astype(F32).astype(BF)
+    affine_load.wait()
     for i in range(steps):
         at = slice(i * rows, (i + 1) * rows)
         loads[i].wait()
@@ -159,7 +169,9 @@
         mapped = dot(hidden, weight_ref[...]).astype(BF).astype(F32)
         for h in range(G):
             one = mapped[:, h * C : (h + 1) * C]
-            query_ref[h, at, :] = (one * inverse_rms(one) * factor_ref[0, h]).astype(BF)
+            query_ref[h, at, :] = (
+                one * inverse_rms(one) * (sharpness_ref[0, h] / C)
+            ).astype(BF)
     send = copy(query_ref, query_hbm, query_sem)
     send.start()
     for store in stores:
@@ -167,23 +179,25 @@
     send.wait()
 
 
-def modulate(act, affine, weight, factor, tail, after):
+def modulate(act, affine, weight, sharpness, owner, slot, held, after):
     patches, depth = act.shape
     steps = 2
     rows = patches // steps
     shape = (G, patches + PAD, C)
     return pl.pallas_call(
-        modulate_kernel,
-        in_specs=[HBM, WHOLE, HBM, SCALARS, WHOLE, ANY],
+        functools.partial(modulate_kernel, held),
+        in_specs=[HBM, HBM, HBM, SCALARS, SCALARS, SCALARS, ANY],
         out_specs=[HBM, HBM],
         out_shape=[hbm_out((patches, depth)), hbm_out(shape)],
         scratch_shapes=[
             pltpu.VMEM((steps, rows, depth), BF),
+            pltpu.VMEM(affine.shape, F32),
             pltpu.VMEM((depth, HW), BF),
             pltpu.VMEM((steps, rows, depth), BF),
             pltpu.VMEM(shape, BF),
             DMA((steps,)),
             DMA,
+            DMA,
             DMA((steps,)),
             DMA,
         ],
@@ -192,11 +206,11 @@
         cost_estimate=cost(
             2 * patches * depth * HW, 4 * patches * depth + 2 * depth * HW + 2 * patches * HW
         ),
-    )(in_hbm(act), affine, in_hbm(weight), factor, tail, in_hbm(after))
+    )(in_hbm(act), in_hbm(affine), in_hbm(weight), sharpness, owner, slot, in_hbm(after))
 
 
 def temporal_entry_kernel(
-    quarters, hidden_hbm, weight_hbm, factor_ref, _, out_hbm,
+    quarters, hidden_hbm, weight_hbm, sharpness_ref, _, out_hbm,
     hidden_ref, weight_ref, out_ref, hidden_sem, weight_sem, store_sem,
 ):
     rows = hidden_ref.shape[0] // quarters
@@ -222,7 +236,7 @@
                 one = done.astype(F32)
                 one = one * inverse_rms(one)
                 if part == 0:
-                    one = one * factor_ref[1, h]
+                    one = one * (sharpness_ref[1, h] / C)
                 done = one.astype(BF)
             for z in range(quarters):
                 out_ref[part, z, h] = done[z * rows : (z + 1) * rows, :]
@@ -232,7 +246,7 @@
         store.wait()
 
 
-def temporal_entry(hidden, weight, factor, quarters, after):
+def temporal_entry(hidden, weight, sharpness, quarters, after):
     patches, depth = hidden.shape
     rows = patches // quarters
     return pl.pallas_call(
@@ -253,7 +267,7 @@
         cost_estimate=cost(
             6 * patches * depth * HW, 2 * patches * depth + 6 * depth * HW + 6 * patches * HW
         ),
-    )(in_hbm(hidden), in_hbm(weight), factor, in_hbm(after))
+    )(in_hbm(hidden), in_hbm(weight), sharpness, in_hbm(after))
 
 
 def temporal_attend_kernel(length_ref, in_hbm_ref, _, out_hbm, in_ref, out_ref, sem):
@@ -610,17 +624,14 @@
         pieces = swap_apart(split)
 
     with jax.named_scope("queries"):
-        factor = softmax_sharpness / C
-        index = recalled_picture_holder.reshape(TOPM) * held + recalled_picture_position.reshape(
-            TOPM
-        )
-        tail = jnp.zeros((PAD, C), BF).at[0, :TOPM].set(index.astype(BF))
         hidden, query = modulate(
             patch_activation_tensor.reshape(patches, depth),
             conditioning_affine.reshape(2, depth),
             entry_projection_matrix,
-            factor,
-            tail,
+            softmax_sharpness,
+            recalled_picture_holder.reshape(TOPM),
+            recalled_picture_position.reshape(TOPM),
+            held,
             after=split[0],
         )
         here = swap(query, "x")
@@ -630,25 +641,30 @@
         above = lax.ppermute(joined, "y", turn(-1))
         below = lax.ppermute(joined, "y", turn(1))
 
+    with jax.named_scope("temporal"):
+        parts = temporal_entry(
+            hidden, entry_projection_matrix, softmax_sharpness, rings, after=joined
+        )
+        sent = swap(parts.reshape((rings * G,) + parts.shape[2:]), ("z", "x"))
+
     with jax.named_scope("queries"):
-        here, joined = lax.optimization_barrier((here, joined))
-        groups = [here] + [lax.ppermute(here, "z", turn(-step)) for step in (1, 2, 3)]
-
-    with jax.named_scope("own"):
-        own = own_attend(hidden, entry_projection_matrix, query, after=joined)
+        here, parts = lax.optimization_barrier((here, parts))
+        z_above = lax.ppermute(here, "z", turn(-1))
+        z_below = lax.ppermute(here, "z", turn(1))
+        z_far = lax.ppermute(z_below, "z", turn(1))
+        groups = [here, z_above, z_far, z_below]
 
     with jax.named_scope("store"):
-        joined, above, below, own = lax.optimization_barrier((joined, above, below, own))
+        above, below, parts = lax.optimization_barrier((above, below, parts))
         far_first = lax.ppermute(above[: held // 2], "y", turn(-1))
         far_last = lax.ppermute(below[held // 2 :], "y", turn(1))
 
-    with jax.named_scope("temporal"):
-        parts = temporal_entry(hidden, entry_projection_matrix, factor, rings, after=own)
-        sent = swap(parts.reshape((rings * G,) + parts.shape[2:]), ("z", "x"))
+    with jax.named_scope("own"):
+        own = own_attend(hidden, entry_projection_matrix, query, after=parts)
 
     with jax.named_scope("store"):
         near = [joined, above, far_first, far_last, below]
-        *near, parts = lax.optimization_barrier((*near, parts))
+        *near, own = lax.optimization_barrier((*near, own))
         blocks = near + [lax.ppermute(block, "c", other) for block in near]
 
     def attend(queries, after):
@@ -660,7 +676,7 @@
         return memory_attend(index, queries, blocks, after)
 
     with jax.named_scope("memory"):
-        sum_far, sum_above = attend([groups[2], groups[1]], parts)
+        sum_far, sum_above = attend([groups[2], groups[1]], own)
         from_far = lax.ppermute(sum_far, "z", turn(2))
         from_below = lax.ppermute(sum_above, "z", turn(1))
         sum_below, sum_here = attend([groups[3], here], sum_far)

time: 172 us -> 160 us (0.930)
  blocking collectives: 12.6 us -> 0 us
    all_to_all x1 -> x0, blocking collectives: 12.6 us -> none  [swap(): return lax.all_to_all(blocks, axes, split_axis=0, concat_axis=0, tiled=True)]
    ppermute x6, waiting for transfers between devices: 5.69 us -> 17.7 us  [swap_apart(): lax.ppermute(blocks[j], 'x', turn(j))]
    ppermute x3, waiting for transfers between devices: 29.9 us -> 22.6 us  [the longest x1 19 us: on_device(): z_below = lax.ppermute(here, 'z', turn(1))]
    ppermute x1, waiting for transfers between devices: 4.13 us -> 0.01 us  [on_device(): far_first = lax.ppermute(above[:held // 2], 'y', turn(-1))]
    ppermute x1, waiting for transfers between devices: 3.89 us -> 0.01 us  [on_device(): far_last = lax.ppermute(below[held // 2:], 'y', turn(1))]
    ppermute x1, waiting for transfers between devices: 12.2 us -> 14.9 us  [on_device(): from_above = lax.ppermute(sum_below, 'z', turn(3))]
    ppermute x1, starting transfers between devices: 3.52 us -> 1.73 us  [on_device(): from_above = lax.ppermute(sum_below, 'z', turn(3))]
    all_to_all x2 -> x3, starting transfers between devices: 13.2 us -> 14.9 us  [swap(): return lax.all_to_all(blocks, axes, split_axis=0, concat_axis=0, tiled=True)]
  transfers between devices with their start and end apart: 23 -> 24, of which waited for: 9 -> 8; matrix products, arithmetic and copies ran while one was open for 3% -> 2% of each run, Pallas kernels for 21% -> 26%
where the time goes in v7:
time: 160 us; the launch traced here: 159 us
  waiting for transfers between devices  55.9 us (35%)
  Pallas kernels  53.5 us (33%)
  starting transfers between devices  41.6 us (26%)
  local copies, waits for them, and re-layouts  6.94 us (4%)
    ppermute x1, waiting for transfers between devices, on_device(): z_below = lax.ppermute(here, 'z', turn(1))  19 us
    ppermute x6, waiting for transfers between devices, swap_apart(): lax.ppermute(blocks[j], 'x', turn(j))  17.7 us
    pallas_call x2, Pallas kernels, memory_attend(): pl.pallas_call(functools.partial(memory_attend_kernel, groups, count), in...  17 us
    ppermute x1, waiting for transfers between devices, on_device(): from_above = lax.ppermute(sum_below, 'z', turn(3))  14.9 us
    all_to_all x3, starting transfers between devices, swap(): return lax.all_to_all(blocks, axes, split_axis=0, concat_axis=0, tiled=True)  14.9 us
    ppermute x6, starting transfers between devices, swap_apart(): lax.ppermute(blocks[j], 'x', turn(j))  10.1 us
    pallas_call x1, Pallas kernels, temporal_entry(): pl.pallas_call(functools.partial(temporal_entry_kernel, quarters), in_spe...  8.57 us
    pallas_call x1, Pallas kernels, own_attend(): pl.pallas_call(own_attend_kernel, in_specs=[HBM, HBM, HBM, ANY], out_spec...  8.08 us
  transfers between devices with their start and end apart: 24, of which 8 were waited for; matrix products, arithmetic and copies ran while one was open for 2% of the time, Pallas kernels for 26%

profile of v7, /device:TPU:0, one launch (start us, length us, event | category | flops | bytes accessed | tf_op | source)
XLA Modules:
  0.0 159.1 jit_solution(9497972975884752920)
XLA Ops:
  0.0 1.1 copy.14
  1.2 1.0 split_store.1
  2.2 0.0 copy-start.4
  2.2 0.7 copy-done.4
  2.8 0.7 copy-done.6
  3.5 0.7 copy-done.7
  4.2 5.6 %modulate.1 = (bf16[576,2048]{1,0:T(8,128)(2,1)}, bf16[4,592,128]{2,1,0:T(8,128)(2,1)}) custom-call(bf16[576,2048]{1,0:T(8,128)(2,1)} %bitcast.26, f32[2,2048]{1,0:T(2,128)} %bitcast.28, bf16[2048,3072]{1,0:T(8,128)(2,1)} %weight_hbm.6, f32[2,4]{1,0:T(2,128)S(1)} %copy-done.4, s32[6]{0:T(128)S(1)} %bitcast.23, s32[6]{0:T(128)S(1)} %bitcast.24, ...), custom_call_target="tpu_custom_call" | custom-call | flops 75497472 | bytes 462848 | tf_op jit(solution)/shard_map/queries/modulate/pallas_call | solution.py:187
  9.8 0.0 copy-start.5
  9.8 4.4 %all-to-all-start = ((bf16[4,592,128]{2,1,0:T(8,128)(2,1)}), bf16[4,592,128]{2,1,0:T(8,128)(2,1)}, u32[]{:S(2)}, u32[]{:S(2)}) async-start(bf16[4,592,128]{2,1,0:T(8,128)(2,1)} %get-tuple-element.35.query_hbm), calls=%async_computation | async-start | bytes 1212416 | tf_op jit(solution)/shard_map/queries/all_to_all | solution.py:617
  14.2 2.0 %collective-permute-start = (bf16[288,256]{1,0:T(8,128)(2,1)S(1)}, bf16[288,256]{1,0:T(8,128)(2,1)S(1)}, u32[]{:S(2)}, u32[]{:S(2)}) collective-permute-start(bf16[288,256]{1,0:T(8,128)(2,1)S(1)} %copy-done.10), channel_id=1, source_target_pairs={{0,1},{1,2},{2,3},{3,0},{4,5},{5,6},{6,7},{7,4},{8,9},{9,10},{10,1... | collective-permute-start | bytes 442376 | tf_op jit(solution)/shard_map/store/ppermute | solution.py:620
  16.2 2.7 %collective-permute-start.1 = (bf16[288,256]{1,0:T(8,128)(2,1)S(1)}, bf16[288,256]{1,0:T(8,128)(2,1)S(1)}, u32[]{:S(2)}, u32[]{:S(2)}) collective-permute-start(bf16[288,256]{1,0:T(8,128)(2,1)S(1)} %copy-done.9), channel_id=1, source_target_pairs={{0,2},{1,3},{2,0},{3,1},{4,6},{5,7},{6,4},{7,5},{8,10},{9,11},{10,... | collective-permute-start | bytes 442376 | tf_op jit(solution)/shard_map/store/ppermute | solution.py:620
  18.9 1.5 collective-permute-start.2
  20.3 8.2 %collective-permute-done.refs_1_ = bf16[288,256]{1,0:T(8,128)(2,1)S(1)} collective-permute-done((bf16[288,256]{1,0:T(8,128)(2,1)S(1)}, bf16[288,256]{1,0:T(8,128)(2,1)S(1)}, u32[]{:S(2)}, u32[]{:S(2)}) %collective-permute-start) | collective-permute-done | bytes 147488 | tf_op jit(solution)/shard_map/store/ppermute | solution.py:620
  28.5 2.3 %collective-permute-done.1.refs_2_ = bf16[288,256]{1,0:T(8,128)(2,1)S(1)} collective-permute-done((bf16[288,256]{1,0:T(8,128)(2,1)S(1)}, bf16[288,256]{1,0:T(8,128)(2,1)S(1)}, u32[]{:S(2)}, u32[]{:S(2)}) %collective-permute-start.1) | collective-permute-done | bytes 147488 | tf_op jit(solution)/shard_map/store/ppermute | solution.py:620
  30.8 0.0 collective-permute-done.2.refs_3_
  30.8 1.8 %join_pieces.1._.refs_2_ = bf16[8,144,256]{2,1,0:T(8,128)(2,1)} custom-call(bf16[288,256]{1,0:T(8,128)(2,1)S(1)} %copy-done.2, bf16[288,256]{1,0:T(8,128)(2,1)S(1)} %collective-permute-done.refs_1_, bf16[288,256]{1,0:T(8,128)(2,1)S(1)} %collective-permute-done.1.refs_2_, bf16[288,256]{1,0:T(8,128)(2,1)S(1)} %collective-permute-done.2.refs_3_, ...), custom_call_target="tpu_custom_call" | custom-call | flops 18432 | bytes 73728 | tf_op jit(solution)/shard_map/store/join_pieces/pallas_call | solution.py:113
  32.6 8.6 %temporal_entry.1._ = bf16[4,4,3,144,128]{4,3,2,1,0:T(8,128)(2,1)} custom-call(bf16[576,2048]{1,0:T(8,128)(2,1)} %get-tuple-element.34.refs_4_.hidden_hbm, bf16[2048,3072]{1,0:T(8,128)(2,1)} %weight_hbm.6, f32[2,4]{1,0:T(2,128)S(1)} %copy-done.5, bf16[8,144,256]{2,1,0:T(8,128)(2,1)} %join_pieces.1._.refs_2_), custom_call_target="tpu_custom_call" | custom-call | flops 226492416 | bytes 651264 | tf_op jit(solution)/shard_map/temporal/temporal_entry/pallas_call | solution.py:252
  41.2 0.0 all-to-all-done.refs_1_
  41.2 2.1 %collective-permute-start.7 = (bf16[4,592,128]{2,1,0:T(8,128)(2,1)}, bf16[4,592,128]{2,1,0:T(8,128)(2,1)}, u32[]{:S(2)}, u32[]{:S(2)}) collective-permute-start(bf16[4,592,128]{2,1,0:T(8,128)(2,1)} %all-to-all-done.refs_1_), channel_id=1, source_target_pairs={{0,4},{4,8},{8,12},{12,0},{1,5},{5,9},{9,13},{13,1},{2,6},{6,10},{... | collective-permute-start | bytes 1818632 | tf_op jit(solution)/shard_map/queries/ppermute | solution.py:653
  43.3 3.0 %collective-permute-start.3 = (bf16[8,144,256]{2,1,0:T(8,128)(2,1)S(1)}, bf16[8,144,256]{2,1,0:T(8,128)(2,1)S(1)}, u32[]{:S(2)}, u32[]{:S(2)}) collective-permute-start(bf16[8,144,256]{2,1,0:T(8,128)(2,1)S(1)} %copy-done), channel_id=1, source_target_pairs={{0,96},{32,0},{64,32},{96,64},{1,97},{33,1},{65,33},{97,65},{2,98}... | collective-permute-start | bytes 1769480 | tf_op jit(solution)/shard_map/store/ppermute | solution.py:641
  46.3 0.0 collective-permute-start.4
  46.3 5.6 %all-to-all-start.1 = ((bf16[16,3,144,128]{3,2,1,0:T(8,128)(2,1)}), bf16[16,3,144,128]{3,2,1,0:T(8,128)(2,1)S(1)}, u32[]{:S(2)}, u32[]{:S(2)}) async-start(bf16[16,3,144,128]{3,2,1,0:T(8,128)(2,1)} %bitcast.25), calls=%async_computation.1 | async-start | bytes 3538944 | tf_op jit(solution)/shard_map/temporal/all_to_all | solution.py:617
  51.9 3.1 %collective-permute-start.14 = (bf16[4,592,128]{2,1,0:T(8,128)(2,1)}, bf16[4,592,128]{2,1,0:T(8,128)(2,1)}, u32[]{:S(2)}, u32[]{:S(2)}) collective-permute-start(bf16[4,592,128]{2,1,0:T(8,128)(2,1)} %all-to-all-done.refs_1_), channel_id=1, source_target_pairs={{0,12},{4,0},{8,4},{12,8},{1,13},{5,1},{9,5},{13,9},{2,14},{6,2},{... | collective-permute-start | bytes 1818632 | tf_op jit(solution)/shard_map/queries/ppermute | solution.py:652
  55.1 19.0 %collective-permute-done.7.refs_0_ = bf16[4,592,128]{2,1,0:T(8,128)(2,1)} collective-permute-done((bf16[4,592,128]{2,1,0:T(8,128)(2,1)}, bf16[4,592,128]{2,1,0:T(8,128)(2,1)}, u32[]{:S(2)}, u32[]{:S(2)}) %collective-permute-start.7) | collective-permute-done | bytes 606240 | tf_op jit(solution)/shard_map/queries/ppermute | solution.py:653
  74.1 0.0 collective-permute-start.13
  74.1 0.0 collective-permute-done.3.refs_3_
  74.1 0.0 collective-permute-done.4.refs_6_
  74.1 3.1 %collective-permute-start.5 = (bf16[4,144,256]{2,1,0:T(8,128)(2,1)S(1)}, bf16[4,144,256]{2,1,0:T(8,128)(2,1)}, u32[]{:S(2)}, u32[]{:S(2)}) collective-permute-start(bf16[4,144,256]{2,1,0:T(8,128)(2,1)S(1)} %slice.18), channel_id=1, source_target_pairs={{0,96},{32,0},{64,32},{96,64},{1,97},{33,1},{65,33},{97,65},{2,98}... | collective-permute-start | bytes 884744 | tf_op jit(solution)/shard_map/store/ppermute | solution.py:659
  77.2 0.3 collective-permute-start.6
  77.5 8.1 %own_attend.1.refs_12_.own_hbm = bf16[4,592,128]{2,1,0:T(8,128)(2,1)} custom-call(bf16[576,2048]{1,0:T(8,128)(2,1)} %get-tuple-element.34.refs_4_.hidden_hbm, bf16[2048,3072]{1,0:T(8,128)(2,1)} %weight_hbm.6, bf16[4,592,128]{2,1,0:T(8,128)(2,1)} %get-tuple-element.35.query_hbm, bf16[4,4,3,144,128]{4,3,2,1,0:T(8,128)(2,1)} %temporal_entry.1._), custom_call_target="tpu_custom_call" | custom-call | flops 214695936 | bytes 593920 | tf_op jit(solution)/shard_map/own/own_attend/pallas_call | solution.py:380
  85.6 0.0 collective-permute-done.5.refs_4_
  85.6 0.0 collective-permute-done.6.refs_5_
  85.6 0.1 collective-permute-start.12
  85.7 0.5 collective-permute-start.8
  86.2 0.1 collective-permute-start.9
  86.3 0.0 collective-permute-done.14.refs_1_
  86.3 0.4 collective-permute-start.10
  86.7 3.6 %collective-permute-done.13.refs_0_ = bf16[4,592,128]{2,1,0:T(8,128)(2,1)} collective-permute-done((bf16[4,592,128]{2,1,0:T(8,128)(2,1)}, bf16[4,592,128]{2,1,0:T(8,128)(2,1)}, u32[]{:S(2)}, u32[]{:S(2)}) %collective-permute-start.13) | collective-permute-done | bytes 606240 | tf_op jit(solution)/shard_map/queries/ppermute | solution.py:654
  90.3 0.0 collective-permute-start.11
  90.3 0.7 slice.21
  91.0 0.7 slice.26
  91.8 0.7 slice.24
  92.5 0.7 slice.25
  93.2 0.0 collective-permute-done.10.refs_9_
  93.3 0.0 collective-permute-done.8.refs_7_
  93.3 0.0 collective-permute-done.9.refs_8_
  93.3 8.5 %memory_attend.2 = (bf16[4,592,128]{2,1,0:T(8,128)(2,1)}, bf16[4,592,128]{2,1,0:T(8,128)(2,1)}) custom-call(s32[8,6]{1,0:T(8,128)S(1)} %fusion.24.index_ref, bf16[4,592,128]{2,1,0:T(8,128)(2,1)} %collective-permute-done.13.refs_0_, bf16[4,592,128]{2,1,0:T(8,128)(2,1)} %collective-permute-done.14.refs_1_, bf16[8,144,256]{2,1,0:T(8,128)(2,1)S(1)} %copy-done, ...), custom_call_target="tpu_custom_call" | custom-call | flops 261881856 | bytes 446464 | tf_op jit(solution)/shard_map/memory/memory_attend/pallas_call | solution.py:444
  101.8 1.9 %collective-permute-start.15 = (bf16[4,592,128]{2,1,0:T(8,128)(2,1)}, bf16[4,592,128]{2,1,0:T(8,128)(2,1)}, u32[]{:S(2)}, u32[]{:S(2)}) collective-permute-start(bf16[4,592,128]{2,1,0:T(8,128)(2,1)} %get-tuple-element.47.refs_12_), channel_id=1, source_target_pairs={{0,8},{4,12},{8,0},{12,4},{1,9},{5,13},{9,1},{13,5},{2,10},{6,14},... | collective-permute-start | bytes 1818632 | tf_op jit(solution)/shard_map/memory/ppermute | solution.py:680
  103.7 8.5 %memory_attend.3 = (bf16[4,592,128]{2,1,0:T(8,128)(2,1)}, bf16[4,592,128]{2,1,0:T(8,128)(2,1)}) custom-call(s32[8,6]{1,0:T(8,128)S(1)} %fusion.14.index_ref, bf16[4,592,128]{2,1,0:T(8,128)(2,1)} %collective-permute-done.7.refs_0_, bf16[4,592,128]{2,1,0:T(8,128)(2,1)} %all-to-all-done.refs_1_, bf16[8,144,256]{2,1,0:T(8,128)(2,1)S(1)} %copy-done, ...), custom_call_target="tpu_custom_call" | custom-call | flops 261881856 | bytes 446464 | tf_op jit(solution)/shard_map/memory/memory_attend/pallas_call | solution.py:444
  112.2 1.7 %collective-permute-start.17 = (bf16[4,592,128]{2,1,0:T(8,128)(2,1)}, bf16[4,592,128]{2,1,0:T(8,128)(2,1)}, u32[]{:S(2)}, u32[]{:S(2)}) collective-permute-start(bf16[4,592,128]{2,1,0:T(8,128)(2,1)} %get-tuple-element.50._), channel_id=1, source_target_pairs={{0,12},{4,0},{8,4},{12,8},{1,13},{5,1},{9,5},{13,9},{2,14},{6,2},{... | collective-permute-start | bytes 1818632 | tf_op jit(solution)/shard_map/memory/ppermute | solution.py:683
  113.9 0.4 collective-permute-start.16
  114.9 2.5 %temporal_attend.1 = bf16[16,144,128]{2,1,0:T(8,128)(2,1)} custom-call(s32[1]{0:T(128)S(6)} %copy.23.length_ref, bf16[16,3,144,128]{3,2,1,0:T(8,128)(2,1)S(1)} %all-to-all-done.1.in_hbm_ref, bf16[4,592,128]{2,1,0:T(8,128)(2,1)} %get-tuple-element.50._), custom_call_target="tpu_custom_call" | custom-call | flops 18874368 | bytes 147456 | tf_op jit(solution)/shard_map/temporal/temporal_attend/pallas_call | solution.py:302
  117.4 4.9 %all-to-all-start.2 = ((bf16[16,144,128]{2,1,0:T(8,128)(2,1)}), bf16[16,144,128]{2,1,0:T(8,128)(2,1)S(1)}, u32[]{:S(2)}, u32[]{:S(2)}) async-start(bf16[16,144,128]{2,1,0:T(8,128)(2,1)} %temporal_attend.1), calls=%async_computation.2 | async-start | bytes 1179648 | tf_op jit(solution)/shard_map/temporal/all_to_all | solution.py:617
  122.3 14.9 %collective-permute-done.17.refs_3_ = bf16[4,592,128]{2,1,0:T(8,128)(2,1)} collective-permute-done((bf16[4,592,128]{2,1,0:T(8,128)(2,1)}, bf16[4,592,128]{2,1,0:T(8,128)(2,1)}, u32[]{:S(2)}, u32[]{:S(2)}) %collective-permute-start.17) | collective-permute-done | bytes 606240 | tf_op jit(solution)/shard_map/memory/ppermute | solution.py:683
  137.2 0.0 collective-permute-done.15.refs_1_
  137.2 0.6 collective-permute-done.16.refs_2_
  137.8 2.8 %add_partials.1 = (bf16[592,128]{1,0:T(8,128)(2,1)}, bf16[592,128]{1,0:T(8,128)(2,1)}, bf16[592,128]{1,0:T(8,128)(2,1)}, bf16[592,128]{1,0:T(8,128)(2,1)}) custom-call(s32[1]{0:T(128)} %bitcast.x_ref, bf16[4,592,128]{2,1,0:T(8,128)(2,1)S(1)} %copy-done.1, bf16[4,592,128]{2,1,0:T(8,128)(2,1)} %collective-permute-done.15.refs_1_, ...), custom_call_target="tpu_custom_call" | custom-call | flops 75776 | bytes 151552 | tf_op jit(solution)/shard_map/memory/add_partials/pallas_call | solution.py:496
  140.6 0.1 collective-permute-start.18
  140.7 2.9 %collective-permute-start.19 = (bf16[592,128]{1,0:T(8,128)(2,1)}, bf16[592,128]{1,0:T(8,128)(2,1)S(1)}, u32[]{:S(2)}, u32[]{:S(2)}) collective-permute-start(bf16[592,128]{1,0:T(8,128)(2,1)} %get-tuple-element.53), channel_id=1, source_target_pairs={{0,2},{1,3},{2,0},{3,1},{4,6},{5,7},{6,4},{7,5},{8,10},{9,11},{10,... | collective-permute-start | bytes 454664 | tf_op jit(solution)/shard_map/memory/ppermute | solution.py:620
  143.6 1.0 collective-permute-start.20
  144.5 6.6 %collective-permute-done.18.memory_1 = bf16[592,128]{1,0:T(8,128)(2,1)S(1)} collective-permute-done((bf16[592,128]{1,0:T(8,128)(2,1)}, bf16[592,128]{1,0:T(8,128)(2,1)S(1)}, u32[]{:S(2)}, u32[]{:S(2)}) %collective-permute-start.18) | collective-permute-done | bytes 151584 | tf_op jit(solution)/shard_map/memory/ppermute | solution.py:620
  151.1 0.6 collective-permute-done.20.memory_3
  151.8 0.9 copy-done.3
  152.7 6.2 %leave.1 = bf16[576,2048]{1,0:T(8,128)(2,1)} custom-call(s32[1]{0:T(128)} %bitcast.x_ref, bf16[4,592,128]{2,1,0:T(8,128)(2,1)} %own_attend.1.refs_12_.own_hbm, bf16[592,128]{1,0:T(8,128)(2,1)S(1)} %copy-done.3, bf16[592,128]{1,0:T(8,128)(2,1)S(1)} %collective-permute-done.18.memory_1, bf16[592,128]{1,0:T(8,128)(2,1)S(1)} %collective-permute-done.19.memory_2, ...), custom_call_target="tpu_custom_call" | custom-call | flops 150994944 | bytes 630784 | tf_op jit(solution)/shard_map/exit/leave/pallas_call | solution.py:567
  (29 shorter events, 0.2 us)
Async XLA Ops:
  2.2 0.7 copy-start.4
  2.8 0.7 copy-start.6
  3.5 0.7 copy-start.7
  4.2 10.0 %copy-start.10 = (bf16[288,256]{1,0:T(8,128)(2,1)S(1)}, bf16[288,256]{1,0:T(8,128)(2,1)}, u32[]{:S(2)}) copy-start(bf16[288,256]{1,0:T(8,128)(2,1)} %get-tuple-element.31) | copy-start | bytes 442372
  4.2 12.0 %copy-start.9 = (bf16[288,256]{1,0:T(8,128)(2,1)S(1)}, bf16[288,256]{1,0:T(8,128)(2,1)}, u32[]{:S(2)}) copy-start(bf16[288,256]{1,0:T(8,128)(2,1)} %get-tuple-element.32) | copy-start | bytes 442372
  4.2 14.7 %copy-start.8 = (bf16[288,256]{1,0:T(8,128)(2,1)S(1)}, bf16[288,256]{1,0:T(8,128)(2,1)}, u32[]{:S(2)}) copy-start(bf16[288,256]{1,0:T(8,128)(2,1)} %get-tuple-element.33) | copy-start | bytes 442372
  4.2 26.7 %copy-start.2 = (bf16[288,256]{1,0:T(8,128)(2,1)S(1)}, bf16[288,256]{1,0:T(8,128)(2,1)}, u32[]{:S(2)}) copy-start(bf16[288,256]{1,0:T(8,128)(2,1)} %get-tuple-element.30._.refs_0_) | copy-start | bytes 442372
  9.8 22.9 %copy-start.5 = (f32[2,4]{1,0:T(2,128)S(1)}, f32[2,4]{1,0:T(2,128)}, u32[]{:S(2)}) copy-start(f32[2,4]{1,0:T(2,128)} %sharpness_ref.3) | copy-start | bytes 100
  9.8 31.4 %all-to-all-start = ((bf16[4,592,128]{2,1,0:T(8,128)(2,1)}), bf16[4,592,128]{2,1,0:T(8,128)(2,1)}, u32[]{:S(2)}, u32[]{:S(2)}) async-start(bf16[4,592,128]{2,1,0:T(8,128)(2,1)} %get-tuple-element.35.query_hbm), calls=%async_computation | async-start | bytes 1212416 | tf_op jit(solution)/shard_map/queries/all_to_all | solution.py:617
  14.2 14.4 %collective-permute-start = (bf16[288,256]{1,0:T(8,128)(2,1)S(1)}, bf16[288,256]{1,0:T(8,128)(2,1)S(1)}, u32[]{:S(2)}, u32[]{:S(2)}) collective-permute-start(bf16[288,256]{1,0:T(8,128)(2,1)S(1)} %copy-done.10), channel_id=1, source_target_pairs={{0,1},{1,2},{2,3},{3,0},{4,5},{5,6},{6,7},{7,4},{8,9},{9,10},{10,1... | collective-permute-start | bytes 442376 | tf_op jit(solution)/shard_map/store/ppermute | solution.py:620
  16.2 14.6 %collective-permute-start.1 = (bf16[288,256]{1,0:T(8,128)(2,1)S(1)}, bf16[288,256]{1,0:T(8,128)(2,1)S(1)}, u32[]{:S(2)}, u32[]{:S(2)}) collective-permute-start(bf16[288,256]{1,0:T(8,128)(2,1)S(1)} %copy-done.9), channel_id=1, source_target_pairs={{0,2},{1,3},{2,0},{3,1},{4,6},{5,7},{6,4},{7,5},{8,10},{9,11},{10,... | collective-permute-start | bytes 442376 | tf_op jit(solution)/shard_map/store/ppermute | solution.py:620
  18.9 12.0 %collective-permute-start.2 = (bf16[288,256]{1,0:T(8,128)(2,1)S(1)}, bf16[288,256]{1,0:T(8,128)(2,1)S(1)}, u32[]{:S(2)}, u32[]{:S(2)}) collective-permute-start(bf16[288,256]{1,0:T(8,128)(2,1)S(1)} %copy-done.8), channel_id=1, source_target_pairs={{0,3},{1,0},{2,1},{3,2},{4,7},{5,4},{6,5},{7,6},{8,11},{9,8},{10,9... | collective-permute-start | bytes 442376 | tf_op jit(solution)/shard_map/store/ppermute | solution.py:620
  32.6 10.7 %copy-start = (bf16[8,144,256]{2,1,0:T(8,128)(2,1)S(1)}, bf16[8,144,256]{2,1,0:T(8,128)(2,1)}, u32[]{:S(2)}) copy-start(bf16[8,144,256]{2,1,0:T(8,128)(2,1)} %join_pieces.1._.refs_2_) | copy-start | bytes 1769476
  41.2 32.8 %collective-permute-start.7 = (bf16[4,592,128]{2,1,0:T(8,128)(2,1)}, bf16[4,592,128]{2,1,0:T(8,128)(2,1)}, u32[]{:S(2)}, u32[]{:S(2)}) collective-permute-start(bf16[4,592,128]{2,1,0:T(8,128)(2,1)} %all-to-all-done.refs_1_), channel_id=1, source_target_pairs={{0,4},{4,8},{8,12},{12,0},{1,5},{5,9},{9,13},{13,1},{2,6},{6,10},{... | collective-permute-start | bytes 1818632 | tf_op jit(solution)/shard_map/queries/ppermute | solution.py:653
  43.3 30.7 %collective-permute-start.3 = (bf16[8,144,256]{2,1,0:T(8,128)(2,1)S(1)}, bf16[8,144,256]{2,1,0:T(8,128)(2,1)S(1)}, u32[]{:S(2)}, u32[]{:S(2)}) collective-permute-start(bf16[8,144,256]{2,1,0:T(8,128)(2,1)S(1)} %copy-done), channel_id=1, source_target_pairs={{0,96},{32,0},{64,32},{96,64},{1,97},{33,1},{65,33},{97,65},{2,98}... | collective-permute-start | bytes 1769480 | tf_op jit(solution)/shard_map/store/ppermute | solution.py:641
  46.3 27.7 %collective-permute-start.4 = (bf16[8,144,256]{2,1,0:T(8,128)(2,1)S(1)}, bf16[8,144,256]{2,1,0:T(8,128)(2,1)S(1)}, u32[]{:S(2)}, u32[]{:S(2)}) collective-permute-start(bf16[8,144,256]{2,1,0:T(8,128)(2,1)S(1)} %copy-done), channel_id=1, source_target_pairs={{0,32},{32,64},{64,96},{96,0},{1,33},{33,65},{65,97},{97,1},{2,34}... | collective-permute-start | bytes 1769480 | tf_op jit(solution)/shard_map/store/ppermute | solution.py:642
  46.3 68.6 %all-to-all-start.1 = ((bf16[16,3,144,128]{3,2,1,0:T(8,128)(2,1)}), bf16[16,3,144,128]{3,2,1,0:T(8,128)(2,1)S(1)}, u32[]{:S(2)}, u32[]{:S(2)}) async-start(bf16[16,3,144,128]{3,2,1,0:T(8,128)(2,1)} %bitcast.25), calls=%async_computation.1 | async-start | bytes 3538944 | tf_op jit(solution)/shard_map/temporal/all_to_all | solution.py:617
  51.9 34.3 %collective-permute-start.14 = (bf16[4,592,128]{2,1,0:T(8,128)(2,1)}, bf16[4,592,128]{2,1,0:T(8,128)(2,1)}, u32[]{:S(2)}, u32[]{:S(2)}) collective-permute-start(bf16[4,592,128]{2,1,0:T(8,128)(2,1)} %all-to-all-done.refs_1_), channel_id=1, source_target_pairs={{0,12},{4,0},{8,4},{12,8},{1,13},{5,1},{9,5},{13,9},{2,14},{6,2},{... | collective-permute-start | bytes 1818632 | tf_op jit(solution)/shard_map/queries/ppermute | solution.py:652
  74.1 16.3 %collective-permute-start.13 = (bf16[4,592,128]{2,1,0:T(8,128)(2,1)}, bf16[4,592,128]{2,1,0:T(8,128)(2,1)}, u32[]{:S(2)}, u32[]{:S(2)}) collective-permute-start(bf16[4,592,128]{2,1,0:T(8,128)(2,1)} %collective-permute-done.7.refs_0_), channel_id=1, source_target_pairs={{0,4},{4,8},{8,12},{12,0},{1,5},{5,9},{9,13},{13,1},{2,6},{6,10},{... | collective-permute-start | bytes 1818632 | tf_op jit(solution)/shard_map/queries/ppermute | solution.py:654
  74.1 11.5 %collective-permute-start.5 = (bf16[4,144,256]{2,1,0:T(8,128)(2,1)S(1)}, bf16[4,144,256]{2,1,0:T(8,128)(2,1)}, u32[]{:S(2)}, u32[]{:S(2)}) collective-permute-start(bf16[4,144,256]{2,1,0:T(8,128)(2,1)S(1)} %slice.18), channel_id=1, source_target_pairs={{0,96},{32,0},{64,32},{96,64},{1,97},{33,1},{65,33},{97,65},{2,98}... | collective-permute-start | bytes 884744 | tf_op jit(solution)/shard_map/store/ppermute | solution.py:659
  77.2 8.4 %collective-permute-start.6 = (bf16[4,144,256]{2,1,0:T(8,128)(2,1)S(1)}, bf16[4,144,256]{2,1,0:T(8,128)(2,1)}, u32[]{:S(2)}, u32[]{:S(2)}) collective-permute-start(bf16[4,144,256]{2,1,0:T(8,128)(2,1)S(1)} %slice.19), channel_id=1, source_target_pairs={{0,32},{32,64},{64,96},{96,0},{1,33},{33,65},{65,97},{97,1},{2,34}... | collective-permute-start | bytes 884744 | tf_op jit(solution)/shard_map/store/ppermute | solution.py:660
  85.6 7.6 %collective-permute-start.12 = (bf16[8,144,256]{2,1,0:T(8,128)(2,1)S(1)}, bf16[8,144,256]{2,1,0:T(8,128)(2,1)}, u32[]{:S(2)}, u32[]{:S(2)}) collective-permute-start(bf16[8,144,256]{2,1,0:T(8,128)(2,1)S(1)} %collective-permute-done.4.refs_6_), channel_id=1, source_target_pairs={{0,16},{16,0},{1,17},{17,1},{2,18},{18,2},{3,19},{19,3},{4,20},{20... | collective-permute-start | bytes 1769480 | tf_op jit(solution)/shard_map/store/ppermute | solution.py:668
  85.7 7.6 %collective-permute-start.8 = (bf16[8,144,256]{2,1,0:T(8,128)(2,1)S(1)}, bf16[8,144,256]{2,1,0:T(8,128)(2,1)}, u32[]{:S(2)}, u32[]{:S(2)}) collective-permute-start(bf16[8,144,256]{2,1,0:T(8,128)(2,1)S(1)} %copy-done), channel_id=1, source_target_pairs={{0,16},{16,0},{1,17},{17,1},{2,18},{18,2},{3,19},{19,3},{4,20},{20... | collective-permute-start | bytes 1769480 | tf_op jit(solution)/shard_map/store/ppermute | solution.py:668
  86.2 7.1 %collective-permute-start.9 = (bf16[8,144,256]{2,1,0:T(8,128)(2,1)S(1)}, bf16[8,144,256]{2,1,0:T(8,128)(2,1)}, u32[]{:S(2)}, u32[]{:S(2)}) collective-permute-start(bf16[8,144,256]{2,1,0:T(8,128)(2,1)S(1)} %collective-permute-done.3.refs_3_), channel_id=1, source_target_pairs={{0,16},{16,0},{1,17},{17,1},{2,18},{18,2},{3,19},{19,3},{4,20},{20... | collective-permute-start | bytes 1769480 | tf_op jit(solution)/shard_map/store/ppermute | solution.py:668
  86.3 6.9 %collective-permute-start.10 = (bf16[4,144,256]{2,1,0:T(8,128)(2,1)}, bf16[4,144,256]{2,1,0:T(8,128)(2,1)}, u32[]{:S(2)}, u32[]{:S(2)}) collective-permute-start(bf16[4,144,256]{2,1,0:T(8,128)(2,1)} %collective-permute-done.5.refs_4_), channel_id=1, source_target_pairs={{0,16},{16,0},{1,17},{17,1},{2,18},{18,2},{3,19},{19,3},{4,20},{20... | collective-permute-start | bytes 884744 | tf_op jit(solution)/shard_map/store/ppermute | solution.py:668
  90.3 2.9 %collective-permute-start.11 = (bf16[4,144,256]{2,1,0:T(8,128)(2,1)}, bf16[4,144,256]{2,1,0:T(8,128)(2,1)}, u32[]{:S(2)}, u32[]{:S(2)}) collective-permute-start(bf16[4,144,256]{2,1,0:T(8,128)(2,1)} %collective-permute-done.6.refs_5_), channel_id=1, source_target_pairs={{0,16},{16,0},{1,17},{17,1},{2,18},{18,2},{3,19},{19,3},{4,20},{20... | collective-permute-start | bytes 884744 | tf_op jit(solution)/shard_map/store/ppermute | solution.py:668
  101.8 35.4 %collective-permute-start.15 = (bf16[4,592,128]{2,1,0:T(8,128)(2,1)}, bf16[4,592,128]{2,1,0:T(8,128)(2,1)}, u32[]{:S(2)}, u32[]{:S(2)}) collective-permute-start(bf16[4,592,128]{2,1,0:T(8,128)(2,1)} %get-tuple-element.47.refs_12_), channel_id=1, source_target_pairs={{0,8},{4,12},{8,0},{12,4},{1,9},{5,13},{9,1},{13,5},{2,10},{6,14},... | collective-permute-start | bytes 1818632 | tf_op jit(solution)/shard_map/memory/ppermute | solution.py:680
  112.2 25.6 %copy-start.1 = (bf16[4,592,128]{2,1,0:T(8,128)(2,1)S(1)}, bf16[4,592,128]{2,1,0:T(8,128)(2,1)}, u32[]{:S(2)}) copy-start(bf16[4,592,128]{2,1,0:T(8,128)(2,1)} %get-tuple-element.48.refs_0_) | copy-start | bytes 1818628
  112.2 25.0 %collective-permute-start.17 = (bf16[4,592,128]{2,1,0:T(8,128)(2,1)}, bf16[4,592,128]{2,1,0:T(8,128)(2,1)}, u32[]{:S(2)}, u32[]{:S(2)}) collective-permute-start(bf16[4,592,128]{2,1,0:T(8,128)(2,1)} %get-tuple-element.50._), channel_id=1, source_target_pairs={{0,12},{4,0},{8,4},{12,8},{1,13},{5,1},{9,5},{13,9},{2,14},{6,2},{... | collective-permute-start | bytes 1818632 | tf_op jit(solution)/shard_map/memory/ppermute | solution.py:683
  113.9 23.9 %collective-permute-start.16 = (bf16[4,592,128]{2,1,0:T(8,128)(2,1)}, bf16[4,592,128]{2,1,0:T(8,128)(2,1)}, u32[]{:S(2)}, u32[]{:S(2)}) collective-permute-start(bf16[4,592,128]{2,1,0:T(8,128)(2,1)} %get-tuple-element.49), channel_id=1, source_target_pairs={{0,4},{4,8},{8,12},{12,0},{1,5},{5,9},{9,13},{13,1},{2,6},{6,10},{... | collective-permute-start | bytes 1818632 | tf_op jit(solution)/shard_map/memory/ppermute | solution.py:681
  117.4 27.2 %all-to-all-start.2 = ((bf16[16,144,128]{2,1,0:T(8,128)(2,1)}), bf16[16,144,128]{2,1,0:T(8,128)(2,1)S(1)}, u32[]{:S(2)}, u32[]{:S(2)}) async-start(bf16[16,144,128]{2,1,0:T(8,128)(2,1)} %temporal_attend.1), calls=%async_computation.2 | async-start | bytes 1179648 | tf_op jit(solution)/shard_map/temporal/all_to_all | solution.py:617
  140.6 10.5 %collective-permute-start.18 = (bf16[592,128]{1,0:T(8,128)(2,1)}, bf16[592,128]{1,0:T(8,128)(2,1)S(1)}, u32[]{:S(2)}, u32[]{:S(2)}) collective-permute-start(bf16[592,128]{1,0:T(8,128)(2,1)} %get-tuple-element.52), channel_id=1, source_target_pairs={{0,1},{1,2},{2,3},{3,0},{4,5},{5,6},{6,7},{7,4},{8,9},{9,10},{10,1... | collective-permute-start | bytes 454664 | tf_op jit(solution)/shard_map/memory/ppermute | solution.py:620
  140.7 10.4 %collective-permute-start.19 = (bf16[592,128]{1,0:T(8,128)(2,1)}, bf16[592,128]{1,0:T(8,128)(2,1)S(1)}, u32[]{:S(2)}, u32[]{:S(2)}) collective-permute-start(bf16[592,128]{1,0:T(8,128)(2,1)} %get-tuple-element.53), channel_id=1, source_target_pairs={{0,2},{1,3},{2,0},{3,1},{4,6},{5,7},{6,4},{7,5},{8,10},{9,11},{10,... | collective-permute-start | bytes 454664 | tf_op jit(solution)/shard_map/memory/ppermute | solution.py:620
  143.6 8.2 %collective-permute-start.20 = (bf16[592,128]{1,0:T(8,128)(2,1)}, bf16[592,128]{1,0:T(8,128)(2,1)S(1)}, u32[]{:S(2)}, u32[]{:S(2)}) collective-permute-start(bf16[592,128]{1,0:T(8,128)(2,1)} %get-tuple-element.54), channel_id=1, source_target_pairs={{0,3},{1,0},{2,1},{3,2},{4,7},{5,4},{6,5},{7,6},{8,11},{9,8},{10,9... | collective-permute-start | bytes 454664 | tf_op jit(solution)/shard_map/memory/ppermute | solution.py:620
  151.8 0.9 copy-start.3

commit v8 on v7

--- a/solution.py
+++ b/solution.py
@@ -57,46 +57,41 @@
 copy = pltpu.make_async_copy
 
 
-def split_store_kernel(x_ref, rows_ref, *refs):
-    outs, out_ref, sem = refs[:G], refs[G], refs[G + 1]
+def split_store_kernel(rows_ref, out_hbm, out_ref, sem):
     sends = []
-    for j in range(G):
-        start = lax.rem(x_ref[0] + j, G) * C
-        key = rows_ref[:, pl.ds(pl.multiple_of(start, C), C)].astype(F32)
-        out_ref[j, :, :C] = (key * inverse_rms(key)).astype(BF)
-        out_ref[j, :, C:] = rows_ref[:, pl.ds(pl.multiple_of(HW + start, C), C)]
-        sends.append(copy(out_ref.at[j], outs[j], sem.at[j]))
+    for h in range(G):
+        key = rows_ref[:, h * C : (h + 1) * C].astype(F32)
+        out_ref[h, :, :C] = (key * inverse_rms(key)).astype(BF)
+        out_ref[h, :, C:] = rows_ref[:, HW + h * C : HW + (h + 1) * C]
+        sends.append(copy(out_ref.at[h], out_hbm.at[h], sem.at[h]))
         sends[-1].start()
     for send in sends:
         send.wait()
 
 
-def split_store(x, rows):
+def split_store(rows):
     n = rows.shape[0]
     return pl.pallas_call(
         split_store_kernel,
-        in_specs=[SCALARS, WHOLE],
-        out_specs=[HBM] * G,
-        out_shape=[hbm_out((n, 2 * C))] * G,
+        in_specs=[WHOLE],
+        out_specs=HBM,
+        out_shape=hbm_out((G, n, 2 * C)),
         scratch_shapes=[pltpu.VMEM((G, n, 2 * C), BF), DMA((G,))],
         compiler_params=params(),
         name="split_store",
         cost_estimate=cost(8 * n * HW, 8 * n * HW),
-    )(x, rows)
-
-
-def join_pieces_kernel(pieces, *refs):
-    ins = refs[:pieces]
-    out_hbm, in_ref, wide_ref, joined_ref, out_ref, sem = refs[pieces + 1 :]
-    frames = out_ref.shape[0]
-    piece = in_ref.shape[1] // frames
-    loads = [copy(ins[i], in_ref.at[i], sem.at[i]) for i in range(pieces)]
+    )(rows)
+
+
+def join_pieces_kernel(piece, in_hbm, _, out_hbm, in_ref, wide_ref, joined_ref, out_ref, sem):
+    pieces = in_ref.shape[0]
+    loads = [copy(in_hbm.at[i], in_ref.at[i], sem.at[i]) for i in range(pieces)]
     for load in loads:
         load.start()
     for i in range(pieces):
         loads[i].wait()
         wide_ref[i] = in_ref[i].astype(F32)
-        for m in range(frames):
+        for m in range(out_ref.shape[0]):
             joined_ref[m, i * piece : (i + 1) * piece, :] = wide_ref[
                 i, m * piece : (m + 1) * piece, :
             ]
@@ -107,25 +102,25 @@
 
 
 def join_pieces(parts, frames, after):
-    pieces = len(parts)
-    rows, width = parts[0].shape
-    shape = (frames, pieces * rows // frames, width)
-    return pl.pallas_call(
-        functools.partial(join_pieces_kernel, pieces),
-        in_specs=[ANY] * (pieces + 1),
+    pieces, rows, width = parts.shape
+    piece = rows // frames
+    shape = (frames, pieces * piece, width)
+    return pl.pallas_call(
+        functools.partial(join_pieces_kernel, piece),
+        in_specs=[ANY, ANY],
         out_specs=HBM,
         out_shape=hbm_out(shape),
         scratch_shapes=[
-            pltpu.VMEM((pieces, rows, width), BF),
-            pltpu.VMEM((pieces, rows, width), F32),
+            pltpu.VMEM(parts.shape, BF),
+            pltpu.VMEM(parts.shape, F32),
             pltpu.VMEM(shape, F32),
             pltpu.VMEM(shape, BF),
             DMA((pieces,)),
         ],
         compiler_params=params(),
         name="join_pieces",
-        cost_estimate=cost(pieces * rows * width, 4 * pieces * rows * width),
-    )(*parts, in_hbm(after))
+        cost_estimate=cost(parts.size, 4 * parts.size),
+    )(parts, in_hbm(after))
 
 
 def modulate_kernel(
@@ -320,7 +315,7 @@
     return jnp.concatenate([high, denominators - high], axis=0).astype(BF)
 
 
-def attend_rows(query, keys, both, out_ref):
+def attend_rows(query, keys, both, out_ref, carry=None):
     patches = out_ref.shape[0] - PAD
     row = lax.broadcasted_iota(jnp.int32, (LINE, C), 0)
     column = lax.broadcasted_iota(jnp.int32, (LINE, C), 1)
@@ -329,12 +324,19 @@
         at = slice(start, start + CHUNK)
         weights = jnp.exp(dot_t(query(at), keys)).astype(BF)
         result = dot(weights, both)
-        out_ref[at, :] = result[:, :C].astype(BF)
+        top = result[:, :C]
+        if carry is not None:
+            top = top + carry[at, :].astype(F32)
+        out_ref[at, :] = top.astype(BF)
         for j in range(0, CHUNK, LINE):
             diagonal = jnp.where(row == column, result[j : j + LINE, C:], 0.0)
             lines.append(jnp.sum(diagonal, axis=0, keepdims=True))
     lines.append(jnp.zeros((8 - len(lines), C), F32))
-    out_ref[patches:, :] = halves(jnp.concatenate(lines, axis=0))
+    total = jnp.concatenate(lines, axis=0)
+    if carry is not None:
+        tail = carry[patches:, :].astype(F32)
+        total = total + tail[:8] + tail[8:]
+    out_ref[patches:, :] = halves(total)
 
 
 def with_ones(values):
@@ -342,9 +344,10 @@
 
 
 def own_attend_kernel(
-    hidden_hbm, weight_hbm, query_hbm, _, out_hbm,
-    hidden_ref, weight_ref, query_ref, out_ref, hidden_sem, weight_sem, query_sem, store_sem,
+    hidden_hbm, weight_hbm, query_hbm, *refs
 ):
+    out_hbm, hidden_ref, weight_ref, query_ref, out_ref = refs[-9:-4]
+    hidden_sem, weight_sem, query_sem, store_sem = refs[-4:]
     hidden_load = copy(hidden_hbm, hidden_ref, hidden_sem)
     query_load = copy(query_hbm, query_ref, query_sem)
     loads = [
@@ -379,7 +382,7 @@
     patches, depth = hidden.shape
     return pl.pallas_call(
         own_attend_kernel,
-        in_specs=[HBM, HBM, HBM, ANY],
+        in_specs=[HBM, HBM, HBM] + [ANY] * len(after),
         out_specs=HBM,
         out_shape=hbm_out(query.shape),
         scratch_shapes=[
@@ -398,13 +401,15 @@
             4 * patches * depth * HW + 6 * patches * patches * HW,
             2 * patches * depth + 4 * depth * HW + 10 * patches * HW,
         ),
-    )(in_hbm(hidden), in_hbm(weight), in_hbm(query), in_hbm(after))
-
-
-def memory_attend_kernel(groups, count, index_ref, *refs):
-    queries, blocks = refs[:groups], refs[groups : groups + count]
-    outs = refs[groups + count + 1 : 2 * groups + count + 1]
-    query_ref, store_ref, out_ref, query_sem, block_sem, store_sem = refs[2 * groups + count + 1 :]
+    )(in_hbm(hidden), in_hbm(weight), in_hbm(query), *after)
+
+
+def memory_attend_kernel(groups, count, carried, pieces, index_ref, *refs):
+    queries, refs = refs[:groups], refs[groups:]
+    blocks, refs = refs[:count], refs[count:]
+    carries, refs = refs[: len(carried)], refs[len(carried) + 1 :]
+    outs, refs = refs[: groups * pieces], refs[groups * pieces :]
+    query_ref, store_ref, carry_ref, out_ref, query_sem, block_sem, carry_sem, store_sem = refs
     frames = queries[0].shape[0]
     loads, start = [], 0
     for i, block in enumerate(blocks):
@@ -412,46 +417,57 @@
         loads.append(copy(block, store_ref.at[pl.ds(start, held)], block_sem.at[i]))
         start += held
     query_loads = [copy(queries[k], query_ref.at[k], query_sem.at[k]) for k in range(groups)]
-    for load in query_loads[:1] + loads + query_loads[1:]:
+    carry_loads = [copy(ref, carry_ref.at[i], carry_sem.at[i]) for i, ref in enumerate(carries)]
+    for load in query_loads[:1] + loads + carry_loads + query_loads[1:]:
         load.start()
-    for load in loads:
+    for load in loads + carry_loads:
         load.wait()
     stores = []
+    piece = frames // pieces
     for k in range(groups):
         query_loads[k].wait()
         for i in range(frames):
             chosen = [store_ref[index_ref[k * frames + i, j]] for j in range(TOPM)]
             keys = jnp.concatenate([block[:, :C] for block in chosen], axis=0)
             values = jnp.concatenate([block[:, C:] for block in chosen], axis=0)
+            carry = None
+            for at, (group, first) in enumerate(carried):
+                if group == k and first <= i < first + carries[at].shape[0]:
+                    carry = carry_ref.at[at, i - first]
             attend_rows(
                 lambda at, k=k, i=i: query_ref[k, i, at, :],
                 keys,
                 with_ones(values),
                 out_ref.at[k, i],
+                carry,
             )
-            stores.append(copy(out_ref.at[k, i], outs[k].at[i], store_sem.at[k, i]))
+            out = outs[k * pieces + i // piece].at[i % piece]
+            stores.append(copy(out_ref.at[k, i], out, store_sem.at[k, i]))
             stores[-1].start()
     for store in stores:
         store.wait()
 
 
-def memory_attend(index, queries, blocks, after):
+def memory_attend(index, queries, blocks, after, carries=(), carried=(), pieces=1):
     groups, count = len(queries), len(blocks)
     frames, rows, _ = queries[0].shape
     _, quarter, width = blocks[0].shape
     total = sum(block.shape[0] for block in blocks)
     shape = (groups, frames, rows, C)
-    return pl.pallas_call(
-        functools.partial(memory_attend_kernel, groups, count),
-        in_specs=[SCALARS] + [ANY] * (groups + count + 1),
-        out_specs=[HBM] * groups,
-        out_shape=[hbm_out(shape[1:])] * groups,
+    held = max([1] + [carry.shape[0] for carry in carries])
+    return pl.pallas_call(
+        functools.partial(memory_attend_kernel, groups, count, tuple(carried), pieces),
+        in_specs=[SCALARS] + [ANY] * (groups + count + len(carries) + 1),
+        out_specs=[HBM] * (groups * pieces),
+        out_shape=[hbm_out((frames // pieces, rows, C))] * (groups * pieces),
         scratch_shapes=[
             pltpu.VMEM(shape, BF),
             pltpu.VMEM((total, quarter, width), BF),
+            pltpu.VMEM((max(1, len(carries)), held, rows, C), BF),
             pltpu.VMEM(shape, BF),
             DMA((groups,)),
             DMA((count,)),
+            DMA((max(1, len(carries)),)),
             DMA((groups, frames)),
         ],
         compiler_params=params(),
@@ -460,7 +476,7 @@
             8 * groups * frames * rows * TOPM * quarter * C,
             4 * groups * frames * rows * C + 2 * total * quarter * width,
         ),
-    )(index, *queries, *blocks, in_hbm(after))
+    )(index, *queries, *blocks, *carries, in_hbm(after))
 
 
 def add_partials_kernel(count, x_ref, *refs):
@@ -620,8 +636,8 @@
         return [blocks[0]] + [lax.ppermute(blocks[j], "x", turn(j)) for j in range(1, G)]
 
     with jax.named_scope("store"):
-        split = split_store(x, cached_past_pairs.reshape(held * piece, 2 * HW))
-        pieces = swap_apart(split)
+        split = split_store(cached_past_pairs.reshape(held * piece, 2 * HW))
+        pieces = swap(split, "x")
 
     with jax.named_scope("queries"):
         hidden, query = modulate(
@@ -632,7 +648,7 @@
             recalled_picture_holder.reshape(TOPM),
             recalled_picture_position.reshape(TOPM),
             held,
-            after=split[0],
+            after=split,
         )
         here = swap(query, "x")
 
@@ -648,46 +664,55 @@
         sent = swap(parts.reshape((rings * G,) + parts.shape[2:]), ("z", "x"))
 
     with jax.named_scope("queries"):
-        here, parts = lax.optimization_barrier((here, parts))
         z_above = lax.ppermute(here, "z", turn(-1))
         z_below = lax.ppermute(here, "z", turn(1))
+
+    with jax.named_scope("own"):
+        own = own_attend(
+            hidden,
+            entry_projection_matrix,
+            query,
+            after=[parts, above, below, z_above, z_below],
+        )
+
+    with jax.named_scope("queries"):
         z_far = lax.ppermute(z_below, "z", turn(1))
-        groups = [here, z_above, z_far, z_below]
 
     with jax.named_scope("store"):
-        above, below, parts = lax.optimization_barrier((above, below, parts))
         far_first = lax.ppermute(above[: held // 2], "y", turn(-1))
         far_last = lax.ppermute(below[held // 2 :], "y", turn(1))
-
-    with jax.named_scope("own"):
-        own = own_attend(hidden, entry_projection_matrix, query, after=parts)
-
-    with jax.named_scope("store"):
         near = [joined, above, far_first, far_last, below]
         *near, own = lax.optimization_barrier((*near, own))
         blocks = near + [lax.ppermute(block, "c", other) for block in near]
 
-    def attend(queries, after):
+    def attend(queries, after, **more):
         named = jnp.concatenate([group[:, patches, :TOPM] for group in queries], axis=0)
         named = named.astype(jnp.int32)
         y = (named // (cores * held) - lax.axis_index("y")) & (rolls_y - 1)
         c = (named // held & (cores - 1)) ^ lax.axis_index("c")
         index = (c * rolls_y + y) * held + (named & (held - 1))
-        return memory_attend(index, queries, blocks, after)
+        return memory_attend(index, queries, blocks, after, **more)
 
     with jax.named_scope("memory"):
-        sum_far, sum_above = attend([groups[2], groups[1]], own)
-        from_far = lax.ppermute(sum_far, "z", turn(2))
+        sum_first, sum_last = attend([z_far], own, pieces=2)
+        carry_first = lax.ppermute(sum_first, "z", turn(-1))
+        carry_last = lax.ppermute(sum_last, "z", turn(1))
+        (sum_here,) = attend([here], sum_first)
+        sum_below, sum_above = attend(
+            [z_below, z_above],
+            sum_here,
+            carries=[carry_first, carry_last],
+            carried=[(0, 0), (1, here.shape[0] // 2)],
+        )
+        from_above = lax.ppermute(sum_below, "z", turn(-1))
         from_below = lax.ppermute(sum_above, "z", turn(1))
-        sum_below, sum_here = attend([groups[3], here], sum_far)
-        from_above = lax.ppermute(sum_below, "z", turn(3))
 
     with jax.named_scope("temporal"):
         timed = temporal_attend(lookback_lengths, sent, after=sum_below)
         time = swap(timed, ("z", "x"))
 
     with jax.named_scope("memory"):
-        memory = swap_apart(add_partials(x, [sum_here, from_far, from_below, from_above]))
+        memory = swap_apart(add_partials(x, [sum_here, from_below, from_above]))
 
     with jax.named_scope("exit"):
         attended = leave(x, own, memory, time, exit_projection_matrix)

time: 160 us -> 159 us (level)
  waiting for transfers between devices: 55.9 us -> 40.9 us
  blocking collectives: 0 us -> 14.9 us
  starting transfers between devices: 41.6 us -> 39.3 us
  Pallas kernels: 53.5 us -> 55.5 us
  local copies, waits for them, and re-layouts: 6.94 us -> 5.03 us
    ppermute x1, waiting for transfers between devices: 19 us -> 0.01 us  [on_device(): z_below = lax.ppermute(here, 'z', turn(1))]
    all_to_all x0 -> x1, blocking collectives: none -> 14.9 us  [swap(): return lax.all_to_all(blocks, axes, split_axis=0, concat_axis=0, tiled=True)]
    ppermute x6 -> x3, waiting for transfers between devices: 17.7 us -> 3.97 us  [swap_apart(): lax.ppermute(blocks[j], 'x', turn(j))]
    ppermute x1, waiting for transfers between devices: 3.63 us -> 16.3 us  [on_device(): z_far = lax.ppermute(z_below, 'z', turn(1))]
    ppermute x2 -> x3, waiting for transfers between devices: 14.9 us -> 2.82 us  [the longest x1 1.8 us: on_device(): carry_last = lax.ppermute(sum_last, 'z', turn(1))]
    ppermute x1, waiting for transfers between devices: 0.59 us -> 9.8 us  [on_device(): from_below = lax.ppermute(sum_above, 'z', turn(1))]
    all_to_all x3, waiting for transfers between devices: 0.01 us -> 7.15 us  [swap(): return lax.all_to_all(blocks, axes, split_axis=0, concat_axis=0, tiled=True)]
    ppermute x6 -> x3, starting transfers between devices: 10.1 us -> 6 us  [swap_apart(): lax.ppermute(blocks[j], 'x', turn(j))]
  transfers between devices with their start and end apart: 24 -> 22, of which waited for: 8 -> 9; matrix products, arithmetic and copies ran while one was open for 2% -> 3% of each run, Pallas kernels for 26% -> 27%
where the time goes in v8:
time: 159 us; the launch traced here: 158 us
  Pallas kernels  55.5 us (35%)
  waiting for transfers between devices  40.9 us (26%)
  starting transfers between devices  39.3 us (25%)
  blocking collectives  14.9 us (9%)
  local copies, waits for them, and re-layouts  5.03 us (3%)
    pallas_call x3, Pallas kernels, memory_attend(): pl.pallas_call(functools.partial(memory_attend_kernel, groups, count, tup...  17.4 us
    ppermute x1, waiting for transfers between devices, on_device(): z_far = lax.ppermute(z_below, 'z', turn(1))  16.3 us
    all_to_all x1, blocking collectives, swap(): return lax.all_to_all(blocks, axes, split_axis=0, concat_axis=0, tiled=True)  14.9 us
    all_to_all x3, starting transfers between devices, swap(): return lax.all_to_all(blocks, axes, split_axis=0, concat_axis=0, tiled=True)  12.3 us
    ppermute x1, waiting for transfers between devices, on_device(): from_below = lax.ppermute(sum_above, 'z', turn(1))  9.8 us
    pallas_call x1, Pallas kernels, temporal_entry(): pl.pallas_call(functools.partial(temporal_entry_kernel, quarters), in_spe...  8.54 us
    pallas_call x1, Pallas kernels, own_attend(): pl.pallas_call(own_attend_kernel, in_specs=[HBM, HBM, HBM] + [ANY] * len(...  8.13 us
    all_to_all x3, waiting for transfers between devices, swap(): return lax.all_to_all(blocks, axes, split_axis=0, concat_axis=0, tiled=True)  7.15 us
  transfers between devices with their start and end apart: 22, of which 9 were waited for; matrix products, arithmetic and copies ran while one was open for 3% of the time, Pallas kernels for 27%

profile of v8, /device:TPU:0, one launch (start us, length us, event | category | flops | bytes accessed | tf_op | source)
XLA Modules:
  0.0 158.2 jit_solution(14741956556402976854)
XLA Ops:
  0.0 1.2 copy.12
  1.2 1.0 split_store.1._
  2.2 5.6 %modulate.1 = (bf16[576,2048]{1,0:T(8,128)(2,1)}, bf16[4,592,128]{2,1,0:T(8,128)(2,1)}) custom-call(bf16[576,2048]{1,0:T(8,128)(2,1)} %bitcast.22, f32[2,2048]{1,0:T(2,128)} %bitcast.24, bf16[2048,3072]{1,0:T(8,128)(2,1)} %weight_hbm.6, f32[2,4]{1,0:T(2,128)S(1)} %copy-done.4, s32[6]{0:T(128)S(1)} %bitcast.20, s32[6]{0:T(128)S(1)} %bitcast.21, ...), custom_call_target="tpu_custom_call" | custom-call | flops 75497472 | bytes 462848 | tf_op jit(solution)/shard_map/queries/modulate/pallas_call | solution.py:182
  7.8 14.9 %all_to_all.20.refs_0_ = bf16[4,592,128]{2,1,0:T(8,128)(2,1)} all-to-all(bf16[4,592,128]{2,1,0:T(8,128)(2,1)} %get-tuple-element.22.query_hbm), channel_id=1, replica_groups=mesh['y'=4,'c'=2,'z'=4,'x'=4] {'x'}, dimensions={0} | all-to-all | bytes 1212416 | tf_op jit(solution)/shard_map/queries/all_to_all | solution.py:633
  22.7 3.5 %all-to-all-start = ((bf16[4,288,256]{2,1,0:T(8,128)(2,1)}), bf16[4,288,256]{2,1,0:T(8,128)(2,1)S(1)}, u32[]{:S(2)}, u32[]{:S(2)}) async-start(bf16[4,288,256]{2,1,0:T(8,128)(2,1)} %split_store.1._), calls=%async_computation | async-start | bytes 1179648 | tf_op jit(solution)/shard_map/store/all_to_all | solution.py:633
  26.2 2.1 %collective-permute-start.5 = (bf16[4,592,128]{2,1,0:T(8,128)(2,1)}, bf16[4,592,128]{2,1,0:T(8,128)(2,1)}, u32[]{:S(2)}, u32[]{:S(2)}) collective-permute-start(bf16[4,592,128]{2,1,0:T(8,128)(2,1)} %all_to_all.20.refs_0_), channel_id=1, source_target_pairs={{0,4},{4,8},{8,12},{12,0},{1,5},{5,9},{9,13},{13,1},{2,6},{6,10},{... | collective-permute-start | bytes 1818632 | tf_op jit(solution)/shard_map/queries/ppermute | solution.py:668
  28.3 7.1 %all-to-all-done.in_hbm = bf16[4,288,256]{2,1,0:T(8,128)(2,1)S(1)} async-done(((bf16[4,288,256]{2,1,0:T(8,128)(2,1)}), bf16[4,288,256]{2,1,0:T(8,128)(2,1)S(1)}, u32[]{:S(2)}, u32[]{:S(2)}) %all-to-all-start) | async-done | bytes 589856 | tf_op jit(solution)/shard_map/store/all_to_all | solution.py:633
  35.4 1.7 %join_pieces.1._.refs_1_.refs_2_ = bf16[8,144,256]{2,1,0:T(8,128)(2,1)} custom-call(bf16[4,288,256]{2,1,0:T(8,128)(2,1)S(1)} %all-to-all-done.in_hbm, bf16[576,2048]{1,0:T(8,128)(2,1)} %get-tuple-element.21._.hidden_hbm), custom_call_target="tpu_custom_call" | custom-call | flops 18432 | bytes 73728 | tf_op jit(solution)/shard_map/store/join_pieces/pallas_call | solution.py:108
  37.2 3.3 %collective-permute-start = (bf16[8,144,256]{2,1,0:T(8,128)(2,1)}, bf16[8,144,256]{2,1,0:T(8,128)(2,1)S(1)}, u32[]{:S(2)}, u32[]{:S(2)}) collective-permute-start(bf16[8,144,256]{2,1,0:T(8,128)(2,1)} %join_pieces.1._.refs_1_.refs_2_), channel_id=1, source_target_pairs={{0,96},{32,0},{64,32},{96,64},{1,97},{33,1},{65,33},{97,65},{2,98}... | collective-permute-start | bytes 1769480 | tf_op jit(solution)/shard_map/store/ppermute | solution.py:657
  40.5 0.0 collective-permute-start.2
  40.5 4.0 %collective-permute-start.4 = (bf16[4,592,128]{2,1,0:T(8,128)(2,1)}, bf16[4,592,128]{2,1,0:T(8,128)(2,1)}, u32[]{:S(2)}, u32[]{:S(2)}) collective-permute-start(bf16[4,592,128]{2,1,0:T(8,128)(2,1)} %all_to_all.20.refs_0_), channel_id=1, source_target_pairs={{0,12},{4,0},{8,4},{12,8},{1,13},{5,1},{9,5},{13,9},{2,14},{6,2},{... | collective-permute-start | bytes 1818632 | tf_op jit(solution)/shard_map/queries/ppermute | solution.py:667
  44.5 8.5 %temporal_entry.1.refs_0_ = bf16[4,4,3,144,128]{4,3,2,1,0:T(8,128)(2,1)} custom-call(bf16[576,2048]{1,0:T(8,128)(2,1)} %get-tuple-element.21._.hidden_hbm, bf16[2048,3072]{1,0:T(8,128)(2,1)} %weight_hbm.6, f32[2,4]{1,0:T(2,128)S(1)} %copy-done.4, bf16[8,144,256]{2,1,0:T(8,128)(2,1)} %join_pieces.1._.refs_1_.refs_2_), custom_call_target="tpu_custom_call" | custom-call | flops 226492416 | bytes 651264 | tf_op jit(solution)/shard_map/temporal/temporal_entry/pallas_call | solution.py:247
  53.1 4.6 %all-to-all-start.2 = ((bf16[16,3,144,128]{3,2,1,0:T(8,128)(2,1)}), bf16[16,3,144,128]{3,2,1,0:T(8,128)(2,1)}, u32[]{:S(2)}, u32[]{:S(2)}) async-start(bf16[16,3,144,128]{3,2,1,0:T(8,128)(2,1)} %bitcast.18), calls=%async_computation.2 | async-start | bytes 3538944 | tf_op jit(solution)/shard_map/temporal/all_to_all | solution.py:633
  57.6 0.0 collective-permute-done.5.refs_4_.refs_0_
  57.6 1.8 %collective-permute-start.11 = (bf16[4,592,128]{2,1,0:T(8,128)(2,1)}, bf16[4,592,128]{2,1,0:T(8,128)(2,1)}, u32[]{:S(2)}, u32[]{:S(2)}) collective-permute-start(bf16[4,592,128]{2,1,0:T(8,128)(2,1)} %collective-permute-done.5.refs_4_.refs_0_), channel_id=1, source_target_pairs={{0,4},{4,8},{8,12},{12,0},{1,5},{5,9},{9,13},{13,1},{2,6},{6,10},{... | collective-permute-start | bytes 1818632 | tf_op jit(solution)/shard_map/queries/ppermute | solution.py:679
  59.5 0.0 collective-permute-done.refs_1_.refs_2_.refs_3_
  59.5 0.8 slice.24
  60.2 3.2 %collective-permute-start.1 = (bf16[4,144,256]{2,1,0:T(8,128)(2,1)}, bf16[4,144,256]{2,1,0:T(8,128)(2,1)S(1)}, u32[]{:S(2)}, u32[]{:S(2)}) collective-permute-start(bf16[4,144,256]{2,1,0:T(8,128)(2,1)} %slice.24), channel_id=1, source_target_pairs={{0,96},{32,0},{64,32},{96,64},{1,97},{33,1},{65,33},{97,65},{2,98}... | collective-permute-start | bytes 884744 | tf_op jit(solution)/shard_map/store/ppermute | solution.py:682
  63.5 0.0 collective-permute-done.2.refs_2_.refs_5_.refs_6_
  63.5 0.7 slice.25
  64.2 0.0 collective-permute-start.3
  64.2 0.0 collective-permute-done.4.refs_3_.refs_1_
  64.2 8.1 %own_attend.1.refs_11_.own_hbm = bf16[4,592,128]{2,1,0:T(8,128)(2,1)} custom-call(bf16[576,2048]{1,0:T(8,128)(2,1)} %get-tuple-element.21._.hidden_hbm, bf16[2048,3072]{1,0:T(8,128)(2,1)} %weight_hbm.6, bf16[4,592,128]{2,1,0:T(8,128)(2,1)} %get-tuple-element.22.query_hbm, bf16[4,4,3,144,128]{4,3,2,1,0:T(8,128)(2,1)S(1)} %copy-done, ...), custom_call_target="tpu_custom_call" | custom-call | flops 214695936 | bytes 593920 | tf_op jit(solution)/shard_map/own/own_attend/pallas_call | solution.py:383
  72.4 0.0 collective-permute-done.1.refs_3_.refs_4_
  72.4 0.0 collective-permute-done.3.refs_4_.refs_5_
  72.4 0.1 collective-permute-start.10
  72.5 0.5 collective-permute-start.6
  73.0 0.1 collective-permute-start.7
  73.1 0.7 slice_convert_fusion.1
  73.8 0.4 collective-permute-start.8
  74.2 16.3 %collective-permute-done.11.refs_0_ = bf16[4,592,128]{2,1,0:T(8,128)(2,1)} collective-permute-done((bf16[4,592,128]{2,1,0:T(8,128)(2,1)}, bf16[4,592,128]{2,1,0:T(8,128)(2,1)}, u32[]{:S(2)}, u32[]{:S(2)}) %collective-permute-start.11) | collective-permute-done | bytes 606240 | tf_op jit(solution)/shard_map/queries/ppermute | solution.py:679
  90.5 0.0 collective-permute-start.9
  90.5 0.7 slice_convert_fusion
  91.2 0.0 collective-permute-done.8.refs_8_.refs_9_
  91.2 0.8 collective-permute-done.9.refs_9_.refs_10_
  92.1 0.0 collective-permute-done.10.refs_10_.refs_11_
  92.1 0.0 collective-permute-done.6.refs_6_.refs_7_
  92.1 0.0 collective-permute-done.7.refs_7_.refs_8_
  92.1 4.9 %memory_attend.3 = (bf16[2,592,128]{2,1,0:T(8,128)(2,1)}, bf16[2,592,128]{2,1,0:T(8,128)(2,1)}) custom-call(s32[4,6]{1,0:T(4,128)S(1)} %fusion.33.index_ref, bf16[4,592,128]{2,1,0:T(8,128)(2,1)} %collective-permute-done.11.refs_0_, bf16[8,144,256]{2,1,0:T(8,128)(2,1)S(1)} %copy-done.1, bf16[8,144,256]{2,1,0:T(8,128)(2,1)S(1)} %collective-permute-done.refs_1_.refs_2_.refs_3_, ...), custom_call_target="tpu_custom_call" | custom-call | flops 130940928 | bytes 370688 | tf_op jit(solution)/shard_map/memory/memory_attend/pallas_call | solution.py:458
  97.0 0.9 collective-permute-start.12
  98.0 1.2 collective-permute-start.13
  99.1 0.7 slice.28
  99.8 0.7 slice.29
  100.6 4.9 %memory_attend.4.refs_14_.refs_0_ = bf16[4,592,128]{2,1,0:T(8,128)(2,1)} custom-call(s32[4,6]{1,0:T(4,128)S(1)} %fusion.23.index_ref, bf16[4,592,128]{2,1,0:T(8,128)(2,1)} %all_to_all.20.refs_0_, bf16[8,144,256]{2,1,0:T(8,128)(2,1)S(1)} %copy-done.1, bf16[8,144,256]{2,1,0:T(8,128)(2,1)S(1)} %collective-permute-done.refs_1_.refs_2_.refs_3_, ...), custom_call_target="tpu_custom_call" | custom-call | flops 130940928 | bytes 370688 | tf_op jit(solution)/shard_map/memory/memory_attend/pallas_call | solution.py:458
  105.5 1.0 collective-permute-done.12.refs_12_
  106.5 1.8 %collective-permute-done.13.refs_13_ = bf16[2,592,128]{2,1,0:T(8,128)(2,1)S(1)} collective-permute-done((bf16[2,592,128]{2,1,0:T(8,128)(2,1)}, bf16[2,592,128]{2,1,0:T(8,128)(2,1)S(1)}, u32[]{:S(2)}, u32[]{:S(2)}) %collective-permute-start.13) | collective-permute-done | bytes 303136 | tf_op jit(solution)/shard_map/memory/ppermute | solution.py:699
  108.3 7.5 %memory_attend.5 = (bf16[4,592,128]{2,1,0:T(8,128)(2,1)}, bf16[4,592,128]{2,1,0:T(8,128)(2,1)}) custom-call(s32[8,6]{1,0:T(8,128)S(1)} %fusion.10.index_ref, bf16[4,592,128]{2,1,0:T(8,128)(2,1)} %collective-permute-done.5.refs_4_.refs_0_, bf16[4,592,128]{2,1,0:T(8,128)(2,1)} %collective-permute-done.4.refs_3_.refs_1_, bf16[8,144,256]{2,1,0:T(8,128)(2,1)S(1)} %copy-done.1, ...), custom_call_target="tpu_custom_call" | custom-call | flops 261881856 | bytes 446464 | tf_op jit(solution)/shard_map/memory/memory_attend/pallas_call | solution.py:458
  115.9 0.0 copy-start.2
  115.9 0.1 collective-permute-start.14
  116.0 3.2 %collective-permute-start.15 = (bf16[4,592,128]{2,1,0:T(8,128)(2,1)}, bf16[4,592,128]{2,1,0:T(8,128)(2,1)S(1)}, u32[]{:S(2)}, u32[]{:S(2)}) collective-permute-start(bf16[4,592,128]{2,1,0:T(8,128)(2,1)} %get-tuple-element.32._), channel_id=1, source_target_pairs={{0,12},{4,0},{8,4},{12,8},{1,13},{5,1},{9,5},{13,9},{2,14},{6,2},{... | collective-permute-start | bytes 1818632 | tf_op jit(solution)/shard_map/memory/ppermute | solution.py:707
  119.9 3.5 %temporal_attend.1 = bf16[16,144,128]{2,1,0:T(8,128)(2,1)} custom-call(s32[1]{0:T(128)S(6)} %copy.17.length_ref, bf16[16,3,144,128]{3,2,1,0:T(8,128)(2,1)} %all-to-all-done.2.in_hbm_ref, bf16[4,592,128]{2,1,0:T(8,128)(2,1)} %get-tuple-element.32._), custom_call_target="tpu_custom_call" | custom-call | flops 18874368 | bytes 147456 | tf_op jit(solution)/shard_map/temporal/temporal_attend/pallas_call | solution.py:297
  123.4 4.3 %all-to-all-start.3 = ((bf16[16,144,128]{2,1,0:T(8,128)(2,1)}), bf16[16,144,128]{2,1,0:T(8,128)(2,1)S(1)}, u32[]{:S(2)}, u32[]{:S(2)}) async-start(bf16[16,144,128]{2,1,0:T(8,128)(2,1)} %temporal_attend.1), calls=%async_computation.3 | async-start | bytes 1179648 | tf_op jit(solution)/shard_map/temporal/all_to_all | solution.py:633
  127.7 9.8 %collective-permute-done.14.refs_1_ = bf16[4,592,128]{2,1,0:T(8,128)(2,1)S(1)} collective-permute-done((bf16[4,592,128]{2,1,0:T(8,128)(2,1)}, bf16[4,592,128]{2,1,0:T(8,128)(2,1)S(1)}, u32[]{:S(2)}, u32[]{:S(2)}) %collective-permute-start.14) | collective-permute-done | bytes 606240 | tf_op jit(solution)/shard_map/memory/ppermute | solution.py:708
  137.5 0.0 collective-permute-done.15.refs_2_
  137.5 3.4 %add_partials.1 = (bf16[592,128]{1,0:T(8,128)(2,1)}, bf16[592,128]{1,0:T(8,128)(2,1)}, bf16[592,128]{1,0:T(8,128)(2,1)}, bf16[592,128]{1,0:T(8,128)(2,1)}) custom-call(s32[1]{0:T(128)} %bitcast.x_ref, bf16[4,592,128]{2,1,0:T(8,128)(2,1)S(1)} %copy-done.2, bf16[4,592,128]{2,1,0:T(8,128)(2,1)S(1)} %collective-permute-done.14.refs_1_, ...), custom_call_target="tpu_custom_call" | custom-call | flops 75776 | bytes 151552 | tf_op jit(solution)/shard_map/memory/add_partials/pallas_call | solution.py:512
  140.9 1.9 %collective-permute-start.16 = (bf16[592,128]{1,0:T(8,128)(2,1)}, bf16[592,128]{1,0:T(8,128)(2,1)S(1)}, u32[]{:S(2)}, u32[]{:S(2)}) collective-permute-start(bf16[592,128]{1,0:T(8,128)(2,1)} %get-tuple-element.34), channel_id=1, source_target_pairs={{0,1},{1,2},{2,3},{3,0},{4,5},{5,6},{6,7},{7,4},{8,9},{9,10},{10,1... | collective-permute-start | bytes 454664 | tf_op jit(solution)/shard_map/memory/ppermute | solution.py:636
  142.8 2.7 %collective-permute-start.17 = (bf16[592,128]{1,0:T(8,128)(2,1)}, bf16[592,128]{1,0:T(8,128)(2,1)S(1)}, u32[]{:S(2)}, u32[]{:S(2)}) collective-permute-start(bf16[592,128]{1,0:T(8,128)(2,1)} %get-tuple-element.35), channel_id=1, source_target_pairs={{0,2},{1,3},{2,0},{3,1},{4,6},{5,7},{6,4},{7,5},{8,10},{9,11},{10,... | collective-permute-start | bytes 454664 | tf_op jit(solution)/shard_map/memory/ppermute | solution.py:636
  145.5 1.4 collective-permute-start.18
  146.9 0.0 all-to-all-done.3.time_hbm
  146.9 0.7 collective-permute-done.16.memory_1
  147.6 2.9 %collective-permute-done.17.memory_2 = bf16[592,128]{1,0:T(8,128)(2,1)S(1)} collective-permute-done((bf16[592,128]{1,0:T(8,128)(2,1)}, bf16[592,128]{1,0:T(8,128)(2,1)S(1)}, u32[]{:S(2)}, u32[]{:S(2)}) %collective-permute-start.17) | collective-permute-done | bytes 151584 | tf_op jit(solution)/shard_map/memory/ppermute | solution.py:636
  150.5 0.4 collective-permute-done.18.memory_3
  150.9 0.9 copy-done.3
  151.8 6.2 %leave.1 = bf16[576,2048]{1,0:T(8,128)(2,1)} custom-call(s32[1]{0:T(128)} %bitcast.x_ref, bf16[4,592,128]{2,1,0:T(8,128)(2,1)} %own_attend.1.refs_11_.own_hbm, bf16[592,128]{1,0:T(8,128)(2,1)S(1)} %copy-done.3, bf16[592,128]{1,0:T(8,128)(2,1)S(1)} %collective-permute-done.16.memory_1, bf16[592,128]{1,0:T(8,128)(2,1)S(1)} %collective-permute-done.17.memory_2, ...), custom_call_target="tpu_custom_call" | custom-call | flops 150994944 | bytes 630784 | tf_op jit(solution)/shard_map/exit/leave/pallas_call | solution.py:583
  (18 shorter events, 0.1 us)
Async XLA Ops:
  0.0 2.2 %copy-start.5 = (s32[1,1,6,1]{2,3,1,0:T(1,128)S(1)}, s32[1,1,6,1]{2,3,1,0:T(1,128)}, u32[]{:S(2)}) copy-start(s32[1,1,6,1]{2,3,1,0:T(1,128)} %param.15) | copy-start | bytes 76
  0.0 2.2 %copy-start.6 = (s32[1,1,6]{2,1,0:T(1,128)S(1)}, s32[1,1,6]{2,1,0:T(1,128)}, u32[]{:S(2)}) copy-start(s32[1,1,6]{2,1,0:T(1,128)} %param.16) | copy-start | bytes 76
  0.0 2.2 %copy-start.4 = (f32[2,4]{1,0:T(2,128)S(1)}, f32[2,4]{1,0:T(2,128)}, u32[]{:S(2)}) copy-start(f32[2,4]{1,0:T(2,128)} %sharpness_ref.3) | copy-start | bytes 100
  22.7 12.7 %all-to-all-start = ((bf16[4,288,256]{2,1,0:T(8,128)(2,1)}), bf16[4,288,256]{2,1,0:T(8,128)(2,1)S(1)}, u32[]{:S(2)}, u32[]{:S(2)}) async-start(bf16[4,288,256]{2,1,0:T(8,128)(2,1)} %split_store.1._), calls=%async_computation | async-start | bytes 1179648 | tf_op jit(solution)/shard_map/store/all_to_all | solution.py:633
  26.2 31.5 %collective-permute-start.5 = (bf16[4,592,128]{2,1,0:T(8,128)(2,1)}, bf16[4,592,128]{2,1,0:T(8,128)(2,1)}, u32[]{:S(2)}, u32[]{:S(2)}) collective-permute-start(bf16[4,592,128]{2,1,0:T(8,128)(2,1)} %all_to_all.20.refs_0_), channel_id=1, source_target_pairs={{0,4},{4,8},{8,12},{12,0},{1,5},{5,9},{9,13},{13,1},{2,6},{6,10},{... | collective-permute-start | bytes 1818632 | tf_op jit(solution)/shard_map/queries/ppermute | solution.py:668
  37.2 22.3 %collective-permute-start = (bf16[8,144,256]{2,1,0:T(8,128)(2,1)}, bf16[8,144,256]{2,1,0:T(8,128)(2,1)S(1)}, u32[]{:S(2)}, u32[]{:S(2)}) collective-permute-start(bf16[8,144,256]{2,1,0:T(8,128)(2,1)} %join_pieces.1._.refs_1_.refs_2_), channel_id=1, source_target_pairs={{0,96},{32,0},{64,32},{96,64},{1,97},{33,1},{65,33},{97,65},{2,98}... | collective-permute-start | bytes 1769480 | tf_op jit(solution)/shard_map/store/ppermute | solution.py:657
  40.5 23.0 %collective-permute-start.2 = (bf16[8,144,256]{2,1,0:T(8,128)(2,1)}, bf16[8,144,256]{2,1,0:T(8,128)(2,1)S(1)}, u32[]{:S(2)}, u32[]{:S(2)}) collective-permute-start(bf16[8,144,256]{2,1,0:T(8,128)(2,1)} %join_pieces.1._.refs_1_.refs_2_), channel_id=1, source_target_pairs={{0,32},{32,64},{64,96},{96,0},{1,33},{33,65},{65,97},{97,1},{2,34}... | collective-permute-start | bytes 1769480 | tf_op jit(solution)/shard_map/store/ppermute | solution.py:658
  40.5 23.7 %collective-permute-start.4 = (bf16[4,592,128]{2,1,0:T(8,128)(2,1)}, bf16[4,592,128]{2,1,0:T(8,128)(2,1)}, u32[]{:S(2)}, u32[]{:S(2)}) collective-permute-start(bf16[4,592,128]{2,1,0:T(8,128)(2,1)} %all_to_all.20.refs_0_), channel_id=1, source_target_pairs={{0,12},{4,0},{8,4},{12,8},{1,13},{5,1},{9,5},{13,9},{2,14},{6,2},{... | collective-permute-start | bytes 1818632 | tf_op jit(solution)/shard_map/queries/ppermute | solution.py:667
  53.0 11.2 %copy-start = (bf16[4,4,3,144,128]{4,3,2,1,0:T(8,128)(2,1)S(1)}, bf16[4,4,3,144,128]{4,3,2,1,0:T(8,128)(2,1)}, u32[]{:S(2)}) copy-start(bf16[4,4,3,144,128]{4,3,2,1,0:T(8,128)(2,1)} %temporal_entry.1.refs_0_) | copy-start | bytes 5308420
  53.1 66.8 %all-to-all-start.2 = ((bf16[16,3,144,128]{3,2,1,0:T(8,128)(2,1)}), bf16[16,3,144,128]{3,2,1,0:T(8,128)(2,1)}, u32[]{:S(2)}, u32[]{:S(2)}) async-start(bf16[16,3,144,128]{3,2,1,0:T(8,128)(2,1)} %bitcast.18), calls=%async_computation.2 | async-start | bytes 3538944 | tf_op jit(solution)/shard_map/temporal/all_to_all | solution.py:633
  57.6 32.8 %collective-permute-start.11 = (bf16[4,592,128]{2,1,0:T(8,128)(2,1)}, bf16[4,592,128]{2,1,0:T(8,128)(2,1)}, u32[]{:S(2)}, u32[]{:S(2)}) collective-permute-start(bf16[4,592,128]{2,1,0:T(8,128)(2,1)} %collective-permute-done.5.refs_4_.refs_0_), channel_id=1, source_target_pairs={{0,4},{4,8},{8,12},{12,0},{1,5},{5,9},{9,13},{13,1},{2,6},{6,10},{... | collective-permute-start | bytes 1818632 | tf_op jit(solution)/shard_map/queries/ppermute | solution.py:679
  60.2 12.1 %collective-permute-start.1 = (bf16[4,144,256]{2,1,0:T(8,128)(2,1)}, bf16[4,144,256]{2,1,0:T(8,128)(2,1)S(1)}, u32[]{:S(2)}, u32[]{:S(2)}) collective-permute-start(bf16[4,144,256]{2,1,0:T(8,128)(2,1)} %slice.24), channel_id=1, source_target_pairs={{0,96},{32,0},{64,32},{96,64},{1,97},{33,1},{65,33},{97,65},{2,98}... | collective-permute-start | bytes 884744 | tf_op jit(solution)/shard_map/store/ppermute | solution.py:682
  64.2 8.2 %collective-permute-start.3 = (bf16[4,144,256]{2,1,0:T(8,128)(2,1)}, bf16[4,144,256]{2,1,0:T(8,128)(2,1)S(1)}, u32[]{:S(2)}, u32[]{:S(2)}) collective-permute-start(bf16[4,144,256]{2,1,0:T(8,128)(2,1)} %slice.25), channel_id=1, source_target_pairs={{0,32},{32,64},{64,96},{96,0},{1,33},{33,65},{65,97},{97,1},{2,34}... | collective-permute-start | bytes 884744 | tf_op jit(solution)/shard_map/store/ppermute | solution.py:683
  64.2 8.3 %copy-start.1 = (bf16[8,144,256]{2,1,0:T(8,128)(2,1)S(1)}, bf16[8,144,256]{2,1,0:T(8,128)(2,1)}, u32[]{:S(2)}) copy-start(bf16[8,144,256]{2,1,0:T(8,128)(2,1)} %join_pieces.1._.refs_1_.refs_2_) | copy-start | bytes 1769476
  72.4 19.7 %collective-permute-start.10 = (bf16[8,144,256]{2,1,0:T(8,128)(2,1)S(1)}, bf16[8,144,256]{2,1,0:T(8,128)(2,1)S(1)}, u32[]{:S(2)}, u32[]{:S(2)}) collective-permute-start(bf16[8,144,256]{2,1,0:T(8,128)(2,1)S(1)} %collective-permute-done.2.refs_2_.refs_5_.refs_6_), channel_id=1, source_target_pairs={{0,16},{16,0},{1,17},{17,1},{2,18},{18,2},{3,19},{19,3},{4,20},{20... | collective-permute-start | bytes 1769480 | tf_op jit(solution)/shard_map/store/ppermute | solution.py:686
  72.5 19.6 %collective-permute-start.6 = (bf16[8,144,256]{2,1,0:T(8,128)(2,1)S(1)}, bf16[8,144,256]{2,1,0:T(8,128)(2,1)S(1)}, u32[]{:S(2)}, u32[]{:S(2)}) collective-permute-start(bf16[8,144,256]{2,1,0:T(8,128)(2,1)S(1)} %copy-done.1), channel_id=1, source_target_pairs={{0,16},{16,0},{1,17},{17,1},{2,18},{18,2},{3,19},{19,3},{4,20},{20... | collective-permute-start | bytes 1769480 | tf_op jit(solution)/shard_map/store/ppermute | solution.py:686
  73.0 19.1 %collective-permute-start.7 = (bf16[8,144,256]{2,1,0:T(8,128)(2,1)S(1)}, bf16[8,144,256]{2,1,0:T(8,128)(2,1)S(1)}, u32[]{:S(2)}, u32[]{:S(2)}) collective-permute-start(bf16[8,144,256]{2,1,0:T(8,128)(2,1)S(1)} %collective-permute-done.refs_1_.refs_2_.refs_3_), channel_id=1, source_target_pairs={{0,16},{16,0},{1,17},{17,1},{2,18},{18,2},{3,19},{19,3},{4,20},{20... | collective-permute-start | bytes 1769480 | tf_op jit(solution)/shard_map/store/ppermute | solution.py:686
  73.8 17.4 %collective-permute-start.8 = (bf16[4,144,256]{2,1,0:T(8,128)(2,1)S(1)}, bf16[4,144,256]{2,1,0:T(8,128)(2,1)S(1)}, u32[]{:S(2)}, u32[]{:S(2)}) collective-permute-start(bf16[4,144,256]{2,1,0:T(8,128)(2,1)S(1)} %collective-permute-done.1.refs_3_.refs_4_), channel_id=1, source_target_pairs={{0,16},{16,0},{1,17},{17,1},{2,18},{18,2},{3,19},{19,3},{4,20},{20... | collective-permute-start | bytes 884744 | tf_op jit(solution)/shard_map/store/ppermute | solution.py:686
  90.5 1.6 %collective-permute-start.9 = (bf16[4,144,256]{2,1,0:T(8,128)(2,1)S(1)}, bf16[4,144,256]{2,1,0:T(8,128)(2,1)S(1)}, u32[]{:S(2)}, u32[]{:S(2)}) collective-permute-start(bf16[4,144,256]{2,1,0:T(8,128)(2,1)S(1)} %collective-permute-done.3.refs_4_.refs_5_), channel_id=1, source_target_pairs={{0,16},{16,0},{1,17},{17,1},{2,18},{18,2},{3,19},{19,3},{4,20},{20... | collective-permute-start | bytes 884744 | tf_op jit(solution)/shard_map/store/ppermute | solution.py:686
  97.0 9.5 %collective-permute-start.12 = (bf16[2,592,128]{2,1,0:T(8,128)(2,1)}, bf16[2,592,128]{2,1,0:T(8,128)(2,1)S(1)}, u32[]{:S(2)}, u32[]{:S(2)}) collective-permute-start(bf16[2,592,128]{2,1,0:T(8,128)(2,1)} %get-tuple-element.29.refs_11_), channel_id=1, source_target_pairs={{0,12},{4,0},{8,4},{12,8},{1,13},{5,1},{9,5},{13,9},{2,14},{6,2},{... | collective-permute-start | bytes 909320 | tf_op jit(solution)/shard_map/memory/ppermute | solution.py:698
  98.0 10.4 %collective-permute-start.13 = (bf16[2,592,128]{2,1,0:T(8,128)(2,1)}, bf16[2,592,128]{2,1,0:T(8,128)(2,1)S(1)}, u32[]{:S(2)}, u32[]{:S(2)}) collective-permute-start(bf16[2,592,128]{2,1,0:T(8,128)(2,1)} %get-tuple-element.30), channel_id=1, source_target_pairs={{0,4},{4,8},{8,12},{12,0},{1,5},{5,9},{9,13},{13,1},{2,6},{6,10},{... | collective-permute-start | bytes 909320 | tf_op jit(solution)/shard_map/memory/ppermute | solution.py:699
  115.9 21.6 %copy-start.2 = (bf16[4,592,128]{2,1,0:T(8,128)(2,1)S(1)}, bf16[4,592,128]{2,1,0:T(8,128)(2,1)}, u32[]{:S(2)}) copy-start(bf16[4,592,128]{2,1,0:T(8,128)(2,1)} %memory_attend.4.refs_14_.refs_0_) | copy-start | bytes 1818628
  115.9 21.6 %collective-permute-start.14 = (bf16[4,592,128]{2,1,0:T(8,128)(2,1)}, bf16[4,592,128]{2,1,0:T(8,128)(2,1)S(1)}, u32[]{:S(2)}, u32[]{:S(2)}) collective-permute-start(bf16[4,592,128]{2,1,0:T(8,128)(2,1)} %get-tuple-element.31), channel_id=1, source_target_pairs={{0,4},{4,8},{8,12},{12,0},{1,5},{5,9},{9,13},{13,1},{2,6},{6,10},{... | collective-permute-start | bytes 1818632 | tf_op jit(solution)/shard_map/memory/ppermute | solution.py:708
  116.0 21.5 %collective-permute-start.15 = (bf16[4,592,128]{2,1,0:T(8,128)(2,1)}, bf16[4,592,128]{2,1,0:T(8,128)(2,1)S(1)}, u32[]{:S(2)}, u32[]{:S(2)}) collective-permute-start(bf16[4,592,128]{2,1,0:T(8,128)(2,1)} %get-tuple-element.32._), channel_id=1, source_target_pairs={{0,12},{4,0},{8,4},{12,8},{1,13},{5,1},{9,5},{13,9},{2,14},{6,2},{... | collective-permute-start | bytes 1818632 | tf_op jit(solution)/shard_map/memory/ppermute | solution.py:707
  123.4 23.5 %all-to-all-start.3 = ((bf16[16,144,128]{2,1,0:T(8,128)(2,1)}), bf16[16,144,128]{2,1,0:T(8,128)(2,1)S(1)}, u32[]{:S(2)}, u32[]{:S(2)}) async-start(bf16[16,144,128]{2,1,0:T(8,128)(2,1)} %temporal_attend.1), calls=%async_computation.3 | async-start | bytes 1179648 | tf_op jit(solution)/shard_map/temporal/all_to_all | solution.py:633
  140.9 6.7 %collective-permute-start.16 = (bf16[592,128]{1,0:T(8,128)(2,1)}, bf16[592,128]{1,0:T(8,128)(2,1)S(1)}, u32[]{:S(2)}, u32[]{:S(2)}) collective-permute-start(bf16[592,128]{1,0:T(8,128)(2,1)} %get-tuple-element.34), channel_id=1, source_target_pairs={{0,1},{1,2},{2,3},{3,0},{4,5},{5,6},{6,7},{7,4},{8,9},{9,10},{10,1... | collective-permute-start | bytes 454664 | tf_op jit(solution)/shard_map/memory/ppermute | solution.py:636
  142.8 7.7 %collective-permute-start.17 = (bf16[592,128]{1,0:T(8,128)(2,1)}, bf16[592,128]{1,0:T(8,128)(2,1)S(1)}, u32[]{:S(2)}, u32[]{:S(2)}) collective-permute-start(bf16[592,128]{1,0:T(8,128)(2,1)} %get-tuple-element.35), channel_id=1, source_target_pairs={{0,2},{1,3},{2,0},{3,1},{4,6},{5,7},{6,4},{7,5},{8,10},{9,11},{10,... | collective-permute-start | bytes 454664 | tf_op jit(solution)/shard_map/memory/ppermute | solution.py:636
  145.5 5.4 %collective-permute-start.18 = (bf16[592,128]{1,0:T(8,128)(2,1)}, bf16[592,128]{1,0:T(8,128)(2,1)S(1)}, u32[]{:S(2)}, u32[]{:S(2)}) collective-permute-start(bf16[592,128]{1,0:T(8,128)(2,1)} %get-tuple-element.36), channel_id=1, source_target_pairs={{0,3},{1,0},{2,1},{3,2},{4,7},{5,4},{6,5},{7,6},{8,11},{9,8},{10,9... | collective-permute-start | bytes 454664 | tf_op jit(solution)/shard_map/memory/ppermute | solution.py:636
  150.9 0.9 copy-start.3

commit v9 on v8

--- a/solution.py
+++ b/solution.py
@@ -63,20 +63,21 @@
         key = rows_ref[:, h * C : (h + 1) * C].astype(F32)
         out_ref[h, :, :C] = (key * inverse_rms(key)).astype(BF)
         out_ref[h, :, C:] = rows_ref[:, HW + h * C : HW + (h + 1) * C]
-        sends.append(copy(out_ref.at[h], out_hbm.at[h], sem.at[h]))
-        sends[-1].start()
+        for k in range(out_hbm.shape[0]):
+            sends.append(copy(out_ref.at[h], out_hbm.at[k, h], sem.at[k, h]))
+            sends[-1].start()
     for send in sends:
         send.wait()
 
 
-def split_store(rows):
+def split_store(rows, copies):
     n = rows.shape[0]
     return pl.pallas_call(
         split_store_kernel,
         in_specs=[WHOLE],
         out_specs=HBM,
-        out_shape=hbm_out((G, n, 2 * C)),
-        scratch_shapes=[pltpu.VMEM((G, n, 2 * C), BF), DMA((G,))],
+        out_shape=hbm_out((copies, G, n, 2 * C)),
+        scratch_shapes=[pltpu.VMEM((G, n, 2 * C), BF), DMA((copies, G))],
         compiler_params=params(),
         name="split_store",
         cost_estimate=cost(8 * n * HW, 8 * n * HW),
@@ -167,14 +168,16 @@
             query_ref[h, at, :] = (
                 one * inverse_rms(one) * (sharpness_ref[0, h] / C)
             ).astype(BF)
-    send = copy(query_ref, query_hbm, query_sem)
-    send.start()
-    for store in stores:
+    sends = [
+        copy(query_ref, query_hbm.at[k], query_sem.at[k]) for k in range(query_hbm.shape[0])
+    ]
+    for send in sends:
+        send.start()
+    for store in stores + sends:
         store.wait()
-    send.wait()
-
-
-def modulate(act, affine, weight, sharpness, owner, slot, held, after):
+
+
+def modulate(act, affine, weight, sharpness, owner, slot, held, copies, after):
     patches, depth = act.shape
     steps = 2
     rows = patches // steps
@@ -183,7 +186,7 @@
         functools.partial(modulate_kernel, held),
         in_specs=[HBM, HBM, HBM, SCALARS, SCALARS, SCALARS, ANY],
         out_specs=[HBM, HBM],
-        out_shape=[hbm_out((patches, depth)), hbm_out(shape)],
+        out_shape=[hbm_out((patches, depth)), hbm_out((copies,) + shape)],
         scratch_shapes=[
             pltpu.VMEM((steps, rows, depth), BF),
             pltpu.VMEM(affine.shape, F32),
@@ -194,7 +197,7 @@
             DMA,
             DMA,
             DMA((steps,)),
-            DMA,
+            DMA((copies,)),
         ],
         compiler_params=params(),
         name="modulate",
@@ -205,9 +208,9 @@
 
 
 def temporal_entry_kernel(
-    quarters, hidden_hbm, weight_hbm, sharpness_ref, _, out_hbm,
-    hidden_ref, weight_ref, out_ref, hidden_sem, weight_sem, store_sem,
+    quarters, hidden_hbm, weight_hbm, sharpness_ref, *refs
 ):
+    out_hbm, hidden_ref, weight_ref, out_ref, hidden_sem, weight_sem, store_sem = refs[-7:]
     rows = hidden_ref.shape[0] // quarters
     hidden_load = copy(hidden_hbm, hidden_ref, hidden_sem)
     loads = [
@@ -246,7 +249,7 @@
     rows = patches // quarters
     return pl.pallas_call(
         functools.partial(temporal_entry_kernel, quarters),
-        in_specs=[HBM, HBM, SCALARS, ANY],
+        in_specs=[HBM, HBM, SCALARS] + [ANY] * len(after),
         out_specs=HBM,
         out_shape=hbm_out((quarters, G, 3, rows, C)),
         scratch_shapes=[
@@ -262,7 +265,7 @@
         cost_estimate=cost(
             6 * patches * depth * HW, 2 * patches * depth + 6 * depth * HW + 6 * patches * HW
         ),
-    )(in_hbm(hidden), in_hbm(weight), sharpness, in_hbm(after))
+    )(in_hbm(hidden), in_hbm(weight), sharpness, *after)
 
 
 def temporal_attend_kernel(length_ref, in_hbm_ref, _, out_hbm, in_ref, out_ref, sem):
@@ -315,7 +318,7 @@
     return jnp.concatenate([high, denominators - high], axis=0).astype(BF)
 
 
-def attend_rows(query, keys, both, out_ref, carry=None):
+def attend_rows(query, keys, both, out_ref):
     patches = out_ref.shape[0] - PAD
     row = lax.broadcasted_iota(jnp.int32, (LINE, C), 0)
     column = lax.broadcasted_iota(jnp.int32, (LINE, C), 1)
@@ -324,19 +327,12 @@
         at = slice(start, start + CHUNK)
         weights = jnp.exp(dot_t(query(at), keys)).astype(BF)
         result = dot(weights, both)
-        top = result[:, :C]
-        if carry is not None:
-            top = top + carry[at, :].astype(F32)
-        out_ref[at, :] = top.astype(BF)
+        out_ref[at, :] = result[:, :C].astype(BF)
         for j in range(0, CHUNK, LINE):
             diagonal = jnp.where(row == column, result[j : j + LINE, C:], 0.0)
             lines.append(jnp.sum(diagonal, axis=0, keepdims=True))
     lines.append(jnp.zeros((8 - len(lines), C), F32))
-    total = jnp.concatenate(lines, axis=0)
-    if carry is not None:
-        tail = carry[patches:, :].astype(F32)
-        total = total + tail[:8] + tail[8:]
-    out_ref[patches:, :] = halves(total)
+    out_ref[patches:, :] = halves(jnp.concatenate(lines, axis=0))
 
 
 def with_ones(values):
@@ -349,7 +345,7 @@
     out_hbm, hidden_ref, weight_ref, query_ref, out_ref = refs[-9:-4]
     hidden_sem, weight_sem, query_sem, store_sem = refs[-4:]
     hidden_load = copy(hidden_hbm, hidden_ref, hidden_sem)
-    query_load = copy(query_hbm, query_ref, query_sem)
+    query_load = copy(query_hbm.at[0], query_ref, query_sem)
     loads = [
         copy(
             weight_hbm.at[:, pl.ds((1 + part) * HW, HW)], weight_ref.at[part], weight_sem.at[part]
@@ -380,16 +376,17 @@
 
 def own_attend(hidden, weight, query, after):
     patches, depth = hidden.shape
+    shape = query.shape[1:]
     return pl.pallas_call(
         own_attend_kernel,
         in_specs=[HBM, HBM, HBM] + [ANY] * len(after),
         out_specs=HBM,
-        out_shape=hbm_out(query.shape),
+        out_shape=hbm_out(shape),
         scratch_shapes=[
             pltpu.VMEM((patches, depth), BF),
             pltpu.VMEM((2, depth, HW), BF),
-            pltpu.VMEM(query.shape, BF),
-            pltpu.VMEM(query.shape, BF),
+            pltpu.VMEM(shape, BF),
+            pltpu.VMEM(shape, BF),
             DMA,
             DMA((2,)),
             DMA,
@@ -404,79 +401,69 @@
     )(in_hbm(hidden), in_hbm(weight), in_hbm(query), *after)
 
 
-def memory_attend_kernel(groups, count, carried, pieces, index_ref, *refs):
-    queries, refs = refs[:groups], refs[groups:]
-    blocks, refs = refs[:count], refs[count:]
-    carries, refs = refs[: len(carried)], refs[len(carried) + 1 :]
-    outs, refs = refs[: groups * pieces], refs[groups * pieces :]
-    query_ref, store_ref, carry_ref, out_ref, query_sem, block_sem, carry_sem, store_sem = refs
-    frames = queries[0].shape[0]
-    loads, start = [], 0
-    for i, block in enumerate(blocks):
-        held = block.shape[0]
-        loads.append(copy(block, store_ref.at[pl.ds(start, held)], block_sem.at[i]))
-        start += held
-    query_loads = [copy(queries[k], query_ref.at[k], query_sem.at[k]) for k in range(groups)]
-    carry_loads = [copy(ref, carry_ref.at[i], carry_sem.at[i]) for i, ref in enumerate(carries)]
-    for load in query_loads[:1] + loads + carry_loads + query_loads[1:]:
-        load.start()
-    for load in loads + carry_loads:
-        load.wait()
+def memory_attend_kernel(count, base_ref, index_ref, query_hbm, *refs):
+    blocks = refs[:count]
+    out_hbm, query_ref, store_ref, out_ref, query_sem, block_sem, store_sem = refs[count + 1 :]
+    frames = query_ref.shape[0]
+    base = base_ref[0]
+    query_load = copy(query_hbm.at[pl.ds(base, frames)], query_ref, query_sem)
+    query_load.start()
+
+    def fetch(t, carry):
+        i, j = t // TOPM, lax.rem(t, TOPM)
+        wanted = index_ref[base + i, j]
+        start = 0
+        for block in blocks:
+            held = block.shape[0]
+
+            @pl.when((wanted >= start) & (wanted < start + held))
+            def _(block=block, start=start):
+                copy(block.at[wanted - start], store_ref.at[i, j], block_sem.at[i]).start()
+
+            start += held
+        return carry
+
+    lax.fori_loop(0, frames * TOPM, fetch, 0)
+    query_load.wait()
     stores = []
-    piece = frames // pieces
-    for k in range(groups):
-        query_loads[k].wait()
-        for i in range(frames):
-            chosen = [store_ref[index_ref[k * frames + i, j]] for j in range(TOPM)]
-            keys = jnp.concatenate([block[:, :C] for block in chosen], axis=0)
-            values = jnp.concatenate([block[:, C:] for block in chosen], axis=0)
-            carry = None
-            for at, (group, first) in enumerate(carried):
-                if group == k and first <= i < first + carries[at].shape[0]:
-                    carry = carry_ref.at[at, i - first]
-            attend_rows(
-                lambda at, k=k, i=i: query_ref[k, i, at, :],
-                keys,
-                with_ones(values),
-                out_ref.at[k, i],
-                carry,
-            )
-            out = outs[k * pieces + i // piece].at[i % piece]
-            stores.append(copy(out_ref.at[k, i], out, store_sem.at[k, i]))
-            stores[-1].start()
+    for i in range(frames):
+        copy(store_ref.at[i], store_ref.at[i], block_sem.at[i]).wait()
+        keys = jnp.concatenate([store_ref[i, j, :, :C] for j in range(TOPM)], axis=0)
+        values = jnp.concatenate([store_ref[i, j, :, C:] for j in range(TOPM)], axis=0)
+        attend_rows(
+            lambda at, i=i: query_ref[i, at, :], keys, with_ones(values), out_ref.at[i]
+        )
+        stores.append(copy(out_ref.at[i], out_hbm.at[i], store_sem.at[i]))
+        stores[-1].start()
     for store in stores:
         store.wait()
 
 
-def memory_attend(index, queries, blocks, after, carries=(), carried=(), pieces=1):
-    groups, count = len(queries), len(blocks)
-    frames, rows, _ = queries[0].shape
-    _, quarter, width = blocks[0].shape
-    total = sum(block.shape[0] for block in blocks)
-    shape = (groups, frames, rows, C)
-    held = max([1] + [carry.shape[0] for carry in carries])
-    return pl.pallas_call(
-        functools.partial(memory_attend_kernel, groups, count, tuple(carried), pieces),
-        in_specs=[SCALARS] + [ANY] * (groups + count + len(carries) + 1),
-        out_specs=[HBM] * (groups * pieces),
-        out_shape=[hbm_out((frames // pieces, rows, C))] * (groups * pieces),
+def memory_attend(base, index, query, frames, blocks, after):
+    count = len(blocks)
+    rows = query.shape[1]
+    _, part, width = blocks[0].shape
+    shape = (frames, rows, C)
+    return pl.pallas_call(
+        functools.partial(memory_attend_kernel, count),
+        in_specs=[SCALARS, SCALARS] + [ANY] * (count + 2),
+        out_specs=HBM,
+        out_shape=hbm_out(shape),
         scratch_shapes=[
             pltpu.VMEM(shape, BF),
-            pltpu.VMEM((total, quarter, width), BF),
-            pltpu.VMEM((max(1, len(carries)), held, rows, C), BF),
+            pltpu.VMEM((frames, TOPM, part, width), BF),
             pltpu.VMEM(shape, BF),
-            DMA((groups,)),
-            DMA((count,)),
-            DMA((max(1, len(carries)),)),
-            DMA((groups, frames)),
+            DMA,
+            DMA((frames,)),
+            DMA((frames,)),
         ],
         compiler_params=params(),
         name="memory_attend",
         cost_estimate=cost(
-            8 * groups * frames * rows * TOPM * quarter * C,
-            4 * groups * frames * rows * C + 2 * total * quarter * width,
+            8 * frames * rows * TOPM * part * C,
+            4 * frames * rows * C + 2 * frames * TOPM * part * width,
         ),
-    )(index, *queries, *blocks, *carries, in_hbm(after))
+    )(base, index, query, *blocks, in_hbm(after))
 
 
 def add_partials_kernel(count, x_ref, *refs):
@@ -618,26 +605,32 @@
     recalled_picture_position,
     lookback_lengths,
 ):
-    rings = lax.axis_size("z")
+    frame = ("zq", "zp", "x")
+    rings, sides = lax.axis_size("y"), lax.axis_size("zp")
+    quarters = lax.axis_size("zq") * sides
     patches, depth = patch_activation_tensor.shape[2:]
     held, piece = cached_past_pairs.shape[:2]
-    rolls_y, cores = lax.axis_size("y"), lax.axis_size("c")
+    cores = lax.axis_size("c")
     x = lax.axis_index("x").astype(jnp.int32).reshape(1)
+    side = lax.axis_index("zp").astype(jnp.int32).reshape(1)
 
     def turn(step):
         return [(s, (s + step) % rings) for s in range(rings)]
 
-    other = [(s, cores - 1 - s) for s in range(cores)]
+    def other(size):
+        return [(s, size - 1 - s) for s in range(size)]
 
     def swap(blocks, axes):
         return lax.all_to_all(blocks, axes, split_axis=0, concat_axis=0, tiled=True)
 
     def swap_apart(blocks):
-        return [blocks[0]] + [lax.ppermute(blocks[j], "x", turn(j)) for j in range(1, G)]
+        return [in_hbm(blocks[0])] + [lax.ppermute(blocks[j], "x", turn(j)) for j in range(1, G)]
 
     with jax.named_scope("store"):
-        split = split_store(cached_past_pairs.reshape(held * piece, 2 * HW))
-        pieces = swap(split, "x")
+        split = split_store(
+            cached_past_pairs.reshape(held * piece, 2 * HW), lax.axis_size("zq")
+        )
+        pieces = swap(split.reshape((-1,) + split.shape[2:]), ("zq", "x"))
 
     with jax.named_scope("queries"):
         hidden, query = modulate(
@@ -648,71 +641,59 @@
             recalled_picture_holder.reshape(TOPM),
             recalled_picture_position.reshape(TOPM),
             held,
+            sides,
             after=split,
         )
-        here = swap(query, "x")
 
     with jax.named_scope("store"):
         joined = join_pieces(pieces, held, after=hidden)
         above = lax.ppermute(joined, "y", turn(-1))
         below = lax.ppermute(joined, "y", turn(1))
 
+    with jax.named_scope("queries"):
+        asked, joined = lax.optimization_barrier((query, joined))
+        asked = swap(asked.reshape((-1,) + asked.shape[2:]), ("zp", "x"))
+
     with jax.named_scope("temporal"):
         parts = temporal_entry(
-            hidden, entry_projection_matrix, softmax_sharpness, rings, after=joined
+            hidden, entry_projection_matrix, softmax_sharpness, quarters, after=[in_hbm(joined)]
         )
-        sent = swap(parts.reshape((rings * G,) + parts.shape[2:]), ("z", "x"))
-
-    with jax.named_scope("queries"):
-        z_above = lax.ppermute(here, "z", turn(-1))
-        z_below = lax.ppermute(here, "z", turn(1))
-
-    with jax.named_scope("own"):
-        own = own_attend(
-            hidden,
-            entry_projection_matrix,
-            query,
-            after=[parts, above, below, z_above, z_below],
-        )
-
-    with jax.named_scope("queries"):
-        z_far = lax.ppermute(z_below, "z", turn(1))
+        sent = swap(parts.reshape((quarters * G,) + parts.shape[2:]), frame)
 
     with jax.named_scope("store"):
+        above, below, parts = lax.optimization_barrier((above, below, parts))
         far_first = lax.ppermute(above[: held // 2], "y", turn(-1))
         far_last = lax.ppermute(below[held // 2 :], "y", turn(1))
         near = [joined, above, far_first, far_last, below]
-        *near, own = lax.optimization_barrier((*near, own))
-        blocks = near + [lax.ppermute(block, "c", other) for block in near]
-
-    def attend(queries, after, **more):
-        named = jnp.concatenate([group[:, patches, :TOPM] for group in queries], axis=0)
-        named = named.astype(jnp.int32)
-        y = (named // (cores * held) - lax.axis_index("y")) & (rolls_y - 1)
+        blocks = near + [lax.ppermute(block, "c", other(cores)) for block in near]
+        blocks[0] = in_hbm(blocks[0])
+
+    with jax.named_scope("own"):
+        own = own_attend(
+            hidden, entry_projection_matrix, query, after=[in_hbm(parts), asked]
+        )
+
+    with jax.named_scope("queries"):
+        named = asked[:, patches, :TOPM].astype(jnp.int32)
+        y = (named // (cores * held) - lax.axis_index("y")) & (rings - 1)
         c = (named // held & (cores - 1)) ^ lax.axis_index("c")
-        index = (c * rolls_y + y) * held + (named & (held - 1))
-        return memory_attend(index, queries, blocks, after, **more)
+        index = (c * rings + y) * held + (named & (held - 1))
+
+    def attend(base, after):
+        return memory_attend(base, index, asked, asked.shape[0] // sides, blocks, after)
 
     with jax.named_scope("memory"):
-        sum_first, sum_last = attend([z_far], own, pieces=2)
-        carry_first = lax.ppermute(sum_first, "z", turn(-1))
-        carry_last = lax.ppermute(sum_last, "z", turn(1))
-        (sum_here,) = attend([here], sum_first)
-        sum_below, sum_above = attend(
-            [z_below, z_above],
-            sum_here,
-            carries=[carry_first, carry_last],
-            carried=[(0, 0), (1, here.shape[0] // 2)],
-        )
-        from_above = lax.ppermute(sum_below, "z", turn(-1))
-        from_below = lax.ppermute(sum_above, "z", turn(1))
+        count = asked.shape[0] // sides
+        sum_beside = attend((sides - 1 - side) * count, own)
+        from_beside = lax.ppermute(sum_beside, "zp", other(sides))
+        sum_here = attend(side * count, sum_beside)
 
     with jax.named_scope("temporal"):
-        timed = temporal_attend(lookback_lengths, sent, after=sum_below)
-        time = swap(timed, ("z", "x"))
+        timed = temporal_attend(lookback_lengths, sent, after=sum_here)
+        time = swap(timed, frame)
 
     with jax.named_scope("memory"):
-        memory = swap_apart(add_partials(x, [sum_here, from_below, from_above]))
+        memory = swap_apart(add_partials(x, [in_hbm(sum_here), from_beside]))
 
     with jax.named_scope("exit"):
         attended = leave(x, own, memory, time, exit_projection_matrix)
@@ -720,8 +701,8 @@
 
 
 def solution(mesh):
-    apart = Mesh(mesh.devices.reshape(4, 2, 4, 4), ("y", "c", "z", "x"))
-    roll, frame = ("y", "c"), ("z", "x")
+    apart = Mesh(mesh.devices.reshape(4, 2, 2, 2, 4), ("y", "c", "zq", "zp", "x"))
+    roll, frame = ("y", "c"), ("zq", "zp", "x")
     return jax.shard_map(
         on_device,
         mesh=apart,

time: 159 us -> 144 us (0.906)
  blocking collectives: 14.9 us -> 0 us
  waiting for transfers between devices: 40.9 us -> 50.4 us
  starting transfers between devices: 39.3 us -> 34.1 us
  local copies, waits for them, and re-layouts: 5.03 us -> 2.3 us
    ppermute x12 -> x6, waiting for transfers between devices: 29.8 us -> 0.02 us  [the longest x5 0.01 us: on_device(): blocks = near + [lax.ppermute(block, 'c', other(cores)) for block in near]]
    all_to_all x3 -> x4, waiting for transfers between devices: 7.15 us -> 23.9 us  [swap(): return lax.all_to_all(blocks, axes, split_axis=0, concat_axis=0, tiled=True)]
    all_to_all x1 -> x0, blocking collectives: 14.9 us -> none  [swap(): return lax.all_to_all(blocks, axes, split_axis=0, concat_axis=0, tiled=True)]
    ppermute x12 -> x6, starting transfers between devices: 14.4 us -> 1.71 us  [the longest x1 1.11 us: on_device(): from_beside = lax.ppermute(sum_beside, 'zp', other(sides))]
    ppermute x1, waiting for transfers between devices: 0.01 us -> 9.98 us  [on_device(): far_first = lax.ppermute(above[:held // 2], 'y', turn(-1))]
    all_to_all x3 -> x4, starting transfers between devices: 12.3 us -> 21 us  [swap(): return lax.all_to_all(blocks, axes, split_axis=0, concat_axis=0, tiled=True)]
    ppermute x1, waiting for transfers between devices: 0.01 us -> 6.44 us  [on_device(): above = lax.ppermute(joined, 'y', turn(-1))]
    ppermute x1, waiting for transfers between devices: 0.01 us -> 3.41 us  [on_device(): below = lax.ppermute(joined, 'y', turn(1))]
  transfers between devices with their start and end apart: 22 -> 17, of which waited for: 9 -> 9; matrix products, arithmetic and copies ran while one was open for 3% -> 1% of each run, Pallas kernels for 27% -> 32%
where the time goes in v9:
time: 144 us
  Pallas kernels  56.1 us (39%)
  waiting for transfers between devices  50.4 us (35%)
  starting transfers between devices  34.1 us (24%)
  local copies, waits for them, and re-layouts  2.3 us (2%)
    all_to_all x4, waiting for transfers between devices, swap(): return lax.all_to_all(blocks, axes, split_axis=0, concat_axis=0, tiled=True)  23.9 us
    all_to_all x4, starting transfers between devices, swap(): return lax.all_to_all(blocks, axes, split_axis=0, concat_axis=0, tiled=True)  21 us
    pallas_call x2, Pallas kernels, memory_attend(): pl.pallas_call(functools.partial(memory_attend_kernel, count), in_specs=[...  17.7 us
    ppermute x1, waiting for transfers between devices, on_device(): far_first = lax.ppermute(above[:held // 2], 'y', turn(-1))  9.98 us
    pallas_call x1, Pallas kernels, temporal_entry(): pl.pallas_call(functools.partial(temporal_entry_kernel, quarters), in_spe...  8.55 us
    pallas_call x1, Pallas kernels, own_attend(): pl.pallas_call(own_attend_kernel, in_specs=[HBM, HBM, HBM] + [ANY] * len(...  8.07 us
    ppermute x1, waiting for transfers between devices, on_device(): above = lax.ppermute(joined, 'y', turn(-1))  6.44 us
    ppermute x3, starting transfers between devices, swap_apart(): lax.ppermute(blocks[j], 'x', turn(j))  6.13 us
  transfers between devices with their start and end apart: 17, of which 9 were waited for; matrix products, arithmetic and copies ran while one was open for 1% of the time, Pallas kernels for 32%

profile of v9, /device:TPU:0, one launch (start us, length us, event | category | flops | bytes accessed | tf_op | source)
XLA Modules:
  0.0 144.0 jit_solution(13506186292233055819)
XLA Ops:
  0.0 1.1 copy.10
  1.2 1.2 split_store.1._
  2.4 0.0 copy-start
  2.4 0.0 copy-start.1
  2.4 0.0 copy-start.2
  2.4 7.8 %all-to-all-start = ((bf16[8,288,256]{2,1,0:T(8,128)(2,1)}), bf16[8,288,256]{2,1,0:T(8,128)(2,1)S(1)}, u32[]{:S(2)}, u32[]{:S(2)}) async-start(bf16[8,288,256]{2,1,0:T(8,128)(2,1)} %bitcast.19), calls=%async_computation | async-start | bytes 2359296 | tf_op jit(solution)/shard_map/store/all_to_all | solution.py:624
  10.3 0.0 copy-done
  10.3 0.0 copy-done.1
  10.3 0.0 copy-done.2
  10.3 5.8 %modulate.1 = (bf16[576,2048]{1,0:T(8,128)(2,1)}, bf16[2,4,592,128]{3,2,1,0:T(8,128)(2,1)}) custom-call(bf16[576,2048]{1,0:T(8,128)(2,1)} %bitcast.21, f32[2,2048]{1,0:T(2,128)} %bitcast.23, bf16[2048,3072]{1,0:T(8,128)(2,1)} %weight_hbm.6, f32[2,4]{1,0:T(2,128)S(1)} %copy-done, s32[6]{0:T(128)S(1)} %bitcast.16, s32[6]{0:T(128)S(1)} %bitcast.17, ...), custom_call_target="tpu_custom_call" | custom-call | flops 75497472 | bytes 462848 | tf_op jit(solution)/shard_map/queries/modulate/pallas_call | solution.py:185
  16.1 12.8 %all-to-all-done.in_hbm = bf16[8,288,256]{2,1,0:T(8,128)(2,1)S(1)} async-done(((bf16[8,288,256]{2,1,0:T(8,128)(2,1)}), bf16[8,288,256]{2,1,0:T(8,128)(2,1)S(1)}, u32[]{:S(2)}, u32[]{:S(2)}) %all-to-all-start) | async-done | bytes 1179680 | tf_op jit(solution)/shard_map/store/all_to_all | solution.py:624
  28.9 2.9 %join_pieces.1.refs_0_ = bf16[8,288,256]{2,1,0:T(8,128)(2,1)} custom-call(bf16[8,288,256]{2,1,0:T(8,128)(2,1)S(1)} %all-to-all-done.in_hbm, bf16[576,2048]{1,0:T(8,128)(2,1)} %get-tuple-element.16._.hidden_hbm), custom_call_target="tpu_custom_call" | custom-call | flops 36864 | bytes 147456 | tf_op jit(solution)/shard_map/store/join_pieces/pallas_call | solution.py:109
  31.8 3.6 %all-to-all-start.1 = ((bf16[8,592,128]{2,1,0:T(8,128)(2,1)}), bf16[8,592,128]{2,1,0:T(8,128)(2,1)S(1)}, u32[]{:S(2)}, u32[]{:S(2)}) async-start(bf16[8,592,128]{2,1,0:T(8,128)(2,1)} %bitcast.20), calls=%async_computation.1 | async-start | bytes 2424832 | tf_op jit(solution)/shard_map/queries/all_to_all | solution.py:624
  35.4 3.1 %collective-permute-start = (bf16[8,288,256]{2,1,0:T(8,128)(2,1)}, bf16[8,288,256]{2,1,0:T(8,128)(2,1)S(1)}, u32[]{:S(2)}, u32[]{:S(2)}) collective-permute-start(bf16[8,288,256]{2,1,0:T(8,128)(2,1)} %join_pieces.1.refs_0_), channel_id=1, source_target_pairs={{0,96},{32,0},{64,32},{96,64},{1,97},{33,1},{65,33},{97,65},{2,98}... | collective-permute-start | bytes 3538952 | tf_op jit(solution)/shard_map/store/ppermute | solution.py:650
  38.5 0.0 collective-permute-start.1
  38.5 8.5 %temporal_entry.1.refs_0_ = bf16[4,4,3,144,128]{4,3,2,1,0:T(8,128)(2,1)} custom-call(bf16[576,2048]{1,0:T(8,128)(2,1)} %get-tuple-element.16._.hidden_hbm, bf16[2048,3072]{1,0:T(8,128)(2,1)} %weight_hbm.6, f32[2,4]{1,0:T(2,128)S(1)} %copy-done, bf16[8,288,256]{2,1,0:T(8,128)(2,1)} %join_pieces.1.refs_0_), custom_call_target="tpu_custom_call" | custom-call | flops 226492416 | bytes 651264 | tf_op jit(solution)/shard_map/temporal/temporal_entry/pallas_call | solution.py:250
  47.1 5.9 %all-to-all-done.1.refs_1_.query_hbm = bf16[8,592,128]{2,1,0:T(8,128)(2,1)S(1)} async-done(((bf16[8,592,128]{2,1,0:T(8,128)(2,1)}), bf16[8,592,128]{2,1,0:T(8,128)(2,1)S(1)}, u32[]{:S(2)}, u32[]{:S(2)}) %all-to-all-start.1) | async-done | bytes 1212448 | tf_op jit(solution)/shard_map/queries/all_to_all | solution.py:624
  52.9 4.4 %all-to-all-start.2 = ((bf16[16,3,144,128]{3,2,1,0:T(8,128)(2,1)}), bf16[16,3,144,128]{3,2,1,0:T(8,128)(2,1)}, u32[]{:S(2)}, u32[]{:S(2)}) async-start(bf16[16,3,144,128]{3,2,1,0:T(8,128)(2,1)} %bitcast.18), calls=%async_computation.2 | async-start | bytes 3538944 | tf_op jit(solution)/shard_map/temporal/all_to_all | solution.py:624
  57.3 0.1 collective-permute-start.4
  57.4 6.4 %collective-permute-done.refs_1_ = bf16[8,288,256]{2,1,0:T(8,128)(2,1)S(1)} collective-permute-done((bf16[8,288,256]{2,1,0:T(8,128)(2,1)}, bf16[8,288,256]{2,1,0:T(8,128)(2,1)S(1)}, u32[]{:S(2)}, u32[]{:S(2)}) %collective-permute-start) | collective-permute-done | bytes 1179680 | tf_op jit(solution)/shard_map/store/ppermute | solution.py:650
  63.9 3.4 %collective-permute-done.1.refs_4_ = bf16[8,288,256]{2,1,0:T(8,128)(2,1)} collective-permute-done((bf16[8,288,256]{2,1,0:T(8,128)(2,1)}, bf16[8,288,256]{2,1,0:T(8,128)(2,1)}, u32[]{:S(2)}, u32[]{:S(2)}) %collective-permute-start.1) | collective-permute-done | bytes 1179680 | tf_op jit(solution)/shard_map/store/ppermute | solution.py:651
  67.3 0.2 collective-permute-start.2
  67.6 1.1 slice.11
  68.7 1.9 %collective-permute-start.3 = (bf16[4,288,256]{2,1,0:T(8,128)(2,1)S(1)}, bf16[4,288,256]{2,1,0:T(8,128)(2,1)}, u32[]{:S(2)}, u32[]{:S(2)}) collective-permute-start(bf16[4,288,256]{2,1,0:T(8,128)(2,1)S(1)} %slice.11), channel_id=1, source_target_pairs={{0,32},{32,64},{64,96},{96,0},{1,33},{33,65},{65,97},{97,1},{2,34}... | collective-permute-start | bytes 1769480 | tf_op jit(solution)/shard_map/store/ppermute | solution.py:666
  70.6 0.0 collective-permute-start.5
  70.6 0.5 collective-permute-start.8
  71.1 10.0 %collective-permute-done.2.refs_2_ = bf16[4,288,256]{2,1,0:T(8,128)(2,1)S(1)} collective-permute-done((bf16[4,288,256]{2,1,0:T(8,128)(2,1)S(1)}, bf16[4,288,256]{2,1,0:T(8,128)(2,1)S(1)}, u32[]{:S(2)}, u32[]{:S(2)}) %collective-permute-start.2) | collective-permute-done | bytes 589856 | tf_op jit(solution)/shard_map/store/ppermute | solution.py:665
  81.1 0.0 collective-permute-start.6
  81.1 2.8 %collective-permute-done.3.refs_3_ = bf16[4,288,256]{2,1,0:T(8,128)(2,1)} collective-permute-done((bf16[4,288,256]{2,1,0:T(8,128)(2,1)S(1)}, bf16[4,288,256]{2,1,0:T(8,128)(2,1)}, u32[]{:S(2)}, u32[]{:S(2)}) %collective-permute-start.3) | collective-permute-done | bytes 589856 | tf_op jit(solution)/shard_map/store/ppermute | solution.py:666
  83.9 0.0 collective-permute-start.7
  83.9 8.1 %own_attend.1.refs_10_.own_hbm = bf16[4,592,128]{2,1,0:T(8,128)(2,1)} custom-call(bf16[576,2048]{1,0:T(8,128)(2,1)} %get-tuple-element.16._.hidden_hbm, bf16[2048,3072]{1,0:T(8,128)(2,1)} %weight_hbm.6, bf16[2,4,592,128]{3,2,1,0:T(8,128)(2,1)} %get-tuple-element.20.query_hbm, bf16[4,4,3,144,128]{4,3,2,1,0:T(8,128)(2,1)} %temporal_entry.1.refs_0_, ...), custom_call_target="tpu_custom_call" | custom-call | flops 214695936 | bytes 593920 | tf_op jit(solution)/shard_map/own/own_attend/pallas_call | solution.py:380
  92.0 0.0 collective-permute-done.4.refs_5_
  92.0 0.0 collective-permute-done.6.refs_7_
  92.0 0.0 collective-permute-done.7.refs_8_
  92.0 0.0 collective-permute-done.5.refs_6_
  92.0 0.0 collective-permute-done.8.refs_9_
  92.1 9.1 %memory_attend.2.refs_10_ = bf16[4,592,128]{2,1,0:T(8,128)(2,1)} custom-call(s32[1]{0:T(128)} %bitcast.9.base_ref, s32[8,6]{1,0:T(8,128)S(1)} %fusion.6.index_ref, bf16[8,592,128]{2,1,0:T(8,128)(2,1)S(1)} %all-to-all-done.1.refs_1_.query_hbm, bf16[8,288,256]{2,1,0:T(8,128)(2,1)} %join_pieces.1.refs_0_, ...), custom_call_target="tpu_custom_call" | custom-call | flops 261881856 | bytes 296960 | tf_op jit(solution)/shard_map/memory/memory_attend/pallas_call | solution.py:447
  101.1 1.1 collective-permute-start.9
  102.9 8.7 %memory_attend.3.refs_0_._ = bf16[4,592,128]{2,1,0:T(8,128)(2,1)} custom-call(s32[1]{0:T(128)} %bitcast.7.base_ref, s32[8,6]{1,0:T(8,128)S(1)} %fusion.6.index_ref, bf16[8,592,128]{2,1,0:T(8,128)(2,1)S(1)} %all-to-all-done.1.refs_1_.query_hbm, bf16[8,288,256]{2,1,0:T(8,128)(2,1)} %join_pieces.1.refs_0_, ...), custom_call_target="tpu_custom_call" | custom-call | flops 261881856 | bytes 296960 | tf_op jit(solution)/shard_map/memory/memory_attend/pallas_call | solution.py:447
  111.6 0.0 all-to-all-done.2.in_hbm_ref
  111.6 3.5 %temporal_attend.1 = bf16[16,144,128]{2,1,0:T(8,128)(2,1)} custom-call(s32[1]{0:T(128)S(6)} %copy.11.length_ref, bf16[16,3,144,128]{3,2,1,0:T(8,128)(2,1)} %all-to-all-done.2.in_hbm_ref, bf16[4,592,128]{2,1,0:T(8,128)(2,1)} %memory_attend.3.refs_0_._), custom_call_target="tpu_custom_call" | custom-call | flops 18874368 | bytes 147456 | tf_op jit(solution)/shard_map/temporal/temporal_attend/pallas_call | solution.py:300
  115.1 5.2 %all-to-all-start.3 = ((bf16[16,144,128]{2,1,0:T(8,128)(2,1)}), bf16[16,144,128]{2,1,0:T(8,128)(2,1)S(1)}, u32[]{:S(2)}, u32[]{:S(2)}) async-start(bf16[16,144,128]{2,1,0:T(8,128)(2,1)} %temporal_attend.1), calls=%async_computation.3 | async-start | bytes 1179648 | tf_op jit(solution)/shard_map/temporal/all_to_all | solution.py:624
  120.3 0.0 collective-permute-done.9.refs_1_
  120.3 2.2 %add_partials.1 = (bf16[592,128]{1,0:T(8,128)(2,1)}, bf16[592,128]{1,0:T(8,128)(2,1)}, bf16[592,128]{1,0:T(8,128)(2,1)}, bf16[592,128]{1,0:T(8,128)(2,1)}) custom-call(s32[1]{0:T(128)} %bitcast.x_ref, bf16[4,592,128]{2,1,0:T(8,128)(2,1)} %memory_attend.3.refs_0_._, bf16[4,592,128]{2,1,0:T(8,128)(2,1)} %collective-permute-done.9.refs_1_), custom_call_target="tpu_custom_call" | custom-call | flops 75776 | bytes 151552 | tf_op jit(solution)/shard_map/memory/add_partials/pallas_call | solution.py:499
  122.5 2.0 %collective-permute-start.10 = (bf16[592,128]{1,0:T(8,128)(2,1)}, bf16[592,128]{1,0:T(8,128)(2,1)S(1)}, u32[]{:S(2)}, u32[]{:S(2)}) collective-permute-start(bf16[592,128]{1,0:T(8,128)(2,1)} %get-tuple-element.24), channel_id=1, source_target_pairs={{0,1},{1,2},{2,3},{3,0},{4,5},{5,6},{6,7},{7,4},{8,9},{9,10},{10,1... | collective-permute-start | bytes 454664 | tf_op jit(solution)/shard_map/memory/ppermute | solution.py:627
  124.5 2.7 %collective-permute-start.11 = (bf16[592,128]{1,0:T(8,128)(2,1)}, bf16[592,128]{1,0:T(8,128)(2,1)S(1)}, u32[]{:S(2)}, u32[]{:S(2)}) collective-permute-start(bf16[592,128]{1,0:T(8,128)(2,1)} %get-tuple-element.25), channel_id=1, source_target_pairs={{0,2},{1,3},{2,0},{3,1},{4,6},{5,7},{6,4},{7,5},{8,10},{9,11},{10,... | collective-permute-start | bytes 454664 | tf_op jit(solution)/shard_map/memory/ppermute | solution.py:627
  127.1 1.5 %collective-permute-start.12 = (bf16[592,128]{1,0:T(8,128)(2,1)}, bf16[592,128]{1,0:T(8,128)(2,1)S(1)}, u32[]{:S(2)}, u32[]{:S(2)}) collective-permute-start(bf16[592,128]{1,0:T(8,128)(2,1)} %get-tuple-element.26), channel_id=1, source_target_pairs={{0,3},{1,0},{2,1},{3,2},{4,7},{5,4},{6,5},{7,6},{8,11},{9,8},{10,9... | collective-permute-start | bytes 454664 | tf_op jit(solution)/shard_map/memory/ppermute | solution.py:627
  128.6 5.3 %all-to-all-done.3.time_hbm = bf16[16,144,128]{2,1,0:T(8,128)(2,1)S(1)} async-done(((bf16[16,144,128]{2,1,0:T(8,128)(2,1)}), bf16[16,144,128]{2,1,0:T(8,128)(2,1)S(1)}, u32[]{:S(2)}, u32[]{:S(2)}) %all-to-all-start.3) | async-done | bytes 589856 | tf_op jit(solution)/shard_map/temporal/all_to_all | solution.py:624
  133.9 0.5 collective-permute-done.10.memory_1
  134.3 3.3 %collective-permute-done.11.memory_2 = bf16[592,128]{1,0:T(8,128)(2,1)S(1)} collective-permute-done((bf16[592,128]{1,0:T(8,128)(2,1)}, bf16[592,128]{1,0:T(8,128)(2,1)S(1)}, u32[]{:S(2)}, u32[]{:S(2)}) %collective-permute-start.11) | collective-permute-done | bytes 151584 | tf_op jit(solution)/shard_map/memory/ppermute | solution.py:627
  137.7 0.0 collective-permute-done.12.memory_3
  137.7 6.1 %leave.1 = bf16[576,2048]{1,0:T(8,128)(2,1)} custom-call(s32[1]{0:T(128)} %bitcast.x_ref, bf16[4,592,128]{2,1,0:T(8,128)(2,1)} %own_attend.1.refs_10_.own_hbm, bf16[592,128]{1,0:T(8,128)(2,1)} %get-tuple-element.23.memory_0, bf16[592,128]{1,0:T(8,128)(2,1)S(1)} %collective-permute-done.10.memory_1, bf16[592,128]{1,0:T(8,128)(2,1)S(1)} %collective-permute-done.11.memory_2, ...), custom_call_target="tpu_custom_call" | custom-call | flops 150994944 | bytes 630784 | tf_op jit(solution)/shard_map/exit/leave/pallas_call | solution.py:570
  (3 shorter events, 0.1 us)
Async XLA Ops:
  2.4 7.9 %copy-start = (f32[2,4]{1,0:T(2,128)S(1)}, f32[2,4]{1,0:T(2,128)}, u32[]{:S(2)}) copy-start(f32[2,4]{1,0:T(2,128)} %sharpness_ref.3) | copy-start | bytes 100
  2.4 7.9 %copy-start.1 = (s32[1,1,6,1]{2,3,1,0:T(1,128)S(1)}, s32[1,1,6,1]{2,3,1,0:T(1,128)}, u32[]{:S(2)}) copy-start(s32[1,1,6,1]{2,3,1,0:T(1,128)} %param.15) | copy-start | bytes 76
  2.4 7.9 %copy-start.2 = (s32[1,1,6]{2,1,0:T(1,128)S(1)}, s32[1,1,6]{2,1,0:T(1,128)}, u32[]{:S(2)}) copy-start(s32[1,1,6]{2,1,0:T(1,128)} %param.16) | copy-start | bytes 76
  2.4 26.4 %all-to-all-start = ((bf16[8,288,256]{2,1,0:T(8,128)(2,1)}), bf16[8,288,256]{2,1,0:T(8,128)(2,1)S(1)}, u32[]{:S(2)}, u32[]{:S(2)}) async-start(bf16[8,288,256]{2,1,0:T(8,128)(2,1)} %bitcast.19), calls=%async_computation | async-start | bytes 2359296 | tf_op jit(solution)/shard_map/store/all_to_all | solution.py:624
  31.8 21.1 %all-to-all-start.1 = ((bf16[8,592,128]{2,1,0:T(8,128)(2,1)}), bf16[8,592,128]{2,1,0:T(8,128)(2,1)S(1)}, u32[]{:S(2)}, u32[]{:S(2)}) async-start(bf16[8,592,128]{2,1,0:T(8,128)(2,1)} %bitcast.20), calls=%async_computation.1 | async-start | bytes 2424832 | tf_op jit(solution)/shard_map/queries/all_to_all | solution.py:624
  35.4 28.5 %collective-permute-start = (bf16[8,288,256]{2,1,0:T(8,128)(2,1)}, bf16[8,288,256]{2,1,0:T(8,128)(2,1)S(1)}, u32[]{:S(2)}, u32[]{:S(2)}) collective-permute-start(bf16[8,288,256]{2,1,0:T(8,128)(2,1)} %join_pieces.1.refs_0_), channel_id=1, source_target_pairs={{0,96},{32,0},{64,32},{96,64},{1,97},{33,1},{65,33},{97,65},{2,98}... | collective-permute-start | bytes 3538952 | tf_op jit(solution)/shard_map/store/ppermute | solution.py:650
  38.5 28.8 %collective-permute-start.1 = (bf16[8,288,256]{2,1,0:T(8,128)(2,1)}, bf16[8,288,256]{2,1,0:T(8,128)(2,1)}, u32[]{:S(2)}, u32[]{:S(2)}) collective-permute-start(bf16[8,288,256]{2,1,0:T(8,128)(2,1)} %join_pieces.1.refs_0_), channel_id=1, source_target_pairs={{0,32},{32,64},{64,96},{96,0},{1,33},{33,65},{65,97},{97,1},{2,34}... | collective-permute-start | bytes 3538952 | tf_op jit(solution)/shard_map/store/ppermute | solution.py:651
  52.9 58.6 %all-to-all-start.2 = ((bf16[16,3,144,128]{3,2,1,0:T(8,128)(2,1)}), bf16[16,3,144,128]{3,2,1,0:T(8,128)(2,1)}, u32[]{:S(2)}, u32[]{:S(2)}) async-start(bf16[16,3,144,128]{3,2,1,0:T(8,128)(2,1)} %bitcast.18), calls=%async_computation.2 | async-start | bytes 3538944 | tf_op jit(solution)/shard_map/temporal/all_to_all | solution.py:624
  57.3 34.7 %collective-permute-start.4 = (bf16[8,288,256]{2,1,0:T(8,128)(2,1)}, bf16[8,288,256]{2,1,0:T(8,128)(2,1)}, u32[]{:S(2)}, u32[]{:S(2)}) collective-permute-start(bf16[8,288,256]{2,1,0:T(8,128)(2,1)} %join_pieces.1.refs_0_), channel_id=1, source_target_pairs={{0,16},{16,0},{1,17},{17,1},{2,18},{18,2},{3,19},{19,3},{4,20},{20... | collective-permute-start | bytes 3538952 | tf_op jit(solution)/shard_map/store/ppermute | solution.py:668
  67.3 13.8 %collective-permute-start.2 = (bf16[4,288,256]{2,1,0:T(8,128)(2,1)S(1)}, bf16[4,288,256]{2,1,0:T(8,128)(2,1)S(1)}, u32[]{:S(2)}, u32[]{:S(2)}) collective-permute-start(bf16[4,288,256]{2,1,0:T(8,128)(2,1)S(1)} %slice.10), channel_id=1, source_target_pairs={{0,96},{32,0},{64,32},{96,64},{1,97},{33,1},{65,33},{97,65},{2,98}... | collective-permute-start | bytes 1769480 | tf_op jit(solution)/shard_map/store/ppermute | solution.py:665
  68.7 15.2 %collective-permute-start.3 = (bf16[4,288,256]{2,1,0:T(8,128)(2,1)S(1)}, bf16[4,288,256]{2,1,0:T(8,128)(2,1)}, u32[]{:S(2)}, u32[]{:S(2)}) collective-permute-start(bf16[4,288,256]{2,1,0:T(8,128)(2,1)S(1)} %slice.11), channel_id=1, source_target_pairs={{0,32},{32,64},{64,96},{96,0},{1,33},{33,65},{65,97},{97,1},{2,34}... | collective-permute-start | bytes 1769480 | tf_op jit(solution)/shard_map/store/ppermute | solution.py:666
  70.6 21.4 %collective-permute-start.5 = (bf16[8,288,256]{2,1,0:T(8,128)(2,1)S(1)}, bf16[8,288,256]{2,1,0:T(8,128)(2,1)}, u32[]{:S(2)}, u32[]{:S(2)}) collective-permute-start(bf16[8,288,256]{2,1,0:T(8,128)(2,1)S(1)} %collective-permute-done.refs_1_), channel_id=1, source_target_pairs={{0,16},{16,0},{1,17},{17,1},{2,18},{18,2},{3,19},{19,3},{4,20},{20... | collective-permute-start | bytes 3538952 | tf_op jit(solution)/shard_map/store/ppermute | solution.py:668
  70.6 21.5 %collective-permute-start.8 = (bf16[8,288,256]{2,1,0:T(8,128)(2,1)}, bf16[8,288,256]{2,1,0:T(8,128)(2,1)}, u32[]{:S(2)}, u32[]{:S(2)}) collective-permute-start(bf16[8,288,256]{2,1,0:T(8,128)(2,1)} %collective-permute-done.1.refs_4_), channel_id=1, source_target_pairs={{0,16},{16,0},{1,17},{17,1},{2,18},{18,2},{3,19},{19,3},{4,20},{20... | collective-permute-start | bytes 3538952 | tf_op jit(solution)/shard_map/store/ppermute | solution.py:668
  81.1 10.9 %collective-permute-start.6 = (bf16[4,288,256]{2,1,0:T(8,128)(2,1)S(1)}, bf16[4,288,256]{2,1,0:T(8,128)(2,1)}, u32[]{:S(2)}, u32[]{:S(2)}) collective-permute-start(bf16[4,288,256]{2,1,0:T(8,128)(2,1)S(1)} %collective-permute-done.2.refs_2_), channel_id=1, source_target_pairs={{0,16},{16,0},{1,17},{17,1},{2,18},{18,2},{3,19},{19,3},{4,20},{20... | collective-permute-start | bytes 1769480 | tf_op jit(solution)/shard_map/store/ppermute | solution.py:668
  83.9 8.1 %collective-permute-start.7 = (bf16[4,288,256]{2,1,0:T(8,128)(2,1)}, bf16[4,288,256]{2,1,0:T(8,128)(2,1)}, u32[]{:S(2)}, u32[]{:S(2)}) collective-permute-start(bf16[4,288,256]{2,1,0:T(8,128)(2,1)} %collective-permute-done.3.refs_3_), channel_id=1, source_target_pairs={{0,16},{16,0},{1,17},{17,1},{2,18},{18,2},{3,19},{19,3},{4,20},{20... | collective-permute-start | bytes 1769480 | tf_op jit(solution)/shard_map/store/ppermute | solution.py:668
  101.1 19.2 %collective-permute-start.9 = (bf16[4,592,128]{2,1,0:T(8,128)(2,1)}, bf16[4,592,128]{2,1,0:T(8,128)(2,1)}, u32[]{:S(2)}, u32[]{:S(2)}) collective-permute-start(bf16[4,592,128]{2,1,0:T(8,128)(2,1)} %memory_attend.2.refs_10_), channel_id=1, source_target_pairs={{0,4},{4,0},{1,5},{5,1},{2,6},{6,2},{3,7},{7,3},{8,12},{12,8},{9,1... | collective-permute-start | bytes 1818632 | tf_op jit(solution)/shard_map/memory/ppermute | solution.py:688
  115.1 18.8 %all-to-all-start.3 = ((bf16[16,144,128]{2,1,0:T(8,128)(2,1)}), bf16[16,144,128]{2,1,0:T(8,128)(2,1)S(1)}, u32[]{:S(2)}, u32[]{:S(2)}) async-start(bf16[16,144,128]{2,1,0:T(8,128)(2,1)} %temporal_attend.1), calls=%async_computation.3 | async-start | bytes 1179648 | tf_op jit(solution)/shard_map/temporal/all_to_all | solution.py:624
  122.5 11.9 %collective-permute-start.10 = (bf16[592,128]{1,0:T(8,128)(2,1)}, bf16[592,128]{1,0:T(8,128)(2,1)S(1)}, u32[]{:S(2)}, u32[]{:S(2)}) collective-permute-start(bf16[592,128]{1,0:T(8,128)(2,1)} %get-tuple-element.24), channel_id=1, source_target_pairs={{0,1},{1,2},{2,3},{3,0},{4,5},{5,6},{6,7},{7,4},{8,9},{9,10},{10,1... | collective-permute-start | bytes 454664 | tf_op jit(solution)/shard_map/memory/ppermute | solution.py:627
  124.5 13.2 %collective-permute-start.11 = (bf16[592,128]{1,0:T(8,128)(2,1)}, bf16[592,128]{1,0:T(8,128)(2,1)S(1)}, u32[]{:S(2)}, u32[]{:S(2)}) collective-permute-start(bf16[592,128]{1,0:T(8,128)(2,1)} %get-tuple-element.25), channel_id=1, source_target_pairs={{0,2},{1,3},{2,0},{3,1},{4,6},{5,7},{6,4},{7,5},{8,10},{9,11},{10,... | collective-permute-start | bytes 454664 | tf_op jit(solution)/shard_map/memory/ppermute | solution.py:627
  127.1 10.5 %collective-permute-start.12 = (bf16[592,128]{1,0:T(8,128)(2,1)}, bf16[592,128]{1,0:T(8,128)(2,1)S(1)}, u32[]{:S(2)}, u32[]{:S(2)}) collective-permute-start(bf16[592,128]{1,0:T(8,128)(2,1)} %get-tuple-element.26), channel_id=1, source_target_pairs={{0,3},{1,0},{2,1},{3,2},{4,7},{5,4},{6,5},{7,6},{8,11},{9,8},{10,9... | collective-permute-start | bytes 454664 | tf_op jit(solution)/shard_map/memory/ppermute | solution.py:627

commit v10 on v9

--- a/solution.py
+++ b/solution.py
@@ -405,6 +405,7 @@
     blocks = refs[:count]
     out_hbm, query_ref, store_ref, out_ref, query_sem, block_sem, store_sem = refs[count + 1 :]
     frames = query_ref.shape[0]
+    held = blocks[0].shape[0]
     base = base_ref[0]
     query_load = copy(query_hbm.at[pl.ds(base, frames)], query_ref, query_sem)
     query_load.start()
@@ -412,15 +413,15 @@
     def fetch(t, carry):
         i, j = t // TOPM, lax.rem(t, TOPM)
         wanted = index_ref[base + i, j]
-        start = 0
-        for block in blocks:
-            held = block.shape[0]
-
-            @pl.when((wanted >= start) & (wanted < start + held))
-            def _(block=block, start=start):
-                copy(block.at[wanted - start], store_ref.at[i, j], block_sem.at[i]).start()
-
-            start += held
+        for b in range(count // 2):
+
+            @pl.when(wanted // held == b)
+            def _(b=b):
+                slot = lax.rem(wanted, held)
+                for part in range(2):
+                    block = blocks[2 * b + part].at[slot]
+                    copy(block, store_ref.at[i, j, part], block_sem.at[i]).start()
+
         return carry
 
     lax.fori_loop(0, frames * TOPM, fetch, 0)
@@ -428,8 +429,9 @@
     stores = []
     for i in range(frames):
         copy(store_ref.at[i], store_ref.at[i], block_sem.at[i]).wait()
-        keys = jnp.concatenate([store_ref[i, j, :, :C] for j in range(TOPM)], axis=0)
-        values = jnp.concatenate([store_ref[i, j, :, C:] for j in range(TOPM)], axis=0)
+        both = [store_ref[i, j, part] for j in range(TOPM) for part in range(2)]
+        keys = jnp.concatenate([block[:, :C] for block in both], axis=0)
+        values = jnp.concatenate([block[:, C:] for block in both], axis=0)
         attend_rows(
             lambda at, i=i: query_ref[i, at, :], keys, with_ones(values), out_ref.at[i]
         )
@@ -451,7 +453,7 @@
         out_shape=hbm_out(shape),
         scratch_shapes=[
             pltpu.VMEM(shape, BF),
-            pltpu.VMEM((frames, TOPM, part, width), BF),
+            pltpu.VMEM((frames, TOPM, 2, part, width), BF),
             pltpu.VMEM(shape, BF),
             DMA,
             DMA((frames,)),
@@ -460,7 +462,7 @@
         compiler_params=params(),
         name="memory_attend",
         cost_estimate=cost(
-            8 * frames * rows * TOPM * part * C,
+            16 * frames * rows * TOPM * part * C,
             4 * frames * rows * C + 2 * frames * TOPM * part * width,
         ),
     )(base, index, query, *blocks, in_hbm(after))
@@ -606,13 +608,13 @@
     lookback_lengths,
 ):
     frame = ("zq", "zp", "x")
-    rings, sides = lax.axis_size("y"), lax.axis_size("zp")
-    quarters = lax.axis_size("zq") * sides
+    rings, sides = lax.axis_size("y"), lax.axis_size("zq")
+    quarters = lax.axis_size("zp") * sides
     patches, depth = patch_activation_tensor.shape[2:]
     held, piece = cached_past_pairs.shape[:2]
     cores = lax.axis_size("c")
     x = lax.axis_index("x").astype(jnp.int32).reshape(1)
-    side = lax.axis_index("zp").astype(jnp.int32).reshape(1)
+    side = lax.axis_index("zq").astype(jnp.int32).reshape(1)
 
     def turn(step):
         return [(s, (s + step) % rings) for s in range(rings)]
@@ -627,10 +629,8 @@
         return [in_hbm(blocks[0])] + [lax.ppermute(blocks[j], "x", turn(j)) for j in range(1, G)]
 
     with jax.named_scope("store"):
-        split = split_store(
-            cached_past_pairs.reshape(held * piece, 2 * HW), lax.axis_size("zq")
-        )
-        pieces = swap(split.reshape((-1,) + split.shape[2:]), ("zq", "x"))
+        split = split_store(cached_past_pairs.reshape(held * piece, 2 * HW), 1)
+        pieces = swap(split[0], "x")
 
     with jax.named_scope("queries"):
         hidden, query = modulate(
@@ -649,10 +649,11 @@
         joined = join_pieces(pieces, held, after=hidden)
         above = lax.ppermute(joined, "y", turn(-1))
         below = lax.ppermute(joined, "y", turn(1))
+        second = lax.ppermute(joined, "zp", other(sides))
 
     with jax.named_scope("queries"):
         asked, joined = lax.optimization_barrier((query, joined))
-        asked = swap(asked.reshape((-1,) + asked.shape[2:]), ("zp", "x"))
+        asked = swap(asked.reshape((-1,) + asked.shape[2:]), ("zq", "x"))
 
     with jax.named_scope("temporal"):
         parts = temporal_entry(
@@ -661,17 +662,22 @@
         sent = swap(parts.reshape((quarters * G,) + parts.shape[2:]), frame)
 
     with jax.named_scope("store"):
-        above, below, parts = lax.optimization_barrier((above, below, parts))
-        far_first = lax.ppermute(above[: held // 2], "y", turn(-1))
-        far_last = lax.ppermute(below[held // 2 :], "y", turn(1))
-        near = [joined, above, far_first, far_last, below]
+        second, parts = lax.optimization_barrier((second, parts))
+        second_above = lax.ppermute(second, "y", turn(-1))
+        second_below = lax.ppermute(second, "y", turn(1))
+
+    with jax.named_scope("own"):
+        own = own_attend(
+            hidden, entry_projection_matrix, query, after=[in_hbm(parts), second]
+        )
+
+    with jax.named_scope("store"):
+        below, second_above, own = lax.optimization_barrier((below, second_above, own))
+        far = lax.ppermute(below, "y", turn(1))
+        second_far = lax.ppermute(second_above, "y", turn(-1))
+        near = [joined, second, above, second_above, far, second_far, below, second_below]
         blocks = near + [lax.ppermute(block, "c", other(cores)) for block in near]
         blocks[0] = in_hbm(blocks[0])
-
-    with jax.named_scope("own"):
-        own = own_attend(
-            hidden, entry_projection_matrix, query, after=[in_hbm(parts), asked]
-        )
 
     with jax.named_scope("queries"):
         named = asked[:, patches, :TOPM].astype(jnp.int32)
@@ -685,7 +691,7 @@
     with jax.named_scope("memory"):
         count = asked.shape[0] // sides
         sum_beside = attend((sides - 1 - side) * count, own)
-        from_beside = lax.ppermute(sum_beside, "zp", other(sides))
+        from_beside = lax.ppermute(sum_beside, "zq", other(sides))
         sum_here = attend(side * count, sum_beside)
 
     with jax.named_scope("temporal"):

time: 144 us -> 150 us (1.042)
  starting transfers between devices: 34.1 us -> 44.4 us
  waiting for transfers between devices: 50.4 us -> 44 us
  local copies, waits for them, and re-layouts: 2.3 us -> 7.1 us
  Pallas kernels: 56.1 us -> 53 us
    ppermute x3 -> x6, waiting for transfers between devices: 12.8 us -> 28.8 us  [the longest x1 13.3 us: on_device(): second = lax.ppermute(joined, 'zp', other(sides))]
    all_to_all x4, waiting for transfers between devices: 23.9 us -> 9.76 us  [swap(): return lax.all_to_all(blocks, axes, split_axis=0, concat_axis=0, tiled=True)]
    ppermute x3 -> x6, starting transfers between devices: 3.27 us -> 10.9 us  [the longest x1 3.3 us: on_device(): from_beside = lax.ppermute(sum_beside, 'zq', other(sides))]
    ppermute x1, waiting for transfers between devices: 6.44 us -> 0.01 us  [on_device(): above = lax.ppermute(joined, 'y', turn(-1))]
    unnamed x7 -> x19, local copies, waits for them, and re-layouts: 1.16 us -> 7.1 us
    ppermute x1, waiting for transfers between devices: 3.41 us -> 0.01 us  [on_device(): below = lax.ppermute(joined, 'y', turn(1))]
    ppermute x5 -> x8, waiting for transfers between devices: 0.01 us -> 2.63 us  [on_device(): blocks = near + [lax.ppermute(block, 'c', other(cores)) for block in near]]
    ppermute x1, starting transfers between devices: 0.01 us -> 1.58 us  [on_device(): below = lax.ppermute(joined, 'y', turn(1))]
  transfers between devices with their start and end apart: 17 -> 23, of which waited for: 9 -> 9; matrix products, arithmetic and copies ran while one was open for 1% -> 0% of each run, Pallas kernels for 32% -> 30%
where the time goes in v10:
time: 150 us
  Pallas kernels  53 us (35%)
  starting transfers between devices  44.4 us (30%)
  waiting for transfers between devices  44 us (29%)
  local copies, waits for them, and re-layouts  7.1 us (5%)
    all_to_all x4, starting transfers between devices, swap(): return lax.all_to_all(blocks, axes, split_axis=0, concat_axis=0, tiled=True)  22.6 us
    pallas_call x2, Pallas kernels, memory_attend(): pl.pallas_call(functools.partial(memory_attend_kernel, count), in_specs=[...  17.1 us
    ppermute x1, waiting for transfers between devices, on_device(): second = lax.ppermute(joined, 'zp', other(sides))  13.3 us
    ppermute x1, waiting for transfers between devices, on_device(): far = lax.ppermute(below, 'y', turn(1))  9.76 us
    all_to_all x4, waiting for transfers between devices, swap(): return lax.all_to_all(blocks, axes, split_axis=0, concat_axis=0, tiled=True)  9.76 us
    pallas_call x1, Pallas kernels, temporal_entry(): pl.pallas_call(functools.partial(temporal_entry_kernel, quarters), in_spe...  8.59 us
    pallas_call x1, Pallas kernels, own_attend(): pl.pallas_call(own_attend_kernel, in_specs=[HBM, HBM, HBM] + [ANY] * len(...  8.07 us
    unnamed x19, local copies, waits for them, and re-layouts  7.1 us
  transfers between devices with their start and end apart: 23, of which 9 were waited for; matrix products, arithmetic and copies ran while one was open for 0% of the time, Pallas kernels for 30%

profile of v10, /device:TPU:0, one launch (start us, length us, event | category | flops | bytes accessed | tf_op | source)
XLA Modules:
  0.0 149.6 jit_solution(17537673829679383367)
XLA Ops:
  0.0 1.2 copy.10
  1.2 1.0 split_store.1._
  2.2 4.4 %all-to-all-start = ((bf16[4,288,256]{2,1,0:T(8,128)(2,1)}), bf16[4,288,256]{2,1,0:T(8,128)(2,1)S(1)}, u32[]{:S(2)}, u32[]{:S(2)}) async-start(bf16[4,288,256]{2,1,0:T(8,128)(2,1)} %bitcast.19), calls=%async_computation | async-start | bytes 1179648 | tf_op jit(solution)/shard_map/store/all_to_all | solution.py:626
  6.6 0.0 copy-done.7
  6.6 5.8 %modulate.1 = (bf16[576,2048]{1,0:T(8,128)(2,1)}, bf16[2,4,592,128]{3,2,1,0:T(8,128)(2,1)}) custom-call(bf16[576,2048]{1,0:T(8,128)(2,1)} %bitcast.20, f32[2,2048]{1,0:T(2,128)} %bitcast.22, bf16[2048,3072]{1,0:T(8,128)(2,1)} %weight_hbm.6, f32[2,4]{1,0:T(2,128)S(1)} %copy-done.6, s32[6]{0:T(128)S(1)} %bitcast.16, s32[6]{0:T(128)S(1)} %bitcast.17, ...), custom_call_target="tpu_custom_call" | custom-call | flops 75497472 | bytes 462848 | tf_op jit(solution)/shard_map/queries/modulate/pallas_call | solution.py:185
  12.4 4.4 %all-to-all-done.in_hbm = bf16[4,288,256]{2,1,0:T(8,128)(2,1)S(1)} async-done(((bf16[4,288,256]{2,1,0:T(8,128)(2,1)}), bf16[4,288,256]{2,1,0:T(8,128)(2,1)S(1)}, u32[]{:S(2)}, u32[]{:S(2)}) %all-to-all-start) | async-done | bytes 589856 | tf_op jit(solution)/shard_map/store/all_to_all | solution.py:626
  16.8 1.8 %join_pieces.1.refs_0_ = bf16[8,144,256]{2,1,0:T(8,128)(2,1)} custom-call(bf16[4,288,256]{2,1,0:T(8,128)(2,1)S(1)} %all-to-all-done.in_hbm, bf16[576,2048]{1,0:T(8,128)(2,1)} %get-tuple-element.18._.hidden_hbm), custom_call_target="tpu_custom_call" | custom-call | flops 18432 | bytes 73728 | tf_op jit(solution)/shard_map/store/join_pieces/pallas_call | solution.py:109
  18.5 5.8 %all-to-all-start.1 = ((bf16[8,592,128]{2,1,0:T(8,128)(2,1)}), bf16[8,592,128]{2,1,0:T(8,128)(2,1)S(1)}, u32[]{:S(2)}, u32[]{:S(2)}) async-start(bf16[8,592,128]{2,1,0:T(8,128)(2,1)} %bitcast.7), calls=%async_computation.1 | async-start | bytes 2424832 | tf_op jit(solution)/shard_map/queries/all_to_all | solution.py:626
  24.3 1.0 collective-permute-start.1
  25.3 1.6 %collective-permute-start = (bf16[8,144,256]{2,1,0:T(8,128)(2,1)}, bf16[8,144,256]{2,1,0:T(8,128)(2,1)}, u32[]{:S(2)}, u32[]{:S(2)}) collective-permute-start(bf16[8,144,256]{2,1,0:T(8,128)(2,1)} %join_pieces.1.refs_0_), channel_id=1, source_target_pairs={{0,32},{32,64},{64,96},{96,0},{1,33},{33,65},{65,97},{97,1},{2,34}... | collective-permute-start | bytes 1769480 | tf_op jit(solution)/shard_map/store/ppermute | solution.py:651
  26.9 1.7 %collective-permute-start.3 = (bf16[8,144,256]{2,1,0:T(8,128)(2,1)}, bf16[8,144,256]{2,1,0:T(8,128)(2,1)}, u32[]{:S(2)}, u32[]{:S(2)}) collective-permute-start(bf16[8,144,256]{2,1,0:T(8,128)(2,1)} %join_pieces.1.refs_0_), channel_id=1, source_target_pairs={{0,96},{32,0},{64,32},{96,64},{1,97},{33,1},{65,33},{97,65},{2,98}... | collective-permute-start | bytes 1769480 | tf_op jit(solution)/shard_map/store/ppermute | solution.py:650
  28.5 8.6 %temporal_entry.1.refs_0_ = bf16[4,4,3,144,128]{4,3,2,1,0:T(8,128)(2,1)} custom-call(bf16[576,2048]{1,0:T(8,128)(2,1)} %get-tuple-element.18._.hidden_hbm, bf16[2048,3072]{1,0:T(8,128)(2,1)} %weight_hbm.6, f32[2,4]{1,0:T(2,128)S(1)} %copy-done.6, bf16[8,144,256]{2,1,0:T(8,128)(2,1)} %join_pieces.1.refs_0_), custom_call_target="tpu_custom_call" | custom-call | flops 226492416 | bytes 651264 | tf_op jit(solution)/shard_map/temporal/temporal_entry/pallas_call | solution.py:250
  37.1 13.3 %collective-permute-done.1.refs_1_ = bf16[8,144,256]{2,1,0:T(8,128)(2,1)} collective-permute-done((bf16[8,144,256]{2,1,0:T(8,128)(2,1)}, bf16[8,144,256]{2,1,0:T(8,128)(2,1)}, u32[]{:S(2)}, u32[]{:S(2)}) %collective-permute-start.1) | collective-permute-done | bytes 589856 | tf_op jit(solution)/shard_map/store/ppermute | solution.py:652
  50.5 3.0 %collective-permute-start.2 = (bf16[8,144,256]{2,1,0:T(8,128)(2,1)}, bf16[8,144,256]{2,1,0:T(8,128)(2,1)}, u32[]{:S(2)}, u32[]{:S(2)}) collective-permute-start(bf16[8,144,256]{2,1,0:T(8,128)(2,1)} %collective-permute-done.1.refs_1_), channel_id=1, source_target_pairs={{0,96},{32,0},{64,32},{96,64},{1,97},{33,1},{65,33},{97,65},{2,98}... | collective-permute-start | bytes 1769480 | tf_op jit(solution)/shard_map/store/ppermute | solution.py:666
  53.5 0.0 collective-permute-start.7
  53.5 0.0 all-to-all-done.1.query_hbm
  53.5 7.6 %all-to-all-start.2 = ((bf16[16,3,144,128]{3,2,1,0:T(8,128)(2,1)}), bf16[16,3,144,128]{3,2,1,0:T(8,128)(2,1)S(1)}, u32[]{:S(2)}, u32[]{:S(2)}) async-start(bf16[16,3,144,128]{3,2,1,0:T(8,128)(2,1)} %bitcast.18), calls=%async_computation.2 | async-start | bytes 3538944 | tf_op jit(solution)/shard_map/temporal/all_to_all | solution.py:626
  61.1 0.3 collective-permute-start.6
  61.4 8.1 %own_attend.1.refs_16_.own_hbm = bf16[4,592,128]{2,1,0:T(8,128)(2,1)} custom-call(bf16[576,2048]{1,0:T(8,128)(2,1)} %get-tuple-element.18._.hidden_hbm, bf16[2048,3072]{1,0:T(8,128)(2,1)} %weight_hbm.6, bf16[2,4,592,128]{3,2,1,0:T(8,128)(2,1)} %get-tuple-element.24.query_hbm, bf16[4,4,3,144,128]{4,3,2,1,0:T(8,128)(2,1)} %temporal_entry.1.refs_0_, ...), custom_call_target="tpu_custom_call" | custom-call | flops 214695936 | bytes 593920 | tf_op jit(solution)/shard_map/own/own_attend/pallas_call | solution.py:380
  69.5 0.0 collective-permute-done.refs_6_
  69.5 0.3 collective-permute-start.8
  69.8 0.0 collective-permute-done.3.refs_2_
  69.8 0.3 collective-permute-start.9
  70.1 0.0 collective-permute-done.2.refs_3_
  70.1 0.6 collective-permute-start.4
  70.7 0.0 collective-permute-done.7.refs_8_
  70.7 2.7 %collective-permute-start.5 = (bf16[8,144,256]{2,1,0:T(8,128)(2,1)}, bf16[8,144,256]{2,1,0:T(8,128)(2,1)}, u32[]{:S(2)}, u32[]{:S(2)}) collective-permute-start(bf16[8,144,256]{2,1,0:T(8,128)(2,1)} %collective-permute-done.2.refs_3_), channel_id=1, source_target_pairs={{0,96},{32,0},{64,32},{96,64},{1,97},{33,1},{65,33},{97,65},{2,98}... | collective-permute-start | bytes 1769480 | tf_op jit(solution)/shard_map/store/ppermute | solution.py:677
  73.4 5.7 %collective-permute-done.6.refs_7_ = bf16[8,144,256]{2,1,0:T(8,128)(2,1)} collective-permute-done((bf16[8,144,256]{2,1,0:T(8,128)(2,1)}, bf16[8,144,256]{2,1,0:T(8,128)(2,1)}, u32[]{:S(2)}, u32[]{:S(2)}) %collective-permute-start.6) | collective-permute-done | bytes 589856 | tf_op jit(solution)/shard_map/store/ppermute | solution.py:667
  79.1 0.0 collective-permute-start.10
  79.1 0.0 collective-permute-done.8.refs_9_
  79.1 0.8 copy-done
  79.9 0.5 collective-permute-start.13
  80.4 0.0 collective-permute-done.9.refs_10_
  80.4 0.8 copy-done.3
  81.2 0.0 collective-permute-start.14
  81.2 9.8 %collective-permute-done.4.refs_4_ = bf16[8,144,256]{2,1,0:T(8,128)(2,1)} collective-permute-done((bf16[8,144,256]{2,1,0:T(8,128)(2,1)}, bf16[8,144,256]{2,1,0:T(8,128)(2,1)}, u32[]{:S(2)}, u32[]{:S(2)}) %collective-permute-start.4) | collective-permute-done | bytes 589856 | tf_op jit(solution)/shard_map/store/ppermute | solution.py:676
  91.0 0.0 collective-permute-start.11
  91.0 0.0 collective-permute-done.5.refs_5_
  91.0 0.5 collective-permute-start.12
  91.6 0.0 collective-permute-done.10.refs_11_
  91.6 0.0 collective-permute-done.13.refs_14_
  91.6 0.0 collective-permute-done.14.refs_15_
  91.6 1.8 %collective-permute-done.11.refs_12_ = bf16[8,144,256]{2,1,0:T(8,128)(2,1)} collective-permute-done((bf16[8,144,256]{2,1,0:T(8,128)(2,1)}, bf16[8,144,256]{2,1,0:T(8,128)(2,1)}, u32[]{:S(2)}, u32[]{:S(2)}) %collective-permute-start.11) | collective-permute-done | bytes 589856 | tf_op jit(solution)/shard_map/store/ppermute | solution.py:679
  93.4 0.8 collective-permute-done.12.refs_13_
  94.2 1.1 copy-done.1
  95.3 1.1 copy-done.4
  96.3 8.5 %memory_attend.2.refs_16_ = bf16[4,592,128]{2,1,0:T(8,128)(2,1)} custom-call(s32[1]{0:T(128)} %bitcast.9.base_ref, s32[8,6]{1,0:T(8,128)S(1)} %fusion.6.index_ref, bf16[8,592,128]{2,1,0:T(8,128)(2,1)S(1)} %all-to-all-done.1.query_hbm, bf16[8,144,256]{2,1,0:T(8,128)(2,1)} %join_pieces.1.refs_0_, bf16[8,144,256]{2,1,0:T(8,128)(2,1)} %collective-permute-done.1.refs_1_, ...), custom_call_target="tpu_custom_call" | custom-call | flops 261881856 | bytes 186368 | tf_op jit(solution)/shard_map/memory/memory_attend/pallas_call | solution.py:449
  104.9 3.3 %collective-permute-start.15 = (bf16[4,592,128]{2,1,0:T(8,128)(2,1)}, bf16[4,592,128]{2,1,0:T(8,128)(2,1)}, u32[]{:S(2)}, u32[]{:S(2)}) collective-permute-start(bf16[4,592,128]{2,1,0:T(8,128)(2,1)} %memory_attend.2.refs_16_), channel_id=1, source_target_pairs={{0,8},{8,0},{1,9},{9,1},{2,10},{10,2},{3,11},{11,3},{4,12},{12,4},... | collective-permute-start | bytes 1818632 | tf_op jit(solution)/shard_map/memory/ppermute | solution.py:694
  108.8 1.1 copy-done.2
  109.9 1.1 copy-done.5
  110.9 8.6 %memory_attend.3.refs_0_._ = bf16[4,592,128]{2,1,0:T(8,128)(2,1)} custom-call(s32[1]{0:T(128)} %bitcast.6.base_ref, s32[8,6]{1,0:T(8,128)S(1)} %fusion.6.index_ref, bf16[8,592,128]{2,1,0:T(8,128)(2,1)S(1)} %all-to-all-done.1.query_hbm, bf16[8,144,256]{2,1,0:T(8,128)(2,1)} %join_pieces.1.refs_0_, bf16[8,144,256]{2,1,0:T(8,128)(2,1)} %collective-permute-done.1.refs_1_, ...), custom_call_target="tpu_custom_call" | custom-call | flops 261881856 | bytes 186368 | tf_op jit(solution)/shard_map/memory/memory_attend/pallas_call | solution.py:449
  119.6 0.0 all-to-all-done.2.in_hbm_ref
  119.6 2.4 %temporal_attend.1 = bf16[16,144,128]{2,1,0:T(8,128)(2,1)} custom-call(s32[1]{0:T(128)S(6)} %copy.11.length_ref, bf16[16,3,144,128]{3,2,1,0:T(8,128)(2,1)S(1)} %all-to-all-done.2.in_hbm_ref, bf16[4,592,128]{2,1,0:T(8,128)(2,1)} %memory_attend.3.refs_0_._), custom_call_target="tpu_custom_call" | custom-call | flops 18874368 | bytes 147456 | tf_op jit(solution)/shard_map/temporal/temporal_attend/pallas_call | solution.py:300
  122.0 4.8 %all-to-all-start.3 = ((bf16[16,144,128]{2,1,0:T(8,128)(2,1)}), bf16[16,144,128]{2,1,0:T(8,128)(2,1)S(1)}, u32[]{:S(2)}, u32[]{:S(2)}) async-start(bf16[16,144,128]{2,1,0:T(8,128)(2,1)} %temporal_attend.1), calls=%async_computation.3 | async-start | bytes 1179648 | tf_op jit(solution)/shard_map/temporal/all_to_all | solution.py:626
  126.8 0.0 collective-permute-done.15.refs_1_
  126.8 2.2 %add_partials.1 = (bf16[592,128]{1,0:T(8,128)(2,1)}, bf16[592,128]{1,0:T(8,128)(2,1)}, bf16[592,128]{1,0:T(8,128)(2,1)}, bf16[592,128]{1,0:T(8,128)(2,1)}) custom-call(s32[1]{0:T(128)} %bitcast.x_ref, bf16[4,592,128]{2,1,0:T(8,128)(2,1)} %memory_attend.3.refs_0_._, bf16[4,592,128]{2,1,0:T(8,128)(2,1)} %collective-permute-done.15.refs_1_), custom_call_target="tpu_custom_call" | custom-call | flops 75776 | bytes 151552 | tf_op jit(solution)/shard_map/memory/add_partials/pallas_call | solution.py:501
  129.0 2.0 %collective-permute-start.16 = (bf16[592,128]{1,0:T(8,128)(2,1)}, bf16[592,128]{1,0:T(8,128)(2,1)S(1)}, u32[]{:S(2)}, u32[]{:S(2)}) collective-permute-start(bf16[592,128]{1,0:T(8,128)(2,1)} %get-tuple-element.28), channel_id=1, source_target_pairs={{0,1},{1,2},{2,3},{3,0},{4,5},{5,6},{6,7},{7,4},{8,9},{9,10},{10,1... | collective-permute-start | bytes 454664 | tf_op jit(solution)/shard_map/memory/ppermute | solution.py:629
  131.0 2.7 %collective-permute-start.17 = (bf16[592,128]{1,0:T(8,128)(2,1)}, bf16[592,128]{1,0:T(8,128)(2,1)S(1)}, u32[]{:S(2)}, u32[]{:S(2)}) collective-permute-start(bf16[592,128]{1,0:T(8,128)(2,1)} %get-tuple-element.29), channel_id=1, source_target_pairs={{0,2},{1,3},{2,0},{3,1},{4,6},{5,7},{6,4},{7,5},{8,10},{9,11},{10,... | collective-permute-start | bytes 454664 | tf_op jit(solution)/shard_map/memory/ppermute | solution.py:629
  133.6 1.5 collective-permute-start.18
  135.1 5.4 %all-to-all-done.3.time_hbm = bf16[16,144,128]{2,1,0:T(8,128)(2,1)S(1)} async-done(((bf16[16,144,128]{2,1,0:T(8,128)(2,1)}), bf16[16,144,128]{2,1,0:T(8,128)(2,1)S(1)}, u32[]{:S(2)}, u32[]{:S(2)}) %all-to-all-start.3) | async-done | bytes 589856 | tf_op jit(solution)/shard_map/temporal/all_to_all | solution.py:626
  140.5 0.5 collective-permute-done.16.memory_1
  140.9 2.3 %collective-permute-done.17.memory_2 = bf16[592,128]{1,0:T(8,128)(2,1)S(1)} collective-permute-done((bf16[592,128]{1,0:T(8,128)(2,1)}, bf16[592,128]{1,0:T(8,128)(2,1)S(1)}, u32[]{:S(2)}, u32[]{:S(2)}) %collective-permute-start.17) | collective-permute-done | bytes 151584 | tf_op jit(solution)/shard_map/memory/ppermute | solution.py:629
  143.3 0.0 collective-permute-done.18.memory_3
  143.3 6.1 %leave.1 = bf16[576,2048]{1,0:T(8,128)(2,1)} custom-call(s32[1]{0:T(128)} %bitcast.x_ref, bf16[4,592,128]{2,1,0:T(8,128)(2,1)} %own_attend.1.refs_16_.own_hbm, bf16[592,128]{1,0:T(8,128)(2,1)} %get-tuple-element.27.memory_0, bf16[592,128]{1,0:T(8,128)(2,1)S(1)} %collective-permute-done.16.memory_1, bf16[592,128]{1,0:T(8,128)(2,1)S(1)} %collective-permute-done.17.memory_2, ...), custom_call_target="tpu_custom_call" | custom-call | flops 150994944 | bytes 630784 | tf_op jit(solution)/shard_map/exit/leave/pallas_call | solution.py:572
  (13 shorter events, 0.0 us)
Async XLA Ops:
  0.0 6.6 %copy-start.7 = (s32[1,1,6,1]{2,3,1,0:T(1,128)S(1)}, s32[1,1,6,1]{2,3,1,0:T(1,128)}, u32[]{:S(2)}) copy-start(s32[1,1,6,1]{2,3,1,0:T(1,128)} %param.15) | copy-start | bytes 76
  0.0 6.6 %copy-start.8 = (s32[1,1,6]{2,1,0:T(1,128)S(1)}, s32[1,1,6]{2,1,0:T(1,128)}, u32[]{:S(2)}) copy-start(s32[1,1,6]{2,1,0:T(1,128)} %param.16) | copy-start | bytes 76
  0.0 6.6 %copy-start.6 = (f32[2,4]{1,0:T(2,128)S(1)}, f32[2,4]{1,0:T(2,128)}, u32[]{:S(2)}) copy-start(f32[2,4]{1,0:T(2,128)} %sharpness_ref.3) | copy-start | bytes 100
  2.2 14.6 %all-to-all-start = ((bf16[4,288,256]{2,1,0:T(8,128)(2,1)}), bf16[4,288,256]{2,1,0:T(8,128)(2,1)S(1)}, u32[]{:S(2)}, u32[]{:S(2)}) async-start(bf16[4,288,256]{2,1,0:T(8,128)(2,1)} %bitcast.19), calls=%async_computation | async-start | bytes 1179648 | tf_op jit(solution)/shard_map/store/all_to_all | solution.py:626
  18.5 35.0 %all-to-all-start.1 = ((bf16[8,592,128]{2,1,0:T(8,128)(2,1)}), bf16[8,592,128]{2,1,0:T(8,128)(2,1)S(1)}, u32[]{:S(2)}, u32[]{:S(2)}) async-start(bf16[8,592,128]{2,1,0:T(8,128)(2,1)} %bitcast.7), calls=%async_computation.1 | async-start | bytes 2424832 | tf_op jit(solution)/shard_map/queries/all_to_all | solution.py:626
  24.3 26.2 %collective-permute-start.1 = (bf16[8,144,256]{2,1,0:T(8,128)(2,1)}, bf16[8,144,256]{2,1,0:T(8,128)(2,1)}, u32[]{:S(2)}, u32[]{:S(2)}) collective-permute-start(bf16[8,144,256]{2,1,0:T(8,128)(2,1)} %join_pieces.1.refs_0_), channel_id=1, source_target_pairs={{0,4},{4,0},{1,5},{5,1},{2,6},{6,2},{3,7},{7,3},{8,12},{12,8},{9,1... | collective-permute-start | bytes 1769480 | tf_op jit(solution)/shard_map/store/ppermute | solution.py:652
  25.3 44.2 %collective-permute-start = (bf16[8,144,256]{2,1,0:T(8,128)(2,1)}, bf16[8,144,256]{2,1,0:T(8,128)(2,1)}, u32[]{:S(2)}, u32[]{:S(2)}) collective-permute-start(bf16[8,144,256]{2,1,0:T(8,128)(2,1)} %join_pieces.1.refs_0_), channel_id=1, source_target_pairs={{0,32},{32,64},{64,96},{96,0},{1,33},{33,65},{65,97},{97,1},{2,34}... | collective-permute-start | bytes 1769480 | tf_op jit(solution)/shard_map/store/ppermute | solution.py:651
  26.9 42.9 %collective-permute-start.3 = (bf16[8,144,256]{2,1,0:T(8,128)(2,1)}, bf16[8,144,256]{2,1,0:T(8,128)(2,1)}, u32[]{:S(2)}, u32[]{:S(2)}) collective-permute-start(bf16[8,144,256]{2,1,0:T(8,128)(2,1)} %join_pieces.1.refs_0_), channel_id=1, source_target_pairs={{0,96},{32,0},{64,32},{96,64},{1,97},{33,1},{65,33},{97,65},{2,98}... | collective-permute-start | bytes 1769480 | tf_op jit(solution)/shard_map/store/ppermute | solution.py:650
  50.5 19.6 %collective-permute-start.2 = (bf16[8,144,256]{2,1,0:T(8,128)(2,1)}, bf16[8,144,256]{2,1,0:T(8,128)(2,1)}, u32[]{:S(2)}, u32[]{:S(2)}) collective-permute-start(bf16[8,144,256]{2,1,0:T(8,128)(2,1)} %collective-permute-done.1.refs_1_), channel_id=1, source_target_pairs={{0,96},{32,0},{64,32},{96,64},{1,97},{33,1},{65,33},{97,65},{2,98}... | collective-permute-start | bytes 1769480 | tf_op jit(solution)/shard_map/store/ppermute | solution.py:666
  53.5 17.2 %collective-permute-start.7 = (bf16[8,144,256]{2,1,0:T(8,128)(2,1)}, bf16[8,144,256]{2,1,0:T(8,128)(2,1)}, u32[]{:S(2)}, u32[]{:S(2)}) collective-permute-start(bf16[8,144,256]{2,1,0:T(8,128)(2,1)} %join_pieces.1.refs_0_), channel_id=1, source_target_pairs={{0,16},{16,0},{1,17},{17,1},{2,18},{18,2},{3,19},{19,3},{4,20},{20... | collective-permute-start | bytes 1769480 | tf_op jit(solution)/shard_map/store/ppermute | solution.py:679
  53.5 66.1 %all-to-all-start.2 = ((bf16[16,3,144,128]{3,2,1,0:T(8,128)(2,1)}), bf16[16,3,144,128]{3,2,1,0:T(8,128)(2,1)S(1)}, u32[]{:S(2)}, u32[]{:S(2)}) async-start(bf16[16,3,144,128]{3,2,1,0:T(8,128)(2,1)} %bitcast.18), calls=%async_computation.2 | async-start | bytes 3538944 | tf_op jit(solution)/shard_map/temporal/all_to_all | solution.py:626
  61.1 17.9 %collective-permute-start.6 = (bf16[8,144,256]{2,1,0:T(8,128)(2,1)}, bf16[8,144,256]{2,1,0:T(8,128)(2,1)}, u32[]{:S(2)}, u32[]{:S(2)}) collective-permute-start(bf16[8,144,256]{2,1,0:T(8,128)(2,1)} %collective-permute-done.1.refs_1_), channel_id=1, source_target_pairs={{0,32},{32,64},{64,96},{96,0},{1,33},{33,65},{65,97},{97,1},{2,34}... | collective-permute-start | bytes 1769480 | tf_op jit(solution)/shard_map/store/ppermute | solution.py:667
  69.5 9.6 %collective-permute-start.8 = (bf16[8,144,256]{2,1,0:T(8,128)(2,1)}, bf16[8,144,256]{2,1,0:T(8,128)(2,1)S(1)}, u32[]{:S(2)}, u32[]{:S(2)}) collective-permute-start(bf16[8,144,256]{2,1,0:T(8,128)(2,1)} %collective-permute-done.1.refs_1_), channel_id=1, source_target_pairs={{0,16},{16,0},{1,17},{17,1},{2,18},{18,2},{3,19},{19,3},{4,20},{20... | collective-permute-start | bytes 1769480 | tf_op jit(solution)/shard_map/store/ppermute | solution.py:679
  69.8 10.6 %collective-permute-start.9 = (bf16[8,144,256]{2,1,0:T(8,128)(2,1)}, bf16[8,144,256]{2,1,0:T(8,128)(2,1)S(1)}, u32[]{:S(2)}, u32[]{:S(2)}) collective-permute-start(bf16[8,144,256]{2,1,0:T(8,128)(2,1)} %collective-permute-done.3.refs_2_), channel_id=1, source_target_pairs={{0,16},{16,0},{1,17},{17,1},{2,18},{18,2},{3,19},{19,3},{4,20},{20... | collective-permute-start | bytes 1769480 | tf_op jit(solution)/shard_map/store/ppermute | solution.py:679
  70.1 20.9 %collective-permute-start.4 = (bf16[8,144,256]{2,1,0:T(8,128)(2,1)}, bf16[8,144,256]{2,1,0:T(8,128)(2,1)}, u32[]{:S(2)}, u32[]{:S(2)}) collective-permute-start(bf16[8,144,256]{2,1,0:T(8,128)(2,1)} %collective-permute-done.refs_6_), channel_id=1, source_target_pairs={{0,32},{32,64},{64,96},{96,0},{1,33},{33,65},{65,97},{97,1},{2,34}... | collective-permute-start | bytes 1769480 | tf_op jit(solution)/shard_map/store/ppermute | solution.py:676
  70.7 20.4 %collective-permute-start.5 = (bf16[8,144,256]{2,1,0:T(8,128)(2,1)}, bf16[8,144,256]{2,1,0:T(8,128)(2,1)}, u32[]{:S(2)}, u32[]{:S(2)}) collective-permute-start(bf16[8,144,256]{2,1,0:T(8,128)(2,1)} %collective-permute-done.2.refs_3_), channel_id=1, source_target_pairs={{0,96},{32,0},{64,32},{96,64},{1,97},{33,1},{65,33},{97,65},{2,98}... | collective-permute-start | bytes 1769480 | tf_op jit(solution)/shard_map/store/ppermute | solution.py:677
  79.1 12.5 %collective-permute-start.10 = (bf16[8,144,256]{2,1,0:T(8,128)(2,1)}, bf16[8,144,256]{2,1,0:T(8,128)(2,1)}, u32[]{:S(2)}, u32[]{:S(2)}) collective-permute-start(bf16[8,144,256]{2,1,0:T(8,128)(2,1)} %collective-permute-done.2.refs_3_), channel_id=1, source_target_pairs={{0,16},{16,0},{1,17},{17,1},{2,18},{18,2},{3,19},{19,3},{4,20},{20... | collective-permute-start | bytes 1769480 | tf_op jit(solution)/shard_map/store/ppermute | solution.py:679
  79.1 0.8 copy-start
  79.9 11.7 %collective-permute-start.13 = (bf16[8,144,256]{2,1,0:T(8,128)(2,1)}, bf16[8,144,256]{2,1,0:T(8,128)(2,1)}, u32[]{:S(2)}, u32[]{:S(2)}) collective-permute-start(bf16[8,144,256]{2,1,0:T(8,128)(2,1)} %collective-permute-done.refs_6_), channel_id=1, source_target_pairs={{0,16},{16,0},{1,17},{17,1},{2,18},{18,2},{3,19},{19,3},{4,20},{20... | collective-permute-start | bytes 1769480 | tf_op jit(solution)/shard_map/store/ppermute | solution.py:679
  80.4 0.8 copy-start.3
  81.2 10.3 %collective-permute-start.14 = (bf16[8,144,256]{2,1,0:T(8,128)(2,1)}, bf16[8,144,256]{2,1,0:T(8,128)(2,1)}, u32[]{:S(2)}, u32[]{:S(2)}) collective-permute-start(bf16[8,144,256]{2,1,0:T(8,128)(2,1)} %collective-permute-done.6.refs_7_), channel_id=1, source_target_pairs={{0,16},{16,0},{1,17},{17,1},{2,18},{18,2},{3,19},{19,3},{4,20},{20... | collective-permute-start | bytes 1769480 | tf_op jit(solution)/shard_map/store/ppermute | solution.py:679
  91.0 2.3 %collective-permute-start.11 = (bf16[8,144,256]{2,1,0:T(8,128)(2,1)}, bf16[8,144,256]{2,1,0:T(8,128)(2,1)}, u32[]{:S(2)}, u32[]{:S(2)}) collective-permute-start(bf16[8,144,256]{2,1,0:T(8,128)(2,1)} %collective-permute-done.4.refs_4_), channel_id=1, source_target_pairs={{0,16},{16,0},{1,17},{17,1},{2,18},{18,2},{3,19},{19,3},{4,20},{20... | collective-permute-start | bytes 1769480 | tf_op jit(solution)/shard_map/store/ppermute | solution.py:679
  91.0 3.2 %collective-permute-start.12 = (bf16[8,144,256]{2,1,0:T(8,128)(2,1)}, bf16[8,144,256]{2,1,0:T(8,128)(2,1)}, u32[]{:S(2)}, u32[]{:S(2)}) collective-permute-start(bf16[8,144,256]{2,1,0:T(8,128)(2,1)} %collective-permute-done.5.refs_5_), channel_id=1, source_target_pairs={{0,16},{16,0},{1,17},{17,1},{2,18},{18,2},{3,19},{19,3},{4,20},{20... | collective-permute-start | bytes 1769480 | tf_op jit(solution)/shard_map/store/ppermute | solution.py:679
  94.2 1.1 copy-start.1
  95.3 1.1 copy-start.4
  104.9 22.0 %collective-permute-start.15 = (bf16[4,592,128]{2,1,0:T(8,128)(2,1)}, bf16[4,592,128]{2,1,0:T(8,128)(2,1)}, u32[]{:S(2)}, u32[]{:S(2)}) collective-permute-start(bf16[4,592,128]{2,1,0:T(8,128)(2,1)} %memory_attend.2.refs_16_), channel_id=1, source_target_pairs={{0,8},{8,0},{1,9},{9,1},{2,10},{10,2},{3,11},{11,3},{4,12},{12,4},... | collective-permute-start | bytes 1818632 | tf_op jit(solution)/shard_map/memory/ppermute | solution.py:694
  108.8 1.1 copy-start.2
  109.9 1.1 copy-start.5
  122.0 18.5 %all-to-all-start.3 = ((bf16[16,144,128]{2,1,0:T(8,128)(2,1)}), bf16[16,144,128]{2,1,0:T(8,128)(2,1)S(1)}, u32[]{:S(2)}, u32[]{:S(2)}) async-start(bf16[16,144,128]{2,1,0:T(8,128)(2,1)} %temporal_attend.1), calls=%async_computation.3 | async-start | bytes 1179648 | tf_op jit(solution)/shard_map/temporal/all_to_all | solution.py:626
  129.0 12.0 %collective-permute-start.16 = (bf16[592,128]{1,0:T(8,128)(2,1)}, bf16[592,128]{1,0:T(8,128)(2,1)S(1)}, u32[]{:S(2)}, u32[]{:S(2)}) collective-permute-start(bf16[592,128]{1,0:T(8,128)(2,1)} %get-tuple-element.28), channel_id=1, source_target_pairs={{0,1},{1,2},{2,3},{3,0},{4,5},{5,6},{6,7},{7,4},{8,9},{9,10},{10,1... | collective-permute-start | bytes 454664 | tf_op jit(solution)/shard_map/memory/ppermute | solution.py:629
  131.0 12.3 %collective-permute-start.17 = (bf16[592,128]{1,0:T(8,128)(2,1)}, bf16[592,128]{1,0:T(8,128)(2,1)S(1)}, u32[]{:S(2)}, u32[]{:S(2)}) collective-permute-start(bf16[592,128]{1,0:T(8,128)(2,1)} %get-tuple-element.29), channel_id=1, source_target_pairs={{0,2},{1,3},{2,0},{3,1},{4,6},{5,7},{6,4},{7,5},{8,10},{9,11},{10,... | collective-permute-start | bytes 454664 | tf_op jit(solution)/shard_map/memory/ppermute | solution.py:629
  133.6 9.6 %collective-permute-start.18 = (bf16[592,128]{1,0:T(8,128)(2,1)}, bf16[592,128]{1,0:T(8,128)(2,1)S(1)}, u32[]{:S(2)}, u32[]{:S(2)}) collective-permute-start(bf16[592,128]{1,0:T(8,128)(2,1)} %get-tuple-element.30), channel_id=1, source_target_pairs={{0,3},{1,0},{2,1},{3,2},{4,7},{5,4},{6,5},{7,6},{8,11},{9,8},{10,9... | collective-permute-start | bytes 454664 | tf_op jit(solution)/shard_map/memory/ppermute | solution.py:629

commit v11 on v10

--- a/solution.py
+++ b/solution.py
@@ -652,7 +652,7 @@
         second = lax.ppermute(joined, "zp", other(sides))
 
     with jax.named_scope("queries"):
-        asked, joined = lax.optimization_barrier((query, joined))
+        asked, second = lax.optimization_barrier((query, second))
         asked = swap(asked.reshape((-1,) + asked.shape[2:]), ("zq", "x"))
 
     with jax.named_scope("temporal"):
@@ -677,7 +677,7 @@
         second_far = lax.ppermute(second_above, "y", turn(-1))
         near = [joined, second, above, second_above, far, second_far, below, second_below]
         blocks = near + [lax.ppermute(block, "c", other(cores)) for block in near]
-        blocks[0] = in_hbm(blocks[0])
+        blocks = [in_hbm(block) for block in blocks]
 
     with jax.named_scope("queries"):
         named = asked[:, patches, :TOPM].astype(jnp.int32)

time: 150 us -> 144 us (0.960)
  local copies, waits for them, and re-layouts: 7.1 us -> 1.2 us
  waiting for transfers between devices: 44 us -> 47.1 us
  starting transfers between devices: 44.4 us -> 41.8 us
    unnamed x19 -> x7, local copies, waits for them, and re-layouts: 7.1 us -> 1.2 us
    all_to_all x4, starting transfers between devices: 22.6 us -> 19.3 us  [swap(): return lax.all_to_all(blocks, axes, split_axis=0, concat_axis=0, tiled=True)]
    all_to_all x4, waiting for transfers between devices: 9.76 us -> 12.9 us  [swap(): return lax.all_to_all(blocks, axes, split_axis=0, concat_axis=0, tiled=True)]
    ppermute x1, waiting for transfers between devices: 9.76 us -> 11.3 us  [on_device(): far = lax.ppermute(below, 'y', turn(1))]
  transfers between devices with their start and end apart: 23 -> 23, of which waited for: 9 -> 10; matrix products, arithmetic and copies ran while one was open for 0% -> 0% of each run, Pallas kernels for 30% -> 30%
where the time goes in v11:
time: 144 us
  Pallas kernels  52.4 us (36%)
  waiting for transfers between devices  47.1 us (33%)
  starting transfers between devices  41.8 us (29%)
    all_to_all x4, starting transfers between devices, swap(): return lax.all_to_all(blocks, axes, split_axis=0, concat_axis=0, tiled=True)  19.3 us
    pallas_call x2, Pallas kernels, memory_attend(): pl.pallas_call(functools.partial(memory_attend_kernel, count), in_specs=[...  16.5 us
    all_to_all x4, waiting for transfers between devices, swap(): return lax.all_to_all(blocks, axes, split_axis=0, concat_axis=0, tiled=True)  12.9 us
    ppermute x1, waiting for transfers between devices, on_device(): second = lax.ppermute(joined, 'zp', other(sides))  12.5 us
    ppermute x1, waiting for transfers between devices, on_device(): far = lax.ppermute(below, 'y', turn(1))  11.3 us
    pallas_call x1, Pallas kernels, temporal_entry(): pl.pallas_call(functools.partial(temporal_entry_kernel, quarters), in_spe...  8.58 us
    pallas_call x1, Pallas kernels, own_attend(): pl.pallas_call(own_attend_kernel, in_specs=[HBM, HBM, HBM] + [ANY] * len(...  8.07 us
    ppermute x3, starting transfers between devices, swap_apart(): lax.ppermute(blocks[j], 'x', turn(j))  6.13 us
  transfers between devices with their start and end apart: 23, of which 10 were waited for; matrix products, arithmetic and copies ran while one was open for 0% of the time, Pallas kernels for 30%

profile of v11, /device:TPU:0, one launch (start us, length us, event | category | flops | bytes accessed | tf_op | source)
XLA Modules:
  0.0 143.5 jit_solution(9943804046682109801)
XLA Ops:
  0.0 0.0 copy-start.1
  0.0 0.0 copy-start.2
  0.0 0.0 copy-start
  0.0 1.2 copy.10
  1.2 1.0 split_store.1._
  2.2 4.4 %all-to-all-start = ((bf16[4,288,256]{2,1,0:T(8,128)(2,1)}), bf16[4,288,256]{2,1,0:T(8,128)(2,1)S(1)}, u32[]{:S(2)}, u32[]{:S(2)}) async-start(bf16[4,288,256]{2,1,0:T(8,128)(2,1)} %bitcast.19), calls=%async_computation | async-start | bytes 1179648 | tf_op jit(solution)/shard_map/store/all_to_all | solution.py:626
  6.6 0.0 copy-done.1
  6.6 0.0 copy-done.2
  6.6 0.0 copy-done
  6.6 5.8 %modulate.1 = (bf16[576,2048]{1,0:T(8,128)(2,1)}, bf16[2,4,592,128]{3,2,1,0:T(8,128)(2,1)}) custom-call(bf16[576,2048]{1,0:T(8,128)(2,1)} %bitcast.20, f32[2,2048]{1,0:T(2,128)} %bitcast.22, bf16[2048,3072]{1,0:T(8,128)(2,1)} %weight_hbm.6, f32[2,4]{1,0:T(2,128)S(1)} %copy-done, s32[6]{0:T(128)S(1)} %bitcast.16, s32[6]{0:T(128)S(1)} %bitcast.17, ...), custom_call_target="tpu_custom_call" | custom-call | flops 75497472 | bytes 462848 | tf_op jit(solution)/shard_map/queries/modulate/pallas_call | solution.py:185
  12.4 4.4 %all-to-all-done.in_hbm = bf16[4,288,256]{2,1,0:T(8,128)(2,1)S(1)} async-done(((bf16[4,288,256]{2,1,0:T(8,128)(2,1)}), bf16[4,288,256]{2,1,0:T(8,128)(2,1)S(1)}, u32[]{:S(2)}, u32[]{:S(2)}) %all-to-all-start) | async-done | bytes 589856 | tf_op jit(solution)/shard_map/store/all_to_all | solution.py:626
  16.8 1.7 %join_pieces.1.refs_0_ = bf16[8,144,256]{2,1,0:T(8,128)(2,1)} custom-call(bf16[4,288,256]{2,1,0:T(8,128)(2,1)S(1)} %all-to-all-done.in_hbm, bf16[576,2048]{1,0:T(8,128)(2,1)} %get-tuple-element.18._.hidden_hbm), custom_call_target="tpu_custom_call" | custom-call | flops 18432 | bytes 73728 | tf_op jit(solution)/shard_map/store/join_pieces/pallas_call | solution.py:109
  18.5 2.0 %collective-permute-start.1 = (bf16[8,144,256]{2,1,0:T(8,128)(2,1)}, bf16[8,144,256]{2,1,0:T(8,128)(2,1)}, u32[]{:S(2)}, u32[]{:S(2)}) collective-permute-start(bf16[8,144,256]{2,1,0:T(8,128)(2,1)} %join_pieces.1.refs_0_), channel_id=1, source_target_pairs={{0,4},{4,0},{1,5},{5,1},{2,6},{6,2},{3,7},{7,3},{8,12},{12,8},{9,1... | collective-permute-start | bytes 1769480 | tf_op jit(solution)/shard_map/store/ppermute | solution.py:652
  20.5 12.5 %collective-permute-done.1.refs_1_ = bf16[8,144,256]{2,1,0:T(8,128)(2,1)} collective-permute-done((bf16[8,144,256]{2,1,0:T(8,128)(2,1)}, bf16[8,144,256]{2,1,0:T(8,128)(2,1)}, u32[]{:S(2)}, u32[]{:S(2)}) %collective-permute-start.1) | collective-permute-done | bytes 589856 | tf_op jit(solution)/shard_map/store/ppermute | solution.py:652
  33.0 5.6 %all-to-all-start.1 = ((bf16[8,592,128]{2,1,0:T(8,128)(2,1)}), bf16[8,592,128]{2,1,0:T(8,128)(2,1)S(1)}, u32[]{:S(2)}, u32[]{:S(2)}) async-start(bf16[8,592,128]{2,1,0:T(8,128)(2,1)} %bitcast.7), calls=%async_computation.1 | async-start | bytes 2424832 | tf_op jit(solution)/shard_map/queries/all_to_all | solution.py:626
  38.5 1.6 %collective-permute-start = (bf16[8,144,256]{2,1,0:T(8,128)(2,1)}, bf16[8,144,256]{2,1,0:T(8,128)(2,1)}, u32[]{:S(2)}, u32[]{:S(2)}) collective-permute-start(bf16[8,144,256]{2,1,0:T(8,128)(2,1)} %join_pieces.1.refs_0_), channel_id=1, source_target_pairs={{0,32},{32,64},{64,96},{96,0},{1,33},{33,65},{65,97},{97,1},{2,34}... | collective-permute-start | bytes 1769480 | tf_op jit(solution)/shard_map/store/ppermute | solution.py:651
  40.1 1.7 %collective-permute-start.3 = (bf16[8,144,256]{2,1,0:T(8,128)(2,1)}, bf16[8,144,256]{2,1,0:T(8,128)(2,1)}, u32[]{:S(2)}, u32[]{:S(2)}) collective-permute-start(bf16[8,144,256]{2,1,0:T(8,128)(2,1)} %join_pieces.1.refs_0_), channel_id=1, source_target_pairs={{0,96},{32,0},{64,32},{96,64},{1,97},{33,1},{65,33},{97,65},{2,98}... | collective-permute-start | bytes 1769480 | tf_op jit(solution)/shard_map/store/ppermute | solution.py:650
  41.8 8.6 %temporal_entry.1.refs_0_ = bf16[4,4,3,144,128]{4,3,2,1,0:T(8,128)(2,1)} custom-call(bf16[576,2048]{1,0:T(8,128)(2,1)} %get-tuple-element.18._.hidden_hbm, bf16[2048,3072]{1,0:T(8,128)(2,1)} %weight_hbm.6, f32[2,4]{1,0:T(2,128)S(1)} %copy-done, bf16[8,144,256]{2,1,0:T(8,128)(2,1)} %join_pieces.1.refs_0_), custom_call_target="tpu_custom_call" | custom-call | flops 226492416 | bytes 651264 | tf_op jit(solution)/shard_map/temporal/temporal_entry/pallas_call | solution.py:250
  50.4 1.9 %collective-permute-start.2 = (bf16[8,144,256]{2,1,0:T(8,128)(2,1)}, bf16[8,144,256]{2,1,0:T(8,128)(2,1)}, u32[]{:S(2)}, u32[]{:S(2)}) collective-permute-start(bf16[8,144,256]{2,1,0:T(8,128)(2,1)} %collective-permute-done.1.refs_1_), channel_id=1, source_target_pairs={{0,96},{32,0},{64,32},{96,64},{1,97},{33,1},{65,33},{97,65},{2,98}... | collective-permute-start | bytes 1769480 | tf_op jit(solution)/shard_map/store/ppermute | solution.py:666
  52.2 0.0 collective-permute-start.7
  52.2 3.2 %all-to-all-done.1.query_hbm = bf16[8,592,128]{2,1,0:T(8,128)(2,1)S(1)} async-done(((bf16[8,592,128]{2,1,0:T(8,128)(2,1)}), bf16[8,592,128]{2,1,0:T(8,128)(2,1)S(1)}, u32[]{:S(2)}, u32[]{:S(2)}) %all-to-all-start.1) | async-done | bytes 1212448 | tf_op jit(solution)/shard_map/queries/all_to_all | solution.py:626
  55.4 4.3 %all-to-all-start.2 = ((bf16[16,3,144,128]{3,2,1,0:T(8,128)(2,1)}), bf16[16,3,144,128]{3,2,1,0:T(8,128)(2,1)S(1)}, u32[]{:S(2)}, u32[]{:S(2)}) async-start(bf16[16,3,144,128]{3,2,1,0:T(8,128)(2,1)} %bitcast.18), calls=%async_computation.2 | async-start | bytes 3538944 | tf_op jit(solution)/shard_map/temporal/all_to_all | solution.py:626
  59.7 1.2 collective-permute-start.6
  60.9 8.1 %own_attend.1.refs_16_.own_hbm = bf16[4,592,128]{2,1,0:T(8,128)(2,1)} custom-call(bf16[576,2048]{1,0:T(8,128)(2,1)} %get-tuple-element.18._.hidden_hbm, bf16[2048,3072]{1,0:T(8,128)(2,1)} %weight_hbm.6, bf16[2,4,592,128]{3,2,1,0:T(8,128)(2,1)} %get-tuple-element.24.query_hbm, bf16[4,4,3,144,128]{4,3,2,1,0:T(8,128)(2,1)} %temporal_entry.1.refs_0_, ...), custom_call_target="tpu_custom_call" | custom-call | flops 214695936 | bytes 593920 | tf_op jit(solution)/shard_map/own/own_attend/pallas_call | solution.py:380
  69.0 0.0 collective-permute-done.refs_6_
  69.0 0.1 collective-permute-start.8
  69.1 0.0 collective-permute-done.3.refs_2_
  69.1 0.5 collective-permute-start.9
  69.6 0.0 collective-permute-done.2.refs_3_
  69.6 1.6 %collective-permute-start.4 = (bf16[8,144,256]{2,1,0:T(8,128)(2,1)}, bf16[8,144,256]{2,1,0:T(8,128)(2,1)}, u32[]{:S(2)}, u32[]{:S(2)}) collective-permute-start(bf16[8,144,256]{2,1,0:T(8,128)(2,1)} %collective-permute-done.refs_6_), channel_id=1, source_target_pairs={{0,32},{32,64},{64,96},{96,0},{1,33},{33,65},{65,97},{97,1},{2,34}... | collective-permute-start | bytes 1769480 | tf_op jit(solution)/shard_map/store/ppermute | solution.py:676
  71.2 0.0 collective-permute-done.7.refs_8_
  71.2 1.7 %collective-permute-start.5 = (bf16[8,144,256]{2,1,0:T(8,128)(2,1)}, bf16[8,144,256]{2,1,0:T(8,128)(2,1)}, u32[]{:S(2)}, u32[]{:S(2)}) collective-permute-start(bf16[8,144,256]{2,1,0:T(8,128)(2,1)} %collective-permute-done.2.refs_3_), channel_id=1, source_target_pairs={{0,96},{32,0},{64,32},{96,64},{1,97},{33,1},{65,33},{97,65},{2,98}... | collective-permute-start | bytes 1769480 | tf_op jit(solution)/shard_map/store/ppermute | solution.py:677
  72.9 4.8 %collective-permute-done.6.refs_7_ = bf16[8,144,256]{2,1,0:T(8,128)(2,1)} collective-permute-done((bf16[8,144,256]{2,1,0:T(8,128)(2,1)}, bf16[8,144,256]{2,1,0:T(8,128)(2,1)}, u32[]{:S(2)}, u32[]{:S(2)}) %collective-permute-start.6) | collective-permute-done | bytes 589856 | tf_op jit(solution)/shard_map/store/ppermute | solution.py:667
  77.7 0.0 collective-permute-start.10
  77.7 0.0 collective-permute-done.8.refs_9_
  77.7 0.5 collective-permute-start.13
  78.2 0.0 collective-permute-done.9.refs_10_
  78.2 0.1 collective-permute-start.14
  78.3 11.3 %collective-permute-done.4.refs_4_ = bf16[8,144,256]{2,1,0:T(8,128)(2,1)} collective-permute-done((bf16[8,144,256]{2,1,0:T(8,128)(2,1)}, bf16[8,144,256]{2,1,0:T(8,128)(2,1)}, u32[]{:S(2)}, u32[]{:S(2)}) %collective-permute-start.4) | collective-permute-done | bytes 589856 | tf_op jit(solution)/shard_map/store/ppermute | solution.py:676
  89.6 0.0 collective-permute-start.11
  89.6 0.0 collective-permute-done.5.refs_5_
  89.6 0.5 collective-permute-start.12
  90.1 0.0 collective-permute-done.10.refs_11_
  90.1 0.0 collective-permute-done.13.refs_14_
  90.2 0.0 collective-permute-done.14.refs_15_
  90.2 1.8 %collective-permute-done.11.refs_12_ = bf16[8,144,256]{2,1,0:T(8,128)(2,1)} collective-permute-done((bf16[8,144,256]{2,1,0:T(8,128)(2,1)}, bf16[8,144,256]{2,1,0:T(8,128)(2,1)}, u32[]{:S(2)}, u32[]{:S(2)}) %collective-permute-start.11) | collective-permute-done | bytes 589856 | tf_op jit(solution)/shard_map/store/ppermute | solution.py:679
  91.9 0.8 collective-permute-done.12.refs_13_
  92.8 8.2 %memory_attend.2.refs_16_ = bf16[4,592,128]{2,1,0:T(8,128)(2,1)} custom-call(s32[1]{0:T(128)} %bitcast.9.base_ref, s32[8,6]{1,0:T(8,128)S(1)} %fusion.6.index_ref, bf16[8,592,128]{2,1,0:T(8,128)(2,1)S(1)} %all-to-all-done.1.query_hbm, bf16[8,144,256]{2,1,0:T(8,128)(2,1)} %join_pieces.1.refs_0_, bf16[8,144,256]{2,1,0:T(8,128)(2,1)} %collective-permute-done.1.refs_1_, ...), custom_call_target="tpu_custom_call" | custom-call | flops 261881856 | bytes 186368 | tf_op jit(solution)/shard_map/memory/memory_attend/pallas_call | solution.py:449
  101.0 3.2 %collective-permute-start.15 = (bf16[4,592,128]{2,1,0:T(8,128)(2,1)}, bf16[4,592,128]{2,1,0:T(8,128)(2,1)}, u32[]{:S(2)}, u32[]{:S(2)}) collective-permute-start(bf16[4,592,128]{2,1,0:T(8,128)(2,1)} %memory_attend.2.refs_16_), channel_id=1, source_target_pairs={{0,8},{8,0},{1,9},{9,1},{2,10},{10,2},{3,11},{11,3},{4,12},{12,4},... | collective-permute-start | bytes 1818632 | tf_op jit(solution)/shard_map/memory/ppermute | solution.py:694
  104.9 8.2 %memory_attend.3.refs_0_._ = bf16[4,592,128]{2,1,0:T(8,128)(2,1)} custom-call(s32[1]{0:T(128)} %bitcast.6.base_ref, s32[8,6]{1,0:T(8,128)S(1)} %fusion.6.index_ref, bf16[8,592,128]{2,1,0:T(8,128)(2,1)S(1)} %all-to-all-done.1.query_hbm, bf16[8,144,256]{2,1,0:T(8,128)(2,1)} %join_pieces.1.refs_0_, bf16[8,144,256]{2,1,0:T(8,128)(2,1)} %collective-permute-done.1.refs_1_, ...), custom_call_target="tpu_custom_call" | custom-call | flops 261881856 | bytes 186368 | tf_op jit(solution)/shard_map/memory/memory_attend/pallas_call | solution.py:449
  113.2 0.0 all-to-all-done.2.in_hbm_ref
  113.2 2.4 %temporal_attend.1 = bf16[16,144,128]{2,1,0:T(8,128)(2,1)} custom-call(s32[1]{0:T(128)S(6)} %copy.11.length_ref, bf16[16,3,144,128]{3,2,1,0:T(8,128)(2,1)S(1)} %all-to-all-done.2.in_hbm_ref, bf16[4,592,128]{2,1,0:T(8,128)(2,1)} %memory_attend.3.refs_0_._), custom_call_target="tpu_custom_call" | custom-call | flops 18874368 | bytes 147456 | tf_op jit(solution)/shard_map/temporal/temporal_attend/pallas_call | solution.py:300
  115.6 5.0 %all-to-all-start.3 = ((bf16[16,144,128]{2,1,0:T(8,128)(2,1)}), bf16[16,144,128]{2,1,0:T(8,128)(2,1)S(1)}, u32[]{:S(2)}, u32[]{:S(2)}) async-start(bf16[16,144,128]{2,1,0:T(8,128)(2,1)} %temporal_attend.1), calls=%async_computation.3 | async-start | bytes 1179648 | tf_op jit(solution)/shard_map/temporal/all_to_all | solution.py:626
  120.6 0.0 collective-permute-done.15.refs_1_
  120.6 2.2 %add_partials.1 = (bf16[592,128]{1,0:T(8,128)(2,1)}, bf16[592,128]{1,0:T(8,128)(2,1)}, bf16[592,128]{1,0:T(8,128)(2,1)}, bf16[592,128]{1,0:T(8,128)(2,1)}) custom-call(s32[1]{0:T(128)} %bitcast.x_ref, bf16[4,592,128]{2,1,0:T(8,128)(2,1)} %memory_attend.3.refs_0_._, bf16[4,592,128]{2,1,0:T(8,128)(2,1)} %collective-permute-done.15.refs_1_), custom_call_target="tpu_custom_call" | custom-call | flops 75776 | bytes 151552 | tf_op jit(solution)/shard_map/memory/add_partials/pallas_call | solution.py:501
  122.8 2.0 %collective-permute-start.16 = (bf16[592,128]{1,0:T(8,128)(2,1)}, bf16[592,128]{1,0:T(8,128)(2,1)S(1)}, u32[]{:S(2)}, u32[]{:S(2)}) collective-permute-start(bf16[592,128]{1,0:T(8,128)(2,1)} %get-tuple-element.28), channel_id=1, source_target_pairs={{0,1},{1,2},{2,3},{3,0},{4,5},{5,6},{6,7},{7,4},{8,9},{9,10},{10,1... | collective-permute-start | bytes 454664 | tf_op jit(solution)/shard_map/memory/ppermute | solution.py:629
  124.8 2.7 %collective-permute-start.17 = (bf16[592,128]{1,0:T(8,128)(2,1)}, bf16[592,128]{1,0:T(8,128)(2,1)S(1)}, u32[]{:S(2)}, u32[]{:S(2)}) collective-permute-start(bf16[592,128]{1,0:T(8,128)(2,1)} %get-tuple-element.29), channel_id=1, source_target_pairs={{0,2},{1,3},{2,0},{3,1},{4,6},{5,7},{6,4},{7,5},{8,10},{9,11},{10,... | collective-permute-start | bytes 454664 | tf_op jit(solution)/shard_map/memory/ppermute | solution.py:629
  127.4 1.5 %collective-permute-start.18 = (bf16[592,128]{1,0:T(8,128)(2,1)}, bf16[592,128]{1,0:T(8,128)(2,1)S(1)}, u32[]{:S(2)}, u32[]{:S(2)}) collective-permute-start(bf16[592,128]{1,0:T(8,128)(2,1)} %get-tuple-element.30), channel_id=1, source_target_pairs={{0,3},{1,0},{2,1},{3,2},{4,7},{5,4},{6,5},{7,6},{8,11},{9,8},{10,9... | collective-permute-start | bytes 454664 | tf_op jit(solution)/shard_map/memory/ppermute | solution.py:629
  128.9 5.3 %all-to-all-done.3.time_hbm = bf16[16,144,128]{2,1,0:T(8,128)(2,1)S(1)} async-done(((bf16[16,144,128]{2,1,0:T(8,128)(2,1)}), bf16[16,144,128]{2,1,0:T(8,128)(2,1)S(1)}, u32[]{:S(2)}, u32[]{:S(2)}) %all-to-all-start.3) | async-done | bytes 589856 | tf_op jit(solution)/shard_map/temporal/all_to_all | solution.py:626
  134.2 0.5 collective-permute-done.16.memory_1
  134.7 2.5 %collective-permute-done.17.memory_2 = bf16[592,128]{1,0:T(8,128)(2,1)S(1)} collective-permute-done((bf16[592,128]{1,0:T(8,128)(2,1)}, bf16[592,128]{1,0:T(8,128)(2,1)S(1)}, u32[]{:S(2)}, u32[]{:S(2)}) %collective-permute-start.17) | collective-permute-done | bytes 151584 | tf_op jit(solution)/shard_map/memory/ppermute | solution.py:629
  137.2 0.0 collective-permute-done.18.memory_3
  137.2 6.1 %leave.1 = bf16[576,2048]{1,0:T(8,128)(2,1)} custom-call(s32[1]{0:T(128)} %bitcast.x_ref, bf16[4,592,128]{2,1,0:T(8,128)(2,1)} %own_attend.1.refs_16_.own_hbm, bf16[592,128]{1,0:T(8,128)(2,1)} %get-tuple-element.27.memory_0, bf16[592,128]{1,0:T(8,128)(2,1)S(1)} %collective-permute-done.16.memory_1, bf16[592,128]{1,0:T(8,128)(2,1)S(1)} %collective-permute-done.17.memory_2, ...), custom_call_target="tpu_custom_call" | custom-call | flops 150994944 | bytes 630784 | tf_op jit(solution)/shard_map/exit/leave/pallas_call | solution.py:572
  (2 shorter events, 0.0 us)
Async XLA Ops:
  0.0 6.6 %copy-start.1 = (s32[1,1,6,1]{2,3,1,0:T(1,128)S(1)}, s32[1,1,6,1]{2,3,1,0:T(1,128)}, u32[]{:S(2)}) copy-start(s32[1,1,6,1]{2,3,1,0:T(1,128)} %param.15) | copy-start | bytes 76
  0.0 6.6 %copy-start.2 = (s32[1,1,6]{2,1,0:T(1,128)S(1)}, s32[1,1,6]{2,1,0:T(1,128)}, u32[]{:S(2)}) copy-start(s32[1,1,6]{2,1,0:T(1,128)} %param.16) | copy-start | bytes 76
  0.0 6.6 %copy-start = (f32[2,4]{1,0:T(2,128)S(1)}, f32[2,4]{1,0:T(2,128)}, u32[]{:S(2)}) copy-start(f32[2,4]{1,0:T(2,128)} %sharpness_ref.3) | copy-start | bytes 100
  2.2 14.6 %all-to-all-start = ((bf16[4,288,256]{2,1,0:T(8,128)(2,1)}), bf16[4,288,256]{2,1,0:T(8,128)(2,1)S(1)}, u32[]{:S(2)}, u32[]{:S(2)}) async-start(bf16[4,288,256]{2,1,0:T(8,128)(2,1)} %bitcast.19), calls=%async_computation | async-start | bytes 1179648 | tf_op jit(solution)/shard_map/store/all_to_all | solution.py:626
  18.5 14.5 %collective-permute-start.1 = (bf16[8,144,256]{2,1,0:T(8,128)(2,1)}, bf16[8,144,256]{2,1,0:T(8,128)(2,1)}, u32[]{:S(2)}, u32[]{:S(2)}) collective-permute-start(bf16[8,144,256]{2,1,0:T(8,128)(2,1)} %join_pieces.1.refs_0_), channel_id=1, source_target_pairs={{0,4},{4,0},{1,5},{5,1},{2,6},{6,2},{3,7},{7,3},{8,12},{12,8},{9,1... | collective-permute-start | bytes 1769480 | tf_op jit(solution)/shard_map/store/ppermute | solution.py:652
  33.0 22.4 %all-to-all-start.1 = ((bf16[8,592,128]{2,1,0:T(8,128)(2,1)}), bf16[8,592,128]{2,1,0:T(8,128)(2,1)S(1)}, u32[]{:S(2)}, u32[]{:S(2)}) async-start(bf16[8,592,128]{2,1,0:T(8,128)(2,1)} %bitcast.7), calls=%async_computation.1 | async-start | bytes 2424832 | tf_op jit(solution)/shard_map/queries/all_to_all | solution.py:626
  38.5 30.5 %collective-permute-start = (bf16[8,144,256]{2,1,0:T(8,128)(2,1)}, bf16[8,144,256]{2,1,0:T(8,128)(2,1)}, u32[]{:S(2)}, u32[]{:S(2)}) collective-permute-start(bf16[8,144,256]{2,1,0:T(8,128)(2,1)} %join_pieces.1.refs_0_), channel_id=1, source_target_pairs={{0,32},{32,64},{64,96},{96,0},{1,33},{33,65},{65,97},{97,1},{2,34}... | collective-permute-start | bytes 1769480 | tf_op jit(solution)/shard_map/store/ppermute | solution.py:651
  40.1 29.0 %collective-permute-start.3 = (bf16[8,144,256]{2,1,0:T(8,128)(2,1)}, bf16[8,144,256]{2,1,0:T(8,128)(2,1)}, u32[]{:S(2)}, u32[]{:S(2)}) collective-permute-start(bf16[8,144,256]{2,1,0:T(8,128)(2,1)} %join_pieces.1.refs_0_), channel_id=1, source_target_pairs={{0,96},{32,0},{64,32},{96,64},{1,97},{33,1},{65,33},{97,65},{2,98}... | collective-permute-start | bytes 1769480 | tf_op jit(solution)/shard_map/store/ppermute | solution.py:650
  50.4 19.3 %collective-permute-start.2 = (bf16[8,144,256]{2,1,0:T(8,128)(2,1)}, bf16[8,144,256]{2,1,0:T(8,128)(2,1)}, u32[]{:S(2)}, u32[]{:S(2)}) collective-permute-start(bf16[8,144,256]{2,1,0:T(8,128)(2,1)} %collective-permute-done.1.refs_1_), channel_id=1, source_target_pairs={{0,96},{32,0},{64,32},{96,64},{1,97},{33,1},{65,33},{97,65},{2,98}... | collective-permute-start | bytes 1769480 | tf_op jit(solution)/shard_map/store/ppermute | solution.py:666
  52.2 19.0 %collective-permute-start.7 = (bf16[8,144,256]{2,1,0:T(8,128)(2,1)}, bf16[8,144,256]{2,1,0:T(8,128)(2,1)}, u32[]{:S(2)}, u32[]{:S(2)}) collective-permute-start(bf16[8,144,256]{2,1,0:T(8,128)(2,1)} %join_pieces.1.refs_0_), channel_id=1, source_target_pairs={{0,16},{16,0},{1,17},{17,1},{2,18},{18,2},{3,19},{19,3},{4,20},{20... | collective-permute-start | bytes 1769480 | tf_op jit(solution)/shard_map/store/ppermute | solution.py:679
  55.4 57.8 %all-to-all-start.2 = ((bf16[16,3,144,128]{3,2,1,0:T(8,128)(2,1)}), bf16[16,3,144,128]{3,2,1,0:T(8,128)(2,1)S(1)}, u32[]{:S(2)}, u32[]{:S(2)}) async-start(bf16[16,3,144,128]{3,2,1,0:T(8,128)(2,1)} %bitcast.18), calls=%async_computation.2 | async-start | bytes 3538944 | tf_op jit(solution)/shard_map/temporal/all_to_all | solution.py:626
  59.7 17.9 %collective-permute-start.6 = (bf16[8,144,256]{2,1,0:T(8,128)(2,1)}, bf16[8,144,256]{2,1,0:T(8,128)(2,1)}, u32[]{:S(2)}, u32[]{:S(2)}) collective-permute-start(bf16[8,144,256]{2,1,0:T(8,128)(2,1)} %collective-permute-done.1.refs_1_), channel_id=1, source_target_pairs={{0,32},{32,64},{64,96},{96,0},{1,33},{33,65},{65,97},{97,1},{2,34}... | collective-permute-start | bytes 1769480 | tf_op jit(solution)/shard_map/store/ppermute | solution.py:667
  69.0 8.6 %collective-permute-start.8 = (bf16[8,144,256]{2,1,0:T(8,128)(2,1)}, bf16[8,144,256]{2,1,0:T(8,128)(2,1)}, u32[]{:S(2)}, u32[]{:S(2)}) collective-permute-start(bf16[8,144,256]{2,1,0:T(8,128)(2,1)} %collective-permute-done.1.refs_1_), channel_id=1, source_target_pairs={{0,16},{16,0},{1,17},{17,1},{2,18},{18,2},{3,19},{19,3},{4,20},{20... | collective-permute-start | bytes 1769480 | tf_op jit(solution)/shard_map/store/ppermute | solution.py:679
  69.1 9.0 %collective-permute-start.9 = (bf16[8,144,256]{2,1,0:T(8,128)(2,1)}, bf16[8,144,256]{2,1,0:T(8,128)(2,1)}, u32[]{:S(2)}, u32[]{:S(2)}) collective-permute-start(bf16[8,144,256]{2,1,0:T(8,128)(2,1)} %collective-permute-done.3.refs_2_), channel_id=1, source_target_pairs={{0,16},{16,0},{1,17},{17,1},{2,18},{18,2},{3,19},{19,3},{4,20},{20... | collective-permute-start | bytes 1769480 | tf_op jit(solution)/shard_map/store/ppermute | solution.py:679
  69.6 20.0 %collective-permute-start.4 = (bf16[8,144,256]{2,1,0:T(8,128)(2,1)}, bf16[8,144,256]{2,1,0:T(8,128)(2,1)}, u32[]{:S(2)}, u32[]{:S(2)}) collective-permute-start(bf16[8,144,256]{2,1,0:T(8,128)(2,1)} %collective-permute-done.refs_6_), channel_id=1, source_target_pairs={{0,32},{32,64},{64,96},{96,0},{1,33},{33,65},{65,97},{97,1},{2,34}... | collective-permute-start | bytes 1769480 | tf_op jit(solution)/shard_map/store/ppermute | solution.py:676
  71.2 18.4 %collective-permute-start.5 = (bf16[8,144,256]{2,1,0:T(8,128)(2,1)}, bf16[8,144,256]{2,1,0:T(8,128)(2,1)}, u32[]{:S(2)}, u32[]{:S(2)}) collective-permute-start(bf16[8,144,256]{2,1,0:T(8,128)(2,1)} %collective-permute-done.2.refs_3_), channel_id=1, source_target_pairs={{0,96},{32,0},{64,32},{96,64},{1,97},{33,1},{65,33},{97,65},{2,98}... | collective-permute-start | bytes 1769480 | tf_op jit(solution)/shard_map/store/ppermute | solution.py:677
  77.7 12.5 %collective-permute-start.10 = (bf16[8,144,256]{2,1,0:T(8,128)(2,1)}, bf16[8,144,256]{2,1,0:T(8,128)(2,1)}, u32[]{:S(2)}, u32[]{:S(2)}) collective-permute-start(bf16[8,144,256]{2,1,0:T(8,128)(2,1)} %collective-permute-done.2.refs_3_), channel_id=1, source_target_pairs={{0,16},{16,0},{1,17},{17,1},{2,18},{18,2},{3,19},{19,3},{4,20},{20... | collective-permute-start | bytes 1769480 | tf_op jit(solution)/shard_map/store/ppermute | solution.py:679
  77.7 12.5 %collective-permute-start.13 = (bf16[8,144,256]{2,1,0:T(8,128)(2,1)}, bf16[8,144,256]{2,1,0:T(8,128)(2,1)}, u32[]{:S(2)}, u32[]{:S(2)}) collective-permute-start(bf16[8,144,256]{2,1,0:T(8,128)(2,1)} %collective-permute-done.refs_6_), channel_id=1, source_target_pairs={{0,16},{16,0},{1,17},{17,1},{2,18},{18,2},{3,19},{19,3},{4,20},{20... | collective-permute-start | bytes 1769480 | tf_op jit(solution)/shard_map/store/ppermute | solution.py:679
  78.2 12.0 %collective-permute-start.14 = (bf16[8,144,256]{2,1,0:T(8,128)(2,1)}, bf16[8,144,256]{2,1,0:T(8,128)(2,1)}, u32[]{:S(2)}, u32[]{:S(2)}) collective-permute-start(bf16[8,144,256]{2,1,0:T(8,128)(2,1)} %collective-permute-done.6.refs_7_), channel_id=1, source_target_pairs={{0,16},{16,0},{1,17},{17,1},{2,18},{18,2},{3,19},{19,3},{4,20},{20... | collective-permute-start | bytes 1769480 | tf_op jit(solution)/shard_map/store/ppermute | solution.py:679
  89.6 2.3 %collective-permute-start.11 = (bf16[8,144,256]{2,1,0:T(8,128)(2,1)}, bf16[8,144,256]{2,1,0:T(8,128)(2,1)}, u32[]{:S(2)}, u32[]{:S(2)}) collective-permute-start(bf16[8,144,256]{2,1,0:T(8,128)(2,1)} %collective-permute-done.4.refs_4_), channel_id=1, source_target_pairs={{0,16},{16,0},{1,17},{17,1},{2,18},{18,2},{3,19},{19,3},{4,20},{20... | collective-permute-start | bytes 1769480 | tf_op jit(solution)/shard_map/store/ppermute | solution.py:679
  89.6 3.2 %collective-permute-start.12 = (bf16[8,144,256]{2,1,0:T(8,128)(2,1)}, bf16[8,144,256]{2,1,0:T(8,128)(2,1)}, u32[]{:S(2)}, u32[]{:S(2)}) collective-permute-start(bf16[8,144,256]{2,1,0:T(8,128)(2,1)} %collective-permute-done.5.refs_5_), channel_id=1, source_target_pairs={{0,16},{16,0},{1,17},{17,1},{2,18},{18,2},{3,19},{19,3},{4,20},{20... | collective-permute-start | bytes 1769480 | tf_op jit(solution)/shard_map/store/ppermute | solution.py:679
  101.0 19.6 %collective-permute-start.15 = (bf16[4,592,128]{2,1,0:T(8,128)(2,1)}, bf16[4,592,128]{2,1,0:T(8,128)(2,1)}, u32[]{:S(2)}, u32[]{:S(2)}) collective-permute-start(bf16[4,592,128]{2,1,0:T(8,128)(2,1)} %memory_attend.2.refs_16_), channel_id=1, source_target_pairs={{0,8},{8,0},{1,9},{9,1},{2,10},{10,2},{3,11},{11,3},{4,12},{12,4},... | collective-permute-start | bytes 1818632 | tf_op jit(solution)/shard_map/memory/ppermute | solution.py:694
  115.6 18.6 %all-to-all-start.3 = ((bf16[16,144,128]{2,1,0:T(8,128)(2,1)}), bf16[16,144,128]{2,1,0:T(8,128)(2,1)S(1)}, u32[]{:S(2)}, u32[]{:S(2)}) async-start(bf16[16,144,128]{2,1,0:T(8,128)(2,1)} %temporal_attend.1), calls=%async_computation.3 | async-start | bytes 1179648 | tf_op jit(solution)/shard_map/temporal/all_to_all | solution.py:626
  122.8 11.9 %collective-permute-start.16 = (bf16[592,128]{1,0:T(8,128)(2,1)}, bf16[592,128]{1,0:T(8,128)(2,1)S(1)}, u32[]{:S(2)}, u32[]{:S(2)}) collective-permute-start(bf16[592,128]{1,0:T(8,128)(2,1)} %get-tuple-element.28), channel_id=1, source_target_pairs={{0,1},{1,2},{2,3},{3,0},{4,5},{5,6},{6,7},{7,4},{8,9},{9,10},{10,1... | collective-permute-start | bytes 454664 | tf_op jit(solution)/shard_map/memory/ppermute | solution.py:629
  124.8 12.5 %collective-permute-start.17 = (bf16[592,128]{1,0:T(8,128)(2,1)}, bf16[592,128]{1,0:T(8,128)(2,1)S(1)}, u32[]{:S(2)}, u32[]{:S(2)}) collective-permute-start(bf16[592,128]{1,0:T(8,128)(2,1)} %get-tuple-element.29), channel_id=1, source_target_pairs={{0,2},{1,3},{2,0},{3,1},{4,6},{5,7},{6,4},{7,5},{8,10},{9,11},{10,... | collective-permute-start | bytes 454664 | tf_op jit(solution)/shard_map/memory/ppermute | solution.py:629
  127.4 9.8 %collective-permute-start.18 = (bf16[592,128]{1,0:T(8,128)(2,1)}, bf16[592,128]{1,0:T(8,128)(2,1)S(1)}, u32[]{:S(2)}, u32[]{:S(2)}) collective-permute-start(bf16[592,128]{1,0:T(8,128)(2,1)} %get-tuple-element.30), channel_id=1, source_target_pairs={{0,3},{1,0},{2,1},{3,2},{4,7},{5,4},{6,5},{7,6},{8,11},{9,8},{10,9... | collective-permute-start | bytes 454664 | tf_op jit(solution)/shard_map/memory/ppermute | solution.py:629

commit v12 on v11

--- a/solution.py
+++ b/solution.py
@@ -651,8 +651,11 @@
         below = lax.ppermute(joined, "y", turn(1))
         second = lax.ppermute(joined, "zp", other(sides))
 
+        second_above = lax.ppermute(second, "y", turn(-1))
+        second_below = lax.ppermute(second, "y", turn(1))
+
     with jax.named_scope("queries"):
-        asked, second = lax.optimization_barrier((query, second))
+        asked, second, above, below = lax.optimization_barrier((query, second, above, below))
         asked = swap(asked.reshape((-1,) + asked.shape[2:]), ("zq", "x"))
 
     with jax.named_scope("temporal"):
@@ -661,18 +664,13 @@
         )
         sent = swap(parts.reshape((quarters * G,) + parts.shape[2:]), frame)
 
-    with jax.named_scope("store"):
-        second, parts = lax.optimization_barrier((second, parts))
-        second_above = lax.ppermute(second, "y", turn(-1))
-        second_below = lax.ppermute(second, "y", turn(1))
-
     with jax.named_scope("own"):
         own = own_attend(
-            hidden, entry_projection_matrix, query, after=[in_hbm(parts), second]
+            hidden, entry_projection_matrix, query, after=[in_hbm(parts)]
         )
 
     with jax.named_scope("store"):
-        below, second_above, own = lax.optimization_barrier((below, second_above, own))
+        below, second_above, parts = lax.optimization_barrier((below, second_above, parts))
         far = lax.ppermute(below, "y", turn(1))
         second_far = lax.ppermute(second_above, "y", turn(-1))
         near = [joined, second, above, second_above, far, second_far, below, second_below]

time: 144 us -> 154 us (1.069)
  waiting for transfers between devices: 47.1 us -> 60.6 us
  starting transfers between devices: 41.8 us -> 38.5 us
    ppermute x1, waiting for transfers between devices: 4.79 us -> 14.4 us  [on_device(): second_below = lax.ppermute(second, 'y', turn(1))]
    all_to_all x4, waiting for transfers between devices: 12.9 us -> 17.4 us  [swap(): return lax.all_to_all(blocks, axes, split_axis=0, concat_axis=0, tiled=True)]
    ppermute x1, waiting for transfers between devices: 0.01 us -> 3.41 us  [on_device(): below = lax.ppermute(joined, 'y', turn(1))]
    ppermute x1, waiting for transfers between devices: 12.5 us -> 9.44 us  [on_device(): second = lax.ppermute(joined, 'zp', other(sides))]
    ppermute x8, waiting for transfers between devices: 2.63 us -> 0.02 us  [on_device(): blocks = near + [lax.ppermute(block, 'c', other(cores)) for block in near]]
    ppermute x1, waiting for transfers between devices: 0.01 us -> 1.99 us  [on_device(): above = lax.ppermute(joined, 'y', turn(-1))]
    ppermute x1, starting transfers between devices: 1.66 us -> 3.29 us  [on_device(): second_far = lax.ppermute(second_above, 'y', turn(-1))]
    ppermute x1, starting transfers between devices: 1.87 us -> 0.28 us  [on_device(): second_above = lax.ppermute(second, 'y', turn(-1))]
  transfers between devices with their start and end apart: 23 -> 23, of which waited for: 10 -> 10; matrix products, arithmetic and copies ran while one was open for 0% -> 0% of each run, Pallas kernels for 30% -> 28%
where the time goes in v12:
time: 154 us
  waiting for transfers between devices  60.6 us (39%)
  Pallas kernels  52.4 us (34%)
  starting transfers between devices  38.5 us (25%)
    all_to_all x4, starting transfers between devices, swap(): return lax.all_to_all(blocks, axes, split_axis=0, concat_axis=0, tiled=True)  18.5 us
    all_to_all x4, waiting for transfers between devices, swap(): return lax.all_to_all(blocks, axes, split_axis=0, concat_axis=0, tiled=True)  17.4 us
    pallas_call x2, Pallas kernels, memory_attend(): pl.pallas_call(functools.partial(memory_attend_kernel, count), in_specs=[...  16.5 us
    ppermute x1, waiting for transfers between devices, on_device(): second_below = lax.ppermute(second, 'y', turn(1))  14.4 us
    ppermute x1, waiting for transfers between devices, on_device(): far = lax.ppermute(below, 'y', turn(1))  11.2 us
    ppermute x1, waiting for transfers between devices, on_device(): second = lax.ppermute(joined, 'zp', other(sides))  9.44 us
    pallas_call x1, Pallas kernels, temporal_entry(): pl.pallas_call(functools.partial(temporal_entry_kernel, quarters), in_spe...  8.58 us
    pallas_call x1, Pallas kernels, own_attend(): pl.pallas_call(own_attend_kernel, in_specs=[HBM, HBM, HBM] + [ANY] * len(...  8.07 us
  transfers between devices with their start and end apart: 23, of which 10 were waited for; matrix products, arithmetic and copies ran while one was open for 0% of the time, Pallas kernels for 28%

profile of v12, /device:TPU:0, one launch (start us, length us, event | category | flops | bytes accessed | tf_op | source)
XLA Modules:
  0.0 153.8 jit_solution(14053352270838709285)
XLA Ops:
  0.0 0.0 copy-start
  0.0 0.0 copy-start.1
  0.0 0.0 copy-start.2
  0.0 1.2 copy.10
  1.2 1.0 split_store.1._
  2.2 4.4 %all-to-all-start = ((bf16[4,288,256]{2,1,0:T(8,128)(2,1)}), bf16[4,288,256]{2,1,0:T(8,128)(2,1)S(1)}, u32[]{:S(2)}, u32[]{:S(2)}) async-start(bf16[4,288,256]{2,1,0:T(8,128)(2,1)} %bitcast.19), calls=%async_computation | async-start | bytes 1179648 | tf_op jit(solution)/shard_map/store/all_to_all | solution.py:626
  6.6 0.0 copy-done
  6.6 0.0 copy-done.1
  6.6 0.0 copy-done.2
  6.6 5.8 %modulate.1 = (bf16[576,2048]{1,0:T(8,128)(2,1)}, bf16[2,4,592,128]{3,2,1,0:T(8,128)(2,1)}) custom-call(bf16[576,2048]{1,0:T(8,128)(2,1)} %bitcast.20, f32[2,2048]{1,0:T(2,128)} %bitcast.22, bf16[2048,3072]{1,0:T(8,128)(2,1)} %weight_hbm.6, f32[2,4]{1,0:T(2,128)S(1)} %copy-done, s32[6]{0:T(128)S(1)} %bitcast.16, s32[6]{0:T(128)S(1)} %bitcast.17, ...), custom_call_target="tpu_custom_call" | custom-call | flops 75497472 | bytes 462848 | tf_op jit(solution)/shard_map/queries/modulate/pallas_call | solution.py:185
  12.4 4.4 %all-to-all-done.in_hbm = bf16[4,288,256]{2,1,0:T(8,128)(2,1)S(1)} async-done(((bf16[4,288,256]{2,1,0:T(8,128)(2,1)}), bf16[4,288,256]{2,1,0:T(8,128)(2,1)S(1)}, u32[]{:S(2)}, u32[]{:S(2)}) %all-to-all-start) | async-done | bytes 589856 | tf_op jit(solution)/shard_map/store/all_to_all | solution.py:626
  16.8 1.7 %join_pieces.1.refs_0_ = bf16[8,144,256]{2,1,0:T(8,128)(2,1)} custom-call(bf16[4,288,256]{2,1,0:T(8,128)(2,1)S(1)} %all-to-all-done.in_hbm, bf16[576,2048]{1,0:T(8,128)(2,1)} %get-tuple-element.17._.hidden_hbm), custom_call_target="tpu_custom_call" | custom-call | flops 18432 | bytes 73728 | tf_op jit(solution)/shard_map/store/join_pieces/pallas_call | solution.py:109
  18.5 2.0 %collective-permute-start = (bf16[8,144,256]{2,1,0:T(8,128)(2,1)}, bf16[8,144,256]{2,1,0:T(8,128)(2,1)}, u32[]{:S(2)}, u32[]{:S(2)}) collective-permute-start(bf16[8,144,256]{2,1,0:T(8,128)(2,1)} %join_pieces.1.refs_0_), channel_id=1, source_target_pairs={{0,4},{4,0},{1,5},{5,1},{2,6},{6,2},{3,7},{7,3},{8,12},{12,8},{9,1... | collective-permute-start | bytes 1769480 | tf_op jit(solution)/shard_map/store/ppermute | solution.py:652
  20.5 3.0 %collective-permute-start.1 = (bf16[8,144,256]{2,1,0:T(8,128)(2,1)}, bf16[8,144,256]{2,1,0:T(8,128)(2,1)}, u32[]{:S(2)}, u32[]{:S(2)}) collective-permute-start(bf16[8,144,256]{2,1,0:T(8,128)(2,1)} %join_pieces.1.refs_0_), channel_id=1, source_target_pairs={{0,96},{32,0},{64,32},{96,64},{1,97},{33,1},{65,33},{97,65},{2,98}... | collective-permute-start | bytes 1769480 | tf_op jit(solution)/shard_map/store/ppermute | solution.py:650
  23.5 0.0 collective-permute-start.2
  23.5 9.4 %collective-permute-done.refs_1_ = bf16[8,144,256]{2,1,0:T(8,128)(2,1)} collective-permute-done((bf16[8,144,256]{2,1,0:T(8,128)(2,1)}, bf16[8,144,256]{2,1,0:T(8,128)(2,1)}, u32[]{:S(2)}, u32[]{:S(2)}) %collective-permute-start) | collective-permute-done | bytes 589856 | tf_op jit(solution)/shard_map/store/ppermute | solution.py:652
  33.0 2.0 %collective-permute-done.1.refs_2_ = bf16[8,144,256]{2,1,0:T(8,128)(2,1)} collective-permute-done((bf16[8,144,256]{2,1,0:T(8,128)(2,1)}, bf16[8,144,256]{2,1,0:T(8,128)(2,1)}, u32[]{:S(2)}, u32[]{:S(2)}) %collective-permute-start.1) | collective-permute-done | bytes 589856 | tf_op jit(solution)/shard_map/store/ppermute | solution.py:650
  34.9 3.4 %collective-permute-done.2.refs_6_ = bf16[8,144,256]{2,1,0:T(8,128)(2,1)} collective-permute-done((bf16[8,144,256]{2,1,0:T(8,128)(2,1)}, bf16[8,144,256]{2,1,0:T(8,128)(2,1)}, u32[]{:S(2)}, u32[]{:S(2)}) %collective-permute-start.2) | collective-permute-done | bytes 589856 | tf_op jit(solution)/shard_map/store/ppermute | solution.py:651
  38.4 5.5 %all-to-all-start.1 = ((bf16[8,592,128]{2,1,0:T(8,128)(2,1)}), bf16[8,592,128]{2,1,0:T(8,128)(2,1)S(1)}, u32[]{:S(2)}, u32[]{:S(2)}) async-start(bf16[8,592,128]{2,1,0:T(8,128)(2,1)} %bitcast.7), calls=%async_computation.1 | async-start | bytes 2424832 | tf_op jit(solution)/shard_map/queries/all_to_all | solution.py:626
  43.8 0.3 collective-permute-start.3
  44.1 0.0 collective-permute-start.7
  44.1 8.6 %temporal_entry.1.refs_0_ = bf16[4,4,3,144,128]{4,3,2,1,0:T(8,128)(2,1)} custom-call(bf16[576,2048]{1,0:T(8,128)(2,1)} %get-tuple-element.17._.hidden_hbm, bf16[2048,3072]{1,0:T(8,128)(2,1)} %weight_hbm.6, f32[2,4]{1,0:T(2,128)S(1)} %copy-done, bf16[8,144,256]{2,1,0:T(8,128)(2,1)} %join_pieces.1.refs_0_), custom_call_target="tpu_custom_call" | custom-call | flops 226492416 | bytes 651264 | tf_op jit(solution)/shard_map/temporal/temporal_entry/pallas_call | solution.py:250
  52.7 7.6 %all-to-all-done.1.query_hbm = bf16[8,592,128]{2,1,0:T(8,128)(2,1)S(1)} async-done(((bf16[8,592,128]{2,1,0:T(8,128)(2,1)}), bf16[8,592,128]{2,1,0:T(8,128)(2,1)S(1)}, u32[]{:S(2)}, u32[]{:S(2)}) %all-to-all-start.1) | async-done | bytes 1212448 | tf_op jit(solution)/shard_map/queries/all_to_all | solution.py:626
  60.3 3.7 %all-to-all-start.2 = ((bf16[16,3,144,128]{3,2,1,0:T(8,128)(2,1)}), bf16[16,3,144,128]{3,2,1,0:T(8,128)(2,1)S(1)}, u32[]{:S(2)}, u32[]{:S(2)}) async-start(bf16[16,3,144,128]{3,2,1,0:T(8,128)(2,1)} %bitcast.18), calls=%async_computation.2 | async-start | bytes 3538944 | tf_op jit(solution)/shard_map/temporal/all_to_all | solution.py:626
  64.0 0.1 collective-permute-start.8
  64.1 0.5 collective-permute-start.9
  64.6 0.0 collective-permute-start.6
  64.6 0.0 collective-permute-done.3.refs_3_
  64.6 0.0 collective-permute-start.4
  64.6 0.0 collective-permute-done.7.refs_8_
  64.6 3.3 %collective-permute-start.5 = (bf16[8,144,256]{2,1,0:T(8,128)(2,1)}, bf16[8,144,256]{2,1,0:T(8,128)(2,1)}, u32[]{:S(2)}, u32[]{:S(2)}) collective-permute-start(bf16[8,144,256]{2,1,0:T(8,128)(2,1)} %collective-permute-done.3.refs_3_), channel_id=1, source_target_pairs={{0,96},{32,0},{64,32},{96,64},{1,97},{33,1},{65,33},{97,65},{2,98}... | collective-permute-start | bytes 1769480 | tf_op jit(solution)/shard_map/store/ppermute | solution.py:675
  67.9 14.4 %collective-permute-done.6.refs_7_ = bf16[8,144,256]{2,1,0:T(8,128)(2,1)} collective-permute-done((bf16[8,144,256]{2,1,0:T(8,128)(2,1)}, bf16[8,144,256]{2,1,0:T(8,128)(2,1)}, u32[]{:S(2)}, u32[]{:S(2)}) %collective-permute-start.6) | collective-permute-done | bytes 589856 | tf_op jit(solution)/shard_map/store/ppermute | solution.py:655
  82.3 0.0 collective-permute-start.10
  82.3 0.0 collective-permute-done.8.refs_9_
  82.3 0.5 collective-permute-start.13
  82.8 0.0 collective-permute-done.9.refs_10_
  82.8 0.1 collective-permute-start.14
  82.9 11.2 %collective-permute-done.4.refs_4_ = bf16[8,144,256]{2,1,0:T(8,128)(2,1)} collective-permute-done((bf16[8,144,256]{2,1,0:T(8,128)(2,1)}, bf16[8,144,256]{2,1,0:T(8,128)(2,1)}, u32[]{:S(2)}, u32[]{:S(2)}) %collective-permute-start.4) | collective-permute-done | bytes 589856 | tf_op jit(solution)/shard_map/store/ppermute | solution.py:674
  94.1 0.0 collective-permute-start.11
  94.1 0.0 collective-permute-done.5.refs_5_
  94.1 0.5 collective-permute-start.12
  94.6 8.1 %own_attend.1.refs_16_.own_hbm = bf16[4,592,128]{2,1,0:T(8,128)(2,1)} custom-call(bf16[576,2048]{1,0:T(8,128)(2,1)} %get-tuple-element.17._.hidden_hbm, bf16[2048,3072]{1,0:T(8,128)(2,1)} %weight_hbm.6, bf16[2,4,592,128]{3,2,1,0:T(8,128)(2,1)} %get-tuple-element.19.query_hbm, bf16[4,4,3,144,128]{4,3,2,1,0:T(8,128)(2,1)} %temporal_entry.1.refs_0_), custom_call_target="tpu_custom_call" | custom-call | flops 214695936 | bytes 593920 | tf_op jit(solution)/shard_map/own/own_attend/pallas_call | solution.py:380
  102.7 0.0 collective-permute-done.10.refs_11_
  102.8 0.0 collective-permute-done.13.refs_14_
  102.8 0.0 collective-permute-done.14.refs_15_
  102.8 0.0 collective-permute-done.11.refs_12_
  102.8 0.0 collective-permute-done.12.refs_13_
  102.8 8.3 %memory_attend.2.refs_16_ = bf16[4,592,128]{2,1,0:T(8,128)(2,1)} custom-call(s32[1]{0:T(128)} %bitcast.9.base_ref, s32[8,6]{1,0:T(8,128)S(1)} %fusion.6.index_ref, bf16[8,592,128]{2,1,0:T(8,128)(2,1)S(1)} %all-to-all-done.1.query_hbm, bf16[8,144,256]{2,1,0:T(8,128)(2,1)} %join_pieces.1.refs_0_, bf16[8,144,256]{2,1,0:T(8,128)(2,1)} %collective-permute-done.refs_1_, ...), custom_call_target="tpu_custom_call" | custom-call | flops 261881856 | bytes 186368 | tf_op jit(solution)/shard_map/memory/memory_attend/pallas_call | solution.py:449
  111.1 3.6 %collective-permute-start.15 = (bf16[4,592,128]{2,1,0:T(8,128)(2,1)}, bf16[4,592,128]{2,1,0:T(8,128)(2,1)}, u32[]{:S(2)}, u32[]{:S(2)}) collective-permute-start(bf16[4,592,128]{2,1,0:T(8,128)(2,1)} %memory_attend.2.refs_16_), channel_id=1, source_target_pairs={{0,8},{8,0},{1,9},{9,1},{2,10},{10,2},{3,11},{11,3},{4,12},{12,4},... | collective-permute-start | bytes 1818632 | tf_op jit(solution)/shard_map/memory/ppermute | solution.py:692
  115.3 8.3 %memory_attend.3.refs_0_._ = bf16[4,592,128]{2,1,0:T(8,128)(2,1)} custom-call(s32[1]{0:T(128)} %bitcast.6.base_ref, s32[8,6]{1,0:T(8,128)S(1)} %fusion.6.index_ref, bf16[8,592,128]{2,1,0:T(8,128)(2,1)S(1)} %all-to-all-done.1.query_hbm, bf16[8,144,256]{2,1,0:T(8,128)(2,1)} %join_pieces.1.refs_0_, bf16[8,144,256]{2,1,0:T(8,128)(2,1)} %collective-permute-done.refs_1_, ...), custom_call_target="tpu_custom_call" | custom-call | flops 261881856 | bytes 186368 | tf_op jit(solution)/shard_map/memory/memory_attend/pallas_call | solution.py:449
  123.6 0.0 all-to-all-done.2.in_hbm_ref
  123.6 2.4 %temporal_attend.1 = bf16[16,144,128]{2,1,0:T(8,128)(2,1)} custom-call(s32[1]{0:T(128)S(6)} %copy.11.length_ref, bf16[16,3,144,128]{3,2,1,0:T(8,128)(2,1)S(1)} %all-to-all-done.2.in_hbm_ref, bf16[4,592,128]{2,1,0:T(8,128)(2,1)} %memory_attend.3.refs_0_._), custom_call_target="tpu_custom_call" | custom-call | flops 18874368 | bytes 147456 | tf_op jit(solution)/shard_map/temporal/temporal_attend/pallas_call | solution.py:300
  126.0 4.9 %all-to-all-start.3 = ((bf16[16,144,128]{2,1,0:T(8,128)(2,1)}), bf16[16,144,128]{2,1,0:T(8,128)(2,1)S(1)}, u32[]{:S(2)}, u32[]{:S(2)}) async-start(bf16[16,144,128]{2,1,0:T(8,128)(2,1)} %temporal_attend.1), calls=%async_computation.3 | async-start | bytes 1179648 | tf_op jit(solution)/shard_map/temporal/all_to_all | solution.py:626
  131.0 0.0 collective-permute-done.15.refs_1_
  131.0 2.2 %add_partials.1 = (bf16[592,128]{1,0:T(8,128)(2,1)}, bf16[592,128]{1,0:T(8,128)(2,1)}, bf16[592,128]{1,0:T(8,128)(2,1)}, bf16[592,128]{1,0:T(8,128)(2,1)}) custom-call(s32[1]{0:T(128)} %bitcast.x_ref, bf16[4,592,128]{2,1,0:T(8,128)(2,1)} %memory_attend.3.refs_0_._, bf16[4,592,128]{2,1,0:T(8,128)(2,1)} %collective-permute-done.15.refs_1_), custom_call_target="tpu_custom_call" | custom-call | flops 75776 | bytes 151552 | tf_op jit(solution)/shard_map/memory/add_partials/pallas_call | solution.py:501
  133.1 2.0 %collective-permute-start.16 = (bf16[592,128]{1,0:T(8,128)(2,1)}, bf16[592,128]{1,0:T(8,128)(2,1)S(1)}, u32[]{:S(2)}, u32[]{:S(2)}) collective-permute-start(bf16[592,128]{1,0:T(8,128)(2,1)} %get-tuple-element.26), channel_id=1, source_target_pairs={{0,1},{1,2},{2,3},{3,0},{4,5},{5,6},{6,7},{7,4},{8,9},{9,10},{10,1... | collective-permute-start | bytes 454664 | tf_op jit(solution)/shard_map/memory/ppermute | solution.py:629
  135.1 2.7 %collective-permute-start.17 = (bf16[592,128]{1,0:T(8,128)(2,1)}, bf16[592,128]{1,0:T(8,128)(2,1)S(1)}, u32[]{:S(2)}, u32[]{:S(2)}) collective-permute-start(bf16[592,128]{1,0:T(8,128)(2,1)} %get-tuple-element.27), channel_id=1, source_target_pairs={{0,2},{1,3},{2,0},{3,1},{4,6},{5,7},{6,4},{7,5},{8,10},{9,11},{10,... | collective-permute-start | bytes 454664 | tf_op jit(solution)/shard_map/memory/ppermute | solution.py:629
  137.8 1.5 collective-permute-start.18
  139.3 5.4 %all-to-all-done.3.time_hbm = bf16[16,144,128]{2,1,0:T(8,128)(2,1)S(1)} async-done(((bf16[16,144,128]{2,1,0:T(8,128)(2,1)}), bf16[16,144,128]{2,1,0:T(8,128)(2,1)S(1)}, u32[]{:S(2)}, u32[]{:S(2)}) %all-to-all-start.3) | async-done | bytes 589856 | tf_op jit(solution)/shard_map/temporal/all_to_all | solution.py:626
  144.6 0.5 collective-permute-done.16.memory_1
  145.1 2.4 %collective-permute-done.17.memory_2 = bf16[592,128]{1,0:T(8,128)(2,1)S(1)} collective-permute-done((bf16[592,128]{1,0:T(8,128)(2,1)}, bf16[592,128]{1,0:T(8,128)(2,1)S(1)}, u32[]{:S(2)}, u32[]{:S(2)}) %collective-permute-start.17) | collective-permute-done | bytes 151584 | tf_op jit(solution)/shard_map/memory/ppermute | solution.py:629
  147.5 0.0 collective-permute-done.18.memory_3
  147.5 6.1 %leave.1 = bf16[576,2048]{1,0:T(8,128)(2,1)} custom-call(s32[1]{0:T(128)} %bitcast.x_ref, bf16[4,592,128]{2,1,0:T(8,128)(2,1)} %own_attend.1.refs_16_.own_hbm, bf16[592,128]{1,0:T(8,128)(2,1)} %get-tuple-element.25.memory_0, bf16[592,128]{1,0:T(8,128)(2,1)S(1)} %collective-permute-done.16.memory_1, bf16[592,128]{1,0:T(8,128)(2,1)S(1)} %collective-permute-done.17.memory_2, ...), custom_call_target="tpu_custom_call" | custom-call | flops 150994944 | bytes 630784 | tf_op jit(solution)/shard_map/exit/leave/pallas_call | solution.py:572
  (2 shorter events, 0.0 us)
Async XLA Ops:
  0.0 6.6 %copy-start = (f32[2,4]{1,0:T(2,128)S(1)}, f32[2,4]{1,0:T(2,128)}, u32[]{:S(2)}) copy-start(f32[2,4]{1,0:T(2,128)} %sharpness_ref.3) | copy-start | bytes 100
  0.0 6.6 %copy-start.1 = (s32[1,1,6,1]{2,3,1,0:T(1,128)S(1)}, s32[1,1,6,1]{2,3,1,0:T(1,128)}, u32[]{:S(2)}) copy-start(s32[1,1,6,1]{2,3,1,0:T(1,128)} %param.15) | copy-start | bytes 76
  0.0 6.6 %copy-start.2 = (s32[1,1,6]{2,1,0:T(1,128)S(1)}, s32[1,1,6]{2,1,0:T(1,128)}, u32[]{:S(2)}) copy-start(s32[1,1,6]{2,1,0:T(1,128)} %param.16) | copy-start | bytes 76
  2.2 14.6 %all-to-all-start = ((bf16[4,288,256]{2,1,0:T(8,128)(2,1)}), bf16[4,288,256]{2,1,0:T(8,128)(2,1)S(1)}, u32[]{:S(2)}, u32[]{:S(2)}) async-start(bf16[4,288,256]{2,1,0:T(8,128)(2,1)} %bitcast.19), calls=%async_computation | async-start | bytes 1179648 | tf_op jit(solution)/shard_map/store/all_to_all | solution.py:626
  18.5 14.5 %collective-permute-start = (bf16[8,144,256]{2,1,0:T(8,128)(2,1)}, bf16[8,144,256]{2,1,0:T(8,128)(2,1)}, u32[]{:S(2)}, u32[]{:S(2)}) collective-permute-start(bf16[8,144,256]{2,1,0:T(8,128)(2,1)} %join_pieces.1.refs_0_), channel_id=1, source_target_pairs={{0,4},{4,0},{1,5},{5,1},{2,6},{6,2},{3,7},{7,3},{8,12},{12,8},{9,1... | collective-permute-start | bytes 1769480 | tf_op jit(solution)/shard_map/store/ppermute | solution.py:652
  20.5 14.4 %collective-permute-start.1 = (bf16[8,144,256]{2,1,0:T(8,128)(2,1)}, bf16[8,144,256]{2,1,0:T(8,128)(2,1)}, u32[]{:S(2)}, u32[]{:S(2)}) collective-permute-start(bf16[8,144,256]{2,1,0:T(8,128)(2,1)} %join_pieces.1.refs_0_), channel_id=1, source_target_pairs={{0,96},{32,0},{64,32},{96,64},{1,97},{33,1},{65,33},{97,65},{2,98}... | collective-permute-start | bytes 1769480 | tf_op jit(solution)/shard_map/store/ppermute | solution.py:650
  23.5 14.8 %collective-permute-start.2 = (bf16[8,144,256]{2,1,0:T(8,128)(2,1)}, bf16[8,144,256]{2,1,0:T(8,128)(2,1)}, u32[]{:S(2)}, u32[]{:S(2)}) collective-permute-start(bf16[8,144,256]{2,1,0:T(8,128)(2,1)} %join_pieces.1.refs_0_), channel_id=1, source_target_pairs={{0,32},{32,64},{64,96},{96,0},{1,33},{33,65},{65,97},{97,1},{2,34}... | collective-permute-start | bytes 1769480 | tf_op jit(solution)/shard_map/store/ppermute | solution.py:651
  38.4 21.9 %all-to-all-start.1 = ((bf16[8,592,128]{2,1,0:T(8,128)(2,1)}), bf16[8,592,128]{2,1,0:T(8,128)(2,1)S(1)}, u32[]{:S(2)}, u32[]{:S(2)}) async-start(bf16[8,592,128]{2,1,0:T(8,128)(2,1)} %bitcast.7), calls=%async_computation.1 | async-start | bytes 2424832 | tf_op jit(solution)/shard_map/queries/all_to_all | solution.py:626
  43.8 20.8 %collective-permute-start.3 = (bf16[8,144,256]{2,1,0:T(8,128)(2,1)}, bf16[8,144,256]{2,1,0:T(8,128)(2,1)}, u32[]{:S(2)}, u32[]{:S(2)}) collective-permute-start(bf16[8,144,256]{2,1,0:T(8,128)(2,1)} %collective-permute-done.refs_1_), channel_id=1, source_target_pairs={{0,96},{32,0},{64,32},{96,64},{1,97},{33,1},{65,33},{97,65},{2,98}... | collective-permute-start | bytes 1769480 | tf_op jit(solution)/shard_map/store/ppermute | solution.py:654
  44.1 20.5 %collective-permute-start.7 = (bf16[8,144,256]{2,1,0:T(8,128)(2,1)}, bf16[8,144,256]{2,1,0:T(8,128)(2,1)}, u32[]{:S(2)}, u32[]{:S(2)}) collective-permute-start(bf16[8,144,256]{2,1,0:T(8,128)(2,1)} %join_pieces.1.refs_0_), channel_id=1, source_target_pairs={{0,16},{16,0},{1,17},{17,1},{2,18},{18,2},{3,19},{19,3},{4,20},{20... | collective-permute-start | bytes 1769480 | tf_op jit(solution)/shard_map/store/ppermute | solution.py:677
  60.3 63.2 %all-to-all-start.2 = ((bf16[16,3,144,128]{3,2,1,0:T(8,128)(2,1)}), bf16[16,3,144,128]{3,2,1,0:T(8,128)(2,1)S(1)}, u32[]{:S(2)}, u32[]{:S(2)}) async-start(bf16[16,3,144,128]{3,2,1,0:T(8,128)(2,1)} %bitcast.18), calls=%async_computation.2 | async-start | bytes 3538944 | tf_op jit(solution)/shard_map/temporal/all_to_all | solution.py:626
  64.0 18.3 %collective-permute-start.8 = (bf16[8,144,256]{2,1,0:T(8,128)(2,1)}, bf16[8,144,256]{2,1,0:T(8,128)(2,1)}, u32[]{:S(2)}, u32[]{:S(2)}) collective-permute-start(bf16[8,144,256]{2,1,0:T(8,128)(2,1)} %collective-permute-done.refs_1_), channel_id=1, source_target_pairs={{0,16},{16,0},{1,17},{17,1},{2,18},{18,2},{3,19},{19,3},{4,20},{20... | collective-permute-start | bytes 1769480 | tf_op jit(solution)/shard_map/store/ppermute | solution.py:677
  64.1 18.7 %collective-permute-start.9 = (bf16[8,144,256]{2,1,0:T(8,128)(2,1)}, bf16[8,144,256]{2,1,0:T(8,128)(2,1)}, u32[]{:S(2)}, u32[]{:S(2)}) collective-permute-start(bf16[8,144,256]{2,1,0:T(8,128)(2,1)} %collective-permute-done.1.refs_2_), channel_id=1, source_target_pairs={{0,16},{16,0},{1,17},{17,1},{2,18},{18,2},{3,19},{19,3},{4,20},{20... | collective-permute-start | bytes 1769480 | tf_op jit(solution)/shard_map/store/ppermute | solution.py:677
  64.6 17.7 %collective-permute-start.6 = (bf16[8,144,256]{2,1,0:T(8,128)(2,1)}, bf16[8,144,256]{2,1,0:T(8,128)(2,1)}, u32[]{:S(2)}, u32[]{:S(2)}) collective-permute-start(bf16[8,144,256]{2,1,0:T(8,128)(2,1)} %collective-permute-done.refs_1_), channel_id=1, source_target_pairs={{0,32},{32,64},{64,96},{96,0},{1,33},{33,65},{65,97},{97,1},{2,34}... | collective-permute-start | bytes 1769480 | tf_op jit(solution)/shard_map/store/ppermute | solution.py:655
  64.6 29.5 %collective-permute-start.4 = (bf16[8,144,256]{2,1,0:T(8,128)(2,1)}, bf16[8,144,256]{2,1,0:T(8,128)(2,1)}, u32[]{:S(2)}, u32[]{:S(2)}) collective-permute-start(bf16[8,144,256]{2,1,0:T(8,128)(2,1)} %collective-permute-done.2.refs_6_), channel_id=1, source_target_pairs={{0,32},{32,64},{64,96},{96,0},{1,33},{33,65},{65,97},{97,1},{2,34}... | collective-permute-start | bytes 1769480 | tf_op jit(solution)/shard_map/store/ppermute | solution.py:674
  64.6 29.5 %collective-permute-start.5 = (bf16[8,144,256]{2,1,0:T(8,128)(2,1)}, bf16[8,144,256]{2,1,0:T(8,128)(2,1)}, u32[]{:S(2)}, u32[]{:S(2)}) collective-permute-start(bf16[8,144,256]{2,1,0:T(8,128)(2,1)} %collective-permute-done.3.refs_3_), channel_id=1, source_target_pairs={{0,96},{32,0},{64,32},{96,64},{1,97},{33,1},{65,33},{97,65},{2,98}... | collective-permute-start | bytes 1769480 | tf_op jit(solution)/shard_map/store/ppermute | solution.py:675
  82.3 20.4 %collective-permute-start.10 = (bf16[8,144,256]{2,1,0:T(8,128)(2,1)}, bf16[8,144,256]{2,1,0:T(8,128)(2,1)}, u32[]{:S(2)}, u32[]{:S(2)}) collective-permute-start(bf16[8,144,256]{2,1,0:T(8,128)(2,1)} %collective-permute-done.3.refs_3_), channel_id=1, source_target_pairs={{0,16},{16,0},{1,17},{17,1},{2,18},{18,2},{3,19},{19,3},{4,20},{20... | collective-permute-start | bytes 1769480 | tf_op jit(solution)/shard_map/store/ppermute | solution.py:677
  82.3 20.4 %collective-permute-start.13 = (bf16[8,144,256]{2,1,0:T(8,128)(2,1)}, bf16[8,144,256]{2,1,0:T(8,128)(2,1)}, u32[]{:S(2)}, u32[]{:S(2)}) collective-permute-start(bf16[8,144,256]{2,1,0:T(8,128)(2,1)} %collective-permute-done.2.refs_6_), channel_id=1, source_target_pairs={{0,16},{16,0},{1,17},{17,1},{2,18},{18,2},{3,19},{19,3},{4,20},{20... | collective-permute-start | bytes 1769480 | tf_op jit(solution)/shard_map/store/ppermute | solution.py:677
  82.8 19.9 %collective-permute-start.14 = (bf16[8,144,256]{2,1,0:T(8,128)(2,1)}, bf16[8,144,256]{2,1,0:T(8,128)(2,1)}, u32[]{:S(2)}, u32[]{:S(2)}) collective-permute-start(bf16[8,144,256]{2,1,0:T(8,128)(2,1)} %collective-permute-done.6.refs_7_), channel_id=1, source_target_pairs={{0,16},{16,0},{1,17},{17,1},{2,18},{18,2},{3,19},{19,3},{4,20},{20... | collective-permute-start | bytes 1769480 | tf_op jit(solution)/shard_map/store/ppermute | solution.py:677
  94.1 8.7 %collective-permute-start.11 = (bf16[8,144,256]{2,1,0:T(8,128)(2,1)}, bf16[8,144,256]{2,1,0:T(8,128)(2,1)}, u32[]{:S(2)}, u32[]{:S(2)}) collective-permute-start(bf16[8,144,256]{2,1,0:T(8,128)(2,1)} %collective-permute-done.4.refs_4_), channel_id=1, source_target_pairs={{0,16},{16,0},{1,17},{17,1},{2,18},{18,2},{3,19},{19,3},{4,20},{20... | collective-permute-start | bytes 1769480 | tf_op jit(solution)/shard_map/store/ppermute | solution.py:677
  94.1 8.7 %collective-permute-start.12 = (bf16[8,144,256]{2,1,0:T(8,128)(2,1)}, bf16[8,144,256]{2,1,0:T(8,128)(2,1)}, u32[]{:S(2)}, u32[]{:S(2)}) collective-permute-start(bf16[8,144,256]{2,1,0:T(8,128)(2,1)} %collective-permute-done.5.refs_5_), channel_id=1, source_target_pairs={{0,16},{16,0},{1,17},{17,1},{2,18},{18,2},{3,19},{19,3},{4,20},{20... | collective-permute-start | bytes 1769480 | tf_op jit(solution)/shard_map/store/ppermute | solution.py:677
  111.1 19.9 %collective-permute-start.15 = (bf16[4,592,128]{2,1,0:T(8,128)(2,1)}, bf16[4,592,128]{2,1,0:T(8,128)(2,1)}, u32[]{:S(2)}, u32[]{:S(2)}) collective-permute-start(bf16[4,592,128]{2,1,0:T(8,128)(2,1)} %memory_attend.2.refs_16_), channel_id=1, source_target_pairs={{0,8},{8,0},{1,9},{9,1},{2,10},{10,2},{3,11},{11,3},{4,12},{12,4},... | collective-permute-start | bytes 1818632 | tf_op jit(solution)/shard_map/memory/ppermute | solution.py:692
  126.0 18.6 %all-to-all-start.3 = ((bf16[16,144,128]{2,1,0:T(8,128)(2,1)}), bf16[16,144,128]{2,1,0:T(8,128)(2,1)S(1)}, u32[]{:S(2)}, u32[]{:S(2)}) async-start(bf16[16,144,128]{2,1,0:T(8,128)(2,1)} %temporal_attend.1), calls=%async_computation.3 | async-start | bytes 1179648 | tf_op jit(solution)/shard_map/temporal/all_to_all | solution.py:626
  133.1 12.0 %collective-permute-start.16 = (bf16[592,128]{1,0:T(8,128)(2,1)}, bf16[592,128]{1,0:T(8,128)(2,1)S(1)}, u32[]{:S(2)}, u32[]{:S(2)}) collective-permute-start(bf16[592,128]{1,0:T(8,128)(2,1)} %get-tuple-element.26), channel_id=1, source_target_pairs={{0,1},{1,2},{2,3},{3,0},{4,5},{5,6},{6,7},{7,4},{8,9},{9,10},{10,1... | collective-permute-start | bytes 454664 | tf_op jit(solution)/shard_map/memory/ppermute | solution.py:629
  135.1 12.3 %collective-permute-start.17 = (bf16[592,128]{1,0:T(8,128)(2,1)}, bf16[592,128]{1,0:T(8,128)(2,1)S(1)}, u32[]{:S(2)}, u32[]{:S(2)}) collective-permute-start(bf16[592,128]{1,0:T(8,128)(2,1)} %get-tuple-element.27), channel_id=1, source_target_pairs={{0,2},{1,3},{2,0},{3,1},{4,6},{5,7},{6,4},{7,5},{8,10},{9,11},{10,... | collective-permute-start | bytes 454664 | tf_op jit(solution)/shard_map/memory/ppermute | solution.py:629
  137.8 9.7 %collective-permute-start.18 = (bf16[592,128]{1,0:T(8,128)(2,1)}, bf16[592,128]{1,0:T(8,128)(2,1)S(1)}, u32[]{:S(2)}, u32[]{:S(2)}) collective-permute-start(bf16[592,128]{1,0:T(8,128)(2,1)} %get-tuple-element.28), channel_id=1, source_target_pairs={{0,3},{1,0},{2,1},{3,2},{4,7},{5,4},{6,5},{7,6},{8,11},{9,8},{10,9... | collective-permute-start | bytes 454664 | tf_op jit(solution)/shard_map/memory/ppermute | solution.py:629

commit v13 on v12

--- a/solution.py
+++ b/solution.py
@@ -654,23 +654,28 @@
         second_above = lax.ppermute(second, "y", turn(-1))
         second_below = lax.ppermute(second, "y", turn(1))
 
-    with jax.named_scope("queries"):
-        asked, second, above, below = lax.optimization_barrier((query, second, above, below))
-        asked = swap(asked.reshape((-1,) + asked.shape[2:]), ("zq", "x"))
-
     with jax.named_scope("temporal"):
         parts = temporal_entry(
             hidden, entry_projection_matrix, softmax_sharpness, quarters, after=[in_hbm(joined)]
         )
-        sent = swap(parts.reshape((quarters * G,) + parts.shape[2:]), frame)
+
+    with jax.named_scope("queries"):
+        asked, *_ = lax.optimization_barrier((query, second, above, below, parts))
+        asked = swap(asked.reshape((-1,) + asked.shape[2:]), ("zq", "x"))
 
     with jax.named_scope("own"):
         own = own_attend(
-            hidden, entry_projection_matrix, query, after=[in_hbm(parts)]
+            hidden, entry_projection_matrix, query, after=[in_hbm(parts), above]
         )
 
+    with jax.named_scope("temporal"):
+        sent, *_ = lax.optimization_barrier((parts, second_above, second_below))
+        sent = swap(sent.reshape((quarters * G,) + parts.shape[2:]), frame)
+
     with jax.named_scope("store"):
-        below, second_above, parts = lax.optimization_barrier((below, second_above, parts))
+        below, second_above, second_below, own = lax.optimization_barrier(
+            (below, second_above, second_below, own)
+        )
         far = lax.ppermute(below, "y", turn(1))
         second_far = lax.ppermute(second_above, "y", turn(-1))
         near = [joined, second, above, second_above, far, second_far, below, second_below]

time: 154 us -> 147 us (0.955)
  waiting for transfers between devices: 60.6 us -> 48.1 us
  local copies, waits for them, and re-layouts: 1.2 us -> 3.65 us
  starting transfers between devices: 38.5 us -> 40.8 us
    ppermute x1, waiting for transfers between devices: 14.4 us -> 1.29 us  [on_device(): second_below = lax.ppermute(second, 'y', turn(1))]
    ppermute x1, waiting for transfers between devices: 0.01 us -> 10.2 us  [on_device(): second_above = lax.ppermute(second, 'y', turn(-1))]
    all_to_all x4, waiting for transfers between devices: 17.4 us -> 7.34 us  [swap(): return lax.all_to_all(blocks, axes, split_axis=0, concat_axis=0, tiled=True)]
    ppermute x1, waiting for transfers between devices: 9.44 us -> 1.44 us  [on_device(): second = lax.ppermute(joined, 'zp', other(sides))]
    ppermute x3, waiting for transfers between devices: 2.84 us -> 8.32 us  [swap_apart(): lax.ppermute(blocks[j], 'x', turn(j))]
    ppermute x8, waiting for transfers between devices: 0.02 us -> 2.63 us  [on_device(): blocks = near + [lax.ppermute(block, 'c', other(cores)) for block in near]]
    unnamed x7 -> x21, local copies, waits for them, and re-layouts: 1.2 us -> 3.65 us
    ppermute x1, starting transfers between devices: 0.01 us -> 2.02 us  [on_device(): second_below = lax.ppermute(second, 'y', turn(1))]
  transfers between devices with their start and end apart: 23 -> 23, of which waited for: 10 -> 12; matrix products, arithmetic and copies ran while one was open for 0% -> 0% of each run, Pallas kernels for 28% -> 30%
where the time goes in v13:
time: 147 us; the launch traced here: 146 us
  Pallas kernels  52.5 us (36%)
  waiting for transfers between devices  48.1 us (33%)
  starting transfers between devices  40.8 us (28%)
  local copies, waits for them, and re-layouts  3.65 us (2%)
    all_to_all x4, starting transfers between devices, swap(): return lax.all_to_all(blocks, axes, split_axis=0, concat_axis=0, tiled=True)  19 us
    pallas_call x2, Pallas kernels, memory_attend(): pl.pallas_call(functools.partial(memory_attend_kernel, count), in_specs=[...  16.5 us
    ppermute x1, waiting for transfers between devices, on_device(): far = lax.ppermute(below, 'y', turn(1))  12.9 us
    ppermute x1, waiting for transfers between devices, on_device(): second_above = lax.ppermute(second, 'y', turn(-1))  10.2 us
    pallas_call x1, Pallas kernels, temporal_entry(): pl.pallas_call(functools.partial(temporal_entry_kernel, quarters), in_spe...  8.61 us
    ppermute x3, waiting for transfers between devices, swap_apart(): lax.ppermute(blocks[j], 'x', turn(j))  8.32 us
    pallas_call x1, Pallas kernels, own_attend(): pl.pallas_call(own_attend_kernel, in_specs=[HBM, HBM, HBM] + [ANY] * len(...  8.12 us
    all_to_all x4, waiting for transfers between devices, swap(): return lax.all_to_all(blocks, axes, split_axis=0, concat_axis=0, tiled=True)  7.34 us
  transfers between devices with their start and end apart: 23, of which 12 were waited for; matrix products, arithmetic and copies ran while one was open for 0% of the time, Pallas kernels for 30%

profile of v13, /device:TPU:0, one launch (start us, length us, event | category | flops | bytes accessed | tf_op | source)
XLA Modules:
  0.0 146.0 jit_solution(12137083874002218694)
XLA Ops:
  0.0 1.2 copy.10
  1.2 1.0 split_store.1._
  2.2 4.4 %all-to-all-start = ((bf16[4,288,256]{2,1,0:T(8,128)(2,1)}), bf16[4,288,256]{2,1,0:T(8,128)(2,1)S(1)}, u32[]{:S(2)}, u32[]{:S(2)}) async-start(bf16[4,288,256]{2,1,0:T(8,128)(2,1)} %bitcast.19), calls=%async_computation | async-start | bytes 1179648 | tf_op jit(solution)/shard_map/store/all_to_all | solution.py:626
  6.6 0.0 copy-done.3
  6.6 5.8 %modulate.1 = (bf16[576,2048]{1,0:T(8,128)(2,1)}, bf16[2,4,592,128]{3,2,1,0:T(8,128)(2,1)}) custom-call(bf16[576,2048]{1,0:T(8,128)(2,1)} %bitcast.20, f32[2,2048]{1,0:T(2,128)} %bitcast.22, bf16[2048,3072]{1,0:T(8,128)(2,1)} %weight_hbm.6, f32[2,4]{1,0:T(2,128)S(1)} %copy-done.2, s32[6]{0:T(128)S(1)} %bitcast.16, s32[6]{0:T(128)S(1)} %bitcast.17, ...), custom_call_target="tpu_custom_call" | custom-call | flops 75497472 | bytes 462848 | tf_op jit(solution)/shard_map/queries/modulate/pallas_call | solution.py:185
  12.4 4.4 %all-to-all-done.in_hbm = bf16[4,288,256]{2,1,0:T(8,128)(2,1)S(1)} async-done(((bf16[4,288,256]{2,1,0:T(8,128)(2,1)}), bf16[4,288,256]{2,1,0:T(8,128)(2,1)S(1)}, u32[]{:S(2)}, u32[]{:S(2)}) %all-to-all-start) | async-done | bytes 589856 | tf_op jit(solution)/shard_map/store/all_to_all | solution.py:626
  16.7 1.8 %join_pieces.1.refs_0_ = bf16[8,144,256]{2,1,0:T(8,128)(2,1)} custom-call(bf16[4,288,256]{2,1,0:T(8,128)(2,1)S(1)} %all-to-all-done.in_hbm, bf16[576,2048]{1,0:T(8,128)(2,1)} %get-tuple-element.17._.hidden_hbm), custom_call_target="tpu_custom_call" | custom-call | flops 18432 | bytes 73728 | tf_op jit(solution)/shard_map/store/join_pieces/pallas_call | solution.py:109
  18.5 3.1 %collective-permute-start.4 = (bf16[8,144,256]{2,1,0:T(8,128)(2,1)}, bf16[8,144,256]{2,1,0:T(8,128)(2,1)S(1)}, u32[]{:S(2)}, u32[]{:S(2)}) collective-permute-start(bf16[8,144,256]{2,1,0:T(8,128)(2,1)} %join_pieces.1.refs_0_), channel_id=1, source_target_pairs={{0,96},{32,0},{64,32},{96,64},{1,97},{33,1},{65,33},{97,65},{2,98}... | collective-permute-start | bytes 1769480 | tf_op jit(solution)/shard_map/store/ppermute | solution.py:650
  21.6 1.9 %collective-permute-start.1 = (bf16[8,144,256]{2,1,0:T(8,128)(2,1)}, bf16[8,144,256]{2,1,0:T(8,128)(2,1)S(1)}, u32[]{:S(2)}, u32[]{:S(2)}) collective-permute-start(bf16[8,144,256]{2,1,0:T(8,128)(2,1)} %join_pieces.1.refs_0_), channel_id=1, source_target_pairs={{0,4},{4,0},{1,5},{5,1},{2,6},{6,2},{3,7},{7,3},{8,12},{12,8},{9,1... | collective-permute-start | bytes 1769480 | tf_op jit(solution)/shard_map/store/ppermute | solution.py:652
  23.5 0.0 collective-permute-start
  23.5 8.6 %temporal_entry.1.refs_0_ = bf16[4,4,3,144,128]{4,3,2,1,0:T(8,128)(2,1)} custom-call(bf16[576,2048]{1,0:T(8,128)(2,1)} %get-tuple-element.17._.hidden_hbm, bf16[2048,3072]{1,0:T(8,128)(2,1)} %weight_hbm.6, f32[2,4]{1,0:T(2,128)S(1)} %copy-done.2, bf16[8,144,256]{2,1,0:T(8,128)(2,1)} %join_pieces.1.refs_0_), custom_call_target="tpu_custom_call" | custom-call | flops 226492416 | bytes 651264 | tf_op jit(solution)/shard_map/temporal/temporal_entry/pallas_call | solution.py:250
  32.1 1.2 collective-permute-done.4.refs_1_.refs_2_
  33.3 0.9 copy-done
  34.2 1.4 collective-permute-done.1.refs_1_
  35.6 2.7 %collective-permute-done.refs_6_ = bf16[8,144,256]{2,1,0:T(8,128)(2,1)} collective-permute-done((bf16[8,144,256]{2,1,0:T(8,128)(2,1)}, bf16[8,144,256]{2,1,0:T(8,128)(2,1)}, u32[]{:S(2)}, u32[]{:S(2)}) %collective-permute-start) | collective-permute-done | bytes 589856 | tf_op jit(solution)/shard_map/store/ppermute | solution.py:651
  38.4 5.5 %all-to-all-start.1 = ((bf16[8,592,128]{2,1,0:T(8,128)(2,1)}), bf16[8,592,128]{2,1,0:T(8,128)(2,1)S(1)}, u32[]{:S(2)}, u32[]{:S(2)}) async-start(bf16[8,592,128]{2,1,0:T(8,128)(2,1)} %bitcast.7), calls=%async_computation.1 | async-start | bytes 2424832 | tf_op jit(solution)/shard_map/queries/all_to_all | solution.py:626
  43.8 0.0 collective-permute-start.2
  43.8 2.0 %collective-permute-start.3 = (bf16[8,144,256]{2,1,0:T(8,128)(2,1)S(1)}, bf16[8,144,256]{2,1,0:T(8,128)(2,1)}, u32[]{:S(2)}, u32[]{:S(2)}) collective-permute-start(bf16[8,144,256]{2,1,0:T(8,128)(2,1)S(1)} %collective-permute-done.1.refs_1_), channel_id=1, source_target_pairs={{0,32},{32,64},{64,96},{96,0},{1,33},{33,65},{65,97},{97,1},{2,34}... | collective-permute-start | bytes 1769480 | tf_op jit(solution)/shard_map/store/ppermute | solution.py:655
  45.8 10.2 %collective-permute-done.2.refs_3_ = bf16[8,144,256]{2,1,0:T(8,128)(2,1)} collective-permute-done((bf16[8,144,256]{2,1,0:T(8,128)(2,1)S(1)}, bf16[8,144,256]{2,1,0:T(8,128)(2,1)}, u32[]{:S(2)}, u32[]{:S(2)}) %collective-permute-start.2) | collective-permute-done | bytes 589856 | tf_op jit(solution)/shard_map/store/ppermute | solution.py:654
  56.0 1.3 collective-permute-done.3.refs_7_
  57.3 3.0 %all-to-all-done.1.query_hbm = bf16[8,592,128]{2,1,0:T(8,128)(2,1)S(1)} async-done(((bf16[8,592,128]{2,1,0:T(8,128)(2,1)}), bf16[8,592,128]{2,1,0:T(8,128)(2,1)S(1)}, u32[]{:S(2)}, u32[]{:S(2)}) %all-to-all-start.1) | async-done | bytes 1212448 | tf_op jit(solution)/shard_map/queries/all_to_all | solution.py:626
  60.3 0.0 copy-done.5
  60.3 4.1 %all-to-all-start.2 = ((bf16[16,3,144,128]{3,2,1,0:T(8,128)(2,1)}), bf16[16,3,144,128]{3,2,1,0:T(8,128)(2,1)S(1)}, u32[]{:S(2)}, u32[]{:S(2)}) async-start(bf16[16,3,144,128]{3,2,1,0:T(8,128)(2,1)} %bitcast.18), calls=%async_computation.2 | async-start | bytes 3538944 | tf_op jit(solution)/shard_map/temporal/all_to_all | solution.py:626
  64.5 0.3 collective-permute-start.7
  64.7 1.1 copy-done.1
  65.8 8.1 %own_attend.1.refs_16_.own_hbm = bf16[4,592,128]{2,1,0:T(8,128)(2,1)} custom-call(bf16[576,2048]{1,0:T(8,128)(2,1)} %get-tuple-element.17._.hidden_hbm, bf16[2048,3072]{1,0:T(8,128)(2,1)} %weight_hbm.6, bf16[2,4,592,128]{3,2,1,0:T(8,128)(2,1)} %get-tuple-element.20.query_hbm, bf16[4,4,3,144,128]{4,3,2,1,0:T(8,128)(2,1)} %temporal_entry.1.refs_0_, ...), custom_call_target="tpu_custom_call" | custom-call | flops 214695936 | bytes 593920 | tf_op jit(solution)/shard_map/own/own_attend/pallas_call | solution.py:380
  73.9 0.0 copy-done.6
  73.9 0.6 collective-permute-start.8
  74.5 0.1 collective-permute-start.9
  74.6 0.4 collective-permute-start.5
  75.0 2.9 %collective-permute-start.6 = (bf16[8,144,256]{2,1,0:T(8,128)(2,1)}, bf16[8,144,256]{2,1,0:T(8,128)(2,1)}, u32[]{:S(2)}, u32[]{:S(2)}) collective-permute-start(bf16[8,144,256]{2,1,0:T(8,128)(2,1)} %collective-permute-done.2.refs_3_), channel_id=1, source_target_pairs={{0,96},{32,0},{64,32},{96,64},{1,97},{33,1},{65,33},{97,65},{2,98}... | collective-permute-start | bytes 1769480 | tf_op jit(solution)/shard_map/store/ppermute | solution.py:680
  77.8 0.0 collective-permute-done.7.refs_8_
  77.8 0.0 collective-permute-start.10
  77.9 0.0 collective-permute-done.8.refs_9_
  77.9 0.5 collective-permute-start.13
  78.4 0.0 collective-permute-done.9.refs_10_
  78.4 0.3 copy-done.7
  78.7 0.0 collective-permute-start.14
  78.7 0.2 copy-done.8
  78.9 12.9 %collective-permute-done.5.refs_4_ = bf16[8,144,256]{2,1,0:T(8,128)(2,1)} collective-permute-done((bf16[8,144,256]{2,1,0:T(8,128)(2,1)}, bf16[8,144,256]{2,1,0:T(8,128)(2,1)}, u32[]{:S(2)}, u32[]{:S(2)}) %collective-permute-start.5) | collective-permute-done | bytes 589856 | tf_op jit(solution)/shard_map/store/ppermute | solution.py:679
  91.8 0.0 collective-permute-start.11
  91.8 0.0 collective-permute-done.6.refs_5_
  91.8 0.5 collective-permute-start.12
  92.3 0.0 collective-permute-done.10.refs_11_
  92.3 0.0 collective-permute-done.13.refs_14_
  92.4 0.0 collective-permute-done.14.refs_15_
  92.4 1.8 %collective-permute-done.11.refs_12_ = bf16[8,144,256]{2,1,0:T(8,128)(2,1)} collective-permute-done((bf16[8,144,256]{2,1,0:T(8,128)(2,1)}, bf16[8,144,256]{2,1,0:T(8,128)(2,1)}, u32[]{:S(2)}, u32[]{:S(2)}) %collective-permute-start.11) | collective-permute-done | bytes 589856 | tf_op jit(solution)/shard_map/store/ppermute | solution.py:682
  94.1 0.8 collective-permute-done.12.refs_13_
  95.0 8.2 %memory_attend.2.refs_16_ = bf16[4,592,128]{2,1,0:T(8,128)(2,1)} custom-call(s32[1]{0:T(128)} %bitcast.9.base_ref, s32[8,6]{1,0:T(8,128)S(1)} %fusion.6.index_ref, bf16[8,592,128]{2,1,0:T(8,128)(2,1)S(1)} %all-to-all-done.1.query_hbm, bf16[8,144,256]{2,1,0:T(8,128)(2,1)} %join_pieces.1.refs_0_, bf16[8,144,256]{2,1,0:T(8,128)(2,1)} %copy-done.5, ...), custom_call_target="tpu_custom_call" | custom-call | flops 261881856 | bytes 186368 | tf_op jit(solution)/shard_map/memory/memory_attend/pallas_call | solution.py:449
  103.2 3.5 %collective-permute-start.15 = (bf16[4,592,128]{2,1,0:T(8,128)(2,1)}, bf16[4,592,128]{2,1,0:T(8,128)(2,1)}, u32[]{:S(2)}, u32[]{:S(2)}) collective-permute-start(bf16[4,592,128]{2,1,0:T(8,128)(2,1)} %memory_attend.2.refs_16_), channel_id=1, source_target_pairs={{0,8},{8,0},{1,9},{9,1},{2,10},{10,2},{3,11},{11,3},{4,12},{12,4},... | collective-permute-start | bytes 1818632 | tf_op jit(solution)/shard_map/memory/ppermute | solution.py:697
  107.4 8.3 %memory_attend.3.refs_0_._ = bf16[4,592,128]{2,1,0:T(8,128)(2,1)} custom-call(s32[1]{0:T(128)} %bitcast.6.base_ref, s32[8,6]{1,0:T(8,128)S(1)} %fusion.6.index_ref, bf16[8,592,128]{2,1,0:T(8,128)(2,1)S(1)} %all-to-all-done.1.query_hbm, bf16[8,144,256]{2,1,0:T(8,128)(2,1)} %join_pieces.1.refs_0_, bf16[8,144,256]{2,1,0:T(8,128)(2,1)} %copy-done.5, ...), custom_call_target="tpu_custom_call" | custom-call | flops 261881856 | bytes 186368 | tf_op jit(solution)/shard_map/memory/memory_attend/pallas_call | solution.py:449
  115.6 0.0 all-to-all-done.2.in_hbm_ref
  115.7 2.4 %temporal_attend.1 = bf16[16,144,128]{2,1,0:T(8,128)(2,1)} custom-call(s32[1]{0:T(128)S(6)} %copy.11.length_ref, bf16[16,3,144,128]{3,2,1,0:T(8,128)(2,1)S(1)} %all-to-all-done.2.in_hbm_ref, bf16[4,592,128]{2,1,0:T(8,128)(2,1)} %memory_attend.3.refs_0_._), custom_call_target="tpu_custom_call" | custom-call | flops 18874368 | bytes 147456 | tf_op jit(solution)/shard_map/temporal/temporal_attend/pallas_call | solution.py:300
  118.1 5.0 %all-to-all-start.3 = ((bf16[16,144,128]{2,1,0:T(8,128)(2,1)}), bf16[16,144,128]{2,1,0:T(8,128)(2,1)S(1)}, u32[]{:S(2)}, u32[]{:S(2)}) async-start(bf16[16,144,128]{2,1,0:T(8,128)(2,1)} %temporal_attend.1), calls=%async_computation.3 | async-start | bytes 1179648 | tf_op jit(solution)/shard_map/temporal/all_to_all | solution.py:626
  123.1 0.0 collective-permute-done.15.refs_1_
  123.1 2.2 %add_partials.1 = (bf16[592,128]{1,0:T(8,128)(2,1)}, bf16[592,128]{1,0:T(8,128)(2,1)}, bf16[592,128]{1,0:T(8,128)(2,1)}, bf16[592,128]{1,0:T(8,128)(2,1)}) custom-call(s32[1]{0:T(128)} %bitcast.x_ref, bf16[4,592,128]{2,1,0:T(8,128)(2,1)} %memory_attend.3.refs_0_._, bf16[4,592,128]{2,1,0:T(8,128)(2,1)} %collective-permute-done.15.refs_1_), custom_call_target="tpu_custom_call" | custom-call | flops 75776 | bytes 151552 | tf_op jit(solution)/shard_map/memory/add_partials/pallas_call | solution.py:501
  125.2 2.0 %collective-permute-start.16 = (bf16[592,128]{1,0:T(8,128)(2,1)}, bf16[592,128]{1,0:T(8,128)(2,1)S(1)}, u32[]{:S(2)}, u32[]{:S(2)}) collective-permute-start(bf16[592,128]{1,0:T(8,128)(2,1)} %get-tuple-element.25), channel_id=1, source_target_pairs={{0,1},{1,2},{2,3},{3,0},{4,5},{5,6},{6,7},{7,4},{8,9},{9,10},{10,1... | collective-permute-start | bytes 454664 | tf_op jit(solution)/shard_map/memory/ppermute | solution.py:629
  127.2 2.7 %collective-permute-start.17 = (bf16[592,128]{1,0:T(8,128)(2,1)}, bf16[592,128]{1,0:T(8,128)(2,1)S(1)}, u32[]{:S(2)}, u32[]{:S(2)}) collective-permute-start(bf16[592,128]{1,0:T(8,128)(2,1)} %get-tuple-element.26), channel_id=1, source_target_pairs={{0,2},{1,3},{2,0},{3,1},{4,6},{5,7},{6,4},{7,5},{8,10},{9,11},{10,... | collective-permute-start | bytes 454664 | tf_op jit(solution)/shard_map/memory/ppermute | solution.py:629
  129.9 1.5 %collective-permute-start.18 = (bf16[592,128]{1,0:T(8,128)(2,1)}, bf16[592,128]{1,0:T(8,128)(2,1)S(1)}, u32[]{:S(2)}, u32[]{:S(2)}) collective-permute-start(bf16[592,128]{1,0:T(8,128)(2,1)} %get-tuple-element.27), channel_id=1, source_target_pairs={{0,3},{1,0},{2,1},{3,2},{4,7},{5,4},{6,5},{7,6},{8,11},{9,8},{10,9... | collective-permute-start | bytes 454664 | tf_op jit(solution)/shard_map/memory/ppermute | solution.py:629
  131.4 5.8 %collective-permute-done.16.memory_1 = bf16[592,128]{1,0:T(8,128)(2,1)S(1)} collective-permute-done((bf16[592,128]{1,0:T(8,128)(2,1)}, bf16[592,128]{1,0:T(8,128)(2,1)S(1)}, u32[]{:S(2)}, u32[]{:S(2)}) %collective-permute-start.16) | collective-permute-done | bytes 151584 | tf_op jit(solution)/shard_map/memory/ppermute | solution.py:629
  137.2 2.5 %collective-permute-done.17.memory_2 = bf16[592,128]{1,0:T(8,128)(2,1)S(1)} collective-permute-done((bf16[592,128]{1,0:T(8,128)(2,1)}, bf16[592,128]{1,0:T(8,128)(2,1)S(1)}, u32[]{:S(2)}, u32[]{:S(2)}) %collective-permute-start.17) | collective-permute-done | bytes 151584 | tf_op jit(solution)/shard_map/memory/ppermute | solution.py:629
  139.7 0.0 collective-permute-done.18.memory_3
  139.7 0.0 all-to-all-done.3.time_hbm
  139.7 6.1 %leave.1 = bf16[576,2048]{1,0:T(8,128)(2,1)} custom-call(s32[1]{0:T(128)} %bitcast.x_ref, bf16[4,592,128]{2,1,0:T(8,128)(2,1)} %own_attend.1.refs_16_.own_hbm, bf16[592,128]{1,0:T(8,128)(2,1)} %get-tuple-element.24.memory_0, bf16[592,128]{1,0:T(8,128)(2,1)S(1)} %collective-permute-done.16.memory_1, bf16[592,128]{1,0:T(8,128)(2,1)S(1)} %collective-permute-done.17.memory_2, ...), custom_call_target="tpu_custom_call" | custom-call | flops 150994944 | bytes 630784 | tf_op jit(solution)/shard_map/exit/leave/pallas_call | solution.py:572
  (15 shorter events, 0.0 us)
Async XLA Ops:
  0.0 6.6 %copy-start.3 = (s32[1,1,6,1]{2,3,1,0:T(1,128)S(1)}, s32[1,1,6,1]{2,3,1,0:T(1,128)}, u32[]{:S(2)}) copy-start(s32[1,1,6,1]{2,3,1,0:T(1,128)} %param.15) | copy-start | bytes 76
  0.0 6.6 %copy-start.4 = (s32[1,1,6]{2,1,0:T(1,128)S(1)}, s32[1,1,6]{2,1,0:T(1,128)}, u32[]{:S(2)}) copy-start(s32[1,1,6]{2,1,0:T(1,128)} %param.16) | copy-start | bytes 76
  0.0 6.6 %copy-start.2 = (f32[2,4]{1,0:T(2,128)S(1)}, f32[2,4]{1,0:T(2,128)}, u32[]{:S(2)}) copy-start(f32[2,4]{1,0:T(2,128)} %sharpness_ref.3) | copy-start | bytes 100
  2.2 14.6 %all-to-all-start = ((bf16[4,288,256]{2,1,0:T(8,128)(2,1)}), bf16[4,288,256]{2,1,0:T(8,128)(2,1)S(1)}, u32[]{:S(2)}, u32[]{:S(2)}) async-start(bf16[4,288,256]{2,1,0:T(8,128)(2,1)} %bitcast.19), calls=%async_computation | async-start | bytes 1179648 | tf_op jit(solution)/shard_map/store/all_to_all | solution.py:626
  18.5 14.8 %collective-permute-start.4 = (bf16[8,144,256]{2,1,0:T(8,128)(2,1)}, bf16[8,144,256]{2,1,0:T(8,128)(2,1)S(1)}, u32[]{:S(2)}, u32[]{:S(2)}) collective-permute-start(bf16[8,144,256]{2,1,0:T(8,128)(2,1)} %join_pieces.1.refs_0_), channel_id=1, source_target_pairs={{0,96},{32,0},{64,32},{96,64},{1,97},{33,1},{65,33},{97,65},{2,98}... | collective-permute-start | bytes 1769480 | tf_op jit(solution)/shard_map/store/ppermute | solution.py:650
  21.6 14.0 %collective-permute-start.1 = (bf16[8,144,256]{2,1,0:T(8,128)(2,1)}, bf16[8,144,256]{2,1,0:T(8,128)(2,1)S(1)}, u32[]{:S(2)}, u32[]{:S(2)}) collective-permute-start(bf16[8,144,256]{2,1,0:T(8,128)(2,1)} %join_pieces.1.refs_0_), channel_id=1, source_target_pairs={{0,4},{4,0},{1,5},{5,1},{2,6},{6,2},{3,7},{7,3},{8,12},{12,8},{9,1... | collective-permute-start | bytes 1769480 | tf_op jit(solution)/shard_map/store/ppermute | solution.py:652
  23.5 14.8 %collective-permute-start = (bf16[8,144,256]{2,1,0:T(8,128)(2,1)}, bf16[8,144,256]{2,1,0:T(8,128)(2,1)}, u32[]{:S(2)}, u32[]{:S(2)}) collective-permute-start(bf16[8,144,256]{2,1,0:T(8,128)(2,1)} %join_pieces.1.refs_0_), channel_id=1, source_target_pairs={{0,32},{32,64},{64,96},{96,0},{1,33},{33,65},{65,97},{97,1},{2,34}... | collective-permute-start | bytes 1769480 | tf_op jit(solution)/shard_map/store/ppermute | solution.py:651
  33.3 0.9 copy-start
  35.6 24.7 %copy-start.5 = (bf16[8,144,256]{2,1,0:T(8,128)(2,1)}, bf16[8,144,256]{2,1,0:T(8,128)(2,1)S(1)}, u32[]{:S(2)}) copy-start(bf16[8,144,256]{2,1,0:T(8,128)(2,1)S(1)} %collective-permute-done.1.refs_1_) | copy-start | bytes 1769476
  38.4 21.9 %all-to-all-start.1 = ((bf16[8,592,128]{2,1,0:T(8,128)(2,1)}), bf16[8,592,128]{2,1,0:T(8,128)(2,1)S(1)}, u32[]{:S(2)}, u32[]{:S(2)}) async-start(bf16[8,592,128]{2,1,0:T(8,128)(2,1)} %bitcast.7), calls=%async_computation.1 | async-start | bytes 2424832 | tf_op jit(solution)/shard_map/queries/all_to_all | solution.py:626
  43.8 12.2 %collective-permute-start.2 = (bf16[8,144,256]{2,1,0:T(8,128)(2,1)S(1)}, bf16[8,144,256]{2,1,0:T(8,128)(2,1)}, u32[]{:S(2)}, u32[]{:S(2)}) collective-permute-start(bf16[8,144,256]{2,1,0:T(8,128)(2,1)S(1)} %collective-permute-done.1.refs_1_), channel_id=1, source_target_pairs={{0,96},{32,0},{64,32},{96,64},{1,97},{33,1},{65,33},{97,65},{2,98}... | collective-permute-start | bytes 1769480 | tf_op jit(solution)/shard_map/store/ppermute | solution.py:654
  43.8 13.5 %collective-permute-start.3 = (bf16[8,144,256]{2,1,0:T(8,128)(2,1)S(1)}, bf16[8,144,256]{2,1,0:T(8,128)(2,1)}, u32[]{:S(2)}, u32[]{:S(2)}) collective-permute-start(bf16[8,144,256]{2,1,0:T(8,128)(2,1)S(1)} %collective-permute-done.1.refs_1_), channel_id=1, source_target_pairs={{0,32},{32,64},{64,96},{96,0},{1,33},{33,65},{65,97},{97,1},{2,34}... | collective-permute-start | bytes 1769480 | tf_op jit(solution)/shard_map/store/ppermute | solution.py:655
  60.3 55.3 %all-to-all-start.2 = ((bf16[16,3,144,128]{3,2,1,0:T(8,128)(2,1)}), bf16[16,3,144,128]{3,2,1,0:T(8,128)(2,1)S(1)}, u32[]{:S(2)}, u32[]{:S(2)}) async-start(bf16[16,3,144,128]{3,2,1,0:T(8,128)(2,1)} %bitcast.18), calls=%async_computation.2 | async-start | bytes 3538944 | tf_op jit(solution)/shard_map/temporal/all_to_all | solution.py:626
  64.5 13.4 %collective-permute-start.7 = (bf16[8,144,256]{2,1,0:T(8,128)(2,1)}, bf16[8,144,256]{2,1,0:T(8,128)(2,1)S(1)}, u32[]{:S(2)}, u32[]{:S(2)}) collective-permute-start(bf16[8,144,256]{2,1,0:T(8,128)(2,1)} %join_pieces.1.refs_0_), channel_id=1, source_target_pairs={{0,16},{16,0},{1,17},{17,1},{2,18},{18,2},{3,19},{19,3},{4,20},{20... | collective-permute-start | bytes 1769480 | tf_op jit(solution)/shard_map/store/ppermute | solution.py:682
  64.7 1.1 copy-start.1
  65.8 8.1 %copy-start.6 = (bf16[8,144,256]{2,1,0:T(8,128)(2,1)S(1)}, bf16[8,144,256]{2,1,0:T(8,128)(2,1)}, u32[]{:S(2)}) copy-start(bf16[8,144,256]{2,1,0:T(8,128)(2,1)} %copy-done.5) | copy-start | bytes 1769476
  73.9 3.9 %collective-permute-start.8 = (bf16[8,144,256]{2,1,0:T(8,128)(2,1)S(1)}, bf16[8,144,256]{2,1,0:T(8,128)(2,1)S(1)}, u32[]{:S(2)}, u32[]{:S(2)}) collective-permute-start(bf16[8,144,256]{2,1,0:T(8,128)(2,1)S(1)} %copy-done.6), channel_id=1, source_target_pairs={{0,16},{16,0},{1,17},{17,1},{2,18},{18,2},{3,19},{19,3},{4,20},{20... | collective-permute-start | bytes 1769480 | tf_op jit(solution)/shard_map/store/ppermute | solution.py:682
  74.5 3.9 %collective-permute-start.9 = (bf16[8,144,256]{2,1,0:T(8,128)(2,1)S(1)}, bf16[8,144,256]{2,1,0:T(8,128)(2,1)S(1)}, u32[]{:S(2)}, u32[]{:S(2)}) collective-permute-start(bf16[8,144,256]{2,1,0:T(8,128)(2,1)S(1)} %copy-done.1), channel_id=1, source_target_pairs={{0,16},{16,0},{1,17},{17,1},{2,18},{18,2},{3,19},{19,3},{4,20},{20... | collective-permute-start | bytes 1769480 | tf_op jit(solution)/shard_map/store/ppermute | solution.py:682
  74.6 17.2 %collective-permute-start.5 = (bf16[8,144,256]{2,1,0:T(8,128)(2,1)}, bf16[8,144,256]{2,1,0:T(8,128)(2,1)}, u32[]{:S(2)}, u32[]{:S(2)}) collective-permute-start(bf16[8,144,256]{2,1,0:T(8,128)(2,1)} %collective-permute-done.refs_6_), channel_id=1, source_target_pairs={{0,32},{32,64},{64,96},{96,0},{1,33},{33,65},{65,97},{97,1},{2,34}... | collective-permute-start | bytes 1769480 | tf_op jit(solution)/shard_map/store/ppermute | solution.py:679
  75.0 16.8 %collective-permute-start.6 = (bf16[8,144,256]{2,1,0:T(8,128)(2,1)}, bf16[8,144,256]{2,1,0:T(8,128)(2,1)}, u32[]{:S(2)}, u32[]{:S(2)}) collective-permute-start(bf16[8,144,256]{2,1,0:T(8,128)(2,1)} %collective-permute-done.2.refs_3_), channel_id=1, source_target_pairs={{0,96},{32,0},{64,32},{96,64},{1,97},{33,1},{65,33},{97,65},{2,98}... | collective-permute-start | bytes 1769480 | tf_op jit(solution)/shard_map/store/ppermute | solution.py:680
  77.8 0.9 copy-start.7
  77.8 14.5 %collective-permute-start.10 = (bf16[8,144,256]{2,1,0:T(8,128)(2,1)}, bf16[8,144,256]{2,1,0:T(8,128)(2,1)}, u32[]{:S(2)}, u32[]{:S(2)}) collective-permute-start(bf16[8,144,256]{2,1,0:T(8,128)(2,1)} %collective-permute-done.2.refs_3_), channel_id=1, source_target_pairs={{0,16},{16,0},{1,17},{17,1},{2,18},{18,2},{3,19},{19,3},{4,20},{20... | collective-permute-start | bytes 1769480 | tf_op jit(solution)/shard_map/store/ppermute | solution.py:682
  77.9 1.0 copy-start.8
  77.9 14.5 %collective-permute-start.13 = (bf16[8,144,256]{2,1,0:T(8,128)(2,1)}, bf16[8,144,256]{2,1,0:T(8,128)(2,1)}, u32[]{:S(2)}, u32[]{:S(2)}) collective-permute-start(bf16[8,144,256]{2,1,0:T(8,128)(2,1)} %collective-permute-done.refs_6_), channel_id=1, source_target_pairs={{0,16},{16,0},{1,17},{17,1},{2,18},{18,2},{3,19},{19,3},{4,20},{20... | collective-permute-start | bytes 1769480 | tf_op jit(solution)/shard_map/store/ppermute | solution.py:682
  78.7 13.1 %copy-start.9 = (bf16[8,144,256]{2,1,0:T(8,128)(2,1)}, bf16[8,144,256]{2,1,0:T(8,128)(2,1)S(1)}, u32[]{:S(2)}) copy-start(bf16[8,144,256]{2,1,0:T(8,128)(2,1)S(1)} %collective-permute-done.9.refs_10_) | copy-start | bytes 1769476
  78.7 13.7 %collective-permute-start.14 = (bf16[8,144,256]{2,1,0:T(8,128)(2,1)}, bf16[8,144,256]{2,1,0:T(8,128)(2,1)}, u32[]{:S(2)}, u32[]{:S(2)}) collective-permute-start(bf16[8,144,256]{2,1,0:T(8,128)(2,1)} %collective-permute-done.3.refs_7_), channel_id=1, source_target_pairs={{0,16},{16,0},{1,17},{17,1},{2,18},{18,2},{3,19},{19,3},{4,20},{20... | collective-permute-start | bytes 1769480 | tf_op jit(solution)/shard_map/store/ppermute | solution.py:682
  91.8 2.3 %collective-permute-start.11 = (bf16[8,144,256]{2,1,0:T(8,128)(2,1)}, bf16[8,144,256]{2,1,0:T(8,128)(2,1)}, u32[]{:S(2)}, u32[]{:S(2)}) collective-permute-start(bf16[8,144,256]{2,1,0:T(8,128)(2,1)} %collective-permute-done.5.refs_4_), channel_id=1, source_target_pairs={{0,16},{16,0},{1,17},{17,1},{2,18},{18,2},{3,19},{19,3},{4,20},{20... | collective-permute-start | bytes 1769480 | tf_op jit(solution)/shard_map/store/ppermute | solution.py:682
  91.8 3.2 %collective-permute-start.12 = (bf16[8,144,256]{2,1,0:T(8,128)(2,1)}, bf16[8,144,256]{2,1,0:T(8,128)(2,1)}, u32[]{:S(2)}, u32[]{:S(2)}) collective-permute-start(bf16[8,144,256]{2,1,0:T(8,128)(2,1)} %collective-permute-done.6.refs_5_), channel_id=1, source_target_pairs={{0,16},{16,0},{1,17},{17,1},{2,18},{18,2},{3,19},{19,3},{4,20},{20... | collective-permute-start | bytes 1769480 | tf_op jit(solution)/shard_map/store/ppermute | solution.py:682
  103.2 19.8 %collective-permute-start.15 = (bf16[4,592,128]{2,1,0:T(8,128)(2,1)}, bf16[4,592,128]{2,1,0:T(8,128)(2,1)}, u32[]{:S(2)}, u32[]{:S(2)}) collective-permute-start(bf16[4,592,128]{2,1,0:T(8,128)(2,1)} %memory_attend.2.refs_16_), channel_id=1, source_target_pairs={{0,8},{8,0},{1,9},{9,1},{2,10},{10,2},{3,11},{11,3},{4,12},{12,4},... | collective-permute-start | bytes 1818632 | tf_op jit(solution)/shard_map/memory/ppermute | solution.py:697
  118.1 21.6 %all-to-all-start.3 = ((bf16[16,144,128]{2,1,0:T(8,128)(2,1)}), bf16[16,144,128]{2,1,0:T(8,128)(2,1)S(1)}, u32[]{:S(2)}, u32[]{:S(2)}) async-start(bf16[16,144,128]{2,1,0:T(8,128)(2,1)} %temporal_attend.1), calls=%async_computation.3 | async-start | bytes 1179648 | tf_op jit(solution)/shard_map/temporal/all_to_all | solution.py:626
  125.2 12.0 %collective-permute-start.16 = (bf16[592,128]{1,0:T(8,128)(2,1)}, bf16[592,128]{1,0:T(8,128)(2,1)S(1)}, u32[]{:S(2)}, u32[]{:S(2)}) collective-permute-start(bf16[592,128]{1,0:T(8,128)(2,1)} %get-tuple-element.25), channel_id=1, source_target_pairs={{0,1},{1,2},{2,3},{3,0},{4,5},{5,6},{6,7},{7,4},{8,9},{9,10},{10,1... | collective-permute-start | bytes 454664 | tf_op jit(solution)/shard_map/memory/ppermute | solution.py:629
  127.2 12.5 %collective-permute-start.17 = (bf16[592,128]{1,0:T(8,128)(2,1)}, bf16[592,128]{1,0:T(8,128)(2,1)S(1)}, u32[]{:S(2)}, u32[]{:S(2)}) collective-permute-start(bf16[592,128]{1,0:T(8,128)(2,1)} %get-tuple-element.26), channel_id=1, source_target_pairs={{0,2},{1,3},{2,0},{3,1},{4,6},{5,7},{6,4},{7,5},{8,10},{9,11},{10,... | collective-permute-start | bytes 454664 | tf_op jit(solution)/shard_map/memory/ppermute | solution.py:629
  129.9 9.8 %collective-permute-start.18 = (bf16[592,128]{1,0:T(8,128)(2,1)}, bf16[592,128]{1,0:T(8,128)(2,1)S(1)}, u32[]{:S(2)}, u32[]{:S(2)}) collective-permute-start(bf16[592,128]{1,0:T(8,128)(2,1)} %get-tuple-element.27), channel_id=1, source_target_pairs={{0,3},{1,0},{2,1},{3,2},{4,7},{5,4},{6,5},{7,6},{8,11},{9,8},{10,9... | collective-permute-start | bytes 454664 | tf_op jit(solution)/shard_map/memory/ppermute | solution.py:629

commit v14 on v13

--- a/solution.py
+++ b/solution.py
@@ -669,12 +669,12 @@
         )
 
     with jax.named_scope("temporal"):
-        sent, *_ = lax.optimization_barrier((parts, second_above, second_below))
+        sent, *_ = lax.optimization_barrier((parts, own))
         sent = swap(sent.reshape((quarters * G,) + parts.shape[2:]), frame)
 
     with jax.named_scope("store"):
-        below, second_above, second_below, own = lax.optimization_barrier(
-            (below, second_above, second_below, own)
+        below, second_above, second_below = lax.optimization_barrier(
+            (below, second_above, second_below)
         )
         far = lax.ppermute(below, "y", turn(1))
         second_far = lax.ppermute(second_above, "y", turn(-1))
@@ -695,13 +695,13 @@
         count = asked.shape[0] // sides
         sum_beside = attend((sides - 1 - side) * count, own)
         from_beside = lax.ppermute(sum_beside, "zq", other(sides))
-        sum_here = attend(side * count, sum_beside)
 
     with jax.named_scope("temporal"):
-        timed = temporal_attend(lookback_lengths, sent, after=sum_here)
+        timed = temporal_attend(lookback_lengths, sent, after=sum_beside)
         time = swap(timed, frame)
 
     with jax.named_scope("memory"):
+        sum_here = attend(side * count, timed)
         memory = swap_apart(add_partials(x, [in_hbm(sum_here), from_beside]))
 
     with jax.named_scope("exit"):

time: 147 us -> 137 us (0.932)
  waiting for transfers between devices: 48.1 us -> 40.5 us
  local copies, waits for them, and re-layouts: 3.65 us -> 2.03 us
    ppermute x1, waiting for transfers between devices: 10.2 us -> 0.01 us  [on_device(): second_above = lax.ppermute(second, 'y', turn(-1))]
    ppermute x3, waiting for transfers between devices: 8.32 us -> 4.3 us  [swap_apart(): lax.ppermute(blocks[j], 'x', turn(j))]
    all_to_all x4, waiting for transfers between devices: 7.34 us -> 10.7 us  [swap(): return lax.all_to_all(blocks, axes, split_axis=0, concat_axis=0, tiled=True)]
    ppermute x1, waiting for transfers between devices: 0.01 us -> 3.3 us  [on_device(): from_beside = lax.ppermute(sum_beside, 'zq', other(sides))]
    unnamed x21 -> x11, local copies, waits for them, and re-layouts: 3.65 us -> 2.03 us
  transfers between devices with their start and end apart: 23 -> 23, of which waited for: 12 -> 11; matrix products, arithmetic and copies ran while one was open for 0% -> 0% of each run, Pallas kernels for 30% -> 32%
where the time goes in v14:
time: 137 us; the launch traced here: 136 us
  Pallas kernels  52.4 us (38%)
  waiting for transfers between devices  40.5 us (30%)
  starting transfers between devices  40.1 us (29%)
  local copies, waits for them, and re-layouts  2.03 us (1%)
    all_to_all x4, starting transfers between devices, swap(): return lax.all_to_all(blocks, axes, split_axis=0, concat_axis=0, tiled=True)  18.5 us
    pallas_call x2, Pallas kernels, memory_attend(): pl.pallas_call(functools.partial(memory_attend_kernel, count), in_specs=[...  16.5 us
    ppermute x1, waiting for transfers between devices, on_device(): far = lax.ppermute(below, 'y', turn(1))  13.3 us
    all_to_all x4, waiting for transfers between devices, swap(): return lax.all_to_all(blocks, axes, split_axis=0, concat_axis=0, tiled=True)  10.7 us
    pallas_call x1, Pallas kernels, temporal_entry(): pl.pallas_call(functools.partial(temporal_entry_kernel, quarters), in_spe...  8.59 us
    pallas_call x1, Pallas kernels, own_attend(): pl.pallas_call(own_attend_kernel, in_specs=[HBM, HBM, HBM] + [ANY] * len(...  8.08 us
    ppermute x3, starting transfers between devices, swap_apart(): lax.ppermute(blocks[j], 'x', turn(j))  6.17 us
    pallas_call x1, Pallas kernels, leave(): pl.pallas_call(leave_kernel, in_specs=[SCALARS, HBM] + [ANY] * (G + 1) +...  6.11 us
  transfers between devices with their start and end apart: 23, of which 11 were waited for; matrix products, arithmetic and copies ran while one was open for 0% of the time, Pallas kernels for 32%

profile of v14, /device:TPU:0, one launch (start us, length us, event | category | flops | bytes accessed | tf_op | source)
XLA Modules:
  0.0 136.0 jit_solution(11004464621930433652)
XLA Ops:
  0.0 0.0 copy-start.1
  0.0 0.0 copy-start.3
  0.0 1.2 copy.10
  1.2 1.0 split_store.1._
  2.2 4.4 %all-to-all-start = ((bf16[4,288,256]{2,1,0:T(8,128)(2,1)}), bf16[4,288,256]{2,1,0:T(8,128)(2,1)S(1)}, u32[]{:S(2)}, u32[]{:S(2)}) async-start(bf16[4,288,256]{2,1,0:T(8,128)(2,1)} %bitcast.19), calls=%async_computation | async-start | bytes 1179648 | tf_op jit(solution)/shard_map/store/all_to_all | solution.py:626
  6.6 0.0 copy-done.1
  6.6 0.0 copy-done.2
  6.6 0.0 copy-done.3
  6.6 5.8 %modulate.1 = (bf16[576,2048]{1,0:T(8,128)(2,1)}, bf16[2,4,592,128]{3,2,1,0:T(8,128)(2,1)}) custom-call(bf16[576,2048]{1,0:T(8,128)(2,1)} %bitcast.20, f32[2,2048]{1,0:T(2,128)} %bitcast.22, bf16[2048,3072]{1,0:T(8,128)(2,1)} %weight_hbm.6, f32[2,4]{1,0:T(2,128)S(1)} %copy-done.1, s32[6]{0:T(128)S(1)} %bitcast.16, s32[6]{0:T(128)S(1)} %bitcast.17, ...), custom_call_target="tpu_custom_call" | custom-call | flops 75497472 | bytes 462848 | tf_op jit(solution)/shard_map/queries/modulate/pallas_call | solution.py:185
  12.4 4.4 %all-to-all-done.in_hbm = bf16[4,288,256]{2,1,0:T(8,128)(2,1)S(1)} async-done(((bf16[4,288,256]{2,1,0:T(8,128)(2,1)}), bf16[4,288,256]{2,1,0:T(8,128)(2,1)S(1)}, u32[]{:S(2)}, u32[]{:S(2)}) %all-to-all-start) | async-done | bytes 589856 | tf_op jit(solution)/shard_map/store/all_to_all | solution.py:626
  16.8 1.7 %join_pieces.1.refs_0_ = bf16[8,144,256]{2,1,0:T(8,128)(2,1)} custom-call(bf16[4,288,256]{2,1,0:T(8,128)(2,1)S(1)} %all-to-all-done.in_hbm, bf16[576,2048]{1,0:T(8,128)(2,1)} %get-tuple-element.16._.hidden_hbm), custom_call_target="tpu_custom_call" | custom-call | flops 18432 | bytes 73728 | tf_op jit(solution)/shard_map/store/join_pieces/pallas_call | solution.py:109
  18.5 3.1 %collective-permute-start = (bf16[8,144,256]{2,1,0:T(8,128)(2,1)}, bf16[8,144,256]{2,1,0:T(8,128)(2,1)S(1)}, u32[]{:S(2)}, u32[]{:S(2)}) collective-permute-start(bf16[8,144,256]{2,1,0:T(8,128)(2,1)} %join_pieces.1.refs_0_), channel_id=1, source_target_pairs={{0,96},{32,0},{64,32},{96,64},{1,97},{33,1},{65,33},{97,65},{2,98}... | collective-permute-start | bytes 1769480 | tf_op jit(solution)/shard_map/store/ppermute | solution.py:650
  21.6 1.9 %collective-permute-start.1 = (bf16[8,144,256]{2,1,0:T(8,128)(2,1)}, bf16[8,144,256]{2,1,0:T(8,128)(2,1)}, u32[]{:S(2)}, u32[]{:S(2)}) collective-permute-start(bf16[8,144,256]{2,1,0:T(8,128)(2,1)} %join_pieces.1.refs_0_), channel_id=1, source_target_pairs={{0,4},{4,0},{1,5},{5,1},{2,6},{6,2},{3,7},{7,3},{8,12},{12,8},{9,1... | collective-permute-start | bytes 1769480 | tf_op jit(solution)/shard_map/store/ppermute | solution.py:652
  23.5 0.0 collective-permute-start.2
  23.5 8.6 %temporal_entry.1.refs_0_ = bf16[4,4,3,144,128]{4,3,2,1,0:T(8,128)(2,1)} custom-call(bf16[576,2048]{1,0:T(8,128)(2,1)} %get-tuple-element.16._.hidden_hbm, bf16[2048,3072]{1,0:T(8,128)(2,1)} %weight_hbm.6, f32[2,4]{1,0:T(2,128)S(1)} %copy-done.1, bf16[8,144,256]{2,1,0:T(8,128)(2,1)} %join_pieces.1.refs_0_), custom_call_target="tpu_custom_call" | custom-call | flops 226492416 | bytes 651264 | tf_op jit(solution)/shard_map/temporal/temporal_entry/pallas_call | solution.py:250
  32.1 1.2 collective-permute-done.refs_1_.refs_2_
  33.3 2.4 %collective-permute-done.1.refs_1_ = bf16[8,144,256]{2,1,0:T(8,128)(2,1)} collective-permute-done((bf16[8,144,256]{2,1,0:T(8,128)(2,1)}, bf16[8,144,256]{2,1,0:T(8,128)(2,1)}, u32[]{:S(2)}, u32[]{:S(2)}) %collective-permute-start.1) | collective-permute-done | bytes 589856 | tf_op jit(solution)/shard_map/store/ppermute | solution.py:652
  35.7 2.5 %collective-permute-done.2.refs_6_ = bf16[8,144,256]{2,1,0:T(8,128)(2,1)S(1)} collective-permute-done((bf16[8,144,256]{2,1,0:T(8,128)(2,1)}, bf16[8,144,256]{2,1,0:T(8,128)(2,1)S(1)}, u32[]{:S(2)}, u32[]{:S(2)}) %collective-permute-start.2) | collective-permute-done | bytes 589856 | tf_op jit(solution)/shard_map/store/ppermute | solution.py:651
  38.2 0.8 copy-done.4
  39.1 5.5 %all-to-all-start.1 = ((bf16[8,592,128]{2,1,0:T(8,128)(2,1)}), bf16[8,592,128]{2,1,0:T(8,128)(2,1)S(1)}, u32[]{:S(2)}, u32[]{:S(2)}) async-start(bf16[8,592,128]{2,1,0:T(8,128)(2,1)} %bitcast.7), calls=%async_computation.1 | async-start | bytes 2424832 | tf_op jit(solution)/shard_map/queries/all_to_all | solution.py:626
  44.5 0.0 collective-permute-start.3
  44.5 2.0 %collective-permute-start.4 = (bf16[8,144,256]{2,1,0:T(8,128)(2,1)}, bf16[8,144,256]{2,1,0:T(8,128)(2,1)}, u32[]{:S(2)}, u32[]{:S(2)}) collective-permute-start(bf16[8,144,256]{2,1,0:T(8,128)(2,1)} %collective-permute-done.1.refs_1_), channel_id=1, source_target_pairs={{0,32},{32,64},{64,96},{96,0},{1,33},{33,65},{65,97},{97,1},{2,34}... | collective-permute-start | bytes 1769480 | tf_op jit(solution)/shard_map/store/ppermute | solution.py:655
  46.6 8.1 %own_attend.1.refs_16_.own_hbm = bf16[4,592,128]{2,1,0:T(8,128)(2,1)} custom-call(bf16[576,2048]{1,0:T(8,128)(2,1)} %get-tuple-element.16._.hidden_hbm, bf16[2048,3072]{1,0:T(8,128)(2,1)} %weight_hbm.6, bf16[2,4,592,128]{3,2,1,0:T(8,128)(2,1)} %get-tuple-element.18.query_hbm, bf16[4,4,3,144,128]{4,3,2,1,0:T(8,128)(2,1)} %temporal_entry.1.refs_0_, ...), custom_call_target="tpu_custom_call" | custom-call | flops 214695936 | bytes 593920 | tf_op jit(solution)/shard_map/own/own_attend/pallas_call | solution.py:380
  54.6 0.0 copy-done
  54.7 6.4 %all-to-all-done.1.query_hbm = bf16[8,592,128]{2,1,0:T(8,128)(2,1)S(1)} async-done(((bf16[8,592,128]{2,1,0:T(8,128)(2,1)}), bf16[8,592,128]{2,1,0:T(8,128)(2,1)S(1)}, u32[]{:S(2)}, u32[]{:S(2)}) %all-to-all-start.1) | async-done | bytes 1212448 | tf_op jit(solution)/shard_map/queries/all_to_all | solution.py:626
  61.0 3.7 %all-to-all-start.2 = ((bf16[16,3,144,128]{3,2,1,0:T(8,128)(2,1)}), bf16[16,3,144,128]{3,2,1,0:T(8,128)(2,1)S(1)}, u32[]{:S(2)}, u32[]{:S(2)}) async-start(bf16[16,3,144,128]{3,2,1,0:T(8,128)(2,1)} %bitcast.18), calls=%async_computation.2 | async-start | bytes 3538944 | tf_op jit(solution)/shard_map/temporal/all_to_all | solution.py:626
  64.7 0.3 collective-permute-start.7
  65.0 0.5 collective-permute-start.8
  65.5 0.1 collective-permute-start.9
  65.6 0.0 collective-permute-done.3.refs_3_
  65.6 0.0 collective-permute-done.4.refs_7_
  65.6 0.0 collective-permute-start.5
  65.6 3.2 %collective-permute-start.6 = (bf16[8,144,256]{2,1,0:T(8,128)(2,1)}, bf16[8,144,256]{2,1,0:T(8,128)(2,1)}, u32[]{:S(2)}, u32[]{:S(2)}) collective-permute-start(bf16[8,144,256]{2,1,0:T(8,128)(2,1)} %collective-permute-done.3.refs_3_), channel_id=1, source_target_pairs={{0,96},{32,0},{64,32},{96,64},{1,97},{33,1},{65,33},{97,65},{2,98}... | collective-permute-start | bytes 1769480 | tf_op jit(solution)/shard_map/store/ppermute | solution.py:680
  68.8 0.0 collective-permute-done.7.refs_8_
  68.8 0.0 collective-permute-start.10
  68.8 0.0 collective-permute-done.8.refs_9_
  68.9 0.5 collective-permute-start.13
  69.4 0.0 collective-permute-done.9.refs_10_
  69.4 0.1 collective-permute-start.14
  69.4 13.3 %collective-permute-done.5.refs_4_ = bf16[8,144,256]{2,1,0:T(8,128)(2,1)} collective-permute-done((bf16[8,144,256]{2,1,0:T(8,128)(2,1)}, bf16[8,144,256]{2,1,0:T(8,128)(2,1)}, u32[]{:S(2)}, u32[]{:S(2)}) %collective-permute-start.5) | collective-permute-done | bytes 589856 | tf_op jit(solution)/shard_map/store/ppermute | solution.py:679
  82.8 0.0 collective-permute-start.11
  82.8 0.0 collective-permute-done.6.refs_5_
  82.8 0.5 collective-permute-start.12
  83.3 0.0 collective-permute-done.10.refs_11_
  83.3 0.0 collective-permute-done.13.refs_14_
  83.4 0.0 collective-permute-done.14.refs_15_
  83.4 1.8 %collective-permute-done.11.refs_12_ = bf16[8,144,256]{2,1,0:T(8,128)(2,1)} collective-permute-done((bf16[8,144,256]{2,1,0:T(8,128)(2,1)}, bf16[8,144,256]{2,1,0:T(8,128)(2,1)}, u32[]{:S(2)}, u32[]{:S(2)}) %collective-permute-start.11) | collective-permute-done | bytes 589856 | tf_op jit(solution)/shard_map/store/ppermute | solution.py:682
  85.1 0.8 collective-permute-done.12.refs_13_
  86.0 8.2 %memory_attend.2._ = bf16[4,592,128]{2,1,0:T(8,128)(2,1)} custom-call(s32[1]{0:T(128)} %bitcast.10.base_ref, s32[8,6]{1,0:T(8,128)S(1)} %fusion.6.index_ref, bf16[8,592,128]{2,1,0:T(8,128)(2,1)S(1)} %all-to-all-done.1.query_hbm, bf16[8,144,256]{2,1,0:T(8,128)(2,1)} %join_pieces.1.refs_0_, bf16[8,144,256]{2,1,0:T(8,128)(2,1)} %collective-permute-done.1.refs_1_, ...), custom_call_target="tpu_custom_call" | custom-call | flops 261881856 | bytes 186368 | tf_op jit(solution)/shard_map/memory/memory_attend/pallas_call | solution.py:449
  94.2 3.2 %collective-permute-start.15 = (bf16[4,592,128]{2,1,0:T(8,128)(2,1)}, bf16[4,592,128]{2,1,0:T(8,128)(2,1)}, u32[]{:S(2)}, u32[]{:S(2)}) collective-permute-start(bf16[4,592,128]{2,1,0:T(8,128)(2,1)} %memory_attend.2._), channel_id=1, source_target_pairs={{0,8},{8,0},{1,9},{9,1},{2,10},{10,2},{3,11},{11,3},{4,12},{12,4},... | collective-permute-start | bytes 1818632 | tf_op jit(solution)/shard_map/memory/ppermute | solution.py:697
  98.1 0.0 all-to-all-done.2.in_hbm_ref
  98.1 2.4 %temporal_attend.1.refs_16_ = bf16[16,144,128]{2,1,0:T(8,128)(2,1)} custom-call(s32[1]{0:T(128)S(6)} %copy.11.length_ref, bf16[16,3,144,128]{3,2,1,0:T(8,128)(2,1)S(1)} %all-to-all-done.2.in_hbm_ref, bf16[4,592,128]{2,1,0:T(8,128)(2,1)} %memory_attend.2._), custom_call_target="tpu_custom_call" | custom-call | flops 18874368 | bytes 147456 | tf_op jit(solution)/shard_map/temporal/temporal_attend/pallas_call | solution.py:300
  100.5 5.0 %all-to-all-start.3 = ((bf16[16,144,128]{2,1,0:T(8,128)(2,1)}), bf16[16,144,128]{2,1,0:T(8,128)(2,1)S(1)}, u32[]{:S(2)}, u32[]{:S(2)}) async-start(bf16[16,144,128]{2,1,0:T(8,128)(2,1)} %temporal_attend.1.refs_16_), calls=%async_computation.3 | async-start | bytes 1179648 | tf_op jit(solution)/shard_map/temporal/all_to_all | solution.py:626
  105.5 8.3 %memory_attend.3.refs_0_ = bf16[4,592,128]{2,1,0:T(8,128)(2,1)} custom-call(s32[1]{0:T(128)} %bitcast.6.base_ref, s32[8,6]{1,0:T(8,128)S(1)} %fusion.6.index_ref, bf16[8,592,128]{2,1,0:T(8,128)(2,1)S(1)} %all-to-all-done.1.query_hbm, bf16[8,144,256]{2,1,0:T(8,128)(2,1)} %join_pieces.1.refs_0_, bf16[8,144,256]{2,1,0:T(8,128)(2,1)} %collective-permute-done.1.refs_1_, ...), custom_call_target="tpu_custom_call" | custom-call | flops 261881856 | bytes 186368 | tf_op jit(solution)/shard_map/memory/memory_attend/pallas_call | solution.py:449
  113.8 3.3 %collective-permute-done.15.refs_1_ = bf16[4,592,128]{2,1,0:T(8,128)(2,1)} collective-permute-done((bf16[4,592,128]{2,1,0:T(8,128)(2,1)}, bf16[4,592,128]{2,1,0:T(8,128)(2,1)}, u32[]{:S(2)}, u32[]{:S(2)}) %collective-permute-start.15) | collective-permute-done | bytes 606240 | tf_op jit(solution)/shard_map/memory/ppermute | solution.py:697
  117.1 2.1 %add_partials.1 = (bf16[592,128]{1,0:T(8,128)(2,1)}, bf16[592,128]{1,0:T(8,128)(2,1)}, bf16[592,128]{1,0:T(8,128)(2,1)}, bf16[592,128]{1,0:T(8,128)(2,1)}) custom-call(s32[1]{0:T(128)} %bitcast.x_ref, bf16[4,592,128]{2,1,0:T(8,128)(2,1)} %memory_attend.3.refs_0_, bf16[4,592,128]{2,1,0:T(8,128)(2,1)} %collective-permute-done.15.refs_1_), custom_call_target="tpu_custom_call" | custom-call | flops 75776 | bytes 151552 | tf_op jit(solution)/shard_map/memory/add_partials/pallas_call | solution.py:501
  119.2 2.0 %collective-permute-start.16 = (bf16[592,128]{1,0:T(8,128)(2,1)}, bf16[592,128]{1,0:T(8,128)(2,1)S(1)}, u32[]{:S(2)}, u32[]{:S(2)}) collective-permute-start(bf16[592,128]{1,0:T(8,128)(2,1)} %get-tuple-element.24), channel_id=1, source_target_pairs={{0,1},{1,2},{2,3},{3,0},{4,5},{5,6},{6,7},{7,4},{8,9},{9,10},{10,1... | collective-permute-start | bytes 454664 | tf_op jit(solution)/shard_map/memory/ppermute | solution.py:629
  121.2 2.7 %collective-permute-start.17 = (bf16[592,128]{1,0:T(8,128)(2,1)}, bf16[592,128]{1,0:T(8,128)(2,1)S(1)}, u32[]{:S(2)}, u32[]{:S(2)}) collective-permute-start(bf16[592,128]{1,0:T(8,128)(2,1)} %get-tuple-element.25), channel_id=1, source_target_pairs={{0,2},{1,3},{2,0},{3,1},{4,6},{5,7},{6,4},{7,5},{8,10},{9,11},{10,... | collective-permute-start | bytes 454664 | tf_op jit(solution)/shard_map/memory/ppermute | solution.py:629
  123.9 1.5 %collective-permute-start.18 = (bf16[592,128]{1,0:T(8,128)(2,1)}, bf16[592,128]{1,0:T(8,128)(2,1)S(1)}, u32[]{:S(2)}, u32[]{:S(2)}) collective-permute-start(bf16[592,128]{1,0:T(8,128)(2,1)} %get-tuple-element.26), channel_id=1, source_target_pairs={{0,3},{1,0},{2,1},{3,2},{4,7},{5,4},{6,5},{7,6},{8,11},{9,8},{10,9... | collective-permute-start | bytes 454664 | tf_op jit(solution)/shard_map/memory/ppermute | solution.py:629
  125.4 0.0 all-to-all-done.3.time_hbm
  125.4 2.1 %collective-permute-done.16.memory_1 = bf16[592,128]{1,0:T(8,128)(2,1)S(1)} collective-permute-done((bf16[592,128]{1,0:T(8,128)(2,1)}, bf16[592,128]{1,0:T(8,128)(2,1)S(1)}, u32[]{:S(2)}, u32[]{:S(2)}) %collective-permute-start.16) | collective-permute-done | bytes 151584 | tf_op jit(solution)/shard_map/memory/ppermute | solution.py:629
  127.5 2.2 %collective-permute-done.17.memory_2 = bf16[592,128]{1,0:T(8,128)(2,1)S(1)} collective-permute-done((bf16[592,128]{1,0:T(8,128)(2,1)}, bf16[592,128]{1,0:T(8,128)(2,1)S(1)}, u32[]{:S(2)}, u32[]{:S(2)}) %collective-permute-start.17) | collective-permute-done | bytes 151584 | tf_op jit(solution)/shard_map/memory/ppermute | solution.py:629
  129.7 0.0 collective-permute-done.18.memory_3
  129.7 6.1 %leave.1 = bf16[576,2048]{1,0:T(8,128)(2,1)} custom-call(s32[1]{0:T(128)} %bitcast.x_ref, bf16[4,592,128]{2,1,0:T(8,128)(2,1)} %own_attend.1.refs_16_.own_hbm, bf16[592,128]{1,0:T(8,128)(2,1)} %get-tuple-element.23.memory_0, bf16[592,128]{1,0:T(8,128)(2,1)S(1)} %collective-permute-done.16.memory_1, bf16[592,128]{1,0:T(8,128)(2,1)S(1)} %collective-permute-done.17.memory_2, ...), custom_call_target="tpu_custom_call" | custom-call | flops 150994944 | bytes 630784 | tf_op jit(solution)/shard_map/exit/leave/pallas_call | solution.py:572
  (5 shorter events, 0.0 us)
Async XLA Ops:
  0.0 6.6 %copy-start.1 = (f32[2,4]{1,0:T(2,128)S(1)}, f32[2,4]{1,0:T(2,128)}, u32[]{:S(2)}) copy-start(f32[2,4]{1,0:T(2,128)} %sharpness_ref.3) | copy-start | bytes 100
  0.0 6.6 %copy-start.2 = (s32[1,1,6,1]{2,3,1,0:T(1,128)S(1)}, s32[1,1,6,1]{2,3,1,0:T(1,128)}, u32[]{:S(2)}) copy-start(s32[1,1,6,1]{2,3,1,0:T(1,128)} %param.15) | copy-start | bytes 76
  0.0 6.6 %copy-start.3 = (s32[1,1,6]{2,1,0:T(1,128)S(1)}, s32[1,1,6]{2,1,0:T(1,128)}, u32[]{:S(2)}) copy-start(s32[1,1,6]{2,1,0:T(1,128)} %param.16) | copy-start | bytes 76
  2.2 14.6 %all-to-all-start = ((bf16[4,288,256]{2,1,0:T(8,128)(2,1)}), bf16[4,288,256]{2,1,0:T(8,128)(2,1)S(1)}, u32[]{:S(2)}, u32[]{:S(2)}) async-start(bf16[4,288,256]{2,1,0:T(8,128)(2,1)} %bitcast.19), calls=%async_computation | async-start | bytes 1179648 | tf_op jit(solution)/shard_map/store/all_to_all | solution.py:626
  18.5 14.8 %collective-permute-start = (bf16[8,144,256]{2,1,0:T(8,128)(2,1)}, bf16[8,144,256]{2,1,0:T(8,128)(2,1)S(1)}, u32[]{:S(2)}, u32[]{:S(2)}) collective-permute-start(bf16[8,144,256]{2,1,0:T(8,128)(2,1)} %join_pieces.1.refs_0_), channel_id=1, source_target_pairs={{0,96},{32,0},{64,32},{96,64},{1,97},{33,1},{65,33},{97,65},{2,98}... | collective-permute-start | bytes 1769480 | tf_op jit(solution)/shard_map/store/ppermute | solution.py:650
  21.6 14.1 %collective-permute-start.1 = (bf16[8,144,256]{2,1,0:T(8,128)(2,1)}, bf16[8,144,256]{2,1,0:T(8,128)(2,1)}, u32[]{:S(2)}, u32[]{:S(2)}) collective-permute-start(bf16[8,144,256]{2,1,0:T(8,128)(2,1)} %join_pieces.1.refs_0_), channel_id=1, source_target_pairs={{0,4},{4,0},{1,5},{5,1},{2,6},{6,2},{3,7},{7,3},{8,12},{12,8},{9,1... | collective-permute-start | bytes 1769480 | tf_op jit(solution)/shard_map/store/ppermute | solution.py:652
  23.5 14.7 %collective-permute-start.2 = (bf16[8,144,256]{2,1,0:T(8,128)(2,1)}, bf16[8,144,256]{2,1,0:T(8,128)(2,1)S(1)}, u32[]{:S(2)}, u32[]{:S(2)}) collective-permute-start(bf16[8,144,256]{2,1,0:T(8,128)(2,1)} %join_pieces.1.refs_0_), channel_id=1, source_target_pairs={{0,32},{32,64},{64,96},{96,0},{1,33},{33,65},{65,97},{97,1},{2,34}... | collective-permute-start | bytes 1769480 | tf_op jit(solution)/shard_map/store/ppermute | solution.py:651
  33.3 21.4 %copy-start = (bf16[8,144,256]{2,1,0:T(8,128)(2,1)}, bf16[8,144,256]{2,1,0:T(8,128)(2,1)S(1)}, u32[]{:S(2)}) copy-start(bf16[8,144,256]{2,1,0:T(8,128)(2,1)S(1)} %collective-permute-done.refs_1_.refs_2_) | copy-start | bytes 1769476
  38.2 0.8 copy-start.4
  39.1 21.9 %all-to-all-start.1 = ((bf16[8,592,128]{2,1,0:T(8,128)(2,1)}), bf16[8,592,128]{2,1,0:T(8,128)(2,1)S(1)}, u32[]{:S(2)}, u32[]{:S(2)}) async-start(bf16[8,592,128]{2,1,0:T(8,128)(2,1)} %bitcast.7), calls=%async_computation.1 | async-start | bytes 2424832 | tf_op jit(solution)/shard_map/queries/all_to_all | solution.py:626
  44.5 21.1 %collective-permute-start.3 = (bf16[8,144,256]{2,1,0:T(8,128)(2,1)}, bf16[8,144,256]{2,1,0:T(8,128)(2,1)}, u32[]{:S(2)}, u32[]{:S(2)}) collective-permute-start(bf16[8,144,256]{2,1,0:T(8,128)(2,1)} %collective-permute-done.1.refs_1_), channel_id=1, source_target_pairs={{0,96},{32,0},{64,32},{96,64},{1,97},{33,1},{65,33},{97,65},{2,98}... | collective-permute-start | bytes 1769480 | tf_op jit(solution)/shard_map/store/ppermute | solution.py:654
  44.5 21.1 %collective-permute-start.4 = (bf16[8,144,256]{2,1,0:T(8,128)(2,1)}, bf16[8,144,256]{2,1,0:T(8,128)(2,1)}, u32[]{:S(2)}, u32[]{:S(2)}) collective-permute-start(bf16[8,144,256]{2,1,0:T(8,128)(2,1)} %collective-permute-done.1.refs_1_), channel_id=1, source_target_pairs={{0,32},{32,64},{64,96},{96,0},{1,33},{33,65},{65,97},{97,1},{2,34}... | collective-permute-start | bytes 1769480 | tf_op jit(solution)/shard_map/store/ppermute | solution.py:655
  61.0 37.1 %all-to-all-start.2 = ((bf16[16,3,144,128]{3,2,1,0:T(8,128)(2,1)}), bf16[16,3,144,128]{3,2,1,0:T(8,128)(2,1)S(1)}, u32[]{:S(2)}, u32[]{:S(2)}) async-start(bf16[16,3,144,128]{3,2,1,0:T(8,128)(2,1)} %bitcast.18), calls=%async_computation.2 | async-start | bytes 3538944 | tf_op jit(solution)/shard_map/temporal/all_to_all | solution.py:626
  64.7 4.1 %collective-permute-start.7 = (bf16[8,144,256]{2,1,0:T(8,128)(2,1)}, bf16[8,144,256]{2,1,0:T(8,128)(2,1)}, u32[]{:S(2)}, u32[]{:S(2)}) collective-permute-start(bf16[8,144,256]{2,1,0:T(8,128)(2,1)} %join_pieces.1.refs_0_), channel_id=1, source_target_pairs={{0,16},{16,0},{1,17},{17,1},{2,18},{18,2},{3,19},{19,3},{4,20},{20... | collective-permute-start | bytes 1769480 | tf_op jit(solution)/shard_map/store/ppermute | solution.py:682
  65.0 3.8 %collective-permute-start.8 = (bf16[8,144,256]{2,1,0:T(8,128)(2,1)}, bf16[8,144,256]{2,1,0:T(8,128)(2,1)}, u32[]{:S(2)}, u32[]{:S(2)}) collective-permute-start(bf16[8,144,256]{2,1,0:T(8,128)(2,1)} %collective-permute-done.1.refs_1_), channel_id=1, source_target_pairs={{0,16},{16,0},{1,17},{17,1},{2,18},{18,2},{3,19},{19,3},{4,20},{20... | collective-permute-start | bytes 1769480 | tf_op jit(solution)/shard_map/store/ppermute | solution.py:682
  65.5 3.9 %collective-permute-start.9 = (bf16[8,144,256]{2,1,0:T(8,128)(2,1)}, bf16[8,144,256]{2,1,0:T(8,128)(2,1)}, u32[]{:S(2)}, u32[]{:S(2)}) collective-permute-start(bf16[8,144,256]{2,1,0:T(8,128)(2,1)} %copy-done), channel_id=1, source_target_pairs={{0,16},{16,0},{1,17},{17,1},{2,18},{18,2},{3,19},{19,3},{4,20},{20... | collective-permute-start | bytes 1769480 | tf_op jit(solution)/shard_map/store/ppermute | solution.py:682
  65.6 17.2 %collective-permute-start.5 = (bf16[8,144,256]{2,1,0:T(8,128)(2,1)}, bf16[8,144,256]{2,1,0:T(8,128)(2,1)}, u32[]{:S(2)}, u32[]{:S(2)}) collective-permute-start(bf16[8,144,256]{2,1,0:T(8,128)(2,1)} %copy-done.4), channel_id=1, source_target_pairs={{0,32},{32,64},{64,96},{96,0},{1,33},{33,65},{65,97},{97,1},{2,34}... | collective-permute-start | bytes 1769480 | tf_op jit(solution)/shard_map/store/ppermute | solution.py:679
  65.6 17.2 %collective-permute-start.6 = (bf16[8,144,256]{2,1,0:T(8,128)(2,1)}, bf16[8,144,256]{2,1,0:T(8,128)(2,1)}, u32[]{:S(2)}, u32[]{:S(2)}) collective-permute-start(bf16[8,144,256]{2,1,0:T(8,128)(2,1)} %collective-permute-done.3.refs_3_), channel_id=1, source_target_pairs={{0,96},{32,0},{64,32},{96,64},{1,97},{33,1},{65,33},{97,65},{2,98}... | collective-permute-start | bytes 1769480 | tf_op jit(solution)/shard_map/store/ppermute | solution.py:680
  68.8 14.5 %collective-permute-start.10 = (bf16[8,144,256]{2,1,0:T(8,128)(2,1)}, bf16[8,144,256]{2,1,0:T(8,128)(2,1)}, u32[]{:S(2)}, u32[]{:S(2)}) collective-permute-start(bf16[8,144,256]{2,1,0:T(8,128)(2,1)} %collective-permute-done.3.refs_3_), channel_id=1, source_target_pairs={{0,16},{16,0},{1,17},{17,1},{2,18},{18,2},{3,19},{19,3},{4,20},{20... | collective-permute-start | bytes 1769480 | tf_op jit(solution)/shard_map/store/ppermute | solution.py:682
  68.9 14.5 %collective-permute-start.13 = (bf16[8,144,256]{2,1,0:T(8,128)(2,1)}, bf16[8,144,256]{2,1,0:T(8,128)(2,1)}, u32[]{:S(2)}, u32[]{:S(2)}) collective-permute-start(bf16[8,144,256]{2,1,0:T(8,128)(2,1)} %copy-done.4), channel_id=1, source_target_pairs={{0,16},{16,0},{1,17},{17,1},{2,18},{18,2},{3,19},{19,3},{4,20},{20... | collective-permute-start | bytes 1769480 | tf_op jit(solution)/shard_map/store/ppermute | solution.py:682
  69.4 14.0 %collective-permute-start.14 = (bf16[8,144,256]{2,1,0:T(8,128)(2,1)}, bf16[8,144,256]{2,1,0:T(8,128)(2,1)}, u32[]{:S(2)}, u32[]{:S(2)}) collective-permute-start(bf16[8,144,256]{2,1,0:T(8,128)(2,1)} %collective-permute-done.4.refs_7_), channel_id=1, source_target_pairs={{0,16},{16,0},{1,17},{17,1},{2,18},{18,2},{3,19},{19,3},{4,20},{20... | collective-permute-start | bytes 1769480 | tf_op jit(solution)/shard_map/store/ppermute | solution.py:682
  82.8 2.3 %collective-permute-start.11 = (bf16[8,144,256]{2,1,0:T(8,128)(2,1)}, bf16[8,144,256]{2,1,0:T(8,128)(2,1)}, u32[]{:S(2)}, u32[]{:S(2)}) collective-permute-start(bf16[8,144,256]{2,1,0:T(8,128)(2,1)} %collective-permute-done.5.refs_4_), channel_id=1, source_target_pairs={{0,16},{16,0},{1,17},{17,1},{2,18},{18,2},{3,19},{19,3},{4,20},{20... | collective-permute-start | bytes 1769480 | tf_op jit(solution)/shard_map/store/ppermute | solution.py:682
  82.8 3.2 %collective-permute-start.12 = (bf16[8,144,256]{2,1,0:T(8,128)(2,1)}, bf16[8,144,256]{2,1,0:T(8,128)(2,1)}, u32[]{:S(2)}, u32[]{:S(2)}) collective-permute-start(bf16[8,144,256]{2,1,0:T(8,128)(2,1)} %collective-permute-done.6.refs_5_), channel_id=1, source_target_pairs={{0,16},{16,0},{1,17},{17,1},{2,18},{18,2},{3,19},{19,3},{4,20},{20... | collective-permute-start | bytes 1769480 | tf_op jit(solution)/shard_map/store/ppermute | solution.py:682
  94.2 22.8 %collective-permute-start.15 = (bf16[4,592,128]{2,1,0:T(8,128)(2,1)}, bf16[4,592,128]{2,1,0:T(8,128)(2,1)}, u32[]{:S(2)}, u32[]{:S(2)}) collective-permute-start(bf16[4,592,128]{2,1,0:T(8,128)(2,1)} %memory_attend.2._), channel_id=1, source_target_pairs={{0,8},{8,0},{1,9},{9,1},{2,10},{10,2},{3,11},{11,3},{4,12},{12,4},... | collective-permute-start | bytes 1818632 | tf_op jit(solution)/shard_map/memory/ppermute | solution.py:697
  100.5 24.9 %all-to-all-start.3 = ((bf16[16,144,128]{2,1,0:T(8,128)(2,1)}), bf16[16,144,128]{2,1,0:T(8,128)(2,1)S(1)}, u32[]{:S(2)}, u32[]{:S(2)}) async-start(bf16[16,144,128]{2,1,0:T(8,128)(2,1)} %temporal_attend.1.refs_16_), calls=%async_computation.3 | async-start | bytes 1179648 | tf_op jit(solution)/shard_map/temporal/all_to_all | solution.py:626
  119.2 8.3 %collective-permute-start.16 = (bf16[592,128]{1,0:T(8,128)(2,1)}, bf16[592,128]{1,0:T(8,128)(2,1)S(1)}, u32[]{:S(2)}, u32[]{:S(2)}) collective-permute-start(bf16[592,128]{1,0:T(8,128)(2,1)} %get-tuple-element.24), channel_id=1, source_target_pairs={{0,1},{1,2},{2,3},{3,0},{4,5},{5,6},{6,7},{7,4},{8,9},{9,10},{10,1... | collective-permute-start | bytes 454664 | tf_op jit(solution)/shard_map/memory/ppermute | solution.py:629
  121.2 8.5 %collective-permute-start.17 = (bf16[592,128]{1,0:T(8,128)(2,1)}, bf16[592,128]{1,0:T(8,128)(2,1)S(1)}, u32[]{:S(2)}, u32[]{:S(2)}) collective-permute-start(bf16[592,128]{1,0:T(8,128)(2,1)} %get-tuple-element.25), channel_id=1, source_target_pairs={{0,2},{1,3},{2,0},{3,1},{4,6},{5,7},{6,4},{7,5},{8,10},{9,11},{10,... | collective-permute-start | bytes 454664 | tf_op jit(solution)/shard_map/memory/ppermute | solution.py:629
  123.9 5.8 %collective-permute-start.18 = (bf16[592,128]{1,0:T(8,128)(2,1)}, bf16[592,128]{1,0:T(8,128)(2,1)S(1)}, u32[]{:S(2)}, u32[]{:S(2)}) collective-permute-start(bf16[592,128]{1,0:T(8,128)(2,1)} %get-tuple-element.26), channel_id=1, source_target_pairs={{0,3},{1,0},{2,1},{3,2},{4,7},{5,4},{6,5},{7,6},{8,11},{9,8},{10,9... | collective-permute-start | bytes 454664 | tf_op jit(solution)/shard_map/memory/ppermute | solution.py:629

commit v15 on v14

--- a/solution.py
+++ b/solution.py
@@ -401,18 +401,17 @@
     )(in_hbm(hidden), in_hbm(weight), in_hbm(query), *after)
 
 
-def memory_attend_kernel(count, base_ref, index_ref, query_hbm, *refs):
+def memory_attend_kernel(count, first, index_ref, query_hbm, *refs):
     blocks = refs[:count]
     out_hbm, query_ref, store_ref, out_ref, query_sem, block_sem, store_sem = refs[count + 1 :]
     frames = query_ref.shape[0]
     held = blocks[0].shape[0]
-    base = base_ref[0]
-    query_load = copy(query_hbm.at[pl.ds(base, frames)], query_ref, query_sem)
+    query_load = copy(query_hbm, query_ref, query_sem)
     query_load.start()
 
     def fetch(t, carry):
         i, j = t // TOPM, lax.rem(t, TOPM)
-        wanted = index_ref[base + i, j]
+        wanted = index_ref[first + i, j]
         for b in range(count // 2):
 
             @pl.when(wanted // held == b)
@@ -441,14 +440,14 @@
         store.wait()
 
 
-def memory_attend(base, index, query, frames, blocks, after):
+def memory_attend(first, index, query, blocks, after):
     count = len(blocks)
-    rows = query.shape[1]
+    frames, rows, _ = query.shape
     _, part, width = blocks[0].shape
     shape = (frames, rows, C)
     return pl.pallas_call(
-        functools.partial(memory_attend_kernel, count),
-        in_specs=[SCALARS, SCALARS] + [ANY] * (count + 2),
+        functools.partial(memory_attend_kernel, count, first),
+        in_specs=[SCALARS] + [ANY] * (count + 2),
         out_specs=HBM,
         out_shape=hbm_out(shape),
         scratch_shapes=[
@@ -465,7 +464,7 @@
             16 * frames * rows * TOPM * part * C,
             4 * frames * rows * C + 2 * frames * TOPM * part * width,
         ),
-    )(base, index, query, *blocks, in_hbm(after))
+    )(index, query, *blocks, in_hbm(after))
 
 
 def add_partials_kernel(count, x_ref, *refs):
@@ -614,7 +613,6 @@
     held, piece = cached_past_pairs.shape[:2]
     cores = lax.axis_size("c")
     x = lax.axis_index("x").astype(jnp.int32).reshape(1)
-    side = lax.axis_index("zq").astype(jnp.int32).reshape(1)
 
     def turn(step):
         return [(s, (s + step) % rings) for s in range(rings)]
@@ -641,9 +639,10 @@
             recalled_picture_holder.reshape(TOPM),
             recalled_picture_position.reshape(TOPM),
             held,
-            sides,
+            1,
             after=split,
         )
+        here = swap(query[0], "x")
 
     with jax.named_scope("store"):
         joined = join_pieces(pieces, held, after=hidden)
@@ -660,8 +659,8 @@
         )
 
     with jax.named_scope("queries"):
-        asked, *_ = lax.optimization_barrier((query, second, above, below, parts))
-        asked = swap(asked.reshape((-1,) + asked.shape[2:]), ("zq", "x"))
+        here, *_ = lax.optimization_barrier((here, second, above, below, parts))
+        beside = lax.ppermute(here, "zq", other(sides))
 
     with jax.named_scope("own"):
         own = own_attend(
@@ -669,7 +668,7 @@
         )
 
     with jax.named_scope("temporal"):
-        sent, *_ = lax.optimization_barrier((parts, own))
+        sent, *_ = lax.optimization_barrier((parts, own, beside))
         sent = swap(sent.reshape((quarters * G,) + parts.shape[2:]), frame)
 
     with jax.named_scope("store"):
@@ -683,17 +682,14 @@
         blocks = [in_hbm(block) for block in blocks]
 
     with jax.named_scope("queries"):
-        named = asked[:, patches, :TOPM].astype(jnp.int32)
+        named = jnp.concatenate([group[:, patches, :TOPM] for group in (beside, here)], axis=0)
+        named = named.astype(jnp.int32)
         y = (named // (cores * held) - lax.axis_index("y")) & (rings - 1)
         c = (named // held & (cores - 1)) ^ lax.axis_index("c")
         index = (c * rings + y) * held + (named & (held - 1))
 
-    def attend(base, after):
-        return memory_attend(base, index, asked, asked.shape[0] // sides, blocks, after)
-
     with jax.named_scope("memory"):
-        count = asked.shape[0] // sides
-        sum_beside = attend((sides - 1 - side) * count, own)
+        sum_beside = memory_attend(0, index, beside, blocks, own)
         from_beside = lax.ppermute(sum_beside, "zq", other(sides))
 
     with jax.named_scope("temporal"):
@@ -701,7 +697,7 @@
         time = swap(timed, frame)
 
     with jax.named_scope("memory"):
-        sum_here = attend(side * count, timed)
+        sum_here = memory_attend(beside.shape[0], index, here, blocks, timed)
         memory = swap_apart(add_partials(x, [in_hbm(sum_here), from_beside]))
 
     with jax.named_scope("exit"):

time: 137 us -> 133 us (0.971)
  waiting for transfers between devices: 40.5 us -> 30 us
  starting transfers between devices: 40.1 us -> 44.1 us
  local copies, waits for them, and re-layouts: 2.03 us -> 4.41 us
    all_to_all x4, waiting for transfers between devices: 10.7 us -> 4.9 us  [swap(): return lax.all_to_all(blocks, axes, split_axis=0, concat_axis=0, tiled=True)]
    ppermute x0 -> x1, starting transfers between devices: none -> 3.58 us  [on_device(): beside = lax.ppermute(here, 'zq', other(sides))]
    ppermute x1, waiting for transfers between devices: 2.41 us -> 0.01 us  [on_device(): second = lax.ppermute(joined, 'zp', other(sides))]
    unnamed x11 -> x27, local copies, waits for them, and re-layouts: 2.03 us -> 3.7 us
  transfers between devices with their start and end apart: 23 -> 24, of which waited for: 11 -> 10; matrix products, arithmetic and copies ran while one was open for 0% -> 1% of each run, Pallas kernels for 32% -> 33%
where the time goes in v15:
time: 133 us; the launch traced here: 132 us
  Pallas kernels  52.4 us (39%)
  starting transfers between devices  44.1 us (33%)
  waiting for transfers between devices  30 us (23%)
  local copies, waits for them, and re-layouts  4.41 us (3%)
    all_to_all x4, starting transfers between devices, swap(): return lax.all_to_all(blocks, axes, split_axis=0, concat_axis=0, tiled=True)  18.5 us
    pallas_call x2, Pallas kernels, memory_attend(): pl.pallas_call(functools.partial(memory_attend_kernel, count, first), in_...  16.5 us
    ppermute x1, waiting for transfers between devices, on_device(): far = lax.ppermute(below, 'y', turn(1))  12.8 us
    pallas_call x1, Pallas kernels, temporal_entry(): pl.pallas_call(functools.partial(temporal_entry_kernel, quarters), in_spe...  8.54 us
    pallas_call x1, Pallas kernels, own_attend(): pl.pallas_call(own_attend_kernel, in_specs=[HBM, HBM, HBM] + [ANY] * len(...  8.08 us
    ppermute x3, starting transfers between devices, swap_apart(): lax.ppermute(blocks[j], 'x', turn(j))  6.59 us
    pallas_call x1, Pallas kernels, leave(): pl.pallas_call(leave_kernel, in_specs=[SCALARS, HBM] + [ANY] * (G + 1) +...  6.11 us
    pallas_call x1, Pallas kernels, modulate(): pl.pallas_call(functools.partial(modulate_kernel, held), in_specs=[HBM, H...  5.57 us
  transfers between devices with their start and end apart: 24, of which 10 were waited for; matrix products, arithmetic and copies ran while one was open for 1% of the time, Pallas kernels for 33%

profile of v15, /device:TPU:0, one launch (start us, length us, event | category | flops | bytes accessed | tf_op | source)
XLA Modules:
  0.0 132.0 jit_solution(15414018242314068903)
XLA Ops:
  0.0 1.2 copy.12
  1.2 1.0 split_store.1._
  2.2 4.4 %all-to-all-start = ((bf16[4,288,256]{2,1,0:T(8,128)(2,1)}), bf16[4,288,256]{2,1,0:T(8,128)(2,1)S(1)}, u32[]{:S(2)}, u32[]{:S(2)}) async-start(bf16[4,288,256]{2,1,0:T(8,128)(2,1)} %bitcast.22), calls=%async_computation | async-start | bytes 1179648 | tf_op jit(solution)/shard_map/store/all_to_all | solution.py:624
  6.6 5.6 %modulate.1 = (bf16[576,2048]{1,0:T(8,128)(2,1)}, bf16[1,4,592,128]{3,2,1,0:T(8,128)(2,1)}) custom-call(bf16[576,2048]{1,0:T(8,128)(2,1)} %bitcast.23, f32[2,2048]{1,0:T(2,128)} %bitcast.25, bf16[2048,3072]{1,0:T(8,128)(2,1)} %weight_hbm.6, f32[2,4]{1,0:T(2,128)S(1)} %copy-done.3, s32[6]{0:T(128)S(1)} %bitcast.19, s32[6]{0:T(128)S(1)} %bitcast.20, ...), custom_call_target="tpu_custom_call" | custom-call | flops 75497472 | bytes 462848 | tf_op jit(solution)/shard_map/queries/modulate/pallas_call | solution.py:185
  12.2 4.6 %all-to-all-done.in_hbm = bf16[4,288,256]{2,1,0:T(8,128)(2,1)S(1)} async-done(((bf16[4,288,256]{2,1,0:T(8,128)(2,1)}), bf16[4,288,256]{2,1,0:T(8,128)(2,1)S(1)}, u32[]{:S(2)}, u32[]{:S(2)}) %all-to-all-start) | async-done | bytes 589856 | tf_op jit(solution)/shard_map/store/all_to_all | solution.py:624
  16.8 1.7 %join_pieces.1.refs_0_ = bf16[8,144,256]{2,1,0:T(8,128)(2,1)} custom-call(bf16[4,288,256]{2,1,0:T(8,128)(2,1)S(1)} %all-to-all-done.in_hbm, bf16[576,2048]{1,0:T(8,128)(2,1)} %get-tuple-element.16._.hidden_hbm), custom_call_target="tpu_custom_call" | custom-call | flops 18432 | bytes 73728 | tf_op jit(solution)/shard_map/store/join_pieces/pallas_call | solution.py:109
  18.5 2.0 %collective-permute-start.1 = (bf16[8,144,256]{2,1,0:T(8,128)(2,1)}, bf16[8,144,256]{2,1,0:T(8,128)(2,1)}, u32[]{:S(2)}, u32[]{:S(2)}) collective-permute-start(bf16[8,144,256]{2,1,0:T(8,128)(2,1)} %join_pieces.1.refs_0_), channel_id=1, source_target_pairs={{0,4},{4,0},{1,5},{5,1},{2,6},{6,2},{3,7},{7,3},{8,12},{12,8},{9,1... | collective-permute-start | bytes 1769480 | tf_op jit(solution)/shard_map/store/ppermute | solution.py:651
  20.5 3.0 %collective-permute-start = (bf16[8,144,256]{2,1,0:T(8,128)(2,1)}, bf16[8,144,256]{2,1,0:T(8,128)(2,1)S(1)}, u32[]{:S(2)}, u32[]{:S(2)}) collective-permute-start(bf16[8,144,256]{2,1,0:T(8,128)(2,1)} %join_pieces.1.refs_0_), channel_id=1, source_target_pairs={{0,96},{32,0},{64,32},{96,64},{1,97},{33,1},{65,33},{97,65},{2,98}... | collective-permute-start | bytes 1769480 | tf_op jit(solution)/shard_map/store/ppermute | solution.py:649
  23.5 0.0 collective-permute-start.2
  23.5 3.5 %all-to-all-start.1 = ((bf16[4,592,128]{2,1,0:T(8,128)(2,1)}), bf16[4,592,128]{2,1,0:T(8,128)(2,1)S(1)}, u32[]{:S(2)}, u32[]{:S(2)}) async-start(bf16[4,592,128]{2,1,0:T(8,128)(2,1)} %bitcast.6), calls=%async_computation.1 | async-start | bytes 1212416 | tf_op jit(solution)/shard_map/queries/all_to_all | solution.py:624
  27.0 8.5 %temporal_entry.1.refs_0_ = bf16[4,4,3,144,128]{4,3,2,1,0:T(8,128)(2,1)} custom-call(bf16[576,2048]{1,0:T(8,128)(2,1)} %get-tuple-element.16._.hidden_hbm, bf16[2048,3072]{1,0:T(8,128)(2,1)} %weight_hbm.6, f32[2,4]{1,0:T(2,128)S(1)} %copy-done.3, bf16[8,144,256]{2,1,0:T(8,128)(2,1)} %join_pieces.1.refs_0_), custom_call_target="tpu_custom_call" | custom-call | flops 226492416 | bytes 651264 | tf_op jit(solution)/shard_map/temporal/temporal_entry/pallas_call | solution.py:250
  35.6 0.3 all-to-all-done.1.query_hbm
  35.9 0.0 collective-permute-done.1.refs_1_
  35.9 0.0 collective-permute-done.refs_1_.refs_2_
  35.9 2.4 %collective-permute-done.2.refs_6_ = bf16[8,144,256]{2,1,0:T(8,128)(2,1)S(1)} collective-permute-done((bf16[8,144,256]{2,1,0:T(8,128)(2,1)}, bf16[8,144,256]{2,1,0:T(8,128)(2,1)S(1)}, u32[]{:S(2)}, u32[]{:S(2)}) %collective-permute-start.2) | collective-permute-done | bytes 589856 | tf_op jit(solution)/shard_map/store/ppermute | solution.py:650
  38.3 3.6 %collective-permute-start.3 = (bf16[4,592,128]{2,1,0:T(8,128)(2,1)S(1)}, bf16[4,592,128]{2,1,0:T(8,128)(2,1)S(1)}, u32[]{:S(2)}, u32[]{:S(2)}) collective-permute-start(bf16[4,592,128]{2,1,0:T(8,128)(2,1)S(1)} %all-to-all-done.1.query_hbm), channel_id=1, source_target_pairs={{0,8},{8,0},{1,9},{9,1},{2,10},{10,2},{3,11},{11,3},{4,12},{12,4},... | collective-permute-start | bytes 1818632 | tf_op jit(solution)/shard_map/queries/ppermute | solution.py:663
  41.8 0.7 collective-permute-start.4
  42.5 1.4 %collective-permute-start.5 = (bf16[8,144,256]{2,1,0:T(8,128)(2,1)}, bf16[8,144,256]{2,1,0:T(8,128)(2,1)}, u32[]{:S(2)}, u32[]{:S(2)}) collective-permute-start(bf16[8,144,256]{2,1,0:T(8,128)(2,1)} %collective-permute-done.1.refs_1_), channel_id=1, source_target_pairs={{0,32},{32,64},{64,96},{96,0},{1,33},{33,65},{65,97},{97,1},{2,34}... | collective-permute-start | bytes 1769480 | tf_op jit(solution)/shard_map/store/ppermute | solution.py:654
  43.9 8.1 %own_attend.1.refs_16_.own_hbm = bf16[4,592,128]{2,1,0:T(8,128)(2,1)} custom-call(bf16[576,2048]{1,0:T(8,128)(2,1)} %get-tuple-element.16._.hidden_hbm, bf16[2048,3072]{1,0:T(8,128)(2,1)} %weight_hbm.6, bf16[1,4,592,128]{3,2,1,0:T(8,128)(2,1)} %get-tuple-element.17.query_hbm, bf16[4,4,3,144,128]{4,3,2,1,0:T(8,128)(2,1)} %temporal_entry.1.refs_0_, ...), custom_call_target="tpu_custom_call" | custom-call | flops 214695936 | bytes 593920 | tf_op jit(solution)/shard_map/own/own_attend/pallas_call | solution.py:380
  52.0 0.9 collective-permute-done.3.query_hbm
  52.8 0.8 copy-done.1
  53.7 5.6 %all-to-all-start.2 = ((bf16[16,3,144,128]{3,2,1,0:T(8,128)(2,1)}), bf16[16,3,144,128]{3,2,1,0:T(8,128)(2,1)S(1)}, u32[]{:S(2)}, u32[]{:S(2)}) async-start(bf16[16,3,144,128]{3,2,1,0:T(8,128)(2,1)} %bitcast.21), calls=%async_computation.2 | async-start | bytes 3538944 | tf_op jit(solution)/shard_map/temporal/all_to_all | solution.py:624
  59.3 0.1 collective-permute-start.8
  59.4 0.5 collective-permute-start.9
  59.9 0.1 collective-permute-start.10
  60.0 0.0 collective-permute-done.4.refs_3_
  60.0 0.0 collective-permute-done.5.refs_7_
  60.0 0.3 collective-permute-start.6
  60.3 2.9 %collective-permute-start.7 = (bf16[8,144,256]{2,1,0:T(8,128)(2,1)}, bf16[8,144,256]{2,1,0:T(8,128)(2,1)}, u32[]{:S(2)}, u32[]{:S(2)}) collective-permute-start(bf16[8,144,256]{2,1,0:T(8,128)(2,1)} %collective-permute-done.4.refs_3_), channel_id=1, source_target_pairs={{0,96},{32,0},{64,32},{96,64},{1,97},{33,1},{65,33},{97,65},{2,98}... | collective-permute-start | bytes 1769480 | tf_op jit(solution)/shard_map/store/ppermute | solution.py:679
  63.3 0.0 collective-permute-done.8.refs_8_
  63.3 0.0 collective-permute-start.11
  63.3 0.0 collective-permute-done.9.refs_9_
  63.3 0.5 collective-permute-start.14
  63.8 0.0 collective-permute-done.10.refs_10_
  63.8 0.3 copy-done.8
  64.1 0.0 collective-permute-start.15
  64.1 0.3 copy-done.9
  64.4 12.8 %collective-permute-done.6.refs_4_ = bf16[8,144,256]{2,1,0:T(8,128)(2,1)} collective-permute-done((bf16[8,144,256]{2,1,0:T(8,128)(2,1)}, bf16[8,144,256]{2,1,0:T(8,128)(2,1)}, u32[]{:S(2)}, u32[]{:S(2)}) %collective-permute-start.6) | collective-permute-done | bytes 589856 | tf_op jit(solution)/shard_map/store/ppermute | solution.py:678
  77.2 0.0 collective-permute-start.12
  77.2 0.0 collective-permute-done.7.refs_5_
  77.2 0.5 collective-permute-start.13
  77.7 0.7 slice.8
  78.5 0.0 collective-permute-done.11.refs_11_
  78.5 0.0 collective-permute-done.14.refs_14_
  78.5 0.0 collective-permute-done.15.refs_15_
  78.5 1.0 collective-permute-done.12.refs_12_
  79.6 0.8 collective-permute-done.13.refs_13_
  80.4 1.1 copy-done.2
  81.5 8.3 %memory_attend.2._ = bf16[4,592,128]{2,1,0:T(8,128)(2,1)} custom-call(s32[8,6]{1,0:T(8,128)S(1)} %fusion.10.index_ref, bf16[4,592,128]{2,1,0:T(8,128)(2,1)S(1)} %copy-done.2, bf16[8,144,256]{2,1,0:T(8,128)(2,1)} %join_pieces.1.refs_0_, bf16[8,144,256]{2,1,0:T(8,128)(2,1)} %collective-permute-done.1.refs_1_, bf16[8,144,256]{2,1,0:T(8,128)(2,1)} %copy-done, ...), custom_call_target="tpu_custom_call" | custom-call | flops 261881856 | bytes 186368 | tf_op jit(solution)/shard_map/memory/memory_attend/pallas_call | solution.py:448
  89.7 3.5 %collective-permute-start.16 = (bf16[4,592,128]{2,1,0:T(8,128)(2,1)}, bf16[4,592,128]{2,1,0:T(8,128)(2,1)S(1)}, u32[]{:S(2)}, u32[]{:S(2)}) collective-permute-start(bf16[4,592,128]{2,1,0:T(8,128)(2,1)} %memory_attend.2._), channel_id=1, source_target_pairs={{0,8},{8,0},{1,9},{9,1},{2,10},{10,2},{3,11},{11,3},{4,12},{12,4},... | collective-permute-start | bytes 1818632 | tf_op jit(solution)/shard_map/memory/ppermute | solution.py:693
  93.9 0.0 all-to-all-done.2.in_hbm_ref
  93.9 2.5 %temporal_attend.1.refs_16_ = bf16[16,144,128]{2,1,0:T(8,128)(2,1)} custom-call(s32[1]{0:T(128)S(6)} %copy.17.length_ref, bf16[16,3,144,128]{3,2,1,0:T(8,128)(2,1)S(1)} %all-to-all-done.2.in_hbm_ref, bf16[4,592,128]{2,1,0:T(8,128)(2,1)} %memory_attend.2._), custom_call_target="tpu_custom_call" | custom-call | flops 18874368 | bytes 147456 | tf_op jit(solution)/shard_map/temporal/temporal_attend/pallas_call | solution.py:300
  96.4 5.0 %all-to-all-start.3 = ((bf16[16,144,128]{2,1,0:T(8,128)(2,1)}), bf16[16,144,128]{2,1,0:T(8,128)(2,1)S(1)}, u32[]{:S(2)}, u32[]{:S(2)}) async-start(bf16[16,144,128]{2,1,0:T(8,128)(2,1)} %temporal_attend.1.refs_16_), calls=%async_computation.3 | async-start | bytes 1179648 | tf_op jit(solution)/shard_map/temporal/all_to_all | solution.py:624
  101.4 8.3 %memory_attend.3.refs_0_ = bf16[4,592,128]{2,1,0:T(8,128)(2,1)} custom-call(s32[8,6]{1,0:T(8,128)S(1)} %fusion.10.index_ref, bf16[4,592,128]{2,1,0:T(8,128)(2,1)S(1)} %all-to-all-done.1.query_hbm, bf16[8,144,256]{2,1,0:T(8,128)(2,1)} %join_pieces.1.refs_0_, bf16[8,144,256]{2,1,0:T(8,128)(2,1)} %collective-permute-done.1.refs_1_, ...), custom_call_target="tpu_custom_call" | custom-call | flops 261881856 | bytes 186368 | tf_op jit(solution)/shard_map/memory/memory_attend/pallas_call | solution.py:448
  109.7 2.8 %collective-permute-done.16.refs_1_ = bf16[4,592,128]{2,1,0:T(8,128)(2,1)S(1)} collective-permute-done((bf16[4,592,128]{2,1,0:T(8,128)(2,1)}, bf16[4,592,128]{2,1,0:T(8,128)(2,1)S(1)}, u32[]{:S(2)}, u32[]{:S(2)}) %collective-permute-start.16) | collective-permute-done | bytes 606240 | tf_op jit(solution)/shard_map/memory/ppermute | solution.py:693
  112.4 2.3 %add_partials.1 = (bf16[592,128]{1,0:T(8,128)(2,1)}, bf16[592,128]{1,0:T(8,128)(2,1)}, bf16[592,128]{1,0:T(8,128)(2,1)}, bf16[592,128]{1,0:T(8,128)(2,1)}) custom-call(s32[1]{0:T(128)} %bitcast.x_ref, bf16[4,592,128]{2,1,0:T(8,128)(2,1)} %memory_attend.3.refs_0_, bf16[4,592,128]{2,1,0:T(8,128)(2,1)S(1)} %collective-permute-done.16.refs_1_), custom_call_target="tpu_custom_call" | custom-call | flops 75776 | bytes 151552 | tf_op jit(solution)/shard_map/memory/add_partials/pallas_call | solution.py:500
  114.8 2.4 %collective-permute-start.17 = (bf16[592,128]{1,0:T(8,128)(2,1)}, bf16[592,128]{1,0:T(8,128)(2,1)S(1)}, u32[]{:S(2)}, u32[]{:S(2)}) collective-permute-start(bf16[592,128]{1,0:T(8,128)(2,1)} %get-tuple-element.24), channel_id=1, source_target_pairs={{0,1},{1,2},{2,3},{3,0},{4,5},{5,6},{6,7},{7,4},{8,9},{9,10},{10,1... | collective-permute-start | bytes 454664 | tf_op jit(solution)/shard_map/memory/ppermute | solution.py:627
  117.2 2.7 %collective-permute-start.18 = (bf16[592,128]{1,0:T(8,128)(2,1)}, bf16[592,128]{1,0:T(8,128)(2,1)S(1)}, u32[]{:S(2)}, u32[]{:S(2)}) collective-permute-start(bf16[592,128]{1,0:T(8,128)(2,1)} %get-tuple-element.25), channel_id=1, source_target_pairs={{0,2},{1,3},{2,0},{3,1},{4,6},{5,7},{6,4},{7,5},{8,10},{9,11},{10,... | collective-permute-start | bytes 454664 | tf_op jit(solution)/shard_map/memory/ppermute | solution.py:627
  119.9 1.5 %collective-permute-start.19 = (bf16[592,128]{1,0:T(8,128)(2,1)}, bf16[592,128]{1,0:T(8,128)(2,1)S(1)}, u32[]{:S(2)}, u32[]{:S(2)}) collective-permute-start(bf16[592,128]{1,0:T(8,128)(2,1)} %get-tuple-element.26), channel_id=1, source_target_pairs={{0,3},{1,0},{2,1},{3,2},{4,7},{5,4},{6,5},{7,6},{8,11},{9,8},{10,9... | collective-permute-start | bytes 454664 | tf_op jit(solution)/shard_map/memory/ppermute | solution.py:627
  121.4 2.1 %collective-permute-done.17.memory_1 = bf16[592,128]{1,0:T(8,128)(2,1)S(1)} collective-permute-done((bf16[592,128]{1,0:T(8,128)(2,1)}, bf16[592,128]{1,0:T(8,128)(2,1)S(1)}, u32[]{:S(2)}, u32[]{:S(2)}) %collective-permute-start.17) | collective-permute-done | bytes 151584 | tf_op jit(solution)/shard_map/memory/ppermute | solution.py:627
  123.4 2.2 %collective-permute-done.18.memory_2 = bf16[592,128]{1,0:T(8,128)(2,1)S(1)} collective-permute-done((bf16[592,128]{1,0:T(8,128)(2,1)}, bf16[592,128]{1,0:T(8,128)(2,1)S(1)}, u32[]{:S(2)}, u32[]{:S(2)}) %collective-permute-start.18) | collective-permute-done | bytes 151584 | tf_op jit(solution)/shard_map/memory/ppermute | solution.py:627
  125.7 0.0 collective-permute-done.19.memory_3
  125.7 0.0 all-to-all-done.3.time_hbm
  125.7 6.1 %leave.1 = bf16[576,2048]{1,0:T(8,128)(2,1)} custom-call(s32[1]{0:T(128)} %bitcast.x_ref, bf16[4,592,128]{2,1,0:T(8,128)(2,1)} %own_attend.1.refs_16_.own_hbm, bf16[592,128]{1,0:T(8,128)(2,1)} %get-tuple-element.23.memory_0, bf16[592,128]{1,0:T(8,128)(2,1)S(1)} %collective-permute-done.17.memory_1, bf16[592,128]{1,0:T(8,128)(2,1)S(1)} %collective-permute-done.18.memory_2, ...), custom_call_target="tpu_custom_call" | custom-call | flops 150994944 | bytes 630784 | tf_op jit(solution)/shard_map/exit/leave/pallas_call | solution.py:571
  (24 shorter events, 0.1 us)
Async XLA Ops:
  0.0 6.6 %copy-start.4 = (s32[1,1,6,1]{2,3,1,0:T(1,128)S(1)}, s32[1,1,6,1]{2,3,1,0:T(1,128)}, u32[]{:S(2)}) copy-start(s32[1,1,6,1]{2,3,1,0:T(1,128)} %param.15) | copy-start | bytes 76
  0.0 6.6 %copy-start.5 = (s32[1,1,6]{2,1,0:T(1,128)S(1)}, s32[1,1,6]{2,1,0:T(1,128)}, u32[]{:S(2)}) copy-start(s32[1,1,6]{2,1,0:T(1,128)} %param.16) | copy-start | bytes 76
  0.0 6.6 %copy-start.3 = (f32[2,4]{1,0:T(2,128)S(1)}, f32[2,4]{1,0:T(2,128)}, u32[]{:S(2)}) copy-start(f32[2,4]{1,0:T(2,128)} %sharpness_ref.3) | copy-start | bytes 100
  2.2 14.6 %all-to-all-start = ((bf16[4,288,256]{2,1,0:T(8,128)(2,1)}), bf16[4,288,256]{2,1,0:T(8,128)(2,1)S(1)}, u32[]{:S(2)}, u32[]{:S(2)}) async-start(bf16[4,288,256]{2,1,0:T(8,128)(2,1)} %bitcast.22), calls=%async_computation | async-start | bytes 1179648 | tf_op jit(solution)/shard_map/store/all_to_all | solution.py:624
  18.5 17.4 %collective-permute-start.1 = (bf16[8,144,256]{2,1,0:T(8,128)(2,1)}, bf16[8,144,256]{2,1,0:T(8,128)(2,1)}, u32[]{:S(2)}, u32[]{:S(2)}) collective-permute-start(bf16[8,144,256]{2,1,0:T(8,128)(2,1)} %join_pieces.1.refs_0_), channel_id=1, source_target_pairs={{0,4},{4,0},{1,5},{5,1},{2,6},{6,2},{3,7},{7,3},{8,12},{12,8},{9,1... | collective-permute-start | bytes 1769480 | tf_op jit(solution)/shard_map/store/ppermute | solution.py:651
  20.5 15.4 %collective-permute-start = (bf16[8,144,256]{2,1,0:T(8,128)(2,1)}, bf16[8,144,256]{2,1,0:T(8,128)(2,1)S(1)}, u32[]{:S(2)}, u32[]{:S(2)}) collective-permute-start(bf16[8,144,256]{2,1,0:T(8,128)(2,1)} %join_pieces.1.refs_0_), channel_id=1, source_target_pairs={{0,96},{32,0},{64,32},{96,64},{1,97},{33,1},{65,33},{97,65},{2,98}... | collective-permute-start | bytes 1769480 | tf_op jit(solution)/shard_map/store/ppermute | solution.py:649
  23.5 14.7 %collective-permute-start.2 = (bf16[8,144,256]{2,1,0:T(8,128)(2,1)}, bf16[8,144,256]{2,1,0:T(8,128)(2,1)S(1)}, u32[]{:S(2)}, u32[]{:S(2)}) collective-permute-start(bf16[8,144,256]{2,1,0:T(8,128)(2,1)} %join_pieces.1.refs_0_), channel_id=1, source_target_pairs={{0,32},{32,64},{64,96},{96,0},{1,33},{33,65},{65,97},{97,1},{2,34}... | collective-permute-start | bytes 1769480 | tf_op jit(solution)/shard_map/store/ppermute | solution.py:650
  23.5 12.3 %all-to-all-start.1 = ((bf16[4,592,128]{2,1,0:T(8,128)(2,1)}), bf16[4,592,128]{2,1,0:T(8,128)(2,1)S(1)}, u32[]{:S(2)}, u32[]{:S(2)}) async-start(bf16[4,592,128]{2,1,0:T(8,128)(2,1)} %bitcast.6), calls=%async_computation.1 | async-start | bytes 1212416 | tf_op jit(solution)/shard_map/queries/all_to_all | solution.py:624
  35.9 24.0 %copy-start = (bf16[8,144,256]{2,1,0:T(8,128)(2,1)}, bf16[8,144,256]{2,1,0:T(8,128)(2,1)S(1)}, u32[]{:S(2)}) copy-start(bf16[8,144,256]{2,1,0:T(8,128)(2,1)S(1)} %collective-permute-done.refs_1_.refs_2_) | copy-start | bytes 1769476
  38.3 13.7 %copy-start.7 = (bf16[8,144,256]{2,1,0:T(8,128)(2,1)}, bf16[8,144,256]{2,1,0:T(8,128)(2,1)S(1)}, u32[]{:S(2)}) copy-start(bf16[8,144,256]{2,1,0:T(8,128)(2,1)S(1)} %collective-permute-done.2.refs_6_) | copy-start | bytes 1769476
  38.3 14.6 %collective-permute-start.3 = (bf16[4,592,128]{2,1,0:T(8,128)(2,1)S(1)}, bf16[4,592,128]{2,1,0:T(8,128)(2,1)S(1)}, u32[]{:S(2)}, u32[]{:S(2)}) collective-permute-start(bf16[4,592,128]{2,1,0:T(8,128)(2,1)S(1)} %all-to-all-done.1.query_hbm), channel_id=1, source_target_pairs={{0,8},{8,0},{1,9},{9,1},{2,10},{10,2},{3,11},{11,3},{4,12},{12,4},... | collective-permute-start | bytes 1818632 | tf_op jit(solution)/shard_map/queries/ppermute | solution.py:663
  41.8 18.2 %collective-permute-start.4 = (bf16[8,144,256]{2,1,0:T(8,128)(2,1)}, bf16[8,144,256]{2,1,0:T(8,128)(2,1)}, u32[]{:S(2)}, u32[]{:S(2)}) collective-permute-start(bf16[8,144,256]{2,1,0:T(8,128)(2,1)} %collective-permute-done.1.refs_1_), channel_id=1, source_target_pairs={{0,96},{32,0},{64,32},{96,64},{1,97},{33,1},{65,33},{97,65},{2,98}... | collective-permute-start | bytes 1769480 | tf_op jit(solution)/shard_map/store/ppermute | solution.py:653
  42.5 17.5 %collective-permute-start.5 = (bf16[8,144,256]{2,1,0:T(8,128)(2,1)}, bf16[8,144,256]{2,1,0:T(8,128)(2,1)}, u32[]{:S(2)}, u32[]{:S(2)}) collective-permute-start(bf16[8,144,256]{2,1,0:T(8,128)(2,1)} %collective-permute-done.1.refs_1_), channel_id=1, source_target_pairs={{0,32},{32,64},{64,96},{96,0},{1,33},{33,65},{65,97},{97,1},{2,34}... | collective-permute-start | bytes 1769480 | tf_op jit(solution)/shard_map/store/ppermute | solution.py:654
  52.0 7.3 %copy-start.6 = (bf16[8,144,256]{2,1,0:T(8,128)(2,1)S(1)}, bf16[8,144,256]{2,1,0:T(8,128)(2,1)}, u32[]{:S(2)}) copy-start(bf16[8,144,256]{2,1,0:T(8,128)(2,1)} %join_pieces.1.refs_0_) | copy-start | bytes 1769476
  52.8 0.8 copy-start.1
  53.7 40.2 %all-to-all-start.2 = ((bf16[16,3,144,128]{3,2,1,0:T(8,128)(2,1)}), bf16[16,3,144,128]{3,2,1,0:T(8,128)(2,1)S(1)}, u32[]{:S(2)}, u32[]{:S(2)}) async-start(bf16[16,3,144,128]{3,2,1,0:T(8,128)(2,1)} %bitcast.21), calls=%async_computation.2 | async-start | bytes 3538944 | tf_op jit(solution)/shard_map/temporal/all_to_all | solution.py:624
  59.3 3.9 %collective-permute-start.8 = (bf16[8,144,256]{2,1,0:T(8,128)(2,1)S(1)}, bf16[8,144,256]{2,1,0:T(8,128)(2,1)S(1)}, u32[]{:S(2)}, u32[]{:S(2)}) collective-permute-start(bf16[8,144,256]{2,1,0:T(8,128)(2,1)S(1)} %copy-done.6), channel_id=1, source_target_pairs={{0,16},{16,0},{1,17},{17,1},{2,18},{18,2},{3,19},{19,3},{4,20},{20... | collective-permute-start | bytes 1769480 | tf_op jit(solution)/shard_map/store/ppermute | solution.py:681
  59.4 3.9 %collective-permute-start.9 = (bf16[8,144,256]{2,1,0:T(8,128)(2,1)}, bf16[8,144,256]{2,1,0:T(8,128)(2,1)S(1)}, u32[]{:S(2)}, u32[]{:S(2)}) collective-permute-start(bf16[8,144,256]{2,1,0:T(8,128)(2,1)} %collective-permute-done.1.refs_1_), channel_id=1, source_target_pairs={{0,16},{16,0},{1,17},{17,1},{2,18},{18,2},{3,19},{19,3},{4,20},{20... | collective-permute-start | bytes 1769480 | tf_op jit(solution)/shard_map/store/ppermute | solution.py:681
  59.9 3.9 %collective-permute-start.10 = (bf16[8,144,256]{2,1,0:T(8,128)(2,1)S(1)}, bf16[8,144,256]{2,1,0:T(8,128)(2,1)S(1)}, u32[]{:S(2)}, u32[]{:S(2)}) collective-permute-start(bf16[8,144,256]{2,1,0:T(8,128)(2,1)S(1)} %collective-permute-done.refs_1_.refs_2_), channel_id=1, source_target_pairs={{0,16},{16,0},{1,17},{17,1},{2,18},{18,2},{3,19},{19,3},{4,20},{20... | collective-permute-start | bytes 1769480 | tf_op jit(solution)/shard_map/store/ppermute | solution.py:681
  60.0 17.2 %collective-permute-start.6 = (bf16[8,144,256]{2,1,0:T(8,128)(2,1)}, bf16[8,144,256]{2,1,0:T(8,128)(2,1)}, u32[]{:S(2)}, u32[]{:S(2)}) collective-permute-start(bf16[8,144,256]{2,1,0:T(8,128)(2,1)} %copy-done.7), channel_id=1, source_target_pairs={{0,32},{32,64},{64,96},{96,0},{1,33},{33,65},{65,97},{97,1},{2,34}... | collective-permute-start | bytes 1769480 | tf_op jit(solution)/shard_map/store/ppermute | solution.py:678
  60.3 16.9 %collective-permute-start.7 = (bf16[8,144,256]{2,1,0:T(8,128)(2,1)}, bf16[8,144,256]{2,1,0:T(8,128)(2,1)}, u32[]{:S(2)}, u32[]{:S(2)}) collective-permute-start(bf16[8,144,256]{2,1,0:T(8,128)(2,1)} %collective-permute-done.4.refs_3_), channel_id=1, source_target_pairs={{0,96},{32,0},{64,32},{96,64},{1,97},{33,1},{65,33},{97,65},{2,98}... | collective-permute-start | bytes 1769480 | tf_op jit(solution)/shard_map/store/ppermute | solution.py:679
  63.3 0.8 copy-start.8
  63.3 15.2 %collective-permute-start.11 = (bf16[8,144,256]{2,1,0:T(8,128)(2,1)}, bf16[8,144,256]{2,1,0:T(8,128)(2,1)S(1)}, u32[]{:S(2)}, u32[]{:S(2)}) collective-permute-start(bf16[8,144,256]{2,1,0:T(8,128)(2,1)} %collective-permute-done.4.refs_3_), channel_id=1, source_target_pairs={{0,16},{16,0},{1,17},{17,1},{2,18},{18,2},{3,19},{19,3},{4,20},{20... | collective-permute-start | bytes 1769480 | tf_op jit(solution)/shard_map/store/ppermute | solution.py:681
  63.3 1.1 copy-start.9
  63.3 15.2 %collective-permute-start.14 = (bf16[8,144,256]{2,1,0:T(8,128)(2,1)}, bf16[8,144,256]{2,1,0:T(8,128)(2,1)}, u32[]{:S(2)}, u32[]{:S(2)}) collective-permute-start(bf16[8,144,256]{2,1,0:T(8,128)(2,1)} %copy-done.7), channel_id=1, source_target_pairs={{0,16},{16,0},{1,17},{17,1},{2,18},{18,2},{3,19},{19,3},{4,20},{20... | collective-permute-start | bytes 1769480 | tf_op jit(solution)/shard_map/store/ppermute | solution.py:681
  64.1 13.1 %copy-start.10 = (bf16[8,144,256]{2,1,0:T(8,128)(2,1)}, bf16[8,144,256]{2,1,0:T(8,128)(2,1)S(1)}, u32[]{:S(2)}) copy-start(bf16[8,144,256]{2,1,0:T(8,128)(2,1)S(1)} %collective-permute-done.10.refs_10_) | copy-start | bytes 1769476
  64.1 14.4 %collective-permute-start.15 = (bf16[8,144,256]{2,1,0:T(8,128)(2,1)}, bf16[8,144,256]{2,1,0:T(8,128)(2,1)}, u32[]{:S(2)}, u32[]{:S(2)}) collective-permute-start(bf16[8,144,256]{2,1,0:T(8,128)(2,1)} %collective-permute-done.5.refs_7_), channel_id=1, source_target_pairs={{0,16},{16,0},{1,17},{17,1},{2,18},{18,2},{3,19},{19,3},{4,20},{20... | collective-permute-start | bytes 1769480 | tf_op jit(solution)/shard_map/store/ppermute | solution.py:681
  77.2 2.3 %collective-permute-start.12 = (bf16[8,144,256]{2,1,0:T(8,128)(2,1)}, bf16[8,144,256]{2,1,0:T(8,128)(2,1)}, u32[]{:S(2)}, u32[]{:S(2)}) collective-permute-start(bf16[8,144,256]{2,1,0:T(8,128)(2,1)} %collective-permute-done.6.refs_4_), channel_id=1, source_target_pairs={{0,16},{16,0},{1,17},{17,1},{2,18},{18,2},{3,19},{19,3},{4,20},{20... | collective-permute-start | bytes 1769480 | tf_op jit(solution)/shard_map/store/ppermute | solution.py:681
  77.2 3.2 %collective-permute-start.13 = (bf16[8,144,256]{2,1,0:T(8,128)(2,1)}, bf16[8,144,256]{2,1,0:T(8,128)(2,1)}, u32[]{:S(2)}, u32[]{:S(2)}) collective-permute-start(bf16[8,144,256]{2,1,0:T(8,128)(2,1)} %collective-permute-done.7.refs_5_), channel_id=1, source_target_pairs={{0,16},{16,0},{1,17},{17,1},{2,18},{18,2},{3,19},{19,3},{4,20},{20... | collective-permute-start | bytes 1769480 | tf_op jit(solution)/shard_map/store/ppermute | solution.py:681
  78.5 1.9 %copy-start.11 = (bf16[8,144,256]{2,1,0:T(8,128)(2,1)}, bf16[8,144,256]{2,1,0:T(8,128)(2,1)S(1)}, u32[]{:S(2)}) copy-start(bf16[8,144,256]{2,1,0:T(8,128)(2,1)S(1)} %collective-permute-done.11.refs_11_) | copy-start | bytes 1769476
  80.4 1.1 copy-start.2
  89.7 22.7 %collective-permute-start.16 = (bf16[4,592,128]{2,1,0:T(8,128)(2,1)}, bf16[4,592,128]{2,1,0:T(8,128)(2,1)S(1)}, u32[]{:S(2)}, u32[]{:S(2)}) collective-permute-start(bf16[4,592,128]{2,1,0:T(8,128)(2,1)} %memory_attend.2._), channel_id=1, source_target_pairs={{0,8},{8,0},{1,9},{9,1},{2,10},{10,2},{3,11},{11,3},{4,12},{12,4},... | collective-permute-start | bytes 1818632 | tf_op jit(solution)/shard_map/memory/ppermute | solution.py:693
  96.4 29.3 %all-to-all-start.3 = ((bf16[16,144,128]{2,1,0:T(8,128)(2,1)}), bf16[16,144,128]{2,1,0:T(8,128)(2,1)S(1)}, u32[]{:S(2)}, u32[]{:S(2)}) async-start(bf16[16,144,128]{2,1,0:T(8,128)(2,1)} %temporal_attend.1.refs_16_), calls=%async_computation.3 | async-start | bytes 1179648 | tf_op jit(solution)/shard_map/temporal/all_to_all | solution.py:624
  114.8 8.7 %collective-permute-start.17 = (bf16[592,128]{1,0:T(8,128)(2,1)}, bf16[592,128]{1,0:T(8,128)(2,1)S(1)}, u32[]{:S(2)}, u32[]{:S(2)}) collective-permute-start(bf16[592,128]{1,0:T(8,128)(2,1)} %get-tuple-element.24), channel_id=1, source_target_pairs={{0,1},{1,2},{2,3},{3,0},{4,5},{5,6},{6,7},{7,4},{8,9},{9,10},{10,1... | collective-permute-start | bytes 454664 | tf_op jit(solution)/shard_map/memory/ppermute | solution.py:627
  117.2 8.5 %collective-permute-start.18 = (bf16[592,128]{1,0:T(8,128)(2,1)}, bf16[592,128]{1,0:T(8,128)(2,1)S(1)}, u32[]{:S(2)}, u32[]{:S(2)}) collective-permute-start(bf16[592,128]{1,0:T(8,128)(2,1)} %get-tuple-element.25), channel_id=1, source_target_pairs={{0,2},{1,3},{2,0},{3,1},{4,6},{5,7},{6,4},{7,5},{8,10},{9,11},{10,... | collective-permute-start | bytes 454664 | tf_op jit(solution)/shard_map/memory/ppermute | solution.py:627
  119.9 5.8 %collective-permute-start.19 = (bf16[592,128]{1,0:T(8,128)(2,1)}, bf16[592,128]{1,0:T(8,128)(2,1)S(1)}, u32[]{:S(2)}, u32[]{:S(2)}) collective-permute-start(bf16[592,128]{1,0:T(8,128)(2,1)} %get-tuple-element.26), channel_id=1, source_target_pairs={{0,3},{1,0},{2,1},{3,2},{4,7},{5,4},{6,5},{7,6},{8,11},{9,8},{10,9... | collective-permute-start | bytes 454664 | tf_op jit(solution)/shard_map/memory/ppermute | solution.py:627

commit v16 on v15

--- a/solution.py
+++ b/solution.py
@@ -664,11 +664,14 @@
 
     with jax.named_scope("own"):
         own = own_attend(
-            hidden, entry_projection_matrix, query, after=[in_hbm(parts), above]
+            hidden,
+            entry_projection_matrix,
+            query,
+            after=[in_hbm(parts), second_above, second_below],
         )
 
     with jax.named_scope("temporal"):
-        sent, *_ = lax.optimization_barrier((parts, own, beside))
+        sent, *_ = lax.optimization_barrier((parts, beside, second_above, second_below))
         sent = swap(sent.reshape((quarters * G,) + parts.shape[2:]), frame)
 
     with jax.named_scope("store"):
@@ -691,13 +694,13 @@
     with jax.named_scope("memory"):
         sum_beside = memory_attend(0, index, beside, blocks, own)
         from_beside = lax.ppermute(sum_beside, "zq", other(sides))
+        sum_here = memory_attend(beside.shape[0], index, here, blocks, sum_beside)
 
     with jax.named_scope("temporal"):
-        timed = temporal_attend(lookback_lengths, sent, after=sum_beside)
+        timed = temporal_attend(lookback_lengths, sent, after=sum_here)
         time = swap(timed, frame)
 
     with jax.named_scope("memory"):
-        sum_here = memory_attend(beside.shape[0], index, here, blocks, timed)
         memory = swap_apart(add_partials(x, [in_hbm(sum_here), from_beside]))
 
     with jax.named_scope("exit"):

time: 133 us -> 142 us (1.068)
  waiting for transfers between devices: 30 us -> 41.1 us
  local copies, waits for them, and re-layouts: 4.41 us -> 2.99 us
    ppermute x1, waiting for transfers between devices: 0.01 us -> 10.1 us  [on_device(): second_above = lax.ppermute(second, 'y', turn(-1))]
    ppermute x3, waiting for transfers between devices: 4.29 us -> 8.24 us  [swap_apart(): lax.ppermute(blocks[j], 'x', turn(j))]
    ppermute x1, waiting for transfers between devices: 0.01 us -> 3.08 us  [on_device(): second_below = lax.ppermute(second, 'y', turn(1))]
    ppermute x1, waiting for transfers between devices: 2.76 us -> 0.01 us  [on_device(): from_beside = lax.ppermute(sum_beside, 'zq', other(sides))]
    ppermute x8, waiting for transfers between devices: 1.93 us -> 0.02 us  [on_device(): blocks = near + [lax.ppermute(block, 'c', other(cores)) for block in near]]
    unnamed x27 -> x29, local copies, waits for them, and re-layouts: 3.7 us -> 2.98 us
  transfers between devices with their start and end apart: 24 -> 24, of which waited for: 10 -> 8; matrix products, arithmetic and copies ran while one was open for 1% -> 0% of each run, Pallas kernels for 33% -> 31%
where the time goes in v16:
time: 142 us; the launch traced here: 141 us
  Pallas kernels  52.6 us (37%)
  starting transfers between devices  43.4 us (31%)
  waiting for transfers between devices  41.1 us (29%)
  local copies, waits for them, and re-layouts  2.99 us (2%)
    all_to_all x4, starting transfers between devices, swap(): return lax.all_to_all(blocks, axes, split_axis=0, concat_axis=0, tiled=True)  18 us
    pallas_call x2, Pallas kernels, memory_attend(): pl.pallas_call(functools.partial(memory_attend_kernel, count, first), in_...  16.5 us
    ppermute x1, waiting for transfers between devices, on_device(): far = lax.ppermute(below, 'y', turn(1))  13.3 us
    ppermute x1, waiting for transfers between devices, on_device(): second_above = lax.ppermute(second, 'y', turn(-1))  10.1 us
    pallas_call x1, Pallas kernels, temporal_entry(): pl.pallas_call(functools.partial(temporal_entry_kernel, quarters), in_spe...  8.58 us
    ppermute x3, waiting for transfers between devices, swap_apart(): lax.ppermute(blocks[j], 'x', turn(j))  8.24 us
    pallas_call x1, Pallas kernels, own_attend(): pl.pallas_call(own_attend_kernel, in_specs=[HBM, HBM, HBM] + [ANY] * len(...  8.14 us
    ppermute x3, starting transfers between devices, swap_apart(): lax.ppermute(blocks[j], 'x', turn(j))  6.13 us
  transfers between devices with their start and end apart: 24, of which 8 were waited for; matrix products, arithmetic and copies ran while one was open for 0% of the time, Pallas kernels for 31%

profile of v16, /device:TPU:0, one launch (start us, length us, event | category | flops | bytes accessed | tf_op | source)
XLA Modules:
  0.0 141.2 jit_solution(4996154514959722741)
XLA Ops:
  0.0 1.2 copy.12
  1.2 1.0 split_store.1._
  2.2 4.4 %all-to-all-start = ((bf16[4,288,256]{2,1,0:T(8,128)(2,1)}), bf16[4,288,256]{2,1,0:T(8,128)(2,1)S(1)}, u32[]{:S(2)}, u32[]{:S(2)}) async-start(bf16[4,288,256]{2,1,0:T(8,128)(2,1)} %bitcast.22), calls=%async_computation | async-start | bytes 1179648 | tf_op jit(solution)/shard_map/store/all_to_all | solution.py:624
  6.6 0.0 copy-done.5
  6.6 5.6 %modulate.1 = (bf16[576,2048]{1,0:T(8,128)(2,1)}, bf16[1,4,592,128]{3,2,1,0:T(8,128)(2,1)}) custom-call(bf16[576,2048]{1,0:T(8,128)(2,1)} %bitcast.23, f32[2,2048]{1,0:T(2,128)} %bitcast.25, bf16[2048,3072]{1,0:T(8,128)(2,1)} %weight_hbm.6, f32[2,4]{1,0:T(2,128)S(1)} %copy-done.4, s32[6]{0:T(128)S(1)} %bitcast.19, s32[6]{0:T(128)S(1)} %bitcast.20, ...), custom_call_target="tpu_custom_call" | custom-call | flops 75497472 | bytes 462848 | tf_op jit(solution)/shard_map/queries/modulate/pallas_call | solution.py:185
  12.2 4.6 %all-to-all-done.in_hbm = bf16[4,288,256]{2,1,0:T(8,128)(2,1)S(1)} async-done(((bf16[4,288,256]{2,1,0:T(8,128)(2,1)}), bf16[4,288,256]{2,1,0:T(8,128)(2,1)S(1)}, u32[]{:S(2)}, u32[]{:S(2)}) %all-to-all-start) | async-done | bytes 589856 | tf_op jit(solution)/shard_map/store/all_to_all | solution.py:624
  16.8 1.8 %join_pieces.1.refs_0_ = bf16[8,144,256]{2,1,0:T(8,128)(2,1)} custom-call(bf16[4,288,256]{2,1,0:T(8,128)(2,1)S(1)} %all-to-all-done.in_hbm, bf16[576,2048]{1,0:T(8,128)(2,1)} %get-tuple-element.16._.hidden_hbm), custom_call_target="tpu_custom_call" | custom-call | flops 18432 | bytes 73728 | tf_op jit(solution)/shard_map/store/join_pieces/pallas_call | solution.py:109
  18.5 2.0 %collective-permute-start = (bf16[8,144,256]{2,1,0:T(8,128)(2,1)}, bf16[8,144,256]{2,1,0:T(8,128)(2,1)S(1)}, u32[]{:S(2)}, u32[]{:S(2)}) collective-permute-start(bf16[8,144,256]{2,1,0:T(8,128)(2,1)} %join_pieces.1.refs_0_), channel_id=1, source_target_pairs={{0,4},{4,0},{1,5},{5,1},{2,6},{6,2},{3,7},{7,3},{8,12},{12,8},{9,1... | collective-permute-start | bytes 1769480 | tf_op jit(solution)/shard_map/store/ppermute | solution.py:651
  20.5 3.0 %collective-permute-start.3 = (bf16[8,144,256]{2,1,0:T(8,128)(2,1)}, bf16[8,144,256]{2,1,0:T(8,128)(2,1)S(1)}, u32[]{:S(2)}, u32[]{:S(2)}) collective-permute-start(bf16[8,144,256]{2,1,0:T(8,128)(2,1)} %join_pieces.1.refs_0_), channel_id=1, source_target_pairs={{0,96},{32,0},{64,32},{96,64},{1,97},{33,1},{65,33},{97,65},{2,98}... | collective-permute-start | bytes 1769480 | tf_op jit(solution)/shard_map/store/ppermute | solution.py:649
  23.5 0.0 collective-permute-start.4
  23.5 3.5 %all-to-all-start.1 = ((bf16[4,592,128]{2,1,0:T(8,128)(2,1)}), bf16[4,592,128]{2,1,0:T(8,128)(2,1)S(1)}, u32[]{:S(2)}, u32[]{:S(2)}) async-start(bf16[4,592,128]{2,1,0:T(8,128)(2,1)} %bitcast.6), calls=%async_computation.1 | async-start | bytes 1212416 | tf_op jit(solution)/shard_map/queries/all_to_all | solution.py:624
  27.0 8.6 %temporal_entry.1.refs_0_ = bf16[4,4,3,144,128]{4,3,2,1,0:T(8,128)(2,1)} custom-call(bf16[576,2048]{1,0:T(8,128)(2,1)} %get-tuple-element.16._.hidden_hbm, bf16[2048,3072]{1,0:T(8,128)(2,1)} %weight_hbm.6, f32[2,4]{1,0:T(2,128)S(1)} %copy-done.4, bf16[8,144,256]{2,1,0:T(8,128)(2,1)} %join_pieces.1.refs_0_), custom_call_target="tpu_custom_call" | custom-call | flops 226492416 | bytes 651264 | tf_op jit(solution)/shard_map/temporal/temporal_entry/pallas_call | solution.py:250
  35.6 0.3 all-to-all-done.1.query_hbm
  35.9 0.0 collective-permute-done.refs_1_
  35.9 0.0 collective-permute-done.3.refs_2_
  35.9 0.9 copy-done.8
  36.8 1.5 %collective-permute-done.4.refs_6_ = bf16[8,144,256]{2,1,0:T(8,128)(2,1)S(1)} collective-permute-done((bf16[8,144,256]{2,1,0:T(8,128)(2,1)}, bf16[8,144,256]{2,1,0:T(8,128)(2,1)S(1)}, u32[]{:S(2)}, u32[]{:S(2)}) %collective-permute-start.4) | collective-permute-done | bytes 589856 | tf_op jit(solution)/shard_map/store/ppermute | solution.py:650
  38.3 3.6 %collective-permute-start.5 = (bf16[4,592,128]{2,1,0:T(8,128)(2,1)S(1)}, bf16[4,592,128]{2,1,0:T(8,128)(2,1)S(1)}, u32[]{:S(2)}, u32[]{:S(2)}) collective-permute-start(bf16[4,592,128]{2,1,0:T(8,128)(2,1)S(1)} %all-to-all-done.1.query_hbm), channel_id=1, source_target_pairs={{0,8},{8,0},{1,9},{9,1},{2,10},{10,2},{3,11},{11,3},{4,12},{12,4},... | collective-permute-start | bytes 1818632 | tf_op jit(solution)/shard_map/queries/ppermute | solution.py:663
  41.9 1.5 %collective-permute-start.1 = (bf16[8,144,256]{2,1,0:T(8,128)(2,1)S(1)}, bf16[8,144,256]{2,1,0:T(8,128)(2,1)S(1)}, u32[]{:S(2)}, u32[]{:S(2)}) collective-permute-start(bf16[8,144,256]{2,1,0:T(8,128)(2,1)S(1)} %collective-permute-done.refs_1_), channel_id=1, source_target_pairs={{0,96},{32,0},{64,32},{96,64},{1,97},{33,1},{65,33},{97,65},{2,98}... | collective-permute-start | bytes 1769480 | tf_op jit(solution)/shard_map/store/ppermute | solution.py:653
  43.4 0.5 collective-permute-start.2
  43.9 10.1 %collective-permute-done.1.refs_1_.refs_3_ = bf16[8,144,256]{2,1,0:T(8,128)(2,1)S(1)} collective-permute-done((bf16[8,144,256]{2,1,0:T(8,128)(2,1)S(1)}, bf16[8,144,256]{2,1,0:T(8,128)(2,1)S(1)}, u32[]{:S(2)}, u32[]{:S(2)}) %collective-permute-start.1) | collective-permute-done | bytes 589856 | tf_op jit(solution)/shard_map/store/ppermute | solution.py:653
  54.0 3.1 %collective-permute-done.2.refs_2_.refs_7_ = bf16[8,144,256]{2,1,0:T(8,128)(2,1)S(1)} collective-permute-done((bf16[8,144,256]{2,1,0:T(8,128)(2,1)S(1)}, bf16[8,144,256]{2,1,0:T(8,128)(2,1)S(1)}, u32[]{:S(2)}, u32[]{:S(2)}) %collective-permute-start.2) | collective-permute-done | bytes 589856 | tf_op jit(solution)/shard_map/store/ppermute | solution.py:654
  57.1 0.0 collective-permute-done.5.query_hbm
  57.1 0.9 copy-done.2
  57.9 5.1 %all-to-all-start.2 = ((bf16[16,3,144,128]{3,2,1,0:T(8,128)(2,1)}), bf16[16,3,144,128]{3,2,1,0:T(8,128)(2,1)S(1)}, u32[]{:S(2)}, u32[]{:S(2)}) async-start(bf16[16,3,144,128]{3,2,1,0:T(8,128)(2,1)} %bitcast.21), calls=%async_computation.2 | async-start | bytes 3538944 | tf_op jit(solution)/shard_map/temporal/all_to_all | solution.py:624
  63.1 0.1 collective-permute-start.8
  63.2 0.5 collective-permute-start.9
  63.7 0.1 collective-permute-start.10
  63.8 0.0 collective-permute-start.6
  63.8 3.2 %collective-permute-start.7 = (bf16[8,144,256]{2,1,0:T(8,128)(2,1)S(1)}, bf16[8,144,256]{2,1,0:T(8,128)(2,1)}, u32[]{:S(2)}, u32[]{:S(2)}) collective-permute-start(bf16[8,144,256]{2,1,0:T(8,128)(2,1)S(1)} %collective-permute-done.1.refs_1_.refs_3_), channel_id=1, source_target_pairs={{0,96},{32,0},{64,32},{96,64},{1,97},{33,1},{65,33},{97,65},{2,98}... | collective-permute-start | bytes 1769480 | tf_op jit(solution)/shard_map/store/ppermute | solution.py:682
  67.0 0.0 collective-permute-done.8.refs_8_
  67.0 0.0 collective-permute-start.11
  67.0 0.0 collective-permute-done.9.refs_9_
  67.0 0.0 copy-start.11
  67.0 0.5 collective-permute-start.14
  67.5 0.0 collective-permute-done.10.refs_10_
  67.5 0.1 collective-permute-start.15
  67.6 13.3 %collective-permute-done.6.refs_4_ = bf16[8,144,256]{2,1,0:T(8,128)(2,1)} collective-permute-done((bf16[8,144,256]{2,1,0:T(8,128)(2,1)}, bf16[8,144,256]{2,1,0:T(8,128)(2,1)}, u32[]{:S(2)}, u32[]{:S(2)}) %collective-permute-start.6) | collective-permute-done | bytes 589856 | tf_op jit(solution)/shard_map/store/ppermute | solution.py:681
  81.0 0.0 collective-permute-start.12
  81.0 0.0 collective-permute-done.7.refs_5_
  81.0 0.5 collective-permute-start.13
  81.5 0.0 copy-done.11
  81.5 8.1 %own_attend.1.refs_16_.own_hbm = bf16[4,592,128]{2,1,0:T(8,128)(2,1)} custom-call(bf16[576,2048]{1,0:T(8,128)(2,1)} %get-tuple-element.16._.hidden_hbm, bf16[2048,3072]{1,0:T(8,128)(2,1)} %weight_hbm.6, bf16[1,4,592,128]{3,2,1,0:T(8,128)(2,1)} %get-tuple-element.17.query_hbm, bf16[4,4,3,144,128]{4,3,2,1,0:T(8,128)(2,1)} %temporal_entry.1.refs_0_, ...), custom_call_target="tpu_custom_call" | custom-call | flops 214695936 | bytes 593920 | tf_op jit(solution)/shard_map/own/own_attend/pallas_call | solution.py:380
  89.7 0.0 collective-permute-done.11.refs_11_
  89.8 0.0 collective-permute-done.14.refs_14_
  89.8 0.0 collective-permute-done.15.refs_15_
  89.8 0.0 collective-permute-done.12.refs_12_
  89.8 0.0 collective-permute-done.13.refs_13_
  89.8 8.3 %memory_attend.2.refs_16_ = bf16[4,592,128]{2,1,0:T(8,128)(2,1)} custom-call(s32[8,6]{1,0:T(8,128)S(1)} %fusion.10.index_ref, bf16[4,592,128]{2,1,0:T(8,128)(2,1)S(1)} %copy-done.3, bf16[8,144,256]{2,1,0:T(8,128)(2,1)} %join_pieces.1.refs_0_, bf16[8,144,256]{2,1,0:T(8,128)(2,1)} %copy-done.7, bf16[8,144,256]{2,1,0:T(8,128)(2,1)} %copy-done.8, ...), custom_call_target="tpu_custom_call" | custom-call | flops 261881856 | bytes 186368 | tf_op jit(solution)/shard_map/memory/memory_attend/pallas_call | solution.py:448
  98.1 3.6 %collective-permute-start.16 = (bf16[4,592,128]{2,1,0:T(8,128)(2,1)}, bf16[4,592,128]{2,1,0:T(8,128)(2,1)S(1)}, u32[]{:S(2)}, u32[]{:S(2)}) collective-permute-start(bf16[4,592,128]{2,1,0:T(8,128)(2,1)} %memory_attend.2.refs_16_), channel_id=1, source_target_pairs={{0,8},{8,0},{1,9},{9,1},{2,10},{10,2},{3,11},{11,3},{4,12},{12,4},... | collective-permute-start | bytes 1818632 | tf_op jit(solution)/shard_map/memory/ppermute | solution.py:696
  102.4 8.3 %memory_attend.3.refs_0_._ = bf16[4,592,128]{2,1,0:T(8,128)(2,1)} custom-call(s32[8,6]{1,0:T(8,128)S(1)} %fusion.10.index_ref, bf16[4,592,128]{2,1,0:T(8,128)(2,1)S(1)} %all-to-all-done.1.query_hbm, bf16[8,144,256]{2,1,0:T(8,128)(2,1)} %join_pieces.1.refs_0_, bf16[8,144,256]{2,1,0:T(8,128)(2,1)} %copy-done.7, bf16[8,144,256]{2,1,0:T(8,128)(2,1)} %copy-done.8, ...), custom_call_target="tpu_custom_call" | custom-call | flops 261881856 | bytes 186368 | tf_op jit(solution)/shard_map/memory/memory_attend/pallas_call | solution.py:448
  110.7 0.0 all-to-all-done.2.in_hbm_ref
  110.7 2.5 %temporal_attend.1 = bf16[16,144,128]{2,1,0:T(8,128)(2,1)} custom-call(s32[1]{0:T(128)S(6)} %copy.17.length_ref, bf16[16,3,144,128]{3,2,1,0:T(8,128)(2,1)S(1)} %all-to-all-done.2.in_hbm_ref, bf16[4,592,128]{2,1,0:T(8,128)(2,1)} %memory_attend.3.refs_0_._), custom_call_target="tpu_custom_call" | custom-call | flops 18874368 | bytes 147456 | tf_op jit(solution)/shard_map/temporal/temporal_attend/pallas_call | solution.py:300
  113.1 5.0 %all-to-all-start.3 = ((bf16[16,144,128]{2,1,0:T(8,128)(2,1)}), bf16[16,144,128]{2,1,0:T(8,128)(2,1)S(1)}, u32[]{:S(2)}, u32[]{:S(2)}) async-start(bf16[16,144,128]{2,1,0:T(8,128)(2,1)} %temporal_attend.1), calls=%async_computation.3 | async-start | bytes 1179648 | tf_op jit(solution)/shard_map/temporal/all_to_all | solution.py:624
  118.1 0.0 collective-permute-done.16.refs_1_
  118.1 2.4 %add_partials.1 = (bf16[592,128]{1,0:T(8,128)(2,1)}, bf16[592,128]{1,0:T(8,128)(2,1)}, bf16[592,128]{1,0:T(8,128)(2,1)}, bf16[592,128]{1,0:T(8,128)(2,1)}) custom-call(s32[1]{0:T(128)} %bitcast.x_ref, bf16[4,592,128]{2,1,0:T(8,128)(2,1)} %memory_attend.3.refs_0_._, bf16[4,592,128]{2,1,0:T(8,128)(2,1)S(1)} %collective-permute-done.16.refs_1_), custom_call_target="tpu_custom_call" | custom-call | flops 75776 | bytes 151552 | tf_op jit(solution)/shard_map/memory/add_partials/pallas_call | solution.py:500
  120.5 2.0 %collective-permute-start.17 = (bf16[592,128]{1,0:T(8,128)(2,1)}, bf16[592,128]{1,0:T(8,128)(2,1)S(1)}, u32[]{:S(2)}, u32[]{:S(2)}) collective-permute-start(bf16[592,128]{1,0:T(8,128)(2,1)} %get-tuple-element.23), channel_id=1, source_target_pairs={{0,1},{1,2},{2,3},{3,0},{4,5},{5,6},{6,7},{7,4},{8,9},{9,10},{10,1... | collective-permute-start | bytes 454664 | tf_op jit(solution)/shard_map/memory/ppermute | solution.py:627
  122.5 2.7 %collective-permute-start.18 = (bf16[592,128]{1,0:T(8,128)(2,1)}, bf16[592,128]{1,0:T(8,128)(2,1)S(1)}, u32[]{:S(2)}, u32[]{:S(2)}) collective-permute-start(bf16[592,128]{1,0:T(8,128)(2,1)} %get-tuple-element.24), channel_id=1, source_target_pairs={{0,2},{1,3},{2,0},{3,1},{4,6},{5,7},{6,4},{7,5},{8,10},{9,11},{10,... | collective-permute-start | bytes 454664 | tf_op jit(solution)/shard_map/memory/ppermute | solution.py:627
  125.2 1.5 %collective-permute-start.19 = (bf16[592,128]{1,0:T(8,128)(2,1)}, bf16[592,128]{1,0:T(8,128)(2,1)S(1)}, u32[]{:S(2)}, u32[]{:S(2)}) collective-permute-start(bf16[592,128]{1,0:T(8,128)(2,1)} %get-tuple-element.25), channel_id=1, source_target_pairs={{0,3},{1,0},{2,1},{3,2},{4,7},{5,4},{6,5},{7,6},{8,11},{9,8},{10,9... | collective-permute-start | bytes 454664 | tf_op jit(solution)/shard_map/memory/ppermute | solution.py:627
  126.7 5.6 %collective-permute-done.17.memory_1 = bf16[592,128]{1,0:T(8,128)(2,1)S(1)} collective-permute-done((bf16[592,128]{1,0:T(8,128)(2,1)}, bf16[592,128]{1,0:T(8,128)(2,1)S(1)}, u32[]{:S(2)}, u32[]{:S(2)}) %collective-permute-start.17) | collective-permute-done | bytes 151584 | tf_op jit(solution)/shard_map/memory/ppermute | solution.py:627
  132.2 2.7 %collective-permute-done.18.memory_2 = bf16[592,128]{1,0:T(8,128)(2,1)S(1)} collective-permute-done((bf16[592,128]{1,0:T(8,128)(2,1)}, bf16[592,128]{1,0:T(8,128)(2,1)S(1)}, u32[]{:S(2)}, u32[]{:S(2)}) %collective-permute-start.18) | collective-permute-done | bytes 151584 | tf_op jit(solution)/shard_map/memory/ppermute | solution.py:627
  134.9 0.0 collective-permute-done.19.memory_3
  134.9 0.0 all-to-all-done.3.time_hbm
  134.9 6.1 %leave.1 = bf16[576,2048]{1,0:T(8,128)(2,1)} custom-call(s32[1]{0:T(128)} %bitcast.x_ref, bf16[4,592,128]{2,1,0:T(8,128)(2,1)} %own_attend.1.refs_16_.own_hbm, bf16[592,128]{1,0:T(8,128)(2,1)} %get-tuple-element.22.memory_0, bf16[592,128]{1,0:T(8,128)(2,1)S(1)} %collective-permute-done.17.memory_1, bf16[592,128]{1,0:T(8,128)(2,1)S(1)} %collective-permute-done.18.memory_2, ...), custom_call_target="tpu_custom_call" | custom-call | flops 150994944 | bytes 630784 | tf_op jit(solution)/shard_map/exit/leave/pallas_call | solution.py:571
  (26 shorter events, 0.1 us)
Async XLA Ops:
  0.0 6.6 %copy-start.5 = (s32[1,1,6,1]{2,3,1,0:T(1,128)S(1)}, s32[1,1,6,1]{2,3,1,0:T(1,128)}, u32[]{:S(2)}) copy-start(s32[1,1,6,1]{2,3,1,0:T(1,128)} %param.15) | copy-start | bytes 76
  0.0 6.6 %copy-start.6 = (s32[1,1,6]{2,1,0:T(1,128)S(1)}, s32[1,1,6]{2,1,0:T(1,128)}, u32[]{:S(2)}) copy-start(s32[1,1,6]{2,1,0:T(1,128)} %param.16) | copy-start | bytes 76
  0.0 6.6 %copy-start.4 = (f32[2,4]{1,0:T(2,128)S(1)}, f32[2,4]{1,0:T(2,128)}, u32[]{:S(2)}) copy-start(f32[2,4]{1,0:T(2,128)} %sharpness_ref.3) | copy-start | bytes 100
  2.2 14.6 %all-to-all-start = ((bf16[4,288,256]{2,1,0:T(8,128)(2,1)}), bf16[4,288,256]{2,1,0:T(8,128)(2,1)S(1)}, u32[]{:S(2)}, u32[]{:S(2)}) async-start(bf16[4,288,256]{2,1,0:T(8,128)(2,1)} %bitcast.22), calls=%async_computation | async-start | bytes 1179648 | tf_op jit(solution)/shard_map/store/all_to_all | solution.py:624
  18.5 17.4 %collective-permute-start = (bf16[8,144,256]{2,1,0:T(8,128)(2,1)}, bf16[8,144,256]{2,1,0:T(8,128)(2,1)S(1)}, u32[]{:S(2)}, u32[]{:S(2)}) collective-permute-start(bf16[8,144,256]{2,1,0:T(8,128)(2,1)} %join_pieces.1.refs_0_), channel_id=1, source_target_pairs={{0,4},{4,0},{1,5},{5,1},{2,6},{6,2},{3,7},{7,3},{8,12},{12,8},{9,1... | collective-permute-start | bytes 1769480 | tf_op jit(solution)/shard_map/store/ppermute | solution.py:651
  20.5 15.4 %collective-permute-start.3 = (bf16[8,144,256]{2,1,0:T(8,128)(2,1)}, bf16[8,144,256]{2,1,0:T(8,128)(2,1)S(1)}, u32[]{:S(2)}, u32[]{:S(2)}) collective-permute-start(bf16[8,144,256]{2,1,0:T(8,128)(2,1)} %join_pieces.1.refs_0_), channel_id=1, source_target_pairs={{0,96},{32,0},{64,32},{96,64},{1,97},{33,1},{65,33},{97,65},{2,98}... | collective-permute-start | bytes 1769480 | tf_op jit(solution)/shard_map/store/ppermute | solution.py:649
  23.5 14.7 %collective-permute-start.4 = (bf16[8,144,256]{2,1,0:T(8,128)(2,1)}, bf16[8,144,256]{2,1,0:T(8,128)(2,1)S(1)}, u32[]{:S(2)}, u32[]{:S(2)}) collective-permute-start(bf16[8,144,256]{2,1,0:T(8,128)(2,1)} %join_pieces.1.refs_0_), channel_id=1, source_target_pairs={{0,32},{32,64},{64,96},{96,0},{1,33},{33,65},{65,97},{97,1},{2,34}... | collective-permute-start | bytes 1769480 | tf_op jit(solution)/shard_map/store/ppermute | solution.py:650
  23.5 12.3 %all-to-all-start.1 = ((bf16[4,592,128]{2,1,0:T(8,128)(2,1)}), bf16[4,592,128]{2,1,0:T(8,128)(2,1)S(1)}, u32[]{:S(2)}, u32[]{:S(2)}) async-start(bf16[4,592,128]{2,1,0:T(8,128)(2,1)} %bitcast.6), calls=%async_computation.1 | async-start | bytes 1212416 | tf_op jit(solution)/shard_map/queries/all_to_all | solution.py:624
  35.9 22.1 %copy-start.7 = (bf16[8,144,256]{2,1,0:T(8,128)(2,1)}, bf16[8,144,256]{2,1,0:T(8,128)(2,1)S(1)}, u32[]{:S(2)}) copy-start(bf16[8,144,256]{2,1,0:T(8,128)(2,1)S(1)} %collective-permute-done.refs_1_) | copy-start | bytes 1769476
  35.9 0.9 copy-start.8
  38.3 3.6 %copy-start.9 = (bf16[8,144,256]{2,1,0:T(8,128)(2,1)}, bf16[8,144,256]{2,1,0:T(8,128)(2,1)S(1)}, u32[]{:S(2)}) copy-start(bf16[8,144,256]{2,1,0:T(8,128)(2,1)S(1)} %collective-permute-done.4.refs_6_) | copy-start | bytes 1769476
  38.3 18.8 %collective-permute-start.5 = (bf16[4,592,128]{2,1,0:T(8,128)(2,1)S(1)}, bf16[4,592,128]{2,1,0:T(8,128)(2,1)S(1)}, u32[]{:S(2)}, u32[]{:S(2)}) collective-permute-start(bf16[4,592,128]{2,1,0:T(8,128)(2,1)S(1)} %all-to-all-done.1.query_hbm), channel_id=1, source_target_pairs={{0,8},{8,0},{1,9},{9,1},{2,10},{10,2},{3,11},{11,3},{4,12},{12,4},... | collective-permute-start | bytes 1818632 | tf_op jit(solution)/shard_map/queries/ppermute | solution.py:663
  41.9 12.1 %collective-permute-start.1 = (bf16[8,144,256]{2,1,0:T(8,128)(2,1)S(1)}, bf16[8,144,256]{2,1,0:T(8,128)(2,1)S(1)}, u32[]{:S(2)}, u32[]{:S(2)}) collective-permute-start(bf16[8,144,256]{2,1,0:T(8,128)(2,1)S(1)} %collective-permute-done.refs_1_), channel_id=1, source_target_pairs={{0,96},{32,0},{64,32},{96,64},{1,97},{33,1},{65,33},{97,65},{2,98}... | collective-permute-start | bytes 1769480 | tf_op jit(solution)/shard_map/store/ppermute | solution.py:653
  43.4 13.7 %collective-permute-start.2 = (bf16[8,144,256]{2,1,0:T(8,128)(2,1)S(1)}, bf16[8,144,256]{2,1,0:T(8,128)(2,1)S(1)}, u32[]{:S(2)}, u32[]{:S(2)}) collective-permute-start(bf16[8,144,256]{2,1,0:T(8,128)(2,1)S(1)} %collective-permute-done.refs_1_), channel_id=1, source_target_pairs={{0,32},{32,64},{64,96},{96,0},{1,33},{33,65},{65,97},{97,1},{2,34}... | collective-permute-start | bytes 1769480 | tf_op jit(solution)/shard_map/store/ppermute | solution.py:654
  54.0 35.7 %copy-start = (bf16[8,144,256]{2,1,0:T(8,128)(2,1)}, bf16[8,144,256]{2,1,0:T(8,128)(2,1)S(1)}, u32[]{:S(2)}) copy-start(bf16[8,144,256]{2,1,0:T(8,128)(2,1)S(1)} %collective-permute-done.1.refs_1_.refs_3_) | copy-start | bytes 1769476
  57.1 32.6 %copy-start.1 = (bf16[8,144,256]{2,1,0:T(8,128)(2,1)}, bf16[8,144,256]{2,1,0:T(8,128)(2,1)S(1)}, u32[]{:S(2)}) copy-start(bf16[8,144,256]{2,1,0:T(8,128)(2,1)S(1)} %collective-permute-done.2.refs_2_.refs_7_) | copy-start | bytes 1769476
  57.1 0.9 copy-start.2
  57.9 52.7 %all-to-all-start.2 = ((bf16[16,3,144,128]{3,2,1,0:T(8,128)(2,1)}), bf16[16,3,144,128]{3,2,1,0:T(8,128)(2,1)S(1)}, u32[]{:S(2)}, u32[]{:S(2)}) async-start(bf16[16,3,144,128]{3,2,1,0:T(8,128)(2,1)} %bitcast.21), calls=%async_computation.2 | async-start | bytes 3538944 | tf_op jit(solution)/shard_map/temporal/all_to_all | solution.py:624
  63.1 3.9 %collective-permute-start.8 = (bf16[8,144,256]{2,1,0:T(8,128)(2,1)}, bf16[8,144,256]{2,1,0:T(8,128)(2,1)S(1)}, u32[]{:S(2)}, u32[]{:S(2)}) collective-permute-start(bf16[8,144,256]{2,1,0:T(8,128)(2,1)} %join_pieces.1.refs_0_), channel_id=1, source_target_pairs={{0,16},{16,0},{1,17},{17,1},{2,18},{18,2},{3,19},{19,3},{4,20},{20... | collective-permute-start | bytes 1769480 | tf_op jit(solution)/shard_map/store/ppermute | solution.py:684
  63.2 3.8 %collective-permute-start.9 = (bf16[8,144,256]{2,1,0:T(8,128)(2,1)}, bf16[8,144,256]{2,1,0:T(8,128)(2,1)S(1)}, u32[]{:S(2)}, u32[]{:S(2)}) collective-permute-start(bf16[8,144,256]{2,1,0:T(8,128)(2,1)} %copy-done.7), channel_id=1, source_target_pairs={{0,16},{16,0},{1,17},{17,1},{2,18},{18,2},{3,19},{19,3},{4,20},{20... | collective-permute-start | bytes 1769480 | tf_op jit(solution)/shard_map/store/ppermute | solution.py:684
  63.7 3.9 %collective-permute-start.10 = (bf16[8,144,256]{2,1,0:T(8,128)(2,1)}, bf16[8,144,256]{2,1,0:T(8,128)(2,1)S(1)}, u32[]{:S(2)}, u32[]{:S(2)}) collective-permute-start(bf16[8,144,256]{2,1,0:T(8,128)(2,1)} %copy-done.8), channel_id=1, source_target_pairs={{0,16},{16,0},{1,17},{17,1},{2,18},{18,2},{3,19},{19,3},{4,20},{20... | collective-permute-start | bytes 1769480 | tf_op jit(solution)/shard_map/store/ppermute | solution.py:684
  63.8 17.2 %collective-permute-start.6 = (bf16[8,144,256]{2,1,0:T(8,128)(2,1)}, bf16[8,144,256]{2,1,0:T(8,128)(2,1)}, u32[]{:S(2)}, u32[]{:S(2)}) collective-permute-start(bf16[8,144,256]{2,1,0:T(8,128)(2,1)} %copy-done.9), channel_id=1, source_target_pairs={{0,32},{32,64},{64,96},{96,0},{1,33},{33,65},{65,97},{97,1},{2,34}... | collective-permute-start | bytes 1769480 | tf_op jit(solution)/shard_map/store/ppermute | solution.py:681
  63.8 17.2 %collective-permute-start.7 = (bf16[8,144,256]{2,1,0:T(8,128)(2,1)S(1)}, bf16[8,144,256]{2,1,0:T(8,128)(2,1)}, u32[]{:S(2)}, u32[]{:S(2)}) collective-permute-start(bf16[8,144,256]{2,1,0:T(8,128)(2,1)S(1)} %collective-permute-done.1.refs_1_.refs_3_), channel_id=1, source_target_pairs={{0,96},{32,0},{64,32},{96,64},{1,97},{33,1},{65,33},{97,65},{2,98}... | collective-permute-start | bytes 1769480 | tf_op jit(solution)/shard_map/store/ppermute | solution.py:682
  67.0 14.0 %copy-start.10 = (bf16[8,144,256]{2,1,0:T(8,128)(2,1)}, bf16[8,144,256]{2,1,0:T(8,128)(2,1)S(1)}, u32[]{:S(2)}) copy-start(bf16[8,144,256]{2,1,0:T(8,128)(2,1)S(1)} %collective-permute-done.8.refs_8_) | copy-start | bytes 1769476
  67.0 22.7 %collective-permute-start.11 = (bf16[8,144,256]{2,1,0:T(8,128)(2,1)S(1)}, bf16[8,144,256]{2,1,0:T(8,128)(2,1)}, u32[]{:S(2)}, u32[]{:S(2)}) collective-permute-start(bf16[8,144,256]{2,1,0:T(8,128)(2,1)S(1)} %collective-permute-done.1.refs_1_.refs_3_), channel_id=1, source_target_pairs={{0,16},{16,0},{1,17},{17,1},{2,18},{18,2},{3,19},{19,3},{4,20},{20... | collective-permute-start | bytes 1769480 | tf_op jit(solution)/shard_map/store/ppermute | solution.py:684
  67.0 14.5 %copy-start.11 = (bf16[8,144,256]{2,1,0:T(8,128)(2,1)}, bf16[8,144,256]{2,1,0:T(8,128)(2,1)S(1)}, u32[]{:S(2)}) copy-start(bf16[8,144,256]{2,1,0:T(8,128)(2,1)S(1)} %collective-permute-done.9.refs_9_) | copy-start | bytes 1769476
  67.0 22.7 %collective-permute-start.14 = (bf16[8,144,256]{2,1,0:T(8,128)(2,1)}, bf16[8,144,256]{2,1,0:T(8,128)(2,1)}, u32[]{:S(2)}, u32[]{:S(2)}) collective-permute-start(bf16[8,144,256]{2,1,0:T(8,128)(2,1)} %copy-done.9), channel_id=1, source_target_pairs={{0,16},{16,0},{1,17},{17,1},{2,18},{18,2},{3,19},{19,3},{4,20},{20... | collective-permute-start | bytes 1769480 | tf_op jit(solution)/shard_map/store/ppermute | solution.py:684
  67.5 14.0 %copy-start.12 = (bf16[8,144,256]{2,1,0:T(8,128)(2,1)}, bf16[8,144,256]{2,1,0:T(8,128)(2,1)S(1)}, u32[]{:S(2)}) copy-start(bf16[8,144,256]{2,1,0:T(8,128)(2,1)S(1)} %collective-permute-done.10.refs_10_) | copy-start | bytes 1769476
  67.5 22.2 %collective-permute-start.15 = (bf16[8,144,256]{2,1,0:T(8,128)(2,1)S(1)}, bf16[8,144,256]{2,1,0:T(8,128)(2,1)}, u32[]{:S(2)}, u32[]{:S(2)}) collective-permute-start(bf16[8,144,256]{2,1,0:T(8,128)(2,1)S(1)} %collective-permute-done.2.refs_2_.refs_7_), channel_id=1, source_target_pairs={{0,16},{16,0},{1,17},{17,1},{2,18},{18,2},{3,19},{19,3},{4,20},{20... | collective-permute-start | bytes 1769480 | tf_op jit(solution)/shard_map/store/ppermute | solution.py:684
  81.0 8.8 %collective-permute-start.12 = (bf16[8,144,256]{2,1,0:T(8,128)(2,1)}, bf16[8,144,256]{2,1,0:T(8,128)(2,1)}, u32[]{:S(2)}, u32[]{:S(2)}) collective-permute-start(bf16[8,144,256]{2,1,0:T(8,128)(2,1)} %collective-permute-done.6.refs_4_), channel_id=1, source_target_pairs={{0,16},{16,0},{1,17},{17,1},{2,18},{18,2},{3,19},{19,3},{4,20},{20... | collective-permute-start | bytes 1769480 | tf_op jit(solution)/shard_map/store/ppermute | solution.py:684
  81.0 8.8 %collective-permute-start.13 = (bf16[8,144,256]{2,1,0:T(8,128)(2,1)}, bf16[8,144,256]{2,1,0:T(8,128)(2,1)}, u32[]{:S(2)}, u32[]{:S(2)}) collective-permute-start(bf16[8,144,256]{2,1,0:T(8,128)(2,1)} %collective-permute-done.7.refs_5_), channel_id=1, source_target_pairs={{0,16},{16,0},{1,17},{17,1},{2,18},{18,2},{3,19},{19,3},{4,20},{20... | collective-permute-start | bytes 1769480 | tf_op jit(solution)/shard_map/store/ppermute | solution.py:684
  81.5 8.2 %copy-start.3 = (bf16[4,592,128]{2,1,0:T(8,128)(2,1)S(1)}, bf16[4,592,128]{2,1,0:T(8,128)(2,1)}, u32[]{:S(2)}) copy-start(bf16[4,592,128]{2,1,0:T(8,128)(2,1)} %copy-done.2) | copy-start | bytes 1818628
  98.1 20.0 %collective-permute-start.16 = (bf16[4,592,128]{2,1,0:T(8,128)(2,1)}, bf16[4,592,128]{2,1,0:T(8,128)(2,1)S(1)}, u32[]{:S(2)}, u32[]{:S(2)}) collective-permute-start(bf16[4,592,128]{2,1,0:T(8,128)(2,1)} %memory_attend.2.refs_16_), channel_id=1, source_target_pairs={{0,8},{8,0},{1,9},{9,1},{2,10},{10,2},{3,11},{11,3},{4,12},{12,4},... | collective-permute-start | bytes 1818632 | tf_op jit(solution)/shard_map/memory/ppermute | solution.py:696
  113.1 21.8 %all-to-all-start.3 = ((bf16[16,144,128]{2,1,0:T(8,128)(2,1)}), bf16[16,144,128]{2,1,0:T(8,128)(2,1)S(1)}, u32[]{:S(2)}, u32[]{:S(2)}) async-start(bf16[16,144,128]{2,1,0:T(8,128)(2,1)} %temporal_attend.1), calls=%async_computation.3 | async-start | bytes 1179648 | tf_op jit(solution)/shard_map/temporal/all_to_all | solution.py:624
  120.5 11.7 %collective-permute-start.17 = (bf16[592,128]{1,0:T(8,128)(2,1)}, bf16[592,128]{1,0:T(8,128)(2,1)S(1)}, u32[]{:S(2)}, u32[]{:S(2)}) collective-permute-start(bf16[592,128]{1,0:T(8,128)(2,1)} %get-tuple-element.23), channel_id=1, source_target_pairs={{0,1},{1,2},{2,3},{3,0},{4,5},{5,6},{6,7},{7,4},{8,9},{9,10},{10,1... | collective-permute-start | bytes 454664 | tf_op jit(solution)/shard_map/memory/ppermute | solution.py:627
  122.5 12.4 %collective-permute-start.18 = (bf16[592,128]{1,0:T(8,128)(2,1)}, bf16[592,128]{1,0:T(8,128)(2,1)S(1)}, u32[]{:S(2)}, u32[]{:S(2)}) collective-permute-start(bf16[592,128]{1,0:T(8,128)(2,1)} %get-tuple-element.24), channel_id=1, source_target_pairs={{0,2},{1,3},{2,0},{3,1},{4,6},{5,7},{6,4},{7,5},{8,10},{9,11},{10,... | collective-permute-start | bytes 454664 | tf_op jit(solution)/shard_map/memory/ppermute | solution.py:627
  125.2 9.7 %collective-permute-start.19 = (bf16[592,128]{1,0:T(8,128)(2,1)}, bf16[592,128]{1,0:T(8,128)(2,1)S(1)}, u32[]{:S(2)}, u32[]{:S(2)}) collective-permute-start(bf16[592,128]{1,0:T(8,128)(2,1)} %get-tuple-element.25), channel_id=1, source_target_pairs={{0,3},{1,0},{2,1},{3,2},{4,7},{5,4},{6,5},{7,6},{8,11},{9,8},{10,9... | collective-permute-start | bytes 454664 | tf_op jit(solution)/shard_map/memory/ppermute | solution.py:627

commit v17 on v15

--- a/solution.py
+++ b/solution.py
@@ -668,7 +668,7 @@
         )
 
     with jax.named_scope("temporal"):
-        sent, *_ = lax.optimization_barrier((parts, own, beside))
+        sent, *_ = lax.optimization_barrier((parts, second))
         sent = swap(sent.reshape((quarters * G,) + parts.shape[2:]), frame)
 
     with jax.named_scope("store"):
@@ -688,16 +688,14 @@
         c = (named // held & (cores - 1)) ^ lax.axis_index("c")
         index = (c * rings + y) * held + (named & (held - 1))
 
+    with jax.named_scope("temporal"):
+        timed = temporal_attend(lookback_lengths, sent, after=own)
+        time = swap(timed, frame)
+
     with jax.named_scope("memory"):
-        sum_beside = memory_attend(0, index, beside, blocks, own)
+        sum_beside = memory_attend(0, index, beside, blocks, timed)
         from_beside = lax.ppermute(sum_beside, "zq", other(sides))
-
-    with jax.named_scope("temporal"):
-        timed = temporal_attend(lookback_lengths, sent, after=sum_beside)
-        time = swap(timed, frame)
-
-    with jax.named_scope("memory"):
-        sum_here = memory_attend(beside.shape[0], index, here, blocks, timed)
+        sum_here = memory_attend(beside.shape[0], index, here, blocks, sum_beside)
         memory = swap_apart(add_partials(x, [in_hbm(sum_here), from_beside]))
 
     with jax.named_scope("exit"):

time: 133 us -> 153 us (1.15)
  waiting for transfers between devices: 30 us -> 50.7 us
    ppermute x1, waiting for transfers between devices: 0.87 us -> 28.4 us  [on_device(): beside = lax.ppermute(here, 'zq', other(sides))]
    ppermute x1, waiting for transfers between devices: 12.8 us -> 0.01 us  [on_device(): far = lax.ppermute(below, 'y', turn(1))]
    ppermute x1, waiting for transfers between devices: 0.01 us -> 5.78 us  [on_device(): second = lax.ppermute(joined, 'zp', other(sides))]
    ppermute x1, waiting for transfers between devices: 2.76 us -> 6.99 us  [on_device(): from_beside = lax.ppermute(sum_beside, 'zq', other(sides))]
    ppermute x1, starting transfers between devices: 3.5 us -> 0.45 us  [on_device(): from_beside = lax.ppermute(sum_beside, 'zq', other(sides))]
    all_to_all x4, starting transfers between devices: 18.5 us -> 21.1 us  [swap(): return lax.all_to_all(blocks, axes, split_axis=0, concat_axis=0, tiled=True)]
    ppermute x1, waiting for transfers between devices: 2.39 us -> 0.01 us  [on_device(): below = lax.ppermute(joined, 'y', turn(1))]
    ppermute x1, starting transfers between devices: 0.67 us -> 3.01 us  [on_device(): second_above = lax.ppermute(second, 'y', turn(-1))]
  transfers between devices with their start and end apart: 24 -> 24, of which waited for: 10 -> 7; matrix products, arithmetic and copies ran while one was open for 1% -> 0% of each run, Pallas kernels for 33% -> 23%
where the time goes in v17:
time: 153 us; the launch traced here: 152 us
  Pallas kernels  52.4 us (34%)
  waiting for transfers between devices  50.7 us (33%)
  starting transfers between devices  44 us (29%)
  local copies, waits for them, and re-layouts  3.83 us (3%)
    ppermute x1, waiting for transfers between devices, on_device(): beside = lax.ppermute(here, 'zq', other(sides))  28.4 us
    all_to_all x4, starting transfers between devices, swap(): return lax.all_to_all(blocks, axes, split_axis=0, concat_axis=0, tiled=True)  21.1 us
    pallas_call x2, Pallas kernels, memory_attend(): pl.pallas_call(functools.partial(memory_attend_kernel, count, first), in_...  16.5 us
    pallas_call x1, Pallas kernels, temporal_entry(): pl.pallas_call(functools.partial(temporal_entry_kernel, quarters), in_spe...  8.61 us
    pallas_call x1, Pallas kernels, own_attend(): pl.pallas_call(own_attend_kernel, in_specs=[HBM, HBM, HBM] + [ANY] * len(...  8.06 us
    ppermute x1, waiting for transfers between devices, on_device(): from_beside = lax.ppermute(sum_beside, 'zq', other(sides))  6.99 us
    pallas_call x1, Pallas kernels, leave(): pl.pallas_call(leave_kernel, in_specs=[SCALARS, HBM] + [ANY] * (G + 1) +...  6.11 us
    ppermute x1, waiting for transfers between devices, on_device(): second = lax.ppermute(joined, 'zp', other(sides))  5.78 us
  transfers between devices with their start and end apart: 24, of which 7 were waited for; matrix products, arithmetic and copies ran while one was open for 0% of the time, Pallas kernels for 23%

profile of v17, /device:TPU:0, one launch (start us, length us, event | category | flops | bytes accessed | tf_op | source)
XLA Modules:
  0.0 152.0 jit_solution(2458487768957509808)
XLA Ops:
  0.0 1.2 copy.12
  1.2 1.0 split_store.1._
  2.2 4.4 %all-to-all-start = ((bf16[4,288,256]{2,1,0:T(8,128)(2,1)}), bf16[4,288,256]{2,1,0:T(8,128)(2,1)S(1)}, u32[]{:S(2)}, u32[]{:S(2)}) async-start(bf16[4,288,256]{2,1,0:T(8,128)(2,1)} %bitcast.22), calls=%async_computation | async-start | bytes 1179648 | tf_op jit(solution)/shard_map/store/all_to_all | solution.py:624
  6.6 0.0 copy-done.4
  6.6 0.0 copy-done.5
  6.6 5.6 %modulate.1 = (bf16[576,2048]{1,0:T(8,128)(2,1)}, bf16[1,4,592,128]{3,2,1,0:T(8,128)(2,1)}) custom-call(bf16[576,2048]{1,0:T(8,128)(2,1)} %bitcast.23, f32[2,2048]{1,0:T(2,128)} %bitcast.25, bf16[2048,3072]{1,0:T(8,128)(2,1)} %weight_hbm.6, f32[2,4]{1,0:T(2,128)S(1)} %copy-done.3, s32[6]{0:T(128)S(1)} %bitcast.19, s32[6]{0:T(128)S(1)} %bitcast.20, ...), custom_call_target="tpu_custom_call" | custom-call | flops 75497472 | bytes 462848 | tf_op jit(solution)/shard_map/queries/modulate/pallas_call | solution.py:185
  12.2 4.6 %all-to-all-done.in_hbm = bf16[4,288,256]{2,1,0:T(8,128)(2,1)S(1)} async-done(((bf16[4,288,256]{2,1,0:T(8,128)(2,1)}), bf16[4,288,256]{2,1,0:T(8,128)(2,1)S(1)}, u32[]{:S(2)}, u32[]{:S(2)}) %all-to-all-start) | async-done | bytes 589856 | tf_op jit(solution)/shard_map/store/all_to_all | solution.py:624
  16.7 1.8 %join_pieces.1.refs_0_ = bf16[8,144,256]{2,1,0:T(8,128)(2,1)} custom-call(bf16[4,288,256]{2,1,0:T(8,128)(2,1)S(1)} %all-to-all-done.in_hbm, bf16[576,2048]{1,0:T(8,128)(2,1)} %get-tuple-element.16._.hidden_hbm), custom_call_target="tpu_custom_call" | custom-call | flops 18432 | bytes 73728 | tf_op jit(solution)/shard_map/store/join_pieces/pallas_call | solution.py:109
  18.5 2.0 %collective-permute-start.1 = (bf16[8,144,256]{2,1,0:T(8,128)(2,1)}, bf16[8,144,256]{2,1,0:T(8,128)(2,1)S(1)}, u32[]{:S(2)}, u32[]{:S(2)}) collective-permute-start(bf16[8,144,256]{2,1,0:T(8,128)(2,1)} %join_pieces.1.refs_0_), channel_id=1, source_target_pairs={{0,4},{4,0},{1,5},{5,1},{2,6},{6,2},{3,7},{7,3},{8,12},{12,8},{9,1... | collective-permute-start | bytes 1769480 | tf_op jit(solution)/shard_map/store/ppermute | solution.py:651
  20.5 3.5 %all-to-all-start.1 = ((bf16[4,592,128]{2,1,0:T(8,128)(2,1)}), bf16[4,592,128]{2,1,0:T(8,128)(2,1)S(1)}, u32[]{:S(2)}, u32[]{:S(2)}) async-start(bf16[4,592,128]{2,1,0:T(8,128)(2,1)} %bitcast.6), calls=%async_computation.1 | async-start | bytes 1212416 | tf_op jit(solution)/shard_map/queries/all_to_all | solution.py:624
  24.0 3.1 %collective-permute-start = (bf16[8,144,256]{2,1,0:T(8,128)(2,1)}, bf16[8,144,256]{2,1,0:T(8,128)(2,1)S(1)}, u32[]{:S(2)}, u32[]{:S(2)}) collective-permute-start(bf16[8,144,256]{2,1,0:T(8,128)(2,1)} %join_pieces.1.refs_0_), channel_id=1, source_target_pairs={{0,96},{32,0},{64,32},{96,64},{1,97},{33,1},{65,33},{97,65},{2,98}... | collective-permute-start | bytes 1769480 | tf_op jit(solution)/shard_map/store/ppermute | solution.py:649
  27.1 0.0 collective-permute-start.2
  27.1 5.8 %collective-permute-done.1.refs_1_ = bf16[8,144,256]{2,1,0:T(8,128)(2,1)S(1)} collective-permute-done((bf16[8,144,256]{2,1,0:T(8,128)(2,1)}, bf16[8,144,256]{2,1,0:T(8,128)(2,1)S(1)}, u32[]{:S(2)}, u32[]{:S(2)}) %collective-permute-start.1) | collective-permute-done | bytes 589856 | tf_op jit(solution)/shard_map/store/ppermute | solution.py:651
  32.9 3.0 %collective-permute-start.4 = (bf16[8,144,256]{2,1,0:T(8,128)(2,1)S(1)}, bf16[8,144,256]{2,1,0:T(8,128)(2,1)}, u32[]{:S(2)}, u32[]{:S(2)}) collective-permute-start(bf16[8,144,256]{2,1,0:T(8,128)(2,1)S(1)} %collective-permute-done.1.refs_1_), channel_id=1, source_target_pairs={{0,96},{32,0},{64,32},{96,64},{1,97},{33,1},{65,33},{97,65},{2,98}... | collective-permute-start | bytes 1769480 | tf_op jit(solution)/shard_map/store/ppermute | solution.py:653
  35.9 0.0 collective-permute-start.5
  35.9 0.0 collective-permute-start.8
  35.9 8.6 %temporal_entry.1.refs_0_ = bf16[4,4,3,144,128]{4,3,2,1,0:T(8,128)(2,1)} custom-call(bf16[576,2048]{1,0:T(8,128)(2,1)} %get-tuple-element.16._.hidden_hbm, bf16[2048,3072]{1,0:T(8,128)(2,1)} %weight_hbm.6, f32[2,4]{1,0:T(2,128)S(1)} %copy-done.3, bf16[8,144,256]{2,1,0:T(8,128)(2,1)} %join_pieces.1.refs_0_), custom_call_target="tpu_custom_call" | custom-call | flops 226492416 | bytes 651264 | tf_op jit(solution)/shard_map/temporal/temporal_entry/pallas_call | solution.py:250
  44.5 0.0 all-to-all-done.1.query_hbm
  44.5 5.9 %all-to-all-start.2 = ((bf16[16,3,144,128]{3,2,1,0:T(8,128)(2,1)}), bf16[16,3,144,128]{3,2,1,0:T(8,128)(2,1)S(1)}, u32[]{:S(2)}, u32[]{:S(2)}) async-start(bf16[16,3,144,128]{3,2,1,0:T(8,128)(2,1)} %bitcast.21), calls=%async_computation.2 | async-start | bytes 3538944 | tf_op jit(solution)/shard_map/temporal/all_to_all | solution.py:624
  50.4 0.0 collective-permute-done.refs_1_.refs_2_
  50.4 0.0 collective-permute-done.2.refs_6_
  50.4 3.5 %collective-permute-start.3 = (bf16[4,592,128]{2,1,0:T(8,128)(2,1)S(1)}, bf16[4,592,128]{2,1,0:T(8,128)(2,1)S(1)}, u32[]{:S(2)}, u32[]{:S(2)}) collective-permute-start(bf16[4,592,128]{2,1,0:T(8,128)(2,1)S(1)} %all-to-all-done.1.query_hbm), channel_id=1, source_target_pairs={{0,8},{8,0},{1,9},{9,1},{2,10},{10,2},{3,11},{11,3},{4,12},{12,4},... | collective-permute-start | bytes 1818632 | tf_op jit(solution)/shard_map/queries/ppermute | solution.py:663
  53.9 0.0 collective-permute-start.9
  53.9 0.0 collective-permute-done.4.refs_3_
  53.9 0.5 collective-permute-start.10
  54.4 0.1 collective-permute-done.5.refs_7_
  54.6 0.5 collective-permute-start.6
  55.0 0.0 collective-permute-done.8.refs_8_
  55.0 2.8 %collective-permute-start.7 = (bf16[8,144,256]{2,1,0:T(8,128)(2,1)}, bf16[8,144,256]{2,1,0:T(8,128)(2,1)}, u32[]{:S(2)}, u32[]{:S(2)}) collective-permute-start(bf16[8,144,256]{2,1,0:T(8,128)(2,1)} %collective-permute-done.4.refs_3_), channel_id=1, source_target_pairs={{0,96},{32,0},{64,32},{96,64},{1,97},{33,1},{65,33},{97,65},{2,98}... | collective-permute-start | bytes 1769480 | tf_op jit(solution)/shard_map/store/ppermute | solution.py:679
  57.8 0.0 collective-permute-done.9.refs_9_
  57.8 0.0 collective-permute-start.11
  57.8 0.0 collective-permute-done.10.refs_10_
  57.8 0.5 collective-permute-start.14
  58.3 28.4 %collective-permute-done.3.query_hbm = bf16[4,592,128]{2,1,0:T(8,128)(2,1)S(1)} collective-permute-done((bf16[4,592,128]{2,1,0:T(8,128)(2,1)S(1)}, bf16[4,592,128]{2,1,0:T(8,128)(2,1)S(1)}, u32[]{:S(2)}, u32[]{:S(2)}) %collective-permute-start.3) | collective-permute-done | bytes 606240 | tf_op jit(solution)/shard_map/queries/ppermute | solution.py:663
  86.8 0.8 copy-done.1
  87.6 0.0 collective-permute-start.15
  87.6 0.0 collective-permute-done.6.refs_4_
  87.6 0.6 collective-permute-start.12
  88.2 0.0 collective-permute-done.7.refs_5_
  88.2 0.3 collective-permute-start.13
  89.1 8.1 %own_attend.1._.own_hbm = bf16[4,592,128]{2,1,0:T(8,128)(2,1)} custom-call(bf16[576,2048]{1,0:T(8,128)(2,1)} %get-tuple-element.16._.hidden_hbm, bf16[2048,3072]{1,0:T(8,128)(2,1)} %weight_hbm.6, bf16[1,4,592,128]{3,2,1,0:T(8,128)(2,1)} %get-tuple-element.17.query_hbm, bf16[4,4,3,144,128]{4,3,2,1,0:T(8,128)(2,1)} %temporal_entry.1.refs_0_, ...), custom_call_target="tpu_custom_call" | custom-call | flops 214695936 | bytes 593920 | tf_op jit(solution)/shard_map/own/own_attend/pallas_call | solution.py:380
  97.2 0.7 slice.8
  98.0 0.0 all-to-all-done.2.in_hbm_ref
  98.0 2.4 %temporal_attend.1.refs_16_ = bf16[16,144,128]{2,1,0:T(8,128)(2,1)} custom-call(s32[1]{0:T(128)S(6)} %copy.17.length_ref, bf16[16,3,144,128]{3,2,1,0:T(8,128)(2,1)S(1)} %all-to-all-done.2.in_hbm_ref, bf16[4,592,128]{2,1,0:T(8,128)(2,1)} %own_attend.1._.own_hbm), custom_call_target="tpu_custom_call" | custom-call | flops 18874368 | bytes 147456 | tf_op jit(solution)/shard_map/temporal/temporal_attend/pallas_call | solution.py:300
  100.4 0.0 collective-permute-done.11.refs_11_
  100.4 0.0 collective-permute-done.14.refs_14_
  100.5 0.0 collective-permute-done.15.refs_15_
  100.5 0.0 collective-permute-done.12.refs_12_
  100.5 0.0 collective-permute-done.13.refs_13_
  100.5 1.1 copy-done.2
  101.6 8.3 %memory_attend.2.refs_16_ = bf16[4,592,128]{2,1,0:T(8,128)(2,1)} custom-call(s32[8,6]{1,0:T(8,128)S(1)} %fusion.10.index_ref, bf16[4,592,128]{2,1,0:T(8,128)(2,1)S(1)} %copy-done.2, bf16[8,144,256]{2,1,0:T(8,128)(2,1)} %join_pieces.1.refs_0_, bf16[8,144,256]{2,1,0:T(8,128)(2,1)} %copy-done.6, bf16[8,144,256]{2,1,0:T(8,128)(2,1)} %copy-done, ...), custom_call_target="tpu_custom_call" | custom-call | flops 261881856 | bytes 186368 | tf_op jit(solution)/shard_map/memory/memory_attend/pallas_call | solution.py:448
  109.8 0.4 collective-permute-start.16
  110.3 7.4 %all-to-all-start.3 = ((bf16[16,144,128]{2,1,0:T(8,128)(2,1)}), bf16[16,144,128]{2,1,0:T(8,128)(2,1)S(1)}, u32[]{:S(2)}, u32[]{:S(2)}) async-start(bf16[16,144,128]{2,1,0:T(8,128)(2,1)} %temporal_attend.1.refs_16_), calls=%async_computation.3 | async-start | bytes 1179648 | tf_op jit(solution)/shard_map/temporal/all_to_all | solution.py:624
  117.7 8.3 %memory_attend.3.refs_0_ = bf16[4,592,128]{2,1,0:T(8,128)(2,1)} custom-call(s32[8,6]{1,0:T(8,128)S(1)} %fusion.10.index_ref, bf16[4,592,128]{2,1,0:T(8,128)(2,1)S(1)} %all-to-all-done.1.query_hbm, bf16[8,144,256]{2,1,0:T(8,128)(2,1)} %join_pieces.1.refs_0_, bf16[8,144,256]{2,1,0:T(8,128)(2,1)} %copy-done.6, bf16[8,144,256]{2,1,0:T(8,128)(2,1)} %copy-done, ...), custom_call_target="tpu_custom_call" | custom-call | flops 261881856 | bytes 186368 | tf_op jit(solution)/shard_map/memory/memory_attend/pallas_call | solution.py:448
  126.0 7.0 %collective-permute-done.16.refs_1_ = bf16[4,592,128]{2,1,0:T(8,128)(2,1)S(1)} collective-permute-done((bf16[4,592,128]{2,1,0:T(8,128)(2,1)}, bf16[4,592,128]{2,1,0:T(8,128)(2,1)S(1)}, u32[]{:S(2)}, u32[]{:S(2)}) %collective-permute-start.16) | collective-permute-done | bytes 606240 | tf_op jit(solution)/shard_map/memory/ppermute | solution.py:697
  133.0 2.3 %add_partials.1 = (bf16[592,128]{1,0:T(8,128)(2,1)}, bf16[592,128]{1,0:T(8,128)(2,1)}, bf16[592,128]{1,0:T(8,128)(2,1)}, bf16[592,128]{1,0:T(8,128)(2,1)}) custom-call(s32[1]{0:T(128)} %bitcast.x_ref, bf16[4,592,128]{2,1,0:T(8,128)(2,1)} %memory_attend.3.refs_0_, bf16[4,592,128]{2,1,0:T(8,128)(2,1)S(1)} %collective-permute-done.16.refs_1_), custom_call_target="tpu_custom_call" | custom-call | flops 75776 | bytes 151552 | tf_op jit(solution)/shard_map/memory/add_partials/pallas_call | solution.py:500
  135.3 2.3 %collective-permute-start.17 = (bf16[592,128]{1,0:T(8,128)(2,1)}, bf16[592,128]{1,0:T(8,128)(2,1)S(1)}, u32[]{:S(2)}, u32[]{:S(2)}) collective-permute-start(bf16[592,128]{1,0:T(8,128)(2,1)} %get-tuple-element.24), channel_id=1, source_target_pairs={{0,1},{1,2},{2,3},{3,0},{4,5},{5,6},{6,7},{7,4},{8,9},{9,10},{10,1... | collective-permute-start | bytes 454664 | tf_op jit(solution)/shard_map/memory/ppermute | solution.py:627
  137.6 2.1 %collective-permute-start.18 = (bf16[592,128]{1,0:T(8,128)(2,1)}, bf16[592,128]{1,0:T(8,128)(2,1)S(1)}, u32[]{:S(2)}, u32[]{:S(2)}) collective-permute-start(bf16[592,128]{1,0:T(8,128)(2,1)} %get-tuple-element.25), channel_id=1, source_target_pairs={{0,2},{1,3},{2,0},{3,1},{4,6},{5,7},{6,4},{7,5},{8,10},{9,11},{10,... | collective-permute-start | bytes 454664 | tf_op jit(solution)/shard_map/memory/ppermute | solution.py:627
  139.7 1.3 collective-permute-start.19
  141.0 0.0 all-to-all-done.3.time_hbm
  141.0 2.6 %collective-permute-done.17.memory_1 = bf16[592,128]{1,0:T(8,128)(2,1)S(1)} collective-permute-done((bf16[592,128]{1,0:T(8,128)(2,1)}, bf16[592,128]{1,0:T(8,128)(2,1)S(1)}, u32[]{:S(2)}, u32[]{:S(2)}) %collective-permute-start.17) | collective-permute-done | bytes 151584 | tf_op jit(solution)/shard_map/memory/ppermute | solution.py:627
  143.6 2.1 %collective-permute-done.18.memory_2 = bf16[592,128]{1,0:T(8,128)(2,1)S(1)} collective-permute-done((bf16[592,128]{1,0:T(8,128)(2,1)}, bf16[592,128]{1,0:T(8,128)(2,1)S(1)}, u32[]{:S(2)}, u32[]{:S(2)}) %collective-permute-start.18) | collective-permute-done | bytes 151584 | tf_op jit(solution)/shard_map/memory/ppermute | solution.py:627
  145.7 0.0 collective-permute-done.19.memory_3
  145.7 6.1 %leave.1 = bf16[576,2048]{1,0:T(8,128)(2,1)} custom-call(s32[1]{0:T(128)} %bitcast.x_ref, bf16[4,592,128]{2,1,0:T(8,128)(2,1)} %own_attend.1._.own_hbm, bf16[592,128]{1,0:T(8,128)(2,1)} %get-tuple-element.23.memory_0, bf16[592,128]{1,0:T(8,128)(2,1)S(1)} %collective-permute-done.17.memory_1, bf16[592,128]{1,0:T(8,128)(2,1)S(1)} %collective-permute-done.18.memory_2, ...), custom_call_target="tpu_custom_call" | custom-call | flops 150994944 | bytes 630784 | tf_op jit(solution)/shard_map/exit/leave/pallas_call | solution.py:571
  (18 shorter events, 0.1 us)
Async XLA Ops:
  0.0 6.6 %copy-start.4 = (s32[1,1,6,1]{2,3,1,0:T(1,128)S(1)}, s32[1,1,6,1]{2,3,1,0:T(1,128)}, u32[]{:S(2)}) copy-start(s32[1,1,6,1]{2,3,1,0:T(1,128)} %param.15) | copy-start | bytes 76
  0.0 6.6 %copy-start.5 = (s32[1,1,6]{2,1,0:T(1,128)S(1)}, s32[1,1,6]{2,1,0:T(1,128)}, u32[]{:S(2)}) copy-start(s32[1,1,6]{2,1,0:T(1,128)} %param.16) | copy-start | bytes 76
  0.0 6.6 %copy-start.3 = (f32[2,4]{1,0:T(2,128)S(1)}, f32[2,4]{1,0:T(2,128)}, u32[]{:S(2)}) copy-start(f32[2,4]{1,0:T(2,128)} %sharpness_ref.3) | copy-start | bytes 100
  2.2 14.6 %all-to-all-start = ((bf16[4,288,256]{2,1,0:T(8,128)(2,1)}), bf16[4,288,256]{2,1,0:T(8,128)(2,1)S(1)}, u32[]{:S(2)}, u32[]{:S(2)}) async-start(bf16[4,288,256]{2,1,0:T(8,128)(2,1)} %bitcast.22), calls=%async_computation | async-start | bytes 1179648 | tf_op jit(solution)/shard_map/store/all_to_all | solution.py:624
  18.5 14.3 %collective-permute-start.1 = (bf16[8,144,256]{2,1,0:T(8,128)(2,1)}, bf16[8,144,256]{2,1,0:T(8,128)(2,1)S(1)}, u32[]{:S(2)}, u32[]{:S(2)}) collective-permute-start(bf16[8,144,256]{2,1,0:T(8,128)(2,1)} %join_pieces.1.refs_0_), channel_id=1, source_target_pairs={{0,4},{4,0},{1,5},{5,1},{2,6},{6,2},{3,7},{7,3},{8,12},{12,8},{9,1... | collective-permute-start | bytes 1769480 | tf_op jit(solution)/shard_map/store/ppermute | solution.py:651
  20.5 24.0 %all-to-all-start.1 = ((bf16[4,592,128]{2,1,0:T(8,128)(2,1)}), bf16[4,592,128]{2,1,0:T(8,128)(2,1)S(1)}, u32[]{:S(2)}, u32[]{:S(2)}) async-start(bf16[4,592,128]{2,1,0:T(8,128)(2,1)} %bitcast.6), calls=%async_computation.1 | async-start | bytes 1212416 | tf_op jit(solution)/shard_map/queries/all_to_all | solution.py:624
  24.0 26.4 %collective-permute-start = (bf16[8,144,256]{2,1,0:T(8,128)(2,1)}, bf16[8,144,256]{2,1,0:T(8,128)(2,1)S(1)}, u32[]{:S(2)}, u32[]{:S(2)}) collective-permute-start(bf16[8,144,256]{2,1,0:T(8,128)(2,1)} %join_pieces.1.refs_0_), channel_id=1, source_target_pairs={{0,96},{32,0},{64,32},{96,64},{1,97},{33,1},{65,33},{97,65},{2,98}... | collective-permute-start | bytes 1769480 | tf_op jit(solution)/shard_map/store/ppermute | solution.py:649
  27.1 23.3 %collective-permute-start.2 = (bf16[8,144,256]{2,1,0:T(8,128)(2,1)}, bf16[8,144,256]{2,1,0:T(8,128)(2,1)}, u32[]{:S(2)}, u32[]{:S(2)}) collective-permute-start(bf16[8,144,256]{2,1,0:T(8,128)(2,1)} %join_pieces.1.refs_0_), channel_id=1, source_target_pairs={{0,32},{32,64},{64,96},{96,0},{1,33},{33,65},{65,97},{97,1},{2,34}... | collective-permute-start | bytes 1769480 | tf_op jit(solution)/shard_map/store/ppermute | solution.py:650
  32.9 21.1 %copy-start.6 = (bf16[8,144,256]{2,1,0:T(8,128)(2,1)}, bf16[8,144,256]{2,1,0:T(8,128)(2,1)S(1)}, u32[]{:S(2)}) copy-start(bf16[8,144,256]{2,1,0:T(8,128)(2,1)S(1)} %collective-permute-done.1.refs_1_) | copy-start | bytes 1769476
  32.9 21.1 %collective-permute-start.4 = (bf16[8,144,256]{2,1,0:T(8,128)(2,1)S(1)}, bf16[8,144,256]{2,1,0:T(8,128)(2,1)}, u32[]{:S(2)}, u32[]{:S(2)}) collective-permute-start(bf16[8,144,256]{2,1,0:T(8,128)(2,1)S(1)} %collective-permute-done.1.refs_1_), channel_id=1, source_target_pairs={{0,96},{32,0},{64,32},{96,64},{1,97},{33,1},{65,33},{97,65},{2,98}... | collective-permute-start | bytes 1769480 | tf_op jit(solution)/shard_map/store/ppermute | solution.py:653
  35.9 18.7 %collective-permute-start.5 = (bf16[8,144,256]{2,1,0:T(8,128)(2,1)S(1)}, bf16[8,144,256]{2,1,0:T(8,128)(2,1)}, u32[]{:S(2)}, u32[]{:S(2)}) collective-permute-start(bf16[8,144,256]{2,1,0:T(8,128)(2,1)S(1)} %collective-permute-done.1.refs_1_), channel_id=1, source_target_pairs={{0,32},{32,64},{64,96},{96,0},{1,33},{33,65},{65,97},{97,1},{2,34}... | collective-permute-start | bytes 1769480 | tf_op jit(solution)/shard_map/store/ppermute | solution.py:654
  35.9 19.1 %collective-permute-start.8 = (bf16[8,144,256]{2,1,0:T(8,128)(2,1)}, bf16[8,144,256]{2,1,0:T(8,128)(2,1)}, u32[]{:S(2)}, u32[]{:S(2)}) collective-permute-start(bf16[8,144,256]{2,1,0:T(8,128)(2,1)} %join_pieces.1.refs_0_), channel_id=1, source_target_pairs={{0,16},{16,0},{1,17},{17,1},{2,18},{18,2},{3,19},{19,3},{4,20},{20... | collective-permute-start | bytes 1769480 | tf_op jit(solution)/shard_map/store/ppermute | solution.py:681
  44.5 53.5 %all-to-all-start.2 = ((bf16[16,3,144,128]{3,2,1,0:T(8,128)(2,1)}), bf16[16,3,144,128]{3,2,1,0:T(8,128)(2,1)S(1)}, u32[]{:S(2)}, u32[]{:S(2)}) async-start(bf16[16,3,144,128]{3,2,1,0:T(8,128)(2,1)} %bitcast.21), calls=%async_computation.2 | async-start | bytes 3538944 | tf_op jit(solution)/shard_map/temporal/all_to_all | solution.py:624
  50.4 46.8 %copy-start = (bf16[8,144,256]{2,1,0:T(8,128)(2,1)}, bf16[8,144,256]{2,1,0:T(8,128)(2,1)S(1)}, u32[]{:S(2)}) copy-start(bf16[8,144,256]{2,1,0:T(8,128)(2,1)S(1)} %collective-permute-done.refs_1_.refs_2_) | copy-start | bytes 1769476
  50.4 36.4 %collective-permute-start.3 = (bf16[4,592,128]{2,1,0:T(8,128)(2,1)S(1)}, bf16[4,592,128]{2,1,0:T(8,128)(2,1)S(1)}, u32[]{:S(2)}, u32[]{:S(2)}) collective-permute-start(bf16[4,592,128]{2,1,0:T(8,128)(2,1)S(1)} %all-to-all-done.1.query_hbm), channel_id=1, source_target_pairs={{0,8},{8,0},{1,9},{9,1},{2,10},{10,2},{3,11},{11,3},{4,12},{12,4},... | collective-permute-start | bytes 1818632 | tf_op jit(solution)/shard_map/queries/ppermute | solution.py:663
  53.9 3.9 %collective-permute-start.9 = (bf16[8,144,256]{2,1,0:T(8,128)(2,1)S(1)}, bf16[8,144,256]{2,1,0:T(8,128)(2,1)S(1)}, u32[]{:S(2)}, u32[]{:S(2)}) collective-permute-start(bf16[8,144,256]{2,1,0:T(8,128)(2,1)S(1)} %collective-permute-done.1.refs_1_), channel_id=1, source_target_pairs={{0,16},{16,0},{1,17},{17,1},{2,18},{18,2},{3,19},{19,3},{4,20},{20... | collective-permute-start | bytes 1769480 | tf_op jit(solution)/shard_map/store/ppermute | solution.py:681
  53.9 3.9 %collective-permute-start.10 = (bf16[8,144,256]{2,1,0:T(8,128)(2,1)S(1)}, bf16[8,144,256]{2,1,0:T(8,128)(2,1)S(1)}, u32[]{:S(2)}, u32[]{:S(2)}) collective-permute-start(bf16[8,144,256]{2,1,0:T(8,128)(2,1)S(1)} %collective-permute-done.refs_1_.refs_2_), channel_id=1, source_target_pairs={{0,16},{16,0},{1,17},{17,1},{2,18},{18,2},{3,19},{19,3},{4,20},{20... | collective-permute-start | bytes 1769480 | tf_op jit(solution)/shard_map/store/ppermute | solution.py:681
  54.6 33.0 %collective-permute-start.6 = (bf16[8,144,256]{2,1,0:T(8,128)(2,1)}, bf16[8,144,256]{2,1,0:T(8,128)(2,1)}, u32[]{:S(2)}, u32[]{:S(2)}) collective-permute-start(bf16[8,144,256]{2,1,0:T(8,128)(2,1)} %collective-permute-done.2.refs_6_), channel_id=1, source_target_pairs={{0,32},{32,64},{64,96},{96,0},{1,33},{33,65},{65,97},{97,1},{2,34}... | collective-permute-start | bytes 1769480 | tf_op jit(solution)/shard_map/store/ppermute | solution.py:678
  55.0 33.2 %collective-permute-start.7 = (bf16[8,144,256]{2,1,0:T(8,128)(2,1)}, bf16[8,144,256]{2,1,0:T(8,128)(2,1)}, u32[]{:S(2)}, u32[]{:S(2)}) collective-permute-start(bf16[8,144,256]{2,1,0:T(8,128)(2,1)} %collective-permute-done.4.refs_3_), channel_id=1, source_target_pairs={{0,96},{32,0},{64,32},{96,64},{1,97},{33,1},{65,33},{97,65},{2,98}... | collective-permute-start | bytes 1769480 | tf_op jit(solution)/shard_map/store/ppermute | solution.py:679
  57.8 29.8 %copy-start.7 = (bf16[8,144,256]{2,1,0:T(8,128)(2,1)}, bf16[8,144,256]{2,1,0:T(8,128)(2,1)S(1)}, u32[]{:S(2)}) copy-start(bf16[8,144,256]{2,1,0:T(8,128)(2,1)S(1)} %collective-permute-done.9.refs_9_) | copy-start | bytes 1769476
  57.8 42.6 %collective-permute-start.11 = (bf16[8,144,256]{2,1,0:T(8,128)(2,1)}, bf16[8,144,256]{2,1,0:T(8,128)(2,1)}, u32[]{:S(2)}, u32[]{:S(2)}) collective-permute-start(bf16[8,144,256]{2,1,0:T(8,128)(2,1)} %collective-permute-done.4.refs_3_), channel_id=1, source_target_pairs={{0,16},{16,0},{1,17},{17,1},{2,18},{18,2},{3,19},{19,3},{4,20},{20... | collective-permute-start | bytes 1769480 | tf_op jit(solution)/shard_map/store/ppermute | solution.py:681
  57.8 29.8 %copy-start.8 = (bf16[8,144,256]{2,1,0:T(8,128)(2,1)}, bf16[8,144,256]{2,1,0:T(8,128)(2,1)S(1)}, u32[]{:S(2)}) copy-start(bf16[8,144,256]{2,1,0:T(8,128)(2,1)S(1)} %collective-permute-done.10.refs_10_) | copy-start | bytes 1769476
  57.8 42.6 %collective-permute-start.14 = (bf16[8,144,256]{2,1,0:T(8,128)(2,1)}, bf16[8,144,256]{2,1,0:T(8,128)(2,1)}, u32[]{:S(2)}, u32[]{:S(2)}) collective-permute-start(bf16[8,144,256]{2,1,0:T(8,128)(2,1)} %collective-permute-done.2.refs_6_), channel_id=1, source_target_pairs={{0,16},{16,0},{1,17},{17,1},{2,18},{18,2},{3,19},{19,3},{4,20},{20... | collective-permute-start | bytes 1769480 | tf_op jit(solution)/shard_map/store/ppermute | solution.py:681
  86.8 0.8 copy-start.1
  87.6 12.9 %collective-permute-start.15 = (bf16[8,144,256]{2,1,0:T(8,128)(2,1)}, bf16[8,144,256]{2,1,0:T(8,128)(2,1)}, u32[]{:S(2)}, u32[]{:S(2)}) collective-permute-start(bf16[8,144,256]{2,1,0:T(8,128)(2,1)} %collective-permute-done.5.refs_7_), channel_id=1, source_target_pairs={{0,16},{16,0},{1,17},{17,1},{2,18},{18,2},{3,19},{19,3},{4,20},{20... | collective-permute-start | bytes 1769480 | tf_op jit(solution)/shard_map/store/ppermute | solution.py:681
  87.6 12.9 %collective-permute-start.12 = (bf16[8,144,256]{2,1,0:T(8,128)(2,1)}, bf16[8,144,256]{2,1,0:T(8,128)(2,1)}, u32[]{:S(2)}, u32[]{:S(2)}) collective-permute-start(bf16[8,144,256]{2,1,0:T(8,128)(2,1)} %collective-permute-done.6.refs_4_), channel_id=1, source_target_pairs={{0,16},{16,0},{1,17},{17,1},{2,18},{18,2},{3,19},{19,3},{4,20},{20... | collective-permute-start | bytes 1769480 | tf_op jit(solution)/shard_map/store/ppermute | solution.py:681
  88.2 12.3 %collective-permute-start.13 = (bf16[8,144,256]{2,1,0:T(8,128)(2,1)}, bf16[8,144,256]{2,1,0:T(8,128)(2,1)}, u32[]{:S(2)}, u32[]{:S(2)}) collective-permute-start(bf16[8,144,256]{2,1,0:T(8,128)(2,1)} %collective-permute-done.7.refs_5_), channel_id=1, source_target_pairs={{0,16},{16,0},{1,17},{17,1},{2,18},{18,2},{3,19},{19,3},{4,20},{20... | collective-permute-start | bytes 1769480 | tf_op jit(solution)/shard_map/store/ppermute | solution.py:681
  100.5 1.1 copy-start.2
  109.8 23.1 %collective-permute-start.16 = (bf16[4,592,128]{2,1,0:T(8,128)(2,1)}, bf16[4,592,128]{2,1,0:T(8,128)(2,1)S(1)}, u32[]{:S(2)}, u32[]{:S(2)}) collective-permute-start(bf16[4,592,128]{2,1,0:T(8,128)(2,1)} %memory_attend.2.refs_16_), channel_id=1, source_target_pairs={{0,8},{8,0},{1,9},{9,1},{2,10},{10,2},{3,11},{11,3},{4,12},{12,4},... | collective-permute-start | bytes 1818632 | tf_op jit(solution)/shard_map/memory/ppermute | solution.py:697
  110.3 30.7 %all-to-all-start.3 = ((bf16[16,144,128]{2,1,0:T(8,128)(2,1)}), bf16[16,144,128]{2,1,0:T(8,128)(2,1)S(1)}, u32[]{:S(2)}, u32[]{:S(2)}) async-start(bf16[16,144,128]{2,1,0:T(8,128)(2,1)} %temporal_attend.1.refs_16_), calls=%async_computation.3 | async-start | bytes 1179648 | tf_op jit(solution)/shard_map/temporal/all_to_all | solution.py:624
  135.3 8.3 %collective-permute-start.17 = (bf16[592,128]{1,0:T(8,128)(2,1)}, bf16[592,128]{1,0:T(8,128)(2,1)S(1)}, u32[]{:S(2)}, u32[]{:S(2)}) collective-permute-start(bf16[592,128]{1,0:T(8,128)(2,1)} %get-tuple-element.24), channel_id=1, source_target_pairs={{0,1},{1,2},{2,3},{3,0},{4,5},{5,6},{6,7},{7,4},{8,9},{9,10},{10,1... | collective-permute-start | bytes 454664 | tf_op jit(solution)/shard_map/memory/ppermute | solution.py:627
  137.6 8.0 %collective-permute-start.18 = (bf16[592,128]{1,0:T(8,128)(2,1)}, bf16[592,128]{1,0:T(8,128)(2,1)S(1)}, u32[]{:S(2)}, u32[]{:S(2)}) collective-permute-start(bf16[592,128]{1,0:T(8,128)(2,1)} %get-tuple-element.25), channel_id=1, source_target_pairs={{0,2},{1,3},{2,0},{3,1},{4,6},{5,7},{6,4},{7,5},{8,10},{9,11},{10,... | collective-permute-start | bytes 454664 | tf_op jit(solution)/shard_map/memory/ppermute | solution.py:627
  139.7 6.0 %collective-permute-start.19 = (bf16[592,128]{1,0:T(8,128)(2,1)}, bf16[592,128]{1,0:T(8,128)(2,1)S(1)}, u32[]{:S(2)}, u32[]{:S(2)}) collective-permute-start(bf16[592,128]{1,0:T(8,128)(2,1)} %get-tuple-element.26), channel_id=1, source_target_pairs={{0,3},{1,0},{2,1},{3,2},{4,7},{5,4},{6,5},{7,6},{8,11},{9,8},{10,9... | collective-permute-start | bytes 454664 | tf_op jit(solution)/shard_map/memory/ppermute | solution.py:627

commit v18 on v15

--- a/solution.py
+++ b/solution.py
@@ -464,7 +464,7 @@
             16 * frames * rows * TOPM * part * C,
             4 * frames * rows * C + 2 * frames * TOPM * part * width,
         ),
-    )(index, query, *blocks, in_hbm(after))
+    )(index, in_hbm(query), *blocks, in_hbm(after))
 
 
 def add_partials_kernel(count, x_ref, *refs):
@@ -514,27 +514,87 @@
     )(x, *parts)
 
 
+STEPS = 4
+
+
+def leave_time_kernel(
+    time_hbm, weight_hbm, _, out_hbm,
+    time_ref, combined_ref, weight_ref, out_ref, time_sem, weight_sem, store_sem,
+):
+    quarters = time_ref.shape[0] // G
+    rows = time_ref.shape[1]
+    depth, width = weight_ref.shape[1:]
+    time_load = copy(time_hbm, time_ref, time_sem)
+    time_load.start()
+    loads, stores = [], []
+    for i in range(STEPS):
+        at = pl.ds(i * width, width)
+        loads.append(
+            copy(weight_hbm.at[pl.ds(HW, depth), at], weight_ref.at[i], weight_sem.at[i])
+        )
+        stores.append(copy(out_ref.at[i], out_hbm.at[i], store_sem.at[i]))
+        loads[i].start()
+    time_load.wait()
+    for h in range(G):
+        for z in range(quarters):
+            combined_ref[z * rows : (z + 1) * rows, h * C : (h + 1) * C] = time_ref[z * G + h]
+    for i in range(STEPS):
+        loads[i].wait()
+        out_ref[i] = dot(combined_ref[...], weight_ref[i])
+        stores[i].start()
+    for store in stores:
+        store.wait()
+
+
+def leave_time(time, weight, after):
+    patches = time.shape[0] // G * time.shape[1]
+    depth, width = weight.shape
+    step = width // STEPS
+    shape = (STEPS, patches, step)
+    return pl.pallas_call(
+        leave_time_kernel,
+        in_specs=[ANY, HBM, ANY],
+        out_specs=HBM,
+        out_shape=hbm_out(shape, F32),
+        scratch_shapes=[
+            pltpu.VMEM(time.shape, BF),
+            pltpu.VMEM((patches, depth - HW), BF),
+            pltpu.VMEM((STEPS, depth - HW, step), BF),
+            pltpu.VMEM(shape, F32),
+            DMA,
+            DMA((STEPS,)),
+            DMA((STEPS,)),
+        ],
+        compiler_params=params(),
+        name="leave_time",
+        cost_estimate=cost(
+            patches * depth * width, depth * width + 4 * patches * width + 2 * time.size
+        ),
+    )(time, in_hbm(weight), in_hbm(after))
+
+
 def leave_kernel(
-    x_ref, own_hbm, memory_0, memory_1, memory_2, memory_3, time_hbm, weight_hbm, out_hbm,
-    own_ref, memory_ref, time_ref, combined_ref, weight_ref, out_ref,
-    own_sem, memory_sem, time_sem, weight_sem, store_sem,
+    x_ref, own_hbm, memory_0, memory_1, memory_2, memory_3, partial_hbm, weight_hbm, out_hbm,
+    own_ref, memory_ref, combined_ref, partial_ref, weight_ref, out_ref,
+    own_sem, memory_sem, partial_sem, weight_sem, store_sem,
 ):
     patches = own_ref.shape[1] - PAD
-    quarters = time_ref.shape[0] // G
-    rows = time_ref.shape[1]
-    steps, _, width = weight_ref.shape
+    width = weight_ref.shape[2]
     heads = [lax.rem(x_ref[0] + G - j, G) for j in range(G)]
     memories = (memory_0, memory_1, memory_2, memory_3)
     own_loads = [copy(own_hbm.at[heads[j]], own_ref.at[j], own_sem.at[j]) for j in range(G)]
     memory_loads = [copy(memories[j], memory_ref.at[j], memory_sem.at[j]) for j in range(G)]
-    time_load = copy(time_hbm, time_ref, time_sem)
-    loads, stores = [], []
-    for i in range(steps):
+    loads, partial_loads, stores = [], [], []
+    for i in range(STEPS):
         at = pl.ds(i * width, width)
-        loads.append(copy(weight_hbm.at[:, at], weight_ref.at[i], weight_sem.at[i]))
+        loads.append(copy(weight_hbm.at[pl.ds(0, HW), at], weight_ref.at[i], weight_sem.at[i]))
+        partial_loads.append(copy(partial_hbm.at[i], partial_ref.at[i], partial_sem.at[i]))
         stores.append(copy(out_ref.at[i], out_hbm.at[:, at], store_sem.at[i]))
-    for load in own_loads + memory_loads + [time_load] + loads:
+    for load in own_loads + memory_loads:
         load.start()
+    for i in range(STEPS):
+        loads[i].start()
+        partial_loads[i].start()
     row = lax.broadcasted_iota(jnp.int32, (LINE, C), 0)
     column = lax.broadcasted_iota(jnp.int32, (LINE, C), 1)
     for h in range(G):
@@ -549,50 +609,43 @@
             total = jnp.sum(jnp.where(row == column, line, 0.0), axis=1, keepdims=True)
             top = own_ref[h, at, :].astype(F32) + memory_ref[h, at, :].astype(F32)
             combined_ref[at, column_at] = (top / total).astype(BF)
-    time_load.wait()
-    for h in range(G):
-        for z in range(quarters):
-            combined_ref[z * rows : (z + 1) * rows, HW + h * C : HW + (h + 1) * C] = time_ref[
-                z * G + h
-            ]
-    for i in range(steps):
+    for i in range(STEPS):
         loads[i].wait()
-        out_ref[i] = dot(combined_ref[...], weight_ref[i]).astype(BF)
+        partial_loads[i].wait()
+        out_ref[i] = (dot(combined_ref[...], weight_ref[i]) + partial_ref[i]).astype(BF)
         stores[i].start()
     for store in stores:
         store.wait()
 
 
-def leave(x, own, memory, time, weight):
+def leave(x, own, memory, partial, weight):
     patches = own.shape[1] - PAD
-    depth, width = weight.shape
-    steps = 4
-    step = width // steps
+    width = weight.shape[1]
+    step = width // STEPS
     return pl.pallas_call(
         leave_kernel,
-        in_specs=[SCALARS, HBM] + [ANY] * (G + 1) + [HBM],
+        in_specs=[SCALARS, HBM] + [ANY] * G + [HBM, HBM],
         out_specs=HBM,
         out_shape=hbm_out((patches, width)),
         scratch_shapes=[
             pltpu.VMEM(own.shape, BF),
             pltpu.VMEM(own.shape, BF),
-            pltpu.VMEM(time.shape, BF),
-            pltpu.VMEM((patches, depth), BF),
-            pltpu.VMEM((steps, depth, step), BF),
-            pltpu.VMEM((steps, patches, step), BF),
+            pltpu.VMEM((patches, HW), BF),
+            pltpu.VMEM(partial.shape, F32),
+            pltpu.VMEM((STEPS, HW, step), BF),
+            pltpu.VMEM((STEPS, patches, step), BF),
             DMA((G,)),
             DMA((G,)),
-            DMA,
-            DMA((steps,)),
-            DMA((steps,)),
+            DMA((STEPS,)),
+            DMA((STEPS,)),
+            DMA((STEPS,)),
         ],
         compiler_params=params(),
         name="leave",
         cost_estimate=cost(
-            2 * patches * depth * width,
-            2 * depth * width + 2 * patches * width + 6 * patches * depth,
+            2 * patches * HW * width, 2 * HW * width + 6 * patches * width + 4 * patches * HW
         ),
-    )(x, in_hbm(own), *memory, time, in_hbm(weight))
+    )(x, in_hbm(own), *memory, in_hbm(partial), in_hbm(weight))
 
 
 def on_device(
@@ -701,7 +754,8 @@
         memory = swap_apart(add_partials(x, [in_hbm(sum_here), from_beside]))
 
     with jax.named_scope("exit"):
-        attended = leave(x, own, memory, time, exit_projection_matrix)
+        partial = leave_time(time, exit_projection_matrix, after=memory[0])
+        attended = leave(x, own, memory, partial, exit_projection_matrix)
     return attended.reshape(1, 1, patches, depth)
 
 

time: 133 us -> 130 us (0.977)
  waiting for transfers between devices: 30 us -> 26.1 us
  Pallas kernels: 52.4 us -> 55.3 us
    ppermute x3, waiting for transfers between devices: 4.29 us -> 0.17 us  [swap_apart(): lax.ppermute(blocks[j], 'x', turn(j))]
    pallas_call x1 -> x2, Pallas kernels: 6.11 us -> 9.28 us  [the longest x1 5.16 us: leave(): pl.pallas_call(leave_kernel, in_specs=[SCALARS, HBM] + [ANY] * G + [HBM,...]
  transfers between devices with their start and end apart: 24 -> 24, of which waited for: 10 -> 9; matrix products, arithmetic and copies ran while one was open for 1% -> 1% of each run, Pallas kernels for 33% -> 37%
where the time goes in v18:
time: 130 us
  Pallas kernels  55.3 us (43%)
  starting transfers between devices  44.1 us (34%)
  waiting for transfers between devices  26.1 us (20%)
  local copies, waits for them, and re-layouts  3.26 us (3%)
    all_to_all x4, starting transfers between devices, swap(): return lax.all_to_all(blocks, axes, split_axis=0, concat_axis=0, tiled=True)  18.5 us
    pallas_call x2, Pallas kernels, memory_attend(): pl.pallas_call(functools.partial(memory_attend_kernel, count, first), in_...  16.3 us
    ppermute x1, waiting for transfers between devices, on_device(): far = lax.ppermute(below, 'y', turn(1))  12.9 us
    pallas_call x1, Pallas kernels, temporal_entry(): pl.pallas_call(functools.partial(temporal_entry_kernel, quarters), in_spe...  8.54 us
    pallas_call x1, Pallas kernels, own_attend(): pl.pallas_call(own_attend_kernel, in_specs=[HBM, HBM, HBM] + [ANY] * len(...  8.08 us
    ppermute x3, starting transfers between devices, swap_apart(): lax.ppermute(blocks[j], 'x', turn(j))  6.62 us
    pallas_call x1, Pallas kernels, modulate(): pl.pallas_call(functools.partial(modulate_kernel, held), in_specs=[HBM, H...  5.57 us
    pallas_call x1, Pallas kernels, leave(): pl.pallas_call(leave_kernel, in_specs=[SCALARS, HBM] + [ANY] * G + [HBM,...  5.16 us
  transfers between devices with their start and end apart: 24, of which 9 were waited for; matrix products, arithmetic and copies ran while one was open for 1% of the time, Pallas kernels for 37%

profile of v18, /device:TPU:0, one launch (start us, length us, event | category | flops | bytes accessed | tf_op | source)
XLA Modules:
  0.0 129.8 jit_solution(12478778620577706142)
XLA Ops:
  0.0 1.2 copy.12
  1.2 1.0 split_store.1._
  2.2 4.4 %all-to-all-start = ((bf16[4,288,256]{2,1,0:T(8,128)(2,1)}), bf16[4,288,256]{2,1,0:T(8,128)(2,1)S(1)}, u32[]{:S(2)}, u32[]{:S(2)}) async-start(bf16[4,288,256]{2,1,0:T(8,128)(2,1)} %bitcast.22), calls=%async_computation | async-start | bytes 1179648 | tf_op jit(solution)/shard_map/store/all_to_all | solution.py:677
  6.6 5.6 %modulate.1 = (bf16[576,2048]{1,0:T(8,128)(2,1)}, bf16[1,4,592,128]{3,2,1,0:T(8,128)(2,1)}) custom-call(bf16[576,2048]{1,0:T(8,128)(2,1)} %bitcast.23, f32[2,2048]{1,0:T(2,128)} %bitcast.25, bf16[2048,3072]{1,0:T(8,128)(2,1)} %weight_hbm.7, f32[2,4]{1,0:T(2,128)S(1)} %copy-done.1, s32[6]{0:T(128)S(1)} %bitcast.19, s32[6]{0:T(128)S(1)} %bitcast.20, ...), custom_call_target="tpu_custom_call" | custom-call | flops 75497472 | bytes 462848 | tf_op jit(solution)/shard_map/queries/modulate/pallas_call | solution.py:185
  12.2 4.6 %all-to-all-done.in_hbm = bf16[4,288,256]{2,1,0:T(8,128)(2,1)S(1)} async-done(((bf16[4,288,256]{2,1,0:T(8,128)(2,1)}), bf16[4,288,256]{2,1,0:T(8,128)(2,1)S(1)}, u32[]{:S(2)}, u32[]{:S(2)}) %all-to-all-start) | async-done | bytes 589856 | tf_op jit(solution)/shard_map/store/all_to_all | solution.py:677
  16.8 1.7 %join_pieces.1.refs_0_ = bf16[8,144,256]{2,1,0:T(8,128)(2,1)} custom-call(bf16[4,288,256]{2,1,0:T(8,128)(2,1)S(1)} %all-to-all-done.in_hbm, bf16[576,2048]{1,0:T(8,128)(2,1)} %get-tuple-element.16._.hidden_hbm), custom_call_target="tpu_custom_call" | custom-call | flops 18432 | bytes 73728 | tf_op jit(solution)/shard_map/store/join_pieces/pallas_call | solution.py:109
  18.5 2.0 %collective-permute-start.1 = (bf16[8,144,256]{2,1,0:T(8,128)(2,1)}, bf16[8,144,256]{2,1,0:T(8,128)(2,1)}, u32[]{:S(2)}, u32[]{:S(2)}) collective-permute-start(bf16[8,144,256]{2,1,0:T(8,128)(2,1)} %join_pieces.1.refs_0_), channel_id=1, source_target_pairs={{0,4},{4,0},{1,5},{5,1},{2,6},{6,2},{3,7},{7,3},{8,12},{12,8},{9,1... | collective-permute-start | bytes 1769480 | tf_op jit(solution)/shard_map/store/ppermute | solution.py:704
  20.5 3.0 %collective-permute-start = (bf16[8,144,256]{2,1,0:T(8,128)(2,1)}, bf16[8,144,256]{2,1,0:T(8,128)(2,1)S(1)}, u32[]{:S(2)}, u32[]{:S(2)}) collective-permute-start(bf16[8,144,256]{2,1,0:T(8,128)(2,1)} %join_pieces.1.refs_0_), channel_id=1, source_target_pairs={{0,96},{32,0},{64,32},{96,64},{1,97},{33,1},{65,33},{97,65},{2,98}... | collective-permute-start | bytes 1769480 | tf_op jit(solution)/shard_map/store/ppermute | solution.py:702
  23.5 0.0 collective-permute-start.2
  23.5 3.5 %all-to-all-start.1 = ((bf16[4,592,128]{2,1,0:T(8,128)(2,1)}), bf16[4,592,128]{2,1,0:T(8,128)(2,1)S(1)}, u32[]{:S(2)}, u32[]{:S(2)}) async-start(bf16[4,592,128]{2,1,0:T(8,128)(2,1)} %bitcast.6), calls=%async_computation.1 | async-start | bytes 1212416 | tf_op jit(solution)/shard_map/queries/all_to_all | solution.py:677
  27.0 8.5 %temporal_entry.1.refs_0_ = bf16[4,4,3,144,128]{4,3,2,1,0:T(8,128)(2,1)} custom-call(bf16[576,2048]{1,0:T(8,128)(2,1)} %get-tuple-element.16._.hidden_hbm, bf16[2048,3072]{1,0:T(8,128)(2,1)} %weight_hbm.7, f32[2,4]{1,0:T(2,128)S(1)} %copy-done.1, bf16[8,144,256]{2,1,0:T(8,128)(2,1)} %join_pieces.1.refs_0_), custom_call_target="tpu_custom_call" | custom-call | flops 226492416 | bytes 651264 | tf_op jit(solution)/shard_map/temporal/temporal_entry/pallas_call | solution.py:250
  35.6 0.3 all-to-all-done.1.query_hbm
  35.9 0.0 collective-permute-done.1.refs_1_
  35.9 0.0 collective-permute-done.refs_1_.refs_2_
  35.9 2.4 %collective-permute-done.2.refs_6_ = bf16[8,144,256]{2,1,0:T(8,128)(2,1)S(1)} collective-permute-done((bf16[8,144,256]{2,1,0:T(8,128)(2,1)}, bf16[8,144,256]{2,1,0:T(8,128)(2,1)S(1)}, u32[]{:S(2)}, u32[]{:S(2)}) %collective-permute-start.2) | collective-permute-done | bytes 589856 | tf_op jit(solution)/shard_map/store/ppermute | solution.py:703
  38.3 3.6 %collective-permute-start.3 = (bf16[4,592,128]{2,1,0:T(8,128)(2,1)S(1)}, bf16[4,592,128]{2,1,0:T(8,128)(2,1)S(1)}, u32[]{:S(2)}, u32[]{:S(2)}) collective-permute-start(bf16[4,592,128]{2,1,0:T(8,128)(2,1)S(1)} %all-to-all-done.1.query_hbm), channel_id=1, source_target_pairs={{0,8},{8,0},{1,9},{9,1},{2,10},{10,2},{3,11},{11,3},{4,12},{12,4},... | collective-permute-start | bytes 1818632 | tf_op jit(solution)/shard_map/queries/ppermute | solution.py:716
  41.8 0.7 collective-permute-start.4
  42.5 1.3 %collective-permute-start.5 = (bf16[8,144,256]{2,1,0:T(8,128)(2,1)}, bf16[8,144,256]{2,1,0:T(8,128)(2,1)}, u32[]{:S(2)}, u32[]{:S(2)}) collective-permute-start(bf16[8,144,256]{2,1,0:T(8,128)(2,1)} %collective-permute-done.1.refs_1_), channel_id=1, source_target_pairs={{0,32},{32,64},{64,96},{96,0},{1,33},{33,65},{65,97},{97,1},{2,34}... | collective-permute-start | bytes 1769480 | tf_op jit(solution)/shard_map/store/ppermute | solution.py:707
  43.9 8.1 %own_attend.1.refs_16_.own_hbm = bf16[4,592,128]{2,1,0:T(8,128)(2,1)} custom-call(bf16[576,2048]{1,0:T(8,128)(2,1)} %get-tuple-element.16._.hidden_hbm, bf16[2048,3072]{1,0:T(8,128)(2,1)} %weight_hbm.7, bf16[1,4,592,128]{3,2,1,0:T(8,128)(2,1)} %get-tuple-element.17.query_hbm, bf16[4,4,3,144,128]{4,3,2,1,0:T(8,128)(2,1)} %temporal_entry.1.refs_0_, ...), custom_call_target="tpu_custom_call" | custom-call | flops 214695936 | bytes 593920 | tf_op jit(solution)/shard_map/own/own_attend/pallas_call | solution.py:380
  52.0 0.9 collective-permute-done.3.query_hbm
  52.8 0.8 copy-done.11
  53.7 5.6 %all-to-all-start.2 = ((bf16[16,3,144,128]{3,2,1,0:T(8,128)(2,1)}), bf16[16,3,144,128]{3,2,1,0:T(8,128)(2,1)S(1)}, u32[]{:S(2)}, u32[]{:S(2)}) async-start(bf16[16,3,144,128]{3,2,1,0:T(8,128)(2,1)} %bitcast.21), calls=%async_computation.2 | async-start | bytes 3538944 | tf_op jit(solution)/shard_map/temporal/all_to_all | solution.py:677
  59.3 0.1 collective-permute-start.8
  59.4 0.5 collective-permute-start.9
  59.9 0.1 collective-permute-start.10
  60.0 0.0 collective-permute-done.4.refs_3_
  60.0 0.0 collective-permute-done.5.refs_7_
  60.0 0.3 collective-permute-start.6
  60.3 2.9 %collective-permute-start.7 = (bf16[8,144,256]{2,1,0:T(8,128)(2,1)}, bf16[8,144,256]{2,1,0:T(8,128)(2,1)}, u32[]{:S(2)}, u32[]{:S(2)}) collective-permute-start(bf16[8,144,256]{2,1,0:T(8,128)(2,1)} %collective-permute-done.4.refs_3_), channel_id=1, source_target_pairs={{0,96},{32,0},{64,32},{96,64},{1,97},{33,1},{65,33},{97,65},{2,98}... | collective-permute-start | bytes 1769480 | tf_op jit(solution)/shard_map/store/ppermute | solution.py:732
  63.3 0.0 collective-permute-done.8.refs_8_
  63.3 0.0 collective-permute-start.11
  63.3 0.0 collective-permute-done.9.refs_9_
  63.3 0.5 collective-permute-start.14
  63.8 0.0 collective-permute-done.10.refs_10_
  63.8 0.3 copy-done.7
  64.1 0.0 collective-permute-start.15
  64.1 0.2 copy-done.8
  64.3 12.9 %collective-permute-done.6.refs_4_ = bf16[8,144,256]{2,1,0:T(8,128)(2,1)} collective-permute-done((bf16[8,144,256]{2,1,0:T(8,128)(2,1)}, bf16[8,144,256]{2,1,0:T(8,128)(2,1)}, u32[]{:S(2)}, u32[]{:S(2)}) %collective-permute-start.6) | collective-permute-done | bytes 589856 | tf_op jit(solution)/shard_map/store/ppermute | solution.py:731
  77.2 0.0 collective-permute-start.12
  77.2 0.0 collective-permute-done.7.refs_5_
  77.2 0.5 collective-permute-start.13
  77.7 0.7 slice.8
  78.5 0.0 collective-permute-done.11.refs_11_
  78.5 0.0 collective-permute-done.14.refs_14_
  78.5 0.0 collective-permute-done.15.refs_15_
  78.5 1.0 collective-permute-done.12.refs_12_
  79.6 0.8 collective-permute-done.13.refs_13_
  80.4 8.1 %memory_attend.2._ = bf16[4,592,128]{2,1,0:T(8,128)(2,1)} custom-call(s32[8,6]{1,0:T(8,128)S(1)} %fusion.10.index_ref, bf16[4,592,128]{2,1,0:T(8,128)(2,1)} %copy-done.11, bf16[8,144,256]{2,1,0:T(8,128)(2,1)} %join_pieces.1.refs_0_, bf16[8,144,256]{2,1,0:T(8,128)(2,1)} %collective-permute-done.1.refs_1_, bf16[8,144,256]{2,1,0:T(8,128)(2,1)} %copy-done, ...), custom_call_target="tpu_custom_call" | custom-call | flops 261881856 | bytes 186368 | tf_op jit(solution)/shard_map/memory/memory_attend/pallas_call | solution.py:448
  88.6 3.5 %collective-permute-start.16 = (bf16[4,592,128]{2,1,0:T(8,128)(2,1)}, bf16[4,592,128]{2,1,0:T(8,128)(2,1)S(1)}, u32[]{:S(2)}, u32[]{:S(2)}) collective-permute-start(bf16[4,592,128]{2,1,0:T(8,128)(2,1)} %memory_attend.2._), channel_id=1, source_target_pairs={{0,8},{8,0},{1,9},{9,1},{2,10},{10,2},{3,11},{11,3},{4,12},{12,4},... | collective-permute-start | bytes 1818632 | tf_op jit(solution)/shard_map/memory/ppermute | solution.py:746
  92.7 0.0 all-to-all-done.2.in_hbm_ref
  92.7 2.4 %temporal_attend.1.refs_16_ = bf16[16,144,128]{2,1,0:T(8,128)(2,1)} custom-call(s32[1]{0:T(128)S(6)} %copy.17.length_ref, bf16[16,3,144,128]{3,2,1,0:T(8,128)(2,1)S(1)} %all-to-all-done.2.in_hbm_ref, bf16[4,592,128]{2,1,0:T(8,128)(2,1)} %memory_attend.2._), custom_call_target="tpu_custom_call" | custom-call | flops 18874368 | bytes 147456 | tf_op jit(solution)/shard_map/temporal/temporal_attend/pallas_call | solution.py:300
  95.2 5.0 %all-to-all-start.3 = ((bf16[16,144,128]{2,1,0:T(8,128)(2,1)}), bf16[16,144,128]{2,1,0:T(8,128)(2,1)S(1)}, u32[]{:S(2)}, u32[]{:S(2)}) async-start(bf16[16,144,128]{2,1,0:T(8,128)(2,1)} %temporal_attend.1.refs_16_), calls=%async_computation.3 | async-start | bytes 1179648 | tf_op jit(solution)/shard_map/temporal/all_to_all | solution.py:677
  100.2 8.2 %memory_attend.3.refs_0_ = bf16[4,592,128]{2,1,0:T(8,128)(2,1)} custom-call(s32[8,6]{1,0:T(8,128)S(1)} %fusion.10.index_ref, bf16[4,592,128]{2,1,0:T(8,128)(2,1)} %copy-done.5, bf16[8,144,256]{2,1,0:T(8,128)(2,1)} %join_pieces.1.refs_0_, bf16[8,144,256]{2,1,0:T(8,128)(2,1)} %collective-permute-done.1.refs_1_, bf16[8,144,256]{2,1,0:T(8,128)(2,1)} %copy-done, ...), custom_call_target="tpu_custom_call" | custom-call | flops 261881856 | bytes 186368 | tf_op jit(solution)/shard_map/memory/memory_attend/pallas_call | solution.py:448
  108.3 2.9 %collective-permute-done.16.refs_1_ = bf16[4,592,128]{2,1,0:T(8,128)(2,1)S(1)} collective-permute-done((bf16[4,592,128]{2,1,0:T(8,128)(2,1)}, bf16[4,592,128]{2,1,0:T(8,128)(2,1)S(1)}, u32[]{:S(2)}, u32[]{:S(2)}) %collective-permute-start.16) | collective-permute-done | bytes 606240 | tf_op jit(solution)/shard_map/memory/ppermute | solution.py:746
  111.2 2.3 %add_partials.1 = (bf16[592,128]{1,0:T(8,128)(2,1)}, bf16[592,128]{1,0:T(8,128)(2,1)}, bf16[592,128]{1,0:T(8,128)(2,1)}, bf16[592,128]{1,0:T(8,128)(2,1)}) custom-call(s32[1]{0:T(128)} %bitcast.x_ref, bf16[4,592,128]{2,1,0:T(8,128)(2,1)} %memory_attend.3.refs_0_, bf16[4,592,128]{2,1,0:T(8,128)(2,1)S(1)} %collective-permute-done.16.refs_1_), custom_call_target="tpu_custom_call" | custom-call | flops 75776 | bytes 151552 | tf_op jit(solution)/shard_map/memory/add_partials/pallas_call | solution.py:500
  113.5 2.4 %collective-permute-start.17 = (bf16[592,128]{1,0:T(8,128)(2,1)}, bf16[592,128]{1,0:T(8,128)(2,1)S(1)}, u32[]{:S(2)}, u32[]{:S(2)}) collective-permute-start(bf16[592,128]{1,0:T(8,128)(2,1)} %get-tuple-element.24), channel_id=1, source_target_pairs={{0,1},{1,2},{2,3},{3,0},{4,5},{5,6},{6,7},{7,4},{8,9},{9,10},{10,1... | collective-permute-start | bytes 454664 | tf_op jit(solution)/shard_map/memory/ppermute | solution.py:680
  116.0 2.7 %collective-permute-start.18 = (bf16[592,128]{1,0:T(8,128)(2,1)}, bf16[592,128]{1,0:T(8,128)(2,1)S(1)}, u32[]{:S(2)}, u32[]{:S(2)}) collective-permute-start(bf16[592,128]{1,0:T(8,128)(2,1)} %get-tuple-element.25), channel_id=1, source_target_pairs={{0,2},{1,3},{2,0},{3,1},{4,6},{5,7},{6,4},{7,5},{8,10},{9,11},{10,... | collective-permute-start | bytes 454664 | tf_op jit(solution)/shard_map/memory/ppermute | solution.py:680
  118.7 1.5 %collective-permute-start.19 = (bf16[592,128]{1,0:T(8,128)(2,1)}, bf16[592,128]{1,0:T(8,128)(2,1)S(1)}, u32[]{:S(2)}, u32[]{:S(2)}) collective-permute-start(bf16[592,128]{1,0:T(8,128)(2,1)} %get-tuple-element.26), channel_id=1, source_target_pairs={{0,3},{1,0},{2,1},{3,2},{4,7},{5,4},{6,5},{7,6},{8,11},{9,8},{10,9... | collective-permute-start | bytes 454664 | tf_op jit(solution)/shard_map/memory/ppermute | solution.py:680
  120.2 0.0 all-to-all-done.3.time_hbm
  120.2 4.1 %leave_time.1.partial_hbm = f32[4,576,512]{2,1,0:T(8,128)} custom-call(bf16[16,144,128]{2,1,0:T(8,128)(2,1)S(1)} %all-to-all-done.3.time_hbm, bf16[1024,2048]{1,0:T(8,128)(2,1)} %weight_hbm.9, bf16[592,128]{1,0:T(8,128)(2,1)} %get-tuple-element.23._.memory_0), custom_call_target="tpu_custom_call" | custom-call | flops 75497472 | bytes 462848 | tf_op jit(solution)/shard_map/exit/leave_time/pallas_call | solution.py:554
  124.3 0.0 collective-permute-done.17.memory_1
  124.3 0.2 collective-permute-done.18.memory_2
  124.5 0.0 collective-permute-done.19.memory_3
  124.5 5.2 %leave.1 = bf16[576,2048]{1,0:T(8,128)(2,1)} custom-call(s32[1]{0:T(128)} %bitcast.x_ref, bf16[4,592,128]{2,1,0:T(8,128)(2,1)} %own_attend.1.refs_16_.own_hbm, bf16[592,128]{1,0:T(8,128)(2,1)} %get-tuple-element.23._.memory_0, bf16[592,128]{1,0:T(8,128)(2,1)S(1)} %collective-permute-done.17.memory_1, bf16[592,128]{1,0:T(8,128)(2,1)S(1)} %collective-permute-done.18.memory_2, ...), custom_call_target="tpu_custom_call" | custom-call | flops 75497472 | bytes 647168 | tf_op jit(solution)/shard_map/exit/leave/pallas_call | solution.py:625
  (25 shorter events, 0.1 us)
Async XLA Ops:
  0.0 6.6 %copy-start.2 = (s32[1,1,6,1]{2,3,1,0:T(1,128)S(1)}, s32[1,1,6,1]{2,3,1,0:T(1,128)}, u32[]{:S(2)}) copy-start(s32[1,1,6,1]{2,3,1,0:T(1,128)} %param.15) | copy-start | bytes 76
  0.0 6.6 %copy-start.3 = (s32[1,1,6]{2,1,0:T(1,128)S(1)}, s32[1,1,6]{2,1,0:T(1,128)}, u32[]{:S(2)}) copy-start(s32[1,1,6]{2,1,0:T(1,128)} %param.16) | copy-start | bytes 76
  0.0 6.6 %copy-start.1 = (f32[2,4]{1,0:T(2,128)S(1)}, f32[2,4]{1,0:T(2,128)}, u32[]{:S(2)}) copy-start(f32[2,4]{1,0:T(2,128)} %sharpness_ref.3) | copy-start | bytes 100
  2.2 14.6 %all-to-all-start = ((bf16[4,288,256]{2,1,0:T(8,128)(2,1)}), bf16[4,288,256]{2,1,0:T(8,128)(2,1)S(1)}, u32[]{:S(2)}, u32[]{:S(2)}) async-start(bf16[4,288,256]{2,1,0:T(8,128)(2,1)} %bitcast.22), calls=%async_computation | async-start | bytes 1179648 | tf_op jit(solution)/shard_map/store/all_to_all | solution.py:677
  18.5 17.4 %collective-permute-start.1 = (bf16[8,144,256]{2,1,0:T(8,128)(2,1)}, bf16[8,144,256]{2,1,0:T(8,128)(2,1)}, u32[]{:S(2)}, u32[]{:S(2)}) collective-permute-start(bf16[8,144,256]{2,1,0:T(8,128)(2,1)} %join_pieces.1.refs_0_), channel_id=1, source_target_pairs={{0,4},{4,0},{1,5},{5,1},{2,6},{6,2},{3,7},{7,3},{8,12},{12,8},{9,1... | collective-permute-start | bytes 1769480 | tf_op jit(solution)/shard_map/store/ppermute | solution.py:704
  20.5 15.4 %collective-permute-start = (bf16[8,144,256]{2,1,0:T(8,128)(2,1)}, bf16[8,144,256]{2,1,0:T(8,128)(2,1)S(1)}, u32[]{:S(2)}, u32[]{:S(2)}) collective-permute-start(bf16[8,144,256]{2,1,0:T(8,128)(2,1)} %join_pieces.1.refs_0_), channel_id=1, source_target_pairs={{0,96},{32,0},{64,32},{96,64},{1,97},{33,1},{65,33},{97,65},{2,98}... | collective-permute-start | bytes 1769480 | tf_op jit(solution)/shard_map/store/ppermute | solution.py:702
  23.5 14.7 %collective-permute-start.2 = (bf16[8,144,256]{2,1,0:T(8,128)(2,1)}, bf16[8,144,256]{2,1,0:T(8,128)(2,1)S(1)}, u32[]{:S(2)}, u32[]{:S(2)}) collective-permute-start(bf16[8,144,256]{2,1,0:T(8,128)(2,1)} %join_pieces.1.refs_0_), channel_id=1, source_target_pairs={{0,32},{32,64},{64,96},{96,0},{1,33},{33,65},{65,97},{97,1},{2,34}... | collective-permute-start | bytes 1769480 | tf_op jit(solution)/shard_map/store/ppermute | solution.py:703
  23.5 12.3 %all-to-all-start.1 = ((bf16[4,592,128]{2,1,0:T(8,128)(2,1)}), bf16[4,592,128]{2,1,0:T(8,128)(2,1)S(1)}, u32[]{:S(2)}, u32[]{:S(2)}) async-start(bf16[4,592,128]{2,1,0:T(8,128)(2,1)} %bitcast.6), calls=%async_computation.1 | async-start | bytes 1212416 | tf_op jit(solution)/shard_map/queries/all_to_all | solution.py:677
  35.9 41.9 %copy-start.5 = (bf16[4,592,128]{2,1,0:T(8,128)(2,1)}, bf16[4,592,128]{2,1,0:T(8,128)(2,1)S(1)}, u32[]{:S(2)}) copy-start(bf16[4,592,128]{2,1,0:T(8,128)(2,1)S(1)} %all-to-all-done.1.query_hbm) | copy-start | bytes 1818628
  35.9 24.1 %copy-start = (bf16[8,144,256]{2,1,0:T(8,128)(2,1)}, bf16[8,144,256]{2,1,0:T(8,128)(2,1)S(1)}, u32[]{:S(2)}) copy-start(bf16[8,144,256]{2,1,0:T(8,128)(2,1)S(1)} %collective-permute-done.refs_1_.refs_2_) | copy-start | bytes 1769476
  38.3 5.6 %copy-start.6 = (bf16[8,144,256]{2,1,0:T(8,128)(2,1)}, bf16[8,144,256]{2,1,0:T(8,128)(2,1)S(1)}, u32[]{:S(2)}) copy-start(bf16[8,144,256]{2,1,0:T(8,128)(2,1)S(1)} %collective-permute-done.2.refs_6_) | copy-start | bytes 1769476
  38.3 14.6 %collective-permute-start.3 = (bf16[4,592,128]{2,1,0:T(8,128)(2,1)S(1)}, bf16[4,592,128]{2,1,0:T(8,128)(2,1)S(1)}, u32[]{:S(2)}, u32[]{:S(2)}) collective-permute-start(bf16[4,592,128]{2,1,0:T(8,128)(2,1)S(1)} %all-to-all-done.1.query_hbm), channel_id=1, source_target_pairs={{0,8},{8,0},{1,9},{9,1},{2,10},{10,2},{3,11},{11,3},{4,12},{12,4},... | collective-permute-start | bytes 1818632 | tf_op jit(solution)/shard_map/queries/ppermute | solution.py:716
  41.8 18.2 %collective-permute-start.4 = (bf16[8,144,256]{2,1,0:T(8,128)(2,1)}, bf16[8,144,256]{2,1,0:T(8,128)(2,1)}, u32[]{:S(2)}, u32[]{:S(2)}) collective-permute-start(bf16[8,144,256]{2,1,0:T(8,128)(2,1)} %collective-permute-done.1.refs_1_), channel_id=1, source_target_pairs={{0,96},{32,0},{64,32},{96,64},{1,97},{33,1},{65,33},{97,65},{2,98}... | collective-permute-start | bytes 1769480 | tf_op jit(solution)/shard_map/store/ppermute | solution.py:706
  42.5 17.5 %collective-permute-start.5 = (bf16[8,144,256]{2,1,0:T(8,128)(2,1)}, bf16[8,144,256]{2,1,0:T(8,128)(2,1)}, u32[]{:S(2)}, u32[]{:S(2)}) collective-permute-start(bf16[8,144,256]{2,1,0:T(8,128)(2,1)} %collective-permute-done.1.refs_1_), channel_id=1, source_target_pairs={{0,32},{32,64},{64,96},{96,0},{1,33},{33,65},{65,97},{97,1},{2,34}... | collective-permute-start | bytes 1769480 | tf_op jit(solution)/shard_map/store/ppermute | solution.py:707
  52.0 7.4 %copy-start.4 = (bf16[8,144,256]{2,1,0:T(8,128)(2,1)S(1)}, bf16[8,144,256]{2,1,0:T(8,128)(2,1)}, u32[]{:S(2)}) copy-start(bf16[8,144,256]{2,1,0:T(8,128)(2,1)} %join_pieces.1.refs_0_) | copy-start | bytes 1769476
  52.8 0.8 copy-start.11
  53.7 39.1 %all-to-all-start.2 = ((bf16[16,3,144,128]{3,2,1,0:T(8,128)(2,1)}), bf16[16,3,144,128]{3,2,1,0:T(8,128)(2,1)S(1)}, u32[]{:S(2)}, u32[]{:S(2)}) async-start(bf16[16,3,144,128]{3,2,1,0:T(8,128)(2,1)} %bitcast.21), calls=%async_computation.2 | async-start | bytes 3538944 | tf_op jit(solution)/shard_map/temporal/all_to_all | solution.py:677
  59.3 3.9 %collective-permute-start.8 = (bf16[8,144,256]{2,1,0:T(8,128)(2,1)S(1)}, bf16[8,144,256]{2,1,0:T(8,128)(2,1)S(1)}, u32[]{:S(2)}, u32[]{:S(2)}) collective-permute-start(bf16[8,144,256]{2,1,0:T(8,128)(2,1)S(1)} %copy-done.4), channel_id=1, source_target_pairs={{0,16},{16,0},{1,17},{17,1},{2,18},{18,2},{3,19},{19,3},{4,20},{20... | collective-permute-start | bytes 1769480 | tf_op jit(solution)/shard_map/store/ppermute | solution.py:734
  59.4 3.9 %collective-permute-start.9 = (bf16[8,144,256]{2,1,0:T(8,128)(2,1)}, bf16[8,144,256]{2,1,0:T(8,128)(2,1)S(1)}, u32[]{:S(2)}, u32[]{:S(2)}) collective-permute-start(bf16[8,144,256]{2,1,0:T(8,128)(2,1)} %collective-permute-done.1.refs_1_), channel_id=1, source_target_pairs={{0,16},{16,0},{1,17},{17,1},{2,18},{18,2},{3,19},{19,3},{4,20},{20... | collective-permute-start | bytes 1769480 | tf_op jit(solution)/shard_map/store/ppermute | solution.py:734
  59.9 3.9 %collective-permute-start.10 = (bf16[8,144,256]{2,1,0:T(8,128)(2,1)S(1)}, bf16[8,144,256]{2,1,0:T(8,128)(2,1)S(1)}, u32[]{:S(2)}, u32[]{:S(2)}) collective-permute-start(bf16[8,144,256]{2,1,0:T(8,128)(2,1)S(1)} %collective-permute-done.refs_1_.refs_2_), channel_id=1, source_target_pairs={{0,16},{16,0},{1,17},{17,1},{2,18},{18,2},{3,19},{19,3},{4,20},{20... | collective-permute-start | bytes 1769480 | tf_op jit(solution)/shard_map/store/ppermute | solution.py:734
  60.0 17.2 %collective-permute-start.6 = (bf16[8,144,256]{2,1,0:T(8,128)(2,1)}, bf16[8,144,256]{2,1,0:T(8,128)(2,1)}, u32[]{:S(2)}, u32[]{:S(2)}) collective-permute-start(bf16[8,144,256]{2,1,0:T(8,128)(2,1)} %copy-done.6), channel_id=1, source_target_pairs={{0,32},{32,64},{64,96},{96,0},{1,33},{33,65},{65,97},{97,1},{2,34}... | collective-permute-start | bytes 1769480 | tf_op jit(solution)/shard_map/store/ppermute | solution.py:731
  60.3 16.9 %collective-permute-start.7 = (bf16[8,144,256]{2,1,0:T(8,128)(2,1)}, bf16[8,144,256]{2,1,0:T(8,128)(2,1)}, u32[]{:S(2)}, u32[]{:S(2)}) collective-permute-start(bf16[8,144,256]{2,1,0:T(8,128)(2,1)} %collective-permute-done.4.refs_3_), channel_id=1, source_target_pairs={{0,96},{32,0},{64,32},{96,64},{1,97},{33,1},{65,33},{97,65},{2,98}... | collective-permute-start | bytes 1769480 | tf_op jit(solution)/shard_map/store/ppermute | solution.py:732
  63.3 0.8 copy-start.7
  63.3 15.2 %collective-permute-start.11 = (bf16[8,144,256]{2,1,0:T(8,128)(2,1)}, bf16[8,144,256]{2,1,0:T(8,128)(2,1)S(1)}, u32[]{:S(2)}, u32[]{:S(2)}) collective-permute-start(bf16[8,144,256]{2,1,0:T(8,128)(2,1)} %collective-permute-done.4.refs_3_), channel_id=1, source_target_pairs={{0,16},{16,0},{1,17},{17,1},{2,18},{18,2},{3,19},{19,3},{4,20},{20... | collective-permute-start | bytes 1769480 | tf_op jit(solution)/shard_map/store/ppermute | solution.py:734
  63.3 1.0 copy-start.8
  63.3 15.2 %collective-permute-start.14 = (bf16[8,144,256]{2,1,0:T(8,128)(2,1)}, bf16[8,144,256]{2,1,0:T(8,128)(2,1)}, u32[]{:S(2)}, u32[]{:S(2)}) collective-permute-start(bf16[8,144,256]{2,1,0:T(8,128)(2,1)} %copy-done.6), channel_id=1, source_target_pairs={{0,16},{16,0},{1,17},{17,1},{2,18},{18,2},{3,19},{19,3},{4,20},{20... | collective-permute-start | bytes 1769480 | tf_op jit(solution)/shard_map/store/ppermute | solution.py:734
  64.1 13.1 %copy-start.9 = (bf16[8,144,256]{2,1,0:T(8,128)(2,1)}, bf16[8,144,256]{2,1,0:T(8,128)(2,1)S(1)}, u32[]{:S(2)}) copy-start(bf16[8,144,256]{2,1,0:T(8,128)(2,1)S(1)} %collective-permute-done.10.refs_10_) | copy-start | bytes 1769476
  64.1 14.4 %collective-permute-start.15 = (bf16[8,144,256]{2,1,0:T(8,128)(2,1)}, bf16[8,144,256]{2,1,0:T(8,128)(2,1)}, u32[]{:S(2)}, u32[]{:S(2)}) collective-permute-start(bf16[8,144,256]{2,1,0:T(8,128)(2,1)} %collective-permute-done.5.refs_7_), channel_id=1, source_target_pairs={{0,16},{16,0},{1,17},{17,1},{2,18},{18,2},{3,19},{19,3},{4,20},{20... | collective-permute-start | bytes 1769480 | tf_op jit(solution)/shard_map/store/ppermute | solution.py:734
  77.2 2.3 %collective-permute-start.12 = (bf16[8,144,256]{2,1,0:T(8,128)(2,1)}, bf16[8,144,256]{2,1,0:T(8,128)(2,1)}, u32[]{:S(2)}, u32[]{:S(2)}) collective-permute-start(bf16[8,144,256]{2,1,0:T(8,128)(2,1)} %collective-permute-done.6.refs_4_), channel_id=1, source_target_pairs={{0,16},{16,0},{1,17},{17,1},{2,18},{18,2},{3,19},{19,3},{4,20},{20... | collective-permute-start | bytes 1769480 | tf_op jit(solution)/shard_map/store/ppermute | solution.py:734
  77.2 3.2 %collective-permute-start.13 = (bf16[8,144,256]{2,1,0:T(8,128)(2,1)}, bf16[8,144,256]{2,1,0:T(8,128)(2,1)}, u32[]{:S(2)}, u32[]{:S(2)}) collective-permute-start(bf16[8,144,256]{2,1,0:T(8,128)(2,1)} %collective-permute-done.7.refs_5_), channel_id=1, source_target_pairs={{0,16},{16,0},{1,17},{17,1},{2,18},{18,2},{3,19},{19,3},{4,20},{20... | collective-permute-start | bytes 1769480 | tf_op jit(solution)/shard_map/store/ppermute | solution.py:734
  78.5 1.9 %copy-start.10 = (bf16[8,144,256]{2,1,0:T(8,128)(2,1)}, bf16[8,144,256]{2,1,0:T(8,128)(2,1)S(1)}, u32[]{:S(2)}) copy-start(bf16[8,144,256]{2,1,0:T(8,128)(2,1)S(1)} %collective-permute-done.11.refs_11_) | copy-start | bytes 1769476
  88.6 22.6 %collective-permute-start.16 = (bf16[4,592,128]{2,1,0:T(8,128)(2,1)}, bf16[4,592,128]{2,1,0:T(8,128)(2,1)S(1)}, u32[]{:S(2)}, u32[]{:S(2)}) collective-permute-start(bf16[4,592,128]{2,1,0:T(8,128)(2,1)} %memory_attend.2._), channel_id=1, source_target_pairs={{0,8},{8,0},{1,9},{9,1},{2,10},{10,2},{3,11},{11,3},{4,12},{12,4},... | collective-permute-start | bytes 1818632 | tf_op jit(solution)/shard_map/memory/ppermute | solution.py:746
  95.2 25.0 %all-to-all-start.3 = ((bf16[16,144,128]{2,1,0:T(8,128)(2,1)}), bf16[16,144,128]{2,1,0:T(8,128)(2,1)S(1)}, u32[]{:S(2)}, u32[]{:S(2)}) async-start(bf16[16,144,128]{2,1,0:T(8,128)(2,1)} %temporal_attend.1.refs_16_), calls=%async_computation.3 | async-start | bytes 1179648 | tf_op jit(solution)/shard_map/temporal/all_to_all | solution.py:677
  113.5 10.8 %collective-permute-start.17 = (bf16[592,128]{1,0:T(8,128)(2,1)}, bf16[592,128]{1,0:T(8,128)(2,1)S(1)}, u32[]{:S(2)}, u32[]{:S(2)}) collective-permute-start(bf16[592,128]{1,0:T(8,128)(2,1)} %get-tuple-element.24), channel_id=1, source_target_pairs={{0,1},{1,2},{2,3},{3,0},{4,5},{5,6},{6,7},{7,4},{8,9},{9,10},{10,1... | collective-permute-start | bytes 454664 | tf_op jit(solution)/shard_map/memory/ppermute | solution.py:680
  116.0 8.5 %collective-permute-start.18 = (bf16[592,128]{1,0:T(8,128)(2,1)}, bf16[592,128]{1,0:T(8,128)(2,1)S(1)}, u32[]{:S(2)}, u32[]{:S(2)}) collective-permute-start(bf16[592,128]{1,0:T(8,128)(2,1)} %get-tuple-element.25), channel_id=1, source_target_pairs={{0,2},{1,3},{2,0},{3,1},{4,6},{5,7},{6,4},{7,5},{8,10},{9,11},{10,... | collective-permute-start | bytes 454664 | tf_op jit(solution)/shard_map/memory/ppermute | solution.py:680
  118.7 5.8 %collective-permute-start.19 = (bf16[592,128]{1,0:T(8,128)(2,1)}, bf16[592,128]{1,0:T(8,128)(2,1)S(1)}, u32[]{:S(2)}, u32[]{:S(2)}) collective-permute-start(bf16[592,128]{1,0:T(8,128)(2,1)} %get-tuple-element.26), channel_id=1, source_target_pairs={{0,3},{1,0},{2,1},{3,2},{4,7},{5,4},{6,5},{7,6},{8,11},{9,8},{10,9... | collective-permute-start | bytes 454664 | tf_op jit(solution)/shard_map/memory/ppermute | solution.py:680

commit v19 on v18

--- a/solution.py
+++ b/solution.py
@@ -405,22 +405,23 @@
     blocks = refs[:count]
     out_hbm, query_ref, store_ref, out_ref, query_sem, block_sem, store_sem = refs[count + 1 :]
     frames = query_ref.shape[0]
-    held = blocks[0].shape[0]
     query_load = copy(query_hbm, query_ref, query_sem)
     query_load.start()
 
     def fetch(t, carry):
         i, j = t // TOPM, lax.rem(t, TOPM)
         wanted = index_ref[first + i, j]
+        start = 0
         for b in range(count // 2):
-
-            @pl.when(wanted // held == b)
-            def _(b=b):
-                slot = lax.rem(wanted, held)
+            held = blocks[2 * b].shape[0]
+
+            @pl.when((wanted >= start) & (wanted < start + held))
+            def _(b=b, start=start):
                 for part in range(2):
-                    block = blocks[2 * b + part].at[slot]
+                    block = blocks[2 * b + part].at[wanted - start]
                     copy(block, store_ref.at[i, j, part], block_sem.at[i]).start()
 
+            start += held
         return carry
 
     lax.fori_loop(0, frames * TOPM, fetch, 0)
@@ -712,7 +713,12 @@
         )
 
     with jax.named_scope("queries"):
-        here, *_ = lax.optimization_barrier((here, second, above, below, parts))
+        here, second, above, below, parts = lax.optimization_barrier(
+            (here, second, above, below, parts)
+        )
+        half = held // 2
+        far_first = lax.ppermute(above[:half], "y", turn(-1))
+        far_last = lax.ppermute(below[half:], "y", turn(1))
         beside = lax.ppermute(here, "zq", other(sides))
 
     with jax.named_scope("own"):
@@ -721,16 +727,15 @@
         )
 
     with jax.named_scope("temporal"):
-        sent, *_ = lax.optimization_barrier((parts, own, beside))
+        sent, *_ = lax.optimization_barrier((parts, own, beside, far_first, far_last))
         sent = swap(sent.reshape((quarters * G,) + parts.shape[2:]), frame)
 
     with jax.named_scope("store"):
-        below, second_above, second_below = lax.optimization_barrier(
-            (below, second_above, second_below)
-        )
-        far = lax.ppermute(below, "y", turn(1))
-        second_far = lax.ppermute(second_above, "y", turn(-1))
-        near = [joined, second, above, second_above, far, second_far, below, second_below]
+        second_above, second_below = lax.optimization_barrier((second_above, second_below))
+        near = [joined, second, above, second_above]
+        near += [far_first, lax.ppermute(second_above[:half], "y", turn(-1))]
+        near += [far_last, lax.ppermute(second_below[half:], "y", turn(1))]
+        near += [below, second_below]
         blocks = near + [lax.ppermute(block, "c", other(cores)) for block in near]
         blocks = [in_hbm(block) for block in blocks]
 

time: 130 us -> 131 us (level)
  waiting for transfers between devices: 26.1 us -> 22.1 us
  local copies, waits for them, and re-layouts: 3.26 us -> 7.09 us
    ppermute x2 -> x4, waiting for transfers between devices: 12.9 us -> 8.85 us  [the longest x1 6.26 us: on_device(): near += [far_first, lax.ppermute(second_above[:half], 'y', turn(-1))]]
    slice x0 -> x4, local copies, waits for them, and re-layouts: none -> 2 us  [the longest x1 0.98 us: on_device(): near += [far_last, lax.ppermute(second_below[half:], 'y', turn(1))]]
    ppermute x1, waiting for transfers between devices: 0.01 us -> 1.77 us  [on_device(): second_below = lax.ppermute(second, 'y', turn(1))]
    ppermute x8 -> x10, waiting for transfers between devices: 1.93 us -> 0.46 us  [on_device(): blocks = near + [lax.ppermute(block, 'c', other(cores)) for block in near]]
    unnamed x27 -> x39, local copies, waits for them, and re-layouts: 2.55 us -> 3.68 us
    ppermute x2 -> x4, starting transfers between devices: 3.24 us -> 4.19 us  [the longest x1 1.47 us: on_device(): near += [far_first, lax.ppermute(second_above[:half], 'y', turn(-1))]]
  transfers between devices with their start and end apart: 24 -> 28, of which waited for: 9 -> 9; matrix products, arithmetic and copies ran while one was open for 1% -> 3% of each run, Pallas kernels for 37% -> 36%
where the time goes in v19:
time: 131 us
  Pallas kernels  55.3 us (42%)
  starting transfers between devices  44.7 us (34%)
  waiting for transfers between devices  22.1 us (17%)
  local copies, waits for them, and re-layouts  7.09 us (5%)
    all_to_all x4, starting transfers between devices, swap(): return lax.all_to_all(blocks, axes, split_axis=0, concat_axis=0, tiled=True)  17.6 us
    pallas_call x2, Pallas kernels, memory_attend(): pl.pallas_call(functools.partial(memory_attend_kernel, count, first), in_...  16.3 us
    pallas_call x1, Pallas kernels, temporal_entry(): pl.pallas_call(functools.partial(temporal_entry_kernel, quarters), in_spe...  8.56 us
    pallas_call x1, Pallas kernels, own_attend(): pl.pallas_call(own_attend_kernel, in_specs=[HBM, HBM, HBM] + [ANY] * len(...  8.06 us
    ppermute x3, starting transfers between devices, swap_apart(): lax.ppermute(blocks[j], 'x', turn(j))  6.58 us
    ppermute x1, waiting for transfers between devices, on_device(): near += [far_first, lax.ppermute(second_above[:half], 'y', turn(-1))]  6.26 us
    pallas_call x1, Pallas kernels, modulate(): pl.pallas_call(functools.partial(modulate_kernel, held), in_specs=[HBM, H...  5.57 us
    pallas_call x1, Pallas kernels, leave(): pl.pallas_call(leave_kernel, in_specs=[SCALARS, HBM] + [ANY] * G + [HBM,...  5.16 us
  transfers between devices with their start and end apart: 28, of which 9 were waited for; matrix products, arithmetic and copies ran while one was open for 3% of the time, Pallas kernels for 36%

profile of v19, /device:TPU:0, one launch (start us, length us, event | category | flops | bytes accessed | tf_op | source)
XLA Modules:
  0.0 130.5 jit_solution(1013339240271747447)
XLA Ops:
  0.0 1.2 copy.12
  1.2 1.0 split_store.1._
  2.2 4.4 %all-to-all-start.1 = ((bf16[4,288,256]{2,1,0:T(8,128)(2,1)}), bf16[4,288,256]{2,1,0:T(8,128)(2,1)S(1)}, u32[]{:S(2)}, u32[]{:S(2)}) async-start(bf16[4,288,256]{2,1,0:T(8,128)(2,1)} %bitcast.22), calls=%async_computation.1 | async-start | bytes 1179648 | tf_op jit(solution)/shard_map/store/all_to_all | solution.py:678
  6.6 5.6 %modulate.1 = (bf16[576,2048]{1,0:T(8,128)(2,1)}, bf16[1,4,592,128]{3,2,1,0:T(8,128)(2,1)}) custom-call(bf16[576,2048]{1,0:T(8,128)(2,1)} %bitcast.23, f32[2,2048]{1,0:T(2,128)} %bitcast.25, bf16[2048,3072]{1,0:T(8,128)(2,1)} %weight_hbm.7, f32[2,4]{1,0:T(2,128)S(1)} %copy-done.1, s32[6]{0:T(128)S(1)} %bitcast.19, s32[6]{0:T(128)S(1)} %bitcast.20, ...), custom_call_target="tpu_custom_call" | custom-call | flops 75497472 | bytes 462848 | tf_op jit(solution)/shard_map/queries/modulate/pallas_call | solution.py:185
  12.2 4.6 %all-to-all-done.1.in_hbm = bf16[4,288,256]{2,1,0:T(8,128)(2,1)S(1)} async-done(((bf16[4,288,256]{2,1,0:T(8,128)(2,1)}), bf16[4,288,256]{2,1,0:T(8,128)(2,1)S(1)}, u32[]{:S(2)}, u32[]{:S(2)}) %all-to-all-start.1) | async-done | bytes 589856 | tf_op jit(solution)/shard_map/store/all_to_all | solution.py:678
  16.8 1.7 %join_pieces.1.refs_0_ = bf16[8,144,256]{2,1,0:T(8,128)(2,1)} custom-call(bf16[4,288,256]{2,1,0:T(8,128)(2,1)S(1)} %all-to-all-done.1.in_hbm, bf16[576,2048]{1,0:T(8,128)(2,1)} %get-tuple-element.19._.hidden_hbm), custom_call_target="tpu_custom_call" | custom-call | flops 18432 | bytes 73728 | tf_op jit(solution)/shard_map/store/join_pieces/pallas_call | solution.py:109
  18.5 2.0 %collective-permute-start = (bf16[8,144,256]{2,1,0:T(8,128)(2,1)}, bf16[8,144,256]{2,1,0:T(8,128)(2,1)}, u32[]{:S(2)}, u32[]{:S(2)}) collective-permute-start(bf16[8,144,256]{2,1,0:T(8,128)(2,1)} %join_pieces.1.refs_0_), channel_id=1, source_target_pairs={{0,4},{4,0},{1,5},{5,1},{2,6},{6,2},{3,7},{7,3},{8,12},{12,8},{9,1... | collective-permute-start | bytes 1769480 | tf_op jit(solution)/shard_map/store/ppermute | solution.py:705
  20.5 3.0 %collective-permute-start.1 = (bf16[8,144,256]{2,1,0:T(8,128)(2,1)}, bf16[8,144,256]{2,1,0:T(8,128)(2,1)S(1)}, u32[]{:S(2)}, u32[]{:S(2)}) collective-permute-start(bf16[8,144,256]{2,1,0:T(8,128)(2,1)} %join_pieces.1.refs_0_), channel_id=1, source_target_pairs={{0,96},{32,0},{64,32},{96,64},{1,97},{33,1},{65,33},{97,65},{2,98}... | collective-permute-start | bytes 1769480 | tf_op jit(solution)/shard_map/store/ppermute | solution.py:703
  23.5 0.0 collective-permute-start.2
  23.5 3.5 %all-to-all-start = ((bf16[4,592,128]{2,1,0:T(8,128)(2,1)}), bf16[4,592,128]{2,1,0:T(8,128)(2,1)S(1)}, u32[]{:S(2)}, u32[]{:S(2)}) async-start(bf16[4,592,128]{2,1,0:T(8,128)(2,1)} %bitcast.5), calls=%async_computation | async-start | bytes 1212416 | tf_op jit(solution)/shard_map/queries/all_to_all | solution.py:678
  27.0 8.6 %temporal_entry.1.refs_0_ = bf16[4,4,3,144,128]{4,3,2,1,0:T(8,128)(2,1)} custom-call(bf16[576,2048]{1,0:T(8,128)(2,1)} %get-tuple-element.19._.hidden_hbm, bf16[2048,3072]{1,0:T(8,128)(2,1)} %weight_hbm.7, f32[2,4]{1,0:T(2,128)S(1)} %copy-done.1, bf16[8,144,256]{2,1,0:T(8,128)(2,1)} %join_pieces.1.refs_0_), custom_call_target="tpu_custom_call" | custom-call | flops 226492416 | bytes 651264 | tf_op jit(solution)/shard_map/temporal/temporal_entry/pallas_call | solution.py:250
  35.6 0.3 all-to-all-done.query_hbm
  35.9 2.4 %collective-permute-done.2.refs_8_ = bf16[8,144,256]{2,1,0:T(8,128)(2,1)S(1)} collective-permute-done((bf16[8,144,256]{2,1,0:T(8,128)(2,1)}, bf16[8,144,256]{2,1,0:T(8,128)(2,1)S(1)}, u32[]{:S(2)}, u32[]{:S(2)}) %collective-permute-start.2) | collective-permute-done | bytes 589856 | tf_op jit(solution)/shard_map/store/ppermute | solution.py:704
  38.2 3.6 %collective-permute-start.3 = (bf16[4,592,128]{2,1,0:T(8,128)(2,1)S(1)}, bf16[4,592,128]{2,1,0:T(8,128)(2,1)S(1)}, u32[]{:S(2)}, u32[]{:S(2)}) collective-permute-start(bf16[4,592,128]{2,1,0:T(8,128)(2,1)S(1)} %all-to-all-done.query_hbm), channel_id=1, source_target_pairs={{0,8},{8,0},{1,9},{9,1},{2,10},{10,2},{3,11},{11,3},{4,12},{12,4},... | collective-permute-start | bytes 1818632 | tf_op jit(solution)/shard_map/queries/ppermute | solution.py:722
  41.9 0.8 collective-permute-start.6
  42.6 1.4 %collective-permute-start.8 = (bf16[4,144,256]{2,1,0:T(8,128)(2,1)S(1)}, bf16[4,144,256]{2,1,0:T(8,128)(2,1)S(1)}, u32[]{:S(2)}, u32[]{:S(2)}) collective-permute-start(bf16[4,144,256]{2,1,0:T(8,128)(2,1)S(1)} %slice.22), channel_id=1, source_target_pairs={{0,32},{32,64},{64,96},{96,0},{1,33},{33,65},{65,97},{97,1},{2,34}... | collective-permute-start | bytes 884744 | tf_op jit(solution)/shard_map/queries/ppermute | solution.py:721
  44.0 1.9 %collective-permute-start.4 = (bf16[8,144,256]{2,1,0:T(8,128)(2,1)}, bf16[8,144,256]{2,1,0:T(8,128)(2,1)}, u32[]{:S(2)}, u32[]{:S(2)}) collective-permute-start(bf16[8,144,256]{2,1,0:T(8,128)(2,1)} %collective-permute-done.refs_1_), channel_id=1, source_target_pairs={{0,96},{32,0},{64,32},{96,64},{1,97},{33,1},{65,33},{97,65},{2,98}... | collective-permute-start | bytes 1769480 | tf_op jit(solution)/shard_map/store/ppermute | solution.py:707
  46.0 0.1 collective-permute-start.5
  46.1 8.1 %own_attend.1.refs_20_.own_hbm = bf16[4,592,128]{2,1,0:T(8,128)(2,1)} custom-call(bf16[576,2048]{1,0:T(8,128)(2,1)} %get-tuple-element.19._.hidden_hbm, bf16[2048,3072]{1,0:T(8,128)(2,1)} %weight_hbm.7, bf16[1,4,592,128]{3,2,1,0:T(8,128)(2,1)} %get-tuple-element.20.query_hbm, bf16[4,4,3,144,128]{4,3,2,1,0:T(8,128)(2,1)} %temporal_entry.1.refs_0_, ...), custom_call_target="tpu_custom_call" | custom-call | flops 214695936 | bytes 593920 | tf_op jit(solution)/shard_map/own/own_attend/pallas_call | solution.py:380
  54.2 0.0 collective-permute-done.6.refs_4_
  54.2 0.0 collective-permute-done.3.query_hbm
  54.2 0.0 copy-start.17
  54.2 0.8 copy-done.17
  55.0 0.1 copy-done.12
  55.1 0.1 copy-done.13
  55.2 4.8 %all-to-all-start.2 = ((bf16[16,3,144,128]{3,2,1,0:T(8,128)(2,1)}), bf16[16,3,144,128]{3,2,1,0:T(8,128)(2,1)S(1)}, u32[]{:S(2)}, u32[]{:S(2)}) async-start(bf16[16,3,144,128]{3,2,1,0:T(8,128)(2,1)} %bitcast.21), calls=%async_computation.2 | async-start | bytes 3538944 | tf_op jit(solution)/shard_map/temporal/all_to_all | solution.py:678
  59.9 0.1 collective-permute-start.10
  60.0 0.5 collective-permute-start.12
  60.5 0.1 collective-permute-start.18
  60.6 0.0 collective-permute-done.4.refs_3_
  60.6 0.4 collective-permute-start.14
  61.1 1.8 %collective-permute-done.5.refs_9_ = bf16[8,144,256]{2,1,0:T(8,128)(2,1)} collective-permute-done((bf16[8,144,256]{2,1,0:T(8,128)(2,1)}, bf16[8,144,256]{2,1,0:T(8,128)(2,1)}, u32[]{:S(2)}, u32[]{:S(2)}) %collective-permute-start.5) | collective-permute-done | bytes 589856 | tf_op jit(solution)/shard_map/store/ppermute | solution.py:708
  62.8 0.0 collective-permute-start.16
  62.8 1.0 slice.21
  63.8 1.0 slice.23
  64.8 0.6 collective-permute-start.11
  65.4 1.5 %collective-permute-start.7 = (bf16[4,144,256]{2,1,0:T(8,128)(2,1)S(1)}, bf16[4,144,256]{2,1,0:T(8,128)(2,1)}, u32[]{:S(2)}, u32[]{:S(2)}) collective-permute-start(bf16[4,144,256]{2,1,0:T(8,128)(2,1)S(1)} %slice.21), channel_id=1, source_target_pairs={{0,96},{32,0},{64,32},{96,64},{1,97},{33,1},{65,33},{97,65},{2,98}... | collective-permute-start | bytes 884744 | tf_op jit(solution)/shard_map/store/ppermute | solution.py:736
  66.9 0.6 collective-permute-start.9
  67.5 0.0 collective-permute-start.13
  67.5 0.0 collective-permute-done.18.refs_18_
  67.5 0.6 collective-permute-start.19
  68.0 0.2 copy-done.8
  68.3 6.3 %collective-permute-done.7.refs_5_ = bf16[4,144,256]{2,1,0:T(8,128)(2,1)} collective-permute-done((bf16[4,144,256]{2,1,0:T(8,128)(2,1)S(1)}, bf16[4,144,256]{2,1,0:T(8,128)(2,1)}, u32[]{:S(2)}, u32[]{:S(2)}) %collective-permute-start.7) | collective-permute-done | bytes 294944 | tf_op jit(solution)/shard_map/store/ppermute | solution.py:736
  74.5 2.6 %collective-permute-done.9.refs_7_ = bf16[4,144,256]{2,1,0:T(8,128)(2,1)} collective-permute-done((bf16[4,144,256]{2,1,0:T(8,128)(2,1)S(1)}, bf16[4,144,256]{2,1,0:T(8,128)(2,1)}, u32[]{:S(2)}, u32[]{:S(2)}) %collective-permute-start.9) | collective-permute-done | bytes 294944 | tf_op jit(solution)/shard_map/store/ppermute | solution.py:737
  77.1 0.0 collective-permute-start.17
  77.1 0.7 slice.19
  77.8 0.7 slice.24
  78.6 0.4 collective-permute-done.17.refs_17_
  79.1 0.4 copy-done.10
  79.4 0.1 copy-done.16
  79.5 0.8 copy-done.11
  80.3 8.2 %memory_attend.2._ = bf16[4,592,128]{2,1,0:T(8,128)(2,1)} custom-call(s32[8,6]{1,0:T(8,128)S(1)} %fusion.10.index_ref, bf16[4,592,128]{2,1,0:T(8,128)(2,1)} %copy-done.17, bf16[8,144,256]{2,1,0:T(8,128)(2,1)} %join_pieces.1.refs_0_, bf16[8,144,256]{2,1,0:T(8,128)(2,1)} %collective-permute-done.refs_1_, bf16[8,144,256]{2,1,0:T(8,128)(2,1)} %copy-done, ...), custom_call_target="tpu_custom_call" | custom-call | flops 261881856 | bytes 186368 | tf_op jit(solution)/shard_map/memory/memory_attend/pallas_call | solution.py:449
  88.5 3.5 %collective-permute-start.20 = (bf16[4,592,128]{2,1,0:T(8,128)(2,1)}, bf16[4,592,128]{2,1,0:T(8,128)(2,1)S(1)}, u32[]{:S(2)}, u32[]{:S(2)}) collective-permute-start(bf16[4,592,128]{2,1,0:T(8,128)(2,1)} %memory_attend.2._), channel_id=1, source_target_pairs={{0,8},{8,0},{1,9},{9,1},{2,10},{10,2},{3,11},{11,3},{4,12},{12,4},... | collective-permute-start | bytes 1818632 | tf_op jit(solution)/shard_map/memory/ppermute | solution.py:751
  92.7 2.4 %temporal_attend.1.refs_20_ = bf16[16,144,128]{2,1,0:T(8,128)(2,1)} custom-call(s32[1]{0:T(128)S(6)} %copy.17.length_ref, bf16[16,3,144,128]{3,2,1,0:T(8,128)(2,1)S(1)} %all-to-all-done.2.in_hbm_ref, bf16[4,592,128]{2,1,0:T(8,128)(2,1)} %memory_attend.2._), custom_call_target="tpu_custom_call" | custom-call | flops 18874368 | bytes 147456 | tf_op jit(solution)/shard_map/temporal/temporal_attend/pallas_call | solution.py:300
  95.1 5.0 %all-to-all-start.3 = ((bf16[16,144,128]{2,1,0:T(8,128)(2,1)}), bf16[16,144,128]{2,1,0:T(8,128)(2,1)S(1)}, u32[]{:S(2)}, u32[]{:S(2)}) async-start(bf16[16,144,128]{2,1,0:T(8,128)(2,1)} %temporal_attend.1.refs_20_), calls=%async_computation.3 | async-start | bytes 1179648 | tf_op jit(solution)/shard_map/temporal/all_to_all | solution.py:678
  100.1 8.2 %memory_attend.3.refs_0_ = bf16[4,592,128]{2,1,0:T(8,128)(2,1)} custom-call(s32[8,6]{1,0:T(8,128)S(1)} %fusion.10.index_ref, bf16[4,592,128]{2,1,0:T(8,128)(2,1)} %copy-done.6, bf16[8,144,256]{2,1,0:T(8,128)(2,1)} %join_pieces.1.refs_0_, bf16[8,144,256]{2,1,0:T(8,128)(2,1)} %collective-permute-done.refs_1_, bf16[8,144,256]{2,1,0:T(8,128)(2,1)} %copy-done, ...), custom_call_target="tpu_custom_call" | custom-call | flops 261881856 | bytes 186368 | tf_op jit(solution)/shard_map/memory/memory_attend/pallas_call | solution.py:449
  108.3 2.8 %collective-permute-done.20.refs_1_ = bf16[4,592,128]{2,1,0:T(8,128)(2,1)S(1)} collective-permute-done((bf16[4,592,128]{2,1,0:T(8,128)(2,1)}, bf16[4,592,128]{2,1,0:T(8,128)(2,1)S(1)}, u32[]{:S(2)}, u32[]{:S(2)}) %collective-permute-start.20) | collective-permute-done | bytes 606240 | tf_op jit(solution)/shard_map/memory/ppermute | solution.py:751
  111.1 2.3 %add_partials.1 = (bf16[592,128]{1,0:T(8,128)(2,1)}, bf16[592,128]{1,0:T(8,128)(2,1)}, bf16[592,128]{1,0:T(8,128)(2,1)}, bf16[592,128]{1,0:T(8,128)(2,1)}) custom-call(s32[1]{0:T(128)} %bitcast.x_ref, bf16[4,592,128]{2,1,0:T(8,128)(2,1)} %memory_attend.3.refs_0_, bf16[4,592,128]{2,1,0:T(8,128)(2,1)S(1)} %collective-permute-done.20.refs_1_), custom_call_target="tpu_custom_call" | custom-call | flops 75776 | bytes 151552 | tf_op jit(solution)/shard_map/memory/add_partials/pallas_call | solution.py:501
  113.4 2.2 %collective-permute-start.21 = (bf16[592,128]{1,0:T(8,128)(2,1)}, bf16[592,128]{1,0:T(8,128)(2,1)S(1)}, u32[]{:S(2)}, u32[]{:S(2)}) collective-permute-start(bf16[592,128]{1,0:T(8,128)(2,1)} %get-tuple-element.30), channel_id=1, source_target_pairs={{0,1},{1,2},{2,3},{3,0},{4,5},{5,6},{6,7},{7,4},{8,9},{9,10},{10,1... | collective-permute-start | bytes 454664 | tf_op jit(solution)/shard_map/memory/ppermute | solution.py:681
  115.6 3.0 %collective-permute-start.22 = (bf16[592,128]{1,0:T(8,128)(2,1)}, bf16[592,128]{1,0:T(8,128)(2,1)S(1)}, u32[]{:S(2)}, u32[]{:S(2)}) collective-permute-start(bf16[592,128]{1,0:T(8,128)(2,1)} %get-tuple-element.31), channel_id=1, source_target_pairs={{0,2},{1,3},{2,0},{3,1},{4,6},{5,7},{6,4},{7,5},{8,10},{9,11},{10,... | collective-permute-start | bytes 454664 | tf_op jit(solution)/shard_map/memory/ppermute | solution.py:681
  118.5 1.5 %collective-permute-start.23 = (bf16[592,128]{1,0:T(8,128)(2,1)}, bf16[592,128]{1,0:T(8,128)(2,1)S(1)}, u32[]{:S(2)}, u32[]{:S(2)}) collective-permute-start(bf16[592,128]{1,0:T(8,128)(2,1)} %get-tuple-element.32), channel_id=1, source_target_pairs={{0,3},{1,0},{2,1},{3,2},{4,7},{5,4},{6,5},{7,6},{8,11},{9,8},{10,9... | collective-permute-start | bytes 454664 | tf_op jit(solution)/shard_map/memory/ppermute | solution.py:681
  120.0 4.1 %leave_time.1.partial_hbm = f32[4,576,512]{2,1,0:T(8,128)} custom-call(bf16[16,144,128]{2,1,0:T(8,128)(2,1)S(1)} %all-to-all-done.3.time_hbm, bf16[1024,2048]{1,0:T(8,128)(2,1)} %weight_hbm.9, bf16[592,128]{1,0:T(8,128)(2,1)} %get-tuple-element.29._.memory_0), custom_call_target="tpu_custom_call" | custom-call | flops 75497472 | bytes 462848 | tf_op jit(solution)/shard_map/exit/leave_time/pallas_call | solution.py:555
  124.2 1.0 collective-permute-done.22.memory_2
  125.1 5.2 %leave.1 = bf16[576,2048]{1,0:T(8,128)(2,1)} custom-call(s32[1]{0:T(128)} %bitcast.x_ref, bf16[4,592,128]{2,1,0:T(8,128)(2,1)} %own_attend.1.refs_20_.own_hbm, bf16[592,128]{1,0:T(8,128)(2,1)} %get-tuple-element.29._.memory_0, bf16[592,128]{1,0:T(8,128)(2,1)S(1)} %collective-permute-done.21.memory_1, bf16[592,128]{1,0:T(8,128)(2,1)S(1)} %collective-permute-done.22.memory_2, ...), custom_call_target="tpu_custom_call" | custom-call | flops 75497472 | bytes 647168 | tf_op jit(solution)/shard_map/exit/leave/pallas_call | solution.py:626
  (49 shorter events, 0.2 us)
Async XLA Ops:
  0.0 6.6 %copy-start.2 = (s32[1,1,6,1]{2,3,1,0:T(1,128)S(1)}, s32[1,1,6,1]{2,3,1,0:T(1,128)}, u32[]{:S(2)}) copy-start(s32[1,1,6,1]{2,3,1,0:T(1,128)} %param.15) | copy-start | bytes 76
  0.0 6.6 %copy-start.3 = (s32[1,1,6]{2,1,0:T(1,128)S(1)}, s32[1,1,6]{2,1,0:T(1,128)}, u32[]{:S(2)}) copy-start(s32[1,1,6]{2,1,0:T(1,128)} %param.16) | copy-start | bytes 76
  0.0 6.6 %copy-start.1 = (f32[2,4]{1,0:T(2,128)S(1)}, f32[2,4]{1,0:T(2,128)}, u32[]{:S(2)}) copy-start(f32[2,4]{1,0:T(2,128)} %sharpness_ref.3) | copy-start | bytes 100
  2.2 14.6 %all-to-all-start.1 = ((bf16[4,288,256]{2,1,0:T(8,128)(2,1)}), bf16[4,288,256]{2,1,0:T(8,128)(2,1)S(1)}, u32[]{:S(2)}, u32[]{:S(2)}) async-start(bf16[4,288,256]{2,1,0:T(8,128)(2,1)} %bitcast.22), calls=%async_computation.1 | async-start | bytes 1179648 | tf_op jit(solution)/shard_map/store/all_to_all | solution.py:678
  18.5 17.4 %collective-permute-start = (bf16[8,144,256]{2,1,0:T(8,128)(2,1)}, bf16[8,144,256]{2,1,0:T(8,128)(2,1)}, u32[]{:S(2)}, u32[]{:S(2)}) collective-permute-start(bf16[8,144,256]{2,1,0:T(8,128)(2,1)} %join_pieces.1.refs_0_), channel_id=1, source_target_pairs={{0,4},{4,0},{1,5},{5,1},{2,6},{6,2},{3,7},{7,3},{8,12},{12,8},{9,1... | collective-permute-start | bytes 1769480 | tf_op jit(solution)/shard_map/store/ppermute | solution.py:705
  20.5 15.4 %collective-permute-start.1 = (bf16[8,144,256]{2,1,0:T(8,128)(2,1)}, bf16[8,144,256]{2,1,0:T(8,128)(2,1)S(1)}, u32[]{:S(2)}, u32[]{:S(2)}) collective-permute-start(bf16[8,144,256]{2,1,0:T(8,128)(2,1)} %join_pieces.1.refs_0_), channel_id=1, source_target_pairs={{0,96},{32,0},{64,32},{96,64},{1,97},{33,1},{65,33},{97,65},{2,98}... | collective-permute-start | bytes 1769480 | tf_op jit(solution)/shard_map/store/ppermute | solution.py:703
  23.5 14.7 %collective-permute-start.2 = (bf16[8,144,256]{2,1,0:T(8,128)(2,1)}, bf16[8,144,256]{2,1,0:T(8,128)(2,1)S(1)}, u32[]{:S(2)}, u32[]{:S(2)}) collective-permute-start(bf16[8,144,256]{2,1,0:T(8,128)(2,1)} %join_pieces.1.refs_0_), channel_id=1, source_target_pairs={{0,32},{32,64},{64,96},{96,0},{1,33},{33,65},{65,97},{97,1},{2,34}... | collective-permute-start | bytes 1769480 | tf_op jit(solution)/shard_map/store/ppermute | solution.py:704
  23.5 12.3 %all-to-all-start = ((bf16[4,592,128]{2,1,0:T(8,128)(2,1)}), bf16[4,592,128]{2,1,0:T(8,128)(2,1)S(1)}, u32[]{:S(2)}, u32[]{:S(2)}) async-start(bf16[4,592,128]{2,1,0:T(8,128)(2,1)} %bitcast.5), calls=%async_computation | async-start | bytes 1212416 | tf_op jit(solution)/shard_map/queries/all_to_all | solution.py:678
  35.8 18.3 %copy-start.6 = (bf16[4,592,128]{2,1,0:T(8,128)(2,1)}, bf16[4,592,128]{2,1,0:T(8,128)(2,1)S(1)}, u32[]{:S(2)}) copy-start(bf16[4,592,128]{2,1,0:T(8,128)(2,1)S(1)} %all-to-all-done.query_hbm) | copy-start | bytes 1818628
  35.9 24.2 %copy-start = (bf16[8,144,256]{2,1,0:T(8,128)(2,1)}, bf16[8,144,256]{2,1,0:T(8,128)(2,1)S(1)}, u32[]{:S(2)}) copy-start(bf16[8,144,256]{2,1,0:T(8,128)(2,1)S(1)} %collective-permute-done.1.refs_1_.refs_2_) | copy-start | bytes 1769476
  38.2 22.3 %copy-start.5 = (bf16[8,144,256]{2,1,0:T(8,128)(2,1)}, bf16[8,144,256]{2,1,0:T(8,128)(2,1)S(1)}, u32[]{:S(2)}) copy-start(bf16[8,144,256]{2,1,0:T(8,128)(2,1)S(1)} %collective-permute-done.2.refs_8_) | copy-start | bytes 1769476
  38.2 16.0 %collective-permute-start.3 = (bf16[4,592,128]{2,1,0:T(8,128)(2,1)S(1)}, bf16[4,592,128]{2,1,0:T(8,128)(2,1)S(1)}, u32[]{:S(2)}, u32[]{:S(2)}) collective-permute-start(bf16[4,592,128]{2,1,0:T(8,128)(2,1)S(1)} %all-to-all-done.query_hbm), channel_id=1, source_target_pairs={{0,8},{8,0},{1,9},{9,1},{2,10},{10,2},{3,11},{11,3},{4,12},{12,4},... | collective-permute-start | bytes 1818632 | tf_op jit(solution)/shard_map/queries/ppermute | solution.py:722
  41.9 12.3 %collective-permute-start.6 = (bf16[4,144,256]{2,1,0:T(8,128)(2,1)S(1)}, bf16[4,144,256]{2,1,0:T(8,128)(2,1)S(1)}, u32[]{:S(2)}, u32[]{:S(2)}) collective-permute-start(bf16[4,144,256]{2,1,0:T(8,128)(2,1)S(1)} %slice.20), channel_id=1, source_target_pairs={{0,96},{32,0},{64,32},{96,64},{1,97},{33,1},{65,33},{97,65},{2,98}... | collective-permute-start | bytes 884744 | tf_op jit(solution)/shard_map/queries/ppermute | solution.py:720
  42.6 11.5 %collective-permute-start.8 = (bf16[4,144,256]{2,1,0:T(8,128)(2,1)S(1)}, bf16[4,144,256]{2,1,0:T(8,128)(2,1)S(1)}, u32[]{:S(2)}, u32[]{:S(2)}) collective-permute-start(bf16[4,144,256]{2,1,0:T(8,128)(2,1)S(1)} %slice.22), channel_id=1, source_target_pairs={{0,32},{32,64},{64,96},{96,0},{1,33},{33,65},{65,97},{97,1},{2,34}... | collective-permute-start | bytes 884744 | tf_op jit(solution)/shard_map/queries/ppermute | solution.py:721
  44.0 16.6 %collective-permute-start.4 = (bf16[8,144,256]{2,1,0:T(8,128)(2,1)}, bf16[8,144,256]{2,1,0:T(8,128)(2,1)}, u32[]{:S(2)}, u32[]{:S(2)}) collective-permute-start(bf16[8,144,256]{2,1,0:T(8,128)(2,1)} %collective-permute-done.refs_1_), channel_id=1, source_target_pairs={{0,96},{32,0},{64,32},{96,64},{1,97},{33,1},{65,33},{97,65},{2,98}... | collective-permute-start | bytes 1769480 | tf_op jit(solution)/shard_map/store/ppermute | solution.py:707
  46.0 16.9 %collective-permute-start.5 = (bf16[8,144,256]{2,1,0:T(8,128)(2,1)}, bf16[8,144,256]{2,1,0:T(8,128)(2,1)}, u32[]{:S(2)}, u32[]{:S(2)}) collective-permute-start(bf16[8,144,256]{2,1,0:T(8,128)(2,1)} %collective-permute-done.refs_1_), channel_id=1, source_target_pairs={{0,32},{32,64},{64,96},{96,0},{1,33},{33,65},{65,97},{97,1},{2,34}... | collective-permute-start | bytes 1769480 | tf_op jit(solution)/shard_map/store/ppermute | solution.py:708
  54.1 5.8 %copy-start.4 = (bf16[8,144,256]{2,1,0:T(8,128)(2,1)S(1)}, bf16[8,144,256]{2,1,0:T(8,128)(2,1)}, u32[]{:S(2)}) copy-start(bf16[8,144,256]{2,1,0:T(8,128)(2,1)} %join_pieces.1.refs_0_) | copy-start | bytes 1769476
  54.2 0.9 copy-start.12
  54.2 1.0 copy-start.13
  54.2 0.8 copy-start.17
  55.2 37.5 %all-to-all-start.2 = ((bf16[16,3,144,128]{3,2,1,0:T(8,128)(2,1)}), bf16[16,3,144,128]{3,2,1,0:T(8,128)(2,1)S(1)}, u32[]{:S(2)}, u32[]{:S(2)}) async-start(bf16[16,3,144,128]{3,2,1,0:T(8,128)(2,1)} %bitcast.21), calls=%async_computation.2 | async-start | bytes 3538944 | tf_op jit(solution)/shard_map/temporal/all_to_all | solution.py:678
  59.9 4.9 %collective-permute-start.10 = (bf16[8,144,256]{2,1,0:T(8,128)(2,1)S(1)}, bf16[8,144,256]{2,1,0:T(8,128)(2,1)S(1)}, u32[]{:S(2)}, u32[]{:S(2)}) collective-permute-start(bf16[8,144,256]{2,1,0:T(8,128)(2,1)S(1)} %copy-done.4), channel_id=1, source_target_pairs={{0,16},{16,0},{1,17},{17,1},{2,18},{18,2},{3,19},{19,3},{4,20},{20... | collective-permute-start | bytes 1769480 | tf_op jit(solution)/shard_map/store/ppermute | solution.py:739
  60.0 7.4 %collective-permute-start.12 = (bf16[8,144,256]{2,1,0:T(8,128)(2,1)S(1)}, bf16[8,144,256]{2,1,0:T(8,128)(2,1)S(1)}, u32[]{:S(2)}, u32[]{:S(2)}) collective-permute-start(bf16[8,144,256]{2,1,0:T(8,128)(2,1)S(1)} %collective-permute-done.1.refs_1_.refs_2_), channel_id=1, source_target_pairs={{0,16},{16,0},{1,17},{17,1},{2,18},{18,2},{3,19},{19,3},{4,20},{20... | collective-permute-start | bytes 1769480 | tf_op jit(solution)/shard_map/store/ppermute | solution.py:739
  60.5 6.9 %collective-permute-start.18 = (bf16[8,144,256]{2,1,0:T(8,128)(2,1)S(1)}, bf16[8,144,256]{2,1,0:T(8,128)(2,1)S(1)}, u32[]{:S(2)}, u32[]{:S(2)}) collective-permute-start(bf16[8,144,256]{2,1,0:T(8,128)(2,1)S(1)} %collective-permute-done.2.refs_8_), channel_id=1, source_target_pairs={{0,16},{16,0},{1,17},{17,1},{2,18},{18,2},{3,19},{19,3},{4,20},{20... | collective-permute-start | bytes 1769480 | tf_op jit(solution)/shard_map/store/ppermute | solution.py:739
  60.6 4.8 %collective-permute-start.14 = (bf16[4,144,256]{2,1,0:T(8,128)(2,1)}, bf16[4,144,256]{2,1,0:T(8,128)(2,1)S(1)}, u32[]{:S(2)}, u32[]{:S(2)}) collective-permute-start(bf16[4,144,256]{2,1,0:T(8,128)(2,1)} %copy-done.12), channel_id=1, source_target_pairs={{0,16},{16,0},{1,17},{17,1},{2,18},{18,2},{3,19},{19,3},{4,20},{20... | collective-permute-start | bytes 884744 | tf_op jit(solution)/shard_map/store/ppermute | solution.py:739
  62.8 4.1 %collective-permute-start.16 = (bf16[4,144,256]{2,1,0:T(8,128)(2,1)}, bf16[4,144,256]{2,1,0:T(8,128)(2,1)S(1)}, u32[]{:S(2)}, u32[]{:S(2)}) collective-permute-start(bf16[4,144,256]{2,1,0:T(8,128)(2,1)} %copy-done.13), channel_id=1, source_target_pairs={{0,16},{16,0},{1,17},{17,1},{2,18},{18,2},{3,19},{19,3},{4,20},{20... | collective-permute-start | bytes 884744 | tf_op jit(solution)/shard_map/store/ppermute | solution.py:739
  64.8 2.7 %copy-start.7 = (bf16[8,144,256]{2,1,0:T(8,128)(2,1)}, bf16[8,144,256]{2,1,0:T(8,128)(2,1)S(1)}, u32[]{:S(2)}) copy-start(bf16[8,144,256]{2,1,0:T(8,128)(2,1)S(1)} %collective-permute-done.10.refs_10_) | copy-start | bytes 1769476
  64.8 13.8 %collective-permute-start.11 = (bf16[8,144,256]{2,1,0:T(8,128)(2,1)}, bf16[8,144,256]{2,1,0:T(8,128)(2,1)S(1)}, u32[]{:S(2)}, u32[]{:S(2)}) collective-permute-start(bf16[8,144,256]{2,1,0:T(8,128)(2,1)} %collective-permute-done.refs_1_), channel_id=1, source_target_pairs={{0,16},{16,0},{1,17},{17,1},{2,18},{18,2},{3,19},{19,3},{4,20},{20... | collective-permute-start | bytes 1769480 | tf_op jit(solution)/shard_map/store/ppermute | solution.py:739
  65.4 9.1 %copy-start.14 = (bf16[4,144,256]{2,1,0:T(8,128)(2,1)}, bf16[4,144,256]{2,1,0:T(8,128)(2,1)S(1)}, u32[]{:S(2)}) copy-start(bf16[4,144,256]{2,1,0:T(8,128)(2,1)S(1)} %collective-permute-done.14.refs_14_) | copy-start | bytes 884740
  65.4 9.1 %collective-permute-start.7 = (bf16[4,144,256]{2,1,0:T(8,128)(2,1)S(1)}, bf16[4,144,256]{2,1,0:T(8,128)(2,1)}, u32[]{:S(2)}, u32[]{:S(2)}) collective-permute-start(bf16[4,144,256]{2,1,0:T(8,128)(2,1)S(1)} %slice.21), channel_id=1, source_target_pairs={{0,96},{32,0},{64,32},{96,64},{1,97},{33,1},{65,33},{97,65},{2,98}... | collective-permute-start | bytes 884744 | tf_op jit(solution)/shard_map/store/ppermute | solution.py:736
  66.9 10.2 %copy-start.15 = (bf16[4,144,256]{2,1,0:T(8,128)(2,1)}, bf16[4,144,256]{2,1,0:T(8,128)(2,1)S(1)}, u32[]{:S(2)}) copy-start(bf16[4,144,256]{2,1,0:T(8,128)(2,1)S(1)} %collective-permute-done.16.refs_16_) | copy-start | bytes 884740
  66.9 10.2 %collective-permute-start.9 = (bf16[4,144,256]{2,1,0:T(8,128)(2,1)S(1)}, bf16[4,144,256]{2,1,0:T(8,128)(2,1)}, u32[]{:S(2)}, u32[]{:S(2)}) collective-permute-start(bf16[4,144,256]{2,1,0:T(8,128)(2,1)S(1)} %slice.23), channel_id=1, source_target_pairs={{0,32},{32,64},{64,96},{96,0},{1,33},{33,65},{65,97},{97,1},{2,34}... | collective-permute-start | bytes 884744 | tf_op jit(solution)/shard_map/store/ppermute | solution.py:737
  67.4 0.8 copy-start.8
  67.5 11.6 %collective-permute-start.13 = (bf16[8,144,256]{2,1,0:T(8,128)(2,1)}, bf16[8,144,256]{2,1,0:T(8,128)(2,1)}, u32[]{:S(2)}, u32[]{:S(2)}) collective-permute-start(bf16[8,144,256]{2,1,0:T(8,128)(2,1)} %collective-permute-done.4.refs_3_), channel_id=1, source_target_pairs={{0,16},{16,0},{1,17},{17,1},{2,18},{18,2},{3,19},{19,3},{4,20},{20... | collective-permute-start | bytes 1769480 | tf_op jit(solution)/shard_map/store/ppermute | solution.py:739
  67.5 7.1 %copy-start.9 = (bf16[8,144,256]{2,1,0:T(8,128)(2,1)}, bf16[8,144,256]{2,1,0:T(8,128)(2,1)S(1)}, u32[]{:S(2)}) copy-start(bf16[8,144,256]{2,1,0:T(8,128)(2,1)S(1)} %collective-permute-done.18.refs_18_) | copy-start | bytes 1769476
  67.5 11.6 %collective-permute-start.19 = (bf16[8,144,256]{2,1,0:T(8,128)(2,1)}, bf16[8,144,256]{2,1,0:T(8,128)(2,1)S(1)}, u32[]{:S(2)}, u32[]{:S(2)}) collective-permute-start(bf16[8,144,256]{2,1,0:T(8,128)(2,1)} %collective-permute-done.5.refs_9_), channel_id=1, source_target_pairs={{0,16},{16,0},{1,17},{17,1},{2,18},{18,2},{3,19},{19,3},{4,20},{20... | collective-permute-start | bytes 1769480 | tf_op jit(solution)/shard_map/store/ppermute | solution.py:739
  74.5 4.1 %collective-permute-start.15 = (bf16[4,144,256]{2,1,0:T(8,128)(2,1)}, bf16[4,144,256]{2,1,0:T(8,128)(2,1)S(1)}, u32[]{:S(2)}, u32[]{:S(2)}) collective-permute-start(bf16[4,144,256]{2,1,0:T(8,128)(2,1)} %collective-permute-done.7.refs_5_), channel_id=1, source_target_pairs={{0,16},{16,0},{1,17},{17,1},{2,18},{18,2},{3,19},{19,3},{4,20},{20... | collective-permute-start | bytes 884744 | tf_op jit(solution)/shard_map/store/ppermute | solution.py:739
  77.1 1.9 %collective-permute-start.17 = (bf16[4,144,256]{2,1,0:T(8,128)(2,1)}, bf16[4,144,256]{2,1,0:T(8,128)(2,1)}, u32[]{:S(2)}, u32[]{:S(2)}) collective-permute-start(bf16[4,144,256]{2,1,0:T(8,128)(2,1)} %collective-permute-done.9.refs_7_), channel_id=1, source_target_pairs={{0,16},{16,0},{1,17},{17,1},{2,18},{18,2},{3,19},{19,3},{4,20},{20... | collective-permute-start | bytes 884744 | tf_op jit(solution)/shard_map/store/ppermute | solution.py:739
  78.6 0.8 copy-start.10
  78.6 0.9 copy-start.16
  79.5 0.8 copy-start.11
  88.5 22.6 %collective-permute-start.20 = (bf16[4,592,128]{2,1,0:T(8,128)(2,1)}, bf16[4,592,128]{2,1,0:T(8,128)(2,1)S(1)}, u32[]{:S(2)}, u32[]{:S(2)}) collective-permute-start(bf16[4,592,128]{2,1,0:T(8,128)(2,1)} %memory_attend.2._), channel_id=1, source_target_pairs={{0,8},{8,0},{1,9},{9,1},{2,10},{10,2},{3,11},{11,3},{4,12},{12,4},... | collective-permute-start | bytes 1818632 | tf_op jit(solution)/shard_map/memory/ppermute | solution.py:751
  95.1 24.9 %all-to-all-start.3 = ((bf16[16,144,128]{2,1,0:T(8,128)(2,1)}), bf16[16,144,128]{2,1,0:T(8,128)(2,1)S(1)}, u32[]{:S(2)}, u32[]{:S(2)}) async-start(bf16[16,144,128]{2,1,0:T(8,128)(2,1)} %temporal_attend.1.refs_20_), calls=%async_computation.3 | async-start | bytes 1179648 | tf_op jit(solution)/shard_map/temporal/all_to_all | solution.py:678
  113.4 10.7 %collective-permute-start.21 = (bf16[592,128]{1,0:T(8,128)(2,1)}, bf16[592,128]{1,0:T(8,128)(2,1)S(1)}, u32[]{:S(2)}, u32[]{:S(2)}) collective-permute-start(bf16[592,128]{1,0:T(8,128)(2,1)} %get-tuple-element.30), channel_id=1, source_target_pairs={{0,1},{1,2},{2,3},{3,0},{4,5},{5,6},{6,7},{7,4},{8,9},{9,10},{10,1... | collective-permute-start | bytes 454664 | tf_op jit(solution)/shard_map/memory/ppermute | solution.py:681
  115.6 9.6 %collective-permute-start.22 = (bf16[592,128]{1,0:T(8,128)(2,1)}, bf16[592,128]{1,0:T(8,128)(2,1)S(1)}, u32[]{:S(2)}, u32[]{:S(2)}) collective-permute-start(bf16[592,128]{1,0:T(8,128)(2,1)} %get-tuple-element.31), channel_id=1, source_target_pairs={{0,2},{1,3},{2,0},{3,1},{4,6},{5,7},{6,4},{7,5},{8,10},{9,11},{10,... | collective-permute-start | bytes 454664 | tf_op jit(solution)/shard_map/memory/ppermute | solution.py:681
  118.5 6.6 %collective-permute-start.23 = (bf16[592,128]{1,0:T(8,128)(2,1)}, bf16[592,128]{1,0:T(8,128)(2,1)S(1)}, u32[]{:S(2)}, u32[]{:S(2)}) collective-permute-start(bf16[592,128]{1,0:T(8,128)(2,1)} %get-tuple-element.32), channel_id=1, source_target_pairs={{0,3},{1,0},{2,1},{3,2},{4,7},{5,4},{6,5},{7,6},{8,11},{9,8},{10,9... | collective-permute-start | bytes 454664 | tf_op jit(solution)/shard_map/memory/ppermute | solution.py:681
